TPU v7x, 32 devices: a whole 2x2x4 slice. The times are simulated.
32 devices in a mesh: groups: 1, wide: 32 (over z, y, x, core).
Axes of the slice: x: 2, y: 2, z: 4, core: 2. Of those that a mesh axis runs over, the one named last changes fastest.
Arguments:
- activations: bfloat16 [128, 16384], P('groups', 'wide'), may hold values from -6 to 6
- norm_gain: float32 [16384], replicated, may hold values from 0.1 to 1.9
- query_weight: bfloat16 [16384, 16384], P(None, 'wide'), may hold values from -1 to 1
- key_weight: bfloat16 [16384, 1024], P('wide'), may hold values from -1 to 1
- value_weight: bfloat16 [16384, 1024], P('wide'), may hold values from -0.046875 to 0.046875
- output_weight: bfloat16 [16384, 16384], P('wide'), may hold values from -0.09375 to 0.09375
Outputs:
- layer_output: bfloat16 [128, 16384], P('groups', 'wide')
All inputs are finite; a program needn't handle non-finite values.
Results may differ from a plain program's by a relative error of at most 0.0087.
Values may be sent and summed in bfloat16 or wider, within the bound.
No kernel may reach another device: no remote copies, remote signals or barrier semaphores. Data moves between devices by JAX's collectives and lax.ppermute only.
A program may use at most 128 MiB of HBM per device.

v0:
```python
import jax
import jax.numpy as jnp
from jax import lax
from jax.sharding import PartitionSpec as P

HEADS = 128
KVH = 8
HEAD = 128


def rotary(heads_field, positions):
    half_width = heads_field.shape[-1] // 2
    frequency = 500000.0 ** (
        -(jnp.arange(half_width, dtype=jnp.float32) * 2.0) / heads_field.shape[-1]
    )
    angles = positions[:, None] * frequency[None, :]
    cosine = jnp.cos(angles)[:, None, :]
    sine_part = jnp.sin(angles)[:, None, :]
    first_half = heads_field[..., :half_width]
    second = heads_field[..., half_width:]
    return jnp.concatenate(
        [first_half * cosine - second * sine_part, second * cosine + first_half * sine_part],
        axis=-1,
    )


def per_device(activations, norm_gain, query_weight, key_weight, value_weight, output_weight):
    tokens_here = activations.shape[0]
    local_width = activations.shape[1]
    gathered = lax.all_gather(activations, "wide", axis=1, tiled=True).astype(jnp.float32)
    mean_square = jnp.mean(gathered * gathered, axis=1, keepdims=True)
    normed = (gathered * lax.rsqrt(mean_square + 1e-05) * norm_gain[None, :]).astype(jnp.bfloat16)
    normed_own = lax.dynamic_slice_in_dim(
        normed, lax.axis_index("wide") * local_width, local_width, 1
    )
    heads_here = query_weight.shape[1] // HEAD
    queries = jnp.dot(normed, query_weight, preferred_element_type=jnp.float32)
    kv_weight = jnp.concatenate([key_weight, value_weight], axis=1)
    kv_term = jnp.dot(normed_own, kv_weight, preferred_element_type=jnp.float32)
    kv_rows = lax.psum(kv_term, "wide").astype(jnp.bfloat16)
    key_all = kv_rows[:, : KVH * HEAD]
    value_all = kv_rows[:, KVH * HEAD :]
    positions = jnp.arange(tokens_here, dtype=jnp.float32)
    query_rot = rotary(queries.reshape(tokens_here, heads_here, HEAD), positions).astype(
        jnp.bfloat16
    )
    group_index = lax.axis_index("wide") * heads_here // (HEADS // KVH)
    key_head = lax.dynamic_index_in_dim(
        key_all.reshape(tokens_here, KVH, HEAD), group_index, 1, keepdims=True
    )
    key_rot = rotary(key_head.astype(jnp.float32), positions).astype(jnp.bfloat16)[:, 0, :]
    value_head = lax.dynamic_index_in_dim(
        value_all.reshape(tokens_here, KVH, HEAD), group_index, 1, keepdims=False
    )
    scores = jnp.einsum(
        "qhd,kd->hqk", query_rot, key_rot, preferred_element_type=jnp.float32
    ) * HEAD ** (-0.5)
    causal = jnp.arange(tokens_here)[:, None] >= jnp.arange(tokens_here)[None, :]
    scores = jnp.where(causal[None, :, :], scores, -1e30)
    row_peak = jnp.max(scores, axis=2, keepdims=True)
    weights = jnp.exp(scores - row_peak)
    probabilities = (weights / jnp.sum(weights, axis=2, keepdims=True)).astype(jnp.bfloat16)
    attended = jnp.einsum(
        "hqk,kd->qhd", probabilities, value_head, preferred_element_type=jnp.float32
    )
    attended = attended.astype(jnp.bfloat16).reshape(tokens_here, heads_here * HEAD)
    partial_value = jnp.dot(attended, output_weight, preferred_element_type=jnp.float32)
    summed = lax.psum_scatter(partial_value, "wide", scatter_dimension=1, tiled=True)
    return summed.astype(jnp.bfloat16)


def solution(mesh):
    return jax.shard_map(
        per_device,
        mesh=mesh,
        in_specs=(
            P("groups", "wide"),
            P(),
            P(None, "wide"),
            P("wide", None),
            P("wide", None),
            P("wide", None),
        ),
        out_specs=P("groups", "wide"),
        check_vma=False,
    )
```

profile of v0, /device:TPU:0, one launch (start us, length us, event | category | flops | bytes accessed | tf_op | source)
XLA Modules:
  0.0 311.8 jit_solution(17742135370820224849)
XLA Ops:
  6.5 0.0 all-gather.2.cloned.1.call-start
  6.5 0.7 all-gather.2.cloned.1.call-update
  7.3 0.0 reduce-scatter.2.cloned.1.call-start
  7.4 0.3 fusion.17
  7.6 69.4 %all-gather.2.cloned.1.call-done = bf16[128,16384]{1,0:T(8,128)(2,1)} async-done(((bf16[128,512]{1,0:T(8,128)(2,1)}), bf16[128,16384]{1,0:T(8,128)(2,1)}) %all-gather.2.cloned.1.call-update) | async-done | bytes 4194320 | tf_op jit(solution)/shard_map/all_gather | solution.py:30
  77.0 3.1 fusion.1
  80.1 3.4 %fusion.3 = bf16[128,16384]{1,0:T(8,128)(2,1)S(1)} fusion(bf16[128,16384]{1,0:T(8,128)(2,1)} %all-gather.2.cloned.1.call-done, f32[16384]{0:T(1024)} %param.7, f32[128]{0:T(128)S(1)} %add_rsqrt_fusion), kind=kLoop, calls=%fused_computation.5 | loop fusion | flops 8388608 | bytes 8454656 | tf_op jit(solution)/shard_map/convert_element_type | solution.py:32
  83.5 0.0 copy-start
  83.5 0.0 copy-start.1
  83.5 8.5 %fusion.39 = f32[128,512]{1,0:T(8,128)S(1)} fusion(bf16[128,16384]{1,0:T(8,128)(2,1)S(1)} %fusion.3, bf16[16384,512]{1,0:T(8,128)(2,1)} %param.8), kind=kOutput, calls=%fused_computation.54 | convolution fusion | flops 2147483648 | bytes 21233664 | tf_op jit(solution)/shard_map/dot_general | solution.py:37
  92.0 0.0 copy-done
  92.1 0.0 copy-done.1
  92.1 0.4 fusion.4
  92.5 50.1 %all-reduce.1 = bf16[128,2048]{1,0:T(8,128)(2,1)S(1)} all-reduce(f32[128,2048]{1,0:T(8,128)S(1)} %fusion.4), channel_id=1, replica_groups=mesh['groups'=1,'wide'=32] {'wide'}, use_global_device_ids=true, to_apply=%region_1.0 | all-reduce | flops 262144 | bytes 1572864 | tf_op jit(solution)/shard_map/psum | solution.py:40
  142.7 0.1 reshape.119
  142.9 0.1 constant_dynamic-slice_fusion
  143.1 0.3 fusion.23
  143.4 0.2 fusion.35
  143.6 0.1 subtract_convert_fusion
  143.6 0.3 fusion.36
  144.0 0.3 fusion.10
  144.3 0.1 copy.7
  144.4 0.2 convolution_convert_fusion
  144.6 11.5 %fusion.40 = f32[128,16384]{1,0:T(8,128)} fusion(bf16[128,512]{0,1:T(8,128)(2,1)S(1)} %bitcast.39, bf16[512,16384]{1,0:T(8,128)(2,1)} %param.11), kind=kOutput, calls=%fused_computation.55 | convolution fusion | flops 2147483648 | bytes 25296896 | tf_op jit(solution)/shard_map/dot_general | solution.py:67
  156.1 0.0 reduce-scatter.2.cloned.1.call-update
  156.1 147.3 %reduce-scatter.2.cloned.1.call-done = f32[128,512]{1,0:T(8,128)} async-done(((f32[128,16384]{1,0:T(8,128)}), f32[128,512]{1,0:T(8,128)}) %reduce-scatter.2.cloned.1.call-update) | async-done | bytes 262160 | tf_op jit(solution)/shard_map/reduce_scatter | solution.py:68
  303.4 1.6 convert_element_type.36
  (7 shorter events, 0.2 us)
Async XLA Ops:
  6.5 70.4 %all-gather.2.cloned.1.call-start = ((), (), s32[]{:S(2)}) async-start(), calls=%async_computation.1 | async-start | bytes 4325376 | tf_op jit(solution)/shard_map/all_gather | solution.py:30
  7.3 296.1 %reduce-scatter.2.cloned.1.call-start = ((), (), s32[]{:S(2)}) async-start(), calls=%async_computation.2 | async-start | bytes 8650752 | tf_op jit(solution)/shard_map/reduce_scatter | solution.py:68
  83.5 8.5 %copy-start = (bf16[512,1024]{1,0:T(8,128)(2,1)S(1)}, bf16[512,1024]{1,0:T(8,128)(2,1)}, u32[]{:S(2)}) copy-start(bf16[512,1024]{1,0:T(8,128)(2,1)} %param.10) | copy-start | bytes 3145732
  83.5 8.5 %copy-start.1 = (bf16[512,1024]{1,0:T(8,128)(2,1)S(1)}, bf16[512,1024]{1,0:T(8,128)(2,1)}, u32[]{:S(2)}) copy-start(bf16[512,1024]{1,0:T(8,128)(2,1)} %param.9) | copy-start | bytes 3145732
Sparse Core Ops, SparseCore 0:
  10.2 66.6 all-gather.1
  156.2 147.0 reduce-scatter.1
where the time goes:
time: 312 us
  waiting for transfers between devices  217 us (70%)
  blocking collectives  50.1 us (16%)
  matrix products  21.3 us (7%)
  between operations  13.6 us (4%)
  other arithmetic  8.78 us (3%)
    reduce_scatter x1, waiting for transfers between devices, per_device(): lax.psum_scatter(partial_value, 'wide', scatter_dimension=1, tiled=True)  147 us
    all_gather x1, waiting for transfers between devices, per_device(): lax.all_gather(activations, 'wide', axis=1, tiled=True).astype(jnp.float32)  69.4 us
    psum x1, blocking collectives, per_device(): kv_rows = lax.psum(kv_term, 'wide').astype(jnp.bfloat16)  50.1 us
    dot_general x1, matrix products, per_device(): jnp.dot(attended, output_weight, preferred_element_type=jnp.float32)  11.5 us
    dot_general x1, matrix products, per_device(): queries = jnp.dot(normed, query_weight, preferred_element_type=jnp.float32)  8.51 us
  transfers between devices with their start and end apart: 2, of which 2 were waited for; matrix products, arithmetic and copies ran while one was open for 0% of the time, Pallas kernels for 0%

commit v1 on v0

v1 whole, which is shorter than its diff:
```python
import functools

import jax
import jax.numpy as jnp
from jax import lax
from jax.experimental import pallas as pl
from jax.experimental.pallas import tpu as pltpu
from jax.sharding import PartitionSpec as P

HEADS = 128
KVH = 8
HEAD = 128
EPS = 1e-05
MIB = 1 << 20


def combos(bits):
    out = [0]
    for b in bits:
        out = out + [o ^ b for o in out]
    return out


def exchange(x, offset, n):
    return lax.ppermute(x, "wide", [(i, i ^ offset) for i in range(n)])


def vmem():
    return pl.BlockSpec(memory_space=pltpu.VMEM)


def smem():
    return pl.BlockSpec(memory_space=pltpu.SMEM)


def hbm():
    return pl.BlockSpec(memory_space=pl.ANY)


def dot(a, b):
    return jnp.dot(a, b, preferred_element_type=jnp.float32)


def kv_kernel(table, act, gain, wk, wv, send, keep):
    scaled = (act[...].astype(jnp.float32) * gain[...]).astype(jnp.bfloat16)
    core = table[0]
    for j in range(send.shape[0]):
        cols = pl.ds(pl.multiple_of(table[1 + j] * HEAD, HEAD), HEAD)
        k = dot(scaled, wk[:, cols])
        v = dot(scaled, wv[:, cols])
        keep[j] = jnp.where(core == 0, k, v)
        send[j] = jnp.where(core == 0, v, k).astype(jnp.bfloat16)


def kv_terms(table, act, gain_own, wk, wv):
    tokens = act.shape[0]
    return pl.pallas_call(
        kv_kernel,
        out_shape=[
            jax.ShapeDtypeStruct((KVH, tokens, HEAD), jnp.bfloat16),
            jax.ShapeDtypeStruct((KVH, tokens, HEAD), jnp.float32),
        ],
        in_specs=[smem(), vmem(), vmem(), vmem(), vmem()],
        out_specs=[vmem(), vmem()],
        compiler_params=pltpu.CompilerParams(vmem_limit_bytes=24 * MIB),
        cost_estimate=pl.CostEstimate(
            flops=4 * tokens * act.shape[1] * KVH * HEAD,
            bytes_accessed=2 * wk.size * 2,
            transcendentals=0,
        ),
    )(table, act, gain_own, wk, wv)


def attend(queries, k_sum, v_sum, cosine, sine, scale):
    k_rows = (k_sum * scale).astype(jnp.bfloat16).astype(jnp.float32)
    value = (v_sum * scale).astype(jnp.bfloat16)

    def rotate(x):
        half = HEAD // 2
        turned = jnp.concatenate([x[:, half:], x[:, :half]], axis=1)
        return (x * cosine + turned * sine).astype(jnp.bfloat16)

    key = rotate(k_rows)
    tokens = key.shape[0]
    rows = lax.broadcasted_iota(jnp.int32, (tokens, tokens), 0)
    cols = lax.broadcasted_iota(jnp.int32, (tokens, tokens), 1)
    out = []
    for h in range(queries.shape[1] // HEAD):
        q = rotate(queries[:, h * HEAD : (h + 1) * HEAD] * scale)
        scores = lax.dot_general(
            q, key, (((1,), (1,)), ((), ())), preferred_element_type=jnp.float32
        ) * HEAD ** (-0.5)
        scores = jnp.where(rows >= cols, scores, -1e30)
        weights = jnp.exp(scores - jnp.max(scores, axis=1, keepdims=True))
        probs = (weights / jnp.sum(weights, axis=1, keepdims=True)).astype(jnp.bfloat16)
        out.append(dot(probs, value).astype(jnp.bfloat16))
    return jnp.concatenate(out, axis=1)


def query_kernel(plan, pieces, last, features, *refs):
    table, gain = refs[0], refs[1]
    blocks = refs[2 : 2 + pieces]
    rest = refs[2 + pieces :]
    if last:
        weight, q_in, sq_in, k_sum, v_sum, cosine, sine, out, wbuf, sems = rest
    else:
        weight, q_out, sq_out, wbuf, sems = rest
    depth = wbuf.shape[1]

    def fetch(i):
        start = pl.multiple_of(table[i] * depth, depth)
        return pltpu.make_async_copy(weight.at[pl.ds(start, depth), :], wbuf.at[i], sems.at[i])

    for i in range(len(plan)):
        fetch(i).start()
    if last:
        queries, squares = q_in[...], sq_in[...]
    else:
        queries, squares = None, None
    for i, (piece, block, column) in enumerate(plan):
        x = blocks[piece][block, :, column : column + depth].astype(jnp.float32)
        scaled = (x * gain[pl.ds(table[i], 1), :]).astype(jnp.bfloat16)
        fetch(i).wait()
        term = dot(scaled, wbuf[i])
        queries = term if queries is None else queries + term
        squares = x * x if squares is None else squares + x * x
    if last:
        mean = jnp.sum(squares, axis=1, keepdims=True) * (1.0 / features)
        out[...] = attend(
            queries, k_sum[...], v_sum[...], cosine[...], sine[...], lax.rsqrt(mean + EPS)
        )
    else:
        q_out[...] = queries
        sq_out[...] = squares


def query_call(plan, table, gain, blocks, weight, carry=None, extra=()):
    depth = gain.shape[1]
    tokens, columns = blocks[0].shape[1], weight.shape[1]
    last = carry is not None
    if last:
        out_shape = [jax.ShapeDtypeStruct((tokens, columns), jnp.bfloat16)]
    else:
        out_shape = [
            jax.ShapeDtypeStruct((tokens, columns), jnp.float32),
            jax.ShapeDtypeStruct((tokens, depth), jnp.float32),
        ]
    more = (list(carry) + list(extra)) if last else []
    return pl.pallas_call(
        functools.partial(query_kernel, plan, len(blocks), last, weight.shape[0]),
        out_shape=out_shape,
        in_specs=[smem(), vmem()] + [vmem()] * len(blocks) + [hbm()] + [vmem()] * len(more),
        out_specs=[vmem()] * len(out_shape),
        scratch_shapes=[
            pltpu.VMEM((len(plan), depth, columns), jnp.bfloat16),
            pltpu.SemaphoreType.DMA((len(plan),)),
        ],
        compiler_params=pltpu.CompilerParams(vmem_limit_bytes=32 * MIB),
        cost_estimate=pl.CostEstimate(
            flops=2 * tokens * columns * depth * len(plan),
            bytes_accessed=2 * columns * depth * len(plan),
            transcendentals=0,
        ),
    )(table, gain, *blocks, weight, *more)


def output_kernel(sizes, added, table, attended, *refs):
    if added:
        arrived, weight, refs = refs[0], refs[1], refs[2:]
    else:
        arrived, weight, refs = None, refs[0], refs[1:]
    outs, wbuf, sems = refs[: len(sizes)], refs[len(sizes)], refs[len(sizes) + 1]
    width = wbuf.shape[2]

    def fetch(i):
        start = pl.multiple_of(table[i] * width, width)
        return pltpu.make_async_copy(weight.at[:, pl.ds(start, width)], wbuf.at[i], sems.at[i])

    for i in range(sum(sizes)):
        fetch(i).start()
    i = 0
    for out in outs:
        for j in range(out.shape[0]):
            fetch(i).wait()
            term = dot(attended[...], wbuf[i])
            if added:
                term = term + arrived[i].astype(jnp.float32)
            out[j] = term.astype(out.dtype)
            i += 1


def output_call(sizes, dtype, table, attended, weight, width, arrived=None):
    tokens, depth = attended.shape
    count = sum(sizes)
    added = arrived is not None
    return pl.pallas_call(
        functools.partial(output_kernel, sizes, added),
        out_shape=[jax.ShapeDtypeStruct((s, tokens, width), dtype) for s in sizes],
        in_specs=[smem(), vmem()] + [vmem()] * added + [hbm()],
        out_specs=[vmem()] * len(sizes),
        scratch_shapes=[
            pltpu.VMEM((count, depth, width), jnp.bfloat16),
            pltpu.SemaphoreType.DMA((count,)),
        ],
        compiler_params=pltpu.CompilerParams(vmem_limit_bytes=32 * MIB),
        cost_estimate=pl.CostEstimate(
            flops=2 * tokens * depth * width * count,
            bytes_accessed=2 * depth * width * count,
            transcendentals=0,
        ),
    )(table, attended, *([arrived] if added else []), weight)


def rotary_tables(tokens):
    half = HEAD // 2
    frequency = 500000.0 ** (-(jnp.arange(half, dtype=jnp.float32) * 2.0) / HEAD)
    angles = jnp.arange(tokens, dtype=jnp.float32)[:, None] * frequency[None, :]
    cosine, sine = jnp.cos(angles), jnp.sin(angles)
    return jnp.concatenate([cosine, cosine], axis=1), jnp.concatenate([-sine, sine], axis=1)


def per_device(n, act, norm_gain, wq, wk, wv, wo):
    tokens, width = act.shape
    me = lax.axis_index("wide")
    count = n.bit_length() - 1
    bits = [1 << i for i in range(count)]
    core = bits[0]
    parts = 2 if width % 256 == 0 else 1
    depth = width // parts
    orders = [(bits[1], bits[2]), (bits[2], bits[1])][:parts]
    far = combos(bits[3:])
    swap = functools.partial(exchange, n=n)

    def halves(x, p):
        return x[..., p * depth : (p + 1) * depth]

    def index_of(offset, p):
        return (me ^ offset) * parts + p

    def table_of(pairs):
        return jnp.stack([index_of(o, p) for o, p in pairs]).astype(jnp.int32)

    shared = (n // KVH).bit_length() - 1
    first, others = bits[shared], combos(bits[shared + 1 :])
    head_offsets = [o ^ first for o in others] + others
    is_core0 = (me & core) == 0
    kv_table = jnp.stack([me & core] + [(me ^ o) >> shared for o in head_offsets]).astype(jnp.int32)
    gain_own = lax.dynamic_slice_in_dim(norm_gain, me * width, width)[None, :]
    kv_send, kv_keep = kv_terms(kv_table, act, gain_own, wk, wv)
    kv = kv_keep + swap(kv_send, core).astype(jnp.float32)
    kv = kv[len(others) :] + swap(kv[: len(others)].astype(jnp.bfloat16), first).astype(jnp.float32)
    total = kv[0]
    for i, o in enumerate(others):
        if o:
            total = total + swap(kv[i].astype(jnp.bfloat16), o).astype(jnp.float32)
    for b in bits[1:shared]:
        total = total + swap(total.astype(jnp.bfloat16), b).astype(jnp.float32)
    other = swap(total, core)
    k_sum = jnp.where(is_core0, total, other)
    v_sum = jnp.where(is_core0, other, total)

    held = jnp.stack([act] + [swap(act, o) for o in far[1:]])
    near = [swap(halves(held, p), orders[p][0]) for p in range(parts)]
    last = [
        swap(jnp.concatenate([halves(held, p), near[p]]), orders[p][1]) for p in range(parts)
    ]
    held_other = swap(held, core)
    near_other = [swap(x, core) for x in near]
    last_other = [swap(x, core) for x in last]

    def plan_of(groups):
        plan, pairs = [], []
        for piece, (offsets, ps) in enumerate(groups):
            for p in ps:
                for block, o in enumerate(offsets):
                    plan.append((piece, block, ps.index(p) * depth))
                    pairs.append((o, p))
        return plan, table_of(pairs)

    near_of = [[o ^ orders[p][0] for o in far] for p in range(parts)]
    last_of = [[o ^ orders[p][1] for o in far + near_of[p]] for p in range(parts)]
    every = list(range(parts))
    gain = norm_gain.reshape(n * parts, depth)

    def both(offsets, ps):
        return [(offsets, ps), ([o ^ core for o in offsets], ps)]

    groups = both(far, every)
    blocks = [held, held_other]
    for p in every:
        groups += both(near_of[p], [p])
        blocks += [near[p], near_other[p]]
    plan, table = plan_of(groups)
    carry = query_call(plan, table, gain, blocks, wq)
    groups, blocks = [], []
    for p in every:
        groups += both(last_of[p], [p])
        blocks += [last[p], last_other[p]]
    plan, table = plan_of(groups)
    cosine, sine = rotary_tables(tokens)
    (attended,) = query_call(
        plan, table, gain, blocks, wq, carry, (k_sum, v_sum, cosine, sine)
    )

    def offsets_of(p, first_set):
        a, b = orders[p]
        low = [o ^ b for o in far] + far
        return [o ^ a for o in low] if first_set else low

    sizes = [2 * len(far)] * parts

    def table_for(first_set, other_core):
        return table_of(
            [
                (o ^ core if other_core else o, p)
                for p in every
                for o in offsets_of(p, first_set)
            ]
        )

    whole = [sum(sizes)]
    (send_1,) = output_call(whole, jnp.bfloat16, table_for(True, True), attended, wo, depth)
    got_1 = swap(send_1, core)
    (send_2,) = output_call(whole, jnp.bfloat16, table_for(False, True), attended, wo, depth)
    got_2 = swap(send_2, core)
    firsts = output_call(sizes, jnp.bfloat16, table_for(True, False), attended, wo, depth, got_1)
    got_first = [swap(firsts[p], orders[p][0]) for p in every]
    keeps = output_call(sizes, jnp.float32, table_for(False, False), attended, wo, depth, got_2)
    f = len(far)
    finals = []
    for p in every:
        send = (keeps[p][:f] + got_first[p][:f].astype(jnp.float32)).astype(jnp.bfloat16)
        got = swap(send, orders[p][1])
        keep = keeps[p][f:] + got_first[p][f:].astype(jnp.float32)
        finals.append(keep + got.astype(jnp.float32))
    final = jnp.concatenate(finals, axis=2)
    out = final[0]
    for i in range(1, f):
        out = out + swap(final[i].astype(jnp.bfloat16), far[i]).astype(jnp.float32)
    return out.astype(jnp.bfloat16)


def solution(mesh):
    return jax.shard_map(
        functools.partial(per_device, mesh.shape["wide"]),
        mesh=mesh,
        in_specs=(
            P("groups", "wide"),
            P(),
            P(None, "wide"),
            P("wide", None),
            P("wide", None),
            P("wide", None),
        ),
        out_specs=P("groups", "wide"),
        check_vma=False,
    )
```

time: 312 us -> 147 us (0.47)
  waiting for transfers between devices: 217 us -> 35.8 us
  blocking collectives: 50.1 us -> 0 us
  local copies, waits for them, and re-layouts: 0.69 us -> 40.4 us
  Pallas kernels: 0 us -> 34 us
  starting transfers between devices: 0.04 us -> 32.7 us
  matrix products: 21.3 us -> 0 us
  between operations: 13.6 us -> 0.39 us
  other arithmetic: 8.78 us -> 3.25 us
    reduce_scatter x1 -> x0, waiting for transfers between devices: 147 us -> none  [per_device(): lax.psum_scatter(partial_value, 'wide', scatter_dimension=1, tiled=True)]
    all_gather x1 -> x0, waiting for transfers between devices: 69.4 us -> none  [per_device(): lax.all_gather(activations, 'wide', axis=1, tiled=True).astype(jnp.float32)]
    psum x1 -> x0, blocking collectives: 50.1 us -> none  [per_device(): kv_rows = lax.psum(kv_term, 'wide').astype(jnp.bfloat16)]
    unnamed x7 -> x22, local copies, waits for them, and re-layouts: 0.14 us -> 38 us
    ppermute x0 -> x28, waiting for transfers between devices: none -> 35.8 us  [exchange(): return lax.ppermute(x, 'wide', [(i, i ^ offset) for i in range(n)])]
    pallas_call x0 -> x7, Pallas kernels: none -> 34 us  [the longest x4 21.4 us: output_call(): pl.pallas_call(functools.partial(output_kernel, sizes, added), out_shape=...]
    ppermute x0 -> x28, starting transfers between devices: none -> 32.7 us  [exchange(): return lax.ppermute(x, 'wide', [(i, i ^ offset) for i in range(n)])]
    dot_general x5 -> x0, matrix products: 20.9 us -> none  [the longest x1 11.5 us: per_device(): jnp.dot(attended, output_weight, preferred_element_type=jnp.float32)]
  transfers between devices with their start and end apart: 2 -> 28, of which waited for: 2 -> 10; matrix products, arithmetic and copies ran while one was open for 0% -> 3% of each run, Pallas kernels for 0% -> 14%
where the time goes in v1:
time: 147 us
  local copies, waits for them, and re-layouts  40.4 us (27%)
  waiting for transfers between devices  35.8 us (24%)
  Pallas kernels  34 us (23%)
  starting transfers between devices  32.7 us (22%)
  other arithmetic  3.25 us (2%)
    unnamed x22, local copies, waits for them, and re-layouts  38 us
    ppermute x28, waiting for transfers between devices, exchange(): return lax.ppermute(x, 'wide', [(i, i ^ offset) for i in range(n)])  35.8 us
    ppermute x28, starting transfers between devices, exchange(): return lax.ppermute(x, 'wide', [(i, i ^ offset) for i in range(n)])  32.7 us
    pallas_call x4, Pallas kernels, output_call(): pl.pallas_call(functools.partial(output_kernel, sizes, added), out_shape=...  21.4 us
    pallas_call x2, Pallas kernels, query_call(): pl.pallas_call(functools.partial(query_kernel, plan, len(blocks), last, w...  11.3 us
  transfers between devices with their start and end apart: 28, of which 10 were waited for; matrix products, arithmetic and copies ran while one was open for 3% of the time, Pallas kernels for 14%

profile of v1, /device:TPU:0, one launch (start us, length us, event | category | flops | bytes accessed | tf_op | source)
XLA Modules:
  0.0 146.5 jit_solution(14328367861601455989)
XLA Ops:
  0.0 0.8 dynamic_slice.3
  0.8 1.2 copy-done.6
  2.1 1.2 copy-done.7
  3.3 0.9 copy-done.8
  4.2 1.3 shard_map.65
  5.5 0.5 collective-permute-start.12
  6.0 2.7 %collective-permute-start = (bf16[128,512]{1,0:T(8,128)(2,1)S(1)}, bf16[128,512]{1,0:T(8,128)(2,1)S(1)}, u32[]{:S(2)}, u32[]{:S(2)}) collective-permute-start(bf16[128,512]{1,0:T(8,128)(2,1)S(1)} %copy-done.8), channel_id=1, source_target_pairs={{0,8},{1,9},{2,10},{3,11},{4,12},{5,13},{6,14},{7,15},{8,0},{9,1},... | collective-permute-start | bytes 393224 | tf_op jit(solution)/shard_map/ppermute | solution.py:25
  8.7 2.6 %collective-permute-start.1 = (bf16[128,512]{1,0:T(8,128)(2,1)S(1)}, bf16[128,512]{1,0:T(8,128)(2,1)S(1)}, u32[]{:S(2)}, u32[]{:S(2)}) collective-permute-start(bf16[128,512]{1,0:T(8,128)(2,1)S(1)} %copy-done.8), channel_id=1, source_target_pairs={{0,16},{1,17},{2,18},{3,19},{4,20},{5,21},{6,22},{7,23},{8,24},{9,... | collective-permute-start | bytes 393224 | tf_op jit(solution)/shard_map/ppermute | solution.py:25
  11.3 3.7 %collective-permute-done = bf16[128,512]{1,0:T(8,128)(2,1)S(1)} collective-permute-done((bf16[128,512]{1,0:T(8,128)(2,1)S(1)}, bf16[128,512]{1,0:T(8,128)(2,1)S(1)}, u32[]{:S(2)}, u32[]{:S(2)}) %collective-permute-start) | collective-permute-done | bytes 131104 | tf_op jit(solution)/shard_map/ppermute | solution.py:25
  15.0 6.6 %collective-permute-done.1 = bf16[128,512]{1,0:T(8,128)(2,1)S(1)} collective-permute-done((bf16[128,512]{1,0:T(8,128)(2,1)S(1)}, bf16[128,512]{1,0:T(8,128)(2,1)S(1)}, u32[]{:S(2)}, u32[]{:S(2)}) %collective-permute-start.1) | collective-permute-done | bytes 131104 | tf_op jit(solution)/shard_map/ppermute | solution.py:25
  21.8 1.6 %collective-permute-start.13 = (bf16[4,128,128]{2,1,0:T(8,128)(2,1)S(1)}, bf16[4,128,128]{2,1,0:T(8,128)(2,1)S(1)}, u32[]{:S(2)}, u32[]{:S(2)}) collective-permute-start(bf16[4,128,128]{2,1,0:T(8,128)(2,1)S(1)} %slice.149), channel_id=1, source_target_pairs={{0,4},{1,5},{2,6},{3,7},{4,0},{5,1},{6,2},{7,3},{8,12},{9,13},{10,... | collective-permute-start | bytes 393224 | tf_op jit(solution)/shard_map/ppermute | solution.py:25
  23.4 1.6 %collective-permute-start.3 = (bf16[4,128,256]{2,1,0:T(8,128)(2,1)S(1)}, bf16[4,128,256]{2,1,0:T(8,128)(2,1)S(1)}, u32[]{:S(2)}, u32[]{:S(2)}) collective-permute-start(bf16[4,128,256]{2,1,0:T(8,128)(2,1)S(1)} %get-tuple-element.27), channel_id=1, source_target_pairs={{0,2},{1,3},{2,0},{3,1},{4,6},{5,7},{6,4},{7,5},{8,10},{9,11},{10,... | collective-permute-start | bytes 786440 | tf_op jit(solution)/shard_map/ppermute | solution.py:25
  24.9 0.5 collective-permute-start.6
  25.5 2.5 %collective-permute-done.13 = bf16[4,128,128]{2,1,0:T(8,128)(2,1)S(1)} collective-permute-done((bf16[4,128,128]{2,1,0:T(8,128)(2,1)S(1)}, bf16[4,128,128]{2,1,0:T(8,128)(2,1)S(1)}, u32[]{:S(2)}, u32[]{:S(2)}) %collective-permute-start.13) | collective-permute-done | bytes 131104 | tf_op jit(solution)/shard_map/ppermute | solution.py:25
  28.0 2.0 %collective-permute-start.14 = (bf16[128,128]{1,0:T(8,128)(2,1)S(1)}, bf16[128,128]{1,0:T(8,128)(2,1)S(1)}, u32[]{:S(2)}, u32[]{:S(2)}) collective-permute-start(bf16[128,128]{1,0:T(8,128)(2,1)S(1)} %get-tuple-element.30), channel_id=1, source_target_pairs={{0,8},{1,9},{2,10},{3,11},{4,12},{5,13},{6,14},{7,15},{8,0},{9,1},... | collective-permute-start | bytes 98312 | tf_op jit(solution)/shard_map/ppermute | solution.py:25
  30.0 1.2 collective-permute-start.15
  31.2 1.3 collective-permute-start.16
  32.6 2.5 %collective-permute-start.7 = (bf16[8,128,256]{2,1,0:T(8,128)(2,1)S(1)}, bf16[8,128,256]{2,1,0:T(8,128)(2,1)S(1)}, u32[]{:S(2)}, u32[]{:S(2)}) collective-permute-start(bf16[8,128,256]{2,1,0:T(8,128)(2,1)S(1)} %pad_maximum_fusion.3), channel_id=1, source_target_pairs={{0,2},{1,3},{2,0},{3,1},{4,6},{5,7},{6,4},{7,5},{8,10},{9,11},{10,... | collective-permute-start | bytes 1572872 | tf_op jit(solution)/shard_map/ppermute | solution.py:25
  35.1 1.7 %collective-permute-start.4 = (bf16[8,128,256]{2,1,0:T(8,128)(2,1)S(1)}, bf16[8,128,256]{2,1,0:T(8,128)(2,1)S(1)}, u32[]{:S(2)}, u32[]{:S(2)}) collective-permute-start(bf16[8,128,256]{2,1,0:T(8,128)(2,1)S(1)} %pad_maximum_fusion.2), channel_id=1, source_target_pairs={{0,4},{1,5},{2,6},{3,7},{4,0},{5,1},{6,2},{7,3},{8,12},{9,13},{10,... | collective-permute-start | bytes 1572872 | tf_op jit(solution)/shard_map/ppermute | solution.py:25
  37.0 2.3 %collective-permute-start.17 = (bf16[128,128]{1,0:T(8,128)(2,1)S(1)}, bf16[128,128]{1,0:T(8,128)(2,1)S(1)}, u32[]{:S(2)}, u32[]{:S(2)}) collective-permute-start(bf16[128,128]{1,0:T(8,128)(2,1)S(1)} %fusion.13), channel_id=1, source_target_pairs={{0,2},{1,3},{2,0},{3,1},{4,6},{5,7},{6,4},{7,5},{8,10},{9,11},{10,... | collective-permute-start | bytes 98312 | tf_op jit(solution)/shard_map/ppermute | solution.py:25
  39.3 6.1 %collective-permute-done.17 = bf16[128,128]{1,0:T(8,128)(2,1)S(1)} collective-permute-done((bf16[128,128]{1,0:T(8,128)(2,1)S(1)}, bf16[128,128]{1,0:T(8,128)(2,1)S(1)}, u32[]{:S(2)}, u32[]{:S(2)}) %collective-permute-start.17) | collective-permute-done | bytes 32800 | tf_op jit(solution)/shard_map/ppermute | solution.py:25
  47.1 0.7 pad_maximum_fusion.4
  47.8 0.9 reshape.16.refs_1_
  49.0 0.9 broadcast_select_fusion
  50.0 5.8 %copy-done.4 = bf16[16384,512]{1,0:T(8,128)(2,1)S(1)} copy-done((bf16[16384,512]{1,0:T(8,128)(2,1)S(1)}, bf16[16384,512]{1,0:T(8,128)(2,1)}, u32[]{:S(2)}) %copy-start.4) | copy-done | bytes 16777240
  55.8 5.1 %shard_map.64 = (f32[128,512]{1,0:T(8,128)S(1)}, f32[128,256]{1,0:T(8,128)S(1)}) custom-call(s32[32]{0:T(128)S(1)} %stack.390.refs_0_, f32[64,256]{1,0:T(8,128)S(1)} %reshape.16.refs_1_, bf16[4,128,512]{2,1,0:T(8,128)(2,1)S(1)} %pad_maximum_fusion.1.refs_2_, bf16[4,128,512]{2,1,0:T(8,128)(2,1)S(1)} %collective-permute-done.9.refs_3_, ...), custom_call_target="tpu_custom_call" | custom-call | flops 1073741824 | bytes 8388608 | tf_op jit(solution)/shard_map/pallas_call | solution.py:149
  60.9 5.8 %copy-done.5 = bf16[16384,512]{1,0:T(8,128)(2,1)S(1)} copy-done((bf16[16384,512]{1,0:T(8,128)(2,1)S(1)}, bf16[16384,512]{1,0:T(8,128)(2,1)}, u32[]{:S(2)}) %copy-start.5) | copy-done | bytes 16777240
  66.6 6.3 %shard_map.66.attended = bf16[128,512]{1,0:T(8,128)(2,1)S(1)} custom-call(s32[32]{0:T(128)S(1)} %stack.360.refs_0_, f32[64,256]{1,0:T(8,128)S(1)} %reshape.16.refs_1_, bf16[8,128,256]{2,1,0:T(8,128)(2,1)S(1)} %collective-permute-done.4.refs_2_, bf16[8,128,256]{2,1,0:T(8,128)(2,1)} %collective-permute-done.5.refs_3_, ...), custom_call_target="tpu_custom_call" | custom-call | flops 1073741824 | bytes 8388608 | tf_op jit(solution)/shard_map/pallas_call | solution.py:149
  72.9 5.8 %copy-done = bf16[512,16384]{1,0:T(8,128)(2,1)S(1)} copy-done((bf16[512,16384]{1,0:T(8,128)(2,1)S(1)}, bf16[512,16384]{1,0:T(8,128)(2,1)}, u32[]{:S(2)}) %copy-start) | copy-done | bytes 16777240
  78.7 5.8 %shard_map.69 = bf16[16,128,256]{2,1,0:T(8,128)(2,1)} custom-call(s32[16]{0:T(128)S(1)} %stack.403.table, bf16[128,512]{1,0:T(8,128)(2,1)S(1)} %shard_map.66.attended, bf16[512,16384]{1,0:T(8,128)(2,1)S(1)} %copy-done), custom_call_target="tpu_custom_call" | custom-call | flops 536870912 | bytes 4194304 | tf_op jit(solution)/shard_map/pallas_call | solution.py:196
  85.1 5.8 %copy-done.1 = bf16[512,16384]{1,0:T(8,128)(2,1)S(1)} copy-done((bf16[512,16384]{1,0:T(8,128)(2,1)S(1)}, bf16[512,16384]{1,0:T(8,128)(2,1)}, u32[]{:S(2)}) %copy-start.1) | copy-done | bytes 16777240
  90.8 4.8 %shard_map.67 = bf16[16,128,256]{2,1,0:T(8,128)(2,1)S(1)} custom-call(s32[16]{0:T(128)S(1)} %stack.401.table, bf16[128,512]{1,0:T(8,128)(2,1)S(1)} %shard_map.66.attended, bf16[512,16384]{1,0:T(8,128)(2,1)S(1)} %copy-done.1), custom_call_target="tpu_custom_call" | custom-call | flops 536870912 | bytes 4194304 | tf_op jit(solution)/shard_map/pallas_call | solution.py:196
  96.0 5.8 %copy-done.2 = bf16[512,16384]{1,0:T(8,128)(2,1)S(1)} copy-done((bf16[512,16384]{1,0:T(8,128)(2,1)S(1)}, bf16[512,16384]{1,0:T(8,128)(2,1)}, u32[]{:S(2)}) %copy-start.2) | copy-done | bytes 16777240
  101.7 5.9 %shard_map.70 = (bf16[8,128,256]{2,1,0:T(8,128)(2,1)}, bf16[8,128,256]{2,1,0:T(8,128)(2,1)}) custom-call(s32[16]{0:T(128)S(1)} %stack.402.table, bf16[128,512]{1,0:T(8,128)(2,1)S(1)} %shard_map.66.attended, bf16[16,128,256]{2,1,0:T(8,128)(2,1)S(1)} %collective-permute-done.20.refs_0_, bf16[512,16384]{1,0:T(8,128)(2,1)S(1)} %copy-done.2), custom_call_target="tpu_custom_call" | custom-call | flops 536870912 | bytes 4194304 | tf_op jit(solution)/shard_map/pallas_call | solution.py:196
  107.6 0.6 collective-permute-start.23
  108.2 1.4 collective-permute-start.21
  109.7 5.8 %copy-done.3 = bf16[512,16384]{1,0:T(8,128)(2,1)S(1)} copy-done((bf16[512,16384]{1,0:T(8,128)(2,1)S(1)}, bf16[512,16384]{1,0:T(8,128)(2,1)}, u32[]{:S(2)}) %copy-start.3) | copy-done | bytes 16777240
  115.5 4.8 %shard_map.68 = (f32[8,128,256]{2,1,0:T(8,128)S(1)}, f32[8,128,256]{2,1,0:T(8,128)S(1)}) custom-call(s32[16]{0:T(128)S(1)} %stack.335.table, bf16[128,512]{1,0:T(8,128)(2,1)S(1)} %shard_map.66.attended, bf16[16,128,256]{2,1,0:T(8,128)(2,1)S(1)} %collective-permute-done.19.refs_0_, bf16[512,16384]{1,0:T(8,128)(2,1)S(1)} %copy-done.3), custom_call_target="tpu_custom_call" | custom-call | flops 536870912 | bytes 4194304 | tf_op jit(solution)/shard_map/pallas_call | solution.py:196
  120.3 1.8 %collective-permute-done.23 = bf16[8,128,256]{2,1,0:T(8,128)(2,1)S(1)} collective-permute-done((bf16[8,128,256]{2,1,0:T(8,128)(2,1)}, bf16[8,128,256]{2,1,0:T(8,128)(2,1)S(1)}, u32[]{:S(2)}, u32[]{:S(2)}) %collective-permute-start.23) | collective-permute-done | bytes 524320 | tf_op jit(solution)/shard_map/ppermute | solution.py:25
  122.2 0.7 collective-permute-start.24
  122.9 1.4 collective-permute-start.22
  124.2 5.7 %collective-permute-done.24 = bf16[4,128,256]{2,1,0:T(8,128)(2,1)S(1)} collective-permute-done((bf16[4,128,256]{2,1,0:T(8,128)(2,1)S(1)}, bf16[4,128,256]{2,1,0:T(8,128)(2,1)S(1)}, u32[]{:S(2)}, u32[]{:S(2)}) %collective-permute-start.24) | collective-permute-done | bytes 262176 | tf_op jit(solution)/shard_map/ppermute | solution.py:25
  130.6 3.8 %collective-permute-start.25 = (bf16[128,512]{1,0:T(8,128)(2,1)S(1)}, bf16[128,512]{1,0:T(8,128)(2,1)S(1)}, u32[]{:S(2)}, u32[]{:S(2)}) collective-permute-start(bf16[128,512]{1,0:T(8,128)(2,1)S(1)} %get-tuple-element.23), channel_id=1, source_target_pairs={{0,8},{1,9},{2,10},{3,11},{4,12},{5,13},{6,14},{7,15},{8,0},{9,1},... | collective-permute-start | bytes 393224 | tf_op jit(solution)/shard_map/ppermute | solution.py:25
  134.4 1.1 collective-permute-start.26
  135.6 1.4 collective-permute-start.27
  137.0 1.8 %collective-permute-done.25 = bf16[128,512]{1,0:T(8,128)(2,1)S(1)} collective-permute-done((bf16[128,512]{1,0:T(8,128)(2,1)S(1)}, bf16[128,512]{1,0:T(8,128)(2,1)S(1)}, u32[]{:S(2)}, u32[]{:S(2)}) %collective-permute-start.25) | collective-permute-done | bytes 131104 | tf_op jit(solution)/shard_map/ppermute | solution.py:25
  138.8 7.0 %collective-permute-done.26 = bf16[128,512]{1,0:T(8,128)(2,1)S(1)} collective-permute-done((bf16[128,512]{1,0:T(8,128)(2,1)S(1)}, bf16[128,512]{1,0:T(8,128)(2,1)S(1)}, u32[]{:S(2)}, u32[]{:S(2)}) %collective-permute-start.26) | collective-permute-done | bytes 131104 | tf_op jit(solution)/shard_map/ppermute | solution.py:25
  145.8 0.7 fusion.6
  (67 shorter events, 4.3 us)
Async XLA Ops:
  0.8 1.2 copy-start.6
  2.1 1.2 copy-start.7
  3.3 0.9 copy-start.8
  5.5 16.2 %collective-permute-start.12 = (bf16[8,128,128]{2,1,0:T(8,128)(2,1)S(1)}, bf16[8,128,128]{2,1,0:T(8,128)(2,1)S(1)}, u32[]{:S(2)}, u32[]{:S(2)}) collective-permute-start(bf16[8,128,128]{2,1,0:T(8,128)(2,1)S(1)} %get-tuple-element.16), channel_id=1, source_target_pairs={{0,1},{1,0},{2,3},{3,2},{4,5},{5,4},{6,7},{7,6},{8,9},{9,8},{10,11... | collective-permute-start | bytes 786440 | tf_op jit(solution)/shard_map/ppermute | solution.py:25
  6.0 8.9 %collective-permute-start = (bf16[128,512]{1,0:T(8,128)(2,1)S(1)}, bf16[128,512]{1,0:T(8,128)(2,1)S(1)}, u32[]{:S(2)}, u32[]{:S(2)}) collective-permute-start(bf16[128,512]{1,0:T(8,128)(2,1)S(1)} %copy-done.8), channel_id=1, source_target_pairs={{0,8},{1,9},{2,10},{3,11},{4,12},{5,13},{6,14},{7,15},{8,0},{9,1},... | collective-permute-start | bytes 393224 | tf_op jit(solution)/shard_map/ppermute | solution.py:25
  8.7 12.9 %collective-permute-start.1 = (bf16[128,512]{1,0:T(8,128)(2,1)S(1)}, bf16[128,512]{1,0:T(8,128)(2,1)S(1)}, u32[]{:S(2)}, u32[]{:S(2)}) collective-permute-start(bf16[128,512]{1,0:T(8,128)(2,1)S(1)} %copy-done.8), channel_id=1, source_target_pairs={{0,16},{1,17},{2,18},{3,19},{4,20},{5,21},{6,22},{7,23},{8,24},{9,... | collective-permute-start | bytes 393224 | tf_op jit(solution)/shard_map/ppermute | solution.py:25
  11.3 10.3 %collective-permute-start.2 = (bf16[128,512]{1,0:T(8,128)(2,1)S(1)}, bf16[128,512]{1,0:T(8,128)(2,1)S(1)}, u32[]{:S(2)}, u32[]{:S(2)}) collective-permute-start(bf16[128,512]{1,0:T(8,128)(2,1)S(1)} %copy-done.8), channel_id=1, source_target_pairs={{0,24},{1,25},{2,26},{3,27},{4,28},{5,29},{6,30},{7,31},{8,16},{9,... | collective-permute-start | bytes 393224 | tf_op jit(solution)/shard_map/ppermute | solution.py:25
  21.8 6.1 %collective-permute-start.13 = (bf16[4,128,128]{2,1,0:T(8,128)(2,1)S(1)}, bf16[4,128,128]{2,1,0:T(8,128)(2,1)S(1)}, u32[]{:S(2)}, u32[]{:S(2)}) collective-permute-start(bf16[4,128,128]{2,1,0:T(8,128)(2,1)S(1)} %slice.149), channel_id=1, source_target_pairs={{0,4},{1,5},{2,6},{3,7},{4,0},{5,1},{6,2},{7,3},{8,12},{9,13},{10,... | collective-permute-start | bytes 393224 | tf_op jit(solution)/shard_map/ppermute | solution.py:25
  23.4 11.6 %collective-permute-start.3 = (bf16[4,128,256]{2,1,0:T(8,128)(2,1)S(1)}, bf16[4,128,256]{2,1,0:T(8,128)(2,1)S(1)}, u32[]{:S(2)}, u32[]{:S(2)}) collective-permute-start(bf16[4,128,256]{2,1,0:T(8,128)(2,1)S(1)} %get-tuple-element.27), channel_id=1, source_target_pairs={{0,2},{1,3},{2,0},{3,1},{4,6},{5,7},{6,4},{7,5},{8,10},{9,11},{10,... | collective-permute-start | bytes 786440 | tf_op jit(solution)/shard_map/ppermute | solution.py:25
  24.9 7.6 %collective-permute-start.6 = (bf16[4,128,256]{2,1,0:T(8,128)(2,1)S(1)}, bf16[4,128,256]{2,1,0:T(8,128)(2,1)S(1)}, u32[]{:S(2)}, u32[]{:S(2)}) collective-permute-start(bf16[4,128,256]{2,1,0:T(8,128)(2,1)S(1)} %get-tuple-element.26), channel_id=1, source_target_pairs={{0,4},{1,5},{2,6},{3,7},{4,0},{5,1},{6,2},{7,3},{8,12},{9,13},{10,... | collective-permute-start | bytes 786440 | tf_op jit(solution)/shard_map/ppermute | solution.py:25
  28.0 8.7 %collective-permute-start.14 = (bf16[128,128]{1,0:T(8,128)(2,1)S(1)}, bf16[128,128]{1,0:T(8,128)(2,1)S(1)}, u32[]{:S(2)}, u32[]{:S(2)}) collective-permute-start(bf16[128,128]{1,0:T(8,128)(2,1)S(1)} %get-tuple-element.30), channel_id=1, source_target_pairs={{0,8},{1,9},{2,10},{3,11},{4,12},{5,13},{6,14},{7,15},{8,0},{9,1},... | collective-permute-start | bytes 98312 | tf_op jit(solution)/shard_map/ppermute | solution.py:25
  30.0 6.7 %collective-permute-start.15 = (bf16[128,128]{1,0:T(8,128)(2,1)S(1)}, bf16[128,128]{1,0:T(8,128)(2,1)S(1)}, u32[]{:S(2)}, u32[]{:S(2)}) collective-permute-start(bf16[128,128]{1,0:T(8,128)(2,1)S(1)} %get-tuple-element.32), channel_id=1, source_target_pairs={{0,16},{1,17},{2,18},{3,19},{4,20},{5,21},{6,22},{7,23},{8,24},{9,... | collective-permute-start | bytes 98312 | tf_op jit(solution)/shard_map/ppermute | solution.py:25
  31.2 5.7 %collective-permute-start.16 = (bf16[128,128]{1,0:T(8,128)(2,1)S(1)}, bf16[128,128]{1,0:T(8,128)(2,1)S(1)}, u32[]{:S(2)}, u32[]{:S(2)}) collective-permute-start(bf16[128,128]{1,0:T(8,128)(2,1)S(1)} %get-tuple-element.31), channel_id=1, source_target_pairs={{0,24},{1,25},{2,26},{3,27},{4,28},{5,29},{6,30},{7,31},{8,16},{9,... | collective-permute-start | bytes 98312 | tf_op jit(solution)/shard_map/ppermute | solution.py:25
  32.6 13.0 %collective-permute-start.7 = (bf16[8,128,256]{2,1,0:T(8,128)(2,1)S(1)}, bf16[8,128,256]{2,1,0:T(8,128)(2,1)S(1)}, u32[]{:S(2)}, u32[]{:S(2)}) collective-permute-start(bf16[8,128,256]{2,1,0:T(8,128)(2,1)S(1)} %pad_maximum_fusion.3), channel_id=1, source_target_pairs={{0,2},{1,3},{2,0},{3,1},{4,6},{5,7},{6,4},{7,5},{8,10},{9,11},{10,... | collective-permute-start | bytes 1572872 | tf_op jit(solution)/shard_map/ppermute | solution.py:25
  35.1 11.0 %collective-permute-start.4 = (bf16[8,128,256]{2,1,0:T(8,128)(2,1)S(1)}, bf16[8,128,256]{2,1,0:T(8,128)(2,1)S(1)}, u32[]{:S(2)}, u32[]{:S(2)}) collective-permute-start(bf16[8,128,256]{2,1,0:T(8,128)(2,1)S(1)} %pad_maximum_fusion.2), channel_id=1, source_target_pairs={{0,4},{1,5},{2,6},{3,7},{4,0},{5,1},{6,2},{7,3},{8,12},{9,13},{10,... | collective-permute-start | bytes 1572872 | tf_op jit(solution)/shard_map/ppermute | solution.py:25
  37.0 8.4 %collective-permute-start.17 = (bf16[128,128]{1,0:T(8,128)(2,1)S(1)}, bf16[128,128]{1,0:T(8,128)(2,1)S(1)}, u32[]{:S(2)}, u32[]{:S(2)}) collective-permute-start(bf16[128,128]{1,0:T(8,128)(2,1)S(1)} %fusion.13), channel_id=1, source_target_pairs={{0,2},{1,3},{2,0},{3,1},{4,6},{5,7},{6,4},{7,5},{8,10},{9,11},{10,... | collective-permute-start | bytes 98312 | tf_op jit(solution)/shard_map/ppermute | solution.py:25
  39.3 10.7 %collective-permute-start.9 = (bf16[4,128,512]{2,1,0:T(8,128)(2,1)S(1)}, bf16[4,128,512]{2,1,0:T(8,128)(2,1)S(1)}, u32[]{:S(2)}, u32[]{:S(2)}) collective-permute-start(bf16[4,128,512]{2,1,0:T(8,128)(2,1)S(1)} %pad_maximum_fusion.1.refs_2_), channel_id=1, source_target_pairs={{0,1},{1,0},{2,3},{3,2},{4,5},{5,4},{6,7},{7,6},{8,9},{9,8},{10,11... | collective-permute-start | bytes 1572872 | tf_op jit(solution)/shard_map/ppermute | solution.py:25
  45.4 1.6 %copy-start.10 = (f32[128,128]{1,0:T(8,128)}, f32[128,128]{1,0:T(8,128)S(1)}, u32[]{:S(2)}) copy-start(f32[128,128]{1,0:T(8,128)S(1)} %convert_add_fusion.3) | copy-start | bytes 196612
  45.4 1.5 collective-permute-start.18
  45.5 15.3 %collective-permute-start.8 = (bf16[8,128,256]{2,1,0:T(8,128)(2,1)S(1)}, bf16[8,128,256]{2,1,0:T(8,128)(2,1)S(1)}, u32[]{:S(2)}, u32[]{:S(2)}) collective-permute-start(bf16[8,128,256]{2,1,0:T(8,128)(2,1)S(1)} %collective-permute-done.7.refs_4_), channel_id=1, source_target_pairs={{0,1},{1,0},{2,3},{3,2},{4,5},{5,4},{6,7},{7,6},{8,9},{9,8},{10,11... | collective-permute-start | bytes 1572872 | tf_op jit(solution)/shard_map/ppermute | solution.py:25
  46.0 14.8 %collective-permute-start.5 = (bf16[8,128,256]{2,1,0:T(8,128)(2,1)S(1)}, bf16[8,128,256]{2,1,0:T(8,128)(2,1)}, u32[]{:S(2)}, u32[]{:S(2)}) collective-permute-start(bf16[8,128,256]{2,1,0:T(8,128)(2,1)S(1)} %collective-permute-done.4.refs_2_), channel_id=1, source_target_pairs={{0,1},{1,0},{2,3},{3,2},{4,5},{5,4},{6,7},{7,6},{8,9},{9,8},{10,11... | collective-permute-start | bytes 1572872 | tf_op jit(solution)/shard_map/ppermute | solution.py:25
  46.4 3.6 %collective-permute-start.10 = (bf16[4,128,256]{2,1,0:T(8,128)(2,1)S(1)}, bf16[4,128,256]{2,1,0:T(8,128)(2,1)S(1)}, u32[]{:S(2)}, u32[]{:S(2)}) collective-permute-start(bf16[4,128,256]{2,1,0:T(8,128)(2,1)S(1)} %collective-permute-done.3.refs_4_), channel_id=1, source_target_pairs={{0,1},{1,0},{2,3},{3,2},{4,5},{5,4},{6,7},{7,6},{8,9},{9,8},{10,11... | collective-permute-start | bytes 786440 | tf_op jit(solution)/shard_map/ppermute | solution.py:25
  46.9 3.1 %collective-permute-start.11 = (bf16[4,128,256]{2,1,0:T(8,128)(2,1)S(1)}, bf16[4,128,256]{2,1,0:T(8,128)(2,1)}, u32[]{:S(2)}, u32[]{:S(2)}) collective-permute-start(bf16[4,128,256]{2,1,0:T(8,128)(2,1)S(1)} %collective-permute-done.6.refs_6_), channel_id=1, source_target_pairs={{0,1},{1,0},{2,3},{3,2},{4,5},{5,4},{6,7},{7,6},{8,9},{9,8},{10,11... | collective-permute-start | bytes 786440 | tf_op jit(solution)/shard_map/ppermute | solution.py:25
  49.0 11.8 %copy-start.9 = (f32[128,128]{1,0:T(8,128)S(1)}, f32[128,128]{1,0:T(8,128)}, u32[]{:S(2)}) copy-start(f32[128,128]{1,0:T(8,128)} %get-tuple-element.37.refs_12_) | copy-start | bytes 196612
  50.0 5.8 %copy-start.4 = (bf16[16384,512]{1,0:T(8,128)(2,1)S(1)}, bf16[16384,512]{1,0:T(8,128)(2,1)}, u32[]{:S(2)}) copy-start(bf16[16384,512]{1,0:T(8,128)(2,1)} %refs_6_.1) | copy-start | bytes 50331652
  60.9 5.8 %copy-start.5 = (bf16[16384,512]{1,0:T(8,128)(2,1)S(1)}, bf16[16384,512]{1,0:T(8,128)(2,1)}, u32[]{:S(2)}) copy-start(bf16[16384,512]{1,0:T(8,128)(2,1)} %refs_6_.1) | copy-start | bytes 50331652
  72.9 5.8 %copy-start = (bf16[512,16384]{1,0:T(8,128)(2,1)S(1)}, bf16[512,16384]{1,0:T(8,128)(2,1)}, u32[]{:S(2)}) copy-start(bf16[512,16384]{1,0:T(8,128)(2,1)} %refs_1_.3) | copy-start | bytes 50331652
  84.5 11.4 %collective-permute-start.20 = (bf16[16,128,256]{2,1,0:T(8,128)(2,1)}, bf16[16,128,256]{2,1,0:T(8,128)(2,1)S(1)}, u32[]{:S(2)}, u32[]{:S(2)}) collective-permute-start(bf16[16,128,256]{2,1,0:T(8,128)(2,1)} %shard_map.69), channel_id=1, source_target_pairs={{0,1},{1,0},{2,3},{3,2},{4,5},{5,4},{6,7},{7,6},{8,9},{9,8},{10,11... | collective-permute-start | bytes 3145736 | tf_op jit(solution)/shard_map/ppermute | solution.py:25
  85.0 5.8 %copy-start.1 = (bf16[512,16384]{1,0:T(8,128)(2,1)S(1)}, bf16[512,16384]{1,0:T(8,128)(2,1)}, u32[]{:S(2)}) copy-start(bf16[512,16384]{1,0:T(8,128)(2,1)} %refs_1_.3) | copy-start | bytes 50331652
  95.7 14.0 %collective-permute-start.19 = (bf16[16,128,256]{2,1,0:T(8,128)(2,1)S(1)}, bf16[16,128,256]{2,1,0:T(8,128)(2,1)S(1)}, u32[]{:S(2)}, u32[]{:S(2)}) collective-permute-start(bf16[16,128,256]{2,1,0:T(8,128)(2,1)S(1)} %shard_map.67), channel_id=1, source_target_pairs={{0,1},{1,0},{2,3},{3,2},{4,5},{5,4},{6,7},{7,6},{8,9},{9,8},{10,11... | collective-permute-start | bytes 3145736 | tf_op jit(solution)/shard_map/ppermute | solution.py:25
  96.0 5.8 %copy-start.2 = (bf16[512,16384]{1,0:T(8,128)(2,1)S(1)}, bf16[512,16384]{1,0:T(8,128)(2,1)}, u32[]{:S(2)}) copy-start(bf16[512,16384]{1,0:T(8,128)(2,1)} %refs_1_.3) | copy-start | bytes 50331652
  107.6 14.5 %collective-permute-start.23 = (bf16[8,128,256]{2,1,0:T(8,128)(2,1)}, bf16[8,128,256]{2,1,0:T(8,128)(2,1)S(1)}, u32[]{:S(2)}, u32[]{:S(2)}) collective-permute-start(bf16[8,128,256]{2,1,0:T(8,128)(2,1)} %get-tuple-element.20), channel_id=1, source_target_pairs={{0,4},{1,5},{2,6},{3,7},{4,0},{5,1},{6,2},{7,3},{8,12},{9,13},{10,... | collective-permute-start | bytes 1572872 | tf_op jit(solution)/shard_map/ppermute | solution.py:25
  108.2 14.6 %collective-permute-start.21 = (bf16[8,128,256]{2,1,0:T(8,128)(2,1)}, bf16[8,128,256]{2,1,0:T(8,128)(2,1)S(1)}, u32[]{:S(2)}, u32[]{:S(2)}) collective-permute-start(bf16[8,128,256]{2,1,0:T(8,128)(2,1)} %get-tuple-element.18), channel_id=1, source_target_pairs={{0,2},{1,3},{2,0},{3,1},{4,6},{5,7},{6,4},{7,5},{8,10},{9,11},{10,... | collective-permute-start | bytes 1572872 | tf_op jit(solution)/shard_map/ppermute | solution.py:25
  109.7 5.8 %copy-start.3 = (bf16[512,16384]{1,0:T(8,128)(2,1)S(1)}, bf16[512,16384]{1,0:T(8,128)(2,1)}, u32[]{:S(2)}) copy-start(bf16[512,16384]{1,0:T(8,128)(2,1)} %refs_1_.3) | copy-start | bytes 50331652
  122.2 7.8 %collective-permute-start.24 = (bf16[4,128,256]{2,1,0:T(8,128)(2,1)S(1)}, bf16[4,128,256]{2,1,0:T(8,128)(2,1)S(1)}, u32[]{:S(2)}, u32[]{:S(2)}) collective-permute-start(bf16[4,128,256]{2,1,0:T(8,128)(2,1)S(1)} %add_convert_fusion), channel_id=1, source_target_pairs={{0,2},{1,3},{2,0},{3,1},{4,6},{5,7},{6,4},{7,5},{8,10},{9,11},{10,... | collective-permute-start | bytes 786440 | tf_op jit(solution)/shard_map/ppermute | solution.py:25
  122.9 7.5 %collective-permute-start.22 = (bf16[4,128,256]{2,1,0:T(8,128)(2,1)S(1)}, bf16[4,128,256]{2,1,0:T(8,128)(2,1)S(1)}, u32[]{:S(2)}, u32[]{:S(2)}) collective-permute-start(bf16[4,128,256]{2,1,0:T(8,128)(2,1)S(1)} %add_convert_fusion.1), channel_id=1, source_target_pairs={{0,4},{1,5},{2,6},{3,7},{4,0},{5,1},{6,2},{7,3},{8,12},{9,13},{10,... | collective-permute-start | bytes 786440 | tf_op jit(solution)/shard_map/ppermute | solution.py:25
  130.6 8.2 %collective-permute-start.25 = (bf16[128,512]{1,0:T(8,128)(2,1)S(1)}, bf16[128,512]{1,0:T(8,128)(2,1)S(1)}, u32[]{:S(2)}, u32[]{:S(2)}) collective-permute-start(bf16[128,512]{1,0:T(8,128)(2,1)S(1)} %get-tuple-element.23), channel_id=1, source_target_pairs={{0,8},{1,9},{2,10},{3,11},{4,12},{5,13},{6,14},{7,15},{8,0},{9,1},... | collective-permute-start | bytes 393224 | tf_op jit(solution)/shard_map/ppermute | solution.py:25
  134.4 11.4 %collective-permute-start.26 = (bf16[128,512]{1,0:T(8,128)(2,1)S(1)}, bf16[128,512]{1,0:T(8,128)(2,1)S(1)}, u32[]{:S(2)}, u32[]{:S(2)}) collective-permute-start(bf16[128,512]{1,0:T(8,128)(2,1)S(1)} %get-tuple-element.25), channel_id=1, source_target_pairs={{0,16},{1,17},{2,18},{3,19},{4,20},{5,21},{6,22},{7,23},{8,24},{9,... | collective-permute-start | bytes 393224 | tf_op jit(solution)/shard_map/ppermute | solution.py:25
  135.6 10.2 %collective-permute-start.27 = (bf16[128,512]{1,0:T(8,128)(2,1)S(1)}, bf16[128,512]{1,0:T(8,128)(2,1)S(1)}, u32[]{:S(2)}, u32[]{:S(2)}) collective-permute-start(bf16[128,512]{1,0:T(8,128)(2,1)S(1)} %get-tuple-element.24), channel_id=1, source_target_pairs={{0,24},{1,25},{2,26},{3,27},{4,28},{5,29},{6,30},{7,31},{8,16},{9,... | collective-permute-start | bytes 393224 | tf_op jit(solution)/shard_map/ppermute | solution.py:25

commit v2 on v0

v2 whole, which is shorter than its diff:
```python
import functools

import jax
import jax.numpy as jnp
from jax import lax
from jax.experimental import pallas as pl
from jax.experimental.pallas import tpu as pltpu
from jax.sharding import PartitionSpec as P

HEADS = 128
KVH = 8
HEAD = 128
LANE = 128
EPS = 1e-05
MIB = 1 << 20
CORE = 1


def combos(bits):
    out = [0]
    for b in bits:
        out = out + [o ^ b for o in out]
    return out


def vmem():
    return pl.BlockSpec(memory_space=pltpu.VMEM)


def smem():
    return pl.BlockSpec(memory_space=pltpu.SMEM)


def hbm():
    return pl.BlockSpec(memory_space=pltpu.HBM)


def dot(a, b):
    return jnp.dot(a, b, preferred_element_type=jnp.float32)


def kv_kernel(shared, where, act, gain, wk, wv, send, keep):
    me = where[0]
    width = act.shape[1]
    own = gain[:, pl.ds(pl.multiple_of(me * width, LANE), width)]
    scaled = (act[...].astype(jnp.float32) * own).astype(jnp.bfloat16)
    k, v = dot(scaled, wk[...]), dot(scaled, wv[...])
    core0 = (me & CORE) == 0
    for h in range(KVH):
        off = h ^ (me >> shared)
        spot = ((off & 1) ^ 1) * (KVH // 2) + (off >> 1)
        kh, vh = k[:, h * HEAD : (h + 1) * HEAD], v[:, h * HEAD : (h + 1) * HEAD]
        keep[spot] = jnp.where(core0, kh, vh)
        send[spot] = jnp.where(core0, vh, kh)


def kv_terms(shared, where, act, gain, wk, wv):
    tokens = act.shape[0]
    return pl.pallas_call(
        functools.partial(kv_kernel, shared),
        out_shape=[jax.ShapeDtypeStruct((KVH, tokens, HEAD), jnp.float32)] * 2,
        in_specs=[smem(), vmem(), vmem(), vmem(), vmem()],
        out_specs=[vmem(), vmem()],
        compiler_params=pltpu.CompilerParams(vmem_limit_bytes=24 * MIB),
        cost_estimate=pl.CostEstimate(
            flops=4 * tokens * wk.size, bytes_accessed=4 * wk.size, transcendentals=0
        ),
    )(where, act, gain, wk, wv)


def attend(queries, k_sum, v_sum, cosine, sine, scale):
    k_rows = (k_sum * scale).astype(jnp.bfloat16).astype(jnp.float32)
    value = (v_sum * scale).astype(jnp.bfloat16)

    def rotate(x):
        half = HEAD // 2
        turned = jnp.concatenate([x[:, half:], x[:, :half]], axis=1)
        return (x * cosine + turned * sine).astype(jnp.bfloat16)

    key = rotate(k_rows)
    tokens = key.shape[0]
    rows = lax.broadcasted_iota(jnp.int32, (tokens, tokens), 0)
    cols = lax.broadcasted_iota(jnp.int32, (tokens, tokens), 1)
    out = []
    for h in range(queries.shape[1] // HEAD):
        q = rotate(queries[:, h * HEAD : (h + 1) * HEAD] * scale)
        scores = lax.dot_general(
            q, key, (((1,), (1,)), ((), ())), preferred_element_type=jnp.float32
        ) * HEAD ** (-0.5)
        scores = jnp.where(rows >= cols, scores, -1e30)
        weights = jnp.exp(scores - jnp.max(scores, axis=1, keepdims=True))
        probs = (weights / jnp.sum(weights, axis=1, keepdims=True)).astype(jnp.bfloat16)
        out.append(dot(probs, value).astype(jnp.bfloat16))
    return jnp.concatenate(out, axis=1)


def query_kernel(places, width, carried, last, *refs):
    refs = list(refs)
    where, gain = refs.pop(0), refs.pop(0)
    pieces = [refs.pop(0) for _ in places]
    weight = refs.pop(0)
    queries = refs.pop(0)[...] if carried else None
    squares = refs.pop(0)[...] if carried else None
    extra = [refs.pop(0) for _ in range(4)] if last else None
    outs = [refs.pop(0) for _ in range(1 if last else 2)]
    sems = refs.pop()
    bufs = refs

    fetches, starts, i = [], [], 0
    for piece, (symbols, first), buf in zip(pieces, places, bufs):
        depth = piece.shape[2]
        mine = []
        for block, (const, pick) in enumerate(symbols):
            start = pl.multiple_of((where[pick] ^ const) * width + first, LANE)
            copy = pltpu.make_async_copy(
                weight.at[pl.ds(start, depth), :],
                buf.at[pl.ds(block * depth, depth), :],
                sems.at[i],
            )
            copy.start()
            mine.append((start, copy))
            i += 1
        fetches.append(mine)
    for piece, mine, buf in zip(pieces, fetches, bufs):
        depth = piece.shape[2]
        scaled = []
        for block, (start, _) in enumerate(mine):
            x = piece[block].astype(jnp.float32)
            scaled.append((x * gain[:, pl.ds(start, depth)]).astype(jnp.bfloat16))
            for c in range(0, depth, LANE):
                square = x[:, c : c + LANE] * x[:, c : c + LANE]
                squares = square if squares is None else squares + square
        for _, copy in mine:
            copy.wait()
        term = dot(jnp.concatenate(scaled, axis=1), buf[...])
        queries = term if queries is None else queries + term
    if last:
        mean = jnp.sum(squares, axis=1, keepdims=True) * (1.0 / weight.shape[0])
        mine, other, cosine, sine = extra
        core0 = (where[0] & CORE) == 0
        k_sum = jnp.where(core0, mine[...], other[...])
        v_sum = jnp.where(core0, other[...], mine[...])
        outs[0][...] = attend(
            queries, k_sum, v_sum, cosine[...], sine[...], lax.rsqrt(mean + EPS)
        )
    else:
        outs[0][...] = queries
        outs[1][...] = squares


def query_call(where, gain, pieces, weight, width, carry=(), extra=()):
    arrays = [a for a, _, _ in pieces]
    places = [(symbols, first) for _, symbols, first in pieces]
    tokens, columns = arrays[0].shape[1], weight.shape[1]
    if extra:
        out_shape = [jax.ShapeDtypeStruct((tokens, columns), jnp.bfloat16)]
    else:
        out_shape = [
            jax.ShapeDtypeStruct((tokens, columns), jnp.float32),
            jax.ShapeDtypeStruct((tokens, LANE), jnp.float32),
        ]
    rows = [a.shape[0] * a.shape[2] for a in arrays]
    return pl.pallas_call(
        functools.partial(query_kernel, places, width, bool(carry), bool(extra)),
        out_shape=out_shape,
        in_specs=[smem(), vmem()]
        + [vmem()] * len(arrays)
        + [hbm()]
        + [vmem()] * (len(carry) + len(extra)),
        out_specs=[vmem()] * len(out_shape),
        scratch_shapes=[pltpu.VMEM((r, columns), weight.dtype) for r in rows]
        + [pltpu.SemaphoreType.DMA((sum(a.shape[0] for a in arrays),))],
        compiler_params=pltpu.CompilerParams(vmem_limit_bytes=50 * MIB),
        cost_estimate=pl.CostEstimate(
            flops=2 * tokens * columns * sum(rows),
            bytes_accessed=2 * columns * sum(rows),
            transcendentals=0,
        ),
    )(where, gain, *arrays, weight, *carry, *extra)


def output_kernel(groups, width, where, attended, *refs):
    refs = list(refs)
    added = [refs.pop(0) if g[3] else None for g in groups]
    weight = refs.pop(0)
    outs = [refs.pop(0) for _ in groups]
    sems = refs.pop()
    fetches, i = [], 0
    for (symbols, first, size, _), buf in zip(groups, refs):
        mine = []
        for block, (const, pick) in enumerate(symbols):
            start = pl.multiple_of((where[pick] ^ const) * width + first, LANE)
            copy = pltpu.make_async_copy(
                weight.at[:, pl.ds(start, size)],
                buf.at[:, pl.ds(block * size, size)],
                sems.at[i],
            )
            copy.start()
            mine.append(copy)
            i += 1
        fetches.append(mine)
    left = attended[...]
    for (symbols, _, size, _), arrived, out, mine, buf in zip(groups, added, outs, fetches, refs):
        for copy in mine:
            copy.wait()
        terms = dot(left, buf[...])
        for block in range(len(symbols)):
            term = terms[:, block * size : (block + 1) * size]
            if arrived is not None:
                term = term + arrived[block].astype(jnp.float32)
            out[block] = term.astype(out.dtype)


def output_call(where, attended, weight, width, groups):
    tokens, depth = attended.shape
    columns = [len(symbols) * size for symbols, _, size, _, _ in groups]
    added = [g[4] for g in groups if g[4] is not None]
    return pl.pallas_call(
        functools.partial(
            output_kernel, [(s, f, c, a is not None) for s, f, c, _, a in groups], width
        ),
        out_shape=[
            jax.ShapeDtypeStruct((len(s), tokens, c), dtype) for s, _, c, dtype, _ in groups
        ],
        in_specs=[smem(), vmem()] + [vmem()] * len(added) + [hbm()],
        out_specs=[vmem()] * len(groups),
        scratch_shapes=[pltpu.VMEM((depth, c), weight.dtype) for c in columns]
        + [pltpu.SemaphoreType.DMA((sum(len(g[0]) for g in groups),))],
        compiler_params=pltpu.CompilerParams(vmem_limit_bytes=50 * MIB),
        cost_estimate=pl.CostEstimate(
            flops=2 * tokens * depth * sum(columns),
            bytes_accessed=2 * depth * sum(columns),
            transcendentals=0,
        ),
    )(where, attended, *added, weight)


def rotary_tables(tokens):
    half = HEAD // 2
    frequency = 500000.0 ** (-(jnp.arange(half, dtype=jnp.float32) * 2.0) / HEAD)
    angles = jnp.arange(tokens, dtype=jnp.float32)[:, None] * frequency[None, :]
    cosine, sine = jnp.cos(angles), jnp.sin(angles)
    return jnp.concatenate([cosine, cosine], axis=1), jnp.concatenate([-sine, sine], axis=1)


def per_device(n, act, norm_gain, wq, wk, wv, wo):
    tokens, width = act.shape
    me = lax.axis_index("wide")
    bits = [1 << i for i in range(n.bit_length() - 1)]
    side = (bits[1], bits[2])
    diagonal = bits[1] ^ bits[2]
    far = combos(bits[3:])
    f = len(far)
    late = LANE if width >= 4 * LANE else 0
    early = width - late
    f32, bf16 = jnp.float32, jnp.bfloat16

    def swap(x, offset):
        return lax.ppermute(x, "wide", [(i, i ^ offset) for i in range(n)])

    def turn(x, step):
        return lax.ppermute(x, "wide", [(i, i ^ side[(step + (i & CORE)) % 2]) for i in range(n)])

    bit = jnp.where((me & CORE) == 0, side[0], side[1])
    where = jnp.stack([me, me ^ bit, me ^ bit ^ diagonal]).astype(jnp.int32)
    gain = norm_gain.reshape(1, -1)

    def plain(offsets, pick=0):
        return [(o, pick) for o in offsets]

    def across(symbols):
        return [(const ^ CORE, (0, 2, 1)[pick]) for const, pick in symbols]

    square = [(0, 0), (0, 1), (0, 2), (diagonal, 0)]

    def shift(symbols, offset):
        return [(const ^ offset, pick) for const, pick in symbols]

    mine = act[:, :early]
    got = [swap(mine, o) for o in far[1:]]
    row = jnp.stack([mine] + got)
    if late:
        own = act[:, early:]
        one, two = turn(own, 0), turn(own, 1)
        plane = jnp.stack([own, one, two, turn(one, 1)])
        planes = [swap(plane, o) for o in far[1:]]
    side_1, side_2 = turn(row, 0), turn(row, 1)
    corner = turn(side_1, 1)

    shared = (n // KVH).bit_length() - 1
    act_kv = lax.optimization_barrier((act, got[0]))[0]
    others = combos(bits[shared + 1 :])
    kv_send, kv_keep = kv_terms(shared, where, act_kv, gain, wk, wv)
    kv = kv_keep + swap(kv_send, CORE)
    half = KVH // 2
    kv = kv[half:] + swap(kv[:half].astype(bf16), bits[shared]).astype(f32)
    total = kv[0]
    for i, o in enumerate(others):
        if o:
            total = total + swap(kv[i].astype(bf16), o).astype(f32)
    kv_mine, kv_other = total, None
    for o in combos(bits[:shared])[1:]:
        got = swap(total, o)
        if o & CORE:
            kv_other = got if kv_other is None else kv_other + got
        else:
            kv_mine = kv_mine + got

    def pair(array, symbols, first):
        return [(array, symbols, first)], [(swap(array, CORE), across(symbols), first)]

    row_own, row_other = pair(row, plain(far), 0)
    one_own, one_other = pair(side_1, plain(far, 1), 0)
    two_own, two_other = pair(side_2, plain(far, 2), 0)
    plane_own, plane_other, planes_own, planes_other = [], [], [], []
    if late:
        plane_own, plane_other = pair(plane, square, early)
    call = functools.partial(query_call, where, gain, weight=wq, width=width)
    carry = call(row_own + row_other)
    carry = call(one_own + two_own + plane_own + plane_other, carry=carry)
    corner, *carry = lax.optimization_barrier((corner, *carry))
    corner_own, corner_other = pair(corner, plain([o ^ diagonal for o in far]), 0)
    if late:
        for o, array in zip(far[1:], planes):
            a, b = pair(array, shift(square, o), early)
            planes_own += a
            planes_other += b
    carry = call(one_other + two_other + corner_own, carry=carry)
    (attended,) = call(
        corner_other + planes_own + planes_other,
        carry=carry,
        extra=(kv_mine, kv_other, *rotary_tables(tokens)),
    )

    at_corner = plain([o ^ diagonal for o in far])
    at_one, at_two, at_home = plain(far, 1), plain(far, 2), plain(far)
    leave = [(at_corner, 0, early, bf16)]
    stay = [
        (at_two, 0, early, f32),
        (at_one, 0, early, bf16),
        (at_home, 0, early, f32),
    ]
    if late:
        leave += [(shift(square, o), early, late, bf16) for o in far[1:]]
        stay += [(square, early, late, f32)]

    def project(left, groups, arrived=None):
        if arrived is None:
            groups = [(across(s), first, c, bf16, None) for s, first, c, _ in groups]
        else:
            groups = [(*g, a) for g, a in zip(groups, arrived)]
        return output_call(where, left, wo, width, groups)

    send_1 = project(attended, leave)
    attended, *send_1 = lax.optimization_barrier((attended, *send_1))
    send_2 = project(attended, stay)
    leaving = project(attended, leave, [swap(x, CORE) for x in send_1])
    from_corner = turn(leaving[0], 0)
    from_planes = [swap(x, o) for x, o in zip(leaving[1:], far[1:])]
    staying = project(attended, stay, [swap(x, CORE) for x in send_2])
    two, one, home = staying[:3]
    got_1 = turn(one, 0)
    got_2 = turn((two + from_corner.astype(f32)).astype(bf16), 1)
    home = home + got_1.astype(f32) + got_2.astype(f32)
    out = home[0]
    for i in range(1, f):
        out = out + swap(home[i].astype(bf16), far[i]).astype(f32)
    if late:
        plane = staying[3]
        for x in from_planes:
            plane = plane + x.astype(f32)
        got = turn(plane[3].astype(bf16), 0)
        got_1 = turn(plane[1].astype(bf16), 0)
        got_2 = turn((plane[2] + got.astype(f32)).astype(bf16), 1)
        rest = plane[0] + got_1.astype(f32) + got_2.astype(f32)
        out = jnp.concatenate([out, rest], axis=1)
    return out.astype(bf16)


def solution(mesh):
    return jax.shard_map(
        functools.partial(per_device, mesh.shape["wide"]),
        mesh=mesh,
        in_specs=(
            P("groups", "wide"),
            P(),
            P(None, "wide"),
            P("wide", None),
            P("wide", None),
            P("wide", None),
        ),
        out_specs=P("groups", "wide"),
        check_vma=False,
    )
```

time: 312 us -> 127 us (0.41)
  waiting for transfers between devices: 217 us -> 39.4 us
  starting transfers between devices: 0.04 us -> 50.8 us
  blocking collectives: 50.1 us -> 0 us
  Pallas kernels: 0 us -> 28.7 us
  matrix products: 21.3 us -> 0 us
  between operations: 13.6 us -> 0.32 us
  other arithmetic: 8.78 us -> 1.73 us
  local copies, waits for them, and re-layouts: 0.69 us -> 6.01 us
    reduce_scatter x1 -> x0, waiting for transfers between devices: 147 us -> none  [per_device(): lax.psum_scatter(partial_value, 'wide', scatter_dimension=1, tiled=True)]
    all_gather x1 -> x0, waiting for transfers between devices: 69.4 us -> none  [per_device(): lax.all_gather(activations, 'wide', axis=1, tiled=True).astype(jnp.float32)]
    ppermute x0 -> x48, starting transfers between devices: none -> 50.8 us  [the longest x36 36.3 us: swap(): return lax.ppermute(x, 'wide', [(i, i ^ offset) for i in range(n)])]
    psum x1 -> x0, blocking collectives: 50.1 us -> none  [per_device(): kv_rows = lax.psum(kv_term, 'wide').astype(jnp.bfloat16)]
    ppermute x0 -> x48, waiting for transfers between devices: none -> 39.4 us  [the longest x36 29.9 us: swap(): return lax.ppermute(x, 'wide', [(i, i ^ offset) for i in range(n)])]
    pallas_call x0 -> x9, Pallas kernels: none -> 28.7 us  [the longest x4 14.1 us: query_call(): pl.pallas_call(functools.partial(query_kernel, places, width, bool(carry)...]
    dot_general x5 -> x0, matrix products: 20.9 us -> none  [the longest x1 11.5 us: per_device(): jnp.dot(attended, output_weight, preferred_element_type=jnp.float32)]
    convert_element_type x3 -> x2, other arithmetic: 5.06 us -> 0.13 us  [the longest x1 0.12 us: per_device(): got_2 = turn((two + from_corner.astype(f32)).astype(bf16), 1)]
  transfers between devices with their start and end apart: 2 -> 48, of which waited for: 2 -> 14; matrix products, arithmetic and copies ran while one was open for 0% -> 1% of each run, Pallas kernels for 0% -> 16%
where the time goes in v2:
time: 127 us
  starting transfers between devices  50.8 us (40%)
  waiting for transfers between devices  39.4 us (31%)
  Pallas kernels  28.7 us (23%)
  local copies, waits for them, and re-layouts  6.01 us (5%)
  other arithmetic  1.73 us (1%)
    ppermute x36, starting transfers between devices, swap(): return lax.ppermute(x, 'wide', [(i, i ^ offset) for i in range(n)])  36.3 us
    ppermute x36, waiting for transfers between devices, swap(): return lax.ppermute(x, 'wide', [(i, i ^ offset) for i in range(n)])  29.9 us
    ppermute x12, starting transfers between devices, turn(): lax.ppermute(x, 'wide', [(i, i ^ side[(step + (i & CORE)) % 2]) for i in...  14.5 us
    pallas_call x4, Pallas kernels, query_call(): pl.pallas_call(functools.partial(query_kernel, places, width, bool(carry)...  14.1 us
    pallas_call x4, Pallas kernels, output_call(): pl.pallas_call(functools.partial(output_kernel, [(s, f, c, a is not None)...  13.6 us
    ppermute x12, waiting for transfers between devices, turn(): lax.ppermute(x, 'wide', [(i, i ^ side[(step + (i & CORE)) % 2]) for i in...  9.5 us
    unnamed x10, local copies, waits for them, and re-layouts  5.03 us
  transfers between devices with their start and end apart: 48, of which 14 were waited for; matrix products, arithmetic and copies ran while one was open for 1% of the time, Pallas kernels for 16%

profile of v2, /device:TPU:0, one launch (start us, length us, event | category | flops | bytes accessed | tf_op | source)
XLA Modules:
  0.0 127.0 jit_solution(1241953858606954711)
XLA Ops:
  0.0 0.9 slice_bitcast_fusion.13
  0.9 3.1 %collective-permute-start = (bf16[128,384]{1,0:T(8,128)(2,1)S(1)}, bf16[128,384]{1,0:T(8,128)(2,1)S(1)}, u32[]{:S(2)}, u32[]{:S(2)}) collective-permute-start(bf16[128,384]{1,0:T(8,128)(2,1)S(1)} %get-tuple-element.88), channel_id=1, source_target_pairs={{0,8},{1,9},{2,10},{3,11},{4,12},{5,13},{6,14},{7,15},{8,0},{9,1},... | collective-permute-start | bytes 294920 | tf_op jit(solution)/shard_map/ppermute | solution.py:259
  4.1 2.7 %collective-permute-done = bf16[128,384]{1,0:T(8,128)(2,1)S(1)} collective-permute-done((bf16[128,384]{1,0:T(8,128)(2,1)S(1)}, bf16[128,384]{1,0:T(8,128)(2,1)S(1)}, u32[]{:S(2)}, u32[]{:S(2)}) %collective-permute-start) | collective-permute-done | bytes 98336 | tf_op jit(solution)/shard_map/ppermute | solution.py:259
  6.8 0.8 copy-done
  7.6 1.2 copy-done.2
  8.9 1.2 copy-done.3
  10.1 0.9 copy-done.4
  11.0 1.0 shard_map.67
  12.1 2.9 %collective-permute-start.1 = (bf16[128,384]{1,0:T(8,128)(2,1)S(1)}, bf16[128,384]{1,0:T(8,128)(2,1)S(1)}, u32[]{:S(2)}, u32[]{:S(2)}) collective-permute-start(bf16[128,384]{1,0:T(8,128)(2,1)S(1)} %get-tuple-element.88), channel_id=1, source_target_pairs={{0,16},{1,17},{2,18},{3,19},{4,20},{5,21},{6,22},{7,23},{8,24},{9,... | collective-permute-start | bytes 294920 | tf_op jit(solution)/shard_map/ppermute | solution.py:259
  15.0 1.3 %collective-permute-start.2 = (bf16[128,384]{1,0:T(8,128)(2,1)S(1)}, bf16[128,384]{1,0:T(8,128)(2,1)S(1)}, u32[]{:S(2)}, u32[]{:S(2)}) collective-permute-start(bf16[128,384]{1,0:T(8,128)(2,1)S(1)} %get-tuple-element.88), channel_id=1, source_target_pairs={{0,24},{1,25},{2,26},{3,27},{4,28},{5,29},{6,30},{7,31},{8,16},{9,... | collective-permute-start | bytes 294920 | tf_op jit(solution)/shard_map/ppermute | solution.py:259
  16.3 6.6 %collective-permute-done.1 = bf16[128,384]{1,0:T(8,128)(2,1)S(1)} collective-permute-done((bf16[128,384]{1,0:T(8,128)(2,1)S(1)}, bf16[128,384]{1,0:T(8,128)(2,1)S(1)}, u32[]{:S(2)}, u32[]{:S(2)}) %collective-permute-start.1) | collective-permute-done | bytes 98336 | tf_op jit(solution)/shard_map/ppermute | solution.py:259
  23.0 1.7 %collective-permute-start.3 = (bf16[4,128,384]{2,1,0:T(8,128)(2,1)S(1)}, bf16[4,128,384]{2,1,0:T(8,128)(2,1)S(1)}, u32[]{:S(2)}, u32[]{:S(2)}) collective-permute-start(bf16[4,128,384]{2,1,0:T(8,128)(2,1)S(1)} %pad_maximum_fusion.refs_2_), channel_id=1, source_target_pairs={{0,2},{1,5},{2,0},{3,7},{4,6},{5,1},{6,4},{7,3},{8,10},{9,13},{10,... | collective-permute-start | bytes 1179656 | tf_op jit(solution)/shard_map/ppermute | solution.py:262
  25.1 1.7 %collective-permute-start.7 = (bf16[128,128]{1,0:T(8,128)(2,1)S(1)}, bf16[128,128]{1,0:T(8,128)(2,1)S(1)}, u32[]{:S(2)}, u32[]{:S(2)}) collective-permute-start(bf16[128,128]{1,0:T(8,128)(2,1)S(1)} %get-tuple-element.86), channel_id=1, source_target_pairs={{0,4},{1,3},{2,6},{3,1},{4,0},{5,7},{6,2},{7,5},{8,12},{9,11},{10,... | collective-permute-start | bytes 98312 | tf_op jit(solution)/shard_map/ppermute | solution.py:262
  26.8 4.7 %collective-permute-done.6 = bf16[128,128]{1,0:T(8,128)(2,1)S(1)} collective-permute-done((bf16[128,128]{1,0:T(8,128)(2,1)S(1)}, bf16[128,128]{1,0:T(8,128)(2,1)S(1)}, u32[]{:S(2)}, u32[]{:S(2)}) %collective-permute-start.6) | collective-permute-done | bytes 32800 | tf_op jit(solution)/shard_map/ppermute | solution.py:262
  31.5 1.5 %collective-permute-start.8 = (bf16[128,128]{1,0:T(8,128)(2,1)S(1)}, bf16[128,128]{1,0:T(8,128)(2,1)S(1)}, u32[]{:S(2)}, u32[]{:S(2)}) collective-permute-start(bf16[128,128]{1,0:T(8,128)(2,1)S(1)} %collective-permute-done.6), channel_id=1, source_target_pairs={{0,4},{1,3},{2,6},{3,1},{4,0},{5,7},{6,2},{7,5},{8,12},{9,11},{10,... | collective-permute-start | bytes 98312 | tf_op jit(solution)/shard_map/ppermute | solution.py:262
  33.7 2.1 %collective-permute-done.8 = bf16[128,128]{1,0:T(8,128)(2,1)S(1)} collective-permute-done((bf16[128,128]{1,0:T(8,128)(2,1)S(1)}, bf16[128,128]{1,0:T(8,128)(2,1)S(1)}, u32[]{:S(2)}, u32[]{:S(2)}) %collective-permute-start.8) | collective-permute-done | bytes 32800 | tf_op jit(solution)/shard_map/ppermute | solution.py:262
  35.8 3.3 %collective-permute-start.14 = (bf16[4,128,128]{2,1,0:T(8,128)(2,1)S(1)}, bf16[4,128,128]{2,1,0:T(8,128)(2,1)S(1)}, u32[]{:S(2)}, u32[]{:S(2)}) collective-permute-start(bf16[4,128,128]{2,1,0:T(8,128)(2,1)S(1)} %pad_maximum_fusion.1.refs_4_), channel_id=1, source_target_pairs={{0,24},{1,25},{2,26},{3,27},{4,28},{5,29},{6,30},{7,31},{8,16},{9,... | collective-permute-start | bytes 393224 | tf_op jit(solution)/shard_map/ppermute | solution.py:259
  39.6 1.5 %collective-permute-start.5 = (bf16[4,128,384]{2,1,0:T(8,128)(2,1)S(1)}, bf16[4,128,384]{2,1,0:T(8,128)(2,1)S(1)}, u32[]{:S(2)}, u32[]{:S(2)}) collective-permute-start(bf16[4,128,384]{2,1,0:T(8,128)(2,1)S(1)} %pad_maximum_fusion.refs_2_), channel_id=1, source_target_pairs={{0,4},{1,3},{2,6},{3,1},{4,0},{5,7},{6,2},{7,5},{8,12},{9,11},{10,... | collective-permute-start | bytes 1179656 | tf_op jit(solution)/shard_map/ppermute | solution.py:262
  41.7 1.0 collective-permute-done.14.refs_5_
  42.7 2.1 %collective-permute-start.22 = (bf16[128,128]{1,0:T(8,128)(2,1)S(1)}, bf16[128,128]{1,0:T(8,128)(2,1)S(1)}, u32[]{:S(2)}, u32[]{:S(2)}) collective-permute-start(bf16[128,128]{1,0:T(8,128)(2,1)S(1)} %get-tuple-element.82), channel_id=1, source_target_pairs={{0,8},{1,9},{2,10},{3,11},{4,12},{5,13},{6,14},{7,15},{8,0},{9,1},... | collective-permute-start | bytes 98312 | tf_op jit(solution)/shard_map/ppermute | solution.py:259
  44.8 3.4 %collective-permute-start.24 = (bf16[128,128]{1,0:T(8,128)(2,1)S(1)}, bf16[128,128]{1,0:T(8,128)(2,1)S(1)}, u32[]{:S(2)}, u32[]{:S(2)}) collective-permute-start(bf16[128,128]{1,0:T(8,128)(2,1)S(1)} %get-tuple-element.83), channel_id=1, source_target_pairs={{0,24},{1,25},{2,26},{3,27},{4,28},{5,29},{6,30},{7,31},{8,16},{9,... | collective-permute-start | bytes 98312 | tf_op jit(solution)/shard_map/ppermute | solution.py:259
  48.6 2.6 %collective-permute-start.13 = (bf16[4,128,128]{2,1,0:T(8,128)(2,1)S(1)}, bf16[4,128,128]{2,1,0:T(8,128)(2,1)S(1)}, u32[]{:S(2)}, u32[]{:S(2)}) collective-permute-start(bf16[4,128,128]{2,1,0:T(8,128)(2,1)S(1)} %pad_maximum_fusion.1.refs_4_), channel_id=1, source_target_pairs={{0,16},{1,17},{2,18},{3,19},{4,20},{5,21},{6,22},{7,23},{8,24},{9,... | collective-permute-start | bytes 393224 | tf_op jit(solution)/shard_map/ppermute | solution.py:259
  51.2 0.9 collective-permute-start.12
  52.1 2.3 %collective-permute-done.23 = bf16[128,128]{1,0:T(8,128)(2,1)S(1)} collective-permute-done((bf16[128,128]{1,0:T(8,128)(2,1)S(1)}, bf16[128,128]{1,0:T(8,128)(2,1)S(1)}, u32[]{:S(2)}, u32[]{:S(2)}) %collective-permute-start.23) | collective-permute-done | bytes 32800 | tf_op jit(solution)/shard_map/ppermute | solution.py:259
  54.4 1.5 %collective-permute-start.27 = (f32[128,128]{1,0:T(8,128)S(1)}, f32[128,128]{1,0:T(8,128)S(1)}, u32[]{:S(2)}, u32[]{:S(2)}) collective-permute-start(f32[128,128]{1,0:T(8,128)S(1)} %fusion.11), channel_id=1, source_target_pairs={{0,3},{1,2},{2,1},{3,0},{4,7},{5,6},{6,5},{7,4},{8,11},{9,10},{10,... | collective-permute-start | bytes 196616 | tf_op jit(solution)/shard_map/ppermute | solution.py:259
  56.7 3.0 %shard_map.64 = (f32[128,512]{1,0:T(8,128)S(1)}, f32[128,128]{1,0:T(8,128)S(1)}) custom-call(s32[3]{0:T(128)S(1)} %pad_add_fusion.refs_0_.where, f32[1,16384]{1,0:T(1,128)S(1)} %bitcast.63, bf16[4,128,384]{2,1,0:T(8,128)(2,1)S(1)} %pad_maximum_fusion.refs_2_, bf16[4,128,384]{2,1,0:T(8,128)(2,1)S(1)} %collective-permute-done.10.refs_3_, ...), custom_call_target="tpu_custom_call" | custom-call | flops 402653184 | bytes 3145728 | tf_op jit(solution)/shard_map/pallas_call | solution.py:163
  59.8 3.2 %shard_map.65 = (f32[128,512]{1,0:T(8,128)S(1)}, f32[128,128]{1,0:T(8,128)S(1)}) custom-call(s32[3]{0:T(128)S(1)} %pad_add_fusion.refs_0_.where, f32[1,16384]{1,0:T(1,128)S(1)} %bitcast.64, bf16[4,128,384]{2,1,0:T(8,128)(2,1)S(1)} %collective-permute-done.3.refs_2_, bf16[4,128,384]{2,1,0:T(8,128)(2,1)S(1)} %collective-permute-done.5.refs_3_, ...), custom_call_target="tpu_custom_call" | custom-call | flops 536870912 | bytes 4194304 | tf_op jit(solution)/shard_map/pallas_call | solution.py:163
  65.2 2.7 %collective-permute-done.25 = f32[128,128]{1,0:T(8,128)S(1)} collective-permute-done((f32[128,128]{1,0:T(8,128)S(1)}, f32[128,128]{1,0:T(8,128)S(1)}, u32[]{:S(2)}, u32[]{:S(2)}) %collective-permute-start.25) | collective-permute-done | bytes 65568 | tf_op jit(solution)/shard_map/ppermute | solution.py:259
  68.5 3.3 %shard_map.66 = (f32[128,512]{1,0:T(8,128)S(1)}, f32[128,128]{1,0:T(8,128)S(1)}) custom-call(s32[3]{0:T(128)S(1)} %pad_add_fusion.refs_0_.where, f32[1,16384]{1,0:T(1,128)S(1)} %bitcast.65, bf16[4,128,384]{2,1,0:T(8,128)(2,1)S(1)} %collective-permute-done.18.refs_2_, bf16[4,128,384]{2,1,0:T(8,128)(2,1)S(1)} %collective-permute-done.19.refs_3_, ...), custom_call_target="tpu_custom_call" | custom-call | flops 603979776 | bytes 4718592 | tf_op jit(solution)/shard_map/pallas_call | solution.py:163
  71.9 4.5 %shard_map.68.attended = bf16[128,512]{1,0:T(8,128)(2,1)S(1)} custom-call(s32[3]{0:T(128)S(1)} %pad_add_fusion.refs_0_.where, f32[1,16384]{1,0:T(1,128)S(1)} %bitcast.66, bf16[4,128,384]{2,1,0:T(8,128)(2,1)S(1)} %collective-permute-done.11.refs_2_, bf16[4,128,128]{2,1,0:T(8,128)(2,1)S(1)} %collective-permute-done.12.refs_3_, ...), custom_call_target="tpu_custom_call" | custom-call | flops 603979776 | bytes 4718592 | tf_op jit(solution)/shard_map/pallas_call | solution.py:163
  76.5 3.1 %shard_map.69 = (bf16[4,128,384]{2,1,0:T(8,128)(2,1)S(1)}, bf16[4,128,128]{2,1,0:T(8,128)(2,1)S(1)}, bf16[4,128,128]{2,1,0:T(8,128)(2,1)S(1)}, bf16[4,128,128]{2,1,0:T(8,128)(2,1)S(1)}) custom-call(s32[3]{0:T(128)S(1)} %pad_add_fusion.refs_0_.where, bf16[128,512]{1,0:T(8,128)(2,1)S(1)} %shard_map.68.attended, bf16[512,16384]{1,0:T(8,128)(2,1)} %refs_4_.5), custom_call_target="tpu_custom_call" | custom-call | flops 402653184 | bytes 3145728 | tf_op jit(solution)/shard_map/pallas_call | solution.py:218
  80.3 3.7 %shard_map.70 = (bf16[4,128,384]{2,1,0:T(8,128)(2,1)S(1)}, bf16[4,128,384]{2,1,0:T(8,128)(2,1)S(1)}, bf16[4,128,384]{2,1,0:T(8,128)(2,1)S(1)}, bf16[4,128,128]{2,1,0:T(8,128)(2,1)S(1)}) custom-call(s32[3]{0:T(128)S(1)} %pad_add_fusion.refs_0_.where, bf16[128,512]{1,0:T(8,128)(2,1)S(1)} %shard_map.68.attended, bf16[512,16384]{1,0:T(8,128)(2,1)} %refs_4_.5), custom_call_target="tpu_custom_call" | custom-call | flops 671088640 | bytes 5242880 | tf_op jit(solution)/shard_map/pallas_call | solution.py:218
  85.1 2.0 %collective-permute-done.36.refs_3_ = bf16[4,128,128]{2,1,0:T(8,128)(2,1)S(1)} collective-permute-done((bf16[4,128,128]{2,1,0:T(8,128)(2,1)S(1)}, bf16[4,128,128]{2,1,0:T(8,128)(2,1)S(1)}, u32[]{:S(2)}, u32[]{:S(2)}) %collective-permute-start.36) | collective-permute-done | bytes 131104 | tf_op jit(solution)/shard_map/ppermute | solution.py:259
  87.5 3.2 %shard_map.72 = (bf16[4,128,384]{2,1,0:T(8,128)(2,1)S(1)}, bf16[4,128,128]{2,1,0:T(8,128)(2,1)S(1)}, bf16[4,128,128]{2,1,0:T(8,128)(2,1)S(1)}, bf16[4,128,128]{2,1,0:T(8,128)(2,1)S(1)}) custom-call(s32[3]{0:T(128)S(1)} %pad_add_fusion.refs_0_.where, bf16[128,512]{1,0:T(8,128)(2,1)S(1)} %shard_map.68.attended, ...), custom_call_target="tpu_custom_call" | custom-call | flops 402653184 | bytes 3145728 | tf_op jit(solution)/shard_map/pallas_call | solution.py:218
  91.9 4.0 %collective-permute-start.44 = (bf16[4,128,128]{2,1,0:T(8,128)(2,1)S(1)}, bf16[4,128,128]{2,1,0:T(8,128)(2,1)S(1)}, u32[]{:S(2)}, u32[]{:S(2)}) collective-permute-start(bf16[4,128,128]{2,1,0:T(8,128)(2,1)S(1)} %get-tuple-element.70), channel_id=1, source_target_pairs={{0,24},{1,25},{2,26},{3,27},{4,28},{5,29},{6,30},{7,31},{8,16},{9,... | collective-permute-start | bytes 393224 | tf_op jit(solution)/shard_map/ppermute | solution.py:259
  95.9 3.7 %shard_map.71 = (f32[4,128,384]{2,1,0:T(8,128)S(1)}, bf16[4,128,384]{2,1,0:T(8,128)(2,1)S(1)}, f32[4,128,384]{2,1,0:T(8,128)S(1)}, f32[4,128,128]{2,1,0:T(8,128)S(1)}) custom-call(s32[3]{0:T(128)S(1)} %pad_add_fusion.refs_0_.where, bf16[128,512]{1,0:T(8,128)(2,1)S(1)} %shard_map.68.attended, bf16[4,128,384]{2,1,0:T(8,128)(2,1)S(1)} %collective-permute-done.28.refs_0_, ...), custom_call_target="tpu_custom_call" | custom-call | flops 671088640 | bytes 5242880 | tf_op jit(solution)/shard_map/pallas_call | solution.py:218
  99.5 1.3 %collective-permute-start.32 = (bf16[4,128,384]{2,1,0:T(8,128)(2,1)S(1)}, bf16[4,128,384]{2,1,0:T(8,128)(2,1)S(1)}, u32[]{:S(2)}, u32[]{:S(2)}) collective-permute-start(bf16[4,128,384]{2,1,0:T(8,128)(2,1)S(1)} %get-tuple-element.60), channel_id=1, source_target_pairs={{0,2},{1,5},{2,0},{3,7},{4,6},{5,1},{6,4},{7,3},{8,10},{9,13},{10,... | collective-permute-start | bytes 1179656 | tf_op jit(solution)/shard_map/ppermute | solution.py:262
  100.9 3.6 %collective-permute-done.43 = bf16[4,128,128]{2,1,0:T(8,128)(2,1)S(1)} collective-permute-done((bf16[4,128,128]{2,1,0:T(8,128)(2,1)S(1)}, bf16[4,128,128]{2,1,0:T(8,128)(2,1)S(1)}, u32[]{:S(2)}, u32[]{:S(2)}) %collective-permute-start.43) | collective-permute-done | bytes 131104 | tf_op jit(solution)/shard_map/ppermute | solution.py:259
  104.7 1.5 %collective-permute-start.38 = (bf16[4,128,384]{2,1,0:T(8,128)(2,1)S(1)}, bf16[4,128,384]{2,1,0:T(8,128)(2,1)S(1)}, u32[]{:S(2)}, u32[]{:S(2)}) collective-permute-start(bf16[4,128,384]{2,1,0:T(8,128)(2,1)S(1)} %add_convert_fusion), channel_id=1, source_target_pairs={{0,4},{1,3},{2,6},{3,1},{4,0},{5,7},{6,2},{7,5},{8,12},{9,11},{10,... | collective-permute-start | bytes 1179656 | tf_op jit(solution)/shard_map/ppermute | solution.py:262
  106.2 0.9 collective-permute-start.46
  107.1 1.1 collective-permute-start.45
  108.2 2.3 %collective-permute-done.46 = bf16[128,128]{1,0:T(8,128)(2,1)S(1)} collective-permute-done((bf16[128,128]{1,0:T(8,128)(2,1)S(1)}, bf16[128,128]{1,0:T(8,128)(2,1)S(1)}, u32[]{:S(2)}, u32[]{:S(2)}) %collective-permute-start.46) | collective-permute-done | bytes 32800 | tf_op jit(solution)/shard_map/ppermute | solution.py:262
  110.5 1.6 %collective-permute-start.47 = (bf16[128,128]{1,0:T(8,128)(2,1)S(1)}, bf16[128,128]{1,0:T(8,128)(2,1)S(1)}, u32[]{:S(2)}, u32[]{:S(2)}) collective-permute-start(bf16[128,128]{1,0:T(8,128)(2,1)S(1)} %fusion.5), channel_id=1, source_target_pairs={{0,4},{1,3},{2,6},{3,1},{4,0},{5,7},{6,2},{7,5},{8,12},{9,11},{10,... | collective-permute-start | bytes 98312 | tf_op jit(solution)/shard_map/ppermute | solution.py:262
  112.7 3.1 %collective-permute-start.39 = (bf16[128,384]{1,0:T(8,128)(2,1)S(1)}, bf16[128,384]{1,0:T(8,128)(2,1)S(1)}, u32[]{:S(2)}, u32[]{:S(2)}) collective-permute-start(bf16[128,384]{1,0:T(8,128)(2,1)S(1)} %get-tuple-element.77), channel_id=1, source_target_pairs={{0,8},{1,9},{2,10},{3,11},{4,12},{5,13},{6,14},{7,15},{8,0},{9,1},... | collective-permute-start | bytes 294920 | tf_op jit(solution)/shard_map/ppermute | solution.py:259
  115.8 1.4 %collective-permute-start.41 = (bf16[128,384]{1,0:T(8,128)(2,1)S(1)}, bf16[128,384]{1,0:T(8,128)(2,1)S(1)}, u32[]{:S(2)}, u32[]{:S(2)}) collective-permute-start(bf16[128,384]{1,0:T(8,128)(2,1)S(1)} %get-tuple-element.78), channel_id=1, source_target_pairs={{0,24},{1,25},{2,26},{3,27},{4,28},{5,29},{6,30},{7,31},{8,16},{9,... | collective-permute-start | bytes 294920 | tf_op jit(solution)/shard_map/ppermute | solution.py:259
  117.4 1.7 %collective-permute-done.39 = bf16[128,384]{1,0:T(8,128)(2,1)S(1)} collective-permute-done((bf16[128,384]{1,0:T(8,128)(2,1)S(1)}, bf16[128,384]{1,0:T(8,128)(2,1)S(1)}, u32[]{:S(2)}, u32[]{:S(2)}) %collective-permute-start.39) | collective-permute-done | bytes 98336 | tf_op jit(solution)/shard_map/ppermute | solution.py:259
  119.0 3.9 %collective-permute-done.41 = bf16[128,384]{1,0:T(8,128)(2,1)S(1)} collective-permute-done((bf16[128,384]{1,0:T(8,128)(2,1)S(1)}, bf16[128,384]{1,0:T(8,128)(2,1)S(1)}, u32[]{:S(2)}, u32[]{:S(2)}) %collective-permute-start.41) | collective-permute-done | bytes 98336 | tf_op jit(solution)/shard_map/ppermute | solution.py:259
  123.0 3.3 %collective-permute-done.40 = bf16[128,384]{1,0:T(8,128)(2,1)S(1)} collective-permute-done((bf16[128,384]{1,0:T(8,128)(2,1)S(1)}, bf16[128,384]{1,0:T(8,128)(2,1)S(1)}, u32[]{:S(2)}, u32[]{:S(2)}) %collective-permute-start.40) | collective-permute-done | bytes 98336 | tf_op jit(solution)/shard_map/ppermute | solution.py:259
  (91 shorter events, 11.6 us)
Async XLA Ops:
  0.9 5.9 %collective-permute-start = (bf16[128,384]{1,0:T(8,128)(2,1)S(1)}, bf16[128,384]{1,0:T(8,128)(2,1)S(1)}, u32[]{:S(2)}, u32[]{:S(2)}) collective-permute-start(bf16[128,384]{1,0:T(8,128)(2,1)S(1)} %get-tuple-element.88), channel_id=1, source_target_pairs={{0,8},{1,9},{2,10},{3,11},{4,12},{5,13},{6,14},{7,15},{8,0},{9,1},... | collective-permute-start | bytes 294920 | tf_op jit(solution)/shard_map/ppermute | solution.py:259
  12.0 20.9 %collective-permute-start.20 = (f32[8,128,128]{2,1,0:T(8,128)S(1)}, f32[8,128,128]{2,1,0:T(8,128)S(1)}, u32[]{:S(2)}, u32[]{:S(2)}) collective-permute-start(f32[8,128,128]{2,1,0:T(8,128)S(1)} %get-tuple-element.49), channel_id=1, source_target_pairs={{0,1},{1,0},{2,3},{3,2},{4,5},{5,4},{6,7},{7,6},{8,9},{9,8},{10,11... | collective-permute-start | bytes 1572872 | tf_op jit(solution)/shard_map/ppermute | solution.py:259
  12.1 10.8 %collective-permute-start.1 = (bf16[128,384]{1,0:T(8,128)(2,1)S(1)}, bf16[128,384]{1,0:T(8,128)(2,1)S(1)}, u32[]{:S(2)}, u32[]{:S(2)}) collective-permute-start(bf16[128,384]{1,0:T(8,128)(2,1)S(1)} %get-tuple-element.88), channel_id=1, source_target_pairs={{0,16},{1,17},{2,18},{3,19},{4,20},{5,21},{6,22},{7,23},{8,24},{9,... | collective-permute-start | bytes 294920 | tf_op jit(solution)/shard_map/ppermute | solution.py:259
  15.0 7.9 %collective-permute-start.2 = (bf16[128,384]{1,0:T(8,128)(2,1)S(1)}, bf16[128,384]{1,0:T(8,128)(2,1)S(1)}, u32[]{:S(2)}, u32[]{:S(2)}) collective-permute-start(bf16[128,384]{1,0:T(8,128)(2,1)S(1)} %get-tuple-element.88), channel_id=1, source_target_pairs={{0,24},{1,25},{2,26},{3,27},{4,28},{5,29},{6,30},{7,31},{8,16},{9,... | collective-permute-start | bytes 294920 | tf_op jit(solution)/shard_map/ppermute | solution.py:259
  23.0 16.6 %collective-permute-start.3 = (bf16[4,128,384]{2,1,0:T(8,128)(2,1)S(1)}, bf16[4,128,384]{2,1,0:T(8,128)(2,1)S(1)}, u32[]{:S(2)}, u32[]{:S(2)}) collective-permute-start(bf16[4,128,384]{2,1,0:T(8,128)(2,1)S(1)} %pad_maximum_fusion.refs_2_), channel_id=1, source_target_pairs={{0,2},{1,5},{2,0},{3,7},{4,6},{5,1},{6,4},{7,3},{8,10},{9,13},{10,... | collective-permute-start | bytes 1179656 | tf_op jit(solution)/shard_map/ppermute | solution.py:262
  24.7 6.7 %collective-permute-start.6 = (bf16[128,128]{1,0:T(8,128)(2,1)S(1)}, bf16[128,128]{1,0:T(8,128)(2,1)S(1)}, u32[]{:S(2)}, u32[]{:S(2)}) collective-permute-start(bf16[128,128]{1,0:T(8,128)(2,1)S(1)} %get-tuple-element.86), channel_id=1, source_target_pairs={{0,2},{1,5},{2,0},{3,7},{4,6},{5,1},{6,4},{7,3},{8,10},{9,13},{10,... | collective-permute-start | bytes 98312 | tf_op jit(solution)/shard_map/ppermute | solution.py:262
  25.1 8.6 %collective-permute-start.7 = (bf16[128,128]{1,0:T(8,128)(2,1)S(1)}, bf16[128,128]{1,0:T(8,128)(2,1)S(1)}, u32[]{:S(2)}, u32[]{:S(2)}) collective-permute-start(bf16[128,128]{1,0:T(8,128)(2,1)S(1)} %get-tuple-element.86), channel_id=1, source_target_pairs={{0,4},{1,3},{2,6},{3,1},{4,0},{5,7},{6,2},{7,5},{8,12},{9,11},{10,... | collective-permute-start | bytes 98312 | tf_op jit(solution)/shard_map/ppermute | solution.py:262
  31.5 4.3 %collective-permute-start.8 = (bf16[128,128]{1,0:T(8,128)(2,1)S(1)}, bf16[128,128]{1,0:T(8,128)(2,1)S(1)}, u32[]{:S(2)}, u32[]{:S(2)}) collective-permute-start(bf16[128,128]{1,0:T(8,128)(2,1)S(1)} %collective-permute-done.6), channel_id=1, source_target_pairs={{0,4},{1,3},{2,6},{3,1},{4,0},{5,7},{6,2},{7,5},{8,12},{9,11},{10,... | collective-permute-start | bytes 98312 | tf_op jit(solution)/shard_map/ppermute | solution.py:262
  33.1 8.1 %collective-permute-start.21 = (bf16[4,128,128]{2,1,0:T(8,128)(2,1)S(1)}, bf16[4,128,128]{2,1,0:T(8,128)(2,1)S(1)}, u32[]{:S(2)}, u32[]{:S(2)}) collective-permute-start(bf16[4,128,128]{2,1,0:T(8,128)(2,1)S(1)} %slice.127), channel_id=1, source_target_pairs={{0,4},{1,5},{2,6},{3,7},{4,0},{5,1},{6,2},{7,3},{8,12},{9,13},{10,... | collective-permute-start | bytes 393224 | tf_op jit(solution)/shard_map/ppermute | solution.py:259
  35.8 6.9 %collective-permute-start.14 = (bf16[4,128,128]{2,1,0:T(8,128)(2,1)S(1)}, bf16[4,128,128]{2,1,0:T(8,128)(2,1)S(1)}, u32[]{:S(2)}, u32[]{:S(2)}) collective-permute-start(bf16[4,128,128]{2,1,0:T(8,128)(2,1)S(1)} %pad_maximum_fusion.1.refs_4_), channel_id=1, source_target_pairs={{0,24},{1,25},{2,26},{3,27},{4,28},{5,29},{6,30},{7,31},{8,16},{9,... | collective-permute-start | bytes 393224 | tf_op jit(solution)/shard_map/ppermute | solution.py:259
  39.1 5.7 %collective-permute-start.9 = (bf16[4,128,128]{2,1,0:T(8,128)(2,1)S(1)}, bf16[4,128,128]{2,1,0:T(8,128)(2,1)S(1)}, u32[]{:S(2)}, u32[]{:S(2)}) collective-permute-start(bf16[4,128,128]{2,1,0:T(8,128)(2,1)S(1)} %pad_maximum_fusion.1.refs_4_), channel_id=1, source_target_pairs={{0,1},{1,0},{2,3},{3,2},{4,5},{5,4},{6,7},{7,6},{8,9},{9,8},{10,11... | collective-permute-start | bytes 393224 | tf_op jit(solution)/shard_map/ppermute | solution.py:259
  39.1 15.3 %collective-permute-start.10 = (bf16[4,128,384]{2,1,0:T(8,128)(2,1)S(1)}, bf16[4,128,384]{2,1,0:T(8,128)(2,1)S(1)}, u32[]{:S(2)}, u32[]{:S(2)}) collective-permute-start(bf16[4,128,384]{2,1,0:T(8,128)(2,1)S(1)} %pad_maximum_fusion.refs_2_), channel_id=1, source_target_pairs={{0,1},{1,0},{2,3},{3,2},{4,5},{5,4},{6,7},{7,6},{8,9},{9,8},{10,11... | collective-permute-start | bytes 1179656 | tf_op jit(solution)/shard_map/ppermute | solution.py:259
  39.6 8.6 %collective-permute-start.5 = (bf16[4,128,384]{2,1,0:T(8,128)(2,1)S(1)}, bf16[4,128,384]{2,1,0:T(8,128)(2,1)S(1)}, u32[]{:S(2)}, u32[]{:S(2)}) collective-permute-start(bf16[4,128,384]{2,1,0:T(8,128)(2,1)S(1)} %pad_maximum_fusion.refs_2_), channel_id=1, source_target_pairs={{0,4},{1,3},{2,6},{3,1},{4,0},{5,7},{6,2},{7,5},{8,12},{9,11},{10,... | collective-permute-start | bytes 1179656 | tf_op jit(solution)/shard_map/ppermute | solution.py:262
  41.1 18.6 %collective-permute-start.4 = (bf16[4,128,384]{2,1,0:T(8,128)(2,1)S(1)}, bf16[4,128,384]{2,1,0:T(8,128)(2,1)S(1)}, u32[]{:S(2)}, u32[]{:S(2)}) collective-permute-start(bf16[4,128,384]{2,1,0:T(8,128)(2,1)S(1)} %collective-permute-done.3.refs_2_), channel_id=1, source_target_pairs={{0,4},{1,3},{2,6},{3,1},{4,0},{5,7},{6,2},{7,5},{8,12},{9,11},{10,... | collective-permute-start | bytes 1179656 | tf_op jit(solution)/shard_map/ppermute | solution.py:262
  42.7 5.9 %collective-permute-start.22 = (bf16[128,128]{1,0:T(8,128)(2,1)S(1)}, bf16[128,128]{1,0:T(8,128)(2,1)S(1)}, u32[]{:S(2)}, u32[]{:S(2)}) collective-permute-start(bf16[128,128]{1,0:T(8,128)(2,1)S(1)} %get-tuple-element.82), channel_id=1, source_target_pairs={{0,8},{1,9},{2,10},{3,11},{4,12},{5,13},{6,14},{7,15},{8,0},{9,1},... | collective-permute-start | bytes 98312 | tf_op jit(solution)/shard_map/ppermute | solution.py:259
  44.8 6.4 %collective-permute-start.24 = (bf16[128,128]{1,0:T(8,128)(2,1)S(1)}, bf16[128,128]{1,0:T(8,128)(2,1)S(1)}, u32[]{:S(2)}, u32[]{:S(2)}) collective-permute-start(bf16[128,128]{1,0:T(8,128)(2,1)S(1)} %get-tuple-element.83), channel_id=1, source_target_pairs={{0,24},{1,25},{2,26},{3,27},{4,28},{5,29},{6,30},{7,31},{8,16},{9,... | collective-permute-start | bytes 98312 | tf_op jit(solution)/shard_map/ppermute | solution.py:259
  48.2 6.2 %collective-permute-start.23 = (bf16[128,128]{1,0:T(8,128)(2,1)S(1)}, bf16[128,128]{1,0:T(8,128)(2,1)S(1)}, u32[]{:S(2)}, u32[]{:S(2)}) collective-permute-start(bf16[128,128]{1,0:T(8,128)(2,1)S(1)} %get-tuple-element.84), channel_id=1, source_target_pairs={{0,16},{1,17},{2,18},{3,19},{4,20},{5,21},{6,22},{7,23},{8,24},{9,... | collective-permute-start | bytes 98312 | tf_op jit(solution)/shard_map/ppermute | solution.py:259
  48.6 14.4 %collective-permute-start.13 = (bf16[4,128,128]{2,1,0:T(8,128)(2,1)S(1)}, bf16[4,128,128]{2,1,0:T(8,128)(2,1)S(1)}, u32[]{:S(2)}, u32[]{:S(2)}) collective-permute-start(bf16[4,128,128]{2,1,0:T(8,128)(2,1)S(1)} %pad_maximum_fusion.1.refs_4_), channel_id=1, source_target_pairs={{0,16},{1,17},{2,18},{3,19},{4,20},{5,21},{6,22},{7,23},{8,24},{9,... | collective-permute-start | bytes 393224 | tf_op jit(solution)/shard_map/ppermute | solution.py:259
  51.2 12.4 %collective-permute-start.12 = (bf16[4,128,128]{2,1,0:T(8,128)(2,1)S(1)}, bf16[4,128,128]{2,1,0:T(8,128)(2,1)S(1)}, u32[]{:S(2)}, u32[]{:S(2)}) collective-permute-start(bf16[4,128,128]{2,1,0:T(8,128)(2,1)S(1)} %pad_maximum_fusion.1.refs_4_), channel_id=1, source_target_pairs={{0,8},{1,9},{2,10},{3,11},{4,12},{5,13},{6,14},{7,15},{8,0},{9,1},... | collective-permute-start | bytes 393224 | tf_op jit(solution)/shard_map/ppermute | solution.py:259
  54.4 13.5 %collective-permute-start.19 = (bf16[4,128,384]{2,1,0:T(8,128)(2,1)S(1)}, bf16[4,128,384]{2,1,0:T(8,128)(2,1)S(1)}, u32[]{:S(2)}, u32[]{:S(2)}) collective-permute-start(bf16[4,128,384]{2,1,0:T(8,128)(2,1)S(1)} %collective-permute-done.5.refs_3_), channel_id=1, source_target_pairs={{0,1},{1,0},{2,3},{3,2},{4,5},{5,4},{6,7},{7,6},{8,9},{9,8},{10,11... | collective-permute-start | bytes 1179656 | tf_op jit(solution)/shard_map/ppermute | solution.py:259
  54.4 9.9 %collective-permute-start.27 = (f32[128,128]{1,0:T(8,128)S(1)}, f32[128,128]{1,0:T(8,128)S(1)}, u32[]{:S(2)}, u32[]{:S(2)}) collective-permute-start(f32[128,128]{1,0:T(8,128)S(1)} %fusion.11), channel_id=1, source_target_pairs={{0,3},{1,2},{2,1},{3,0},{4,7},{5,6},{6,5},{7,4},{8,11},{9,10},{10,... | collective-permute-start | bytes 196616 | tf_op jit(solution)/shard_map/ppermute | solution.py:259
  59.8 8.8 %collective-permute-start.18 = (bf16[4,128,384]{2,1,0:T(8,128)(2,1)S(1)}, bf16[4,128,384]{2,1,0:T(8,128)(2,1)S(1)}, u32[]{:S(2)}, u32[]{:S(2)}) collective-permute-start(bf16[4,128,384]{2,1,0:T(8,128)(2,1)S(1)} %collective-permute-done.3.refs_2_), channel_id=1, source_target_pairs={{0,1},{1,0},{2,3},{3,2},{4,5},{5,4},{6,7},{7,6},{8,9},{9,8},{10,11... | collective-permute-start | bytes 1179656 | tf_op jit(solution)/shard_map/ppermute | solution.py:259
  63.0 1.6 %collective-permute-start.26 = (f32[128,128]{1,0:T(8,128)S(1)}, f32[128,128]{1,0:T(8,128)S(1)}, u32[]{:S(2)}, u32[]{:S(2)}) collective-permute-start(f32[128,128]{1,0:T(8,128)S(1)} %fusion.11), channel_id=1, source_target_pairs={{0,1},{1,0},{2,3},{3,2},{4,5},{5,4},{6,7},{7,6},{8,9},{9,8},{10,11... | collective-permute-start | bytes 196616 | tf_op jit(solution)/shard_map/ppermute | solution.py:259
  63.6 4.3 %collective-permute-start.25 = (f32[128,128]{1,0:T(8,128)S(1)}, f32[128,128]{1,0:T(8,128)S(1)}, u32[]{:S(2)}, u32[]{:S(2)}) collective-permute-start(f32[128,128]{1,0:T(8,128)S(1)} %fusion.11), channel_id=1, source_target_pairs={{0,2},{1,3},{2,0},{3,1},{4,6},{5,7},{6,4},{7,5},{8,10},{9,11},{10,... | collective-permute-start | bytes 196616 | tf_op jit(solution)/shard_map/ppermute | solution.py:259
  64.4 7.6 %collective-permute-start.11 = (bf16[4,128,384]{2,1,0:T(8,128)(2,1)S(1)}, bf16[4,128,384]{2,1,0:T(8,128)(2,1)S(1)}, u32[]{:S(2)}, u32[]{:S(2)}) collective-permute-start(bf16[4,128,384]{2,1,0:T(8,128)(2,1)S(1)} %collective-permute-done.4.refs_4_), channel_id=1, source_target_pairs={{0,1},{1,0},{2,3},{3,2},{4,5},{5,4},{6,7},{7,6},{8,9},{9,8},{10,11... | collective-permute-start | bytes 1179656 | tf_op jit(solution)/shard_map/ppermute | solution.py:259
  64.6 7.3 %collective-permute-start.17 = (bf16[4,128,128]{2,1,0:T(8,128)(2,1)S(1)}, bf16[4,128,128]{2,1,0:T(8,128)(2,1)S(1)}, u32[]{:S(2)}, u32[]{:S(2)}) collective-permute-start(bf16[4,128,128]{2,1,0:T(8,128)(2,1)S(1)} %collective-permute-done.14.refs_5_), channel_id=1, source_target_pairs={{0,1},{1,0},{2,3},{3,2},{4,5},{5,4},{6,7},{7,6},{8,9},{9,8},{10,11... | collective-permute-start | bytes 393224 | tf_op jit(solution)/shard_map/ppermute | solution.py:259
  67.9 4.0 %collective-permute-start.16 = (bf16[4,128,128]{2,1,0:T(8,128)(2,1)S(1)}, bf16[4,128,128]{2,1,0:T(8,128)(2,1)S(1)}, u32[]{:S(2)}, u32[]{:S(2)}) collective-permute-start(bf16[4,128,128]{2,1,0:T(8,128)(2,1)S(1)} %collective-permute-done.13.refs_4_), channel_id=1, source_target_pairs={{0,1},{1,0},{2,3},{3,2},{4,5},{5,4},{6,7},{7,6},{8,9},{9,8},{10,11... | collective-permute-start | bytes 393224 | tf_op jit(solution)/shard_map/ppermute | solution.py:259
  67.9 4.0 %collective-permute-start.15 = (bf16[4,128,128]{2,1,0:T(8,128)(2,1)S(1)}, bf16[4,128,128]{2,1,0:T(8,128)(2,1)S(1)}, u32[]{:S(2)}, u32[]{:S(2)}) collective-permute-start(bf16[4,128,128]{2,1,0:T(8,128)(2,1)S(1)} %collective-permute-done.12.refs_3_), channel_id=1, source_target_pairs={{0,1},{1,0},{2,3},{3,2},{4,5},{5,4},{6,7},{7,6},{8,9},{9,8},{10,11... | collective-permute-start | bytes 393224 | tf_op jit(solution)/shard_map/ppermute | solution.py:259
  79.7 4.9 %collective-permute-start.34 = (bf16[4,128,128]{2,1,0:T(8,128)(2,1)S(1)}, bf16[4,128,128]{2,1,0:T(8,128)(2,1)S(1)}, u32[]{:S(2)}, u32[]{:S(2)}) collective-permute-start(bf16[4,128,128]{2,1,0:T(8,128)(2,1)S(1)} %get-tuple-element.63), channel_id=1, source_target_pairs={{0,1},{1,0},{2,3},{3,2},{4,5},{5,4},{6,7},{7,6},{8,9},{9,8},{10,11... | collective-permute-start | bytes 393224 | tf_op jit(solution)/shard_map/ppermute | solution.py:259
  79.7 5.2 %collective-permute-start.35 = (bf16[4,128,128]{2,1,0:T(8,128)(2,1)S(1)}, bf16[4,128,128]{2,1,0:T(8,128)(2,1)S(1)}, u32[]{:S(2)}, u32[]{:S(2)}) collective-permute-start(bf16[4,128,128]{2,1,0:T(8,128)(2,1)S(1)} %get-tuple-element.64), channel_id=1, source_target_pairs={{0,1},{1,0},{2,3},{3,2},{4,5},{5,4},{6,7},{7,6},{8,9},{9,8},{10,11... | collective-permute-start | bytes 393224 | tf_op jit(solution)/shard_map/ppermute | solution.py:259
  80.2 7.3 %collective-permute-start.33 = (bf16[4,128,384]{2,1,0:T(8,128)(2,1)S(1)}, bf16[4,128,384]{2,1,0:T(8,128)(2,1)S(1)}, u32[]{:S(2)}, u32[]{:S(2)}) collective-permute-start(bf16[4,128,384]{2,1,0:T(8,128)(2,1)S(1)} %get-tuple-element.62), channel_id=1, source_target_pairs={{0,1},{1,0},{2,3},{3,2},{4,5},{5,4},{6,7},{7,6},{8,9},{9,8},{10,11... | collective-permute-start | bytes 1179656 | tf_op jit(solution)/shard_map/ppermute | solution.py:259
  84.0 7.5 %collective-permute-start.28 = (bf16[4,128,384]{2,1,0:T(8,128)(2,1)S(1)}, bf16[4,128,384]{2,1,0:T(8,128)(2,1)S(1)}, u32[]{:S(2)}, u32[]{:S(2)}) collective-permute-start(bf16[4,128,384]{2,1,0:T(8,128)(2,1)S(1)} %get-tuple-element.55), channel_id=1, source_target_pairs={{0,1},{1,0},{2,3},{3,2},{4,5},{5,4},{6,7},{7,6},{8,9},{9,8},{10,11... | collective-permute-start | bytes 1179656 | tf_op jit(solution)/shard_map/ppermute | solution.py:259
  84.5 7.4 %collective-permute-start.29 = (bf16[4,128,384]{2,1,0:T(8,128)(2,1)S(1)}, bf16[4,128,384]{2,1,0:T(8,128)(2,1)S(1)}, u32[]{:S(2)}, u32[]{:S(2)}) collective-permute-start(bf16[4,128,384]{2,1,0:T(8,128)(2,1)S(1)} %get-tuple-element.56), channel_id=1, source_target_pairs={{0,1},{1,0},{2,3},{3,2},{4,5},{5,4},{6,7},{7,6},{8,9},{9,8},{10,11... | collective-permute-start | bytes 1179656 | tf_op jit(solution)/shard_map/ppermute | solution.py:259
  84.6 11.3 %collective-permute-start.30 = (bf16[4,128,384]{2,1,0:T(8,128)(2,1)S(1)}, bf16[4,128,384]{2,1,0:T(8,128)(2,1)S(1)}, u32[]{:S(2)}, u32[]{:S(2)}) collective-permute-start(bf16[4,128,384]{2,1,0:T(8,128)(2,1)S(1)} %get-tuple-element.57), channel_id=1, source_target_pairs={{0,1},{1,0},{2,3},{3,2},{4,5},{5,4},{6,7},{7,6},{8,9},{9,8},{10,11... | collective-permute-start | bytes 1179656 | tf_op jit(solution)/shard_map/ppermute | solution.py:259
  85.0 2.1 %collective-permute-start.36 = (bf16[4,128,128]{2,1,0:T(8,128)(2,1)S(1)}, bf16[4,128,128]{2,1,0:T(8,128)(2,1)S(1)}, u32[]{:S(2)}, u32[]{:S(2)}) collective-permute-start(bf16[4,128,128]{2,1,0:T(8,128)(2,1)S(1)} %get-tuple-element.65), channel_id=1, source_target_pairs={{0,1},{1,0},{2,3},{3,2},{4,5},{5,4},{6,7},{7,6},{8,9},{9,8},{10,11... | collective-permute-start | bytes 393224 | tf_op jit(solution)/shard_map/ppermute | solution.py:259
  87.1 4.4 %collective-permute-start.31 = (bf16[4,128,128]{2,1,0:T(8,128)(2,1)S(1)}, bf16[4,128,128]{2,1,0:T(8,128)(2,1)S(1)}, u32[]{:S(2)}, u32[]{:S(2)}) collective-permute-start(bf16[4,128,128]{2,1,0:T(8,128)(2,1)S(1)} %get-tuple-element.58), channel_id=1, source_target_pairs={{0,1},{1,0},{2,3},{3,2},{4,5},{5,4},{6,7},{7,6},{8,9},{9,8},{10,11... | collective-permute-start | bytes 393224 | tf_op jit(solution)/shard_map/ppermute | solution.py:259
  90.7 13.9 %collective-permute-start.37 = (bf16[4,128,384]{2,1,0:T(8,128)(2,1)S(1)}, bf16[4,128,384]{2,1,0:T(8,128)(2,1)S(1)}, u32[]{:S(2)}, u32[]{:S(2)}) collective-permute-start(bf16[4,128,384]{2,1,0:T(8,128)(2,1)S(1)} %get-tuple-element.66), channel_id=1, source_target_pairs={{0,2},{1,5},{2,0},{3,7},{4,6},{5,1},{6,4},{7,3},{8,10},{9,13},{10,... | collective-permute-start | bytes 1179656 | tf_op jit(solution)/shard_map/ppermute | solution.py:262
  91.5 9.4 %collective-permute-start.42 = (bf16[4,128,128]{2,1,0:T(8,128)(2,1)S(1)}, bf16[4,128,128]{2,1,0:T(8,128)(2,1)S(1)}, u32[]{:S(2)}, u32[]{:S(2)}) collective-permute-start(bf16[4,128,128]{2,1,0:T(8,128)(2,1)S(1)} %get-tuple-element.68), channel_id=1, source_target_pairs={{0,8},{1,9},{2,10},{3,11},{4,12},{5,13},{6,14},{7,15},{8,0},{9,1},... | collective-permute-start | bytes 393224 | tf_op jit(solution)/shard_map/ppermute | solution.py:259
  91.5 13.0 %collective-permute-start.43 = (bf16[4,128,128]{2,1,0:T(8,128)(2,1)S(1)}, bf16[4,128,128]{2,1,0:T(8,128)(2,1)S(1)}, u32[]{:S(2)}, u32[]{:S(2)}) collective-permute-start(bf16[4,128,128]{2,1,0:T(8,128)(2,1)S(1)} %get-tuple-element.69), channel_id=1, source_target_pairs={{0,16},{1,17},{2,18},{3,19},{4,20},{5,21},{6,22},{7,23},{8,24},{9,... | collective-permute-start | bytes 393224 | tf_op jit(solution)/shard_map/ppermute | solution.py:259
  91.9 12.6 %collective-permute-start.44 = (bf16[4,128,128]{2,1,0:T(8,128)(2,1)S(1)}, bf16[4,128,128]{2,1,0:T(8,128)(2,1)S(1)}, u32[]{:S(2)}, u32[]{:S(2)}) collective-permute-start(bf16[4,128,128]{2,1,0:T(8,128)(2,1)S(1)} %get-tuple-element.70), channel_id=1, source_target_pairs={{0,24},{1,25},{2,26},{3,27},{4,28},{5,29},{6,30},{7,31},{8,16},{9,... | collective-permute-start | bytes 393224 | tf_op jit(solution)/shard_map/ppermute | solution.py:259
  99.5 12.6 %collective-permute-start.32 = (bf16[4,128,384]{2,1,0:T(8,128)(2,1)S(1)}, bf16[4,128,384]{2,1,0:T(8,128)(2,1)S(1)}, u32[]{:S(2)}, u32[]{:S(2)}) collective-permute-start(bf16[4,128,384]{2,1,0:T(8,128)(2,1)S(1)} %get-tuple-element.60), channel_id=1, source_target_pairs={{0,2},{1,5},{2,0},{3,7},{4,6},{5,1},{6,4},{7,3},{8,10},{9,13},{10,... | collective-permute-start | bytes 1179656 | tf_op jit(solution)/shard_map/ppermute | solution.py:262
  104.7 7.8 %collective-permute-start.38 = (bf16[4,128,384]{2,1,0:T(8,128)(2,1)S(1)}, bf16[4,128,384]{2,1,0:T(8,128)(2,1)S(1)}, u32[]{:S(2)}, u32[]{:S(2)}) collective-permute-start(bf16[4,128,384]{2,1,0:T(8,128)(2,1)S(1)} %add_convert_fusion), channel_id=1, source_target_pairs={{0,4},{1,3},{2,6},{3,1},{4,0},{5,7},{6,2},{7,5},{8,12},{9,11},{10,... | collective-permute-start | bytes 1179656 | tf_op jit(solution)/shard_map/ppermute | solution.py:262
  106.2 4.3 %collective-permute-start.46 = (bf16[128,128]{1,0:T(8,128)(2,1)S(1)}, bf16[128,128]{1,0:T(8,128)(2,1)S(1)}, u32[]{:S(2)}, u32[]{:S(2)}) collective-permute-start(bf16[128,128]{1,0:T(8,128)(2,1)S(1)} %get-tuple-element.81), channel_id=1, source_target_pairs={{0,2},{1,5},{2,0},{3,7},{4,6},{5,1},{6,4},{7,3},{8,10},{9,13},{10,... | collective-permute-start | bytes 98312 | tf_op jit(solution)/shard_map/ppermute | solution.py:262
  107.1 10.3 %collective-permute-start.45 = (bf16[128,128]{1,0:T(8,128)(2,1)S(1)}, bf16[128,128]{1,0:T(8,128)(2,1)S(1)}, u32[]{:S(2)}, u32[]{:S(2)}) collective-permute-start(bf16[128,128]{1,0:T(8,128)(2,1)S(1)} %get-tuple-element.80), channel_id=1, source_target_pairs={{0,2},{1,5},{2,0},{3,7},{4,6},{5,1},{6,4},{7,3},{8,10},{9,13},{10,... | collective-permute-start | bytes 98312 | tf_op jit(solution)/shard_map/ppermute | solution.py:262
  110.5 6.9 %collective-permute-start.47 = (bf16[128,128]{1,0:T(8,128)(2,1)S(1)}, bf16[128,128]{1,0:T(8,128)(2,1)S(1)}, u32[]{:S(2)}, u32[]{:S(2)}) collective-permute-start(bf16[128,128]{1,0:T(8,128)(2,1)S(1)} %fusion.5), channel_id=1, source_target_pairs={{0,4},{1,3},{2,6},{3,1},{4,0},{5,7},{6,2},{7,5},{8,12},{9,11},{10,... | collective-permute-start | bytes 98312 | tf_op jit(solution)/shard_map/ppermute | solution.py:262
  112.7 6.3 %collective-permute-start.39 = (bf16[128,384]{1,0:T(8,128)(2,1)S(1)}, bf16[128,384]{1,0:T(8,128)(2,1)S(1)}, u32[]{:S(2)}, u32[]{:S(2)}) collective-permute-start(bf16[128,384]{1,0:T(8,128)(2,1)S(1)} %get-tuple-element.77), channel_id=1, source_target_pairs={{0,8},{1,9},{2,10},{3,11},{4,12},{5,13},{6,14},{7,15},{8,0},{9,1},... | collective-permute-start | bytes 294920 | tf_op jit(solution)/shard_map/ppermute | solution.py:259
  115.8 7.1 %collective-permute-start.41 = (bf16[128,384]{1,0:T(8,128)(2,1)S(1)}, bf16[128,384]{1,0:T(8,128)(2,1)S(1)}, u32[]{:S(2)}, u32[]{:S(2)}) collective-permute-start(bf16[128,384]{1,0:T(8,128)(2,1)S(1)} %get-tuple-element.78), channel_id=1, source_target_pairs={{0,24},{1,25},{2,26},{3,27},{4,28},{5,29},{6,30},{7,31},{8,16},{9,... | collective-permute-start | bytes 294920 | tf_op jit(solution)/shard_map/ppermute | solution.py:259
  117.2 9.1 %collective-permute-start.40 = (bf16[128,384]{1,0:T(8,128)(2,1)S(1)}, bf16[128,384]{1,0:T(8,128)(2,1)S(1)}, u32[]{:S(2)}, u32[]{:S(2)}) collective-permute-start(bf16[128,384]{1,0:T(8,128)(2,1)S(1)} %get-tuple-element.79), channel_id=1, source_target_pairs={{0,16},{1,17},{2,18},{3,19},{4,20},{5,21},{6,22},{7,23},{8,24},{9,... | collective-permute-start | bytes 294920 | tf_op jit(solution)/shard_map/ppermute | solution.py:259
  (5 other events, 5.0 us)

commit v3 on v2

v3 whole, which is shorter than its diff:
```python
import functools

import jax
import jax.numpy as jnp
from jax import lax
from jax.experimental import pallas as pl
from jax.experimental.pallas import tpu as pltpu
from jax.sharding import PartitionSpec as P

HEADS = 128
KVH = 8
HEAD = 128
LANE = 128
EPS = 1e-05
MIB = 1 << 20
CORE = 1


def combos(bits):
    out = [0]
    for b in bits:
        out = out + [o ^ b for o in out]
    return out


def vmem():
    return pl.BlockSpec(memory_space=pltpu.VMEM)


def smem():
    return pl.BlockSpec(memory_space=pltpu.SMEM)


def hbm():
    return pl.BlockSpec(memory_space=pltpu.HBM)


def in_hbm(x):
    return pltpu.with_memory_space_constraint(x, pltpu.HBM)


def dot(a, b):
    return jnp.dot(a, b, preferred_element_type=jnp.float32)


def fetch_kernel(source, target, sems):
    count = sems.shape[0]
    rows = source.shape[0] // count
    copies = [
        pltpu.make_async_copy(
            source.at[pl.ds(i * rows, rows), :], target.at[pl.ds(i * rows, rows), :], sems.at[i]
        )
        for i in range(count)
    ]
    for copy in copies:
        copy.start()
    for copy in copies:
        copy.wait()


def fetched(weight):
    return pl.pallas_call(
        fetch_kernel,
        out_shape=jax.ShapeDtypeStruct(weight.shape, weight.dtype),
        in_specs=[hbm()],
        out_specs=vmem(),
        scratch_shapes=[pltpu.SemaphoreType.DMA((8,))],
        compiler_params=pltpu.CompilerParams(vmem_limit_bytes=MIB),
        cost_estimate=pl.CostEstimate(
            flops=0, bytes_accessed=4 * weight.size, transcendentals=0
        ),
    )(in_hbm(weight))


def kv_kernel(shared, where, act, gain, wk, wv, send, keep, kbuf, vbuf, sems):
    copies = [
        pltpu.make_async_copy(wk, kbuf, sems.at[0]),
        pltpu.make_async_copy(wv, vbuf, sems.at[1]),
    ]
    for c in copies:
        c.start()
    me = where[0]
    width = act.shape[1]
    own = gain[:, pl.ds(pl.multiple_of(me * width, LANE), width)]
    scaled = (act[...].astype(jnp.float32) * own).astype(jnp.bfloat16)
    for c in copies:
        c.wait()
    k, v = dot(scaled, kbuf[...]), dot(scaled, vbuf[...])
    core0 = (me & CORE) == 0
    for h in range(KVH):
        off = h ^ (me >> shared)
        spot = ((off & 1) ^ 1) * (KVH // 2) + (off >> 1)
        kh, vh = k[:, h * HEAD : (h + 1) * HEAD], v[:, h * HEAD : (h + 1) * HEAD]
        keep[spot] = jnp.where(core0, kh, vh)
        send[spot] = jnp.where(core0, vh, kh)


def kv_terms(shared, where, act, gain, wk, wv):
    tokens = act.shape[0]
    return pl.pallas_call(
        functools.partial(kv_kernel, shared),
        out_shape=[jax.ShapeDtypeStruct((KVH, tokens, HEAD), jnp.float32)] * 2,
        in_specs=[smem(), vmem(), vmem(), hbm(), hbm()],
        out_specs=[vmem(), vmem()],
        scratch_shapes=[
            pltpu.VMEM(wk.shape, wk.dtype),
            pltpu.VMEM(wv.shape, wv.dtype),
            pltpu.SemaphoreType.DMA((2,)),
        ],
        compiler_params=pltpu.CompilerParams(vmem_limit_bytes=12 * MIB),
        cost_estimate=pl.CostEstimate(
            flops=4 * tokens * wk.size, bytes_accessed=4 * wk.size, transcendentals=0
        ),
    )(where, act, gain, in_hbm(wk), in_hbm(wv))


def attend(queries, k_sum, v_sum, cosine, sine, scale):
    k_rows = (k_sum * scale).astype(jnp.bfloat16).astype(jnp.float32)
    value = (v_sum * scale).astype(jnp.bfloat16)

    def rotate(x):
        half = HEAD // 2
        turned = jnp.concatenate([x[:, half:], x[:, :half]], axis=1)
        return (x * cosine + turned * sine).astype(jnp.bfloat16)

    key = rotate(k_rows)
    tokens = key.shape[0]
    rows = lax.broadcasted_iota(jnp.int32, (tokens, tokens), 0)
    cols = lax.broadcasted_iota(jnp.int32, (tokens, tokens), 1)
    out = []
    for h in range(queries.shape[1] // HEAD):
        q = rotate(queries[:, h * HEAD : (h + 1) * HEAD] * scale)
        scores = lax.dot_general(
            q, key, (((1,), (1,)), ((), ())), preferred_element_type=jnp.float32
        ) * HEAD ** (-0.5)
        scores = jnp.where(rows >= cols, scores, -1e30)
        weights = jnp.exp(scores - jnp.max(scores, axis=1, keepdims=True))
        probs = (weights / jnp.sum(weights, axis=1, keepdims=True)).astype(jnp.bfloat16)
        out.append(dot(probs, value).astype(jnp.bfloat16))
    return jnp.concatenate(out, axis=1)


def query_kernel(places, carried, last, *refs):
    refs = list(refs)
    where, gain = refs.pop(0), refs.pop(0)
    pieces = [refs.pop(0) for _ in places]
    weight = refs.pop(0)
    queries = refs.pop(0)[...] if carried else None
    squares = refs.pop(0)[...] if carried else None
    for piece, symbols in zip(pieces, places):
        width = piece.shape[2]
        for block, (const, pick) in enumerate(symbols):
            span = pl.ds(pl.multiple_of((where[pick] ^ const) * width, LANE), width)
            x = piece[block].astype(jnp.float32)
            term = dot((x * gain[:, span]).astype(jnp.bfloat16), weight[span, :])
            queries = term if queries is None else queries + term
            for c in range(0, width, LANE):
                square = x[:, c : c + LANE] * x[:, c : c + LANE]
                squares = square if squares is None else squares + square
    if last:
        mean = jnp.sum(squares, axis=1, keepdims=True) * (1.0 / weight.shape[0])
        mine, other, cosine, sine, out = refs
        core0 = (where[0] & CORE) == 0
        k_sum = jnp.where(core0, mine[...], other[...])
        v_sum = jnp.where(core0, other[...], mine[...])
        out[...] = attend(
            queries, k_sum, v_sum, cosine[...], sine[...], lax.rsqrt(mean + EPS)
        )
    else:
        refs[0][...] = queries
        refs[1][...] = squares


def query_call(where, gain, pieces, weight, carry=(), extra=()):
    arrays, places = [a for a, _ in pieces], [symbols for _, symbols in pieces]
    tokens, columns = arrays[0].shape[1], weight.shape[1]
    if extra:
        out_shape = [jax.ShapeDtypeStruct((tokens, columns), jnp.bfloat16)]
    else:
        out_shape = [
            jax.ShapeDtypeStruct((tokens, columns), jnp.float32),
            jax.ShapeDtypeStruct((tokens, LANE), jnp.float32),
        ]
    rows = sum(a.shape[0] * a.shape[2] for a in arrays)
    count = 1 + len(arrays) + 1 + len(carry) + len(extra)
    return pl.pallas_call(
        functools.partial(query_kernel, places, bool(carry), bool(extra)),
        out_shape=out_shape,
        in_specs=[smem()] + [vmem()] * count,
        out_specs=[vmem()] * len(out_shape),
        compiler_params=pltpu.CompilerParams(vmem_limit_bytes=12 * MIB),
        cost_estimate=pl.CostEstimate(
            flops=2 * tokens * columns * rows,
            bytes_accessed=2 * columns * rows,
            transcendentals=0,
        ),
    )(where, gain, *arrays, weight, *carry, *extra)


def output_kernel(groups, width, where, attended, *refs):
    refs = list(refs)
    added = [refs.pop(0) if g[1] else None for g in groups]
    weight = refs.pop(0)
    left = attended[...]
    for (symbols, _), arrived, out in zip(groups, added, refs):
        for block, (const, pick) in enumerate(symbols):
            span = pl.ds(pl.multiple_of((where[pick] ^ const) * width, LANE), width)
            term = dot(left, weight[:, span])
            if arrived is not None:
                term = term + arrived[block].astype(jnp.float32)
            out[block] = term.astype(out.dtype)


def output_call(where, attended, weight, width, groups):
    tokens, depth = attended.shape
    blocks = sum(len(g[0]) for g in groups)
    added = [g[2] for g in groups if g[2] is not None]
    return pl.pallas_call(
        functools.partial(output_kernel, [(s, a is not None) for s, _, a in groups], width),
        out_shape=[jax.ShapeDtypeStruct((len(s), tokens, width), t) for s, t, _ in groups],
        in_specs=[smem()] + [vmem()] * (2 + len(added)),
        out_specs=[vmem()] * len(groups),
        compiler_params=pltpu.CompilerParams(vmem_limit_bytes=12 * MIB),
        cost_estimate=pl.CostEstimate(
            flops=2 * tokens * depth * width * blocks,
            bytes_accessed=2 * depth * width * blocks,
            transcendentals=0,
        ),
    )(where, attended, *added, weight)


def rotary_tables(tokens):
    half = HEAD // 2
    frequency = 500000.0 ** (-(jnp.arange(half, dtype=jnp.float32) * 2.0) / HEAD)
    angles = jnp.arange(tokens, dtype=jnp.float32)[:, None] * frequency[None, :]
    cosine, sine = jnp.cos(angles), jnp.sin(angles)
    return jnp.concatenate([cosine, cosine], axis=1), jnp.concatenate([-sine, sine], axis=1)


def per_device(n, act, norm_gain, wq, wk, wv, wo):
    tokens, width = act.shape
    me = lax.axis_index("wide")
    bits = [1 << i for i in range(n.bit_length() - 1)]
    side = (bits[1], bits[2])
    diagonal = bits[1] ^ bits[2]
    far = combos(bits[3:])
    f32, bf16 = jnp.float32, jnp.bfloat16

    def swap(x, offset):
        return lax.ppermute(x, "wide", [(i, i ^ offset) for i in range(n)])

    def turn(x, step):
        return lax.ppermute(x, "wide", [(i, i ^ side[(step + (i & CORE)) % 2]) for i in range(n)])

    bit = jnp.where((me & CORE) == 0, side[0], side[1])
    where = jnp.stack([me, me ^ bit, me ^ bit ^ diagonal]).astype(jnp.int32)
    gain = norm_gain.reshape(1, -1)

    def plain(offsets, pick=0):
        return [(o, pick) for o in offsets]

    def across(symbols):
        return [(const ^ CORE, (0, 2, 1)[pick]) for const, pick in symbols]

    at_home, at_one, at_two = plain(far), plain(far, 1), plain(far, 2)
    at_corner = plain([o ^ diagonal for o in far])

    shared = (n // KVH).bit_length() - 1
    others = combos(bits[shared + 1 :])
    kv_send, kv_keep = kv_terms(shared, where, act, gain, wk, wv)
    kv = kv_keep + swap(kv_send, CORE)
    half = KVH // 2
    kv = kv[half:] + swap(kv[:half].astype(bf16), bits[shared]).astype(f32)
    total = kv[0]
    for i, o in enumerate(others):
        if o:
            total = total + swap(kv[i].astype(bf16), o).astype(f32)
    for b in bits[1:shared]:
        total = total + swap(total.astype(bf16), b).astype(f32)
    kv_sums = (total, swap(total, CORE))

    row = jnp.stack([act] + [swap(act, o) for o in far[1:]])
    row, wq = lax.optimization_barrier((row, fetched(wq)))
    side_1, side_2 = turn(row, 0), turn(row, 1)
    corner = turn(side_1, 1)
    call = functools.partial(query_call, where, gain, weight=wq)
    carry = call([(row, at_home), (swap(row, CORE), across(at_home))])
    carry = call([(side_1, at_one), (side_2, at_two)], carry=carry)
    corner, wo, *carry = lax.optimization_barrier((corner, fetched(wo), *carry))
    carry = call(
        [
            (swap(side_1, CORE), across(at_one)),
            (swap(side_2, CORE), across(at_two)),
            (corner, at_corner),
        ],
        carry=carry,
    )
    (attended,) = call(
        [(swap(corner, CORE), across(at_corner))],
        carry=carry,
        extra=(*kv_sums, *rotary_tables(tokens)),
    )

    leave = [(at_corner, bf16)]
    stay = [(at_two, f32), (at_one, bf16), (at_home, f32)]

    def project(left, groups, arrived=None):
        if arrived is None:
            groups = [(across(s), bf16, None) for s, _ in groups]
        else:
            groups = [(*g, a) for g, a in zip(groups, arrived)]
        return output_call(where, left, wo, width, groups)

    send_1 = project(attended, leave)
    attended, *send_1 = lax.optimization_barrier((attended, *send_1))
    send_2 = project(attended, stay)
    (leaving,) = project(attended, leave, [swap(x, CORE) for x in send_1])
    from_corner = turn(leaving, 0)
    two, one, home = project(attended, stay, [swap(x, CORE) for x in send_2])
    got_1 = turn(one, 0)
    got_2 = turn((two + from_corner.astype(f32)).astype(bf16), 1)
    home = home + got_1.astype(f32) + got_2.astype(f32)
    out = home[0]
    for i, o in enumerate(far):
        if o:
            out = out + swap(home[i].astype(bf16), o).astype(f32)
    return out.astype(bf16)


def solution(mesh):
    return jax.shard_map(
        functools.partial(per_device, mesh.shape["wide"]),
        mesh=mesh,
        in_specs=(
            P("groups", "wide"),
            P(),
            P(None, "wide"),
            P("wide", None),
            P("wide", None),
            P("wide", None),
        ),
        out_specs=P("groups", "wide"),
        check_vma=False,
    )
```

time: 127 us -> 97.3 us (0.77)
  starting transfers between devices: 50.8 us -> 27.9 us
  waiting for transfers between devices: 39.4 us -> 33.3 us
  Pallas kernels: 28.7 us -> 26.2 us
  local copies, waits for them, and re-layouts: 6.01 us -> 7.59 us
    ppermute x36 -> x21, starting transfers between devices: 36.3 us -> 18.2 us  [swap(): return lax.ppermute(x, 'wide', [(i, i ^ offset) for i in range(n)])]
    ppermute x36 -> x21, waiting for transfers between devices: 29.9 us -> 17.1 us  [swap(): return lax.ppermute(x, 'wide', [(i, i ^ offset) for i in range(n)])]
    ppermute x12 -> x6, waiting for transfers between devices: 9.5 us -> 16.2 us  [turn(): lax.ppermute(x, 'wide', [(i, i ^ side[(step + (i & CORE)) % 2]) for i in...]
    ppermute x12 -> x6, starting transfers between devices: 14.5 us -> 9.74 us  [turn(): lax.ppermute(x, 'wide', [(i, i ^ side[(step + (i & CORE)) % 2]) for i in...]
    pallas_call x8 -> x10, Pallas kernels: 27.7 us -> 23.6 us  [the longest x2 12.1 us: fetched(): pl.pallas_call(fetch_kernel, out_shape=jax.ShapeDtypeStruct(weight.shape,...]
    unnamed x10 -> x18, local copies, waits for them, and re-layouts: 5.03 us -> 7.53 us
    pallas_call x1, Pallas kernels: 1.02 us -> 2.57 us  [kv_terms(): pl.pallas_call(functools.partial(kv_kernel, shared), out_shape=[jax.Shape...]
  transfers between devices with their start and end apart: 48 -> 27, of which waited for: 14 -> 11; matrix products, arithmetic and copies ran while one was open for 1% -> 1% of each run, Pallas kernels for 16% -> 24%
where the time goes in v3:
time: 97.3 us; the launch traced here: 97.1 us
  waiting for transfers between devices  33.3 us (34%)
  starting transfers between devices  27.9 us (29%)
  Pallas kernels  26.2 us (27%)
  local copies, waits for them, and re-layouts  7.59 us (8%)
  other arithmetic  1.81 us (2%)
    ppermute x21, starting transfers between devices, swap(): return lax.ppermute(x, 'wide', [(i, i ^ offset) for i in range(n)])  18.2 us
    ppermute x21, waiting for transfers between devices, swap(): return lax.ppermute(x, 'wide', [(i, i ^ offset) for i in range(n)])  17.1 us
    ppermute x6, waiting for transfers between devices, turn(): lax.ppermute(x, 'wide', [(i, i ^ side[(step + (i & CORE)) % 2]) for i in...  16.2 us
    pallas_call x2, Pallas kernels, fetched(): pl.pallas_call(fetch_kernel, out_shape=jax.ShapeDtypeStruct(weight.shape,...  12.1 us
    ppermute x6, starting transfers between devices, turn(): lax.ppermute(x, 'wide', [(i, i ^ side[(step + (i & CORE)) % 2]) for i in...  9.74 us
    unnamed x18, local copies, waits for them, and re-layouts  7.53 us
    pallas_call x4, Pallas kernels, query_call(): pl.pallas_call(functools.partial(query_kernel, places, bool(carry), bool(...  6.44 us
    pallas_call x4, Pallas kernels, output_call(): pl.pallas_call(functools.partial(output_kernel, [(s, a is not None) for s...  5.09 us
  transfers between devices with their start and end apart: 27, of which 11 were waited for; matrix products, arithmetic and copies ran while one was open for 1% of the time, Pallas kernels for 24%

profile of v3, /device:TPU:0, one launch (start us, length us, event | category | flops | bytes accessed | tf_op | source)
XLA Modules:
  0.0 97.1 jit_solution(108594263139521258)
XLA Ops:
  0.0 4.0 %collective-permute-start.1 = (bf16[128,512]{1,0:T(8,128)(2,1)}, bf16[128,512]{1,0:T(8,128)(2,1)S(1)}, u32[]{:S(2)}, u32[]{:S(2)}) collective-permute-start(bf16[128,512]{1,0:T(8,128)(2,1)} %act.1), channel_id=1, source_target_pairs={{0,16},{1,17},{2,18},{3,19},{4,20},{5,21},{6,22},{7,23},{8,24},{9,... | collective-permute-start | bytes 393224 | tf_op jit(solution)/shard_map/ppermute | solution.py:250
  4.0 1.6 %collective-permute-start = (bf16[128,512]{1,0:T(8,128)(2,1)}, bf16[128,512]{1,0:T(8,128)(2,1)S(1)}, u32[]{:S(2)}, u32[]{:S(2)}) collective-permute-start(bf16[128,512]{1,0:T(8,128)(2,1)} %act.1), channel_id=1, source_target_pairs={{0,8},{1,9},{2,10},{3,11},{4,12},{5,13},{6,14},{7,15},{8,0},{9,1},... | collective-permute-start | bytes 393224 | tf_op jit(solution)/shard_map/ppermute | solution.py:250
  5.7 0.8 copy-done.1
  6.5 0.9 copy-done.3
  7.4 2.6 %shard_map.69 = (f32[8,128,128]{2,1,0:T(8,128)S(1)}, f32[8,128,128]{2,1,0:T(8,128)S(1)}) custom-call(s32[3]{0:T(128)S(1)} %pad_add_fusion.refs_0_.where, bf16[128,512]{1,0:T(8,128)(2,1)S(1)} %copy-done.3, f32[1,16384]{1,0:T(1,128)S(1)} %bitcast.44, bf16[512,1024]{1,0:T(8,128)(2,1)} %wk.1, bf16[512,1024]{1,0:T(8,128)(2,1)} %wv.1), custom_call_target="tpu_custom_call" | custom-call | flops 268435456 | bytes 2097152 | tf_op jit(solution)/shard_map/pallas_call | solution.py:100
  10.1 5.9 %shard_map.64.refs_4_.refs_5_.refs_3_ = bf16[16384,512]{1,0:T(8,128)(2,1)S(1)} custom-call(bf16[16384,512]{1,0:T(8,128)(2,1)} %source.2), custom_call_target="tpu_custom_call" | custom-call | bytes 33554432 | tf_op jit(solution)/shard_map/pallas_call | solution.py:62
  16.1 5.8 %copy-done = bf16[16384,512]{1,0:T(8,128)(2,1)} copy-done((bf16[16384,512]{1,0:T(8,128)(2,1)}, bf16[16384,512]{1,0:T(8,128)(2,1)S(1)}, u32[]{:S(2)}) %copy-start) | copy-done | bytes 16777240
  21.9 1.8 %collective-permute-start.3 = (bf16[4,128,512]{2,1,0:T(8,128)(2,1)S(1)}, bf16[4,128,512]{2,1,0:T(8,128)(2,1)S(1)}, u32[]{:S(2)}, u32[]{:S(2)}) collective-permute-start(bf16[4,128,512]{2,1,0:T(8,128)(2,1)S(1)} %pad_maximum_fusion.refs_2_), channel_id=1, source_target_pairs={{0,2},{1,5},{2,0},{3,7},{4,6},{5,1},{6,4},{7,3},{8,10},{9,13},{10,... | collective-permute-start | bytes 1572872 | tf_op jit(solution)/shard_map/ppermute | solution.py:253
  23.7 0.2 collective-permute-start.6
  23.9 1.3 %collective-permute-start.5 = (bf16[4,128,512]{2,1,0:T(8,128)(2,1)S(1)}, bf16[4,128,512]{2,1,0:T(8,128)(2,1)S(1)}, u32[]{:S(2)}, u32[]{:S(2)}) collective-permute-start(bf16[4,128,512]{2,1,0:T(8,128)(2,1)S(1)} %pad_maximum_fusion.refs_2_), channel_id=1, source_target_pairs={{0,4},{1,3},{2,6},{3,1},{4,0},{5,7},{6,2},{7,5},{8,12},{9,11},{10,... | collective-permute-start | bytes 1572872 | tf_op jit(solution)/shard_map/ppermute | solution.py:253
  25.4 0.7 collective-permute-start.11
  26.1 0.3 fusion.9
  26.4 6.1 %shard_map.65.refs_0_.refs_3_.refs_1_ = bf16[512,16384]{1,0:T(8,128)(2,1)S(1)} custom-call(bf16[512,16384]{1,0:T(8,128)(2,1)} %source.3), custom_call_target="tpu_custom_call" | custom-call | bytes 33554432 | tf_op jit(solution)/shard_map/pallas_call | solution.py:62
  32.6 2.9 %collective-permute-done.3.refs_2_ = bf16[4,128,512]{2,1,0:T(8,128)(2,1)S(1)} collective-permute-done((bf16[4,128,512]{2,1,0:T(8,128)(2,1)S(1)}, bf16[4,128,512]{2,1,0:T(8,128)(2,1)S(1)}, u32[]{:S(2)}, u32[]{:S(2)}) %collective-permute-start.3) | collective-permute-done | bytes 524320 | tf_op jit(solution)/shard_map/ppermute | solution.py:253
  35.5 2.0 %collective-permute-start.4 = (bf16[4,128,512]{2,1,0:T(8,128)(2,1)S(1)}, bf16[4,128,512]{2,1,0:T(8,128)(2,1)S(1)}, u32[]{:S(2)}, u32[]{:S(2)}) collective-permute-start(bf16[4,128,512]{2,1,0:T(8,128)(2,1)S(1)} %collective-permute-done.3.refs_2_), channel_id=1, source_target_pairs={{0,4},{1,3},{2,6},{3,1},{4,0},{5,7},{6,2},{7,5},{8,12},{9,11},{10,... | collective-permute-start | bytes 1572872 | tf_op jit(solution)/shard_map/ppermute | solution.py:253
  37.5 1.6 %collective-permute-done.11 = bf16[4,128,128]{2,1,0:T(8,128)(2,1)S(1)} collective-permute-done((bf16[4,128,128]{2,1,0:T(8,128)(2,1)S(1)}, bf16[4,128,128]{2,1,0:T(8,128)(2,1)S(1)}, u32[]{:S(2)}, u32[]{:S(2)}) %collective-permute-start.11) | collective-permute-done | bytes 131104 | tf_op jit(solution)/shard_map/ppermute | solution.py:250
  39.2 1.0 collective-permute-start.12
  40.1 3.0 %collective-permute-start.14 = (bf16[128,128]{1,0:T(8,128)(2,1)S(1)}, bf16[128,128]{1,0:T(8,128)(2,1)S(1)}, u32[]{:S(2)}, u32[]{:S(2)}) collective-permute-start(bf16[128,128]{1,0:T(8,128)(2,1)S(1)} %get-tuple-element.57), channel_id=1, source_target_pairs={{0,24},{1,25},{2,26},{3,27},{4,28},{5,29},{6,30},{7,31},{8,16},{9,... | collective-permute-start | bytes 98312 | tf_op jit(solution)/shard_map/ppermute | solution.py:250
  43.1 0.5 collective-permute-start.13
  43.7 1.3 %shard_map.66 = (f32[128,512]{1,0:T(8,128)S(1)}, f32[128,128]{1,0:T(8,128)S(1)}) custom-call(s32[3]{0:T(128)S(1)} %pad_add_fusion.refs_0_.where, f32[1,16384]{1,0:T(1,128)S(1)} %bitcast.45, bf16[4,128,512]{2,1,0:T(8,128)(2,1)S(1)} %pad_maximum_fusion.refs_2_, bf16[4,128,512]{2,1,0:T(8,128)(2,1)S(1)} %collective-permute-done.6.refs_3_, ...), custom_call_target="tpu_custom_call" | custom-call | flops 536870912 | bytes 4194304 | tf_op jit(solution)/shard_map/pallas_call | solution.py:186
  45.0 1.3 %shard_map.67 = (f32[128,512]{1,0:T(8,128)S(1)}, f32[128,128]{1,0:T(8,128)S(1)}) custom-call(s32[3]{0:T(128)S(1)} %pad_add_fusion.refs_0_.where, f32[1,16384]{1,0:T(1,128)S(1)} %bitcast.46, bf16[4,128,512]{2,1,0:T(8,128)(2,1)S(1)} %collective-permute-done.3.refs_2_, bf16[4,128,512]{2,1,0:T(8,128)(2,1)S(1)} %collective-permute-done.5.refs_3_, ...), custom_call_target="tpu_custom_call" | custom-call | flops 536870912 | bytes 4194304 | tf_op jit(solution)/shard_map/pallas_call | solution.py:186
  46.3 0.6 collective-permute-start.8
  47.0 1.0 collective-permute-done.13
  48.0 1.6 %collective-permute-start.15 = (bf16[128,128]{1,0:T(8,128)(2,1)S(1)}, bf16[128,128]{1,0:T(8,128)(2,1)S(1)}, u32[]{:S(2)}, u32[]{:S(2)}) collective-permute-start(bf16[128,128]{1,0:T(8,128)(2,1)S(1)} %fusion.10), channel_id=1, source_target_pairs={{0,2},{1,3},{2,0},{3,1},{4,6},{5,7},{6,4},{7,5},{8,10},{9,11},{10,... | collective-permute-start | bytes 98312 | tf_op jit(solution)/shard_map/ppermute | solution.py:250
  49.6 2.3 %collective-permute-done.15 = bf16[128,128]{1,0:T(8,128)(2,1)S(1)} collective-permute-done((bf16[128,128]{1,0:T(8,128)(2,1)S(1)}, bf16[128,128]{1,0:T(8,128)(2,1)S(1)}, u32[]{:S(2)}, u32[]{:S(2)}) %collective-permute-start.15) | collective-permute-done | bytes 32800 | tf_op jit(solution)/shard_map/ppermute | solution.py:250
  52.1 1.6 %shard_map.68 = (f32[128,512]{1,0:T(8,128)S(1)}, f32[128,128]{1,0:T(8,128)S(1)}) custom-call(s32[3]{0:T(128)S(1)} %pad_add_fusion.refs_0_.where, f32[1,16384]{1,0:T(1,128)S(1)} %bitcast.47, bf16[4,128,512]{2,1,0:T(8,128)(2,1)S(1)} %collective-permute-done.8.refs_2_, bf16[4,128,512]{2,1,0:T(8,128)(2,1)S(1)} %collective-permute-done.9.refs_3_, ...), custom_call_target="tpu_custom_call" | custom-call | flops 805306368 | bytes 6291456 | tf_op jit(solution)/shard_map/pallas_call | solution.py:186
  53.7 2.2 %shard_map.70.attended = bf16[128,512]{1,0:T(8,128)(2,1)S(1)} custom-call(s32[3]{0:T(128)S(1)} %pad_add_fusion.refs_0_.where, f32[1,16384]{1,0:T(1,128)S(1)} %bitcast.48, bf16[4,128,512]{2,1,0:T(8,128)(2,1)S(1)} %collective-permute-done.7.refs_2_, bf16[16384,512]{1,0:T(8,128)(2,1)S(1)} %bitcast.43, f32[128,512]{1,0:T(8,128)S(1)} %get-tuple-element.36.refs_4_, ...), custom_call_target="tpu_custom_call" | custom-call | flops 268435456 | bytes 2097152 | tf_op jit(solution)/shard_map/pallas_call | solution.py:186
  55.9 1.0 %shard_map.71 = bf16[4,128,512]{2,1,0:T(8,128)(2,1)S(1)} custom-call(s32[3]{0:T(128)S(1)} %pad_add_fusion.refs_0_.where, bf16[128,512]{1,0:T(8,128)(2,1)S(1)} %shard_map.70.attended, bf16[512,16384]{1,0:T(8,128)(2,1)S(1)} %shard_map.65.refs_0_.refs_3_.refs_1_), custom_call_target="tpu_custom_call" | custom-call | flops 268435456 | bytes 2097152 | tf_op jit(solution)/shard_map/pallas_call | solution.py:218
  56.9 0.6 collective-permute-start.21
  57.5 1.5 %shard_map.72 = (bf16[4,128,512]{2,1,0:T(8,128)(2,1)S(1)}, bf16[4,128,512]{2,1,0:T(8,128)(2,1)S(1)}, bf16[4,128,512]{2,1,0:T(8,128)(2,1)S(1)}) custom-call(s32[3]{0:T(128)S(1)} %pad_add_fusion.refs_0_.where, bf16[128,512]{1,0:T(8,128)(2,1)S(1)} %shard_map.70.attended, bf16[512,16384]{1,0:T(8,128)(2,1)S(1)} %shard_map.65.refs_0_.refs_3_.refs_1_), custom_call_target="tpu_custom_call" | custom-call | flops 805306368 | bytes 6291456 | tf_op jit(solution)/shard_map/pallas_call | solution.py:218
  59.1 0.5 collective-permute-start.18
  59.7 1.0 %shard_map.74 = bf16[4,128,512]{2,1,0:T(8,128)(2,1)S(1)} custom-call(s32[3]{0:T(128)S(1)} %pad_add_fusion.refs_0_.where, bf16[128,512]{1,0:T(8,128)(2,1)S(1)} %shard_map.70.attended, bf16[4,128,512]{2,1,0:T(8,128)(2,1)S(1)} %collective-permute-done.21.refs_0_, bf16[512,16384]{1,0:T(8,128)(2,1)S(1)} %shard_map.65.refs_0_.refs_3_.refs_1_), custom_call_target="tpu_custom_call" | custom-call | flops 268435456 | bytes 2097152 | tf_op jit(solution)/shard_map/pallas_call | solution.py:218
  60.7 1.5 %collective-permute-start.22 = (bf16[4,128,512]{2,1,0:T(8,128)(2,1)S(1)}, bf16[4,128,512]{2,1,0:T(8,128)(2,1)S(1)}, u32[]{:S(2)}, u32[]{:S(2)}) collective-permute-start(bf16[4,128,512]{2,1,0:T(8,128)(2,1)S(1)} %shard_map.74), channel_id=1, source_target_pairs={{0,2},{1,5},{2,0},{3,7},{4,6},{5,1},{6,4},{7,3},{8,10},{9,13},{10,... | collective-permute-start | bytes 1572872 | tf_op jit(solution)/shard_map/ppermute | solution.py:253
  62.3 0.3 collective-permute-done.19.refs_2_
  62.5 1.5 %shard_map.73 = (f32[4,128,512]{2,1,0:T(8,128)S(1)}, bf16[4,128,512]{2,1,0:T(8,128)(2,1)S(1)}, f32[4,128,512]{2,1,0:T(8,128)S(1)}) custom-call(s32[3]{0:T(128)S(1)} %pad_add_fusion.refs_0_.where, bf16[128,512]{1,0:T(8,128)(2,1)S(1)} %shard_map.70.attended, bf16[4,128,512]{2,1,0:T(8,128)(2,1)S(1)} %collective-permute-done.17.refs_0_, ...), custom_call_target="tpu_custom_call" | custom-call | flops 805306368 | bytes 6291456 | tf_op jit(solution)/shard_map/pallas_call | solution.py:218
  64.1 1.5 %collective-permute-start.20 = (bf16[4,128,512]{2,1,0:T(8,128)(2,1)S(1)}, bf16[4,128,512]{2,1,0:T(8,128)(2,1)S(1)}, u32[]{:S(2)}, u32[]{:S(2)}) collective-permute-start(bf16[4,128,512]{2,1,0:T(8,128)(2,1)S(1)} %get-tuple-element.46), channel_id=1, source_target_pairs={{0,2},{1,5},{2,0},{3,7},{4,6},{5,1},{6,4},{7,3},{8,10},{9,13},{10,... | collective-permute-start | bytes 1572872 | tf_op jit(solution)/shard_map/ppermute | solution.py:253
  65.6 4.3 %collective-permute-done.22 = bf16[4,128,512]{2,1,0:T(8,128)(2,1)S(1)} collective-permute-done((bf16[4,128,512]{2,1,0:T(8,128)(2,1)S(1)}, bf16[4,128,512]{2,1,0:T(8,128)(2,1)S(1)}, u32[]{:S(2)}, u32[]{:S(2)}) %collective-permute-start.22) | collective-permute-done | bytes 524320 | tf_op jit(solution)/shard_map/ppermute | solution.py:253
  70.2 1.6 %collective-permute-start.23 = (bf16[4,128,512]{2,1,0:T(8,128)(2,1)S(1)}, bf16[4,128,512]{2,1,0:T(8,128)(2,1)S(1)}, u32[]{:S(2)}, u32[]{:S(2)}) collective-permute-start(bf16[4,128,512]{2,1,0:T(8,128)(2,1)S(1)} %add_convert_fusion), channel_id=1, source_target_pairs={{0,4},{1,3},{2,6},{3,1},{4,0},{5,7},{6,2},{7,5},{8,12},{9,11},{10,... | collective-permute-start | bytes 1572872 | tf_op jit(solution)/shard_map/ppermute | solution.py:253
  71.7 6.9 %collective-permute-done.20 = bf16[4,128,512]{2,1,0:T(8,128)(2,1)S(1)} collective-permute-done((bf16[4,128,512]{2,1,0:T(8,128)(2,1)S(1)}, bf16[4,128,512]{2,1,0:T(8,128)(2,1)S(1)}, u32[]{:S(2)}, u32[]{:S(2)}) %collective-permute-start.20) | collective-permute-done | bytes 524320 | tf_op jit(solution)/shard_map/ppermute | solution.py:253
  78.7 2.0 %collective-permute-done.23 = bf16[4,128,512]{2,1,0:T(8,128)(2,1)S(1)} collective-permute-done((bf16[4,128,512]{2,1,0:T(8,128)(2,1)S(1)}, bf16[4,128,512]{2,1,0:T(8,128)(2,1)S(1)}, u32[]{:S(2)}, u32[]{:S(2)}) %collective-permute-start.23) | collective-permute-done | bytes 524320 | tf_op jit(solution)/shard_map/ppermute | solution.py:253
  80.7 0.2 fusion.11
  80.9 1.1 %collective-permute-start.24 = (bf16[128,512]{1,0:T(8,128)(2,1)S(1)}, bf16[128,512]{1,0:T(8,128)(2,1)S(1)}, u32[]{:S(2)}, u32[]{:S(2)}) collective-permute-start(bf16[128,512]{1,0:T(8,128)(2,1)S(1)} %get-tuple-element.53), channel_id=1, source_target_pairs={{0,8},{1,9},{2,10},{3,11},{4,12},{5,13},{6,14},{7,15},{8,0},{9,1},... | collective-permute-start | bytes 393224 | tf_op jit(solution)/shard_map/ppermute | solution.py:250
  82.1 1.9 %collective-permute-start.26 = (bf16[128,512]{1,0:T(8,128)(2,1)S(1)}, bf16[128,512]{1,0:T(8,128)(2,1)S(1)}, u32[]{:S(2)}, u32[]{:S(2)}) collective-permute-start(bf16[128,512]{1,0:T(8,128)(2,1)S(1)} %get-tuple-element.54), channel_id=1, source_target_pairs={{0,24},{1,25},{2,26},{3,27},{4,28},{5,29},{6,30},{7,31},{8,16},{9,... | collective-permute-start | bytes 393224 | tf_op jit(solution)/shard_map/ppermute | solution.py:250
  83.9 0.6 collective-permute-start.25
  84.5 2.3 %collective-permute-done.24 = bf16[128,512]{1,0:T(8,128)(2,1)S(1)} collective-permute-done((bf16[128,512]{1,0:T(8,128)(2,1)S(1)}, bf16[128,512]{1,0:T(8,128)(2,1)S(1)}, u32[]{:S(2)}, u32[]{:S(2)}) %collective-permute-start.24) | collective-permute-done | bytes 131104 | tf_op jit(solution)/shard_map/ppermute | solution.py:250
  86.8 4.4 %collective-permute-done.26 = bf16[128,512]{1,0:T(8,128)(2,1)S(1)} collective-permute-done((bf16[128,512]{1,0:T(8,128)(2,1)S(1)}, bf16[128,512]{1,0:T(8,128)(2,1)S(1)}, u32[]{:S(2)}, u32[]{:S(2)}) %collective-permute-start.26) | collective-permute-done | bytes 131104 | tf_op jit(solution)/shard_map/ppermute | solution.py:250
  91.1 5.2 %collective-permute-done.25 = bf16[128,512]{1,0:T(8,128)(2,1)S(1)} collective-permute-done((bf16[128,512]{1,0:T(8,128)(2,1)S(1)}, bf16[128,512]{1,0:T(8,128)(2,1)S(1)}, u32[]{:S(2)}, u32[]{:S(2)}) %collective-permute-start.25) | collective-permute-done | bytes 131104 | tf_op jit(solution)/shard_map/ppermute | solution.py:250
  96.4 0.7 fusion.3
  (51 shorter events, 1.1 us)
Async XLA Ops:
  0.0 21.8 %collective-permute-start.1 = (bf16[128,512]{1,0:T(8,128)(2,1)}, bf16[128,512]{1,0:T(8,128)(2,1)S(1)}, u32[]{:S(2)}, u32[]{:S(2)}) collective-permute-start(bf16[128,512]{1,0:T(8,128)(2,1)} %act.1), channel_id=1, source_target_pairs={{0,16},{1,17},{2,18},{3,19},{4,20},{5,21},{6,22},{7,23},{8,24},{9,... | collective-permute-start | bytes 393224 | tf_op jit(solution)/shard_map/ppermute | solution.py:250
  4.0 17.8 %collective-permute-start = (bf16[128,512]{1,0:T(8,128)(2,1)}, bf16[128,512]{1,0:T(8,128)(2,1)S(1)}, u32[]{:S(2)}, u32[]{:S(2)}) collective-permute-start(bf16[128,512]{1,0:T(8,128)(2,1)} %act.1), channel_id=1, source_target_pairs={{0,8},{1,9},{2,10},{3,11},{4,12},{5,13},{6,14},{7,15},{8,0},{9,1},... | collective-permute-start | bytes 393224 | tf_op jit(solution)/shard_map/ppermute | solution.py:250
  5.6 16.2 %collective-permute-start.2 = (bf16[128,512]{1,0:T(8,128)(2,1)}, bf16[128,512]{1,0:T(8,128)(2,1)S(1)}, u32[]{:S(2)}, u32[]{:S(2)}) collective-permute-start(bf16[128,512]{1,0:T(8,128)(2,1)} %act.1), channel_id=1, source_target_pairs={{0,24},{1,25},{2,26},{3,27},{4,28},{5,29},{6,30},{7,31},{8,16},{9,... | collective-permute-start | bytes 393224 | tf_op jit(solution)/shard_map/ppermute | solution.py:250
  5.7 0.8 copy-start.1
  6.5 0.9 copy-start.3
  10.0 11.8 %copy-start.4 = (bf16[128,512]{1,0:T(8,128)(2,1)S(1)}, bf16[128,512]{1,0:T(8,128)(2,1)}, u32[]{:S(2)}) copy-start(bf16[128,512]{1,0:T(8,128)(2,1)} %act.1) | copy-start | bytes 393220
  10.0 15.3 %collective-permute-start.10 = (f32[8,128,128]{2,1,0:T(8,128)S(1)}, f32[8,128,128]{2,1,0:T(8,128)S(1)}, u32[]{:S(2)}, u32[]{:S(2)}) collective-permute-start(f32[8,128,128]{2,1,0:T(8,128)S(1)} %get-tuple-element.39), channel_id=1, source_target_pairs={{0,1},{1,0},{2,3},{3,2},{4,5},{5,4},{6,7},{7,6},{8,9},{9,8},{10,11... | collective-permute-start | bytes 1572872 | tf_op jit(solution)/shard_map/ppermute | solution.py:250
  16.0 5.8 %copy-start = (bf16[16384,512]{1,0:T(8,128)(2,1)}, bf16[16384,512]{1,0:T(8,128)(2,1)S(1)}, u32[]{:S(2)}) copy-start(bf16[16384,512]{1,0:T(8,128)(2,1)S(1)} %shard_map.64.refs_4_.refs_5_.refs_3_) | copy-start | bytes 50331652
  21.9 13.6 %collective-permute-start.3 = (bf16[4,128,512]{2,1,0:T(8,128)(2,1)S(1)}, bf16[4,128,512]{2,1,0:T(8,128)(2,1)S(1)}, u32[]{:S(2)}, u32[]{:S(2)}) collective-permute-start(bf16[4,128,512]{2,1,0:T(8,128)(2,1)S(1)} %pad_maximum_fusion.refs_2_), channel_id=1, source_target_pairs={{0,2},{1,5},{2,0},{3,7},{4,6},{5,1},{6,4},{7,3},{8,10},{9,13},{10,... | collective-permute-start | bytes 1572872 | tf_op jit(solution)/shard_map/ppermute | solution.py:253
  23.7 19.4 %collective-permute-start.6 = (bf16[4,128,512]{2,1,0:T(8,128)(2,1)S(1)}, bf16[4,128,512]{2,1,0:T(8,128)(2,1)S(1)}, u32[]{:S(2)}, u32[]{:S(2)}) collective-permute-start(bf16[4,128,512]{2,1,0:T(8,128)(2,1)S(1)} %pad_maximum_fusion.refs_2_), channel_id=1, source_target_pairs={{0,1},{1,0},{2,3},{3,2},{4,5},{5,4},{6,7},{7,6},{8,9},{9,8},{10,11... | collective-permute-start | bytes 1572872 | tf_op jit(solution)/shard_map/ppermute | solution.py:250
  23.9 19.7 %collective-permute-start.5 = (bf16[4,128,512]{2,1,0:T(8,128)(2,1)S(1)}, bf16[4,128,512]{2,1,0:T(8,128)(2,1)S(1)}, u32[]{:S(2)}, u32[]{:S(2)}) collective-permute-start(bf16[4,128,512]{2,1,0:T(8,128)(2,1)S(1)} %pad_maximum_fusion.refs_2_), channel_id=1, source_target_pairs={{0,4},{1,3},{2,6},{3,1},{4,0},{5,7},{6,2},{7,5},{8,12},{9,11},{10,... | collective-permute-start | bytes 1572872 | tf_op jit(solution)/shard_map/ppermute | solution.py:253
  25.3 18.3 %slice-start = ((s8[16777216]{0:T(1024)(128)(4,1)}), s8[4194304]{0:T(1024)(128)(4,1)S(1)}, s32[]{:S(2)}) async-start(s8[16777216]{0:T(1024)(128)(4,1)} %bitcast.42), calls=%async_computation | async-start | bytes 8388608
  25.4 13.7 %collective-permute-start.11 = (bf16[4,128,128]{2,1,0:T(8,128)(2,1)S(1)}, bf16[4,128,128]{2,1,0:T(8,128)(2,1)S(1)}, u32[]{:S(2)}, u32[]{:S(2)}) collective-permute-start(bf16[4,128,128]{2,1,0:T(8,128)(2,1)S(1)} %slice.85), channel_id=1, source_target_pairs={{0,4},{1,5},{2,6},{3,7},{4,0},{5,1},{6,2},{7,3},{8,12},{9,13},{10,... | collective-permute-start | bytes 393224 | tf_op jit(solution)/shard_map/ppermute | solution.py:250
  26.4 17.2 %slice-start.1 = ((s8[16777216]{0:T(1024)(128)(4,1)}), s8[4194304]{0:T(1024)(128)(4,1)S(1)}, s32[]{:S(2)}) async-start(s8[16777216]{0:T(1024)(128)(4,1)} %bitcast.42), calls=%async_computation.1 | async-start | bytes 8388608
  26.4 17.2 %slice-start.2 = ((s8[16777216]{0:T(1024)(128)(4,1)}), s8[4194304]{0:T(1024)(128)(4,1)S(1)}, s32[]{:S(2)}) async-start(s8[16777216]{0:T(1024)(128)(4,1)} %bitcast.42), calls=%async_computation.2 | async-start | bytes 8388608
  26.4 17.2 %slice-start.3 = ((s8[16777216]{0:T(1024)(128)(4,1)}), s8[4194304]{0:T(1024)(128)(4,1)S(1)}, s32[]{:S(2)}) async-start(s8[16777216]{0:T(1024)(128)(4,1)} %bitcast.42), calls=%async_computation.3 | async-start | bytes 8388608
  26.4 17.2 %copy-start.2 = (f32[16384]{0:T(1024)S(1)}, f32[16384]{0:T(1024)}, u32[]{:S(2)}) copy-start(f32[16384]{0:T(1024)} %param.7) | copy-start | bytes 196612
  35.5 10.9 %collective-permute-start.4 = (bf16[4,128,512]{2,1,0:T(8,128)(2,1)S(1)}, bf16[4,128,512]{2,1,0:T(8,128)(2,1)S(1)}, u32[]{:S(2)}, u32[]{:S(2)}) collective-permute-start(bf16[4,128,512]{2,1,0:T(8,128)(2,1)S(1)} %collective-permute-done.3.refs_2_), channel_id=1, source_target_pairs={{0,4},{1,3},{2,6},{3,1},{4,0},{5,7},{6,2},{7,5},{8,12},{9,11},{10,... | collective-permute-start | bytes 1572872 | tf_op jit(solution)/shard_map/ppermute | solution.py:253
  39.2 7.7 %collective-permute-start.12 = (bf16[128,128]{1,0:T(8,128)(2,1)S(1)}, bf16[128,128]{1,0:T(8,128)(2,1)S(1)}, u32[]{:S(2)}, u32[]{:S(2)}) collective-permute-start(bf16[128,128]{1,0:T(8,128)(2,1)S(1)} %get-tuple-element.56), channel_id=1, source_target_pairs={{0,8},{1,9},{2,10},{3,11},{4,12},{5,13},{6,14},{7,15},{8,0},{9,1},... | collective-permute-start | bytes 98312 | tf_op jit(solution)/shard_map/ppermute | solution.py:250
  40.1 6.9 %collective-permute-start.14 = (bf16[128,128]{1,0:T(8,128)(2,1)S(1)}, bf16[128,128]{1,0:T(8,128)(2,1)S(1)}, u32[]{:S(2)}, u32[]{:S(2)}) collective-permute-start(bf16[128,128]{1,0:T(8,128)(2,1)S(1)} %get-tuple-element.57), channel_id=1, source_target_pairs={{0,24},{1,25},{2,26},{3,27},{4,28},{5,29},{6,30},{7,31},{8,16},{9,... | collective-permute-start | bytes 98312 | tf_op jit(solution)/shard_map/ppermute | solution.py:250
  43.1 4.8 %collective-permute-start.13 = (bf16[128,128]{1,0:T(8,128)(2,1)S(1)}, bf16[128,128]{1,0:T(8,128)(2,1)S(1)}, u32[]{:S(2)}, u32[]{:S(2)}) collective-permute-start(bf16[128,128]{1,0:T(8,128)(2,1)S(1)} %get-tuple-element.58), channel_id=1, source_target_pairs={{0,16},{1,17},{2,18},{3,19},{4,20},{5,21},{6,22},{7,23},{8,24},{9,... | collective-permute-start | bytes 98312 | tf_op jit(solution)/shard_map/ppermute | solution.py:250
  43.6 8.4 %collective-permute-start.9 = (bf16[4,128,512]{2,1,0:T(8,128)(2,1)S(1)}, bf16[4,128,512]{2,1,0:T(8,128)(2,1)S(1)}, u32[]{:S(2)}, u32[]{:S(2)}) collective-permute-start(bf16[4,128,512]{2,1,0:T(8,128)(2,1)S(1)} %collective-permute-done.5.refs_3_), channel_id=1, source_target_pairs={{0,1},{1,0},{2,3},{3,2},{4,5},{5,4},{6,7},{7,6},{8,9},{9,8},{10,11... | collective-permute-start | bytes 1572872 | tf_op jit(solution)/shard_map/ppermute | solution.py:250
  46.3 5.7 %collective-permute-start.8 = (bf16[4,128,512]{2,1,0:T(8,128)(2,1)S(1)}, bf16[4,128,512]{2,1,0:T(8,128)(2,1)S(1)}, u32[]{:S(2)}, u32[]{:S(2)}) collective-permute-start(bf16[4,128,512]{2,1,0:T(8,128)(2,1)S(1)} %collective-permute-done.3.refs_2_), channel_id=1, source_target_pairs={{0,1},{1,0},{2,3},{3,2},{4,5},{5,4},{6,7},{7,6},{8,9},{9,8},{10,11... | collective-permute-start | bytes 1572872 | tf_op jit(solution)/shard_map/ppermute | solution.py:250
  46.9 6.8 %collective-permute-start.7 = (bf16[4,128,512]{2,1,0:T(8,128)(2,1)S(1)}, bf16[4,128,512]{2,1,0:T(8,128)(2,1)S(1)}, u32[]{:S(2)}, u32[]{:S(2)}) collective-permute-start(bf16[4,128,512]{2,1,0:T(8,128)(2,1)S(1)} %collective-permute-done.4.refs_4_), channel_id=1, source_target_pairs={{0,1},{1,0},{2,3},{3,2},{4,5},{5,4},{6,7},{7,6},{8,9},{9,8},{10,11... | collective-permute-start | bytes 1572872 | tf_op jit(solution)/shard_map/ppermute | solution.py:250
  48.0 4.0 %collective-permute-start.15 = (bf16[128,128]{1,0:T(8,128)(2,1)S(1)}, bf16[128,128]{1,0:T(8,128)(2,1)S(1)}, u32[]{:S(2)}, u32[]{:S(2)}) collective-permute-start(bf16[128,128]{1,0:T(8,128)(2,1)S(1)} %fusion.10), channel_id=1, source_target_pairs={{0,2},{1,3},{2,0},{3,1},{4,6},{5,7},{6,4},{7,5},{8,10},{9,11},{10,... | collective-permute-start | bytes 98312 | tf_op jit(solution)/shard_map/ppermute | solution.py:250
  52.0 1.7 %collective-permute-start.16 = (f32[128,128]{1,0:T(8,128)S(1)}, f32[128,128]{1,0:T(8,128)S(1)}, u32[]{:S(2)}, u32[]{:S(2)}) collective-permute-start(f32[128,128]{1,0:T(8,128)S(1)} %convert_add_fusion.1.refs_6_), channel_id=1, source_target_pairs={{0,1},{1,0},{2,3},{3,2},{4,5},{5,4},{6,7},{7,6},{8,9},{9,8},{10,11... | collective-permute-start | bytes 196616 | tf_op jit(solution)/shard_map/ppermute | solution.py:250
  56.9 2.8 %collective-permute-start.21 = (bf16[4,128,512]{2,1,0:T(8,128)(2,1)S(1)}, bf16[4,128,512]{2,1,0:T(8,128)(2,1)S(1)}, u32[]{:S(2)}, u32[]{:S(2)}) collective-permute-start(bf16[4,128,512]{2,1,0:T(8,128)(2,1)S(1)} %shard_map.71), channel_id=1, source_target_pairs={{0,1},{1,0},{2,3},{3,2},{4,5},{5,4},{6,7},{7,6},{8,9},{9,8},{10,11... | collective-permute-start | bytes 1572872 | tf_op jit(solution)/shard_map/ppermute | solution.py:250
  59.1 3.2 %collective-permute-start.17 = (bf16[4,128,512]{2,1,0:T(8,128)(2,1)S(1)}, bf16[4,128,512]{2,1,0:T(8,128)(2,1)S(1)}, u32[]{:S(2)}, u32[]{:S(2)}) collective-permute-start(bf16[4,128,512]{2,1,0:T(8,128)(2,1)S(1)} %get-tuple-element.42), channel_id=1, source_target_pairs={{0,1},{1,0},{2,3},{3,2},{4,5},{5,4},{6,7},{7,6},{8,9},{9,8},{10,11... | collective-permute-start | bytes 1572872 | tf_op jit(solution)/shard_map/ppermute | solution.py:250
  59.1 3.1 %collective-permute-start.18 = (bf16[4,128,512]{2,1,0:T(8,128)(2,1)S(1)}, bf16[4,128,512]{2,1,0:T(8,128)(2,1)S(1)}, u32[]{:S(2)}, u32[]{:S(2)}) collective-permute-start(bf16[4,128,512]{2,1,0:T(8,128)(2,1)S(1)} %get-tuple-element.43), channel_id=1, source_target_pairs={{0,1},{1,0},{2,3},{3,2},{4,5},{5,4},{6,7},{7,6},{8,9},{9,8},{10,11... | collective-permute-start | bytes 1572872 | tf_op jit(solution)/shard_map/ppermute | solution.py:250
  59.6 2.9 %collective-permute-start.19 = (bf16[4,128,512]{2,1,0:T(8,128)(2,1)S(1)}, bf16[4,128,512]{2,1,0:T(8,128)(2,1)S(1)}, u32[]{:S(2)}, u32[]{:S(2)}) collective-permute-start(bf16[4,128,512]{2,1,0:T(8,128)(2,1)S(1)} %get-tuple-element.44), channel_id=1, source_target_pairs={{0,1},{1,0},{2,3},{3,2},{4,5},{5,4},{6,7},{7,6},{8,9},{9,8},{10,11... | collective-permute-start | bytes 1572872 | tf_op jit(solution)/shard_map/ppermute | solution.py:250
  60.7 9.2 %collective-permute-start.22 = (bf16[4,128,512]{2,1,0:T(8,128)(2,1)S(1)}, bf16[4,128,512]{2,1,0:T(8,128)(2,1)S(1)}, u32[]{:S(2)}, u32[]{:S(2)}) collective-permute-start(bf16[4,128,512]{2,1,0:T(8,128)(2,1)S(1)} %shard_map.74), channel_id=1, source_target_pairs={{0,2},{1,5},{2,0},{3,7},{4,6},{5,1},{6,4},{7,3},{8,10},{9,13},{10,... | collective-permute-start | bytes 1572872 | tf_op jit(solution)/shard_map/ppermute | solution.py:253
  64.1 14.6 %collective-permute-start.20 = (bf16[4,128,512]{2,1,0:T(8,128)(2,1)S(1)}, bf16[4,128,512]{2,1,0:T(8,128)(2,1)S(1)}, u32[]{:S(2)}, u32[]{:S(2)}) collective-permute-start(bf16[4,128,512]{2,1,0:T(8,128)(2,1)S(1)} %get-tuple-element.46), channel_id=1, source_target_pairs={{0,2},{1,5},{2,0},{3,7},{4,6},{5,1},{6,4},{7,3},{8,10},{9,13},{10,... | collective-permute-start | bytes 1572872 | tf_op jit(solution)/shard_map/ppermute | solution.py:253
  70.2 10.5 %collective-permute-start.23 = (bf16[4,128,512]{2,1,0:T(8,128)(2,1)S(1)}, bf16[4,128,512]{2,1,0:T(8,128)(2,1)S(1)}, u32[]{:S(2)}, u32[]{:S(2)}) collective-permute-start(bf16[4,128,512]{2,1,0:T(8,128)(2,1)S(1)} %add_convert_fusion), channel_id=1, source_target_pairs={{0,4},{1,3},{2,6},{3,1},{4,0},{5,7},{6,2},{7,5},{8,12},{9,11},{10,... | collective-permute-start | bytes 1572872 | tf_op jit(solution)/shard_map/ppermute | solution.py:253
  80.9 5.8 %collective-permute-start.24 = (bf16[128,512]{1,0:T(8,128)(2,1)S(1)}, bf16[128,512]{1,0:T(8,128)(2,1)S(1)}, u32[]{:S(2)}, u32[]{:S(2)}) collective-permute-start(bf16[128,512]{1,0:T(8,128)(2,1)S(1)} %get-tuple-element.53), channel_id=1, source_target_pairs={{0,8},{1,9},{2,10},{3,11},{4,12},{5,13},{6,14},{7,15},{8,0},{9,1},... | collective-permute-start | bytes 393224 | tf_op jit(solution)/shard_map/ppermute | solution.py:250
  82.1 9.1 %collective-permute-start.26 = (bf16[128,512]{1,0:T(8,128)(2,1)S(1)}, bf16[128,512]{1,0:T(8,128)(2,1)S(1)}, u32[]{:S(2)}, u32[]{:S(2)}) collective-permute-start(bf16[128,512]{1,0:T(8,128)(2,1)S(1)} %get-tuple-element.54), channel_id=1, source_target_pairs={{0,24},{1,25},{2,26},{3,27},{4,28},{5,29},{6,30},{7,31},{8,16},{9,... | collective-permute-start | bytes 393224 | tf_op jit(solution)/shard_map/ppermute | solution.py:250
  83.9 12.4 %collective-permute-start.25 = (bf16[128,512]{1,0:T(8,128)(2,1)S(1)}, bf16[128,512]{1,0:T(8,128)(2,1)S(1)}, u32[]{:S(2)}, u32[]{:S(2)}) collective-permute-start(bf16[128,512]{1,0:T(8,128)(2,1)S(1)} %get-tuple-element.55), channel_id=1, source_target_pairs={{0,16},{1,17},{2,18},{3,19},{4,20},{5,21},{6,22},{7,23},{8,24},{9,... | collective-permute-start | bytes 393224 | tf_op jit(solution)/shard_map/ppermute | solution.py:250

commit v4 on v3

v4 whole, which is shorter than its diff:
```python
import functools

import jax
import jax.numpy as jnp
from jax import lax
from jax.experimental import pallas as pl
from jax.experimental.pallas import tpu as pltpu
from jax.sharding import PartitionSpec as P

HEADS = 128
KVH = 8
HEAD = 128
LANE = 128
EPS = 1e-05
MIB = 1 << 20
CORE = 1


def combos(bits):
    out = [0]
    for b in bits:
        out = out + [o ^ b for o in out]
    return out


def vmem():
    return pl.BlockSpec(memory_space=pltpu.VMEM)


def smem():
    return pl.BlockSpec(memory_space=pltpu.SMEM)


def hbm():
    return pl.BlockSpec(memory_space=pltpu.HBM)


def in_hbm(x):
    return pltpu.with_memory_space_constraint(x, pltpu.HBM)


def dot(a, b):
    return jnp.dot(a, b, preferred_element_type=jnp.float32)


def kv_kernel(shared, where, act, gain, wk, wv, send, keep, abuf, gbuf, kbuf, vbuf, sems):
    me = where[0]
    width = act.shape[1]
    own = pl.ds(pl.multiple_of(me * width, LANE), width)
    pairs = [(act, abuf), (gain.at[:, own], gbuf), (wk, kbuf), (wv, vbuf)]
    copies = [pltpu.make_async_copy(x, y, sems.at[i]) for i, (x, y) in enumerate(pairs)]
    for c in copies:
        c.start()
    for c in copies:
        c.wait()
    scaled = (abuf[...].astype(jnp.float32) * gbuf[...]).astype(jnp.bfloat16)
    k, v = dot(scaled, kbuf[...]), dot(scaled, vbuf[...])
    core0 = (me & CORE) == 0
    for h in range(KVH):
        off = h ^ (me >> shared)
        spot = 0
        for b in range(KVH.bit_length() - 1):
            spot = spot * 2 + (1 - ((off >> b) & 1))
        kh, vh = k[:, h * HEAD : (h + 1) * HEAD], v[:, h * HEAD : (h + 1) * HEAD]
        keep[spot] = jnp.where(core0, kh, vh)
        send[spot] = jnp.where(core0, vh, kh)


def kv_terms(shared, where, act, gain, wk, wv):
    tokens, width = act.shape
    return pl.pallas_call(
        functools.partial(kv_kernel, shared),
        out_shape=[jax.ShapeDtypeStruct((KVH, tokens, HEAD), jnp.float32)] * 2,
        in_specs=[smem()] + [hbm()] * 4,
        out_specs=[vmem(), vmem()],
        scratch_shapes=[
            pltpu.VMEM(act.shape, act.dtype),
            pltpu.VMEM((1, width), gain.dtype),
            pltpu.VMEM(wk.shape, wk.dtype),
            pltpu.VMEM(wv.shape, wv.dtype),
            pltpu.SemaphoreType.DMA((4,)),
        ],
        compiler_params=pltpu.CompilerParams(vmem_limit_bytes=12 * MIB),
        cost_estimate=pl.CostEstimate(
            flops=4 * tokens * wk.size, bytes_accessed=4 * wk.size, transcendentals=0
        ),
    )(where, in_hbm(act), in_hbm(gain), in_hbm(wk), in_hbm(wv))


def attend(queries, k_sum, v_sum, cosine, sine, scale):
    k_rows = (k_sum * scale).astype(jnp.bfloat16).astype(jnp.float32)
    value = (v_sum * scale).astype(jnp.bfloat16)

    def rotate(x):
        half = HEAD // 2
        turned = jnp.concatenate([x[:, half:], x[:, :half]], axis=1)
        return (x * cosine + turned * sine).astype(jnp.bfloat16)

    key = rotate(k_rows)
    tokens = key.shape[0]
    rows = lax.broadcasted_iota(jnp.int32, (tokens, tokens), 0)
    cols = lax.broadcasted_iota(jnp.int32, (tokens, tokens), 1)
    out = []
    for h in range(queries.shape[1] // HEAD):
        q = rotate(queries[:, h * HEAD : (h + 1) * HEAD] * scale)
        scores = lax.dot_general(
            q, key, (((1,), (1,)), ((), ())), preferred_element_type=jnp.float32
        ) * HEAD ** (-0.5)
        scores = jnp.where(rows >= cols, scores, -1e30)
        weights = jnp.exp(scores - jnp.max(scores, axis=1, keepdims=True))
        probs = (weights / jnp.sum(weights, axis=1, keepdims=True)).astype(jnp.bfloat16)
        out.append(dot(probs, value).astype(jnp.bfloat16))
    return jnp.concatenate(out, axis=1)


def query_kernel(places, ahead, carried, last, *refs):
    refs = list(refs)
    where, gain = refs.pop(0), refs.pop(0)
    pieces = [refs.pop(0) for _ in places]
    weight = refs.pop(0)
    queries = refs.pop(0)[...] if carried else None
    squares = refs.pop(0)[...] if carried else None
    extra = [refs.pop(0) for _ in range(4)] if last else None
    outs = [refs.pop(0) for _ in range(1 if last else 3 if ahead else 2)]
    width = pieces[0].shape[2]

    def first_row(symbol):
        return pl.multiple_of((where[symbol[1]] ^ symbol[0]) * width, LANE)

    copies = []
    if refs:
        buf, sems = refs
        wanted = [s for symbols, held in places for s in symbols]
        for i, symbol in enumerate(wanted + list(ahead)):
            target, row = (buf, i) if i < len(wanted) else (outs[2], i - len(wanted))
            copy = pltpu.make_async_copy(
                weight.at[pl.ds(first_row(symbol), width), :],
                target.at[pl.ds(row * width, width), :],
                sems.at[i],
            )
            copy.start()
            copies.append(copy)
    i = 0
    for piece, (symbols, held) in zip(pieces, places):
        for block, symbol in enumerate(symbols):
            x = piece[block].astype(jnp.float32)
            for c in range(0, width, LANE):
                square = x[:, c : c + LANE] * x[:, c : c + LANE]
                squares = square if squares is None else squares + square
            scaled = (x * gain[:, pl.ds(first_row(symbol), width)]).astype(jnp.bfloat16)
            if copies:
                copies[i].wait()
                rows = buf[i * width : (i + 1) * width, :]
            else:
                rows = weight[(held + block) * width : (held + block + 1) * width, :]
            term = dot(scaled, rows)
            queries = term if queries is None else queries + term
            i += 1
    for copy in copies[i:]:
        copy.wait()
    if last:
        mean = jnp.sum(squares, axis=1, keepdims=True) * (1.0 / gain.shape[1])
        mine, other, cosine, sine = extra
        core0 = (where[0] & CORE) == 0
        k_sum = jnp.where(core0, mine[...], other[...])
        v_sum = jnp.where(core0, other[...], mine[...])
        outs[0][...] = attend(
            queries, k_sum, v_sum, cosine[...], sine[...], lax.rsqrt(mean + EPS)
        )
    else:
        outs[0][...] = queries
        outs[1][...] = squares


def query_call(where, gain, pieces, weight, carry=(), extra=(), ahead=(), held=None):
    arrays, places, row = [], [], held or 0
    for array, symbols in pieces:
        arrays.append(array)
        places.append((symbols, row))
        row += len(symbols)
    tokens, width, columns = *arrays[0].shape[1:], weight.shape[1]
    blocks = sum(len(symbols) for symbols, _ in places)
    if extra:
        out_shape = [jax.ShapeDtypeStruct((tokens, columns), jnp.bfloat16)]
    else:
        out_shape = [
            jax.ShapeDtypeStruct((tokens, columns), jnp.float32),
            jax.ShapeDtypeStruct((tokens, LANE), jnp.float32),
        ]
    if ahead:
        out_shape += [jax.ShapeDtypeStruct((len(ahead) * width, columns), weight.dtype)]
    scratch = []
    if held is None:
        weight = in_hbm(weight)
        scratch = [
            pltpu.VMEM((blocks * width, columns), weight.dtype),
            pltpu.SemaphoreType.DMA((blocks + len(ahead),)),
        ]
    return pl.pallas_call(
        functools.partial(query_kernel, places, ahead, bool(carry), bool(extra)),
        out_shape=out_shape,
        in_specs=[smem()]
        + [vmem()] * (1 + len(arrays))
        + [hbm() if held is None else vmem()]
        + [vmem()] * (len(carry) + len(extra)),
        out_specs=[vmem()] * len(out_shape),
        scratch_shapes=scratch,
        compiler_params=pltpu.CompilerParams(vmem_limit_bytes=16 * MIB),
        cost_estimate=pl.CostEstimate(
            flops=2 * tokens * columns * width * blocks,
            bytes_accessed=2 * columns * width * (blocks + len(ahead)),
            transcendentals=0,
        ),
    )(where, gain, *arrays, weight, *carry, *extra)


def output_kernel(groups, width, where, attended, *refs):
    refs = list(refs)
    added = [refs.pop(0) if g[1] else None for g in groups]
    weight = refs.pop(0)
    left = attended[...]
    for (symbols, _), arrived, out in zip(groups, added, refs):
        for block, (const, pick) in enumerate(symbols):
            span = pl.ds(pl.multiple_of((where[pick] ^ const) * width, LANE), width)
            term = dot(left, weight[:, span])
            if arrived is not None:
                term = term + arrived[block].astype(jnp.float32)
            out[block] = term.astype(out.dtype)


def output_call(where, attended, weight, width, groups):
    tokens, depth = attended.shape
    blocks = sum(len(g[0]) for g in groups)
    added = [g[2] for g in groups if g[2] is not None]
    return pl.pallas_call(
        functools.partial(output_kernel, [(s, a is not None) for s, _, a in groups], width),
        out_shape=[jax.ShapeDtypeStruct((len(s), tokens, width), t) for s, t, _ in groups],
        in_specs=[smem()] + [vmem()] * (2 + len(added)),
        out_specs=[vmem()] * len(groups),
        compiler_params=pltpu.CompilerParams(vmem_limit_bytes=12 * MIB),
        cost_estimate=pl.CostEstimate(
            flops=2 * tokens * depth * width * blocks,
            bytes_accessed=2 * depth * width * blocks,
            transcendentals=0,
        ),
    )(where, attended, *added, weight)


def rotary_tables(tokens):
    half = HEAD // 2
    frequency = 500000.0 ** (-(jnp.arange(half, dtype=jnp.float32) * 2.0) / HEAD)
    angles = jnp.arange(tokens, dtype=jnp.float32)[:, None] * frequency[None, :]
    cosine, sine = jnp.cos(angles), jnp.sin(angles)
    return jnp.concatenate([cosine, cosine], axis=1), jnp.concatenate([-sine, sine], axis=1)


def per_device(n, act, norm_gain, wq, wk, wv, wo):
    tokens, width = act.shape
    me = lax.axis_index("wide")
    bits = [1 << i for i in range(n.bit_length() - 1)]
    side = (bits[1], bits[2])
    diagonal = bits[1] ^ bits[2]
    near, top = combos(bits[3:-1]), bits[-1]
    far = [o ^ top for o in near]
    f32, bf16 = jnp.float32, jnp.bfloat16

    def swap(x, offset):
        return lax.ppermute(x, "wide", [(i, i ^ offset) for i in range(n)])

    def turn(x, step):
        return lax.ppermute(x, "wide", [(i, i ^ side[(step + (i & CORE)) % 2]) for i in range(n)])

    bit = jnp.where((me & CORE) == 0, side[0], side[1])
    where = jnp.stack([me, me ^ bit, me ^ bit ^ diagonal]).astype(jnp.int32)
    gain = norm_gain.reshape(1, -1)

    def plain(offsets, pick=0):
        return [(o, pick) for o in offsets]

    def across(symbols):
        return [(const ^ CORE, (0, 2, 1)[pick]) for const, pick in symbols]

    shared = (n // KVH).bit_length() - 1
    kv_send, kv_keep = kv_terms(shared, where, act, gain, wk, wv)
    kv = kv_keep + swap(kv_send, CORE)
    for b in bits[shared:]:
        half = kv.shape[0] // 2
        kv = kv[half:] + swap(kv[:half].astype(bf16), b).astype(f32)
    total = kv[0]
    for b in bits[1:shared]:
        total = total + swap(total.astype(bf16), b).astype(f32)
    kv_sums = (total, swap(total, CORE))

    groups = []
    for offsets, first in ((near, act), (far, swap(act, top))):
        row = jnp.stack([first] + [swap(first, o) for o in near[1:]])
        side_1, side_2 = turn(row, 0), turn(row, 1)
        groups.append((offsets, row, side_1, side_2, turn(side_1, 1)))

    def pieces_of(group):
        offsets, row, side_1, side_2, corner = group
        return [
            (row, plain(offsets)),
            (side_1, plain(offsets, 1)),
            (side_2, plain(offsets, 2)),
            (corner, plain([o ^ diagonal for o in offsets])),
        ]

    def other(pieces):
        return [(swap(x, CORE), across(symbols)) for x, symbols in pieces]

    call = functools.partial(query_call, where, gain)
    early, last = pieces_of(groups[0]), pieces_of(groups[1])
    ahead = [s for _, symbols in last[1:3] for s in across(symbols)] + last[3][1]
    ahead += across(last[3][1])
    *carry, held = call(early + other(early), wq, ahead=ahead)
    carry = call(last[:3] + other(last[:1]), wq, carry=carry)
    corner, *carry = lax.optimization_barrier((last[3][0], *carry))
    corner = [(corner, last[3][1])]
    corner_other = other(corner)
    pieces = other(last[1:3]) + corner
    carry = call(pieces, held, carry=carry, held=0)
    (attended,) = call(
        corner_other,
        held,
        carry=carry,
        extra=(*kv_sums, *rotary_tables(tokens)),
        held=sum(len(symbols) for _, symbols in pieces),
    )

    def project(left, wanted, arrived=None):
        if arrived is None:
            wanted = [(across(s), bf16, None) for s, _ in wanted]
        else:
            wanted = [(*g, a) for g, a in zip(wanted, arrived)]
        return output_call(where, left, wo, width, wanted)

    def blocks_of(offsets):
        leave = [(plain([o ^ diagonal for o in offsets]), bf16)]
        stay = [(plain(offsets, 2), f32), (plain(offsets, 1), bf16), (plain(offsets), f32)]
        return leave, stay

    def round_square(offsets, left, sent):
        leave, stay = blocks_of(offsets)
        got = [swap(x, CORE) for x in sent]
        (leaving,) = project(left, leave, got[:1])
        from_corner = turn(leaving, 0)
        two, one, home = project(left, stay, got[1:])
        got_1 = turn(one, 0)
        got_2 = turn((two + from_corner.astype(f32)).astype(bf16), 1)
        return home + got_1.astype(f32) + got_2.astype(f32)

    def along_z(blocks):
        total = blocks[0]
        for i, o in enumerate(near):
            if o:
                total = total + swap(blocks[i].astype(bf16), o).astype(f32)
        return total

    left = attended
    sent = []
    for offsets in (far, near):
        leave, stay = blocks_of(offsets)
        sent.append(project(left, leave + stay))
        left, *sent[-1] = lax.optimization_barrier((left, *sent[-1]))
    total = along_z(round_square(far, attended, sent[0]))
    got = swap(total.astype(bf16), top)
    out = along_z(round_square(near, attended, sent[1])) + got.astype(f32)
    return out.astype(bf16)


def solution(mesh):
    return jax.shard_map(
        functools.partial(per_device, mesh.shape["wide"]),
        mesh=mesh,
        in_specs=(
            P("groups", "wide"),
            P(),
            P(None, "wide"),
            P("wide", None),
            P("wide", None),
            P("wide", None),
        ),
        out_specs=P("groups", "wide"),
        check_vma=False,
    )
```

time: 97.3 us -> 89.4 us (0.919)
  local copies, waits for them, and re-layouts: 7.59 us -> 0.94 us
  starting transfers between devices: 27.9 us -> 33.5 us
  Pallas kernels: 26.2 us -> 21.7 us
  waiting for transfers between devices: 33.3 us -> 30.1 us
    unnamed x18 -> x10, local copies, waits for them, and re-layouts: 7.53 us -> 0.86 us
    pallas_call x6 -> x4, Pallas kernels: 18.5 us -> 12.5 us  [query_call(): pl.pallas_call(functools.partial(query_kernel, places, ahead, bool(carry)...]
    ppermute x6 -> x12, starting transfers between devices: 9.74 us -> 14.1 us  [turn(): lax.ppermute(x, 'wide', [(i, i ^ side[(step + (i & CORE)) % 2]) for i in...]
    ppermute x6 -> x12, waiting for transfers between devices: 16.2 us -> 13.7 us  [turn(): lax.ppermute(x, 'wide', [(i, i ^ side[(step + (i & CORE)) % 2]) for i in...]
    pallas_call x4 -> x6, Pallas kernels: 5.09 us -> 6.53 us  [output_call(): pl.pallas_call(functools.partial(output_kernel, [(s, a is not None) for s...]
    ppermute x21 -> x28, starting transfers between devices: 18.2 us -> 19.4 us  [swap(): return lax.ppermute(x, 'wide', [(i, i ^ offset) for i in range(n)])]
    ppermute x21 -> x28, waiting for transfers between devices: 17.1 us -> 16.4 us  [swap(): return lax.ppermute(x, 'wide', [(i, i ^ offset) for i in range(n)])]
  transfers between devices with their start and end apart: 27 -> 40, of which waited for: 11 -> 12; matrix products, arithmetic and copies ran while one was open for 1% -> 2% of each run, Pallas kernels for 24% -> 18%
where the time goes in v4:
time: 89.4 us; the launch traced here: 89.2 us
  starting transfers between devices  33.5 us (37%)
  waiting for transfers between devices  30.1 us (34%)
  Pallas kernels  21.7 us (24%)
  other arithmetic  2.58 us (3%)
  local copies, waits for them, and re-layouts  0.94 us (1%)
    ppermute x28, starting transfers between devices, swap(): return lax.ppermute(x, 'wide', [(i, i ^ offset) for i in range(n)])  19.4 us
    ppermute x28, waiting for transfers between devices, swap(): return lax.ppermute(x, 'wide', [(i, i ^ offset) for i in range(n)])  16.4 us
    ppermute x12, starting transfers between devices, turn(): lax.ppermute(x, 'wide', [(i, i ^ side[(step + (i & CORE)) % 2]) for i in...  14.1 us
    ppermute x12, waiting for transfers between devices, turn(): lax.ppermute(x, 'wide', [(i, i ^ side[(step + (i & CORE)) % 2]) for i in...  13.7 us
    pallas_call x4, Pallas kernels, query_call(): pl.pallas_call(functools.partial(query_kernel, places, ahead, bool(carry)...  12.5 us
    pallas_call x6, Pallas kernels, output_call(): pl.pallas_call(functools.partial(output_kernel, [(s, a is not None) for s...  6.53 us
    pallas_call x1, Pallas kernels, kv_terms(): pl.pallas_call(functools.partial(kv_kernel, shared), out_shape=[jax.Shape...  2.66 us
  transfers between devices with their start and end apart: 40, of which 12 were waited for; matrix products, arithmetic and copies ran while one was open for 2% of the time, Pallas kernels for 18%

profile of v4, /device:TPU:0, one launch (start us, length us, event | category | flops | bytes accessed | tf_op | source)
XLA Modules:
  0.0 89.2 jit_solution(2989418863661655357)
XLA Ops:
  0.1 2.7 %shard_map.67 = (f32[8,128,128]{2,1,0:T(8,128)S(1)}, f32[8,128,128]{2,1,0:T(8,128)S(1)}) custom-call(s32[3]{0:T(128)S(1)} %pad_add_fusion.refs_0_.where, bf16[128,512]{1,0:T(8,128)(2,1)} %act.1, f32[1,16384]{1,0:T(1,128)} %bitcast.34, bf16[512,1024]{1,0:T(8,128)(2,1)} %wk.1, bf16[512,1024]{1,0:T(8,128)(2,1)} %wv.1), custom_call_target="tpu_custom_call" | custom-call | flops 268435456 | bytes 2097152 | tf_op jit(solution)/shard_map/pallas_call | solution.py:71
  2.7 0.5 collective-permute-start.17
  3.3 2.7 %collective-permute-start.6 = (bf16[128,512]{1,0:T(8,128)(2,1)}, bf16[128,512]{1,0:T(8,128)(2,1)S(1)}, u32[]{:S(2)}, u32[]{:S(2)}) collective-permute-start(bf16[128,512]{1,0:T(8,128)(2,1)} %act.1), channel_id=1, source_target_pairs={{0,8},{1,9},{2,10},{3,11},{4,12},{5,13},{6,14},{7,15},{8,0},{9,1},... | collective-permute-start | bytes 393224 | tf_op jit(solution)/shard_map/ppermute | solution.py:268
  5.9 2.6 %collective-permute-start = (bf16[128,512]{1,0:T(8,128)(2,1)}, bf16[128,512]{1,0:T(8,128)(2,1)S(1)}, u32[]{:S(2)}, u32[]{:S(2)}) collective-permute-start(bf16[128,512]{1,0:T(8,128)(2,1)} %act.1), channel_id=1, source_target_pairs={{0,16},{1,17},{2,18},{3,19},{4,20},{5,21},{6,22},{7,23},{8,24},{9,... | collective-permute-start | bytes 393224 | tf_op jit(solution)/shard_map/ppermute | solution.py:268
  8.5 4.2 %collective-permute-done.6 = bf16[128,512]{1,0:T(8,128)(2,1)S(1)} collective-permute-done((bf16[128,512]{1,0:T(8,128)(2,1)}, bf16[128,512]{1,0:T(8,128)(2,1)S(1)}, u32[]{:S(2)}, u32[]{:S(2)}) %collective-permute-start.6) | collective-permute-done | bytes 131104 | tf_op jit(solution)/shard_map/ppermute | solution.py:268
  12.7 0.9 %pad_maximum_fusion.1.refs_2_ = bf16[2,128,512]{2,1,0:T(8,128)(2,1)S(1)} fusion(bf16[1,128,512]{2,1,0:T(8,128)(2,1)S(1)} %bitcast.42, bf16[1,128,512]{2,1,0:T(8,128)(2,1)} %bitcast.39), kind=kLoop, calls=%fused_computation.16 | loop fusion | flops 131072 | bytes 524288 | tf_op jit(solution)/shard_map/stack | solution.py:296
  13.6 1.9 %collective-permute-start.7 = (bf16[2,128,512]{2,1,0:T(8,128)(2,1)S(1)}, bf16[2,128,512]{2,1,0:T(8,128)(2,1)S(1)}, u32[]{:S(2)}, u32[]{:S(2)}) collective-permute-start(bf16[2,128,512]{2,1,0:T(8,128)(2,1)S(1)} %pad_maximum_fusion.1.refs_2_), channel_id=1, source_target_pairs={{0,2},{1,5},{2,0},{3,7},{4,6},{5,1},{6,4},{7,3},{8,10},{9,13},{10,... | collective-permute-start | bytes 786440 | tf_op jit(solution)/shard_map/ppermute | solution.py:271
  16.0 1.6 %collective-permute-start.18 = (bf16[4,128,128]{2,1,0:T(8,128)(2,1)S(1)}, bf16[4,128,128]{2,1,0:T(8,128)(2,1)S(1)}, u32[]{:S(2)}, u32[]{:S(2)}) collective-permute-start(bf16[4,128,128]{2,1,0:T(8,128)(2,1)S(1)} %slice.85), channel_id=1, source_target_pairs={{0,4},{1,5},{2,6},{3,7},{4,0},{5,1},{6,2},{7,3},{8,12},{9,13},{10,... | collective-permute-start | bytes 393224 | tf_op jit(solution)/shard_map/ppermute | solution.py:268
  17.6 0.5 collective-permute-start.8
  18.1 2.4 %collective-permute-done.1 = bf16[128,512]{1,0:T(8,128)(2,1)S(1)} collective-permute-done((bf16[128,512]{1,0:T(8,128)(2,1)S(1)}, bf16[128,512]{1,0:T(8,128)(2,1)S(1)}, u32[]{:S(2)}, u32[]{:S(2)}) %collective-permute-start.1) | collective-permute-done | bytes 131104 | tf_op jit(solution)/shard_map/ppermute | solution.py:268
  20.6 1.5 %collective-permute-start.2 = (bf16[2,128,512]{2,1,0:T(8,128)(2,1)S(1)}, bf16[2,128,512]{2,1,0:T(8,128)(2,1)S(1)}, u32[]{:S(2)}, u32[]{:S(2)}) collective-permute-start(bf16[2,128,512]{2,1,0:T(8,128)(2,1)S(1)} %pad_maximum_fusion.refs_2_), channel_id=1, source_target_pairs={{0,2},{1,5},{2,0},{3,7},{4,6},{5,1},{6,4},{7,3},{8,10},{9,13},{10,... | collective-permute-start | bytes 786440 | tf_op jit(solution)/shard_map/ppermute | solution.py:271
  22.0 2.2 %collective-permute-start.9 = (bf16[2,128,512]{2,1,0:T(8,128)(2,1)S(1)}, bf16[2,128,512]{2,1,0:T(8,128)(2,1)S(1)}, u32[]{:S(2)}, u32[]{:S(2)}) collective-permute-start(bf16[2,128,512]{2,1,0:T(8,128)(2,1)S(1)} %collective-permute-done.7.refs_3_), channel_id=1, source_target_pairs={{0,4},{1,3},{2,6},{3,1},{4,0},{5,7},{6,2},{7,5},{8,12},{9,11},{10,... | collective-permute-start | bytes 786440 | tf_op jit(solution)/shard_map/ppermute | solution.py:271
  24.4 4.2 %collective-permute-done.19 = bf16[2,128,128]{2,1,0:T(8,128)(2,1)S(1)} collective-permute-done((bf16[2,128,128]{2,1,0:T(8,128)(2,1)S(1)}, bf16[2,128,128]{2,1,0:T(8,128)(2,1)S(1)}, u32[]{:S(2)}, u32[]{:S(2)}) %collective-permute-start.19) | collective-permute-done | bytes 65568 | tf_op jit(solution)/shard_map/ppermute | solution.py:268
  28.8 0.5 collective-permute-start.12
  29.3 0.7 collective-permute-done.9.refs_5_
  29.9 2.4 %collective-permute-start.20 = (bf16[1,128,128]{2,1,0:T(8,128)(2,1)S(1)}, bf16[1,128,128]{2,1,0:T(8,128)(2,1)S(1)}, u32[]{:S(2)}, u32[]{:S(2)}) collective-permute-start(bf16[1,128,128]{2,1,0:T(8,128)(2,1)S(1)} %slice.87), channel_id=1, source_target_pairs={{0,16},{1,17},{2,18},{3,19},{4,20},{5,21},{6,22},{7,23},{8,24},{9,... | collective-permute-start | bytes 98312 | tf_op jit(solution)/shard_map/ppermute | solution.py:268
  32.6 2.5 %collective-permute-done.4.refs_4_ = bf16[2,128,512]{2,1,0:T(8,128)(2,1)S(1)} collective-permute-done((bf16[2,128,512]{2,1,0:T(8,128)(2,1)S(1)}, bf16[2,128,512]{2,1,0:T(8,128)(2,1)S(1)}, u32[]{:S(2)}, u32[]{:S(2)}) %collective-permute-start.4) | collective-permute-done | bytes 262176 | tf_op jit(solution)/shard_map/ppermute | solution.py:271
  35.0 1.9 %collective-permute-start.3 = (bf16[2,128,512]{2,1,0:T(8,128)(2,1)S(1)}, bf16[2,128,512]{2,1,0:T(8,128)(2,1)S(1)}, u32[]{:S(2)}, u32[]{:S(2)}) collective-permute-start(bf16[2,128,512]{2,1,0:T(8,128)(2,1)S(1)} %collective-permute-done.2.refs_3_), channel_id=1, source_target_pairs={{0,4},{1,3},{2,6},{3,1},{4,0},{5,7},{6,2},{7,5},{8,12},{9,11},{10,... | collective-permute-start | bytes 786440 | tf_op jit(solution)/shard_map/ppermute | solution.py:271
  37.1 0.5 collective-permute-start.16
  37.6 1.5 %collective-permute-start.21 = (bf16[128,128]{1,0:T(8,128)(2,1)S(1)}, bf16[128,128]{1,0:T(8,128)(2,1)S(1)}, u32[]{:S(2)}, u32[]{:S(2)}) collective-permute-start(bf16[128,128]{1,0:T(8,128)(2,1)S(1)} %fusion.10), channel_id=1, source_target_pairs={{0,2},{1,3},{2,0},{3,1},{4,6},{5,7},{6,4},{7,5},{8,10},{9,11},{10,... | collective-permute-start | bytes 98312 | tf_op jit(solution)/shard_map/ppermute | solution.py:268
  39.1 0.8 copy-done
  39.9 5.6 %shard_map.64 = (f32[128,512]{1,0:T(8,128)S(1)}, f32[128,128]{1,0:T(8,128)S(1)}, bf16[4096,512]{1,0:T(8,128)(2,1)S(1)}) custom-call(s32[3]{0:T(128)S(1)} %pad_add_fusion.refs_0_.where, f32[1,16384]{1,0:T(1,128)S(1)} %bitcast.35, bf16[2,128,512]{2,1,0:T(8,128)(2,1)S(1)} %pad_maximum_fusion.1.refs_2_, bf16[2,128,512]{2,1,0:T(8,128)(2,1)S(1)} %collective-permute-done.7.refs_3_, ...), custom_call_target="tpu_custom_call" | custom-call | flops 1073741824 | bytes 12582912 | tf_op jit(solution)/shard_map/pallas_call | solution.py:199
  45.5 3.7 %shard_map.65 = (f32[128,512]{1,0:T(8,128)S(1)}, f32[128,128]{1,0:T(8,128)S(1)}) custom-call(s32[3]{0:T(128)S(1)} %pad_add_fusion.refs_0_.where, f32[1,16384]{1,0:T(1,128)S(1)} %bitcast.36, bf16[2,128,512]{2,1,0:T(8,128)(2,1)S(1)} %pad_maximum_fusion.refs_2_, bf16[2,128,512]{2,1,0:T(8,128)(2,1)S(1)} %collective-permute-done.2.refs_3_, ...), custom_call_target="tpu_custom_call" | custom-call | flops 536870912 | bytes 4194304 | tf_op jit(solution)/shard_map/pallas_call | solution.py:199
  49.4 0.5 collective-permute-start.22
  50.1 1.2 %shard_map.66 = (f32[128,512]{1,0:T(8,128)S(1)}, f32[128,128]{1,0:T(8,128)S(1)}) custom-call(s32[3]{0:T(128)S(1)} %pad_add_fusion.refs_0_.where, f32[1,16384]{1,0:T(1,128)S(1)} %bitcast.37, bf16[2,128,512]{2,1,0:T(8,128)(2,1)S(1)} %collective-permute-done.15.refs_2_, bf16[2,128,512]{2,1,0:T(8,128)(2,1)S(1)} %collective-permute-done.16.refs_3_, ...), custom_call_target="tpu_custom_call" | custom-call | flops 402653184 | bytes 3145728 | tf_op jit(solution)/shard_map/pallas_call | solution.py:199
  51.3 2.0 %shard_map.68.attended = bf16[128,512]{1,0:T(8,128)(2,1)S(1)} custom-call(s32[3]{0:T(128)S(1)} %pad_add_fusion.refs_0_.where, f32[1,16384]{1,0:T(1,128)S(1)} %bitcast.38, bf16[2,128,512]{2,1,0:T(8,128)(2,1)S(1)} %collective-permute-done.14.refs_2_, bf16[4096,512]{1,0:T(8,128)(2,1)S(1)} %get-tuple-element.45.refs_5_.refs_3_, ...), custom_call_target="tpu_custom_call" | custom-call | flops 134217728 | bytes 1048576 | tf_op jit(solution)/shard_map/pallas_call | solution.py:199
  53.3 1.3 %shard_map.69 = (bf16[2,128,512]{2,1,0:T(8,128)(2,1)S(1)}, bf16[2,128,512]{2,1,0:T(8,128)(2,1)S(1)}, bf16[2,128,512]{2,1,0:T(8,128)(2,1)S(1)}, bf16[2,128,512]{2,1,0:T(8,128)(2,1)S(1)}) custom-call(s32[3]{0:T(128)S(1)} %pad_add_fusion.refs_0_.where, bf16[128,512]{1,0:T(8,128)(2,1)S(1)} %shard_map.68.attended, bf16[512,16384]{1,0:T(8,128)(2,1)S(1)} %bitcast.33), custom_call_target="tpu_custom_call" | custom-call | flops 536870912 | bytes 4194304 | tf_op jit(solution)/shard_map/pallas_call | solution.py:235
  54.7 0.5 collective-permute-start.31
  55.7 1.3 %shard_map.70 = (bf16[2,128,512]{2,1,0:T(8,128)(2,1)S(1)}, bf16[2,128,512]{2,1,0:T(8,128)(2,1)S(1)}, bf16[2,128,512]{2,1,0:T(8,128)(2,1)S(1)}, bf16[2,128,512]{2,1,0:T(8,128)(2,1)S(1)}) custom-call(s32[3]{0:T(128)S(1)} %pad_add_fusion.refs_0_.where, bf16[128,512]{1,0:T(8,128)(2,1)S(1)} %shard_map.68.attended, bf16[512,16384]{1,0:T(8,128)(2,1)S(1)} %bitcast.33), custom_call_target="tpu_custom_call" | custom-call | flops 536870912 | bytes 4194304 | tf_op jit(solution)/shard_map/pallas_call | solution.py:235
  57.1 0.9 shard_map.74
  58.0 0.6 collective-permute-start.36
  59.3 1.1 %shard_map.73 = (f32[2,128,512]{2,1,0:T(8,128)S(1)}, bf16[2,128,512]{2,1,0:T(8,128)(2,1)S(1)}, f32[2,128,512]{2,1,0:T(8,128)S(1)}) custom-call(s32[3]{0:T(128)S(1)} %pad_add_fusion.refs_0_.where, bf16[128,512]{1,0:T(8,128)(2,1)S(1)} %shard_map.68.attended, bf16[2,128,512]{2,1,0:T(8,128)(2,1)S(1)} %collective-permute-done.31.refs_0_, ...), custom_call_target="tpu_custom_call" | custom-call | flops 402653184 | bytes 3145728 | tf_op jit(solution)/shard_map/pallas_call | solution.py:235
  60.4 1.5 %collective-permute-start.34 = (bf16[2,128,512]{2,1,0:T(8,128)(2,1)S(1)}, bf16[2,128,512]{2,1,0:T(8,128)(2,1)S(1)}, u32[]{:S(2)}, u32[]{:S(2)}) collective-permute-start(bf16[2,128,512]{2,1,0:T(8,128)(2,1)S(1)} %get-tuple-element.72), channel_id=1, source_target_pairs={{0,2},{1,5},{2,0},{3,7},{4,6},{5,1},{6,4},{7,3},{8,10},{9,13},{10,... | collective-permute-start | bytes 786440 | tf_op jit(solution)/shard_map/ppermute | solution.py:271
  61.9 0.9 shard_map.72
  62.8 1.7 %collective-permute-done.36 = bf16[2,128,512]{2,1,0:T(8,128)(2,1)S(1)} collective-permute-done((bf16[2,128,512]{2,1,0:T(8,128)(2,1)S(1)}, bf16[2,128,512]{2,1,0:T(8,128)(2,1)S(1)}, u32[]{:S(2)}, u32[]{:S(2)}) %collective-permute-start.36) | collective-permute-done | bytes 262176 | tf_op jit(solution)/shard_map/ppermute | solution.py:271
  64.4 0.5 collective-permute-start.28
  65.2 1.1 %shard_map.71 = (f32[2,128,512]{2,1,0:T(8,128)S(1)}, bf16[2,128,512]{2,1,0:T(8,128)(2,1)S(1)}, f32[2,128,512]{2,1,0:T(8,128)S(1)}) custom-call(s32[3]{0:T(128)S(1)} %pad_add_fusion.refs_0_.where, bf16[128,512]{1,0:T(8,128)(2,1)S(1)} %shard_map.68.attended, bf16[2,128,512]{2,1,0:T(8,128)(2,1)S(1)} %collective-permute-done.23.refs_0_, ...), custom_call_target="tpu_custom_call" | custom-call | flops 402653184 | bytes 3145728 | tf_op jit(solution)/shard_map/pallas_call | solution.py:235
  66.4 2.0 %collective-permute-start.26 = (bf16[2,128,512]{2,1,0:T(8,128)(2,1)S(1)}, bf16[2,128,512]{2,1,0:T(8,128)(2,1)S(1)}, u32[]{:S(2)}, u32[]{:S(2)}) collective-permute-start(bf16[2,128,512]{2,1,0:T(8,128)(2,1)S(1)} %get-tuple-element.65), channel_id=1, source_target_pairs={{0,2},{1,5},{2,0},{3,7},{4,6},{5,1},{6,4},{7,3},{8,10},{9,13},{10,... | collective-permute-start | bytes 786440 | tf_op jit(solution)/shard_map/ppermute | solution.py:271
  68.3 4.5 %collective-permute-done.28 = bf16[2,128,512]{2,1,0:T(8,128)(2,1)S(1)} collective-permute-done((bf16[2,128,512]{2,1,0:T(8,128)(2,1)S(1)}, bf16[2,128,512]{2,1,0:T(8,128)(2,1)S(1)}, u32[]{:S(2)}, u32[]{:S(2)}) %collective-permute-start.28) | collective-permute-done | bytes 262176 | tf_op jit(solution)/shard_map/ppermute | solution.py:271
  72.9 1.3 %collective-permute-start.29 = (bf16[2,128,512]{2,1,0:T(8,128)(2,1)S(1)}, bf16[2,128,512]{2,1,0:T(8,128)(2,1)S(1)}, u32[]{:S(2)}, u32[]{:S(2)}) collective-permute-start(bf16[2,128,512]{2,1,0:T(8,128)(2,1)S(1)} %add_convert_fusion.1), channel_id=1, source_target_pairs={{0,4},{1,3},{2,6},{3,1},{4,0},{5,7},{6,2},{7,5},{8,12},{9,11},{10,... | collective-permute-start | bytes 786440 | tf_op jit(solution)/shard_map/ppermute | solution.py:271
  74.5 0.6 collective-permute-start.38
  75.1 3.1 %collective-permute-done.26 = bf16[2,128,512]{2,1,0:T(8,128)(2,1)S(1)} collective-permute-done((bf16[2,128,512]{2,1,0:T(8,128)(2,1)S(1)}, bf16[2,128,512]{2,1,0:T(8,128)(2,1)S(1)}, u32[]{:S(2)}, u32[]{:S(2)}) %collective-permute-start.26) | collective-permute-done | bytes 262176 | tf_op jit(solution)/shard_map/ppermute | solution.py:271
  78.2 1.2 %collective-permute-done.29 = bf16[2,128,512]{2,1,0:T(8,128)(2,1)S(1)} collective-permute-done((bf16[2,128,512]{2,1,0:T(8,128)(2,1)S(1)}, bf16[2,128,512]{2,1,0:T(8,128)(2,1)S(1)}, u32[]{:S(2)}, u32[]{:S(2)}) %collective-permute-start.29) | collective-permute-done | bytes 262176 | tf_op jit(solution)/shard_map/ppermute | solution.py:271
  79.5 0.5 collective-permute-start.30
  80.0 3.0 %collective-permute-start.39 = (bf16[128,512]{1,0:T(8,128)(2,1)S(1)}, bf16[128,512]{1,0:T(8,128)(2,1)S(1)}, u32[]{:S(2)}, u32[]{:S(2)}) collective-permute-start(bf16[128,512]{1,0:T(8,128)(2,1)S(1)} %fusion.1), channel_id=1, source_target_pairs={{0,16},{1,17},{2,18},{3,19},{4,20},{5,21},{6,22},{7,23},{8,24},{9,... | collective-permute-start | bytes 393224 | tf_op jit(solution)/shard_map/ppermute | solution.py:268
  83.1 3.5 %collective-permute-done.30 = bf16[128,512]{1,0:T(8,128)(2,1)S(1)} collective-permute-done((bf16[128,512]{1,0:T(8,128)(2,1)S(1)}, bf16[128,512]{1,0:T(8,128)(2,1)S(1)}, u32[]{:S(2)}, u32[]{:S(2)}) %collective-permute-start.30) | collective-permute-done | bytes 131104 | tf_op jit(solution)/shard_map/ppermute | solution.py:268
  86.5 2.0 %collective-permute-done.39 = bf16[128,512]{1,0:T(8,128)(2,1)S(1)} collective-permute-done((bf16[128,512]{1,0:T(8,128)(2,1)S(1)}, bf16[128,512]{1,0:T(8,128)(2,1)S(1)}, u32[]{:S(2)}, u32[]{:S(2)}) %collective-permute-start.39) | collective-permute-done | bytes 131104 | tf_op jit(solution)/shard_map/ppermute | solution.py:268
  88.5 0.7 fusion.4
  (76 shorter events, 3.4 us)
Async XLA Ops:
  2.7 13.2 %collective-permute-start.17 = (f32[8,128,128]{2,1,0:T(8,128)S(1)}, f32[8,128,128]{2,1,0:T(8,128)S(1)}, u32[]{:S(2)}, u32[]{:S(2)}) collective-permute-start(f32[8,128,128]{2,1,0:T(8,128)S(1)} %get-tuple-element.51), channel_id=1, source_target_pairs={{0,1},{1,0},{2,3},{3,2},{4,5},{5,4},{6,7},{7,6},{8,9},{9,8},{10,11... | collective-permute-start | bytes 1572872 | tf_op jit(solution)/shard_map/ppermute | solution.py:268
  3.3 9.4 %collective-permute-start.6 = (bf16[128,512]{1,0:T(8,128)(2,1)}, bf16[128,512]{1,0:T(8,128)(2,1)S(1)}, u32[]{:S(2)}, u32[]{:S(2)}) collective-permute-start(bf16[128,512]{1,0:T(8,128)(2,1)} %act.1), channel_id=1, source_target_pairs={{0,8},{1,9},{2,10},{3,11},{4,12},{5,13},{6,14},{7,15},{8,0},{9,1},... | collective-permute-start | bytes 393224 | tf_op jit(solution)/shard_map/ppermute | solution.py:268
  5.9 9.7 %collective-permute-start = (bf16[128,512]{1,0:T(8,128)(2,1)}, bf16[128,512]{1,0:T(8,128)(2,1)S(1)}, u32[]{:S(2)}, u32[]{:S(2)}) collective-permute-start(bf16[128,512]{1,0:T(8,128)(2,1)} %act.1), channel_id=1, source_target_pairs={{0,16},{1,17},{2,18},{3,19},{4,20},{5,21},{6,22},{7,23},{8,24},{9,... | collective-permute-start | bytes 393224 | tf_op jit(solution)/shard_map/ppermute | solution.py:268
  13.6 8.4 %collective-permute-start.7 = (bf16[2,128,512]{2,1,0:T(8,128)(2,1)S(1)}, bf16[2,128,512]{2,1,0:T(8,128)(2,1)S(1)}, u32[]{:S(2)}, u32[]{:S(2)}) collective-permute-start(bf16[2,128,512]{2,1,0:T(8,128)(2,1)S(1)} %pad_maximum_fusion.1.refs_2_), channel_id=1, source_target_pairs={{0,2},{1,5},{2,0},{3,7},{4,6},{5,1},{6,4},{7,3},{8,10},{9,13},{10,... | collective-permute-start | bytes 786440 | tf_op jit(solution)/shard_map/ppermute | solution.py:271
  15.6 5.0 %collective-permute-start.1 = (bf16[128,512]{1,0:T(8,128)(2,1)S(1)}, bf16[128,512]{1,0:T(8,128)(2,1)S(1)}, u32[]{:S(2)}, u32[]{:S(2)}) collective-permute-start(bf16[128,512]{1,0:T(8,128)(2,1)S(1)} %collective-permute-done), channel_id=1, source_target_pairs={{0,8},{1,9},{2,10},{3,11},{4,12},{5,13},{6,14},{7,15},{8,0},{9,1},... | collective-permute-start | bytes 393224 | tf_op jit(solution)/shard_map/ppermute | solution.py:268
  16.0 8.3 %collective-permute-start.18 = (bf16[4,128,128]{2,1,0:T(8,128)(2,1)S(1)}, bf16[4,128,128]{2,1,0:T(8,128)(2,1)S(1)}, u32[]{:S(2)}, u32[]{:S(2)}) collective-permute-start(bf16[4,128,128]{2,1,0:T(8,128)(2,1)S(1)} %slice.85), channel_id=1, source_target_pairs={{0,4},{1,5},{2,6},{3,7},{4,0},{5,1},{6,2},{7,3},{8,12},{9,13},{10,... | collective-permute-start | bytes 393224 | tf_op jit(solution)/shard_map/ppermute | solution.py:268
  17.6 11.1 %collective-permute-start.8 = (bf16[2,128,512]{2,1,0:T(8,128)(2,1)S(1)}, bf16[2,128,512]{2,1,0:T(8,128)(2,1)S(1)}, u32[]{:S(2)}, u32[]{:S(2)}) collective-permute-start(bf16[2,128,512]{2,1,0:T(8,128)(2,1)S(1)} %pad_maximum_fusion.1.refs_2_), channel_id=1, source_target_pairs={{0,4},{1,3},{2,6},{3,1},{4,0},{5,7},{6,2},{7,5},{8,12},{9,11},{10,... | collective-permute-start | bytes 786440 | tf_op jit(solution)/shard_map/ppermute | solution.py:271
  18.1 10.7 %collective-permute-start.10 = (bf16[2,128,512]{2,1,0:T(8,128)(2,1)S(1)}, bf16[2,128,512]{2,1,0:T(8,128)(2,1)S(1)}, u32[]{:S(2)}, u32[]{:S(2)}) collective-permute-start(bf16[2,128,512]{2,1,0:T(8,128)(2,1)S(1)} %pad_maximum_fusion.1.refs_2_), channel_id=1, source_target_pairs={{0,1},{1,0},{2,3},{3,2},{4,5},{5,4},{6,7},{7,6},{8,9},{9,8},{10,11... | collective-permute-start | bytes 786440 | tf_op jit(solution)/shard_map/ppermute | solution.py:268
  20.6 9.4 %collective-permute-start.2 = (bf16[2,128,512]{2,1,0:T(8,128)(2,1)S(1)}, bf16[2,128,512]{2,1,0:T(8,128)(2,1)S(1)}, u32[]{:S(2)}, u32[]{:S(2)}) collective-permute-start(bf16[2,128,512]{2,1,0:T(8,128)(2,1)S(1)} %pad_maximum_fusion.refs_2_), channel_id=1, source_target_pairs={{0,2},{1,5},{2,0},{3,7},{4,6},{5,1},{6,4},{7,3},{8,10},{9,13},{10,... | collective-permute-start | bytes 786440 | tf_op jit(solution)/shard_map/ppermute | solution.py:271
  22.0 7.9 %collective-permute-start.9 = (bf16[2,128,512]{2,1,0:T(8,128)(2,1)S(1)}, bf16[2,128,512]{2,1,0:T(8,128)(2,1)S(1)}, u32[]{:S(2)}, u32[]{:S(2)}) collective-permute-start(bf16[2,128,512]{2,1,0:T(8,128)(2,1)S(1)} %collective-permute-done.7.refs_3_), channel_id=1, source_target_pairs={{0,4},{1,3},{2,6},{3,1},{4,0},{5,7},{6,2},{7,5},{8,12},{9,11},{10,... | collective-permute-start | bytes 786440 | tf_op jit(solution)/shard_map/ppermute | solution.py:271
  24.3 4.3 %collective-permute-start.19 = (bf16[2,128,128]{2,1,0:T(8,128)(2,1)S(1)}, bf16[2,128,128]{2,1,0:T(8,128)(2,1)S(1)}, u32[]{:S(2)}, u32[]{:S(2)}) collective-permute-start(bf16[2,128,128]{2,1,0:T(8,128)(2,1)S(1)} %slice.86), channel_id=1, source_target_pairs={{0,8},{1,9},{2,10},{3,11},{4,12},{5,13},{6,14},{7,15},{8,0},{9,1},... | collective-permute-start | bytes 196616 | tf_op jit(solution)/shard_map/ppermute | solution.py:268
  28.6 6.4 %collective-permute-start.4 = (bf16[2,128,512]{2,1,0:T(8,128)(2,1)S(1)}, bf16[2,128,512]{2,1,0:T(8,128)(2,1)S(1)}, u32[]{:S(2)}, u32[]{:S(2)}) collective-permute-start(bf16[2,128,512]{2,1,0:T(8,128)(2,1)S(1)} %pad_maximum_fusion.refs_2_), channel_id=1, source_target_pairs={{0,4},{1,3},{2,6},{3,1},{4,0},{5,7},{6,2},{7,5},{8,12},{9,11},{10,... | collective-permute-start | bytes 786440 | tf_op jit(solution)/shard_map/ppermute | solution.py:271
  28.7 8.3 %collective-permute-start.11 = (bf16[2,128,512]{2,1,0:T(8,128)(2,1)S(1)}, bf16[2,128,512]{2,1,0:T(8,128)(2,1)S(1)}, u32[]{:S(2)}, u32[]{:S(2)}) collective-permute-start(bf16[2,128,512]{2,1,0:T(8,128)(2,1)S(1)} %collective-permute-done.7.refs_3_), channel_id=1, source_target_pairs={{0,1},{1,0},{2,3},{3,2},{4,5},{5,4},{6,7},{7,6},{8,9},{9,8},{10,11... | collective-permute-start | bytes 786440 | tf_op jit(solution)/shard_map/ppermute | solution.py:268
  28.8 8.3 %collective-permute-start.12 = (bf16[2,128,512]{2,1,0:T(8,128)(2,1)S(1)}, bf16[2,128,512]{2,1,0:T(8,128)(2,1)S(1)}, u32[]{:S(2)}, u32[]{:S(2)}) collective-permute-start(bf16[2,128,512]{2,1,0:T(8,128)(2,1)S(1)} %collective-permute-done.8.refs_4_), channel_id=1, source_target_pairs={{0,1},{1,0},{2,3},{3,2},{4,5},{5,4},{6,7},{7,6},{8,9},{9,8},{10,11... | collective-permute-start | bytes 786440 | tf_op jit(solution)/shard_map/ppermute | solution.py:268
  29.9 7.6 %collective-permute-start.13 = (bf16[2,128,512]{2,1,0:T(8,128)(2,1)S(1)}, bf16[2,128,512]{2,1,0:T(8,128)(2,1)S(1)}, u32[]{:S(2)}, u32[]{:S(2)}) collective-permute-start(bf16[2,128,512]{2,1,0:T(8,128)(2,1)S(1)} %collective-permute-done.9.refs_5_), channel_id=1, source_target_pairs={{0,1},{1,0},{2,3},{3,2},{4,5},{5,4},{6,7},{7,6},{8,9},{9,8},{10,11... | collective-permute-start | bytes 786440 | tf_op jit(solution)/shard_map/ppermute | solution.py:268
  29.9 5.1 %collective-permute-start.20 = (bf16[1,128,128]{2,1,0:T(8,128)(2,1)S(1)}, bf16[1,128,128]{2,1,0:T(8,128)(2,1)S(1)}, u32[]{:S(2)}, u32[]{:S(2)}) collective-permute-start(bf16[1,128,128]{2,1,0:T(8,128)(2,1)S(1)} %slice.87), channel_id=1, source_target_pairs={{0,16},{1,17},{2,18},{3,19},{4,20},{5,21},{6,22},{7,23},{8,24},{9,... | collective-permute-start | bytes 98312 | tf_op jit(solution)/shard_map/ppermute | solution.py:268
  35.0 10.5 %collective-permute-start.5 = (bf16[2,128,512]{2,1,0:T(8,128)(2,1)S(1)}, bf16[2,128,512]{2,1,0:T(8,128)(2,1)S(1)}, u32[]{:S(2)}, u32[]{:S(2)}) collective-permute-start(bf16[2,128,512]{2,1,0:T(8,128)(2,1)S(1)} %pad_maximum_fusion.refs_2_), channel_id=1, source_target_pairs={{0,1},{1,0},{2,3},{3,2},{4,5},{5,4},{6,7},{7,6},{8,9},{9,8},{10,11... | collective-permute-start | bytes 786440 | tf_op jit(solution)/shard_map/ppermute | solution.py:268
  35.0 14.2 %collective-permute-start.3 = (bf16[2,128,512]{2,1,0:T(8,128)(2,1)S(1)}, bf16[2,128,512]{2,1,0:T(8,128)(2,1)S(1)}, u32[]{:S(2)}, u32[]{:S(2)}) collective-permute-start(bf16[2,128,512]{2,1,0:T(8,128)(2,1)S(1)} %collective-permute-done.2.refs_3_), channel_id=1, source_target_pairs={{0,4},{1,3},{2,6},{3,1},{4,0},{5,7},{6,2},{7,5},{8,12},{9,11},{10,... | collective-permute-start | bytes 786440 | tf_op jit(solution)/shard_map/ppermute | solution.py:271
  37.0 13.1 %collective-permute-start.15 = (bf16[2,128,512]{2,1,0:T(8,128)(2,1)S(1)}, bf16[2,128,512]{2,1,0:T(8,128)(2,1)S(1)}, u32[]{:S(2)}, u32[]{:S(2)}) collective-permute-start(bf16[2,128,512]{2,1,0:T(8,128)(2,1)S(1)} %collective-permute-done.2.refs_3_), channel_id=1, source_target_pairs={{0,1},{1,0},{2,3},{3,2},{4,5},{5,4},{6,7},{7,6},{8,9},{9,8},{10,11... | collective-permute-start | bytes 786440 | tf_op jit(solution)/shard_map/ppermute | solution.py:268
  37.1 13.0 %collective-permute-start.16 = (bf16[2,128,512]{2,1,0:T(8,128)(2,1)S(1)}, bf16[2,128,512]{2,1,0:T(8,128)(2,1)S(1)}, u32[]{:S(2)}, u32[]{:S(2)}) collective-permute-start(bf16[2,128,512]{2,1,0:T(8,128)(2,1)S(1)} %collective-permute-done.4.refs_4_), channel_id=1, source_target_pairs={{0,1},{1,0},{2,3},{3,2},{4,5},{5,4},{6,7},{7,6},{8,9},{9,8},{10,11... | collective-permute-start | bytes 786440 | tf_op jit(solution)/shard_map/ppermute | solution.py:268
  37.6 11.8 %collective-permute-start.21 = (bf16[128,128]{1,0:T(8,128)(2,1)S(1)}, bf16[128,128]{1,0:T(8,128)(2,1)S(1)}, u32[]{:S(2)}, u32[]{:S(2)}) collective-permute-start(bf16[128,128]{1,0:T(8,128)(2,1)S(1)} %fusion.10), channel_id=1, source_target_pairs={{0,2},{1,3},{2,0},{3,1},{4,6},{5,7},{6,4},{7,5},{8,10},{9,11},{10,... | collective-permute-start | bytes 98312 | tf_op jit(solution)/shard_map/ppermute | solution.py:268
  39.1 0.8 copy-start
  39.9 13.4 %slice-start = ((s8[16777216]{0:T(1024)(128)(4,1)}), s8[4194304]{0:T(1024)(128)(4,1)S(1)}, s32[]{:S(2)}) async-start(s8[16777216]{0:T(1024)(128)(4,1)} %bitcast.32), calls=%async_computation | async-start | bytes 8388608
  39.9 13.4 %slice-start.1 = ((s8[16777216]{0:T(1024)(128)(4,1)}), s8[4194304]{0:T(1024)(128)(4,1)S(1)}, s32[]{:S(2)}) async-start(s8[16777216]{0:T(1024)(128)(4,1)} %bitcast.32), calls=%async_computation.1 | async-start | bytes 8388608
  45.5 7.8 %slice-start.2 = ((s8[16777216]{0:T(1024)(128)(4,1)}), s8[4194304]{0:T(1024)(128)(4,1)S(1)}, s32[]{:S(2)}) async-start(s8[16777216]{0:T(1024)(128)(4,1)} %bitcast.32), calls=%async_computation.2 | async-start | bytes 8388608
  45.5 7.8 %slice-start.3 = ((s8[16777216]{0:T(1024)(128)(4,1)}), s8[4194304]{0:T(1024)(128)(4,1)S(1)}, s32[]{:S(2)}) async-start(s8[16777216]{0:T(1024)(128)(4,1)} %bitcast.32), calls=%async_computation.3 | async-start | bytes 8388608
  49.3 2.0 %collective-permute-start.14 = (bf16[2,128,512]{2,1,0:T(8,128)(2,1)S(1)}, bf16[2,128,512]{2,1,0:T(8,128)(2,1)S(1)}, u32[]{:S(2)}, u32[]{:S(2)}) collective-permute-start(bf16[2,128,512]{2,1,0:T(8,128)(2,1)S(1)} %collective-permute-done.3.refs_4_), channel_id=1, source_target_pairs={{0,1},{1,0},{2,3},{3,2},{4,5},{5,4},{6,7},{7,6},{8,9},{9,8},{10,11... | collective-permute-start | bytes 786440 | tf_op jit(solution)/shard_map/ppermute | solution.py:268
  49.4 1.8 %collective-permute-start.22 = (f32[128,128]{1,0:T(8,128)S(1)}, f32[128,128]{1,0:T(8,128)S(1)}, u32[]{:S(2)}, u32[]{:S(2)}) collective-permute-start(f32[128,128]{1,0:T(8,128)S(1)} %convert_add_fusion.2.refs_6_), channel_id=1, source_target_pairs={{0,1},{1,0},{2,3},{3,2},{4,5},{5,4},{6,7},{7,6},{8,9},{9,8},{10,11... | collective-permute-start | bytes 196616 | tf_op jit(solution)/shard_map/ppermute | solution.py:268
  54.6 2.5 %collective-permute-start.35 = (bf16[2,128,512]{2,1,0:T(8,128)(2,1)S(1)}, bf16[2,128,512]{2,1,0:T(8,128)(2,1)S(1)}, u32[]{:S(2)}, u32[]{:S(2)}) collective-permute-start(bf16[2,128,512]{2,1,0:T(8,128)(2,1)S(1)} %get-tuple-element.74), channel_id=1, source_target_pairs={{0,1},{1,0},{2,3},{3,2},{4,5},{5,4},{6,7},{7,6},{8,9},{9,8},{10,11... | collective-permute-start | bytes 786440 | tf_op jit(solution)/shard_map/ppermute | solution.py:268
  54.7 3.9 %collective-permute-start.31 = (bf16[2,128,512]{2,1,0:T(8,128)(2,1)S(1)}, bf16[2,128,512]{2,1,0:T(8,128)(2,1)S(1)}, u32[]{:S(2)}, u32[]{:S(2)}) collective-permute-start(bf16[2,128,512]{2,1,0:T(8,128)(2,1)S(1)} %get-tuple-element.68), channel_id=1, source_target_pairs={{0,1},{1,0},{2,3},{3,2},{4,5},{5,4},{6,7},{7,6},{8,9},{9,8},{10,11... | collective-permute-start | bytes 786440 | tf_op jit(solution)/shard_map/ppermute | solution.py:268
  55.2 3.5 %collective-permute-start.32 = (bf16[2,128,512]{2,1,0:T(8,128)(2,1)S(1)}, bf16[2,128,512]{2,1,0:T(8,128)(2,1)S(1)}, u32[]{:S(2)}, u32[]{:S(2)}) collective-permute-start(bf16[2,128,512]{2,1,0:T(8,128)(2,1)S(1)} %get-tuple-element.69), channel_id=1, source_target_pairs={{0,1},{1,0},{2,3},{3,2},{4,5},{5,4},{6,7},{7,6},{8,9},{9,8},{10,11... | collective-permute-start | bytes 786440 | tf_op jit(solution)/shard_map/ppermute | solution.py:268
  55.3 3.9 %collective-permute-start.33 = (bf16[2,128,512]{2,1,0:T(8,128)(2,1)S(1)}, bf16[2,128,512]{2,1,0:T(8,128)(2,1)S(1)}, u32[]{:S(2)}, u32[]{:S(2)}) collective-permute-start(bf16[2,128,512]{2,1,0:T(8,128)(2,1)S(1)} %get-tuple-element.70), channel_id=1, source_target_pairs={{0,1},{1,0},{2,3},{3,2},{4,5},{5,4},{6,7},{7,6},{8,9},{9,8},{10,11... | collective-permute-start | bytes 786440 | tf_op jit(solution)/shard_map/ppermute | solution.py:268
  57.0 3.4 %collective-permute-start.27 = (bf16[2,128,512]{2,1,0:T(8,128)(2,1)S(1)}, bf16[2,128,512]{2,1,0:T(8,128)(2,1)S(1)}, u32[]{:S(2)}, u32[]{:S(2)}) collective-permute-start(bf16[2,128,512]{2,1,0:T(8,128)(2,1)S(1)} %get-tuple-element.67), channel_id=1, source_target_pairs={{0,1},{1,0},{2,3},{3,2},{4,5},{5,4},{6,7},{7,6},{8,9},{9,8},{10,11... | collective-permute-start | bytes 786440 | tf_op jit(solution)/shard_map/ppermute | solution.py:268
  58.0 6.4 %collective-permute-start.36 = (bf16[2,128,512]{2,1,0:T(8,128)(2,1)S(1)}, bf16[2,128,512]{2,1,0:T(8,128)(2,1)S(1)}, u32[]{:S(2)}, u32[]{:S(2)}) collective-permute-start(bf16[2,128,512]{2,1,0:T(8,128)(2,1)S(1)} %shard_map.74), channel_id=1, source_target_pairs={{0,2},{1,5},{2,0},{3,7},{4,6},{5,1},{6,4},{7,3},{8,10},{9,13},{10,... | collective-permute-start | bytes 786440 | tf_op jit(solution)/shard_map/ppermute | solution.py:271
  58.6 6.4 %collective-permute-start.23 = (bf16[2,128,512]{2,1,0:T(8,128)(2,1)S(1)}, bf16[2,128,512]{2,1,0:T(8,128)(2,1)S(1)}, u32[]{:S(2)}, u32[]{:S(2)}) collective-permute-start(bf16[2,128,512]{2,1,0:T(8,128)(2,1)S(1)} %get-tuple-element.61), channel_id=1, source_target_pairs={{0,1},{1,0},{2,3},{3,2},{4,5},{5,4},{6,7},{7,6},{8,9},{9,8},{10,11... | collective-permute-start | bytes 786440 | tf_op jit(solution)/shard_map/ppermute | solution.py:268
  58.7 6.5 %collective-permute-start.24 = (bf16[2,128,512]{2,1,0:T(8,128)(2,1)S(1)}, bf16[2,128,512]{2,1,0:T(8,128)(2,1)S(1)}, u32[]{:S(2)}, u32[]{:S(2)}) collective-permute-start(bf16[2,128,512]{2,1,0:T(8,128)(2,1)S(1)} %get-tuple-element.62), channel_id=1, source_target_pairs={{0,1},{1,0},{2,3},{3,2},{4,5},{5,4},{6,7},{7,6},{8,9},{9,8},{10,11... | collective-permute-start | bytes 786440 | tf_op jit(solution)/shard_map/ppermute | solution.py:268
  59.1 6.1 %collective-permute-start.25 = (bf16[2,128,512]{2,1,0:T(8,128)(2,1)S(1)}, bf16[2,128,512]{2,1,0:T(8,128)(2,1)S(1)}, u32[]{:S(2)}, u32[]{:S(2)}) collective-permute-start(bf16[2,128,512]{2,1,0:T(8,128)(2,1)S(1)} %get-tuple-element.63), channel_id=1, source_target_pairs={{0,1},{1,0},{2,3},{3,2},{4,5},{5,4},{6,7},{7,6},{8,9},{9,8},{10,11... | collective-permute-start | bytes 786440 | tf_op jit(solution)/shard_map/ppermute | solution.py:268
  60.4 13.8 %collective-permute-start.34 = (bf16[2,128,512]{2,1,0:T(8,128)(2,1)S(1)}, bf16[2,128,512]{2,1,0:T(8,128)(2,1)S(1)}, u32[]{:S(2)}, u32[]{:S(2)}) collective-permute-start(bf16[2,128,512]{2,1,0:T(8,128)(2,1)S(1)} %get-tuple-element.72), channel_id=1, source_target_pairs={{0,2},{1,5},{2,0},{3,7},{4,6},{5,1},{6,4},{7,3},{8,10},{9,13},{10,... | collective-permute-start | bytes 786440 | tf_op jit(solution)/shard_map/ppermute | solution.py:271
  64.4 8.4 %collective-permute-start.28 = (bf16[2,128,512]{2,1,0:T(8,128)(2,1)S(1)}, bf16[2,128,512]{2,1,0:T(8,128)(2,1)S(1)}, u32[]{:S(2)}, u32[]{:S(2)}) collective-permute-start(bf16[2,128,512]{2,1,0:T(8,128)(2,1)S(1)} %shard_map.72), channel_id=1, source_target_pairs={{0,2},{1,5},{2,0},{3,7},{4,6},{5,1},{6,4},{7,3},{8,10},{9,13},{10,... | collective-permute-start | bytes 786440 | tf_op jit(solution)/shard_map/ppermute | solution.py:271
  65.1 9.3 %collective-permute-start.37 = (bf16[2,128,512]{2,1,0:T(8,128)(2,1)S(1)}, bf16[2,128,512]{2,1,0:T(8,128)(2,1)S(1)}, u32[]{:S(2)}, u32[]{:S(2)}) collective-permute-start(bf16[2,128,512]{2,1,0:T(8,128)(2,1)S(1)} %add_convert_fusion), channel_id=1, source_target_pairs={{0,4},{1,3},{2,6},{3,1},{4,0},{5,7},{6,2},{7,5},{8,12},{9,11},{10,... | collective-permute-start | bytes 786440 | tf_op jit(solution)/shard_map/ppermute | solution.py:271
  66.4 11.8 %collective-permute-start.26 = (bf16[2,128,512]{2,1,0:T(8,128)(2,1)S(1)}, bf16[2,128,512]{2,1,0:T(8,128)(2,1)S(1)}, u32[]{:S(2)}, u32[]{:S(2)}) collective-permute-start(bf16[2,128,512]{2,1,0:T(8,128)(2,1)S(1)} %get-tuple-element.65), channel_id=1, source_target_pairs={{0,2},{1,5},{2,0},{3,7},{4,6},{5,1},{6,4},{7,3},{8,10},{9,13},{10,... | collective-permute-start | bytes 786440 | tf_op jit(solution)/shard_map/ppermute | solution.py:271
  72.9 6.4 %collective-permute-start.29 = (bf16[2,128,512]{2,1,0:T(8,128)(2,1)S(1)}, bf16[2,128,512]{2,1,0:T(8,128)(2,1)S(1)}, u32[]{:S(2)}, u32[]{:S(2)}) collective-permute-start(bf16[2,128,512]{2,1,0:T(8,128)(2,1)S(1)} %add_convert_fusion.1), channel_id=1, source_target_pairs={{0,4},{1,3},{2,6},{3,1},{4,0},{5,7},{6,2},{7,5},{8,12},{9,11},{10,... | collective-permute-start | bytes 786440 | tf_op jit(solution)/shard_map/ppermute | solution.py:271
  74.5 5.5 %collective-permute-start.38 = (bf16[128,512]{1,0:T(8,128)(2,1)S(1)}, bf16[128,512]{1,0:T(8,128)(2,1)S(1)}, u32[]{:S(2)}, u32[]{:S(2)}) collective-permute-start(bf16[128,512]{1,0:T(8,128)(2,1)S(1)} %fusion.6), channel_id=1, source_target_pairs={{0,8},{1,9},{2,10},{3,11},{4,12},{5,13},{6,14},{7,15},{8,0},{9,1},... | collective-permute-start | bytes 393224 | tf_op jit(solution)/shard_map/ppermute | solution.py:268
  79.5 7.0 %collective-permute-start.30 = (bf16[128,512]{1,0:T(8,128)(2,1)S(1)}, bf16[128,512]{1,0:T(8,128)(2,1)S(1)}, u32[]{:S(2)}, u32[]{:S(2)}) collective-permute-start(bf16[128,512]{1,0:T(8,128)(2,1)S(1)} %fusion.5), channel_id=1, source_target_pairs={{0,8},{1,9},{2,10},{3,11},{4,12},{5,13},{6,14},{7,15},{8,0},{9,1},... | collective-permute-start | bytes 393224 | tf_op jit(solution)/shard_map/ppermute | solution.py:268
  80.0 8.5 %collective-permute-start.39 = (bf16[128,512]{1,0:T(8,128)(2,1)S(1)}, bf16[128,512]{1,0:T(8,128)(2,1)S(1)}, u32[]{:S(2)}, u32[]{:S(2)}) collective-permute-start(bf16[128,512]{1,0:T(8,128)(2,1)S(1)} %fusion.1), channel_id=1, source_target_pairs={{0,16},{1,17},{2,18},{3,19},{4,20},{5,21},{6,22},{7,23},{8,24},{9,... | collective-permute-start | bytes 393224 | tf_op jit(solution)/shard_map/ppermute | solution.py:268

commit v5 on v3

v5 whole, which is shorter than its diff:
```python
import functools

import jax
import jax.numpy as jnp
from jax import lax
from jax.experimental import pallas as pl
from jax.experimental.pallas import tpu as pltpu
from jax.sharding import PartitionSpec as P

HEADS = 128
KVH = 8
HEAD = 128
LANE = 128
EPS = 1e-05
MIB = 1 << 20
CORE = 1


def combos(bits):
    out = [0]
    for b in bits:
        out = out + [o ^ b for o in out]
    return out


def vmem():
    return pl.BlockSpec(memory_space=pltpu.VMEM)


def smem():
    return pl.BlockSpec(memory_space=pltpu.SMEM)


def hbm():
    return pl.BlockSpec(memory_space=pltpu.HBM)


def in_hbm(x):
    return pltpu.with_memory_space_constraint(x, pltpu.HBM)


def dot(a, b):
    return jnp.dot(a, b, preferred_element_type=jnp.float32)


def fetch_kernel(symbols, width, where, source, target, sems):
    copies = []
    for i, (const, pick) in enumerate(symbols):
        start = pl.multiple_of((where[pick] ^ const) * width, LANE)
        copy = pltpu.make_async_copy(
            source.at[pl.ds(start, width), :], target.at[pl.ds(i * width, width), :], sems.at[i]
        )
        copy.start()
        copies.append(copy)
    for copy in copies:
        copy.wait()


def fetched(where, weight, width, symbols):
    shape = (len(symbols) * width, weight.shape[1])
    return pl.pallas_call(
        functools.partial(fetch_kernel, symbols, width),
        out_shape=jax.ShapeDtypeStruct(shape, weight.dtype),
        in_specs=[smem(), hbm()],
        out_specs=vmem(),
        scratch_shapes=[pltpu.SemaphoreType.DMA((len(symbols),))],
        compiler_params=pltpu.CompilerParams(vmem_limit_bytes=MIB),
        cost_estimate=pl.CostEstimate(
            flops=0, bytes_accessed=4 * shape[0] * shape[1], transcendentals=0
        ),
    )(where, in_hbm(weight))


def kv_kernel(shared, where, act, gain, wk, wv, send, keep, abuf, gbuf, kbuf, vbuf, sems):
    me = where[0]
    width = act.shape[1]
    own = pl.ds(pl.multiple_of(me * width, LANE), width)
    pairs = [(act, abuf), (gain, gbuf), (wk, kbuf), (wv, vbuf)]
    copies = [pltpu.make_async_copy(x, y, sems.at[i]) for i, (x, y) in enumerate(pairs)]
    for c in copies:
        c.start()
    for c in copies:
        c.wait()
    scaled = (abuf[...].astype(jnp.float32) * gbuf[:, own]).astype(jnp.bfloat16)
    k, v = dot(scaled, kbuf[...]), dot(scaled, vbuf[...])
    core0 = (me & CORE) == 0
    for h in range(KVH):
        off = h ^ (me >> shared)
        spot = 0
        for b in range(KVH.bit_length() - 1):
            spot = spot * 2 + (1 - ((off >> b) & 1))
        kh, vh = k[:, h * HEAD : (h + 1) * HEAD], v[:, h * HEAD : (h + 1) * HEAD]
        keep[spot] = jnp.where(core0, kh, vh)
        send[spot] = jnp.where(core0, vh, kh)


def kv_terms(shared, where, act, gain, wk, wv):
    tokens = act.shape[0]
    return pl.pallas_call(
        functools.partial(kv_kernel, shared),
        out_shape=[jax.ShapeDtypeStruct((KVH, tokens, HEAD), jnp.float32)] * 2
        + [jax.ShapeDtypeStruct(x.shape, x.dtype) for x in (act, gain)],
        in_specs=[smem()] + [hbm()] * 4,
        out_specs=[vmem()] * 4,
        scratch_shapes=[
            pltpu.VMEM(wk.shape, wk.dtype),
            pltpu.VMEM(wv.shape, wv.dtype),
            pltpu.SemaphoreType.DMA((4,)),
        ],
        compiler_params=pltpu.CompilerParams(vmem_limit_bytes=12 * MIB),
        cost_estimate=pl.CostEstimate(
            flops=4 * tokens * wk.size, bytes_accessed=4 * wk.size, transcendentals=0
        ),
    )(where, in_hbm(act), in_hbm(gain), in_hbm(wk), in_hbm(wv))


def attend(queries, k_sum, v_sum, cosine, sine, scale):
    k_rows = (k_sum * scale).astype(jnp.bfloat16).astype(jnp.float32)
    value = (v_sum * scale).astype(jnp.bfloat16)
    tokens, heads = queries.shape[0], queries.shape[1] // HEAD

    def rotate(x, cosine, sine):
        half = HEAD // 2
        turned = jnp.concatenate([x[:, half:], x[:, :half]], axis=1)
        return (x * cosine + turned * sine).astype(jnp.bfloat16)

    def stacked(parts):
        return jnp.concatenate(parts, axis=0)

    key = rotate(k_rows, cosine, sine)
    queries = queries * scale
    rows = stacked([queries[:, h * HEAD : (h + 1) * HEAD] for h in range(heads)])
    query = rotate(rows, stacked([cosine] * heads), stacked([sine] * heads))
    scores = lax.dot_general(
        query, key, (((1,), (1,)), ((), ())), preferred_element_type=jnp.float32
    ) * HEAD ** (-0.5)
    at = lax.broadcasted_iota(jnp.int32, (tokens, tokens), 0)
    seen = at >= lax.broadcasted_iota(jnp.int32, (tokens, tokens), 1)
    bias = jnp.where(seen, 0.0, -jnp.inf)
    scores = scores + stacked([bias] * heads)
    weights = jnp.exp(scores - jnp.max(scores, axis=1, keepdims=True))
    probs = (weights / jnp.sum(weights, axis=1, keepdims=True)).astype(jnp.bfloat16)
    out = dot(probs, value).astype(jnp.bfloat16)
    return jnp.concatenate([out[h * tokens : (h + 1) * tokens] for h in range(heads)], axis=1)


def query_kernel(places, carried, last, *refs):
    refs = list(refs)
    where, gain = refs.pop(0), refs.pop(0)
    pieces = [refs.pop(0) for _ in places]
    weight = refs.pop(0)
    queries = refs.pop(0)[...] if carried else None
    squares = refs.pop(0)[...] if carried else None
    width = pieces[0].shape[2]
    for piece, blocks in zip(pieces, places):
        for block, ((const, pick), row) in enumerate(blocks):
            start = pl.multiple_of((where[pick] ^ const) * width, LANE)
            x = piece[block].astype(jnp.float32)
            for c in range(0, width, LANE):
                square = x[:, c : c + LANE] * x[:, c : c + LANE]
                squares = square if squares is None else squares + square
            scaled = (x * gain[:, pl.ds(start, width)]).astype(jnp.bfloat16)
            term = dot(scaled, weight[row * width : (row + 1) * width, :])
            queries = term if queries is None else queries + term
    if last:
        mean = jnp.sum(squares, axis=1, keepdims=True) * (1.0 / gain.shape[1])
        mine, other, cosine, sine, out = refs
        core0 = (where[0] & CORE) == 0
        k_sum = jnp.where(core0, mine[...], other[...])
        v_sum = jnp.where(core0, other[...], mine[...])
        out[...] = attend(
            queries, k_sum, v_sum, cosine[...], sine[...], lax.rsqrt(mean + EPS)
        )
    else:
        refs[0][...] = queries
        refs[1][...] = squares


def query_call(where, gain, pieces, held, carry=(), extra=()):
    weight, order = held
    arrays = [array for array, _ in pieces]
    places = [[(s, order.index(s)) for s in symbols] for _, symbols in pieces]
    tokens, width, columns = *arrays[0].shape[1:], weight.shape[1]
    rows = width * sum(len(p) for p in places)
    if extra:
        out_shape = [jax.ShapeDtypeStruct((tokens, columns), jnp.bfloat16)]
    else:
        out_shape = [
            jax.ShapeDtypeStruct((tokens, columns), jnp.float32),
            jax.ShapeDtypeStruct((tokens, LANE), jnp.float32),
        ]
    count = 2 + len(arrays) + len(carry) + len(extra)
    return pl.pallas_call(
        functools.partial(query_kernel, places, bool(carry), bool(extra)),
        out_shape=out_shape,
        in_specs=[smem()] + [vmem()] * count,
        out_specs=[vmem()] * len(out_shape),
        compiler_params=pltpu.CompilerParams(vmem_limit_bytes=12 * MIB),
        cost_estimate=pl.CostEstimate(
            flops=2 * tokens * columns * rows,
            bytes_accessed=2 * columns * rows,
            transcendentals=0,
        ),
    )(where, gain, *arrays, weight, *carry, *extra)


def output_kernel(groups, width, where, attended, *refs):
    refs = list(refs)
    added = [refs.pop(0) if g[1] else None for g in groups]
    weight = refs.pop(0)
    left = attended[...]
    for (symbols, _), arrived, out in zip(groups, added, refs):
        for block, (const, pick) in enumerate(symbols):
            span = pl.ds(pl.multiple_of((where[pick] ^ const) * width, LANE), width)
            term = dot(left, weight[:, span])
            if arrived is not None:
                term = term + arrived[block].astype(jnp.float32)
            out[block] = term.astype(out.dtype)


def output_call(where, attended, weight, width, groups):
    tokens, depth = attended.shape
    blocks = sum(len(g[0]) for g in groups)
    added = [g[2] for g in groups if g[2] is not None]
    return pl.pallas_call(
        functools.partial(output_kernel, [(s, a is not None) for s, _, a in groups], width),
        out_shape=[jax.ShapeDtypeStruct((len(s), tokens, width), t) for s, t, _ in groups],
        in_specs=[smem()] + [vmem()] * (2 + len(added)),
        out_specs=[vmem()] * len(groups),
        compiler_params=pltpu.CompilerParams(vmem_limit_bytes=12 * MIB),
        cost_estimate=pl.CostEstimate(
            flops=2 * tokens * depth * width * blocks,
            bytes_accessed=2 * depth * width * blocks,
            transcendentals=0,
        ),
    )(where, attended, *added, weight)


def rotary_tables(tokens):
    half = HEAD // 2
    frequency = 500000.0 ** (-(jnp.arange(half, dtype=jnp.float32) * 2.0) / HEAD)
    angles = jnp.arange(tokens, dtype=jnp.float32)[:, None] * frequency[None, :]
    cosine, sine = jnp.cos(angles), jnp.sin(angles)
    return jnp.concatenate([cosine, cosine], axis=1), jnp.concatenate([-sine, sine], axis=1)


def per_device(n, act, norm_gain, wq, wk, wv, wo):
    tokens, width = act.shape
    me = lax.axis_index("wide")
    bits = [1 << i for i in range(n.bit_length() - 1)]
    ways = (bits[1], bits[2])
    diagonal = bits[1] ^ bits[2]
    near, top = combos(bits[3:-1]), bits[-1]
    far = [o ^ top for o in near]
    f32, bf16 = jnp.float32, jnp.bfloat16

    def swap(x, offset):
        return lax.ppermute(x, "wide", [(i, i ^ offset) for i in range(n)])

    def turn(x, step):
        return lax.ppermute(x, "wide", [(i, i ^ ways[(step + (i & CORE)) % 2]) for i in range(n)])

    bit = jnp.where((me & CORE) == 0, ways[0], ways[1])
    where = jnp.stack([me, me ^ bit, me ^ bit ^ diagonal]).astype(jnp.int32)
    gain = norm_gain.reshape(1, -1)

    def plain(offsets, pick=0):
        return [(o, pick) for o in offsets]

    def across(symbols):
        return [(const ^ CORE, (0, 2, 1)[pick]) for const, pick in symbols]

    def after(x, *others):
        return lax.optimization_barrier((x, *others))[0]

    shared = (n // KVH).bit_length() - 1
    kv_send, kv_keep, act, gain = kv_terms(shared, where, act, gain, wk, wv)

    def symbols_of(offsets):
        square = [(0, 0), (0, 1), (0, 2), (diagonal, 0)]
        return [[(const ^ o, pick) for o in offsets] for const, pick in square]

    def listed(groups):
        return [s for symbols in groups for s in symbols]

    def other(pieces):
        return [(swap(x, CORE), across(symbols)) for x, symbols in pieces]

    def order_of(offsets):
        own = listed(symbols_of(offsets))
        return own + across(own)

    early_order, last_order = order_of(near), order_of(far)

    pieces, joined, rows, early_weight, first = [], [], [], None, act
    for offsets in (near[:1], near[1:], far):
        at = symbols_of(offsets)
        if offsets is far:
            first = after(swap(act, top), pieces[0][2][0], *rows)
        row = jnp.stack([swap(first, o & ~top) if o & ~top else first for o in offsets])
        if offsets is far:
            row = after(row, joined[1])
        rows.append(row)
        side = turn(row, 0)
        if offsets is far:
            early_weight = fetched(after(where, row), wq, width, early_order)
            side = after(side, early_weight, pieces[1][2][0])
        joined.append(jnp.concatenate([row, side]))
        pieces.append([(row, at[0]), (side, at[1]), (turn(joined[-1], 1), at[2] + at[3])])
    last_weight = fetched(where, wq, width, last_order)

    kv = kv_keep + swap(kv_send, CORE)
    for b, step in zip(bits[shared:], joined):
        half = kv.shape[0] // 2
        got = after(swap(kv[:half].astype(bf16), b), step)
        kv = kv[half:] + got.astype(f32)
    total = kv[0]
    for b in bits[1:shared]:
        total = total + swap(total.astype(bf16), b).astype(f32)
    kv_sums = (total, swap(total, CORE))

    call = functools.partial(query_call, where, gain)
    early = pieces[0] + pieces[1]
    early_held, last_held = (early_weight, early_order), (last_weight, last_order)
    carry = call(early + other(early), early_held)
    row, side, both = pieces[2]
    carry = call([row, side] + other([row]), last_held, carry=carry)
    arrived, *carry = lax.optimization_barrier((both[0], *carry))
    both = [(arrived, both[1])]
    final = other(both)
    carry = call(other([side]) + both, last_held, carry=carry)
    (attended,) = call(final, last_held, carry=carry, extra=(*kv_sums, *rotary_tables(tokens)))

    def project(left, wanted, arrived=None):
        if arrived is None:
            wanted = [(across(s), bf16, None) for s, _ in wanted]
        else:
            wanted = [(*g, a) for g, a in zip(wanted, arrived)]
        return output_call(where, left, wo, width, wanted)

    def round_square(offsets, left):
        home, one, two, corner = symbols_of(offsets)
        k = len(offsets)
        leave, stay = [(corner + one, bf16)], [(two, f32), (home, f32)]
        sent = project(left, leave)
        got = [swap(x, CORE) for x in sent]
        left, *_ = lax.optimization_barrier((left, *sent))
        got_stay = [swap(x, CORE) for x in project(left, stay)]
        (leaving,) = project(left, leave, got)
        arrived = turn(leaving, 0)
        left = after(left, leaving)
        two, home = project(left, stay, got_stay)
        two = two + arrived[:k].astype(f32)
        got = turn(two.astype(bf16), 1)
        return [home, arrived[k:], got], after(left, two)

    def added_up(home, *arrived):
        for x in arrived:
            home = home + x.astype(f32)
        return home

    def along_z(blocks, offsets):
        return [swap(blocks[i].astype(bf16), o).astype(f32) for i, o in enumerate(offsets)]

    far_sums, left = round_square(far, attended)
    near_sums, left = round_square(near[1:], left)
    home_sums, left = round_square(near[:1], left)
    total = added_up(*far_sums)
    total = added_up(total[0], *along_z(total[1:], near[1:]))
    out = swap(total.astype(bf16), top).astype(f32)
    out = added_up(out, *along_z(added_up(*near_sums), near[1:]))
    out = out + added_up(*home_sums)[0]
    return out.astype(bf16)


def solution(mesh):
    return jax.shard_map(
        functools.partial(per_device, mesh.shape["wide"]),
        mesh=mesh,
        in_specs=(
            P("groups", "wide"),
            P(),
            P(None, "wide"),
            P("wide", None),
            P("wide", None),
            P("wide", None),
        ),
        out_specs=P("groups", "wide"),
        check_vma=False,
    )
```

time: 97.3 us -> 97.6 us (level)
  local copies, waits for them, and re-layouts: 7.59 us -> 0.12 us
  starting transfers between devices: 27.9 us -> 31.9 us
  waiting for transfers between devices: 33.3 us -> 35.8 us
  Pallas kernels: 26.2 us -> 27.5 us
    unnamed x18 -> x9, local copies, waits for them, and re-layouts: 7.53 us -> 0.04 us
    pallas_call x4 -> x12, Pallas kernels: 5.09 us -> 10.9 us  [output_call(): pl.pallas_call(functools.partial(output_kernel, [(s, a is not None) for s...]
    ppermute x6 -> x12, starting transfers between devices: 9.74 us -> 15 us  [turn(): lax.ppermute(x, 'wide', [(i, i ^ ways[(step + (i & CORE)) % 2]) for i in...]
    pallas_call x2, Pallas kernels: 12.1 us -> 8.13 us  [fetched(): pl.pallas_call(functools.partial(fetch_kernel, symbols, width), out_shape...]
    ppermute x21 -> x30, waiting for transfers between devices: 17.1 us -> 20.7 us  [swap(): return lax.ppermute(x, 'wide', [(i, i ^ offset) for i in range(n)])]
    ppermute x21 -> x30, starting transfers between devices: 18.2 us -> 16.9 us  [swap(): return lax.ppermute(x, 'wide', [(i, i ^ offset) for i in range(n)])]
    ppermute x6 -> x12, waiting for transfers between devices: 16.2 us -> 15 us  [turn(): lax.ppermute(x, 'wide', [(i, i ^ ways[(step + (i & CORE)) % 2]) for i in...]
  transfers between devices with their start and end apart: 27 -> 42, of which waited for: 11 -> 18; matrix products, arithmetic and copies ran while one was open for 1% -> 1% of each run, Pallas kernels for 24% -> 21%
where the time goes in v5:
time: 97.6 us; the launch traced here: 97.4 us
  waiting for transfers between devices  35.8 us (37%)
  starting transfers between devices  31.9 us (33%)
  Pallas kernels  27.5 us (28%)
  other arithmetic  1.69 us (2%)
    ppermute x30, waiting for transfers between devices, swap(): return lax.ppermute(x, 'wide', [(i, i ^ offset) for i in range(n)])  20.7 us
    ppermute x30, starting transfers between devices, swap(): return lax.ppermute(x, 'wide', [(i, i ^ offset) for i in range(n)])  16.9 us
    ppermute x12, waiting for transfers between devices, turn(): lax.ppermute(x, 'wide', [(i, i ^ ways[(step + (i & CORE)) % 2]) for i in...  15 us
    ppermute x12, starting transfers between devices, turn(): lax.ppermute(x, 'wide', [(i, i ^ ways[(step + (i & CORE)) % 2]) for i in...  15 us
    pallas_call x12, Pallas kernels, output_call(): pl.pallas_call(functools.partial(output_kernel, [(s, a is not None) for s...  10.9 us
    pallas_call x2, Pallas kernels, fetched(): pl.pallas_call(functools.partial(fetch_kernel, symbols, width), out_shape...  8.13 us
    pallas_call x4, Pallas kernels, query_call(): pl.pallas_call(functools.partial(query_kernel, places, bool(carry), bool(...  5.84 us
    pallas_call x1, Pallas kernels, kv_terms(): pl.pallas_call(functools.partial(kv_kernel, shared), out_shape=[jax.Shape...  2.69 us
  transfers between devices with their start and end apart: 42, of which 18 were waited for; matrix products, arithmetic and copies ran while one was open for 1% of the time, Pallas kernels for 21%

profile of v5, /device:TPU:0, one launch (start us, length us, event | category | flops | bytes accessed | tf_op | source)
XLA Modules:
  0.0 97.4 jit_solution(5939925643705770272)
XLA Ops:
  0.1 2.7 %shard_map.64 = (f32[8,128,128]{2,1,0:T(8,128)S(1)}, f32[8,128,128]{2,1,0:T(8,128)S(1)}, bf16[128,512]{1,0:T(8,128)(2,1)S(1)}, f32[1,16384]{1,0:T(1,128)S(1)}) custom-call(s32[3]{0:T(128)S(1)} %pad_add_fusion.where.refs_0_, bf16[128,512]{1,0:T(8,128)(2,1)} %act.1, f32[1,16384]{1,0:T(1,128)} %bitcast.40, bf16[512,1024]{1,0:T(8,128)(2,1)} %wk.1, ...), custom_call_target="tpu_custom_call" | custom-call | flops 268435456 | bytes 2097152 | tf_op jit(solution)/shard_map/pallas_call | solution.py:99
  3.3 2.6 %collective-permute-start.1 = (bf16[1,128,512]{2,1,0:T(8,128)(2,1)S(1)}, bf16[1,128,512]{2,1,0:T(8,128)(2,1)S(1)}, u32[]{:S(2)}, u32[]{:S(2)}) collective-permute-start(bf16[1,128,512]{2,1,0:T(8,128)(2,1)S(1)} %bitcast.30), channel_id=1, source_target_pairs={{0,2},{1,5},{2,0},{3,7},{4,6},{5,1},{6,4},{7,3},{8,10},{9,13},{10,... | collective-permute-start | bytes 393224 | tf_op jit(solution)/shard_map/ppermute | solution.py:261
  5.9 2.9 %collective-permute-done.1.refs_3_ = bf16[1,128,512]{2,1,0:T(8,128)(2,1)S(1)} collective-permute-done((bf16[1,128,512]{2,1,0:T(8,128)(2,1)S(1)}, bf16[1,128,512]{2,1,0:T(8,128)(2,1)S(1)}, u32[]{:S(2)}, u32[]{:S(2)}) %collective-permute-start.1) | collective-permute-done | bytes 131104 | tf_op jit(solution)/shard_map/ppermute | solution.py:261
  8.8 2.1 %collective-permute-start.2 = (bf16[2,128,512]{2,1,0:T(8,128)(2,1)S(1)}, bf16[2,128,512]{2,1,0:T(8,128)(2,1)S(1)}, u32[]{:S(2)}, u32[]{:S(2)}) collective-permute-start(bf16[2,128,512]{2,1,0:T(8,128)(2,1)S(1)} %pad_maximum_fusion), channel_id=1, source_target_pairs={{0,4},{1,3},{2,6},{3,1},{4,0},{5,7},{6,2},{7,5},{8,12},{9,11},{10,... | collective-permute-start | bytes 786440 | tf_op jit(solution)/shard_map/ppermute | solution.py:261
  10.9 1.6 %collective-permute-start.3 = (bf16[128,512]{1,0:T(8,128)(2,1)S(1)}, bf16[128,512]{1,0:T(8,128)(2,1)S(1)}, u32[]{:S(2)}, u32[]{:S(2)}) collective-permute-start(bf16[128,512]{1,0:T(8,128)(2,1)S(1)} %get-tuple-element.46), channel_id=1, source_target_pairs={{0,8},{1,9},{2,10},{3,11},{4,12},{5,13},{6,14},{7,15},{8,0},{9,1},... | collective-permute-start | bytes 393224 | tf_op jit(solution)/shard_map/ppermute | solution.py:258
  12.5 2.6 %collective-permute-start = (bf16[128,512]{1,0:T(8,128)(2,1)S(1)}, bf16[128,512]{1,0:T(8,128)(2,1)S(1)}, u32[]{:S(2)}, u32[]{:S(2)}) collective-permute-start(bf16[128,512]{1,0:T(8,128)(2,1)S(1)} %get-tuple-element.46), channel_id=1, source_target_pairs={{0,16},{1,17},{2,18},{3,19},{4,20},{5,21},{6,22},{7,23},{8,24},{9,... | collective-permute-start | bytes 393224 | tf_op jit(solution)/shard_map/ppermute | solution.py:258
  15.1 2.5 %collective-permute-done.3 = bf16[128,512]{1,0:T(8,128)(2,1)S(1)} collective-permute-done((bf16[128,512]{1,0:T(8,128)(2,1)S(1)}, bf16[128,512]{1,0:T(8,128)(2,1)S(1)}, u32[]{:S(2)}, u32[]{:S(2)}) %collective-permute-start.3) | collective-permute-done | bytes 131104 | tf_op jit(solution)/shard_map/ppermute | solution.py:258
  18.3 2.3 %collective-permute-done = bf16[128,512]{1,0:T(8,128)(2,1)S(1)} collective-permute-done((bf16[128,512]{1,0:T(8,128)(2,1)S(1)}, bf16[128,512]{1,0:T(8,128)(2,1)S(1)}, u32[]{:S(2)}, u32[]{:S(2)}) %collective-permute-start) | collective-permute-done | bytes 131104 | tf_op jit(solution)/shard_map/ppermute | solution.py:258
  21.1 1.7 %collective-permute-start.19 = (bf16[4,128,128]{2,1,0:T(8,128)(2,1)S(1)}, bf16[4,128,128]{2,1,0:T(8,128)(2,1)S(1)}, u32[]{:S(2)}, u32[]{:S(2)}) collective-permute-start(bf16[4,128,128]{2,1,0:T(8,128)(2,1)S(1)} %slice.100), channel_id=1, source_target_pairs={{0,4},{1,5},{2,6},{3,7},{4,0},{5,1},{6,2},{7,3},{8,12},{9,13},{10,... | collective-permute-start | bytes 393224 | tf_op jit(solution)/shard_map/ppermute | solution.py:258
  22.8 1.9 %collective-permute-start.7 = (bf16[2,128,512]{2,1,0:T(8,128)(2,1)S(1)}, bf16[2,128,512]{2,1,0:T(8,128)(2,1)S(1)}, u32[]{:S(2)}, u32[]{:S(2)}) collective-permute-start(bf16[2,128,512]{2,1,0:T(8,128)(2,1)S(1)} %pad_maximum_fusion.2), channel_id=1, source_target_pairs={{0,4},{1,3},{2,6},{3,1},{4,0},{5,7},{6,2},{7,5},{8,12},{9,11},{10,... | collective-permute-start | bytes 786440 | tf_op jit(solution)/shard_map/ppermute | solution.py:261
  24.7 0.9 collective-permute-done.4
  25.7 0.8 collective-permute-start.6
  26.5 4.1 %shard_map.65.refs_14_ = bf16[8192,512]{1,0:T(8,128)(2,1)S(1)} custom-call(s32[3]{0:T(128)S(1)} %pad_add_fusion.where.refs_0_, bf16[16384,512]{1,0:T(8,128)(2,1)} %source.3), custom_call_target="tpu_custom_call" | custom-call | bytes 16777216 | tf_op jit(solution)/shard_map/pallas_call | solution.py:61
  31.0 3.9 %collective-permute-done.20 = bf16[2,128,128]{2,1,0:T(8,128)(2,1)S(1)} collective-permute-done((bf16[2,128,128]{2,1,0:T(8,128)(2,1)S(1)}, bf16[2,128,128]{2,1,0:T(8,128)(2,1)S(1)}, u32[]{:S(2)}, u32[]{:S(2)}) %collective-permute-start.20) | collective-permute-done | bytes 65568 | tf_op jit(solution)/shard_map/ppermute | solution.py:258
  35.0 1.5 %collective-permute-start.8 = (bf16[4,128,512]{2,1,0:T(8,128)(2,1)S(1)}, bf16[4,128,512]{2,1,0:T(8,128)(2,1)S(1)}, u32[]{:S(2)}, u32[]{:S(2)}) collective-permute-start(bf16[4,128,512]{2,1,0:T(8,128)(2,1)S(1)} %constant_dynamic-update-slice_fusion), channel_id=1, source_target_pairs={{0,4},{1,3},{2,6},{3,1},{4,0},{5,7},{6,2},{7,5},{8,12},{9,11},{10,... | collective-permute-start | bytes 1572872 | tf_op jit(solution)/shard_map/ppermute | solution.py:261
  36.5 1.1 %collective-permute-start.21 = (bf16[1,128,128]{2,1,0:T(8,128)(2,1)S(1)}, bf16[1,128,128]{2,1,0:T(8,128)(2,1)S(1)}, u32[]{:S(2)}, u32[]{:S(2)}) collective-permute-start(bf16[1,128,128]{2,1,0:T(8,128)(2,1)S(1)} %slice.102), channel_id=1, source_target_pairs={{0,16},{1,17},{2,18},{3,19},{4,20},{5,21},{6,22},{7,23},{8,24},{9,... | collective-permute-start | bytes 98312 | tf_op jit(solution)/shard_map/ppermute | solution.py:258
  38.1 3.3 %collective-permute-done.21 = bf16[1,128,128]{2,1,0:T(8,128)(2,1)S(1)} collective-permute-done((bf16[1,128,128]{2,1,0:T(8,128)(2,1)S(1)}, bf16[1,128,128]{2,1,0:T(8,128)(2,1)S(1)}, u32[]{:S(2)}, u32[]{:S(2)}) %collective-permute-start.21) | collective-permute-done | bytes 32800 | tf_op jit(solution)/shard_map/ppermute | solution.py:258
  41.4 4.1 %shard_map.66.refs_5_.refs_4_.refs_3_ = bf16[8192,512]{1,0:T(8,128)(2,1)S(1)} custom-call(s32[3]{0:T(128)S(1)} %pad_add_fusion.where.refs_0_, bf16[16384,512]{1,0:T(8,128)(2,1)} %source.3), custom_call_target="tpu_custom_call" | custom-call | bytes 16777216 | tf_op jit(solution)/shard_map/pallas_call | solution.py:61
  46.2 0.9 collective-permute-done.14.refs_12_
  47.1 1.6 %collective-permute-start.22 = (bf16[128,128]{1,0:T(8,128)(2,1)S(1)}, bf16[128,128]{1,0:T(8,128)(2,1)S(1)}, u32[]{:S(2)}, u32[]{:S(2)}) collective-permute-start(bf16[128,128]{1,0:T(8,128)(2,1)S(1)} %fusion.8), channel_id=1, source_target_pairs={{0,2},{1,3},{2,0},{3,1},{4,6},{5,7},{6,4},{7,5},{8,10},{9,11},{10,... | collective-permute-start | bytes 98312 | tf_op jit(solution)/shard_map/ppermute | solution.py:258
  48.7 2.0 %shard_map.67 = (f32[128,512]{1,0:T(8,128)S(1)}, f32[128,128]{1,0:T(8,128)S(1)}) custom-call(s32[3]{0:T(128)S(1)} %pad_add_fusion.where.refs_0_, f32[1,16384]{1,0:T(1,128)S(1)} %get-tuple-element.45.refs_1_, bf16[1,128,512]{2,1,0:T(8,128)(2,1)S(1)} %bitcast.33, bf16[1,128,512]{2,1,0:T(8,128)(2,1)S(1)} %collective-permute-done.1.refs_3_, ...), custom_call_target="tpu_custom_call" | custom-call | flops 1073741824 | bytes 8388608 | tf_op jit(solution)/shard_map/pallas_call | solution.py:193
  50.7 1.2 %shard_map.68 = (f32[128,512]{1,0:T(8,128)S(1)}, f32[128,128]{1,0:T(8,128)S(1)}) custom-call(s32[3]{0:T(128)S(1)} %pad_add_fusion.where.refs_0_, f32[1,16384]{1,0:T(1,128)S(1)} %get-tuple-element.45.refs_1_, bf16[2,128,512]{2,1,0:T(8,128)(2,1)S(1)} %pad_maximum_fusion.1.refs_2_, bf16[2,128,512]{2,1,0:T(8,128)(2,1)S(1)} %collective-permute-done.6.refs_3_, ...), custom_call_target="tpu_custom_call" | custom-call | flops 402653184 | bytes 3145728 | tf_op jit(solution)/shard_map/pallas_call | solution.py:193
  53.0 1.2 %collective-permute-done.17.refs_2_ = bf16[2,128,512]{2,1,0:T(8,128)(2,1)S(1)} collective-permute-done((bf16[2,128,512]{2,1,0:T(8,128)(2,1)S(1)}, bf16[2,128,512]{2,1,0:T(8,128)(2,1)S(1)}, u32[]{:S(2)}, u32[]{:S(2)}) %collective-permute-start.17) | collective-permute-done | bytes 262176 | tf_op jit(solution)/shard_map/ppermute | solution.py:258
  54.2 1.2 %shard_map.69 = (f32[128,512]{1,0:T(8,128)S(1)}, f32[128,128]{1,0:T(8,128)S(1)}) custom-call(s32[3]{0:T(128)S(1)} %pad_add_fusion.where.refs_0_, f32[1,16384]{1,0:T(1,128)S(1)} %get-tuple-element.45.refs_1_, bf16[2,128,512]{2,1,0:T(8,128)(2,1)S(1)} %collective-permute-done.17.refs_2_, bf16[4,128,512]{2,1,0:T(8,128)(2,1)S(1)} %collective-permute-done.8.refs_3_, ...), custom_call_target="tpu_custom_call" | custom-call | flops 402653184 | bytes 3145728 | tf_op jit(solution)/shard_map/pallas_call | solution.py:193
  55.4 1.6 %shard_map.70.attended = bf16[128,512]{1,0:T(8,128)(2,1)S(1)} custom-call(s32[3]{0:T(128)S(1)} %pad_add_fusion.where.refs_0_, f32[1,16384]{1,0:T(1,128)S(1)} %get-tuple-element.45.refs_1_, bf16[4,128,512]{2,1,0:T(8,128)(2,1)S(1)} %collective-permute-done.16.refs_2_, bf16[8192,512]{1,0:T(8,128)(2,1)S(1)} %shard_map.66.refs_5_.refs_4_.refs_3_, ...), custom_call_target="tpu_custom_call" | custom-call | flops 268435456 | bytes 2097152 | tf_op jit(solution)/shard_map/pallas_call | solution.py:193
  57.0 1.0 %shard_map.71 = bf16[4,128,512]{2,1,0:T(8,128)(2,1)S(1)} custom-call(s32[3]{0:T(128)S(1)} %pad_add_fusion.where.refs_0_, bf16[128,512]{1,0:T(8,128)(2,1)S(1)} %shard_map.70.attended, bf16[512,16384]{1,0:T(8,128)(2,1)S(1)} %bitcast.29), custom_call_target="tpu_custom_call" | custom-call | flops 268435456 | bytes 2097152 | tf_op jit(solution)/shard_map/pallas_call | solution.py:225
  58.2 1.8 %collective-permute-done.24.refs_0_ = bf16[4,128,512]{2,1,0:T(8,128)(2,1)S(1)} collective-permute-done((bf16[4,128,512]{2,1,0:T(8,128)(2,1)S(1)}, bf16[4,128,512]{2,1,0:T(8,128)(2,1)S(1)}, u32[]{:S(2)}, u32[]{:S(2)}) %collective-permute-start.24) | collective-permute-done | bytes 524320 | tf_op jit(solution)/shard_map/ppermute | solution.py:258
  60.0 1.0 %shard_map.72 = bf16[4,128,512]{2,1,0:T(8,128)(2,1)S(1)} custom-call(s32[3]{0:T(128)S(1)} %pad_add_fusion.where.refs_0_, bf16[128,512]{1,0:T(8,128)(2,1)S(1)} %shard_map.70.attended, bf16[4,128,512]{2,1,0:T(8,128)(2,1)S(1)} %collective-permute-done.24.refs_0_, bf16[512,16384]{1,0:T(8,128)(2,1)S(1)} %bitcast.29), custom_call_target="tpu_custom_call" | custom-call | flops 268435456 | bytes 2097152 | tf_op jit(solution)/shard_map/pallas_call | solution.py:225
  61.5 1.0 %shard_map.73 = (bf16[2,128,512]{2,1,0:T(8,128)(2,1)S(1)}, bf16[2,128,512]{2,1,0:T(8,128)(2,1)S(1)}) custom-call(s32[3]{0:T(128)S(1)} %pad_add_fusion.where.refs_0_, bf16[128,512]{1,0:T(8,128)(2,1)S(1)} %shard_map.70.attended, bf16[512,16384]{1,0:T(8,128)(2,1)S(1)} %bitcast.29), custom_call_target="tpu_custom_call" | custom-call | flops 268435456 | bytes 2097152 | tf_op jit(solution)/shard_map/pallas_call | solution.py:225
  63.0 1.0 %collective-permute-done.25.refs_0_ = bf16[2,128,512]{2,1,0:T(8,128)(2,1)S(1)} collective-permute-done((bf16[2,128,512]{2,1,0:T(8,128)(2,1)S(1)}, bf16[2,128,512]{2,1,0:T(8,128)(2,1)S(1)}, u32[]{:S(2)}, u32[]{:S(2)}) %collective-permute-start.25) | collective-permute-done | bytes 262176 | tf_op jit(solution)/shard_map/ppermute | solution.py:258
  64.4 1.0 %shard_map.74 = (f32[2,128,512]{2,1,0:T(8,128)S(1)}, f32[2,128,512]{2,1,0:T(8,128)S(1)}) custom-call(s32[3]{0:T(128)S(1)} %pad_add_fusion.where.refs_0_, bf16[128,512]{1,0:T(8,128)(2,1)S(1)} %shard_map.70.attended, bf16[2,128,512]{2,1,0:T(8,128)(2,1)S(1)} %collective-permute-done.25.refs_0_, bf16[2,128,512]{2,1,0:T(8,128)(2,1)S(1)} %collective-permute-done.26.refs_1_, ...), custom_call_target="tpu_custom_call" | custom-call | flops 268435456 | bytes 2097152 | tf_op jit(solution)/shard_map/pallas_call | solution.py:225
  65.5 4.8 %collective-permute-done.27 = bf16[4,128,512]{2,1,0:T(8,128)(2,1)S(1)} collective-permute-done((bf16[4,128,512]{2,1,0:T(8,128)(2,1)S(1)}, bf16[4,128,512]{2,1,0:T(8,128)(2,1)S(1)}, u32[]{:S(2)}, u32[]{:S(2)}) %collective-permute-start.27) | collective-permute-done | bytes 524320 | tf_op jit(solution)/shard_map/ppermute | solution.py:261
  70.3 0.9 shard_map.75
  71.7 0.9 shard_map.77
  73.2 0.9 shard_map.76
  74.0 1.4 %collective-permute-start.34 = (bf16[2,128,512]{2,1,0:T(8,128)(2,1)S(1)}, bf16[2,128,512]{2,1,0:T(8,128)(2,1)S(1)}, u32[]{:S(2)}, u32[]{:S(2)}) collective-permute-start(bf16[2,128,512]{2,1,0:T(8,128)(2,1)S(1)} %shard_map.76), channel_id=1, source_target_pairs={{0,2},{1,5},{2,0},{3,7},{4,6},{5,1},{6,4},{7,3},{8,10},{9,13},{10,... | collective-permute-start | bytes 786440 | tf_op jit(solution)/shard_map/ppermute | solution.py:261
  75.4 3.0 %collective-permute-done.28 = bf16[2,128,512]{2,1,0:T(8,128)(2,1)S(1)} collective-permute-done((bf16[2,128,512]{2,1,0:T(8,128)(2,1)S(1)}, bf16[2,128,512]{2,1,0:T(8,128)(2,1)S(1)}, u32[]{:S(2)}, u32[]{:S(2)}) %collective-permute-start.28) | collective-permute-done | bytes 262176 | tf_op jit(solution)/shard_map/ppermute | solution.py:261
  78.9 0.9 shard_map.78
  80.5 0.9 shard_map.79
  81.5 1.6 %collective-permute-start.35 = (bf16[1,128,512]{2,1,0:T(8,128)(2,1)S(1)}, bf16[1,128,512]{2,1,0:T(8,128)(2,1)S(1)}, u32[]{:S(2)}, u32[]{:S(2)}) collective-permute-start(bf16[1,128,512]{2,1,0:T(8,128)(2,1)S(1)} %convert_add_fusion.2), channel_id=1, source_target_pairs={{0,4},{1,3},{2,6},{3,1},{4,0},{5,7},{6,2},{7,5},{8,12},{9,11},{10,... | collective-permute-start | bytes 393224 | tf_op jit(solution)/shard_map/ppermute | solution.py:261
  84.3 0.9 shard_map.80
  85.6 0.9 shard_map.81
  87.1 2.1 %collective-permute-start.36 = (bf16[128,512]{1,0:T(8,128)(2,1)S(1)}, bf16[128,512]{1,0:T(8,128)(2,1)S(1)}, u32[]{:S(2)}, u32[]{:S(2)}) collective-permute-start(bf16[128,512]{1,0:T(8,128)(2,1)S(1)} %fusion.3), channel_id=1, source_target_pairs={{0,8},{1,9},{2,10},{3,11},{4,12},{5,13},{6,14},{7,15},{8,0},{9,1},... | collective-permute-start | bytes 393224 | tf_op jit(solution)/shard_map/ppermute | solution.py:258
  89.1 0.9 shard_map.82
  90.0 1.6 %collective-permute-done.40 = bf16[2,128,512]{2,1,0:T(8,128)(2,1)S(1)} collective-permute-done((bf16[2,128,512]{2,1,0:T(8,128)(2,1)S(1)}, bf16[2,128,512]{2,1,0:T(8,128)(2,1)S(1)}, u32[]{:S(2)}, u32[]{:S(2)}) %collective-permute-start.40) | collective-permute-done | bytes 262176 | tf_op jit(solution)/shard_map/ppermute | solution.py:261
  91.7 1.1 %collective-permute-start.41 = (bf16[1,128,512]{2,1,0:T(8,128)(2,1)S(1)}, bf16[1,128,512]{2,1,0:T(8,128)(2,1)S(1)}, u32[]{:S(2)}, u32[]{:S(2)}) collective-permute-start(bf16[1,128,512]{2,1,0:T(8,128)(2,1)S(1)} %add_convert_fusion), channel_id=1, source_target_pairs={{0,4},{1,3},{2,6},{3,1},{4,0},{5,7},{6,2},{7,5},{8,12},{9,11},{10,... | collective-permute-start | bytes 393224 | tf_op jit(solution)/shard_map/ppermute | solution.py:261
  92.7 2.0 %collective-permute-done.36 = bf16[128,512]{1,0:T(8,128)(2,1)S(1)} collective-permute-done((bf16[128,512]{1,0:T(8,128)(2,1)S(1)}, bf16[128,512]{1,0:T(8,128)(2,1)S(1)}, u32[]{:S(2)}, u32[]{:S(2)}) %collective-permute-start.36) | collective-permute-done | bytes 131104 | tf_op jit(solution)/shard_map/ppermute | solution.py:258
  94.7 2.0 %collective-permute-done.41 = bf16[1,128,512]{2,1,0:T(8,128)(2,1)S(1)} collective-permute-done((bf16[1,128,512]{2,1,0:T(8,128)(2,1)S(1)}, bf16[1,128,512]{2,1,0:T(8,128)(2,1)S(1)}, u32[]{:S(2)}, u32[]{:S(2)}) %collective-permute-start.41) | collective-permute-done | bytes 131104 | tf_op jit(solution)/shard_map/ppermute | solution.py:261
  (89 shorter events, 11.9 us)
Async XLA Ops:
  2.8 18.3 %collective-permute-start.18 = (f32[8,128,128]{2,1,0:T(8,128)S(1)}, f32[8,128,128]{2,1,0:T(8,128)S(1)}, u32[]{:S(2)}, u32[]{:S(2)}) collective-permute-start(f32[8,128,128]{2,1,0:T(8,128)S(1)} %get-tuple-element.61), channel_id=1, source_target_pairs={{0,1},{1,0},{2,3},{3,2},{4,5},{5,4},{6,7},{7,6},{8,9},{9,8},{10,11... | collective-permute-start | bytes 1572872 | tf_op jit(solution)/shard_map/ppermute | solution.py:258
  3.3 5.5 %collective-permute-start.1 = (bf16[1,128,512]{2,1,0:T(8,128)(2,1)S(1)}, bf16[1,128,512]{2,1,0:T(8,128)(2,1)S(1)}, u32[]{:S(2)}, u32[]{:S(2)}) collective-permute-start(bf16[1,128,512]{2,1,0:T(8,128)(2,1)S(1)} %bitcast.30), channel_id=1, source_target_pairs={{0,2},{1,5},{2,0},{3,7},{4,6},{5,1},{6,4},{7,3},{8,10},{9,13},{10,... | collective-permute-start | bytes 393224 | tf_op jit(solution)/shard_map/ppermute | solution.py:261
  8.8 11.8 %collective-permute-start.2 = (bf16[2,128,512]{2,1,0:T(8,128)(2,1)S(1)}, bf16[2,128,512]{2,1,0:T(8,128)(2,1)S(1)}, u32[]{:S(2)}, u32[]{:S(2)}) collective-permute-start(bf16[2,128,512]{2,1,0:T(8,128)(2,1)S(1)} %pad_maximum_fusion), channel_id=1, source_target_pairs={{0,4},{1,3},{2,6},{3,1},{4,0},{5,7},{6,2},{7,5},{8,12},{9,11},{10,... | collective-permute-start | bytes 786440 | tf_op jit(solution)/shard_map/ppermute | solution.py:261
  10.9 6.7 %collective-permute-start.3 = (bf16[128,512]{1,0:T(8,128)(2,1)S(1)}, bf16[128,512]{1,0:T(8,128)(2,1)S(1)}, u32[]{:S(2)}, u32[]{:S(2)}) collective-permute-start(bf16[128,512]{1,0:T(8,128)(2,1)S(1)} %get-tuple-element.46), channel_id=1, source_target_pairs={{0,8},{1,9},{2,10},{3,11},{4,12},{5,13},{6,14},{7,15},{8,0},{9,1},... | collective-permute-start | bytes 393224 | tf_op jit(solution)/shard_map/ppermute | solution.py:258
  12.5 8.1 %collective-permute-start = (bf16[128,512]{1,0:T(8,128)(2,1)S(1)}, bf16[128,512]{1,0:T(8,128)(2,1)S(1)}, u32[]{:S(2)}, u32[]{:S(2)}) collective-permute-start(bf16[128,512]{1,0:T(8,128)(2,1)S(1)} %get-tuple-element.46), channel_id=1, source_target_pairs={{0,16},{1,17},{2,18},{3,19},{4,20},{5,21},{6,22},{7,23},{8,24},{9,... | collective-permute-start | bytes 393224 | tf_op jit(solution)/shard_map/ppermute | solution.py:258
  17.6 5.2 %collective-permute-start.5 = (bf16[1,128,512]{2,1,0:T(8,128)(2,1)S(1)}, bf16[1,128,512]{2,1,0:T(8,128)(2,1)S(1)}, u32[]{:S(2)}, u32[]{:S(2)}) collective-permute-start(bf16[1,128,512]{2,1,0:T(8,128)(2,1)S(1)} %bitcast.34), channel_id=1, source_target_pairs={{0,2},{1,5},{2,0},{3,7},{4,6},{5,1},{6,4},{7,3},{8,10},{9,13},{10,... | collective-permute-start | bytes 393224 | tf_op jit(solution)/shard_map/ppermute | solution.py:261
  20.7 5.0 %collective-permute-start.4 = (bf16[128,512]{1,0:T(8,128)(2,1)S(1)}, bf16[128,512]{1,0:T(8,128)(2,1)S(1)}, u32[]{:S(2)}, u32[]{:S(2)}) collective-permute-start(bf16[128,512]{1,0:T(8,128)(2,1)S(1)} %collective-permute-done), channel_id=1, source_target_pairs={{0,8},{1,9},{2,10},{3,11},{4,12},{5,13},{6,14},{7,15},{8,0},{9,1},... | collective-permute-start | bytes 393224 | tf_op jit(solution)/shard_map/ppermute | solution.py:258
  21.0 17.0 %collective-permute-start.10 = (bf16[1,128,512]{2,1,0:T(8,128)(2,1)S(1)}, bf16[1,128,512]{2,1,0:T(8,128)(2,1)S(1)}, u32[]{:S(2)}, u32[]{:S(2)}) collective-permute-start(bf16[1,128,512]{2,1,0:T(8,128)(2,1)S(1)} %bitcast.32), channel_id=1, source_target_pairs={{0,1},{1,0},{2,3},{3,2},{4,5},{5,4},{6,7},{7,6},{8,9},{9,8},{10,11... | collective-permute-start | bytes 393224 | tf_op jit(solution)/shard_map/ppermute | solution.py:258
  21.1 9.4 %collective-permute-start.19 = (bf16[4,128,128]{2,1,0:T(8,128)(2,1)S(1)}, bf16[4,128,128]{2,1,0:T(8,128)(2,1)S(1)}, u32[]{:S(2)}, u32[]{:S(2)}) collective-permute-start(bf16[4,128,128]{2,1,0:T(8,128)(2,1)S(1)} %slice.100), channel_id=1, source_target_pairs={{0,4},{1,5},{2,6},{3,7},{4,0},{5,1},{6,2},{7,3},{8,12},{9,13},{10,... | collective-permute-start | bytes 393224 | tf_op jit(solution)/shard_map/ppermute | solution.py:258
  22.8 12.1 %collective-permute-start.7 = (bf16[2,128,512]{2,1,0:T(8,128)(2,1)S(1)}, bf16[2,128,512]{2,1,0:T(8,128)(2,1)S(1)}, u32[]{:S(2)}, u32[]{:S(2)}) collective-permute-start(bf16[2,128,512]{2,1,0:T(8,128)(2,1)S(1)} %pad_maximum_fusion.2), channel_id=1, source_target_pairs={{0,4},{1,3},{2,6},{3,1},{4,0},{5,7},{6,2},{7,5},{8,12},{9,11},{10,... | collective-permute-start | bytes 786440 | tf_op jit(solution)/shard_map/ppermute | solution.py:261
  25.7 9.3 %collective-permute-start.6 = (bf16[2,128,512]{2,1,0:T(8,128)(2,1)S(1)}, bf16[2,128,512]{2,1,0:T(8,128)(2,1)S(1)}, u32[]{:S(2)}, u32[]{:S(2)}) collective-permute-start(bf16[2,128,512]{2,1,0:T(8,128)(2,1)S(1)} %pad_maximum_fusion.1.refs_2_), channel_id=1, source_target_pairs={{0,2},{1,5},{2,0},{3,7},{4,6},{5,1},{6,4},{7,3},{8,10},{9,13},{10,... | collective-permute-start | bytes 786440 | tf_op jit(solution)/shard_map/ppermute | solution.py:261
  30.6 4.3 %collective-permute-start.20 = (bf16[2,128,128]{2,1,0:T(8,128)(2,1)S(1)}, bf16[2,128,128]{2,1,0:T(8,128)(2,1)S(1)}, u32[]{:S(2)}, u32[]{:S(2)}) collective-permute-start(bf16[2,128,128]{2,1,0:T(8,128)(2,1)S(1)} %slice.101), channel_id=1, source_target_pairs={{0,8},{1,9},{2,10},{3,11},{4,12},{5,13},{6,14},{7,15},{8,0},{9,1},... | collective-permute-start | bytes 196616 | tf_op jit(solution)/shard_map/ppermute | solution.py:258
  35.0 16.9 %collective-permute-start.8 = (bf16[4,128,512]{2,1,0:T(8,128)(2,1)S(1)}, bf16[4,128,512]{2,1,0:T(8,128)(2,1)S(1)}, u32[]{:S(2)}, u32[]{:S(2)}) collective-permute-start(bf16[4,128,512]{2,1,0:T(8,128)(2,1)S(1)} %constant_dynamic-update-slice_fusion), channel_id=1, source_target_pairs={{0,4},{1,3},{2,6},{3,1},{4,0},{5,7},{6,2},{7,5},{8,12},{9,11},{10,... | collective-permute-start | bytes 1572872 | tf_op jit(solution)/shard_map/ppermute | solution.py:261
  36.5 4.9 %collective-permute-start.21 = (bf16[1,128,128]{2,1,0:T(8,128)(2,1)S(1)}, bf16[1,128,128]{2,1,0:T(8,128)(2,1)S(1)}, u32[]{:S(2)}, u32[]{:S(2)}) collective-permute-start(bf16[1,128,128]{2,1,0:T(8,128)(2,1)S(1)} %slice.102), channel_id=1, source_target_pairs={{0,16},{1,17},{2,18},{3,19},{4,20},{5,21},{6,22},{7,23},{8,24},{9,... | collective-permute-start | bytes 98312 | tf_op jit(solution)/shard_map/ppermute | solution.py:258
  37.5 7.9 %collective-permute-start.11 = (bf16[1,128,512]{2,1,0:T(8,128)(2,1)S(1)}, bf16[1,128,512]{2,1,0:T(8,128)(2,1)S(1)}, u32[]{:S(2)}, u32[]{:S(2)}) collective-permute-start(bf16[1,128,512]{2,1,0:T(8,128)(2,1)S(1)} %collective-permute-done.1.refs_3_), channel_id=1, source_target_pairs={{0,1},{1,0},{2,3},{3,2},{4,5},{5,4},{6,7},{7,6},{8,9},{9,8},{10,11... | collective-permute-start | bytes 393224 | tf_op jit(solution)/shard_map/ppermute | solution.py:258
  37.6 8.5 %collective-permute-start.13 = (bf16[1,128,512]{2,1,0:T(8,128)(2,1)S(1)}, bf16[1,128,512]{2,1,0:T(8,128)(2,1)S(1)}, u32[]{:S(2)}, u32[]{:S(2)}) collective-permute-start(bf16[1,128,512]{2,1,0:T(8,128)(2,1)S(1)} %bitcast.36), channel_id=1, source_target_pairs={{0,1},{1,0},{2,3},{3,2},{4,5},{5,4},{6,7},{7,6},{8,9},{9,8},{10,11... | collective-permute-start | bytes 393224 | tf_op jit(solution)/shard_map/ppermute | solution.py:258
  38.1 10.6 %collective-permute-start.12 = (bf16[2,128,512]{2,1,0:T(8,128)(2,1)S(1)}, bf16[2,128,512]{2,1,0:T(8,128)(2,1)S(1)}, u32[]{:S(2)}, u32[]{:S(2)}) collective-permute-start(bf16[2,128,512]{2,1,0:T(8,128)(2,1)S(1)} %collective-permute-done.2.refs_4_), channel_id=1, source_target_pairs={{0,1},{1,0},{2,3},{3,2},{4,5},{5,4},{6,7},{7,6},{8,9},{9,8},{10,11... | collective-permute-start | bytes 786440 | tf_op jit(solution)/shard_map/ppermute | solution.py:258
  41.4 7.3 %collective-permute-start.15 = (bf16[2,128,512]{2,1,0:T(8,128)(2,1)S(1)}, bf16[2,128,512]{2,1,0:T(8,128)(2,1)S(1)}, u32[]{:S(2)}, u32[]{:S(2)}) collective-permute-start(bf16[2,128,512]{2,1,0:T(8,128)(2,1)S(1)} %collective-permute-done.7.refs_7_), channel_id=1, source_target_pairs={{0,1},{1,0},{2,3},{3,2},{4,5},{5,4},{6,7},{7,6},{8,9},{9,8},{10,11... | collective-permute-start | bytes 786440 | tf_op jit(solution)/shard_map/ppermute | solution.py:258
  45.5 1.6 %collective-permute-start.14 = (bf16[1,128,512]{2,1,0:T(8,128)(2,1)S(1)}, bf16[1,128,512]{2,1,0:T(8,128)(2,1)S(1)}, u32[]{:S(2)}, u32[]{:S(2)}) collective-permute-start(bf16[1,128,512]{2,1,0:T(8,128)(2,1)S(1)} %collective-permute-done.5.refs_6_), channel_id=1, source_target_pairs={{0,1},{1,0},{2,3},{3,2},{4,5},{5,4},{6,7},{7,6},{8,9},{9,8},{10,11... | collective-permute-start | bytes 393224 | tf_op jit(solution)/shard_map/ppermute | solution.py:258
  46.1 4.6 %collective-permute-start.9 = (bf16[2,128,512]{2,1,0:T(8,128)(2,1)S(1)}, bf16[2,128,512]{2,1,0:T(8,128)(2,1)S(1)}, u32[]{:S(2)}, u32[]{:S(2)}) collective-permute-start(bf16[2,128,512]{2,1,0:T(8,128)(2,1)S(1)} %pad_maximum_fusion.1.refs_2_), channel_id=1, source_target_pairs={{0,1},{1,0},{2,3},{3,2},{4,5},{5,4},{6,7},{7,6},{8,9},{9,8},{10,11... | collective-permute-start | bytes 786440 | tf_op jit(solution)/shard_map/ppermute | solution.py:258
  47.1 5.7 %collective-permute-start.22 = (bf16[128,128]{1,0:T(8,128)(2,1)S(1)}, bf16[128,128]{1,0:T(8,128)(2,1)S(1)}, u32[]{:S(2)}, u32[]{:S(2)}) collective-permute-start(bf16[128,128]{1,0:T(8,128)(2,1)S(1)} %fusion.8), channel_id=1, source_target_pairs={{0,2},{1,3},{2,0},{3,1},{4,6},{5,7},{6,4},{7,5},{8,10},{9,11},{10,... | collective-permute-start | bytes 98312 | tf_op jit(solution)/shard_map/ppermute | solution.py:258
  48.7 8.3 %slice-start = ((s8[16777216]{0:T(1024)(128)(4,1)}), s8[4194304]{0:T(1024)(128)(4,1)S(1)}, s32[]{:S(2)}) async-start(s8[16777216]{0:T(1024)(128)(4,1)} %bitcast.28), calls=%async_computation | async-start | bytes 8388608
  48.7 8.3 %slice-start.1 = ((s8[16777216]{0:T(1024)(128)(4,1)}), s8[4194304]{0:T(1024)(128)(4,1)S(1)}, s32[]{:S(2)}) async-start(s8[16777216]{0:T(1024)(128)(4,1)} %bitcast.28), calls=%async_computation.1 | async-start | bytes 8388608
  50.7 6.3 %slice-start.2 = ((s8[16777216]{0:T(1024)(128)(4,1)}), s8[4194304]{0:T(1024)(128)(4,1)S(1)}, s32[]{:S(2)}) async-start(s8[16777216]{0:T(1024)(128)(4,1)} %bitcast.28), calls=%async_computation.2 | async-start | bytes 8388608
  51.8 3.5 %collective-permute-start.16 = (bf16[4,128,512]{2,1,0:T(8,128)(2,1)S(1)}, bf16[4,128,512]{2,1,0:T(8,128)(2,1)S(1)}, u32[]{:S(2)}, u32[]{:S(2)}) collective-permute-start(bf16[4,128,512]{2,1,0:T(8,128)(2,1)S(1)} %collective-permute-done.8.refs_3_), channel_id=1, source_target_pairs={{0,1},{1,0},{2,3},{3,2},{4,5},{5,4},{6,7},{7,6},{8,9},{9,8},{10,11... | collective-permute-start | bytes 1572872 | tf_op jit(solution)/shard_map/ppermute | solution.py:258
  52.2 2.0 %collective-permute-start.17 = (bf16[2,128,512]{2,1,0:T(8,128)(2,1)S(1)}, bf16[2,128,512]{2,1,0:T(8,128)(2,1)S(1)}, u32[]{:S(2)}, u32[]{:S(2)}) collective-permute-start(bf16[2,128,512]{2,1,0:T(8,128)(2,1)S(1)} %collective-permute-done.6.refs_3_), channel_id=1, source_target_pairs={{0,1},{1,0},{2,3},{3,2},{4,5},{5,4},{6,7},{7,6},{8,9},{9,8},{10,11... | collective-permute-start | bytes 786440 | tf_op jit(solution)/shard_map/ppermute | solution.py:258
  52.8 2.6 %collective-permute-start.23 = (f32[128,128]{1,0:T(8,128)S(1)}, f32[128,128]{1,0:T(8,128)S(1)}, u32[]{:S(2)}, u32[]{:S(2)}) collective-permute-start(f32[128,128]{1,0:T(8,128)S(1)} %convert_add_fusion.3.refs_6_), channel_id=1, source_target_pairs={{0,1},{1,0},{2,3},{3,2},{4,5},{5,4},{6,7},{7,6},{8,9},{9,8},{10,11... | collective-permute-start | bytes 196616 | tf_op jit(solution)/shard_map/ppermute | solution.py:258
  53.0 4.0 %slice-start.3 = ((s8[16777216]{0:T(1024)(128)(4,1)}), s8[4194304]{0:T(1024)(128)(4,1)S(1)}, s32[]{:S(2)}) async-start(s8[16777216]{0:T(1024)(128)(4,1)} %bitcast.28), calls=%async_computation.3 | async-start | bytes 8388608
  58.0 2.0 %collective-permute-start.24 = (bf16[4,128,512]{2,1,0:T(8,128)(2,1)S(1)}, bf16[4,128,512]{2,1,0:T(8,128)(2,1)S(1)}, u32[]{:S(2)}, u32[]{:S(2)}) collective-permute-start(bf16[4,128,512]{2,1,0:T(8,128)(2,1)S(1)} %shard_map.71), channel_id=1, source_target_pairs={{0,1},{1,0},{2,3},{3,2},{4,5},{5,4},{6,7},{7,6},{8,9},{9,8},{10,11... | collective-permute-start | bytes 1572872 | tf_op jit(solution)/shard_map/ppermute | solution.py:258
  61.0 9.2 %collective-permute-start.27 = (bf16[4,128,512]{2,1,0:T(8,128)(2,1)S(1)}, bf16[4,128,512]{2,1,0:T(8,128)(2,1)S(1)}, u32[]{:S(2)}, u32[]{:S(2)}) collective-permute-start(bf16[4,128,512]{2,1,0:T(8,128)(2,1)S(1)} %shard_map.72), channel_id=1, source_target_pairs={{0,2},{1,5},{2,0},{3,7},{4,6},{5,1},{6,4},{7,3},{8,10},{9,13},{10,... | collective-permute-start | bytes 1572872 | tf_op jit(solution)/shard_map/ppermute | solution.py:261
  62.5 1.6 %collective-permute-start.25 = (bf16[2,128,512]{2,1,0:T(8,128)(2,1)S(1)}, bf16[2,128,512]{2,1,0:T(8,128)(2,1)S(1)}, u32[]{:S(2)}, u32[]{:S(2)}) collective-permute-start(bf16[2,128,512]{2,1,0:T(8,128)(2,1)S(1)} %get-tuple-element.67), channel_id=1, source_target_pairs={{0,1},{1,0},{2,3},{3,2},{4,5},{5,4},{6,7},{7,6},{8,9},{9,8},{10,11... | collective-permute-start | bytes 786440 | tf_op jit(solution)/shard_map/ppermute | solution.py:258
  62.5 1.9 %collective-permute-start.26 = (bf16[2,128,512]{2,1,0:T(8,128)(2,1)S(1)}, bf16[2,128,512]{2,1,0:T(8,128)(2,1)S(1)}, u32[]{:S(2)}, u32[]{:S(2)}) collective-permute-start(bf16[2,128,512]{2,1,0:T(8,128)(2,1)S(1)} %get-tuple-element.68), channel_id=1, source_target_pairs={{0,1},{1,0},{2,3},{3,2},{4,5},{5,4},{6,7},{7,6},{8,9},{9,8},{10,11... | collective-permute-start | bytes 786440 | tf_op jit(solution)/shard_map/ppermute | solution.py:258
  71.2 2.0 %collective-permute-start.31 = (bf16[2,128,512]{2,1,0:T(8,128)(2,1)S(1)}, bf16[2,128,512]{2,1,0:T(8,128)(2,1)S(1)}, u32[]{:S(2)}, u32[]{:S(2)}) collective-permute-start(bf16[2,128,512]{2,1,0:T(8,128)(2,1)S(1)} %shard_map.75), channel_id=1, source_target_pairs={{0,1},{1,0},{2,3},{3,2},{4,5},{5,4},{6,7},{7,6},{8,9},{9,8},{10,11... | collective-permute-start | bytes 786440 | tf_op jit(solution)/shard_map/ppermute | solution.py:258
  71.2 7.2 %collective-permute-start.28 = (bf16[2,128,512]{2,1,0:T(8,128)(2,1)S(1)}, bf16[2,128,512]{2,1,0:T(8,128)(2,1)S(1)}, u32[]{:S(2)}, u32[]{:S(2)}) collective-permute-start(bf16[2,128,512]{2,1,0:T(8,128)(2,1)S(1)} %convert_add_fusion.1), channel_id=1, source_target_pairs={{0,4},{1,3},{2,6},{3,1},{4,0},{5,7},{6,2},{7,5},{8,12},{9,11},{10,... | collective-permute-start | bytes 786440 | tf_op jit(solution)/shard_map/ppermute | solution.py:261
  72.6 6.3 %collective-permute-start.32 = (bf16[1,128,512]{2,1,0:T(8,128)(2,1)S(1)}, bf16[1,128,512]{2,1,0:T(8,128)(2,1)S(1)}, u32[]{:S(2)}, u32[]{:S(2)}) collective-permute-start(bf16[1,128,512]{2,1,0:T(8,128)(2,1)S(1)} %get-tuple-element.74), channel_id=1, source_target_pairs={{0,1},{1,0},{2,3},{3,2},{4,5},{5,4},{6,7},{7,6},{8,9},{9,8},{10,11... | collective-permute-start | bytes 393224 | tf_op jit(solution)/shard_map/ppermute | solution.py:258
  72.8 6.1 %collective-permute-start.33 = (bf16[1,128,512]{2,1,0:T(8,128)(2,1)S(1)}, bf16[1,128,512]{2,1,0:T(8,128)(2,1)S(1)}, u32[]{:S(2)}, u32[]{:S(2)}) collective-permute-start(bf16[1,128,512]{2,1,0:T(8,128)(2,1)S(1)} %get-tuple-element.75), channel_id=1, source_target_pairs={{0,1},{1,0},{2,3},{3,2},{4,5},{5,4},{6,7},{7,6},{8,9},{9,8},{10,11... | collective-permute-start | bytes 393224 | tf_op jit(solution)/shard_map/ppermute | solution.py:258
  74.0 6.4 %collective-permute-start.34 = (bf16[2,128,512]{2,1,0:T(8,128)(2,1)S(1)}, bf16[2,128,512]{2,1,0:T(8,128)(2,1)S(1)}, u32[]{:S(2)}, u32[]{:S(2)}) collective-permute-start(bf16[2,128,512]{2,1,0:T(8,128)(2,1)S(1)} %shard_map.76), channel_id=1, source_target_pairs={{0,2},{1,5},{2,0},{3,7},{4,6},{5,1},{6,4},{7,3},{8,10},{9,13},{10,... | collective-permute-start | bytes 786440 | tf_op jit(solution)/shard_map/ppermute | solution.py:261
  78.6 5.0 %collective-permute-start.29 = (bf16[128,512]{1,0:T(8,128)(2,1)S(1)}, bf16[128,512]{1,0:T(8,128)(2,1)S(1)}, u32[]{:S(2)}, u32[]{:S(2)}) collective-permute-start(bf16[128,512]{1,0:T(8,128)(2,1)S(1)} %fusion.4), channel_id=1, source_target_pairs={{0,8},{1,9},{2,10},{3,11},{4,12},{5,13},{6,14},{7,15},{8,0},{9,1},... | collective-permute-start | bytes 393224 | tf_op jit(solution)/shard_map/ppermute | solution.py:258
  81.4 3.0 %collective-permute-start.37 = (bf16[2,128,512]{2,1,0:T(8,128)(2,1)S(1)}, bf16[2,128,512]{2,1,0:T(8,128)(2,1)S(1)}, u32[]{:S(2)}, u32[]{:S(2)}) collective-permute-start(bf16[2,128,512]{2,1,0:T(8,128)(2,1)S(1)} %shard_map.79), channel_id=1, source_target_pairs={{0,1},{1,0},{2,3},{3,2},{4,5},{5,4},{6,7},{7,6},{8,9},{9,8},{10,11... | collective-permute-start | bytes 786440 | tf_op jit(solution)/shard_map/ppermute | solution.py:258
  81.5 5.5 %collective-permute-start.35 = (bf16[1,128,512]{2,1,0:T(8,128)(2,1)S(1)}, bf16[1,128,512]{2,1,0:T(8,128)(2,1)S(1)}, u32[]{:S(2)}, u32[]{:S(2)}) collective-permute-start(bf16[1,128,512]{2,1,0:T(8,128)(2,1)S(1)} %convert_add_fusion.2), channel_id=1, source_target_pairs={{0,4},{1,3},{2,6},{3,1},{4,0},{5,7},{6,2},{7,5},{8,12},{9,11},{10,... | collective-permute-start | bytes 393224 | tf_op jit(solution)/shard_map/ppermute | solution.py:261
  83.6 9.1 %collective-permute-start.30 = (bf16[128,512]{1,0:T(8,128)(2,1)S(1)}, bf16[128,512]{1,0:T(8,128)(2,1)S(1)}, u32[]{:S(2)}, u32[]{:S(2)}) collective-permute-start(bf16[128,512]{1,0:T(8,128)(2,1)S(1)} %fusion.1), channel_id=1, source_target_pairs={{0,16},{1,17},{2,18},{3,19},{4,20},{5,21},{6,22},{7,23},{8,24},{9,... | collective-permute-start | bytes 393224 | tf_op jit(solution)/shard_map/ppermute | solution.py:258
  85.2 6.4 %collective-permute-start.40 = (bf16[2,128,512]{2,1,0:T(8,128)(2,1)S(1)}, bf16[2,128,512]{2,1,0:T(8,128)(2,1)S(1)}, u32[]{:S(2)}, u32[]{:S(2)}) collective-permute-start(bf16[2,128,512]{2,1,0:T(8,128)(2,1)S(1)} %shard_map.80), channel_id=1, source_target_pairs={{0,2},{1,5},{2,0},{3,7},{4,6},{5,1},{6,4},{7,3},{8,10},{9,13},{10,... | collective-permute-start | bytes 786440 | tf_op jit(solution)/shard_map/ppermute | solution.py:261
  86.4 2.7 %collective-permute-start.38 = (bf16[1,128,512]{2,1,0:T(8,128)(2,1)S(1)}, bf16[1,128,512]{2,1,0:T(8,128)(2,1)S(1)}, u32[]{:S(2)}, u32[]{:S(2)}) collective-permute-start(bf16[1,128,512]{2,1,0:T(8,128)(2,1)S(1)} %get-tuple-element.81), channel_id=1, source_target_pairs={{0,1},{1,0},{2,3},{3,2},{4,5},{5,4},{6,7},{7,6},{8,9},{9,8},{10,11... | collective-permute-start | bytes 393224 | tf_op jit(solution)/shard_map/ppermute | solution.py:258
  86.5 2.6 %collective-permute-start.39 = (bf16[1,128,512]{2,1,0:T(8,128)(2,1)S(1)}, bf16[1,128,512]{2,1,0:T(8,128)(2,1)S(1)}, u32[]{:S(2)}, u32[]{:S(2)}) collective-permute-start(bf16[1,128,512]{2,1,0:T(8,128)(2,1)S(1)} %get-tuple-element.82), channel_id=1, source_target_pairs={{0,1},{1,0},{2,3},{3,2},{4,5},{5,4},{6,7},{7,6},{8,9},{9,8},{10,11... | collective-permute-start | bytes 393224 | tf_op jit(solution)/shard_map/ppermute | solution.py:258
  87.1 7.6 %collective-permute-start.36 = (bf16[128,512]{1,0:T(8,128)(2,1)S(1)}, bf16[128,512]{1,0:T(8,128)(2,1)S(1)}, u32[]{:S(2)}, u32[]{:S(2)}) collective-permute-start(bf16[128,512]{1,0:T(8,128)(2,1)S(1)} %fusion.3), channel_id=1, source_target_pairs={{0,8},{1,9},{2,10},{3,11},{4,12},{5,13},{6,14},{7,15},{8,0},{9,1},... | collective-permute-start | bytes 393224 | tf_op jit(solution)/shard_map/ppermute | solution.py:258
  91.7 5.0 %collective-permute-start.41 = (bf16[1,128,512]{2,1,0:T(8,128)(2,1)S(1)}, bf16[1,128,512]{2,1,0:T(8,128)(2,1)S(1)}, u32[]{:S(2)}, u32[]{:S(2)}) collective-permute-start(bf16[1,128,512]{2,1,0:T(8,128)(2,1)S(1)} %add_convert_fusion), channel_id=1, source_target_pairs={{0,4},{1,3},{2,6},{3,1},{4,0},{5,7},{6,2},{7,5},{8,12},{9,11},{10,... | collective-permute-start | bytes 393224 | tf_op jit(solution)/shard_map/ppermute | solution.py:261

commit v6 on v5

--- a/solution.py
+++ b/solution.py
@@ -14,6 +14,7 @@
 EPS = 1e-05
 MIB = 1 << 20
 CORE = 1
+KV_WEIGHT = 16
 
 
 def combos(bits):
@@ -41,34 +42,6 @@
 
 def dot(a, b):
     return jnp.dot(a, b, preferred_element_type=jnp.float32)
-
-
-def fetch_kernel(symbols, width, where, source, target, sems):
-    copies = []
-    for i, (const, pick) in enumerate(symbols):
-        start = pl.multiple_of((where[pick] ^ const) * width, LANE)
-        copy = pltpu.make_async_copy(
-            source.at[pl.ds(start, width), :], target.at[pl.ds(i * width, width), :], sems.at[i]
-        )
-        copy.start()
-        copies.append(copy)
-    for copy in copies:
-        copy.wait()
-
-
-def fetched(where, weight, width, symbols):
-    shape = (len(symbols) * width, weight.shape[1])
-    return pl.pallas_call(
-        functools.partial(fetch_kernel, symbols, width),
-        out_shape=jax.ShapeDtypeStruct(shape, weight.dtype),
-        in_specs=[smem(), hbm()],
-        out_specs=vmem(),
-        scratch_shapes=[pltpu.SemaphoreType.DMA((len(symbols),))],
-        compiler_params=pltpu.CompilerParams(vmem_limit_bytes=MIB),
-        cost_estimate=pl.CostEstimate(
-            flops=0, bytes_accessed=4 * shape[0] * shape[1], transcendentals=0
-        ),
-    )(where, in_hbm(weight))
 
 
 def kv_kernel(shared, where, act, gain, wk, wv, send, keep, abuf, gbuf, kbuf, vbuf, sems):
@@ -109,7 +82,9 @@
         ],
         compiler_params=pltpu.CompilerParams(vmem_limit_bytes=12 * MIB),
         cost_estimate=pl.CostEstimate(
-            flops=4 * tokens * wk.size, bytes_accessed=4 * wk.size, transcendentals=0
+            flops=KV_WEIGHT * 4 * tokens * wk.size,
+            bytes_accessed=KV_WEIGHT * 4 * wk.size,
+            transcendentals=0,
         ),
     )(where, in_hbm(act), in_hbm(gain), in_hbm(wk), in_hbm(wv))
 
@@ -153,14 +128,13 @@
     squares = refs.pop(0)[...] if carried else None
     width = pieces[0].shape[2]
     for piece, blocks in zip(pieces, places):
-        for block, ((const, pick), row) in enumerate(blocks):
-            start = pl.multiple_of((where[pick] ^ const) * width, LANE)
+        for block, (const, pick) in enumerate(blocks):
+            span = pl.ds(pl.multiple_of((where[pick] ^ const) * width, LANE), width)
             x = piece[block].astype(jnp.float32)
             for c in range(0, width, LANE):
                 square = x[:, c : c + LANE] * x[:, c : c + LANE]
                 squares = square if squares is None else squares + square
-            scaled = (x * gain[:, pl.ds(start, width)]).astype(jnp.bfloat16)
-            term = dot(scaled, weight[row * width : (row + 1) * width, :])
+            term = dot((x * gain[:, span]).astype(jnp.bfloat16), weight[span, :])
             queries = term if queries is None else queries + term
     if last:
         mean = jnp.sum(squares, axis=1, keepdims=True) * (1.0 / gain.shape[1])
@@ -176,10 +150,8 @@
         refs[1][...] = squares
 
 
-def query_call(where, gain, pieces, held, carry=(), extra=()):
-    weight, order = held
-    arrays = [array for array, _ in pieces]
-    places = [[(s, order.index(s)) for s in symbols] for _, symbols in pieces]
+def query_call(where, gain, pieces, weight, carry=(), extra=()):
+    arrays, places = [array for array, _ in pieces], [symbols for _, symbols in pieces]
     tokens, width, columns = *arrays[0].shape[1:], weight.shape[1]
     rows = width * sum(len(p) for p in places)
     if extra:
@@ -274,62 +246,47 @@
         return lax.optimization_barrier((x, *others))[0]
 
     shared = (n // KVH).bit_length() - 1
+    raw = act
     kv_send, kv_keep, act, gain = kv_terms(shared, where, act, gain, wk, wv)
 
     def symbols_of(offsets):
         square = [(0, 0), (0, 1), (0, 2), (diagonal, 0)]
         return [[(const ^ o, pick) for o in offsets] for const, pick in square]
 
-    def listed(groups):
-        return [s for symbols in groups for s in symbols]
-
     def other(pieces):
         return [(swap(x, CORE), across(symbols)) for x, symbols in pieces]
 
-    def order_of(offsets):
-        own = listed(symbols_of(offsets))
-        return own + across(own)
-
-    early_order, last_order = order_of(near), order_of(far)
-
-    pieces, joined, rows, early_weight, first = [], [], [], None, act
-    for offsets in (near[:1], near[1:], far):
-        at = symbols_of(offsets)
+    groups, z_first = [], [raw] + [swap(raw, o) for o in near[1:]]
+    for offsets in (near, far):
         if offsets is far:
-            first = after(swap(act, top), pieces[0][2][0], *rows)
-        row = jnp.stack([swap(first, o & ~top) if o & ~top else first for o in offsets])
-        if offsets is far:
-            row = after(row, joined[1])
-        rows.append(row)
-        side = turn(row, 0)
-        if offsets is far:
-            early_weight = fetched(after(where, row), wq, width, early_order)
-            side = after(side, early_weight, pieces[1][2][0])
-        joined.append(jnp.concatenate([row, side]))
-        pieces.append([(row, at[0]), (side, at[1]), (turn(joined[-1], 1), at[2] + at[3])])
-    last_weight = fetched(where, wq, width, last_order)
+            first = swap(raw, top)
+            row = jnp.stack([first] + [swap(first, o) for o in near[1:]])
+        else:
+            row = jnp.stack([act] + z_first[1:])
+        one, two = turn(row, 0), turn(row, 1)
+        corner = turn(one, 1)
+        groups.append(list(zip((row, one, two, corner), symbols_of(offsets))))
+    early, last = groups
 
     kv = kv_keep + swap(kv_send, CORE)
-    for b, step in zip(bits[shared:], joined):
+    steps = [early[1][0], early[3][0], last[1][0]]
+    for b, step in zip(bits[shared:], steps):
         half = kv.shape[0] // 2
         got = after(swap(kv[:half].astype(bf16), b), step)
         kv = kv[half:] + got.astype(f32)
-    total = kv[0]
+    total = after(kv[0], last[2][0])
     for b in bits[1:shared]:
         total = total + swap(total.astype(bf16), b).astype(f32)
     kv_sums = (total, swap(total, CORE))
 
-    call = functools.partial(query_call, where, gain)
-    early = pieces[0] + pieces[1]
-    early_held, last_held = (early_weight, early_order), (last_weight, last_order)
-    carry = call(early + other(early), early_held)
-    row, side, both = pieces[2]
-    carry = call([row, side] + other([row]), last_held, carry=carry)
-    arrived, *carry = lax.optimization_barrier((both[0], *carry))
-    both = [(arrived, both[1])]
-    final = other(both)
-    carry = call(other([side]) + both, last_held, carry=carry)
-    (attended,) = call(final, last_held, carry=carry, extra=(*kv_sums, *rotary_tables(tokens)))
+    call = functools.partial(query_call, where, gain, weight=wq)
+    carry = call(early + other(early))
+    carry = call(last[:3] + other(last[:1]), carry=carry)
+    corner, *carry = lax.optimization_barrier((last[3][0], *carry))
+    corner = [(corner, last[3][1])]
+    final = other(corner)
+    carry = call(other(last[1:3]) + corner, carry=carry)
+    (attended,) = call(final, carry=carry, extra=(*kv_sums, *rotary_tables(tokens)))
 
     def project(left, wanted, arrived=None):
         if arrived is None:
@@ -338,38 +295,39 @@
             wanted = [(*g, a) for g, a in zip(wanted, arrived)]
         return output_call(where, left, wo, width, wanted)
 
-    def round_square(offsets, left):
+    def wanted(offsets):
         home, one, two, corner = symbols_of(offsets)
-        k = len(offsets)
-        leave, stay = [(corner + one, bf16)], [(two, f32), (home, f32)]
-        sent = project(left, leave)
-        got = [swap(x, CORE) for x in sent]
-        left, *_ = lax.optimization_barrier((left, *sent))
-        got_stay = [swap(x, CORE) for x in project(left, stay)]
-        (leaving,) = project(left, leave, got)
-        arrived = turn(leaving, 0)
-        left = after(left, leaving)
-        two, home = project(left, stay, got_stay)
-        two = two + arrived[:k].astype(f32)
-        got = turn(two.astype(bf16), 1)
-        return [home, arrived[k:], got], after(left, two)
+        return [(corner, bf16)], [(two, f32), (one, bf16), (home, f32)]
+
+    def round_square(offsets, left, got):
+        leave, stay = wanted(offsets)
+        (leaving,) = project(left, leave, got[:1])
+        from_corner = turn(leaving, 0)
+        two, one, home = project(after(left, leaving), stay, got[1:])
+        got_1 = turn(one, 0)
+        two = (two + from_corner.astype(f32)).astype(bf16)
+        return [home, got_1, turn(two, 1)], after(left, two)
 
     def added_up(home, *arrived):
         for x in arrived:
             home = home + x.astype(f32)
         return home
 
-    def along_z(blocks, offsets):
-        return [swap(blocks[i].astype(bf16), o).astype(f32) for i, o in enumerate(offsets)]
-
-    far_sums, left = round_square(far, attended)
-    near_sums, left = round_square(near[1:], left)
-    home_sums, left = round_square(near[:1], left)
-    total = added_up(*far_sums)
-    total = added_up(total[0], *along_z(total[1:], near[1:]))
-    out = swap(total.astype(bf16), top).astype(f32)
-    out = added_up(out, *along_z(added_up(*near_sums), near[1:]))
-    out = out + added_up(*home_sums)[0]
+    def along_z(blocks):
+        return added_up(
+            blocks[0], *[swap(blocks[i].astype(bf16), o) for i, o in enumerate(near) if o]
+        )
+
+    left, sent = attended, []
+    leave, stay = wanted(far)
+    for groups in (leave, stay, sum(wanted(near), [])):
+        sent += project(left, groups)
+        left = after(left, sent[-1])
+    got = [swap(x, CORE) for x in sent]
+    far_sums, left = round_square(far, attended, got[:4])
+    near_sums, _ = round_square(near, left, got[4:])
+    got = swap(along_z(added_up(*far_sums)).astype(bf16), top)
+    out = added_up(along_z(added_up(*near_sums)), got)
     return out.astype(bf16)
 
 

time: 97.6 us -> 85.9 us (0.88)
  Pallas kernels: 27.5 us -> 16 us
  waiting for transfers between devices: 35.8 us -> 29.4 us
  local copies, waits for them, and re-layouts: 0.12 us -> 3.45 us
  starting transfers between devices: 31.9 us -> 34.7 us
    pallas_call x2 -> x0, Pallas kernels: 8.13 us -> none  [fetched(): pl.pallas_call(functools.partial(fetch_kernel, symbols, width), out_shape...]
    ppermute x12, waiting for transfers between devices: 15 us -> 9.59 us  [turn(): lax.ppermute(x, 'wide', [(i, i ^ ways[(step + (i & CORE)) % 2]) for i in...]
    ppermute x30 -> x28, starting transfers between devices: 16.9 us -> 21.7 us  [swap(): return lax.ppermute(x, 'wide', [(i, i ^ offset) for i in range(n)])]
    pallas_call x12 -> x7, Pallas kernels: 10.9 us -> 7.25 us  [output_call(): pl.pallas_call(functools.partial(output_kernel, [(s, a is not None) for s...]
    unnamed x9 -> x10, local copies, waits for them, and re-layouts: 0.04 us -> 3.38 us
    ppermute x12, starting transfers between devices: 15 us -> 13 us  [turn(): lax.ppermute(x, 'wide', [(i, i ^ ways[(step + (i & CORE)) % 2]) for i in...]
    ppermute x30 -> x28, waiting for transfers between devices: 20.7 us -> 19.8 us  [swap(): return lax.ppermute(x, 'wide', [(i, i ^ offset) for i in range(n)])]
  transfers between devices with their start and end apart: 42 -> 40, of which waited for: 18 -> 13; matrix products, arithmetic and copies ran while one was open for 1% -> 1% of each run, Pallas kernels for 21% -> 13%
where the time goes in v6:
time: 85.9 us; the launch traced here: 85.8 us
  starting transfers between devices  34.7 us (40%)
  waiting for transfers between devices  29.4 us (34%)
  Pallas kernels  16 us (19%)
  local copies, waits for them, and re-layouts  3.45 us (4%)
  other arithmetic  1.72 us (2%)
    ppermute x28, starting transfers between devices, swap(): return lax.ppermute(x, 'wide', [(i, i ^ offset) for i in range(n)])  21.7 us
    ppermute x28, waiting for transfers between devices, swap(): return lax.ppermute(x, 'wide', [(i, i ^ offset) for i in range(n)])  19.8 us
    ppermute x12, starting transfers between devices, turn(): lax.ppermute(x, 'wide', [(i, i ^ ways[(step + (i & CORE)) % 2]) for i in...  13 us
    ppermute x12, waiting for transfers between devices, turn(): lax.ppermute(x, 'wide', [(i, i ^ ways[(step + (i & CORE)) % 2]) for i in...  9.59 us
    pallas_call x7, Pallas kernels, output_call(): pl.pallas_call(functools.partial(output_kernel, [(s, a is not None) for s...  7.25 us
    pallas_call x4, Pallas kernels, query_call(): pl.pallas_call(functools.partial(query_kernel, places, bool(carry), bool(...  5.86 us
    unnamed x10, local copies, waits for them, and re-layouts  3.38 us
    pallas_call x1, Pallas kernels, kv_terms(): pl.pallas_call(functools.partial(kv_kernel, shared), out_shape=[jax.Shape...  2.92 us
  transfers between devices with their start and end apart: 40, of which 13 were waited for; matrix products, arithmetic and copies ran while one was open for 1% of the time, Pallas kernels for 13%

profile of v6, /device:TPU:0, one launch (start us, length us, event | category | flops | bytes accessed | tf_op | source)
XLA Modules:
  0.0 85.8 jit_solution(12449341922286446404)
XLA Ops:
  0.1 2.9 %shard_map.64 = (f32[8,128,128]{2,1,0:T(8,128)S(1)}, f32[8,128,128]{2,1,0:T(8,128)S(1)}, bf16[128,512]{1,0:T(8,128)(2,1)S(1)}, f32[1,16384]{1,0:T(1,128)S(1)}) custom-call(s32[3]{0:T(128)S(1)} %pad_add_fusion.where.refs_0_, bf16[128,512]{1,0:T(8,128)(2,1)} %act.1, f32[1,16384]{1,0:T(1,128)} %bitcast.34, bf16[512,1024]{1,0:T(8,128)(2,1)} %wk.1, ...), custom_call_target="tpu_custom_call" | custom-call | flops 4294967296 | bytes 33554432 | tf_op jit(solution)/shard_map/pallas_call | solution.py:72
  3.0 0.5 collective-permute-start.17
  3.5 2.6 %collective-permute-start.6 = (bf16[128,512]{1,0:T(8,128)(2,1)}, bf16[128,512]{1,0:T(8,128)(2,1)S(1)}, u32[]{:S(2)}, u32[]{:S(2)}) collective-permute-start(bf16[128,512]{1,0:T(8,128)(2,1)} %act.1), channel_id=1, source_target_pairs={{0,8},{1,9},{2,10},{3,11},{4,12},{5,13},{6,14},{7,15},{8,0},{9,1},... | collective-permute-start | bytes 393224 | tf_op jit(solution)/shard_map/ppermute | solution.py:230
  6.2 4.3 %collective-permute-done.6 = bf16[128,512]{1,0:T(8,128)(2,1)S(1)} collective-permute-done((bf16[128,512]{1,0:T(8,128)(2,1)}, bf16[128,512]{1,0:T(8,128)(2,1)S(1)}, u32[]{:S(2)}, u32[]{:S(2)}) %collective-permute-start.6) | collective-permute-done | bytes 131104 | tf_op jit(solution)/shard_map/ppermute | solution.py:230
  10.5 1.7 %collective-permute-start.7 = (bf16[2,128,512]{2,1,0:T(8,128)(2,1)S(1)}, bf16[2,128,512]{2,1,0:T(8,128)(2,1)S(1)}, u32[]{:S(2)}, u32[]{:S(2)}) collective-permute-start(bf16[2,128,512]{2,1,0:T(8,128)(2,1)S(1)} %pad_maximum_fusion.1.refs_2_), channel_id=1, source_target_pairs={{0,2},{1,5},{2,0},{3,7},{4,6},{5,1},{6,4},{7,3},{8,10},{9,13},{10,... | collective-permute-start | bytes 786440 | tf_op jit(solution)/shard_map/ppermute | solution.py:233
  12.2 2.6 %collective-permute-start = (bf16[128,512]{1,0:T(8,128)(2,1)}, bf16[128,512]{1,0:T(8,128)(2,1)S(1)}, u32[]{:S(2)}, u32[]{:S(2)}) collective-permute-start(bf16[128,512]{1,0:T(8,128)(2,1)} %act.1), channel_id=1, source_target_pairs={{0,16},{1,17},{2,18},{3,19},{4,20},{5,21},{6,22},{7,23},{8,24},{9,... | collective-permute-start | bytes 393224 | tf_op jit(solution)/shard_map/ppermute | solution.py:230
  14.9 1.6 %collective-permute-start.18 = (bf16[4,128,128]{2,1,0:T(8,128)(2,1)S(1)}, bf16[4,128,128]{2,1,0:T(8,128)(2,1)S(1)}, u32[]{:S(2)}, u32[]{:S(2)}) collective-permute-start(bf16[4,128,128]{2,1,0:T(8,128)(2,1)S(1)} %slice.81), channel_id=1, source_target_pairs={{0,4},{1,5},{2,6},{3,7},{4,0},{5,1},{6,2},{7,3},{8,12},{9,13},{10,... | collective-permute-start | bytes 393224 | tf_op jit(solution)/shard_map/ppermute | solution.py:230
  17.0 3.9 %collective-permute-done = bf16[128,512]{1,0:T(8,128)(2,1)S(1)} collective-permute-done((bf16[128,512]{1,0:T(8,128)(2,1)}, bf16[128,512]{1,0:T(8,128)(2,1)S(1)}, u32[]{:S(2)}, u32[]{:S(2)}) %collective-permute-start) | collective-permute-done | bytes 131104 | tf_op jit(solution)/shard_map/ppermute | solution.py:230
  21.0 0.8 collective-permute-start.1
  22.3 1.3 %collective-permute-start.19 = (bf16[2,128,128]{2,1,0:T(8,128)(2,1)S(1)}, bf16[2,128,128]{2,1,0:T(8,128)(2,1)S(1)}, u32[]{:S(2)}, u32[]{:S(2)}) collective-permute-start(bf16[2,128,128]{2,1,0:T(8,128)(2,1)S(1)} %slice.82), channel_id=1, source_target_pairs={{0,8},{1,9},{2,10},{3,11},{4,12},{5,13},{6,14},{7,15},{8,0},{9,1},... | collective-permute-start | bytes 196616 | tf_op jit(solution)/shard_map/ppermute | solution.py:230
  23.6 2.8 %collective-permute-done.1 = bf16[128,512]{1,0:T(8,128)(2,1)S(1)} collective-permute-done((bf16[128,512]{1,0:T(8,128)(2,1)S(1)}, bf16[128,512]{1,0:T(8,128)(2,1)S(1)}, u32[]{:S(2)}, u32[]{:S(2)}) %collective-permute-start.1) | collective-permute-done | bytes 131104 | tf_op jit(solution)/shard_map/ppermute | solution.py:230
  26.5 2.0 %collective-permute-start.2 = (bf16[2,128,512]{2,1,0:T(8,128)(2,1)S(1)}, bf16[2,128,512]{2,1,0:T(8,128)(2,1)S(1)}, u32[]{:S(2)}, u32[]{:S(2)}) collective-permute-start(bf16[2,128,512]{2,1,0:T(8,128)(2,1)S(1)} %pad_maximum_fusion.refs_2_), channel_id=1, source_target_pairs={{0,2},{1,5},{2,0},{3,7},{4,6},{5,1},{6,4},{7,3},{8,10},{9,13},{10,... | collective-permute-start | bytes 786440 | tf_op jit(solution)/shard_map/ppermute | solution.py:233
  28.4 1.3 %collective-permute-done.9.refs_5_ = bf16[2,128,512]{2,1,0:T(8,128)(2,1)S(1)} collective-permute-done((bf16[2,128,512]{2,1,0:T(8,128)(2,1)S(1)}, bf16[2,128,512]{2,1,0:T(8,128)(2,1)S(1)}, u32[]{:S(2)}, u32[]{:S(2)}) %collective-permute-start.9) | collective-permute-done | bytes 262176 | tf_op jit(solution)/shard_map/ppermute | solution.py:233
  29.8 0.8 collective-permute-start.4
  30.6 2.3 %collective-permute-start.20 = (bf16[1,128,128]{2,1,0:T(8,128)(2,1)S(1)}, bf16[1,128,128]{2,1,0:T(8,128)(2,1)S(1)}, u32[]{:S(2)}, u32[]{:S(2)}) collective-permute-start(bf16[1,128,128]{2,1,0:T(8,128)(2,1)S(1)} %slice.83), channel_id=1, source_target_pairs={{0,16},{1,17},{2,18},{3,19},{4,20},{5,21},{6,22},{7,23},{8,24},{9,... | collective-permute-start | bytes 98312 | tf_op jit(solution)/shard_map/ppermute | solution.py:230
  32.9 2.3 %collective-permute-done.2.refs_3_ = bf16[2,128,512]{2,1,0:T(8,128)(2,1)S(1)} collective-permute-done((bf16[2,128,512]{2,1,0:T(8,128)(2,1)S(1)}, bf16[2,128,512]{2,1,0:T(8,128)(2,1)S(1)}, u32[]{:S(2)}, u32[]{:S(2)}) %collective-permute-start.2) | collective-permute-done | bytes 262176 | tf_op jit(solution)/shard_map/ppermute | solution.py:233
  36.3 1.3 %collective-permute-start.3 = (bf16[2,128,512]{2,1,0:T(8,128)(2,1)S(1)}, bf16[2,128,512]{2,1,0:T(8,128)(2,1)S(1)}, u32[]{:S(2)}, u32[]{:S(2)}) collective-permute-start(bf16[2,128,512]{2,1,0:T(8,128)(2,1)S(1)} %collective-permute-done.2.refs_3_), channel_id=1, source_target_pairs={{0,4},{1,3},{2,6},{3,1},{4,0},{5,7},{6,2},{7,5},{8,12},{9,11},{10,... | collective-permute-start | bytes 786440 | tf_op jit(solution)/shard_map/ppermute | solution.py:233
  38.2 0.9 %collective-permute-start.21 = (bf16[128,128]{1,0:T(8,128)(2,1)S(1)}, bf16[128,128]{1,0:T(8,128)(2,1)S(1)}, u32[]{:S(2)}, u32[]{:S(2)}) collective-permute-start(bf16[128,128]{1,0:T(8,128)(2,1)S(1)} %convert_element_type.68), channel_id=1, source_target_pairs={{0,2},{1,3},{2,0},{3,1},{4,6},{5,7},{6,4},{7,5},{8,10},{9,11},{10,... | collective-permute-start | bytes 98312 | tf_op jit(solution)/shard_map/ppermute | solution.py:230
  39.1 1.9 %shard_map.65 = (f32[128,512]{1,0:T(8,128)S(1)}, f32[128,128]{1,0:T(8,128)S(1)}) custom-call(s32[3]{0:T(128)S(1)} %pad_add_fusion.where.refs_0_, f32[1,16384]{1,0:T(1,128)S(1)} %get-tuple-element.40.refs_1_, bf16[2,128,512]{2,1,0:T(8,128)(2,1)S(1)} %pad_maximum_fusion.1.refs_2_, bf16[2,128,512]{2,1,0:T(8,128)(2,1)S(1)} %collective-permute-done.7.refs_3_, ...), custom_call_target="tpu_custom_call" | custom-call | flops 1073741824 | bytes 8388608 | tf_op jit(solution)/shard_map/pallas_call | solution.py:165
  41.1 1.3 %shard_map.66 = (f32[128,512]{1,0:T(8,128)S(1)}, f32[128,128]{1,0:T(8,128)S(1)}) custom-call(s32[3]{0:T(128)S(1)} %pad_add_fusion.where.refs_0_, f32[1,16384]{1,0:T(1,128)S(1)} %get-tuple-element.40.refs_1_, bf16[2,128,512]{2,1,0:T(8,128)(2,1)S(1)} %pad_maximum_fusion.refs_2_, bf16[2,128,512]{2,1,0:T(8,128)(2,1)S(1)} %collective-permute-done.2.refs_3_, ...), custom_call_target="tpu_custom_call" | custom-call | flops 536870912 | bytes 4194304 | tf_op jit(solution)/shard_map/pallas_call | solution.py:165
  42.7 0.6 collective-permute-start.22
  43.4 1.2 %shard_map.67 = (f32[128,512]{1,0:T(8,128)S(1)}, f32[128,128]{1,0:T(8,128)S(1)}) custom-call(s32[3]{0:T(128)S(1)} %pad_add_fusion.where.refs_0_, f32[1,16384]{1,0:T(1,128)S(1)} %get-tuple-element.40.refs_1_, bf16[2,128,512]{2,1,0:T(8,128)(2,1)S(1)} %collective-permute-done.15.refs_2_, bf16[2,128,512]{2,1,0:T(8,128)(2,1)S(1)} %collective-permute-done.16.refs_3_, ...), custom_call_target="tpu_custom_call" | custom-call | flops 402653184 | bytes 3145728 | tf_op jit(solution)/shard_map/pallas_call | solution.py:165
  44.6 1.4 %shard_map.68.attended = bf16[128,512]{1,0:T(8,128)(2,1)S(1)} custom-call(s32[3]{0:T(128)S(1)} %pad_add_fusion.where.refs_0_, f32[1,16384]{1,0:T(1,128)S(1)} %get-tuple-element.40.refs_1_, bf16[2,128,512]{2,1,0:T(8,128)(2,1)S(1)} %collective-permute-done.14.refs_2_, bf16[16384,512]{1,0:T(8,128)(2,1)S(1)} %copy-done, ...), custom_call_target="tpu_custom_call" | custom-call | flops 134217728 | bytes 1048576 | tf_op jit(solution)/shard_map/pallas_call | solution.py:165
  46.1 0.8 slice-done.1
  46.8 1.2 %slice-done.2 = s8[4194304]{0:T(1024)(128)(4,1)S(1)} async-done(((s8[16777216]{0:T(1024)(128)(4,1)}), s8[4194304]{0:T(1024)(128)(4,1)S(1)}, s32[]{:S(2)}) %slice-start.2) | async-done | bytes 4194328
  48.0 1.4 %slice-done.3 = s8[4194304]{0:T(1024)(128)(4,1)S(1)} async-done(((s8[16777216]{0:T(1024)(128)(4,1)}), s8[4194304]{0:T(1024)(128)(4,1)S(1)}, s32[]{:S(2)}) %slice-start.3) | async-done | bytes 4194328
  49.4 0.9 shard_map.69
  50.4 1.1 %shard_map.71 = (bf16[2,128,512]{2,1,0:T(8,128)(2,1)S(1)}, bf16[2,128,512]{2,1,0:T(8,128)(2,1)S(1)}, bf16[2,128,512]{2,1,0:T(8,128)(2,1)S(1)}) custom-call(s32[3]{0:T(128)S(1)} %pad_add_fusion.where.refs_0_, bf16[128,512]{1,0:T(8,128)(2,1)S(1)} %shard_map.68.attended, bf16[512,16384]{1,0:T(8,128)(2,1)S(1)} %bitcast.29), custom_call_target="tpu_custom_call" | custom-call | flops 402653184 | bytes 3145728 | tf_op jit(solution)/shard_map/pallas_call | solution.py:197
  51.5 0.6 collective-permute-start.24
  52.6 0.9 %shard_map.70 = bf16[2,128,512]{2,1,0:T(8,128)(2,1)S(1)} custom-call(s32[3]{0:T(128)S(1)} %pad_add_fusion.where.refs_0_, bf16[128,512]{1,0:T(8,128)(2,1)S(1)} %shard_map.68.attended, bf16[2,128,512]{2,1,0:T(8,128)(2,1)S(1)} %collective-permute-done.23.refs_0_, bf16[512,16384]{1,0:T(8,128)(2,1)S(1)} %bitcast.29), custom_call_target="tpu_custom_call" | custom-call | flops 134217728 | bytes 1048576 | tf_op jit(solution)/shard_map/pallas_call | solution.py:197
  53.4 1.5 %collective-permute-start.27 = (bf16[2,128,512]{2,1,0:T(8,128)(2,1)S(1)}, bf16[2,128,512]{2,1,0:T(8,128)(2,1)S(1)}, u32[]{:S(2)}, u32[]{:S(2)}) collective-permute-start(bf16[2,128,512]{2,1,0:T(8,128)(2,1)S(1)} %shard_map.70), channel_id=1, source_target_pairs={{0,2},{1,5},{2,0},{3,7},{4,6},{5,1},{6,4},{7,3},{8,10},{9,13},{10,... | collective-permute-start | bytes 786440 | tf_op jit(solution)/shard_map/ppermute | solution.py:233
  54.9 1.3 %shard_map.73 = (bf16[2,128,512]{2,1,0:T(8,128)(2,1)S(1)}, bf16[2,128,512]{2,1,0:T(8,128)(2,1)S(1)}, bf16[2,128,512]{2,1,0:T(8,128)(2,1)S(1)}, bf16[2,128,512]{2,1,0:T(8,128)(2,1)S(1)}) custom-call(s32[3]{0:T(128)S(1)} %pad_add_fusion.where.refs_0_, bf16[128,512]{1,0:T(8,128)(2,1)S(1)} %shard_map.68.attended, bf16[512,16384]{1,0:T(8,128)(2,1)S(1)} %bitcast.29), custom_call_target="tpu_custom_call" | custom-call | flops 536870912 | bytes 4194304 | tf_op jit(solution)/shard_map/pallas_call | solution.py:197
  57.3 1.1 %shard_map.72 = (f32[2,128,512]{2,1,0:T(8,128)S(1)}, bf16[2,128,512]{2,1,0:T(8,128)(2,1)S(1)}, f32[2,128,512]{2,1,0:T(8,128)S(1)}) custom-call(s32[3]{0:T(128)S(1)} %pad_add_fusion.where.refs_0_, bf16[128,512]{1,0:T(8,128)(2,1)S(1)} %shard_map.68.attended, bf16[2,128,512]{2,1,0:T(8,128)(2,1)S(1)} %collective-permute-done.24.refs_0_, ...), custom_call_target="tpu_custom_call" | custom-call | flops 402653184 | bytes 3145728 | tf_op jit(solution)/shard_map/pallas_call | solution.py:197
  58.4 1.5 %collective-permute-done.27 = bf16[2,128,512]{2,1,0:T(8,128)(2,1)S(1)} collective-permute-done((bf16[2,128,512]{2,1,0:T(8,128)(2,1)S(1)}, bf16[2,128,512]{2,1,0:T(8,128)(2,1)S(1)}, u32[]{:S(2)}, u32[]{:S(2)}) %collective-permute-start.27) | collective-permute-done | bytes 262176 | tf_op jit(solution)/shard_map/ppermute | solution.py:233
  59.9 1.4 %collective-permute-start.36 = (bf16[2,128,512]{2,1,0:T(8,128)(2,1)S(1)}, bf16[2,128,512]{2,1,0:T(8,128)(2,1)S(1)}, u32[]{:S(2)}, u32[]{:S(2)}) collective-permute-start(bf16[2,128,512]{2,1,0:T(8,128)(2,1)S(1)} %get-tuple-element.74), channel_id=1, source_target_pairs={{0,2},{1,5},{2,0},{3,7},{4,6},{5,1},{6,4},{7,3},{8,10},{9,13},{10,... | collective-permute-start | bytes 786440 | tf_op jit(solution)/shard_map/ppermute | solution.py:233
  61.4 0.9 %collective-permute-start.37 = (bf16[2,128,512]{2,1,0:T(8,128)(2,1)S(1)}, bf16[2,128,512]{2,1,0:T(8,128)(2,1)S(1)}, u32[]{:S(2)}, u32[]{:S(2)}) collective-permute-start(bf16[2,128,512]{2,1,0:T(8,128)(2,1)S(1)} %add_convert_fusion.1), channel_id=1, source_target_pairs={{0,4},{1,3},{2,6},{3,1},{4,0},{5,7},{6,2},{7,5},{8,12},{9,11},{10,... | collective-permute-start | bytes 786440 | tf_op jit(solution)/shard_map/ppermute | solution.py:233
  62.2 0.9 %shard_map.74 = bf16[2,128,512]{2,1,0:T(8,128)(2,1)S(1)} custom-call(s32[3]{0:T(128)S(1)} %pad_add_fusion.where.refs_0_, bf16[128,512]{1,0:T(8,128)(2,1)S(1)} %shard_map.68.attended, bf16[2,128,512]{2,1,0:T(8,128)(2,1)S(1)} %collective-permute-done.28.refs_0_, bf16[512,16384]{1,0:T(8,128)(2,1)S(1)} %bitcast.29), custom_call_target="tpu_custom_call" | custom-call | flops 134217728 | bytes 1048576 | tf_op jit(solution)/shard_map/pallas_call | solution.py:197
  63.1 1.2 %collective-permute-start.33 = (bf16[2,128,512]{2,1,0:T(8,128)(2,1)S(1)}, bf16[2,128,512]{2,1,0:T(8,128)(2,1)S(1)}, u32[]{:S(2)}, u32[]{:S(2)}) collective-permute-start(bf16[2,128,512]{2,1,0:T(8,128)(2,1)S(1)} %shard_map.74), channel_id=1, source_target_pairs={{0,2},{1,5},{2,0},{3,7},{4,6},{5,1},{6,4},{7,3},{8,10},{9,13},{10,... | collective-permute-start | bytes 786440 | tf_op jit(solution)/shard_map/ppermute | solution.py:233
  64.3 1.1 %shard_map.75 = (f32[2,128,512]{2,1,0:T(8,128)S(1)}, bf16[2,128,512]{2,1,0:T(8,128)(2,1)S(1)}, f32[2,128,512]{2,1,0:T(8,128)S(1)}) custom-call(s32[3]{0:T(128)S(1)} %pad_add_fusion.where.refs_0_, bf16[128,512]{1,0:T(8,128)(2,1)S(1)} %shard_map.68.attended, bf16[2,128,512]{2,1,0:T(8,128)(2,1)S(1)} %collective-permute-done.29.refs_0_, ...), custom_call_target="tpu_custom_call" | custom-call | flops 402653184 | bytes 3145728 | tf_op jit(solution)/shard_map/pallas_call | solution.py:197
  65.4 1.0 %collective-permute-start.32 = (bf16[2,128,512]{2,1,0:T(8,128)(2,1)S(1)}, bf16[2,128,512]{2,1,0:T(8,128)(2,1)S(1)}, u32[]{:S(2)}, u32[]{:S(2)}) collective-permute-start(bf16[2,128,512]{2,1,0:T(8,128)(2,1)S(1)} %get-tuple-element.71), channel_id=1, source_target_pairs={{0,2},{1,5},{2,0},{3,7},{4,6},{5,1},{6,4},{7,3},{8,10},{9,13},{10,... | collective-permute-start | bytes 786440 | tf_op jit(solution)/shard_map/ppermute | solution.py:233
  66.4 2.0 %collective-permute-done.36 = bf16[2,128,512]{2,1,0:T(8,128)(2,1)S(1)} collective-permute-done((bf16[2,128,512]{2,1,0:T(8,128)(2,1)S(1)}, bf16[2,128,512]{2,1,0:T(8,128)(2,1)S(1)}, u32[]{:S(2)}, u32[]{:S(2)}) %collective-permute-start.36) | collective-permute-done | bytes 262176 | tf_op jit(solution)/shard_map/ppermute | solution.py:233
  68.5 2.2 %collective-permute-done.37 = bf16[2,128,512]{2,1,0:T(8,128)(2,1)S(1)} collective-permute-done((bf16[2,128,512]{2,1,0:T(8,128)(2,1)S(1)}, bf16[2,128,512]{2,1,0:T(8,128)(2,1)S(1)}, u32[]{:S(2)}, u32[]{:S(2)}) %collective-permute-start.37) | collective-permute-done | bytes 262176 | tf_op jit(solution)/shard_map/ppermute | solution.py:233
  70.8 1.0 %collective-permute-start.38 = (bf16[128,512]{1,0:T(8,128)(2,1)S(1)}, bf16[128,512]{1,0:T(8,128)(2,1)S(1)}, u32[]{:S(2)}, u32[]{:S(2)}) collective-permute-start(bf16[128,512]{1,0:T(8,128)(2,1)S(1)} %fusion.6), channel_id=1, source_target_pairs={{0,8},{1,9},{2,10},{3,11},{4,12},{5,13},{6,14},{7,15},{8,0},{9,1},... | collective-permute-start | bytes 393224 | tf_op jit(solution)/shard_map/ppermute | solution.py:230
  72.3 3.5 %collective-permute-done.38 = bf16[128,512]{1,0:T(8,128)(2,1)S(1)} collective-permute-done((bf16[128,512]{1,0:T(8,128)(2,1)S(1)}, bf16[128,512]{1,0:T(8,128)(2,1)S(1)}, u32[]{:S(2)}, u32[]{:S(2)}) %collective-permute-start.38) | collective-permute-done | bytes 131104 | tf_op jit(solution)/shard_map/ppermute | solution.py:230
  75.9 4.0 %collective-permute-start.39 = (bf16[128,512]{1,0:T(8,128)(2,1)S(1)}, bf16[128,512]{1,0:T(8,128)(2,1)S(1)}, u32[]{:S(2)}, u32[]{:S(2)}) collective-permute-start(bf16[128,512]{1,0:T(8,128)(2,1)S(1)} %fusion.1), channel_id=1, source_target_pairs={{0,16},{1,17},{2,18},{3,19},{4,20},{5,21},{6,22},{7,23},{8,24},{9,... | collective-permute-start | bytes 393224 | tf_op jit(solution)/shard_map/ppermute | solution.py:230
  80.1 3.5 %collective-permute-done.39 = bf16[128,512]{1,0:T(8,128)(2,1)S(1)} collective-permute-done((bf16[128,512]{1,0:T(8,128)(2,1)S(1)}, bf16[128,512]{1,0:T(8,128)(2,1)S(1)}, u32[]{:S(2)}, u32[]{:S(2)}) %collective-permute-start.39) | collective-permute-done | bytes 131104 | tf_op jit(solution)/shard_map/ppermute | solution.py:230
  83.6 1.4 %collective-permute-done.35 = bf16[128,512]{1,0:T(8,128)(2,1)S(1)} collective-permute-done((bf16[128,512]{1,0:T(8,128)(2,1)S(1)}, bf16[128,512]{1,0:T(8,128)(2,1)S(1)}, u32[]{:S(2)}, u32[]{:S(2)}) %collective-permute-start.35) | collective-permute-done | bytes 131104 | tf_op jit(solution)/shard_map/ppermute | solution.py:230
  85.1 0.7 fusion.4
  (78 shorter events, 6.1 us)
Async XLA Ops:
  0.0 39.1 %copy-start = (bf16[16384,512]{1,0:T(8,128)(2,1)S(1)}, bf16[16384,512]{1,0:T(8,128)(2,1)}, u32[]{:S(2)}) copy-start(bf16[16384,512]{1,0:T(8,128)(2,1)} %refs_3_.3) | copy-start | bytes 50331652
  3.0 11.8 %collective-permute-start.17 = (f32[8,128,128]{2,1,0:T(8,128)S(1)}, f32[8,128,128]{2,1,0:T(8,128)S(1)}, u32[]{:S(2)}, u32[]{:S(2)}) collective-permute-start(f32[8,128,128]{2,1,0:T(8,128)S(1)} %get-tuple-element.52), channel_id=1, source_target_pairs={{0,1},{1,0},{2,3},{3,2},{4,5},{5,4},{6,7},{7,6},{8,9},{9,8},{10,11... | collective-permute-start | bytes 1572872 | tf_op jit(solution)/shard_map/ppermute | solution.py:230
  3.5 7.0 %collective-permute-start.6 = (bf16[128,512]{1,0:T(8,128)(2,1)}, bf16[128,512]{1,0:T(8,128)(2,1)S(1)}, u32[]{:S(2)}, u32[]{:S(2)}) collective-permute-start(bf16[128,512]{1,0:T(8,128)(2,1)} %act.1), channel_id=1, source_target_pairs={{0,8},{1,9},{2,10},{3,11},{4,12},{5,13},{6,14},{7,15},{8,0},{9,1},... | collective-permute-start | bytes 393224 | tf_op jit(solution)/shard_map/ppermute | solution.py:230
  10.5 11.2 %collective-permute-start.7 = (bf16[2,128,512]{2,1,0:T(8,128)(2,1)S(1)}, bf16[2,128,512]{2,1,0:T(8,128)(2,1)S(1)}, u32[]{:S(2)}, u32[]{:S(2)}) collective-permute-start(bf16[2,128,512]{2,1,0:T(8,128)(2,1)S(1)} %pad_maximum_fusion.1.refs_2_), channel_id=1, source_target_pairs={{0,2},{1,5},{2,0},{3,7},{4,6},{5,1},{6,4},{7,3},{8,10},{9,13},{10,... | collective-permute-start | bytes 786440 | tf_op jit(solution)/shard_map/ppermute | solution.py:233
  12.2 8.7 %collective-permute-start = (bf16[128,512]{1,0:T(8,128)(2,1)}, bf16[128,512]{1,0:T(8,128)(2,1)S(1)}, u32[]{:S(2)}, u32[]{:S(2)}) collective-permute-start(bf16[128,512]{1,0:T(8,128)(2,1)} %act.1), channel_id=1, source_target_pairs={{0,16},{1,17},{2,18},{3,19},{4,20},{5,21},{6,22},{7,23},{8,24},{9,... | collective-permute-start | bytes 393224 | tf_op jit(solution)/shard_map/ppermute | solution.py:230
  14.9 7.3 %collective-permute-start.18 = (bf16[4,128,128]{2,1,0:T(8,128)(2,1)S(1)}, bf16[4,128,128]{2,1,0:T(8,128)(2,1)S(1)}, u32[]{:S(2)}, u32[]{:S(2)}) collective-permute-start(bf16[4,128,128]{2,1,0:T(8,128)(2,1)S(1)} %slice.81), channel_id=1, source_target_pairs={{0,4},{1,5},{2,6},{3,7},{4,0},{5,1},{6,2},{7,3},{8,12},{9,13},{10,... | collective-permute-start | bytes 393224 | tf_op jit(solution)/shard_map/ppermute | solution.py:230
  16.5 16.3 %collective-permute-start.8 = (bf16[2,128,512]{2,1,0:T(8,128)(2,1)S(1)}, bf16[2,128,512]{2,1,0:T(8,128)(2,1)S(1)}, u32[]{:S(2)}, u32[]{:S(2)}) collective-permute-start(bf16[2,128,512]{2,1,0:T(8,128)(2,1)S(1)} %pad_maximum_fusion.1.refs_2_), channel_id=1, source_target_pairs={{0,4},{1,3},{2,6},{3,1},{4,0},{5,7},{6,2},{7,5},{8,12},{9,11},{10,... | collective-permute-start | bytes 786440 | tf_op jit(solution)/shard_map/ppermute | solution.py:233
  17.0 18.9 %collective-permute-start.10 = (bf16[2,128,512]{2,1,0:T(8,128)(2,1)S(1)}, bf16[2,128,512]{2,1,0:T(8,128)(2,1)S(1)}, u32[]{:S(2)}, u32[]{:S(2)}) collective-permute-start(bf16[2,128,512]{2,1,0:T(8,128)(2,1)S(1)} %pad_maximum_fusion.1.refs_2_), channel_id=1, source_target_pairs={{0,1},{1,0},{2,3},{3,2},{4,5},{5,4},{6,7},{7,6},{8,9},{9,8},{10,11... | collective-permute-start | bytes 786440 | tf_op jit(solution)/shard_map/ppermute | solution.py:230
  21.0 5.5 %collective-permute-start.1 = (bf16[128,512]{1,0:T(8,128)(2,1)S(1)}, bf16[128,512]{1,0:T(8,128)(2,1)S(1)}, u32[]{:S(2)}, u32[]{:S(2)}) collective-permute-start(bf16[128,512]{1,0:T(8,128)(2,1)S(1)} %collective-permute-done), channel_id=1, source_target_pairs={{0,8},{1,9},{2,10},{3,11},{4,12},{5,13},{6,14},{7,15},{8,0},{9,1},... | collective-permute-start | bytes 393224 | tf_op jit(solution)/shard_map/ppermute | solution.py:230
  21.7 8.0 %collective-permute-start.9 = (bf16[2,128,512]{2,1,0:T(8,128)(2,1)S(1)}, bf16[2,128,512]{2,1,0:T(8,128)(2,1)S(1)}, u32[]{:S(2)}, u32[]{:S(2)}) collective-permute-start(bf16[2,128,512]{2,1,0:T(8,128)(2,1)S(1)} %collective-permute-done.7.refs_3_), channel_id=1, source_target_pairs={{0,4},{1,3},{2,6},{3,1},{4,0},{5,7},{6,2},{7,5},{8,12},{9,11},{10,... | collective-permute-start | bytes 786440 | tf_op jit(solution)/shard_map/ppermute | solution.py:233
  22.3 8.2 %collective-permute-start.19 = (bf16[2,128,128]{2,1,0:T(8,128)(2,1)S(1)}, bf16[2,128,128]{2,1,0:T(8,128)(2,1)S(1)}, u32[]{:S(2)}, u32[]{:S(2)}) collective-permute-start(bf16[2,128,128]{2,1,0:T(8,128)(2,1)S(1)} %slice.82), channel_id=1, source_target_pairs={{0,8},{1,9},{2,10},{3,11},{4,12},{5,13},{6,14},{7,15},{8,0},{9,1},... | collective-permute-start | bytes 196616 | tf_op jit(solution)/shard_map/ppermute | solution.py:230
  26.5 8.7 %collective-permute-start.2 = (bf16[2,128,512]{2,1,0:T(8,128)(2,1)S(1)}, bf16[2,128,512]{2,1,0:T(8,128)(2,1)S(1)}, u32[]{:S(2)}, u32[]{:S(2)}) collective-permute-start(bf16[2,128,512]{2,1,0:T(8,128)(2,1)S(1)} %pad_maximum_fusion.refs_2_), channel_id=1, source_target_pairs={{0,2},{1,5},{2,0},{3,7},{4,6},{5,1},{6,4},{7,3},{8,10},{9,13},{10,... | collective-permute-start | bytes 786440 | tf_op jit(solution)/shard_map/ppermute | solution.py:233
  29.8 6.5 %collective-permute-start.4 = (bf16[2,128,512]{2,1,0:T(8,128)(2,1)S(1)}, bf16[2,128,512]{2,1,0:T(8,128)(2,1)S(1)}, u32[]{:S(2)}, u32[]{:S(2)}) collective-permute-start(bf16[2,128,512]{2,1,0:T(8,128)(2,1)S(1)} %pad_maximum_fusion.refs_2_), channel_id=1, source_target_pairs={{0,4},{1,3},{2,6},{3,1},{4,0},{5,7},{6,2},{7,5},{8,12},{9,11},{10,... | collective-permute-start | bytes 786440 | tf_op jit(solution)/shard_map/ppermute | solution.py:233
  30.6 4.9 %collective-permute-start.20 = (bf16[1,128,128]{2,1,0:T(8,128)(2,1)S(1)}, bf16[1,128,128]{2,1,0:T(8,128)(2,1)S(1)}, u32[]{:S(2)}, u32[]{:S(2)}) collective-permute-start(bf16[1,128,128]{2,1,0:T(8,128)(2,1)S(1)} %slice.83), channel_id=1, source_target_pairs={{0,16},{1,17},{2,18},{3,19},{4,20},{5,21},{6,22},{7,23},{8,24},{9,... | collective-permute-start | bytes 98312 | tf_op jit(solution)/shard_map/ppermute | solution.py:230
  32.8 4.7 %collective-permute-start.11 = (bf16[2,128,512]{2,1,0:T(8,128)(2,1)S(1)}, bf16[2,128,512]{2,1,0:T(8,128)(2,1)S(1)}, u32[]{:S(2)}, u32[]{:S(2)}) collective-permute-start(bf16[2,128,512]{2,1,0:T(8,128)(2,1)S(1)} %collective-permute-done.7.refs_3_), channel_id=1, source_target_pairs={{0,1},{1,0},{2,3},{3,2},{4,5},{5,4},{6,7},{7,6},{8,9},{9,8},{10,11... | collective-permute-start | bytes 786440 | tf_op jit(solution)/shard_map/ppermute | solution.py:230
  35.2 2.8 %collective-permute-start.12 = (bf16[2,128,512]{2,1,0:T(8,128)(2,1)S(1)}, bf16[2,128,512]{2,1,0:T(8,128)(2,1)S(1)}, u32[]{:S(2)}, u32[]{:S(2)}) collective-permute-start(bf16[2,128,512]{2,1,0:T(8,128)(2,1)S(1)} %collective-permute-done.8.refs_4_), channel_id=1, source_target_pairs={{0,1},{1,0},{2,3},{3,2},{4,5},{5,4},{6,7},{7,6},{8,9},{9,8},{10,11... | collective-permute-start | bytes 786440 | tf_op jit(solution)/shard_map/ppermute | solution.py:230
  35.4 2.7 %collective-permute-start.13 = (bf16[2,128,512]{2,1,0:T(8,128)(2,1)S(1)}, bf16[2,128,512]{2,1,0:T(8,128)(2,1)S(1)}, u32[]{:S(2)}, u32[]{:S(2)}) collective-permute-start(bf16[2,128,512]{2,1,0:T(8,128)(2,1)S(1)} %collective-permute-done.9.refs_5_), channel_id=1, source_target_pairs={{0,1},{1,0},{2,3},{3,2},{4,5},{5,4},{6,7},{7,6},{8,9},{9,8},{10,11... | collective-permute-start | bytes 786440 | tf_op jit(solution)/shard_map/ppermute | solution.py:230
  36.0 5.1 %collective-permute-start.5 = (bf16[2,128,512]{2,1,0:T(8,128)(2,1)S(1)}, bf16[2,128,512]{2,1,0:T(8,128)(2,1)S(1)}, u32[]{:S(2)}, u32[]{:S(2)}) collective-permute-start(bf16[2,128,512]{2,1,0:T(8,128)(2,1)S(1)} %pad_maximum_fusion.refs_2_), channel_id=1, source_target_pairs={{0,1},{1,0},{2,3},{3,2},{4,5},{5,4},{6,7},{7,6},{8,9},{9,8},{10,11... | collective-permute-start | bytes 786440 | tf_op jit(solution)/shard_map/ppermute | solution.py:230
  36.3 6.4 %collective-permute-start.3 = (bf16[2,128,512]{2,1,0:T(8,128)(2,1)S(1)}, bf16[2,128,512]{2,1,0:T(8,128)(2,1)S(1)}, u32[]{:S(2)}, u32[]{:S(2)}) collective-permute-start(bf16[2,128,512]{2,1,0:T(8,128)(2,1)S(1)} %collective-permute-done.2.refs_3_), channel_id=1, source_target_pairs={{0,4},{1,3},{2,6},{3,1},{4,0},{5,7},{6,2},{7,5},{8,12},{9,11},{10,... | collective-permute-start | bytes 786440 | tf_op jit(solution)/shard_map/ppermute | solution.py:233
  37.6 5.8 %collective-permute-start.15 = (bf16[2,128,512]{2,1,0:T(8,128)(2,1)S(1)}, bf16[2,128,512]{2,1,0:T(8,128)(2,1)S(1)}, u32[]{:S(2)}, u32[]{:S(2)}) collective-permute-start(bf16[2,128,512]{2,1,0:T(8,128)(2,1)S(1)} %collective-permute-done.2.refs_3_), channel_id=1, source_target_pairs={{0,1},{1,0},{2,3},{3,2},{4,5},{5,4},{6,7},{7,6},{8,9},{9,8},{10,11... | collective-permute-start | bytes 786440 | tf_op jit(solution)/shard_map/ppermute | solution.py:230
  37.9 5.5 %collective-permute-start.16 = (bf16[2,128,512]{2,1,0:T(8,128)(2,1)S(1)}, bf16[2,128,512]{2,1,0:T(8,128)(2,1)S(1)}, u32[]{:S(2)}, u32[]{:S(2)}) collective-permute-start(bf16[2,128,512]{2,1,0:T(8,128)(2,1)S(1)} %collective-permute-done.4.refs_4_), channel_id=1, source_target_pairs={{0,1},{1,0},{2,3},{3,2},{4,5},{5,4},{6,7},{7,6},{8,9},{9,8},{10,11... | collective-permute-start | bytes 786440 | tf_op jit(solution)/shard_map/ppermute | solution.py:230
  38.2 4.5 %collective-permute-start.21 = (bf16[128,128]{1,0:T(8,128)(2,1)S(1)}, bf16[128,128]{1,0:T(8,128)(2,1)S(1)}, u32[]{:S(2)}, u32[]{:S(2)}) collective-permute-start(bf16[128,128]{1,0:T(8,128)(2,1)S(1)} %convert_element_type.68), channel_id=1, source_target_pairs={{0,2},{1,3},{2,0},{3,1},{4,6},{5,7},{6,4},{7,5},{8,10},{9,11},{10,... | collective-permute-start | bytes 98312 | tf_op jit(solution)/shard_map/ppermute | solution.py:230
  42.7 2.0 %collective-permute-start.14 = (bf16[2,128,512]{2,1,0:T(8,128)(2,1)S(1)}, bf16[2,128,512]{2,1,0:T(8,128)(2,1)S(1)}, u32[]{:S(2)}, u32[]{:S(2)}) collective-permute-start(bf16[2,128,512]{2,1,0:T(8,128)(2,1)S(1)} %collective-permute-done.3.refs_4_), channel_id=1, source_target_pairs={{0,1},{1,0},{2,3},{3,2},{4,5},{5,4},{6,7},{7,6},{8,9},{9,8},{10,11... | collective-permute-start | bytes 786440 | tf_op jit(solution)/shard_map/ppermute | solution.py:230
  42.7 1.9 %collective-permute-start.22 = (f32[128,128]{1,0:T(8,128)S(1)}, f32[128,128]{1,0:T(8,128)S(1)}, u32[]{:S(2)}, u32[]{:S(2)}) collective-permute-start(f32[128,128]{1,0:T(8,128)S(1)} %convert_add_fusion.2.refs_6_), channel_id=1, source_target_pairs={{0,1},{1,0},{2,3},{3,2},{4,5},{5,4},{6,7},{7,6},{8,9},{9,8},{10,11... | collective-permute-start | bytes 196616 | tf_op jit(solution)/shard_map/ppermute | solution.py:230
  43.4 2.7 %slice-start = ((s8[16777216]{0:T(1024)(128)(4,1)}), s8[4194304]{0:T(1024)(128)(4,1)S(1)}, s32[]{:S(2)}) async-start(s8[16777216]{0:T(1024)(128)(4,1)} %bitcast.28), calls=%async_computation | async-start | bytes 8388608
  43.4 3.5 %slice-start.1 = ((s8[16777216]{0:T(1024)(128)(4,1)}), s8[4194304]{0:T(1024)(128)(4,1)S(1)}, s32[]{:S(2)}) async-start(s8[16777216]{0:T(1024)(128)(4,1)} %bitcast.28), calls=%async_computation.1 | async-start | bytes 8388608
  43.4 4.6 %slice-start.2 = ((s8[16777216]{0:T(1024)(128)(4,1)}), s8[4194304]{0:T(1024)(128)(4,1)S(1)}, s32[]{:S(2)}) async-start(s8[16777216]{0:T(1024)(128)(4,1)} %bitcast.28), calls=%async_computation.2 | async-start | bytes 8388608
  44.6 4.8 %slice-start.3 = ((s8[16777216]{0:T(1024)(128)(4,1)}), s8[4194304]{0:T(1024)(128)(4,1)S(1)}, s32[]{:S(2)}) async-start(s8[16777216]{0:T(1024)(128)(4,1)} %bitcast.28), calls=%async_computation.3 | async-start | bytes 8388608
  50.3 2.3 %collective-permute-start.23 = (bf16[2,128,512]{2,1,0:T(8,128)(2,1)S(1)}, bf16[2,128,512]{2,1,0:T(8,128)(2,1)S(1)}, u32[]{:S(2)}, u32[]{:S(2)}) collective-permute-start(bf16[2,128,512]{2,1,0:T(8,128)(2,1)S(1)} %shard_map.69), channel_id=1, source_target_pairs={{0,1},{1,0},{2,3},{3,2},{4,5},{5,4},{6,7},{7,6},{8,9},{9,8},{10,11... | collective-permute-start | bytes 786440 | tf_op jit(solution)/shard_map/ppermute | solution.py:230
  51.5 4.8 %collective-permute-start.24 = (bf16[2,128,512]{2,1,0:T(8,128)(2,1)S(1)}, bf16[2,128,512]{2,1,0:T(8,128)(2,1)S(1)}, u32[]{:S(2)}, u32[]{:S(2)}) collective-permute-start(bf16[2,128,512]{2,1,0:T(8,128)(2,1)S(1)} %get-tuple-element.59), channel_id=1, source_target_pairs={{0,1},{1,0},{2,3},{3,2},{4,5},{5,4},{6,7},{7,6},{8,9},{9,8},{10,11... | collective-permute-start | bytes 786440 | tf_op jit(solution)/shard_map/ppermute | solution.py:230
  52.1 4.7 %collective-permute-start.25 = (bf16[2,128,512]{2,1,0:T(8,128)(2,1)S(1)}, bf16[2,128,512]{2,1,0:T(8,128)(2,1)S(1)}, u32[]{:S(2)}, u32[]{:S(2)}) collective-permute-start(bf16[2,128,512]{2,1,0:T(8,128)(2,1)S(1)} %get-tuple-element.60), channel_id=1, source_target_pairs={{0,1},{1,0},{2,3},{3,2},{4,5},{5,4},{6,7},{7,6},{8,9},{9,8},{10,11... | collective-permute-start | bytes 786440 | tf_op jit(solution)/shard_map/ppermute | solution.py:230
  52.1 4.7 %collective-permute-start.26 = (bf16[2,128,512]{2,1,0:T(8,128)(2,1)S(1)}, bf16[2,128,512]{2,1,0:T(8,128)(2,1)S(1)}, u32[]{:S(2)}, u32[]{:S(2)}) collective-permute-start(bf16[2,128,512]{2,1,0:T(8,128)(2,1)S(1)} %get-tuple-element.61), channel_id=1, source_target_pairs={{0,1},{1,0},{2,3},{3,2},{4,5},{5,4},{6,7},{7,6},{8,9},{9,8},{10,11... | collective-permute-start | bytes 786440 | tf_op jit(solution)/shard_map/ppermute | solution.py:230
  53.4 6.4 %collective-permute-start.27 = (bf16[2,128,512]{2,1,0:T(8,128)(2,1)S(1)}, bf16[2,128,512]{2,1,0:T(8,128)(2,1)S(1)}, u32[]{:S(2)}, u32[]{:S(2)}) collective-permute-start(bf16[2,128,512]{2,1,0:T(8,128)(2,1)S(1)} %shard_map.70), channel_id=1, source_target_pairs={{0,2},{1,5},{2,0},{3,7},{4,6},{5,1},{6,4},{7,3},{8,10},{9,13},{10,... | collective-permute-start | bytes 786440 | tf_op jit(solution)/shard_map/ppermute | solution.py:233
  56.2 5.2 %collective-permute-start.28 = (bf16[2,128,512]{2,1,0:T(8,128)(2,1)S(1)}, bf16[2,128,512]{2,1,0:T(8,128)(2,1)S(1)}, u32[]{:S(2)}, u32[]{:S(2)}) collective-permute-start(bf16[2,128,512]{2,1,0:T(8,128)(2,1)S(1)} %get-tuple-element.65), channel_id=1, source_target_pairs={{0,1},{1,0},{2,3},{3,2},{4,5},{5,4},{6,7},{7,6},{8,9},{9,8},{10,11... | collective-permute-start | bytes 786440 | tf_op jit(solution)/shard_map/ppermute | solution.py:230
  56.3 6.8 %collective-permute-start.29 = (bf16[2,128,512]{2,1,0:T(8,128)(2,1)S(1)}, bf16[2,128,512]{2,1,0:T(8,128)(2,1)S(1)}, u32[]{:S(2)}, u32[]{:S(2)}) collective-permute-start(bf16[2,128,512]{2,1,0:T(8,128)(2,1)S(1)} %get-tuple-element.67), channel_id=1, source_target_pairs={{0,1},{1,0},{2,3},{3,2},{4,5},{5,4},{6,7},{7,6},{8,9},{9,8},{10,11... | collective-permute-start | bytes 786440 | tf_op jit(solution)/shard_map/ppermute | solution.py:230
  56.8 7.5 %collective-permute-start.30 = (bf16[2,128,512]{2,1,0:T(8,128)(2,1)S(1)}, bf16[2,128,512]{2,1,0:T(8,128)(2,1)S(1)}, u32[]{:S(2)}, u32[]{:S(2)}) collective-permute-start(bf16[2,128,512]{2,1,0:T(8,128)(2,1)S(1)} %get-tuple-element.68), channel_id=1, source_target_pairs={{0,1},{1,0},{2,3},{3,2},{4,5},{5,4},{6,7},{7,6},{8,9},{9,8},{10,11... | collective-permute-start | bytes 786440 | tf_op jit(solution)/shard_map/ppermute | solution.py:230
  56.9 7.4 %collective-permute-start.31 = (bf16[2,128,512]{2,1,0:T(8,128)(2,1)S(1)}, bf16[2,128,512]{2,1,0:T(8,128)(2,1)S(1)}, u32[]{:S(2)}, u32[]{:S(2)}) collective-permute-start(bf16[2,128,512]{2,1,0:T(8,128)(2,1)S(1)} %get-tuple-element.69), channel_id=1, source_target_pairs={{0,1},{1,0},{2,3},{3,2},{4,5},{5,4},{6,7},{7,6},{8,9},{9,8},{10,11... | collective-permute-start | bytes 786440 | tf_op jit(solution)/shard_map/ppermute | solution.py:230
  59.9 8.6 %collective-permute-start.36 = (bf16[2,128,512]{2,1,0:T(8,128)(2,1)S(1)}, bf16[2,128,512]{2,1,0:T(8,128)(2,1)S(1)}, u32[]{:S(2)}, u32[]{:S(2)}) collective-permute-start(bf16[2,128,512]{2,1,0:T(8,128)(2,1)S(1)} %get-tuple-element.74), channel_id=1, source_target_pairs={{0,2},{1,5},{2,0},{3,7},{4,6},{5,1},{6,4},{7,3},{8,10},{9,13},{10,... | collective-permute-start | bytes 786440 | tf_op jit(solution)/shard_map/ppermute | solution.py:233
  61.4 9.3 %collective-permute-start.37 = (bf16[2,128,512]{2,1,0:T(8,128)(2,1)S(1)}, bf16[2,128,512]{2,1,0:T(8,128)(2,1)S(1)}, u32[]{:S(2)}, u32[]{:S(2)}) collective-permute-start(bf16[2,128,512]{2,1,0:T(8,128)(2,1)S(1)} %add_convert_fusion.1), channel_id=1, source_target_pairs={{0,4},{1,3},{2,6},{3,1},{4,0},{5,7},{6,2},{7,5},{8,12},{9,11},{10,... | collective-permute-start | bytes 786440 | tf_op jit(solution)/shard_map/ppermute | solution.py:233
  63.1 8.7 %collective-permute-start.33 = (bf16[2,128,512]{2,1,0:T(8,128)(2,1)S(1)}, bf16[2,128,512]{2,1,0:T(8,128)(2,1)S(1)}, u32[]{:S(2)}, u32[]{:S(2)}) collective-permute-start(bf16[2,128,512]{2,1,0:T(8,128)(2,1)S(1)} %shard_map.74), channel_id=1, source_target_pairs={{0,2},{1,5},{2,0},{3,7},{4,6},{5,1},{6,4},{7,3},{8,10},{9,13},{10,... | collective-permute-start | bytes 786440 | tf_op jit(solution)/shard_map/ppermute | solution.py:233
  65.4 14.4 %collective-permute-start.32 = (bf16[2,128,512]{2,1,0:T(8,128)(2,1)S(1)}, bf16[2,128,512]{2,1,0:T(8,128)(2,1)S(1)}, u32[]{:S(2)}, u32[]{:S(2)}) collective-permute-start(bf16[2,128,512]{2,1,0:T(8,128)(2,1)S(1)} %get-tuple-element.71), channel_id=1, source_target_pairs={{0,2},{1,5},{2,0},{3,7},{4,6},{5,1},{6,4},{7,3},{8,10},{9,13},{10,... | collective-permute-start | bytes 786440 | tf_op jit(solution)/shard_map/ppermute | solution.py:233
  70.8 5.0 %collective-permute-start.38 = (bf16[128,512]{1,0:T(8,128)(2,1)S(1)}, bf16[128,512]{1,0:T(8,128)(2,1)S(1)}, u32[]{:S(2)}, u32[]{:S(2)}) collective-permute-start(bf16[128,512]{1,0:T(8,128)(2,1)S(1)} %fusion.6), channel_id=1, source_target_pairs={{0,8},{1,9},{2,10},{3,11},{4,12},{5,13},{6,14},{7,15},{8,0},{9,1},... | collective-permute-start | bytes 393224 | tf_op jit(solution)/shard_map/ppermute | solution.py:230
  72.0 7.9 %collective-permute-start.34 = (bf16[2,128,512]{2,1,0:T(8,128)(2,1)S(1)}, bf16[2,128,512]{2,1,0:T(8,128)(2,1)S(1)}, u32[]{:S(2)}, u32[]{:S(2)}) collective-permute-start(bf16[2,128,512]{2,1,0:T(8,128)(2,1)S(1)} %add_convert_fusion), channel_id=1, source_target_pairs={{0,4},{1,3},{2,6},{3,1},{4,0},{5,7},{6,2},{7,5},{8,12},{9,11},{10,... | collective-permute-start | bytes 786440 | tf_op jit(solution)/shard_map/ppermute | solution.py:233
  75.9 7.7 %collective-permute-start.39 = (bf16[128,512]{1,0:T(8,128)(2,1)S(1)}, bf16[128,512]{1,0:T(8,128)(2,1)S(1)}, u32[]{:S(2)}, u32[]{:S(2)}) collective-permute-start(bf16[128,512]{1,0:T(8,128)(2,1)S(1)} %fusion.1), channel_id=1, source_target_pairs={{0,16},{1,17},{2,18},{3,19},{4,20},{5,21},{6,22},{7,23},{8,24},{9,... | collective-permute-start | bytes 393224 | tf_op jit(solution)/shard_map/ppermute | solution.py:230
  80.0 5.0 %collective-permute-start.35 = (bf16[128,512]{1,0:T(8,128)(2,1)S(1)}, bf16[128,512]{1,0:T(8,128)(2,1)S(1)}, u32[]{:S(2)}, u32[]{:S(2)}) collective-permute-start(bf16[128,512]{1,0:T(8,128)(2,1)S(1)} %fusion.5), channel_id=1, source_target_pairs={{0,8},{1,9},{2,10},{3,11},{4,12},{5,13},{6,14},{7,15},{8,0},{9,1},... | collective-permute-start | bytes 393224 | tf_op jit(solution)/shard_map/ppermute | solution.py:230

commit v7 on v6

--- a/solution.py
+++ b/solution.py
@@ -42,6 +42,35 @@
 
 def dot(a, b):
     return jnp.dot(a, b, preferred_element_type=jnp.float32)
+
+
+def fetch_kernel(symbols, width, where, source, target, sems):
+    copies = []
+    for i, (const, pick) in enumerate(symbols):
+        start = pl.multiple_of((where[pick] ^ const) * width, LANE)
+        copy = pltpu.make_async_copy(
+            source.at[:, pl.ds(start, width)], target.at[:, pl.ds(i * width, width)], sems.at[i]
+        )
+        copy.start()
+        copies.append(copy)
+    for copy in copies:
+        copy.wait()
+
+
+def fetched(where, weight, width, symbols):
+    shape = (weight.shape[0], len(symbols) * width)
+    columns = pl.pallas_call(
+        functools.partial(fetch_kernel, symbols, width),
+        out_shape=jax.ShapeDtypeStruct(shape, weight.dtype),
+        in_specs=[smem(), hbm()],
+        out_specs=vmem(),
+        scratch_shapes=[pltpu.SemaphoreType.DMA((len(symbols),))],
+        compiler_params=pltpu.CompilerParams(vmem_limit_bytes=MIB),
+        cost_estimate=pl.CostEstimate(
+            flops=0, bytes_accessed=4 * shape[0] * shape[1], transcendentals=0
+        ),
+    )(where, in_hbm(weight))
+    return columns, symbols
 
 
 def kv_kernel(shared, where, act, gain, wk, wv, send, keep, abuf, gbuf, kbuf, vbuf, sems):
@@ -167,7 +196,7 @@
         out_shape=out_shape,
         in_specs=[smem()] + [vmem()] * count,
         out_specs=[vmem()] * len(out_shape),
-        compiler_params=pltpu.CompilerParams(vmem_limit_bytes=12 * MIB),
+        compiler_params=pltpu.CompilerParams(vmem_limit_bytes=4 * MIB),
         cost_estimate=pl.CostEstimate(
             flops=2 * tokens * columns * rows,
             bytes_accessed=2 * columns * rows,
@@ -176,36 +205,31 @@
     )(where, gain, *arrays, weight, *carry, *extra)
 
 
-def output_kernel(groups, width, where, attended, *refs):
-    refs = list(refs)
-    added = [refs.pop(0) if g[1] else None for g in groups]
-    weight = refs.pop(0)
+def output_kernel(groups, width, attended, weight, *outs):
     left = attended[...]
-    for (symbols, _), arrived, out in zip(groups, added, refs):
-        for block, (const, pick) in enumerate(symbols):
-            span = pl.ds(pl.multiple_of((where[pick] ^ const) * width, LANE), width)
-            term = dot(left, weight[:, span])
-            if arrived is not None:
-                term = term + arrived[block].astype(jnp.float32)
-            out[block] = term.astype(out.dtype)
-
-
-def output_call(where, attended, weight, width, groups):
+    for spots, out in zip(groups, outs):
+        for block, spot in enumerate(spots):
+            columns = weight[:, spot * width : (spot + 1) * width]
+            out[block] = dot(left, columns).astype(out.dtype)
+
+
+def output_call(attended, held, width, groups):
+    weight, order = held
     tokens, depth = attended.shape
-    blocks = sum(len(g[0]) for g in groups)
-    added = [g[2] for g in groups if g[2] is not None]
+    spots = [[order.index(s) for s in symbols] for symbols, _ in groups]
+    columns = width * sum(len(s) for s in spots)
     return pl.pallas_call(
-        functools.partial(output_kernel, [(s, a is not None) for s, _, a in groups], width),
-        out_shape=[jax.ShapeDtypeStruct((len(s), tokens, width), t) for s, t, _ in groups],
-        in_specs=[smem()] + [vmem()] * (2 + len(added)),
+        functools.partial(output_kernel, spots, width),
+        out_shape=[jax.ShapeDtypeStruct((len(s), tokens, width), t) for s, t in groups],
+        in_specs=[vmem(), vmem()],
         out_specs=[vmem()] * len(groups),
-        compiler_params=pltpu.CompilerParams(vmem_limit_bytes=12 * MIB),
+        compiler_params=pltpu.CompilerParams(vmem_limit_bytes=4 * MIB),
         cost_estimate=pl.CostEstimate(
-            flops=2 * tokens * depth * width * blocks,
-            bytes_accessed=2 * depth * width * blocks,
+            flops=2 * tokens * depth * columns,
+            bytes_accessed=2 * depth * columns,
             transcendentals=0,
         ),
-    )(where, attended, *added, weight)
+    )(attended, weight)
 
 
 def rotary_tables(tokens):
@@ -256,57 +280,71 @@
     def other(pieces):
         return [(swap(x, CORE), across(symbols)) for x, symbols in pieces]
 
-    groups, z_first = [], [raw] + [swap(raw, o) for o in near[1:]]
-    for offsets in (near, far):
-        if offsets is far:
-            first = swap(raw, top)
-            row = jnp.stack([first] + [swap(first, o) for o in near[1:]])
+    def order(offsets):
+        home, one, two, corner = symbols_of(offsets)
+        return [corner, two, one, home]
+
+    def columns_of(offsets):
+        own = sum(order(offsets), [])
+        return own + across(own)
+
+    def halved(kv, arrived=None, offset=0):
+        half = kv.shape[0] // 2
+        if arrived is None:
+            arrived = swap(kv[:half].astype(bf16), offset)
+        return kv[half:] + arrived.astype(f32)
+
+    kv = halved(kv_keep + swap(kv_send, CORE), offset=bits[shared])
+    row = jnp.stack([act, swap(raw, top)])
+    far_columns, far_symbols = fetched(where, wo, width, columns_of(far))
+    row, kv, far_columns = lax.optimization_barrier((row, kv, far_columns))
+    far_held = (far_columns, far_symbols)
+    ride = bits[shared + 1]
+    side = turn(row, 0)
+    rest = []
+    for o in near[1:]:
+        if o == ride:
+            got = swap(jnp.concatenate([row, kv[: kv.shape[0] // 2].astype(bf16)], axis=2), o)
+            kv = halved(kv, got[:, :, width:])
+            got = got[:, :, :width]
         else:
-            row = jnp.stack([act] + z_first[1:])
-        one, two = turn(row, 0), turn(row, 1)
-        corner = turn(one, 1)
-        groups.append(list(zip((row, one, two, corner), symbols_of(offsets))))
+            got = swap(row, o)
+        rest.append(got)
+    groups = []
+    for offsets, row, side in (
+        ([0, top], row, side),
+        ([o ^ t for o in near[1:] for t in (0, top)], jnp.concatenate(rest), None),
+    ):
+        side = turn(row, 0) if side is None else side
+        both = turn(jnp.concatenate([row, side]), 1)
+        at = symbols_of(offsets)
+        groups.append([(row, at[0]), (side, at[1]), (both, at[2] + at[3])])
     early, last = groups
-
-    kv = kv_keep + swap(kv_send, CORE)
-    steps = [early[1][0], early[3][0], last[1][0]]
-    for b, step in zip(bits[shared:], steps):
-        half = kv.shape[0] // 2
-        got = after(swap(kv[:half].astype(bf16), b), step)
-        kv = kv[half:] + got.astype(f32)
-    total = after(kv[0], last[2][0])
+    for b in bits[shared + 2 :]:
+        got = after(swap(kv[: kv.shape[0] // 2].astype(bf16), b), last[1][0])
+        kv = halved(kv, got)
+    total = kv[0]
     for b in bits[1:shared]:
         total = total + swap(total.astype(bf16), b).astype(f32)
     kv_sums = (total, swap(total, CORE))
 
     call = functools.partial(query_call, where, gain, weight=wq)
     carry = call(early + other(early))
-    carry = call(last[:3] + other(last[:1]), carry=carry)
-    corner, *carry = lax.optimization_barrier((last[3][0], *carry))
-    corner = [(corner, last[3][1])]
-    final = other(corner)
-    carry = call(other(last[1:3]) + corner, carry=carry)
+    carry = call(last[:2] + other(last[:1]), carry=carry)
+    both, *carry = lax.optimization_barrier((last[2][0], *carry))
+    both = [(both, last[2][1])]
+    final = other(both)
+    carry = call(other(last[1:2]) + both, carry=carry)
     (attended,) = call(final, carry=carry, extra=(*kv_sums, *rotary_tables(tokens)))
 
-    def project(left, wanted, arrived=None):
-        if arrived is None:
-            wanted = [(across(s), bf16, None) for s, _ in wanted]
-        else:
-            wanted = [(*g, a) for g, a in zip(wanted, arrived)]
-        return output_call(where, left, wo, width, wanted)
-
-    def wanted(offsets):
-        home, one, two, corner = symbols_of(offsets)
-        return [(corner, bf16)], [(two, f32), (one, bf16), (home, f32)]
-
-    def round_square(offsets, left, got):
-        leave, stay = wanted(offsets)
-        (leaving,) = project(left, leave, got[:1])
-        from_corner = turn(leaving, 0)
-        two, one, home = project(after(left, leaving), stay, got[1:])
-        got_1 = turn(one, 0)
-        two = (two + from_corner.astype(f32)).astype(bf16)
-        return [home, got_1, turn(two, 1)], after(left, two)
+    def round_square(corner, terms, wait=False):
+        (two, two_got), (one, one_got), (home, home_got) = terms
+        from_corner = turn(corner, 0)
+        if wait:
+            one = after(one, from_corner)
+        got_1 = turn(added_up(one, one_got).astype(bf16), 0)
+        two = added_up(two, two_got, from_corner).astype(bf16)
+        return [home, home_got, got_1, turn(two, 1)], two
 
     def added_up(home, *arrived):
         for x in arrived:
@@ -318,14 +356,25 @@
             blocks[0], *[swap(blocks[i].astype(bf16), o) for i, o in enumerate(near) if o]
         )
 
-    left, sent = attended, []
-    leave, stay = wanted(far)
-    for groups in (leave, stay, sum(wanted(near), [])):
-        sent += project(left, groups)
-        left = after(left, sent[-1])
-    got = [swap(x, CORE) for x in sent]
-    far_sums, left = round_square(far, attended, got[:4])
-    near_sums, _ = round_square(near, left, got[4:])
+    def theirs(symbols):
+        return [(across(s), bf16) for s in symbols]
+
+    def ours(symbols):
+        return [(s, f32) for s in symbols]
+
+    project = functools.partial(output_call, held=far_held, width=width)
+    sent = project(attended, groups=theirs(order(far)[:1]))
+    own = project(after(attended, *sent), groups=ours(order(far)))
+    corner = added_up(own[0], swap(sent[0], CORE)).astype(bf16)
+    sent = project(after(attended, corner), groups=theirs(order(far)[1:]))
+    terms = [(x, swap(y, CORE)) for x, y in zip(own[1:], sent)]
+    far_sums, two = round_square(corner, terms)
+    near_held = fetched(after(where, sent[-1]), wo, width, columns_of(near))
+    sent = output_call(attended, near_held, width, theirs(order(near)))
+    own = output_call(after(attended, sent[0]), near_held, width, ours(order(near)))
+    terms = [(x, swap(y, CORE)) for x, y in zip(own, sent)]
+    corner = added_up(after(own[0], two), terms[0][1]).astype(bf16)
+    near_sums, _ = round_square(corner, terms[1:], wait=True)
     got = swap(along_z(added_up(*far_sums)).astype(bf16), top)
     out = added_up(along_z(added_up(*near_sums)), got)
     return out.astype(bf16)

time: 85.9 us -> 86.5 us (level)
  Pallas kernels: 16 us -> 20.7 us
  starting transfers between devices: 34.7 us -> 30.7 us
  local copies, waits for them, and re-layouts: 3.45 us -> 0.12 us
  waiting for transfers between devices: 29.4 us -> 32.2 us
    ppermute x12 -> x10, waiting for transfers between devices: 9.59 us -> 20.7 us  [turn(): lax.ppermute(x, 'wide', [(i, i ^ ways[(step + (i & CORE)) % 2]) for i in...]
    ppermute x28 -> x24, waiting for transfers between devices: 19.8 us -> 11.4 us  [swap(): return lax.ppermute(x, 'wide', [(i, i ^ offset) for i in range(n)])]
    pallas_call x7, Pallas kernels: 7.25 us -> 12.2 us  [the longest x2 9.01 us: fetched(): pl.pallas_call(functools.partial(fetch_kernel, symbols, width), out_shape...]
    unnamed x10 -> x8, local copies, waits for them, and re-layouts: 3.38 us -> 0.02 us
    ppermute x28 -> x24, starting transfers between devices: 21.7 us -> 19.1 us  [swap(): return lax.ppermute(x, 'wide', [(i, i ^ offset) for i in range(n)])]
    ppermute x12 -> x10, starting transfers between devices: 13 us -> 11.6 us  [turn(): lax.ppermute(x, 'wide', [(i, i ^ ways[(step + (i & CORE)) % 2]) for i in...]
  transfers between devices with their start and end apart: 40 -> 34, of which waited for: 13 -> 14; matrix products, arithmetic and copies ran while one was open for 1% -> 2% of each run, Pallas kernels for 13% -> 18%
where the time goes in v7:
time: 86.5 us; the launch traced here: 86.4 us
  waiting for transfers between devices  32.2 us (37%)
  starting transfers between devices  30.7 us (35%)
  Pallas kernels  20.7 us (24%)
  other arithmetic  2.22 us (3%)
    ppermute x10, waiting for transfers between devices, turn(): lax.ppermute(x, 'wide', [(i, i ^ ways[(step + (i & CORE)) % 2]) for i in...  20.7 us
    ppermute x24, starting transfers between devices, swap(): return lax.ppermute(x, 'wide', [(i, i ^ offset) for i in range(n)])  19.1 us
    ppermute x10, starting transfers between devices, turn(): lax.ppermute(x, 'wide', [(i, i ^ ways[(step + (i & CORE)) % 2]) for i in...  11.6 us
    ppermute x24, waiting for transfers between devices, swap(): return lax.ppermute(x, 'wide', [(i, i ^ offset) for i in range(n)])  11.4 us
    pallas_call x2, Pallas kernels, fetched(): pl.pallas_call(functools.partial(fetch_kernel, symbols, width), out_shape...  9.01 us
    pallas_call x4, Pallas kernels, query_call(): pl.pallas_call(functools.partial(query_kernel, places, bool(carry), bool(...  5.85 us
    pallas_call x5, Pallas kernels, output_call(): pl.pallas_call(functools.partial(output_kernel, spots, width), out_shape=...  3.2 us
    pallas_call x1, Pallas kernels, kv_terms(): pl.pallas_call(functools.partial(kv_kernel, shared), out_shape=[jax.Shape...  2.69 us
  transfers between devices with their start and end apart: 34, of which 14 were waited for; matrix products, arithmetic and copies ran while one was open for 2% of the time, Pallas kernels for 18%

profile of v7, /device:TPU:0, one launch (start us, length us, event | category | flops | bytes accessed | tf_op | source)
XLA Modules:
  0.0 86.4 jit_solution(11098516996211009312)
XLA Ops:
  0.1 2.7 %shard_map.64 = (f32[8,128,128]{2,1,0:T(8,128)S(1)}, f32[8,128,128]{2,1,0:T(8,128)S(1)}, bf16[128,512]{1,0:T(8,128)(2,1)S(1)}, f32[1,16384]{1,0:T(1,128)S(1)}) custom-call(s32[3]{0:T(128)S(1)} %pad_add_fusion.where.refs_0_, bf16[128,512]{1,0:T(8,128)(2,1)} %act.1, f32[1,16384]{1,0:T(1,128)} %bitcast.34, bf16[512,1024]{1,0:T(8,128)(2,1)} %wk.1, ...), custom_call_target="tpu_custom_call" | custom-call | flops 4294967296 | bytes 33554432 | tf_op jit(solution)/shard_map/pallas_call | solution.py:101
  2.8 0.5 collective-permute-start.1
  3.3 3.7 %collective-permute-start = (bf16[128,512]{1,0:T(8,128)(2,1)}, bf16[128,512]{1,0:T(8,128)(2,1)S(1)}, u32[]{:S(2)}, u32[]{:S(2)}) collective-permute-start(bf16[128,512]{1,0:T(8,128)(2,1)} %act.1), channel_id=1, source_target_pairs={{0,16},{1,17},{2,18},{3,19},{4,20},{5,21},{6,22},{7,23},{8,24},{9,... | collective-permute-start | bytes 393224 | tf_op jit(solution)/shard_map/ppermute | solution.py:254
  7.1 1.6 %collective-permute-start.2 = (bf16[4,128,128]{2,1,0:T(8,128)(2,1)S(1)}, bf16[4,128,128]{2,1,0:T(8,128)(2,1)S(1)}, u32[]{:S(2)}, u32[]{:S(2)}) collective-permute-start(bf16[4,128,128]{2,1,0:T(8,128)(2,1)S(1)} %slice.95), channel_id=1, source_target_pairs={{0,4},{1,5},{2,6},{3,7},{4,0},{5,1},{6,2},{7,3},{8,12},{9,13},{10,... | collective-permute-start | bytes 393224 | tf_op jit(solution)/shard_map/ppermute | solution.py:254
  8.7 4.9 %shard_map.65.weight = bf16[512,8192]{1,0:T(8,128)(2,1)S(1)} custom-call(s32[3]{0:T(128)S(1)} %pad_add_fusion.where.refs_0_, bf16[512,16384]{1,0:T(8,128)(2,1)} %source.3), custom_call_target="tpu_custom_call" | custom-call | bytes 16777216 | tf_op jit(solution)/shard_map/pallas_call | solution.py:62
  13.6 0.5 collective-permute-done
  14.2 1.6 %collective-permute-start.7 = (bf16[2,128,512]{2,1,0:T(8,128)(2,1)S(1)}, bf16[2,128,512]{2,1,0:T(8,128)(2,1)S(1)}, u32[]{:S(2)}, u32[]{:S(2)}) collective-permute-start(bf16[2,128,512]{2,1,0:T(8,128)(2,1)S(1)} %pad_maximum_fusion.3.refs_2_), channel_id=1, source_target_pairs={{0,2},{1,5},{2,0},{3,7},{4,6},{5,1},{6,4},{7,3},{8,10},{9,13},{10,... | collective-permute-start | bytes 786440 | tf_op jit(solution)/shard_map/ppermute | solution.py:257
  15.8 1.1 %collective-permute-start.3 = (bf16[2,128,640]{2,1,0:T(8,128)(2,1)S(1)}, bf16[2,128,640]{2,1,0:T(8,128)(2,1)S(1)}, u32[]{:S(2)}, u32[]{:S(2)}) collective-permute-start(bf16[2,128,640]{2,1,0:T(8,128)(2,1)S(1)} %pad_maximum_fusion.2), channel_id=1, source_target_pairs={{0,8},{1,9},{2,10},{3,11},{4,12},{5,13},{6,14},{7,15},{8,0},{9,1},... | collective-permute-start | bytes 983048 | tf_op jit(solution)/shard_map/ppermute | solution.py:254
  16.9 3.7 %collective-permute-done.7.refs_3_ = bf16[2,128,512]{2,1,0:T(8,128)(2,1)S(1)} collective-permute-done((bf16[2,128,512]{2,1,0:T(8,128)(2,1)S(1)}, bf16[2,128,512]{2,1,0:T(8,128)(2,1)S(1)}, u32[]{:S(2)}, u32[]{:S(2)}) %collective-permute-start.7) | collective-permute-done | bytes 262176 | tf_op jit(solution)/shard_map/ppermute | solution.py:257
  20.6 1.7 %collective-permute-start.8 = (bf16[4,128,512]{2,1,0:T(8,128)(2,1)S(1)}, bf16[4,128,512]{2,1,0:T(8,128)(2,1)S(1)}, u32[]{:S(2)}, u32[]{:S(2)}) collective-permute-start(bf16[4,128,512]{2,1,0:T(8,128)(2,1)S(1)} %pad_maximum_fusion.1), channel_id=1, source_target_pairs={{0,4},{1,3},{2,6},{3,1},{4,0},{5,7},{6,2},{7,5},{8,12},{9,11},{10,... | collective-permute-start | bytes 1572872 | tf_op jit(solution)/shard_map/ppermute | solution.py:257
  22.3 2.6 %collective-permute-done.3 = bf16[2,128,640]{2,1,0:T(8,128)(2,1)S(1)} collective-permute-done((bf16[2,128,640]{2,1,0:T(8,128)(2,1)S(1)}, bf16[2,128,640]{2,1,0:T(8,128)(2,1)S(1)}, u32[]{:S(2)}, u32[]{:S(2)}) %collective-permute-start.3) | collective-permute-done | bytes 327712 | tf_op jit(solution)/shard_map/ppermute | solution.py:254
  24.9 1.6 %collective-permute-start.4 = (bf16[2,128,512]{2,1,0:T(8,128)(2,1)S(1)}, bf16[2,128,512]{2,1,0:T(8,128)(2,1)S(1)}, u32[]{:S(2)}, u32[]{:S(2)}) collective-permute-start(bf16[2,128,512]{2,1,0:T(8,128)(2,1)S(1)} %slice.56.refs_2_), channel_id=1, source_target_pairs={{0,2},{1,5},{2,0},{3,7},{4,6},{5,1},{6,4},{7,3},{8,10},{9,13},{10,... | collective-permute-start | bytes 786440 | tf_op jit(solution)/shard_map/ppermute | solution.py:257
  26.5 0.5 collective-permute-start.10
  27.0 4.4 %collective-permute-done.4.refs_3_ = bf16[2,128,512]{2,1,0:T(8,128)(2,1)S(1)} collective-permute-done((bf16[2,128,512]{2,1,0:T(8,128)(2,1)S(1)}, bf16[2,128,512]{2,1,0:T(8,128)(2,1)S(1)}, u32[]{:S(2)}, u32[]{:S(2)}) %collective-permute-start.4) | collective-permute-done | bytes 262176 | tf_op jit(solution)/shard_map/ppermute | solution.py:257
  31.4 0.8 collective-permute-start.5
  32.2 0.5 collective-permute-done.8.refs_4_
  32.7 1.3 %collective-permute-start.11 = (bf16[4,128,512]{2,1,0:T(8,128)(2,1)S(1)}, bf16[4,128,512]{2,1,0:T(8,128)(2,1)S(1)}, u32[]{:S(2)}, u32[]{:S(2)}) collective-permute-start(bf16[4,128,512]{2,1,0:T(8,128)(2,1)S(1)} %collective-permute-done.8.refs_4_), channel_id=1, source_target_pairs={{0,1},{1,0},{2,3},{3,2},{4,5},{5,4},{6,7},{7,6},{8,9},{9,8},{10,11... | collective-permute-start | bytes 1572872 | tf_op jit(solution)/shard_map/ppermute | solution.py:254
  34.0 1.4 %collective-permute-start.14 = (bf16[1,128,128]{2,1,0:T(8,128)(2,1)S(1)}, bf16[1,128,128]{2,1,0:T(8,128)(2,1)S(1)}, u32[]{:S(2)}, u32[]{:S(2)}) collective-permute-start(bf16[1,128,128]{2,1,0:T(8,128)(2,1)S(1)} %slice.97), channel_id=1, source_target_pairs={{0,16},{1,17},{2,18},{3,19},{4,20},{5,21},{6,22},{7,23},{8,24},{9,... | collective-permute-start | bytes 98312 | tf_op jit(solution)/shard_map/ppermute | solution.py:254
  35.5 3.9 %collective-permute-done.14 = bf16[1,128,128]{2,1,0:T(8,128)(2,1)S(1)} collective-permute-done((bf16[1,128,128]{2,1,0:T(8,128)(2,1)S(1)}, bf16[1,128,128]{2,1,0:T(8,128)(2,1)S(1)}, u32[]{:S(2)}, u32[]{:S(2)}) %collective-permute-start.14) | collective-permute-done | bytes 32800 | tf_op jit(solution)/shard_map/ppermute | solution.py:254
  39.8 1.9 %shard_map.66 = (f32[128,512]{1,0:T(8,128)S(1)}, f32[128,128]{1,0:T(8,128)S(1)}) custom-call(s32[3]{0:T(128)S(1)} %pad_add_fusion.where.refs_0_, f32[1,16384]{1,0:T(1,128)S(1)} %get-tuple-element.43.refs_1_, bf16[2,128,512]{2,1,0:T(8,128)(2,1)S(1)} %pad_maximum_fusion.3.refs_2_, bf16[2,128,512]{2,1,0:T(8,128)(2,1)S(1)} %collective-permute-done.7.refs_3_, ...), custom_call_target="tpu_custom_call" | custom-call | flops 1073741824 | bytes 8388608 | tf_op jit(solution)/shard_map/pallas_call | solution.py:194
  41.7 1.2 %shard_map.67 = (f32[128,512]{1,0:T(8,128)S(1)}, f32[128,128]{1,0:T(8,128)S(1)}) custom-call(s32[3]{0:T(128)S(1)} %pad_add_fusion.where.refs_0_, f32[1,16384]{1,0:T(1,128)S(1)} %get-tuple-element.43.refs_1_, bf16[2,128,512]{2,1,0:T(8,128)(2,1)S(1)} %slice.56.refs_2_, bf16[2,128,512]{2,1,0:T(8,128)(2,1)S(1)} %collective-permute-done.4.refs_3_, ...), custom_call_target="tpu_custom_call" | custom-call | flops 402653184 | bytes 3145728 | tf_op jit(solution)/shard_map/pallas_call | solution.py:194
  42.9 0.4 collective-permute-start.12
  43.9 0.4 collective-permute-start.16
  44.3 1.0 %collective-permute-done.13.refs_2_ = bf16[2,128,512]{2,1,0:T(8,128)(2,1)S(1)} collective-permute-done((bf16[2,128,512]{2,1,0:T(8,128)(2,1)S(1)}, bf16[2,128,512]{2,1,0:T(8,128)(2,1)S(1)}, u32[]{:S(2)}, u32[]{:S(2)}) %collective-permute-start.13) | collective-permute-done | bytes 262176 | tf_op jit(solution)/shard_map/ppermute | solution.py:254
  45.3 1.2 %shard_map.68 = (f32[128,512]{1,0:T(8,128)S(1)}, f32[128,128]{1,0:T(8,128)S(1)}) custom-call(s32[3]{0:T(128)S(1)} %pad_add_fusion.where.refs_0_, f32[1,16384]{1,0:T(1,128)S(1)} %get-tuple-element.43.refs_1_, bf16[2,128,512]{2,1,0:T(8,128)(2,1)S(1)} %collective-permute-done.13.refs_2_, bf16[4,128,512]{2,1,0:T(8,128)(2,1)S(1)} %collective-permute-done.5.refs_3_, ...), custom_call_target="tpu_custom_call" | custom-call | flops 402653184 | bytes 3145728 | tf_op jit(solution)/shard_map/pallas_call | solution.py:194
  46.5 1.6 %shard_map.69.attended = bf16[128,512]{1,0:T(8,128)(2,1)S(1)} custom-call(s32[3]{0:T(128)S(1)} %pad_add_fusion.where.refs_0_, f32[1,16384]{1,0:T(1,128)S(1)} %get-tuple-element.43.refs_1_, bf16[4,128,512]{2,1,0:T(8,128)(2,1)S(1)} %collective-permute-done.12.refs_2_, bf16[16384,512]{1,0:T(8,128)(2,1)S(1)} %bitcast.31, ...), custom_call_target="tpu_custom_call" | custom-call | flops 268435456 | bytes 2097152 | tf_op jit(solution)/shard_map/pallas_call | solution.py:194
  48.7 0.8 shard_map.71
  49.5 0.4 collective-permute-done.17
  50.1 0.6 shard_map.72
  50.7 0.4 collective-permute-start.29
  51.1 1.7 %collective-permute-start.20 = (bf16[2,128,512]{2,1,0:T(8,128)(2,1)S(1)}, bf16[2,128,512]{2,1,0:T(8,128)(2,1)S(1)}, u32[]{:S(2)}, u32[]{:S(2)}) collective-permute-start(bf16[2,128,512]{2,1,0:T(8,128)(2,1)S(1)} %add_convert_fusion.5), channel_id=1, source_target_pairs={{0,2},{1,5},{2,0},{3,7},{4,6},{5,1},{6,4},{7,3},{8,10},{9,13},{10,... | collective-permute-start | bytes 786440 | tf_op jit(solution)/shard_map/ppermute | solution.py:257
  52.8 0.5 collective-permute-start.19
  53.3 4.1 %shard_map.73.weight = bf16[512,8192]{1,0:T(8,128)(2,1)S(1)} custom-call(s32[3]{0:T(128)S(1)} %pad_add_fusion.where.refs_0_, bf16[512,16384]{1,0:T(8,128)(2,1)} %source.3), custom_call_target="tpu_custom_call" | custom-call | bytes 16777216 | tf_op jit(solution)/shard_map/pallas_call | solution.py:62
  57.4 0.7 shard_map.74
  58.3 0.4 collective-permute-start.30
  58.8 1.8 %collective-permute-start.31 = (bf16[2,128,512]{2,1,0:T(8,128)(2,1)S(1)}, bf16[2,128,512]{2,1,0:T(8,128)(2,1)S(1)}, u32[]{:S(2)}, u32[]{:S(2)}) collective-permute-start(bf16[2,128,512]{2,1,0:T(8,128)(2,1)S(1)} %add_convert_fusion.4), channel_id=1, source_target_pairs={{0,4},{1,3},{2,6},{3,1},{4,0},{5,7},{6,2},{7,5},{8,12},{9,11},{10,... | collective-permute-start | bytes 786440 | tf_op jit(solution)/shard_map/ppermute | solution.py:257
  60.6 0.7 shard_map.75
  61.4 0.5 collective-permute-start.25
  62.1 5.2 %collective-permute-done.30 = bf16[2,128,512]{2,1,0:T(8,128)(2,1)S(1)} collective-permute-done((bf16[2,128,512]{2,1,0:T(8,128)(2,1)S(1)}, bf16[2,128,512]{2,1,0:T(8,128)(2,1)S(1)}, u32[]{:S(2)}, u32[]{:S(2)}) %collective-permute-start.30) | collective-permute-done | bytes 262176 | tf_op jit(solution)/shard_map/ppermute | solution.py:257
  67.5 2.2 %collective-permute-start.32 = (bf16[128,512]{1,0:T(8,128)(2,1)S(1)}, bf16[128,512]{1,0:T(8,128)(2,1)S(1)}, u32[]{:S(2)}, u32[]{:S(2)}) collective-permute-start(bf16[128,512]{1,0:T(8,128)(2,1)S(1)} %fusion.6), channel_id=1, source_target_pairs={{0,8},{1,9},{2,10},{3,11},{4,12},{5,13},{6,14},{7,15},{8,0},{9,1},... | collective-permute-start | bytes 393224 | tf_op jit(solution)/shard_map/ppermute | solution.py:254
  69.7 4.0 %collective-permute-done.22 = bf16[2,128,512]{2,1,0:T(8,128)(2,1)S(1)} collective-permute-done((bf16[2,128,512]{2,1,0:T(8,128)(2,1)S(1)}, bf16[2,128,512]{2,1,0:T(8,128)(2,1)S(1)}, u32[]{:S(2)}, u32[]{:S(2)}) %collective-permute-start.22) | collective-permute-done | bytes 262176 | tf_op jit(solution)/shard_map/ppermute | solution.py:257
  74.0 2.1 %collective-permute-start.26 = (bf16[2,128,512]{2,1,0:T(8,128)(2,1)S(1)}, bf16[2,128,512]{2,1,0:T(8,128)(2,1)S(1)}, u32[]{:S(2)}, u32[]{:S(2)}) collective-permute-start(bf16[2,128,512]{2,1,0:T(8,128)(2,1)S(1)} %add_convert_fusion.1), channel_id=1, source_target_pairs={{0,4},{1,3},{2,6},{3,1},{4,0},{5,7},{6,2},{7,5},{8,12},{9,11},{10,... | collective-permute-start | bytes 786440 | tf_op jit(solution)/shard_map/ppermute | solution.py:257
  76.1 1.3 %collective-permute-start.33 = (bf16[128,512]{1,0:T(8,128)(2,1)S(1)}, bf16[128,512]{1,0:T(8,128)(2,1)S(1)}, u32[]{:S(2)}, u32[]{:S(2)}) collective-permute-start(bf16[128,512]{1,0:T(8,128)(2,1)S(1)} %fusion.1), channel_id=1, source_target_pairs={{0,16},{1,17},{2,18},{3,19},{4,20},{5,21},{6,22},{7,23},{8,24},{9,... | collective-permute-start | bytes 393224 | tf_op jit(solution)/shard_map/ppermute | solution.py:254
  77.4 2.9 %collective-permute-done.24 = bf16[2,128,512]{2,1,0:T(8,128)(2,1)S(1)} collective-permute-done((bf16[2,128,512]{2,1,0:T(8,128)(2,1)S(1)}, bf16[2,128,512]{2,1,0:T(8,128)(2,1)S(1)}, u32[]{:S(2)}, u32[]{:S(2)}) %collective-permute-start.24) | collective-permute-done | bytes 262176 | tf_op jit(solution)/shard_map/ppermute | solution.py:257
  80.6 2.2 %collective-permute-start.27 = (bf16[128,512]{1,0:T(8,128)(2,1)S(1)}, bf16[128,512]{1,0:T(8,128)(2,1)S(1)}, u32[]{:S(2)}, u32[]{:S(2)}) collective-permute-start(bf16[128,512]{1,0:T(8,128)(2,1)S(1)} %fusion.5), channel_id=1, source_target_pairs={{0,8},{1,9},{2,10},{3,11},{4,12},{5,13},{6,14},{7,15},{8,0},{9,1},... | collective-permute-start | bytes 393224 | tf_op jit(solution)/shard_map/ppermute | solution.py:254
  82.7 0.8 collective-permute-done.33
  83.5 2.2 %collective-permute-done.27 = bf16[128,512]{1,0:T(8,128)(2,1)S(1)} collective-permute-done((bf16[128,512]{1,0:T(8,128)(2,1)S(1)}, bf16[128,512]{1,0:T(8,128)(2,1)S(1)}, u32[]{:S(2)}, u32[]{:S(2)}) %collective-permute-start.27) | collective-permute-done | bytes 131104 | tf_op jit(solution)/shard_map/ppermute | solution.py:254
  85.7 0.7 fusion.4
  (70 shorter events, 3.4 us)
Async XLA Ops:
  2.8 37.0 %slice-start = ((s8[16777216]{0:T(1024)(128)(4,1)}), s8[4194304]{0:T(1024)(128)(4,1)S(1)}, s32[]{:S(2)}) async-start(s8[16777216]{0:T(1024)(128)(4,1)} %bitcast.30), calls=%async_computation | async-start | bytes 8388608
  2.8 4.2 %collective-permute-start.1 = (f32[8,128,128]{2,1,0:T(8,128)S(1)}, f32[8,128,128]{2,1,0:T(8,128)S(1)}, u32[]{:S(2)}, u32[]{:S(2)}) collective-permute-start(f32[8,128,128]{2,1,0:T(8,128)S(1)} %get-tuple-element.46), channel_id=1, source_target_pairs={{0,1},{1,0},{2,3},{3,2},{4,5},{5,4},{6,7},{7,6},{8,9},{9,8},{10,11... | collective-permute-start | bytes 1572872 | tf_op jit(solution)/shard_map/ppermute | solution.py:254
  3.3 10.8 %collective-permute-start = (bf16[128,512]{1,0:T(8,128)(2,1)}, bf16[128,512]{1,0:T(8,128)(2,1)S(1)}, u32[]{:S(2)}, u32[]{:S(2)}) collective-permute-start(bf16[128,512]{1,0:T(8,128)(2,1)} %act.1), channel_id=1, source_target_pairs={{0,16},{1,17},{2,18},{3,19},{4,20},{5,21},{6,22},{7,23},{8,24},{9,... | collective-permute-start | bytes 393224 | tf_op jit(solution)/shard_map/ppermute | solution.py:254
  7.1 32.7 %slice-start.1 = ((s8[16777216]{0:T(1024)(128)(4,1)}), s8[4194304]{0:T(1024)(128)(4,1)S(1)}, s32[]{:S(2)}) async-start(s8[16777216]{0:T(1024)(128)(4,1)} %bitcast.30), calls=%async_computation.1 | async-start | bytes 8388608
  7.1 32.7 %slice-start.2 = ((s8[16777216]{0:T(1024)(128)(4,1)}), s8[4194304]{0:T(1024)(128)(4,1)S(1)}, s32[]{:S(2)}) async-start(s8[16777216]{0:T(1024)(128)(4,1)} %bitcast.30), calls=%async_computation.2 | async-start | bytes 8388608
  7.1 32.7 %slice-start.3 = ((s8[16777216]{0:T(1024)(128)(4,1)}), s8[4194304]{0:T(1024)(128)(4,1)S(1)}, s32[]{:S(2)}) async-start(s8[16777216]{0:T(1024)(128)(4,1)} %bitcast.30), calls=%async_computation.3 | async-start | bytes 8388608
  7.1 7.0 %collective-permute-start.2 = (bf16[4,128,128]{2,1,0:T(8,128)(2,1)S(1)}, bf16[4,128,128]{2,1,0:T(8,128)(2,1)S(1)}, u32[]{:S(2)}, u32[]{:S(2)}) collective-permute-start(bf16[4,128,128]{2,1,0:T(8,128)(2,1)S(1)} %slice.95), channel_id=1, source_target_pairs={{0,4},{1,5},{2,6},{3,7},{4,0},{5,1},{6,2},{7,3},{8,12},{9,13},{10,... | collective-permute-start | bytes 393224 | tf_op jit(solution)/shard_map/ppermute | solution.py:254
  14.2 6.4 %collective-permute-start.7 = (bf16[2,128,512]{2,1,0:T(8,128)(2,1)S(1)}, bf16[2,128,512]{2,1,0:T(8,128)(2,1)S(1)}, u32[]{:S(2)}, u32[]{:S(2)}) collective-permute-start(bf16[2,128,512]{2,1,0:T(8,128)(2,1)S(1)} %pad_maximum_fusion.3.refs_2_), channel_id=1, source_target_pairs={{0,2},{1,5},{2,0},{3,7},{4,6},{5,1},{6,4},{7,3},{8,10},{9,13},{10,... | collective-permute-start | bytes 786440 | tf_op jit(solution)/shard_map/ppermute | solution.py:257
  15.8 9.1 %collective-permute-start.3 = (bf16[2,128,640]{2,1,0:T(8,128)(2,1)S(1)}, bf16[2,128,640]{2,1,0:T(8,128)(2,1)S(1)}, u32[]{:S(2)}, u32[]{:S(2)}) collective-permute-start(bf16[2,128,640]{2,1,0:T(8,128)(2,1)S(1)} %pad_maximum_fusion.2), channel_id=1, source_target_pairs={{0,8},{1,9},{2,10},{3,11},{4,12},{5,13},{6,14},{7,15},{8,0},{9,1},... | collective-permute-start | bytes 983048 | tf_op jit(solution)/shard_map/ppermute | solution.py:254
  20.6 12.1 %collective-permute-start.8 = (bf16[4,128,512]{2,1,0:T(8,128)(2,1)S(1)}, bf16[4,128,512]{2,1,0:T(8,128)(2,1)S(1)}, u32[]{:S(2)}, u32[]{:S(2)}) collective-permute-start(bf16[4,128,512]{2,1,0:T(8,128)(2,1)S(1)} %pad_maximum_fusion.1), channel_id=1, source_target_pairs={{0,4},{1,3},{2,6},{3,1},{4,0},{5,7},{6,2},{7,5},{8,12},{9,11},{10,... | collective-permute-start | bytes 1572872 | tf_op jit(solution)/shard_map/ppermute | solution.py:257
  24.9 6.4 %collective-permute-start.4 = (bf16[2,128,512]{2,1,0:T(8,128)(2,1)S(1)}, bf16[2,128,512]{2,1,0:T(8,128)(2,1)S(1)}, u32[]{:S(2)}, u32[]{:S(2)}) collective-permute-start(bf16[2,128,512]{2,1,0:T(8,128)(2,1)S(1)} %slice.56.refs_2_), channel_id=1, source_target_pairs={{0,2},{1,5},{2,0},{3,7},{4,6},{5,1},{6,4},{7,3},{8,10},{9,13},{10,... | collective-permute-start | bytes 786440 | tf_op jit(solution)/shard_map/ppermute | solution.py:257
  26.5 12.9 %collective-permute-start.9 = (bf16[2,128,512]{2,1,0:T(8,128)(2,1)S(1)}, bf16[2,128,512]{2,1,0:T(8,128)(2,1)S(1)}, u32[]{:S(2)}, u32[]{:S(2)}) collective-permute-start(bf16[2,128,512]{2,1,0:T(8,128)(2,1)S(1)} %pad_maximum_fusion.3.refs_2_), channel_id=1, source_target_pairs={{0,1},{1,0},{2,3},{3,2},{4,5},{5,4},{6,7},{7,6},{8,9},{9,8},{10,11... | collective-permute-start | bytes 786440 | tf_op jit(solution)/shard_map/ppermute | solution.py:254
  26.5 13.2 %collective-permute-start.10 = (bf16[2,128,512]{2,1,0:T(8,128)(2,1)S(1)}, bf16[2,128,512]{2,1,0:T(8,128)(2,1)S(1)}, u32[]{:S(2)}, u32[]{:S(2)}) collective-permute-start(bf16[2,128,512]{2,1,0:T(8,128)(2,1)S(1)} %collective-permute-done.7.refs_3_), channel_id=1, source_target_pairs={{0,1},{1,0},{2,3},{3,2},{4,5},{5,4},{6,7},{7,6},{8,9},{9,8},{10,11... | collective-permute-start | bytes 786440 | tf_op jit(solution)/shard_map/ppermute | solution.py:254
  31.4 11.5 %collective-permute-start.5 = (bf16[4,128,512]{2,1,0:T(8,128)(2,1)S(1)}, bf16[4,128,512]{2,1,0:T(8,128)(2,1)S(1)}, u32[]{:S(2)}, u32[]{:S(2)}) collective-permute-start(bf16[4,128,512]{2,1,0:T(8,128)(2,1)S(1)} %pad_maximum_fusion), channel_id=1, source_target_pairs={{0,4},{1,3},{2,6},{3,1},{4,0},{5,7},{6,2},{7,5},{8,12},{9,11},{10,... | collective-permute-start | bytes 1572872 | tf_op jit(solution)/shard_map/ppermute | solution.py:257
  32.7 7.0 %collective-permute-start.11 = (bf16[4,128,512]{2,1,0:T(8,128)(2,1)S(1)}, bf16[4,128,512]{2,1,0:T(8,128)(2,1)S(1)}, u32[]{:S(2)}, u32[]{:S(2)}) collective-permute-start(bf16[4,128,512]{2,1,0:T(8,128)(2,1)S(1)} %collective-permute-done.8.refs_4_), channel_id=1, source_target_pairs={{0,1},{1,0},{2,3},{3,2},{4,5},{5,4},{6,7},{7,6},{8,9},{9,8},{10,11... | collective-permute-start | bytes 1572872 | tf_op jit(solution)/shard_map/ppermute | solution.py:254
  34.0 5.4 %collective-permute-start.14 = (bf16[1,128,128]{2,1,0:T(8,128)(2,1)S(1)}, bf16[1,128,128]{2,1,0:T(8,128)(2,1)S(1)}, u32[]{:S(2)}, u32[]{:S(2)}) collective-permute-start(bf16[1,128,128]{2,1,0:T(8,128)(2,1)S(1)} %slice.97), channel_id=1, source_target_pairs={{0,16},{1,17},{2,18},{3,19},{4,20},{5,21},{6,22},{7,23},{8,24},{9,... | collective-permute-start | bytes 98312 | tf_op jit(solution)/shard_map/ppermute | solution.py:254
  39.4 2.3 %collective-permute-start.6 = (bf16[2,128,512]{2,1,0:T(8,128)(2,1)S(1)}, bf16[2,128,512]{2,1,0:T(8,128)(2,1)S(1)}, u32[]{:S(2)}, u32[]{:S(2)}) collective-permute-start(bf16[2,128,512]{2,1,0:T(8,128)(2,1)S(1)} %slice.56.refs_2_), channel_id=1, source_target_pairs={{0,1},{1,0},{2,3},{3,2},{4,5},{5,4},{6,7},{7,6},{8,9},{9,8},{10,11... | collective-permute-start | bytes 786440 | tf_op jit(solution)/shard_map/ppermute | solution.py:254
  39.4 4.4 %collective-permute-start.15 = (bf16[128,128]{1,0:T(8,128)(2,1)S(1)}, bf16[128,128]{1,0:T(8,128)(2,1)S(1)}, u32[]{:S(2)}, u32[]{:S(2)}) collective-permute-start(bf16[128,128]{1,0:T(8,128)(2,1)S(1)} %fusion.10), channel_id=1, source_target_pairs={{0,2},{1,3},{2,0},{3,1},{4,6},{5,7},{6,4},{7,5},{8,10},{9,11},{10,... | collective-permute-start | bytes 98312 | tf_op jit(solution)/shard_map/ppermute | solution.py:254
  42.9 3.5 %collective-permute-start.12 = (bf16[4,128,512]{2,1,0:T(8,128)(2,1)S(1)}, bf16[4,128,512]{2,1,0:T(8,128)(2,1)S(1)}, u32[]{:S(2)}, u32[]{:S(2)}) collective-permute-start(bf16[4,128,512]{2,1,0:T(8,128)(2,1)S(1)} %collective-permute-done.5.refs_3_), channel_id=1, source_target_pairs={{0,1},{1,0},{2,3},{3,2},{4,5},{5,4},{6,7},{7,6},{8,9},{9,8},{10,11... | collective-permute-start | bytes 1572872 | tf_op jit(solution)/shard_map/ppermute | solution.py:254
  43.6 1.7 %collective-permute-start.13 = (bf16[2,128,512]{2,1,0:T(8,128)(2,1)S(1)}, bf16[2,128,512]{2,1,0:T(8,128)(2,1)S(1)}, u32[]{:S(2)}, u32[]{:S(2)}) collective-permute-start(bf16[2,128,512]{2,1,0:T(8,128)(2,1)S(1)} %collective-permute-done.4.refs_3_), channel_id=1, source_target_pairs={{0,1},{1,0},{2,3},{3,2},{4,5},{5,4},{6,7},{7,6},{8,9},{9,8},{10,11... | collective-permute-start | bytes 786440 | tf_op jit(solution)/shard_map/ppermute | solution.py:254
  43.9 2.6 %collective-permute-start.16 = (f32[128,128]{1,0:T(8,128)S(1)}, f32[128,128]{1,0:T(8,128)S(1)}, u32[]{:S(2)}, u32[]{:S(2)}) collective-permute-start(f32[128,128]{1,0:T(8,128)S(1)} %convert_add_fusion.3.refs_6_), channel_id=1, source_target_pairs={{0,1},{1,0},{2,3},{3,2},{4,5},{5,4},{6,7},{7,6},{8,9},{9,8},{10,11... | collective-permute-start | bytes 196616 | tf_op jit(solution)/shard_map/ppermute | solution.py:254
  48.4 1.6 %collective-permute-start.17 = (bf16[2,128,512]{2,1,0:T(8,128)(2,1)S(1)}, bf16[2,128,512]{2,1,0:T(8,128)(2,1)S(1)}, u32[]{:S(2)}, u32[]{:S(2)}) collective-permute-start(bf16[2,128,512]{2,1,0:T(8,128)(2,1)S(1)} %shard_map.70), channel_id=1, source_target_pairs={{0,1},{1,0},{2,3},{3,2},{4,5},{5,4},{6,7},{7,6},{8,9},{9,8},{10,11... | collective-permute-start | bytes 786440 | tf_op jit(solution)/shard_map/ppermute | solution.py:254
  50.7 7.5 %collective-permute-start.29 = (bf16[2,128,512]{2,1,0:T(8,128)(2,1)S(1)}, bf16[2,128,512]{2,1,0:T(8,128)(2,1)S(1)}, u32[]{:S(2)}, u32[]{:S(2)}) collective-permute-start(bf16[2,128,512]{2,1,0:T(8,128)(2,1)S(1)} %get-tuple-element.80), channel_id=1, source_target_pairs={{0,1},{1,0},{2,3},{3,2},{4,5},{5,4},{6,7},{7,6},{8,9},{9,8},{10,11... | collective-permute-start | bytes 786440 | tf_op jit(solution)/shard_map/ppermute | solution.py:254
  51.1 7.6 %collective-permute-start.20 = (bf16[2,128,512]{2,1,0:T(8,128)(2,1)S(1)}, bf16[2,128,512]{2,1,0:T(8,128)(2,1)S(1)}, u32[]{:S(2)}, u32[]{:S(2)}) collective-permute-start(bf16[2,128,512]{2,1,0:T(8,128)(2,1)S(1)} %add_convert_fusion.5), channel_id=1, source_target_pairs={{0,2},{1,5},{2,0},{3,7},{4,6},{5,1},{6,4},{7,3},{8,10},{9,13},{10,... | collective-permute-start | bytes 786440 | tf_op jit(solution)/shard_map/ppermute | solution.py:257
  52.8 9.2 %collective-permute-start.28 = (bf16[2,128,512]{2,1,0:T(8,128)(2,1)S(1)}, bf16[2,128,512]{2,1,0:T(8,128)(2,1)S(1)}, u32[]{:S(2)}, u32[]{:S(2)}) collective-permute-start(bf16[2,128,512]{2,1,0:T(8,128)(2,1)S(1)} %get-tuple-element.63), channel_id=1, source_target_pairs={{0,1},{1,0},{2,3},{3,2},{4,5},{5,4},{6,7},{7,6},{8,9},{9,8},{10,11... | collective-permute-start | bytes 786440 | tf_op jit(solution)/shard_map/ppermute | solution.py:254
  52.8 5.9 %collective-permute-start.19 = (bf16[2,128,512]{2,1,0:T(8,128)(2,1)S(1)}, bf16[2,128,512]{2,1,0:T(8,128)(2,1)S(1)}, u32[]{:S(2)}, u32[]{:S(2)}) collective-permute-start(bf16[2,128,512]{2,1,0:T(8,128)(2,1)S(1)} %get-tuple-element.72), channel_id=1, source_target_pairs={{0,1},{1,0},{2,3},{3,2},{4,5},{5,4},{6,7},{7,6},{8,9},{9,8},{10,11... | collective-permute-start | bytes 786440 | tf_op jit(solution)/shard_map/ppermute | solution.py:254
  58.2 3.2 %collective-permute-start.21 = (bf16[2,128,512]{2,1,0:T(8,128)(2,1)S(1)}, bf16[2,128,512]{2,1,0:T(8,128)(2,1)S(1)}, u32[]{:S(2)}, u32[]{:S(2)}) collective-permute-start(bf16[2,128,512]{2,1,0:T(8,128)(2,1)S(1)} %get-tuple-element.65), channel_id=1, source_target_pairs={{0,1},{1,0},{2,3},{3,2},{4,5},{5,4},{6,7},{7,6},{8,9},{9,8},{10,11... | collective-permute-start | bytes 786440 | tf_op jit(solution)/shard_map/ppermute | solution.py:254
  58.3 9.0 %collective-permute-start.30 = (bf16[2,128,512]{2,1,0:T(8,128)(2,1)S(1)}, bf16[2,128,512]{2,1,0:T(8,128)(2,1)S(1)}, u32[]{:S(2)}, u32[]{:S(2)}) collective-permute-start(bf16[2,128,512]{2,1,0:T(8,128)(2,1)S(1)} %add_convert_fusion), channel_id=1, source_target_pairs={{0,2},{1,5},{2,0},{3,7},{4,6},{5,1},{6,4},{7,3},{8,10},{9,13},{10,... | collective-permute-start | bytes 786440 | tf_op jit(solution)/shard_map/ppermute | solution.py:257
  58.8 8.5 %collective-permute-start.31 = (bf16[2,128,512]{2,1,0:T(8,128)(2,1)S(1)}, bf16[2,128,512]{2,1,0:T(8,128)(2,1)S(1)}, u32[]{:S(2)}, u32[]{:S(2)}) collective-permute-start(bf16[2,128,512]{2,1,0:T(8,128)(2,1)S(1)} %add_convert_fusion.4), channel_id=1, source_target_pairs={{0,4},{1,3},{2,6},{3,1},{4,0},{5,7},{6,2},{7,5},{8,12},{9,11},{10,... | collective-permute-start | bytes 786440 | tf_op jit(solution)/shard_map/ppermute | solution.py:257
  61.3 12.4 %collective-permute-start.23 = (bf16[2,128,512]{2,1,0:T(8,128)(2,1)S(1)}, bf16[2,128,512]{2,1,0:T(8,128)(2,1)S(1)}, u32[]{:S(2)}, u32[]{:S(2)}) collective-permute-start(bf16[2,128,512]{2,1,0:T(8,128)(2,1)S(1)} %get-tuple-element.75), channel_id=1, source_target_pairs={{0,1},{1,0},{2,3},{3,2},{4,5},{5,4},{6,7},{7,6},{8,9},{9,8},{10,11... | collective-permute-start | bytes 786440 | tf_op jit(solution)/shard_map/ppermute | solution.py:254
  61.4 12.5 %collective-permute-start.25 = (bf16[2,128,512]{2,1,0:T(8,128)(2,1)S(1)}, bf16[2,128,512]{2,1,0:T(8,128)(2,1)S(1)}, u32[]{:S(2)}, u32[]{:S(2)}) collective-permute-start(bf16[2,128,512]{2,1,0:T(8,128)(2,1)S(1)} %get-tuple-element.77), channel_id=1, source_target_pairs={{0,1},{1,0},{2,3},{3,2},{4,5},{5,4},{6,7},{7,6},{8,9},{9,8},{10,11... | collective-permute-start | bytes 786440 | tf_op jit(solution)/shard_map/ppermute | solution.py:254
  62.0 15.4 %collective-permute-start.18 = (bf16[2,128,512]{2,1,0:T(8,128)(2,1)S(1)}, bf16[2,128,512]{2,1,0:T(8,128)(2,1)S(1)}, u32[]{:S(2)}, u32[]{:S(2)}) collective-permute-start(bf16[2,128,512]{2,1,0:T(8,128)(2,1)S(1)} %get-tuple-element.68), channel_id=1, source_target_pairs={{0,1},{1,0},{2,3},{3,2},{4,5},{5,4},{6,7},{7,6},{8,9},{9,8},{10,11... | collective-permute-start | bytes 786440 | tf_op jit(solution)/shard_map/ppermute | solution.py:254
  67.3 6.4 %collective-permute-start.22 = (bf16[2,128,512]{2,1,0:T(8,128)(2,1)S(1)}, bf16[2,128,512]{2,1,0:T(8,128)(2,1)S(1)}, u32[]{:S(2)}, u32[]{:S(2)}) collective-permute-start(bf16[2,128,512]{2,1,0:T(8,128)(2,1)S(1)} %add_convert_fusion.3), channel_id=1, source_target_pairs={{0,2},{1,5},{2,0},{3,7},{4,6},{5,1},{6,4},{7,3},{8,10},{9,13},{10,... | collective-permute-start | bytes 786440 | tf_op jit(solution)/shard_map/ppermute | solution.py:257
  67.5 8.5 %collective-permute-start.32 = (bf16[128,512]{1,0:T(8,128)(2,1)S(1)}, bf16[128,512]{1,0:T(8,128)(2,1)S(1)}, u32[]{:S(2)}, u32[]{:S(2)}) collective-permute-start(bf16[128,512]{1,0:T(8,128)(2,1)S(1)} %fusion.6), channel_id=1, source_target_pairs={{0,8},{1,9},{2,10},{3,11},{4,12},{5,13},{6,14},{7,15},{8,0},{9,1},... | collective-permute-start | bytes 393224 | tf_op jit(solution)/shard_map/ppermute | solution.py:254
  73.8 6.6 %collective-permute-start.24 = (bf16[2,128,512]{2,1,0:T(8,128)(2,1)S(1)}, bf16[2,128,512]{2,1,0:T(8,128)(2,1)S(1)}, u32[]{:S(2)}, u32[]{:S(2)}) collective-permute-start(bf16[2,128,512]{2,1,0:T(8,128)(2,1)S(1)} %add_convert_fusion.2), channel_id=1, source_target_pairs={{0,2},{1,5},{2,0},{3,7},{4,6},{5,1},{6,4},{7,3},{8,10},{9,13},{10,... | collective-permute-start | bytes 786440 | tf_op jit(solution)/shard_map/ppermute | solution.py:257
  74.0 6.4 %collective-permute-start.26 = (bf16[2,128,512]{2,1,0:T(8,128)(2,1)S(1)}, bf16[2,128,512]{2,1,0:T(8,128)(2,1)S(1)}, u32[]{:S(2)}, u32[]{:S(2)}) collective-permute-start(bf16[2,128,512]{2,1,0:T(8,128)(2,1)S(1)} %add_convert_fusion.1), channel_id=1, source_target_pairs={{0,4},{1,3},{2,6},{3,1},{4,0},{5,7},{6,2},{7,5},{8,12},{9,11},{10,... | collective-permute-start | bytes 786440 | tf_op jit(solution)/shard_map/ppermute | solution.py:257
  76.1 7.4 %collective-permute-start.33 = (bf16[128,512]{1,0:T(8,128)(2,1)S(1)}, bf16[128,512]{1,0:T(8,128)(2,1)S(1)}, u32[]{:S(2)}, u32[]{:S(2)}) collective-permute-start(bf16[128,512]{1,0:T(8,128)(2,1)S(1)} %fusion.1), channel_id=1, source_target_pairs={{0,16},{1,17},{2,18},{3,19},{4,20},{5,21},{6,22},{7,23},{8,24},{9,... | collective-permute-start | bytes 393224 | tf_op jit(solution)/shard_map/ppermute | solution.py:254
  80.6 5.1 %collective-permute-start.27 = (bf16[128,512]{1,0:T(8,128)(2,1)S(1)}, bf16[128,512]{1,0:T(8,128)(2,1)S(1)}, u32[]{:S(2)}, u32[]{:S(2)}) collective-permute-start(bf16[128,512]{1,0:T(8,128)(2,1)S(1)} %fusion.5), channel_id=1, source_target_pairs={{0,8},{1,9},{2,10},{3,11},{4,12},{5,13},{6,14},{7,15},{8,0},{9,1},... | collective-permute-start | bytes 393224 | tf_op jit(solution)/shard_map/ppermute | solution.py:254

commit v8 on v7

--- a/solution.py
+++ b/solution.py
@@ -49,7 +49,7 @@
     for i, (const, pick) in enumerate(symbols):
         start = pl.multiple_of((where[pick] ^ const) * width, LANE)
         copy = pltpu.make_async_copy(
-            source.at[:, pl.ds(start, width)], target.at[:, pl.ds(i * width, width)], sems.at[i]
+            source.at[:, pl.ds(start, width)], target.at[i], sems.at[i]
         )
         copy.start()
         copies.append(copy)
@@ -58,8 +58,8 @@
 
 
 def fetched(where, weight, width, symbols):
-    shape = (weight.shape[0], len(symbols) * width)
-    columns = pl.pallas_call(
+    shape = (len(symbols), weight.shape[0], width)
+    blocks = pl.pallas_call(
         functools.partial(fetch_kernel, symbols, width),
         out_shape=jax.ShapeDtypeStruct(shape, weight.dtype),
         in_specs=[smem(), hbm()],
@@ -67,10 +67,10 @@
         scratch_shapes=[pltpu.SemaphoreType.DMA((len(symbols),))],
         compiler_params=pltpu.CompilerParams(vmem_limit_bytes=MIB),
         cost_estimate=pl.CostEstimate(
-            flops=0, bytes_accessed=4 * shape[0] * shape[1], transcendentals=0
+            flops=0, bytes_accessed=4 * shape[0] * shape[1] * shape[2], transcendentals=0
         ),
     )(where, in_hbm(weight))
-    return columns, symbols
+    return blocks, symbols
 
 
 def kv_kernel(shared, where, act, gain, wk, wv, send, keep, abuf, gbuf, kbuf, vbuf, sems):
@@ -205,12 +205,11 @@
     )(where, gain, *arrays, weight, *carry, *extra)
 
 
-def output_kernel(groups, width, attended, weight, *outs):
+def output_kernel(groups, attended, weight, *outs):
     left = attended[...]
     for spots, out in zip(groups, outs):
         for block, spot in enumerate(spots):
-            columns = weight[:, spot * width : (spot + 1) * width]
-            out[block] = dot(left, columns).astype(out.dtype)
+            out[block] = dot(left, weight[spot]).astype(out.dtype)
 
 
 def output_call(attended, held, width, groups):
@@ -219,7 +218,7 @@
     spots = [[order.index(s) for s in symbols] for symbols, _ in groups]
     columns = width * sum(len(s) for s in spots)
     return pl.pallas_call(
-        functools.partial(output_kernel, spots, width),
+        functools.partial(output_kernel, spots),
         out_shape=[jax.ShapeDtypeStruct((len(s), tokens, width), t) for s, t in groups],
         in_specs=[vmem(), vmem()],
         out_specs=[vmem()] * len(groups),
@@ -282,7 +281,7 @@
 
     def order(offsets):
         home, one, two, corner = symbols_of(offsets)
-        return [corner, two, one, home]
+        return [corner + one, two, home]
 
     def columns_of(offsets):
         own = sum(order(offsets), [])
@@ -296,9 +295,9 @@
 
     kv = halved(kv_keep + swap(kv_send, CORE), offset=bits[shared])
     row = jnp.stack([act, swap(raw, top)])
-    far_columns, far_symbols = fetched(where, wo, width, columns_of(far))
-    row, kv, far_columns = lax.optimization_barrier((row, kv, far_columns))
-    far_held = (far_columns, far_symbols)
+    far_blocks, far_symbols = fetched(where, wo, width, columns_of(far))
+    row, kv, far_blocks = lax.optimization_barrier((row, kv, far_blocks))
+    far_held = (far_blocks, far_symbols)
     ride = bits[shared + 1]
     side = turn(row, 0)
     rest = []
@@ -315,36 +314,38 @@
         ([0, top], row, side),
         ([o ^ t for o in near[1:] for t in (0, top)], jnp.concatenate(rest), None),
     ):
-        side = turn(row, 0) if side is None else side
+        if side is None:
+            side = turn(row, 0)
+            for b in bits[shared + 2 :]:
+                kv = halved(kv, offset=b)
+            near_blocks, near_symbols = fetched(after(where, row), wo, width, columns_of(near))
+            side, kv, near_blocks = lax.optimization_barrier((side, kv, near_blocks))
+            near_held = (near_blocks, near_symbols)
         both = turn(jnp.concatenate([row, side]), 1)
         at = symbols_of(offsets)
         groups.append([(row, at[0]), (side, at[1]), (both, at[2] + at[3])])
     early, last = groups
-    for b in bits[shared + 2 :]:
-        got = after(swap(kv[: kv.shape[0] // 2].astype(bf16), b), last[1][0])
-        kv = halved(kv, got)
-    total = kv[0]
-    for b in bits[1:shared]:
-        total = total + swap(total.astype(bf16), b).astype(f32)
-    kv_sums = (total, swap(total, CORE))
+    partners = [swap(kv[0].astype(bf16), o) for o in combos(bits[1:shared])[1:]]
 
     call = functools.partial(query_call, where, gain, weight=wq)
     carry = call(early + other(early))
-    carry = call(last[:2] + other(last[:1]), carry=carry)
+    carry = call(last[:2] + other(last[:2]), carry=carry)
     both, *carry = lax.optimization_barrier((last[2][0], *carry))
     both = [(both, last[2][1])]
+    total = kv[0]
+    for x in partners:
+        total = total + after(x, carry[0]).astype(f32)
     final = other(both)
-    carry = call(other(last[1:2]) + both, carry=carry)
-    (attended,) = call(final, carry=carry, extra=(*kv_sums, *rotary_tables(tokens)))
-
-    def round_square(corner, terms, wait=False):
-        (two, two_got), (one, one_got), (home, home_got) = terms
-        from_corner = turn(corner, 0)
-        if wait:
-            one = after(one, from_corner)
-        got_1 = turn(added_up(one, one_got).astype(bf16), 0)
-        two = added_up(two, two_got, from_corner).astype(bf16)
-        return [home, home_got, got_1, turn(two, 1)], two
+    carry = call(both, carry=carry)
+    (attended,) = call(
+        final, carry=carry, extra=(total, swap(total, CORE), *rotary_tables(tokens))
+    )
+
+    def round_square(first, two, home):
+        got = turn(first, 0)
+        k = got.shape[0] // 2
+        two = added_up(*two, got[:k]).astype(bf16)
+        return [*home, got[k:], turn(two, 1)], two
 
     def added_up(home, *arrived):
         for x in arrived:
@@ -362,19 +363,21 @@
     def ours(symbols):
         return [(s, f32) for s in symbols]
 
+    def paired(own, sent):
+        return [(x, swap(y, CORE)) for x, y in zip(own, sent)]
+
     project = functools.partial(output_call, held=far_held, width=width)
     sent = project(attended, groups=theirs(order(far)[:1]))
     own = project(after(attended, *sent), groups=ours(order(far)))
-    corner = added_up(own[0], swap(sent[0], CORE)).astype(bf16)
-    sent = project(after(attended, corner), groups=theirs(order(far)[1:]))
-    terms = [(x, swap(y, CORE)) for x, y in zip(own[1:], sent)]
-    far_sums, two = round_square(corner, terms)
-    near_held = fetched(after(where, sent[-1]), wo, width, columns_of(near))
-    sent = output_call(attended, near_held, width, theirs(order(near)))
-    own = output_call(after(attended, sent[0]), near_held, width, ours(order(near)))
-    terms = [(x, swap(y, CORE)) for x, y in zip(own, sent)]
-    corner = added_up(after(own[0], two), terms[0][1]).astype(bf16)
-    near_sums, _ = round_square(corner, terms[1:], wait=True)
+    first = added_up(own[0], swap(sent[0], CORE)).astype(bf16)
+    sent = project(after(attended, first), groups=theirs(order(far)[1:]))
+    far_sums, two = round_square(first, *paired(own[1:], sent))
+    project = functools.partial(output_call, held=near_held, width=width)
+    sent = project(after(attended, sent[-1]), groups=theirs(order(near)))
+    own = project(after(attended, sent[0]), groups=ours(order(near)))
+    pairs = paired(own, sent)
+    first = added_up(after(pairs[0][0], two), pairs[0][1]).astype(bf16)
+    near_sums, _ = round_square(first, *pairs[1:])
     got = swap(along_z(added_up(*far_sums)).astype(bf16), top)
     out = added_up(along_z(added_up(*near_sums)), got)
     return out.astype(bf16)

time: 86.5 us -> 83.2 us (0.962)
  starting transfers between devices: 30.7 us -> 25.2 us
  waiting for transfers between devices: 32.2 us -> 34.8 us
    ppermute x24 -> x22, waiting for transfers between devices: 11.4 us -> 14.4 us  [swap(): return lax.ppermute(x, 'wide', [(i, i ^ offset) for i in range(n)])]
    ppermute x24 -> x22, starting transfers between devices: 19.1 us -> 16.3 us  [swap(): return lax.ppermute(x, 'wide', [(i, i ^ offset) for i in range(n)])]
    ppermute x10 -> x8, starting transfers between devices: 11.6 us -> 8.94 us  [turn(): lax.ppermute(x, 'wide', [(i, i ^ ways[(step + (i & CORE)) % 2]) for i in...]
    ppermute x10 -> x8, waiting for transfers between devices: 20.7 us -> 20.4 us  [turn(): lax.ppermute(x, 'wide', [(i, i ^ ways[(step + (i & CORE)) % 2]) for i in...]
  transfers between devices with their start and end apart: 34 -> 30, of which waited for: 14 -> 13; matrix products, arithmetic and copies ran while one was open for 2% -> 2% of each run, Pallas kernels for 18% -> 19%
where the time goes in v8:
time: 83.2 us; the launch traced here: 83 us
  waiting for transfers between devices  34.8 us (42%)
  starting transfers between devices  25.2 us (30%)
  Pallas kernels  20.3 us (24%)
  other arithmetic  2.26 us (3%)
    ppermute x8, waiting for transfers between devices, turn(): lax.ppermute(x, 'wide', [(i, i ^ ways[(step + (i & CORE)) % 2]) for i in...  20.4 us
    ppermute x22, starting transfers between devices, swap(): return lax.ppermute(x, 'wide', [(i, i ^ offset) for i in range(n)])  16.3 us
    ppermute x22, waiting for transfers between devices, swap(): return lax.ppermute(x, 'wide', [(i, i ^ offset) for i in range(n)])  14.4 us
    ppermute x8, starting transfers between devices, turn(): lax.ppermute(x, 'wide', [(i, i ^ ways[(step + (i & CORE)) % 2]) for i in...  8.94 us
    pallas_call x2, Pallas kernels, fetched(): pl.pallas_call(functools.partial(fetch_kernel, symbols, width), out_shape...  8.7 us
    pallas_call x4, Pallas kernels, query_call(): pl.pallas_call(functools.partial(query_kernel, places, bool(carry), bool(...  5.86 us
    pallas_call x5, Pallas kernels, output_call(): pl.pallas_call(functools.partial(output_kernel, spots), out_shape=[jax.Sh...  3.03 us
    pallas_call x1, Pallas kernels, kv_terms(): pl.pallas_call(functools.partial(kv_kernel, shared), out_shape=[jax.Shape...  2.69 us
  transfers between devices with their start and end apart: 30, of which 13 were waited for; matrix products, arithmetic and copies ran while one was open for 2% of the time, Pallas kernels for 19%

profile of v8, /device:TPU:0, one launch (start us, length us, event | category | flops | bytes accessed | tf_op | source)
XLA Modules:
  0.0 83.0 jit_solution(2680309631642232850)
XLA Ops:
  0.1 2.7 %shard_map.64 = (f32[8,128,128]{2,1,0:T(8,128)S(1)}, f32[8,128,128]{2,1,0:T(8,128)S(1)}, bf16[128,512]{1,0:T(8,128)(2,1)S(1)}, f32[1,16384]{1,0:T(1,128)S(1)}) custom-call(s32[3]{0:T(128)S(1)} %pad_add_fusion.where.refs_0_, bf16[128,512]{1,0:T(8,128)(2,1)} %act.1, f32[1,16384]{1,0:T(1,128)} %bitcast.31, bf16[512,1024]{1,0:T(8,128)(2,1)} %wk.1, ...), custom_call_target="tpu_custom_call" | custom-call | flops 4294967296 | bytes 33554432 | tf_op jit(solution)/shard_map/pallas_call | solution.py:101
  2.8 0.5 collective-permute-start.1
  3.3 3.7 %collective-permute-start = (bf16[128,512]{1,0:T(8,128)(2,1)}, bf16[128,512]{1,0:T(8,128)(2,1)S(1)}, u32[]{:S(2)}, u32[]{:S(2)}) collective-permute-start(bf16[128,512]{1,0:T(8,128)(2,1)} %act.1), channel_id=1, source_target_pairs={{0,16},{1,17},{2,18},{3,19},{4,20},{5,21},{6,22},{7,23},{8,24},{9,... | collective-permute-start | bytes 393224 | tf_op jit(solution)/shard_map/ppermute | solution.py:253
  7.0 1.6 %collective-permute-start.2 = (bf16[4,128,128]{2,1,0:T(8,128)(2,1)S(1)}, bf16[4,128,128]{2,1,0:T(8,128)(2,1)S(1)}, u32[]{:S(2)}, u32[]{:S(2)}) collective-permute-start(bf16[4,128,128]{2,1,0:T(8,128)(2,1)S(1)} %slice.113), channel_id=1, source_target_pairs={{0,4},{1,5},{2,6},{3,7},{4,0},{5,1},{6,2},{7,3},{8,12},{9,13},{10,... | collective-permute-start | bytes 393224 | tf_op jit(solution)/shard_map/ppermute | solution.py:253
  8.6 4.1 %shard_map.65.weight = bf16[16,512,512]{2,1,0:T(8,128)(2,1)S(1)} custom-call(s32[3]{0:T(128)S(1)} %pad_add_fusion.where.refs_0_, bf16[512,16384]{1,0:T(8,128)(2,1)} %source.3), custom_call_target="tpu_custom_call" | custom-call | bytes 16777216 | tf_op jit(solution)/shard_map/pallas_call | solution.py:62
  12.8 1.3 %collective-permute-done = bf16[128,512]{1,0:T(8,128)(2,1)S(1)} collective-permute-done((bf16[128,512]{1,0:T(8,128)(2,1)}, bf16[128,512]{1,0:T(8,128)(2,1)S(1)}, u32[]{:S(2)}, u32[]{:S(2)}) %collective-permute-start) | collective-permute-done | bytes 131104 | tf_op jit(solution)/shard_map/ppermute | solution.py:253
  14.1 1.6 %collective-permute-start.9 = (bf16[2,128,512]{2,1,0:T(8,128)(2,1)S(1)}, bf16[2,128,512]{2,1,0:T(8,128)(2,1)S(1)}, u32[]{:S(2)}, u32[]{:S(2)}) collective-permute-start(bf16[2,128,512]{2,1,0:T(8,128)(2,1)S(1)} %pad_maximum_fusion.3.refs_2_), channel_id=1, source_target_pairs={{0,2},{1,5},{2,0},{3,7},{4,6},{5,1},{6,4},{7,3},{8,10},{9,13},{10,... | collective-permute-start | bytes 786440 | tf_op jit(solution)/shard_map/ppermute | solution.py:256
  15.8 0.8 %collective-permute-start.3 = (bf16[2,128,640]{2,1,0:T(8,128)(2,1)S(1)}, bf16[2,128,640]{2,1,0:T(8,128)(2,1)S(1)}, u32[]{:S(2)}, u32[]{:S(2)}) collective-permute-start(bf16[2,128,640]{2,1,0:T(8,128)(2,1)S(1)} %pad_maximum_fusion.2), channel_id=1, source_target_pairs={{0,8},{1,9},{2,10},{3,11},{4,12},{5,13},{6,14},{7,15},{8,0},{9,1},... | collective-permute-start | bytes 983048 | tf_op jit(solution)/shard_map/ppermute | solution.py:253
  16.7 3.9 %collective-permute-done.9.refs_3_ = bf16[2,128,512]{2,1,0:T(8,128)(2,1)S(1)} collective-permute-done((bf16[2,128,512]{2,1,0:T(8,128)(2,1)S(1)}, bf16[2,128,512]{2,1,0:T(8,128)(2,1)S(1)}, u32[]{:S(2)}, u32[]{:S(2)}) %collective-permute-start.9) | collective-permute-done | bytes 262176 | tf_op jit(solution)/shard_map/ppermute | solution.py:256
  20.6 1.7 %collective-permute-start.10 = (bf16[4,128,512]{2,1,0:T(8,128)(2,1)S(1)}, bf16[4,128,512]{2,1,0:T(8,128)(2,1)S(1)}, u32[]{:S(2)}, u32[]{:S(2)}) collective-permute-start(bf16[4,128,512]{2,1,0:T(8,128)(2,1)S(1)} %pad_maximum_fusion.1), channel_id=1, source_target_pairs={{0,4},{1,3},{2,6},{3,1},{4,0},{5,7},{6,2},{7,5},{8,12},{9,11},{10,... | collective-permute-start | bytes 1572872 | tf_op jit(solution)/shard_map/ppermute | solution.py:256
  22.3 2.6 %collective-permute-done.3 = bf16[2,128,640]{2,1,0:T(8,128)(2,1)S(1)} collective-permute-done((bf16[2,128,640]{2,1,0:T(8,128)(2,1)S(1)}, bf16[2,128,640]{2,1,0:T(8,128)(2,1)S(1)}, u32[]{:S(2)}, u32[]{:S(2)}) %collective-permute-start.3) | collective-permute-done | bytes 327712 | tf_op jit(solution)/shard_map/ppermute | solution.py:253
  24.9 1.6 %collective-permute-start.4 = (bf16[2,128,512]{2,1,0:T(8,128)(2,1)S(1)}, bf16[2,128,512]{2,1,0:T(8,128)(2,1)S(1)}, u32[]{:S(2)}, u32[]{:S(2)}) collective-permute-start(bf16[2,128,512]{2,1,0:T(8,128)(2,1)S(1)} %slice.72.refs_2_), channel_id=1, source_target_pairs={{0,2},{1,5},{2,0},{3,7},{4,6},{5,1},{6,4},{7,3},{8,10},{9,13},{10,... | collective-permute-start | bytes 786440 | tf_op jit(solution)/shard_map/ppermute | solution.py:256
  26.6 2.6 %collective-permute-start.5 = (bf16[1,128,128]{2,1,0:T(8,128)(2,1)S(1)}, bf16[1,128,128]{2,1,0:T(8,128)(2,1)S(1)}, u32[]{:S(2)}, u32[]{:S(2)}) collective-permute-start(bf16[1,128,128]{2,1,0:T(8,128)(2,1)S(1)} %slice.115), channel_id=1, source_target_pairs={{0,16},{1,17},{2,18},{3,19},{4,20},{5,21},{6,22},{7,23},{8,24},{9,... | collective-permute-start | bytes 98312 | tf_op jit(solution)/shard_map/ppermute | solution.py:253
  29.2 4.6 %shard_map.66.weight = bf16[16,512,512]{2,1,0:T(8,128)(2,1)S(1)} custom-call(s32[3]{0:T(128)S(1)} %pad_add_fusion.where.refs_0_, bf16[512,16384]{1,0:T(8,128)(2,1)} %source.3), custom_call_target="tpu_custom_call" | custom-call | bytes 16777216 | tf_op jit(solution)/shard_map/pallas_call | solution.py:62
  34.0 0.7 collective-permute-start.6
  34.7 0.5 collective-permute-start.7
  35.3 0.9 %collective-permute-done.12.refs_6_ = bf16[2,128,512]{2,1,0:T(8,128)(2,1)S(1)} collective-permute-done((bf16[2,128,512]{2,1,0:T(8,128)(2,1)S(1)}, bf16[2,128,512]{2,1,0:T(8,128)(2,1)S(1)}, u32[]{:S(2)}, u32[]{:S(2)}) %collective-permute-start.12) | collective-permute-done | bytes 262176 | tf_op jit(solution)/shard_map/ppermute | solution.py:253
  36.2 1.2 %collective-permute-start.15 = (bf16[128,128]{1,0:T(8,128)(2,1)S(1)}, bf16[128,128]{1,0:T(8,128)(2,1)S(1)}, u32[]{:S(2)}, u32[]{:S(2)}) collective-permute-start(bf16[128,128]{1,0:T(8,128)(2,1)S(1)} %bitcast_convert_fusion), channel_id=1, source_target_pairs={{0,2},{1,3},{2,0},{3,1},{4,6},{5,7},{6,4},{7,5},{8,10},{9,11},{10,... | collective-permute-start | bytes 98312 | tf_op jit(solution)/shard_map/ppermute | solution.py:253
  37.5 2.0 %shard_map.67 = (f32[128,512]{1,0:T(8,128)S(1)}, f32[128,128]{1,0:T(8,128)S(1)}) custom-call(s32[3]{0:T(128)S(1)} %pad_add_fusion.where.refs_0_, f32[1,16384]{1,0:T(1,128)S(1)} %get-tuple-element.42.refs_1_, bf16[2,128,512]{2,1,0:T(8,128)(2,1)S(1)} %pad_maximum_fusion.3.refs_2_, bf16[2,128,512]{2,1,0:T(8,128)(2,1)S(1)} %collective-permute-done.9.refs_3_, ...), custom_call_target="tpu_custom_call" | custom-call | flops 1073741824 | bytes 8388608 | tf_op jit(solution)/shard_map/pallas_call | solution.py:194
  39.5 1.3 %shard_map.68 = (f32[128,512]{1,0:T(8,128)S(1)}, f32[128,128]{1,0:T(8,128)S(1)}) custom-call(s32[3]{0:T(128)S(1)} %pad_add_fusion.where.refs_0_, f32[1,16384]{1,0:T(1,128)S(1)} %get-tuple-element.42.refs_1_, bf16[2,128,512]{2,1,0:T(8,128)(2,1)S(1)} %slice.72.refs_2_, bf16[2,128,512]{2,1,0:T(8,128)(2,1)S(1)} %collective-permute-done.4.refs_3_, ...), custom_call_target="tpu_custom_call" | custom-call | flops 536870912 | bytes 4194304 | tf_op jit(solution)/shard_map/pallas_call | solution.py:194
  40.8 2.4 %collective-permute-done.6.refs_2_ = bf16[4,128,512]{2,1,0:T(8,128)(2,1)S(1)} collective-permute-done((bf16[4,128,512]{2,1,0:T(8,128)(2,1)S(1)}, bf16[4,128,512]{2,1,0:T(8,128)(2,1)S(1)}, u32[]{:S(2)}, u32[]{:S(2)}) %collective-permute-start.6) | collective-permute-done | bytes 524320 | tf_op jit(solution)/shard_map/ppermute | solution.py:256
  43.2 0.3 fusion.9
  43.5 0.6 collective-permute-start.16
  44.2 1.0 %shard_map.69 = (f32[128,512]{1,0:T(8,128)S(1)}, f32[128,128]{1,0:T(8,128)S(1)}) custom-call(s32[3]{0:T(128)S(1)} %pad_add_fusion.where.refs_0_, f32[1,16384]{1,0:T(1,128)S(1)} %get-tuple-element.42.refs_1_, bf16[4,128,512]{2,1,0:T(8,128)(2,1)S(1)} %collective-permute-done.6.refs_2_, bf16[16384,512]{1,0:T(8,128)(2,1)S(1)} %bitcast.28, ...), custom_call_target="tpu_custom_call" | custom-call | flops 268435456 | bytes 2097152 | tf_op jit(solution)/shard_map/pallas_call | solution.py:194
  45.2 1.6 %shard_map.70.attended = bf16[128,512]{1,0:T(8,128)(2,1)S(1)} custom-call(s32[3]{0:T(128)S(1)} %pad_add_fusion.where.refs_0_, f32[1,16384]{1,0:T(1,128)S(1)} %get-tuple-element.42.refs_1_, bf16[4,128,512]{2,1,0:T(8,128)(2,1)S(1)} %collective-permute-done.14.refs_2_, bf16[16384,512]{1,0:T(8,128)(2,1)S(1)} %bitcast.28, ...), custom_call_target="tpu_custom_call" | custom-call | flops 268435456 | bytes 2097152 | tf_op jit(solution)/shard_map/pallas_call | solution.py:194
  46.8 0.4 shard_map.71
  47.5 0.7 shard_map.72
  48.2 1.1 %collective-permute-done.17 = bf16[4,128,512]{2,1,0:T(8,128)(2,1)S(1)} collective-permute-done((bf16[4,128,512]{2,1,0:T(8,128)(2,1)S(1)}, bf16[4,128,512]{2,1,0:T(8,128)(2,1)S(1)}, u32[]{:S(2)}, u32[]{:S(2)}) %collective-permute-start.17) | collective-permute-done | bytes 524320 | tf_op jit(solution)/shard_map/ppermute | solution.py:253
  49.4 0.8 collective-permute-start.20
  50.2 0.4 shard_map.73
  50.6 0.7 shard_map.74
  51.4 0.5 collective-permute-start.19
  52.0 0.7 shard_map.75
  52.7 1.0 %collective-permute-done.19 = bf16[2,128,512]{2,1,0:T(8,128)(2,1)S(1)} collective-permute-done((bf16[2,128,512]{2,1,0:T(8,128)(2,1)S(1)}, bf16[2,128,512]{2,1,0:T(8,128)(2,1)S(1)}, u32[]{:S(2)}, u32[]{:S(2)}) %collective-permute-start.19) | collective-permute-done | bytes 262176 | tf_op jit(solution)/shard_map/ppermute | solution.py:253
  53.7 4.9 %collective-permute-done.20 = bf16[4,128,512]{2,1,0:T(8,128)(2,1)S(1)} collective-permute-done((bf16[4,128,512]{2,1,0:T(8,128)(2,1)S(1)}, bf16[4,128,512]{2,1,0:T(8,128)(2,1)S(1)}, u32[]{:S(2)}, u32[]{:S(2)}) %collective-permute-start.20) | collective-permute-done | bytes 524320 | tf_op jit(solution)/shard_map/ppermute | solution.py:256
  58.8 0.7 collective-permute-start.27
  59.7 1.3 %collective-permute-start.22 = (bf16[4,128,512]{2,1,0:T(8,128)(2,1)S(1)}, bf16[4,128,512]{2,1,0:T(8,128)(2,1)S(1)}, u32[]{:S(2)}, u32[]{:S(2)}) collective-permute-start(bf16[4,128,512]{2,1,0:T(8,128)(2,1)S(1)} %add_convert_fusion), channel_id=1, source_target_pairs={{0,2},{1,5},{2,0},{3,7},{4,6},{5,1},{6,4},{7,3},{8,10},{9,13},{10,... | collective-permute-start | bytes 1572872 | tf_op jit(solution)/shard_map/ppermute | solution.py:256
  61.0 0.5 collective-permute-start.23
  61.5 6.5 %collective-permute-done.27 = bf16[2,128,512]{2,1,0:T(8,128)(2,1)S(1)} collective-permute-done((bf16[2,128,512]{2,1,0:T(8,128)(2,1)S(1)}, bf16[2,128,512]{2,1,0:T(8,128)(2,1)S(1)}, u32[]{:S(2)}, u32[]{:S(2)}) %collective-permute-start.27) | collective-permute-done | bytes 262176 | tf_op jit(solution)/shard_map/ppermute | solution.py:256
  68.2 2.0 %collective-permute-start.28 = (bf16[128,512]{1,0:T(8,128)(2,1)S(1)}, bf16[128,512]{1,0:T(8,128)(2,1)S(1)}, u32[]{:S(2)}, u32[]{:S(2)}) collective-permute-start(bf16[128,512]{1,0:T(8,128)(2,1)S(1)} %fusion.6), channel_id=1, source_target_pairs={{0,8},{1,9},{2,10},{3,11},{4,12},{5,13},{6,14},{7,15},{8,0},{9,1},... | collective-permute-start | bytes 393224 | tf_op jit(solution)/shard_map/ppermute | solution.py:253
  70.3 0.6 collective-permute-start.24
  70.8 3.0 %collective-permute-done.28 = bf16[128,512]{1,0:T(8,128)(2,1)S(1)} collective-permute-done((bf16[128,512]{1,0:T(8,128)(2,1)S(1)}, bf16[128,512]{1,0:T(8,128)(2,1)S(1)}, u32[]{:S(2)}, u32[]{:S(2)}) %collective-permute-start.28) | collective-permute-done | bytes 131104 | tf_op jit(solution)/shard_map/ppermute | solution.py:253
  73.8 0.3 collective-permute-start.29
  74.1 2.6 %collective-permute-done.24 = bf16[2,128,512]{2,1,0:T(8,128)(2,1)S(1)} collective-permute-done((bf16[2,128,512]{2,1,0:T(8,128)(2,1)S(1)}, bf16[2,128,512]{2,1,0:T(8,128)(2,1)S(1)}, u32[]{:S(2)}, u32[]{:S(2)}) %collective-permute-start.24) | collective-permute-done | bytes 262176 | tf_op jit(solution)/shard_map/ppermute | solution.py:256
  76.9 0.9 %collective-permute-start.25 = (bf16[128,512]{1,0:T(8,128)(2,1)S(1)}, bf16[128,512]{1,0:T(8,128)(2,1)S(1)}, u32[]{:S(2)}, u32[]{:S(2)}) collective-permute-start(bf16[128,512]{1,0:T(8,128)(2,1)S(1)} %fusion.5), channel_id=1, source_target_pairs={{0,8},{1,9},{2,10},{3,11},{4,12},{5,13},{6,14},{7,15},{8,0},{9,1},... | collective-permute-start | bytes 393224 | tf_op jit(solution)/shard_map/ppermute | solution.py:253
  77.8 2.1 %collective-permute-done.29 = bf16[128,512]{1,0:T(8,128)(2,1)S(1)} collective-permute-done((bf16[128,512]{1,0:T(8,128)(2,1)S(1)}, bf16[128,512]{1,0:T(8,128)(2,1)S(1)}, u32[]{:S(2)}, u32[]{:S(2)}) %collective-permute-start.29) | collective-permute-done | bytes 131104 | tf_op jit(solution)/shard_map/ppermute | solution.py:253
  79.9 2.5 %collective-permute-done.25 = bf16[128,512]{1,0:T(8,128)(2,1)S(1)} collective-permute-done((bf16[128,512]{1,0:T(8,128)(2,1)S(1)}, bf16[128,512]{1,0:T(8,128)(2,1)S(1)}, u32[]{:S(2)}, u32[]{:S(2)}) %collective-permute-start.25) | collective-permute-done | bytes 131104 | tf_op jit(solution)/shard_map/ppermute | solution.py:253
  82.3 0.7 fusion.4
  (61 shorter events, 2.0 us)
Async XLA Ops:
  2.8 4.2 %collective-permute-start.1 = (f32[8,128,128]{2,1,0:T(8,128)S(1)}, f32[8,128,128]{2,1,0:T(8,128)S(1)}, u32[]{:S(2)}, u32[]{:S(2)}) collective-permute-start(f32[8,128,128]{2,1,0:T(8,128)S(1)} %get-tuple-element.45), channel_id=1, source_target_pairs={{0,1},{1,0},{2,3},{3,2},{4,5},{5,4},{6,7},{7,6},{8,9},{9,8},{10,11... | collective-permute-start | bytes 1572872 | tf_op jit(solution)/shard_map/ppermute | solution.py:253
  3.3 10.8 %collective-permute-start = (bf16[128,512]{1,0:T(8,128)(2,1)}, bf16[128,512]{1,0:T(8,128)(2,1)S(1)}, u32[]{:S(2)}, u32[]{:S(2)}) collective-permute-start(bf16[128,512]{1,0:T(8,128)(2,1)} %act.1), channel_id=1, source_target_pairs={{0,16},{1,17},{2,18},{3,19},{4,20},{5,21},{6,22},{7,23},{8,24},{9,... | collective-permute-start | bytes 393224 | tf_op jit(solution)/shard_map/ppermute | solution.py:253
  7.0 7.0 %collective-permute-start.2 = (bf16[4,128,128]{2,1,0:T(8,128)(2,1)S(1)}, bf16[4,128,128]{2,1,0:T(8,128)(2,1)S(1)}, u32[]{:S(2)}, u32[]{:S(2)}) collective-permute-start(bf16[4,128,128]{2,1,0:T(8,128)(2,1)S(1)} %slice.113), channel_id=1, source_target_pairs={{0,4},{1,5},{2,6},{3,7},{4,0},{5,1},{6,2},{7,3},{8,12},{9,13},{10,... | collective-permute-start | bytes 393224 | tf_op jit(solution)/shard_map/ppermute | solution.py:253
  12.8 24.7 %slice-start = ((s8[16777216]{0:T(1024)(128)(4,1)}), s8[4194304]{0:T(1024)(128)(4,1)S(1)}, s32[]{:S(2)}) async-start(s8[16777216]{0:T(1024)(128)(4,1)} %bitcast.27), calls=%async_computation | async-start | bytes 8388608
  14.1 6.4 %collective-permute-start.9 = (bf16[2,128,512]{2,1,0:T(8,128)(2,1)S(1)}, bf16[2,128,512]{2,1,0:T(8,128)(2,1)S(1)}, u32[]{:S(2)}, u32[]{:S(2)}) collective-permute-start(bf16[2,128,512]{2,1,0:T(8,128)(2,1)S(1)} %pad_maximum_fusion.3.refs_2_), channel_id=1, source_target_pairs={{0,2},{1,5},{2,0},{3,7},{4,6},{5,1},{6,4},{7,3},{8,10},{9,13},{10,... | collective-permute-start | bytes 786440 | tf_op jit(solution)/shard_map/ppermute | solution.py:256
  15.8 9.1 %collective-permute-start.3 = (bf16[2,128,640]{2,1,0:T(8,128)(2,1)S(1)}, bf16[2,128,640]{2,1,0:T(8,128)(2,1)S(1)}, u32[]{:S(2)}, u32[]{:S(2)}) collective-permute-start(bf16[2,128,640]{2,1,0:T(8,128)(2,1)S(1)} %pad_maximum_fusion.2), channel_id=1, source_target_pairs={{0,8},{1,9},{2,10},{3,11},{4,12},{5,13},{6,14},{7,15},{8,0},{9,1},... | collective-permute-start | bytes 983048 | tf_op jit(solution)/shard_map/ppermute | solution.py:253
  20.6 13.1 %collective-permute-start.10 = (bf16[4,128,512]{2,1,0:T(8,128)(2,1)S(1)}, bf16[4,128,512]{2,1,0:T(8,128)(2,1)S(1)}, u32[]{:S(2)}, u32[]{:S(2)}) collective-permute-start(bf16[4,128,512]{2,1,0:T(8,128)(2,1)S(1)} %pad_maximum_fusion.1), channel_id=1, source_target_pairs={{0,4},{1,3},{2,6},{3,1},{4,0},{5,7},{6,2},{7,5},{8,12},{9,11},{10,... | collective-permute-start | bytes 1572872 | tf_op jit(solution)/shard_map/ppermute | solution.py:256
  24.9 9.0 %collective-permute-start.4 = (bf16[2,128,512]{2,1,0:T(8,128)(2,1)S(1)}, bf16[2,128,512]{2,1,0:T(8,128)(2,1)S(1)}, u32[]{:S(2)}, u32[]{:S(2)}) collective-permute-start(bf16[2,128,512]{2,1,0:T(8,128)(2,1)S(1)} %slice.72.refs_2_), channel_id=1, source_target_pairs={{0,2},{1,5},{2,0},{3,7},{4,6},{5,1},{6,4},{7,3},{8,10},{9,13},{10,... | collective-permute-start | bytes 786440 | tf_op jit(solution)/shard_map/ppermute | solution.py:256
  26.5 10.9 %slice-start.1 = ((s8[16777216]{0:T(1024)(128)(4,1)}), s8[4194304]{0:T(1024)(128)(4,1)S(1)}, s32[]{:S(2)}) async-start(s8[16777216]{0:T(1024)(128)(4,1)} %bitcast.27), calls=%async_computation.1 | async-start | bytes 8388608
  26.5 10.9 %slice-start.2 = ((s8[16777216]{0:T(1024)(128)(4,1)}), s8[4194304]{0:T(1024)(128)(4,1)S(1)}, s32[]{:S(2)}) async-start(s8[16777216]{0:T(1024)(128)(4,1)} %bitcast.27), calls=%async_computation.2 | async-start | bytes 8388608
  26.6 10.9 %slice-start.3 = ((s8[16777216]{0:T(1024)(128)(4,1)}), s8[4194304]{0:T(1024)(128)(4,1)S(1)}, s32[]{:S(2)}) async-start(s8[16777216]{0:T(1024)(128)(4,1)} %bitcast.27), calls=%async_computation.3 | async-start | bytes 8388608
  26.6 7.3 %collective-permute-start.5 = (bf16[1,128,128]{2,1,0:T(8,128)(2,1)S(1)}, bf16[1,128,128]{2,1,0:T(8,128)(2,1)S(1)}, u32[]{:S(2)}, u32[]{:S(2)}) collective-permute-start(bf16[1,128,128]{2,1,0:T(8,128)(2,1)S(1)} %slice.115), channel_id=1, source_target_pairs={{0,16},{1,17},{2,18},{3,19},{4,20},{5,21},{6,22},{7,23},{8,24},{9,... | collective-permute-start | bytes 98312 | tf_op jit(solution)/shard_map/ppermute | solution.py:253
  29.2 6.1 %collective-permute-start.11 = (bf16[2,128,512]{2,1,0:T(8,128)(2,1)S(1)}, bf16[2,128,512]{2,1,0:T(8,128)(2,1)S(1)}, u32[]{:S(2)}, u32[]{:S(2)}) collective-permute-start(bf16[2,128,512]{2,1,0:T(8,128)(2,1)S(1)} %pad_maximum_fusion.3.refs_2_), channel_id=1, source_target_pairs={{0,1},{1,0},{2,3},{3,2},{4,5},{5,4},{6,7},{7,6},{8,9},{9,8},{10,11... | collective-permute-start | bytes 786440 | tf_op jit(solution)/shard_map/ppermute | solution.py:253
  33.8 3.7 %collective-permute-start.13 = (bf16[4,128,512]{2,1,0:T(8,128)(2,1)S(1)}, bf16[4,128,512]{2,1,0:T(8,128)(2,1)S(1)}, u32[]{:S(2)}, u32[]{:S(2)}) collective-permute-start(bf16[4,128,512]{2,1,0:T(8,128)(2,1)S(1)} %collective-permute-done.10.refs_4_), channel_id=1, source_target_pairs={{0,1},{1,0},{2,3},{3,2},{4,5},{5,4},{6,7},{7,6},{8,9},{9,8},{10,11... | collective-permute-start | bytes 1572872 | tf_op jit(solution)/shard_map/ppermute | solution.py:253
  34.0 9.2 %collective-permute-start.6 = (bf16[4,128,512]{2,1,0:T(8,128)(2,1)S(1)}, bf16[4,128,512]{2,1,0:T(8,128)(2,1)S(1)}, u32[]{:S(2)}, u32[]{:S(2)}) collective-permute-start(bf16[4,128,512]{2,1,0:T(8,128)(2,1)S(1)} %pad_maximum_fusion), channel_id=1, source_target_pairs={{0,4},{1,3},{2,6},{3,1},{4,0},{5,7},{6,2},{7,5},{8,12},{9,11},{10,... | collective-permute-start | bytes 1572872 | tf_op jit(solution)/shard_map/ppermute | solution.py:256
  34.7 1.5 %collective-permute-start.12 = (bf16[2,128,512]{2,1,0:T(8,128)(2,1)S(1)}, bf16[2,128,512]{2,1,0:T(8,128)(2,1)S(1)}, u32[]{:S(2)}, u32[]{:S(2)}) collective-permute-start(bf16[2,128,512]{2,1,0:T(8,128)(2,1)S(1)} %collective-permute-done.9.refs_3_), channel_id=1, source_target_pairs={{0,1},{1,0},{2,3},{3,2},{4,5},{5,4},{6,7},{7,6},{8,9},{9,8},{10,11... | collective-permute-start | bytes 786440 | tf_op jit(solution)/shard_map/ppermute | solution.py:253
  34.7 4.7 %collective-permute-start.7 = (bf16[2,128,512]{2,1,0:T(8,128)(2,1)S(1)}, bf16[2,128,512]{2,1,0:T(8,128)(2,1)S(1)}, u32[]{:S(2)}, u32[]{:S(2)}) collective-permute-start(bf16[2,128,512]{2,1,0:T(8,128)(2,1)S(1)} %slice.72.refs_2_), channel_id=1, source_target_pairs={{0,1},{1,0},{2,3},{3,2},{4,5},{5,4},{6,7},{7,6},{8,9},{9,8},{10,11... | collective-permute-start | bytes 786440 | tf_op jit(solution)/shard_map/ppermute | solution.py:253
  35.2 4.2 %collective-permute-start.8 = (bf16[2,128,512]{2,1,0:T(8,128)(2,1)S(1)}, bf16[2,128,512]{2,1,0:T(8,128)(2,1)S(1)}, u32[]{:S(2)}, u32[]{:S(2)}) collective-permute-start(bf16[2,128,512]{2,1,0:T(8,128)(2,1)S(1)} %collective-permute-done.4.refs_3_), channel_id=1, source_target_pairs={{0,1},{1,0},{2,3},{3,2},{4,5},{5,4},{6,7},{7,6},{8,9},{9,8},{10,11... | collective-permute-start | bytes 786440 | tf_op jit(solution)/shard_map/ppermute | solution.py:253
  36.2 7.3 %collective-permute-start.15 = (bf16[128,128]{1,0:T(8,128)(2,1)S(1)}, bf16[128,128]{1,0:T(8,128)(2,1)S(1)}, u32[]{:S(2)}, u32[]{:S(2)}) collective-permute-start(bf16[128,128]{1,0:T(8,128)(2,1)S(1)} %bitcast_convert_fusion), channel_id=1, source_target_pairs={{0,2},{1,3},{2,0},{3,1},{4,6},{5,7},{6,4},{7,5},{8,10},{9,11},{10,... | collective-permute-start | bytes 98312 | tf_op jit(solution)/shard_map/ppermute | solution.py:253
  43.2 2.0 %collective-permute-start.14 = (bf16[4,128,512]{2,1,0:T(8,128)(2,1)S(1)}, bf16[4,128,512]{2,1,0:T(8,128)(2,1)S(1)}, u32[]{:S(2)}, u32[]{:S(2)}) collective-permute-start(bf16[4,128,512]{2,1,0:T(8,128)(2,1)S(1)} %collective-permute-done.6.refs_2_), channel_id=1, source_target_pairs={{0,1},{1,0},{2,3},{3,2},{4,5},{5,4},{6,7},{7,6},{8,9},{9,8},{10,11... | collective-permute-start | bytes 1572872 | tf_op jit(solution)/shard_map/ppermute | solution.py:253
  43.5 1.7 %collective-permute-start.16 = (f32[128,128]{1,0:T(8,128)S(1)}, f32[128,128]{1,0:T(8,128)S(1)}, u32[]{:S(2)}, u32[]{:S(2)}) collective-permute-start(f32[128,128]{1,0:T(8,128)S(1)} %bitcast_add_fusion.refs_6_), channel_id=1, source_target_pairs={{0,1},{1,0},{2,3},{3,2},{4,5},{5,4},{6,7},{7,6},{8,9},{9,8},{10,11... | collective-permute-start | bytes 196616 | tf_op jit(solution)/shard_map/ppermute | solution.py:253
  47.3 2.0 %collective-permute-start.17 = (bf16[4,128,512]{2,1,0:T(8,128)(2,1)S(1)}, bf16[4,128,512]{2,1,0:T(8,128)(2,1)S(1)}, u32[]{:S(2)}, u32[]{:S(2)}) collective-permute-start(bf16[4,128,512]{2,1,0:T(8,128)(2,1)S(1)} %shard_map.71), channel_id=1, source_target_pairs={{0,1},{1,0},{2,3},{3,2},{4,5},{5,4},{6,7},{7,6},{8,9},{9,8},{10,11... | collective-permute-start | bytes 1572872 | tf_op jit(solution)/shard_map/ppermute | solution.py:253
  49.4 9.2 %collective-permute-start.20 = (bf16[4,128,512]{2,1,0:T(8,128)(2,1)S(1)}, bf16[4,128,512]{2,1,0:T(8,128)(2,1)S(1)}, u32[]{:S(2)}, u32[]{:S(2)}) collective-permute-start(bf16[4,128,512]{2,1,0:T(8,128)(2,1)S(1)} %add_convert_fusion.1), channel_id=1, source_target_pairs={{0,2},{1,5},{2,0},{3,7},{4,6},{5,1},{6,4},{7,3},{8,10},{9,13},{10,... | collective-permute-start | bytes 1572872 | tf_op jit(solution)/shard_map/ppermute | solution.py:256
  51.4 8.1 %collective-permute-start.21 = (bf16[4,128,512]{2,1,0:T(8,128)(2,1)S(1)}, bf16[4,128,512]{2,1,0:T(8,128)(2,1)S(1)}, u32[]{:S(2)}, u32[]{:S(2)}) collective-permute-start(bf16[4,128,512]{2,1,0:T(8,128)(2,1)S(1)} %get-tuple-element.68), channel_id=1, source_target_pairs={{0,1},{1,0},{2,3},{3,2},{4,5},{5,4},{6,7},{7,6},{8,9},{9,8},{10,11... | collective-permute-start | bytes 1572872 | tf_op jit(solution)/shard_map/ppermute | solution.py:253
  51.4 2.3 %collective-permute-start.19 = (bf16[2,128,512]{2,1,0:T(8,128)(2,1)S(1)}, bf16[2,128,512]{2,1,0:T(8,128)(2,1)S(1)}, u32[]{:S(2)}, u32[]{:S(2)}) collective-permute-start(bf16[2,128,512]{2,1,0:T(8,128)(2,1)S(1)} %get-tuple-element.74), channel_id=1, source_target_pairs={{0,1},{1,0},{2,3},{3,2},{4,5},{5,4},{6,7},{7,6},{8,9},{9,8},{10,11... | collective-permute-start | bytes 786440 | tf_op jit(solution)/shard_map/ppermute | solution.py:253
  51.9 9.5 %collective-permute-start.26 = (bf16[2,128,512]{2,1,0:T(8,128)(2,1)S(1)}, bf16[2,128,512]{2,1,0:T(8,128)(2,1)S(1)}, u32[]{:S(2)}, u32[]{:S(2)}) collective-permute-start(bf16[2,128,512]{2,1,0:T(8,128)(2,1)S(1)} %get-tuple-element.65), channel_id=1, source_target_pairs={{0,1},{1,0},{2,3},{3,2},{4,5},{5,4},{6,7},{7,6},{8,9},{9,8},{10,11... | collective-permute-start | bytes 786440 | tf_op jit(solution)/shard_map/ppermute | solution.py:253
  58.8 9.2 %collective-permute-start.27 = (bf16[2,128,512]{2,1,0:T(8,128)(2,1)S(1)}, bf16[2,128,512]{2,1,0:T(8,128)(2,1)S(1)}, u32[]{:S(2)}, u32[]{:S(2)}) collective-permute-start(bf16[2,128,512]{2,1,0:T(8,128)(2,1)S(1)} %add_convert_fusion.3), channel_id=1, source_target_pairs={{0,4},{1,3},{2,6},{3,1},{4,0},{5,7},{6,2},{7,5},{8,12},{9,11},{10,... | collective-permute-start | bytes 786440 | tf_op jit(solution)/shard_map/ppermute | solution.py:256
  59.7 10.5 %collective-permute-start.22 = (bf16[4,128,512]{2,1,0:T(8,128)(2,1)S(1)}, bf16[4,128,512]{2,1,0:T(8,128)(2,1)S(1)}, u32[]{:S(2)}, u32[]{:S(2)}) collective-permute-start(bf16[4,128,512]{2,1,0:T(8,128)(2,1)S(1)} %add_convert_fusion), channel_id=1, source_target_pairs={{0,2},{1,5},{2,0},{3,7},{4,6},{5,1},{6,4},{7,3},{8,10},{9,13},{10,... | collective-permute-start | bytes 1572872 | tf_op jit(solution)/shard_map/ppermute | solution.py:256
  60.9 13.2 %collective-permute-start.18 = (bf16[2,128,512]{2,1,0:T(8,128)(2,1)S(1)}, bf16[2,128,512]{2,1,0:T(8,128)(2,1)S(1)}, u32[]{:S(2)}, u32[]{:S(2)}) collective-permute-start(bf16[2,128,512]{2,1,0:T(8,128)(2,1)S(1)} %get-tuple-element.71), channel_id=1, source_target_pairs={{0,1},{1,0},{2,3},{3,2},{4,5},{5,4},{6,7},{7,6},{8,9},{9,8},{10,11... | collective-permute-start | bytes 786440 | tf_op jit(solution)/shard_map/ppermute | solution.py:253
  61.0 9.2 %collective-permute-start.23 = (bf16[2,128,512]{2,1,0:T(8,128)(2,1)S(1)}, bf16[2,128,512]{2,1,0:T(8,128)(2,1)S(1)}, u32[]{:S(2)}, u32[]{:S(2)}) collective-permute-start(bf16[2,128,512]{2,1,0:T(8,128)(2,1)S(1)} %get-tuple-element.77), channel_id=1, source_target_pairs={{0,1},{1,0},{2,3},{3,2},{4,5},{5,4},{6,7},{7,6},{8,9},{9,8},{10,11... | collective-permute-start | bytes 786440 | tf_op jit(solution)/shard_map/ppermute | solution.py:253
  68.2 5.6 %collective-permute-start.28 = (bf16[128,512]{1,0:T(8,128)(2,1)S(1)}, bf16[128,512]{1,0:T(8,128)(2,1)S(1)}, u32[]{:S(2)}, u32[]{:S(2)}) collective-permute-start(bf16[128,512]{1,0:T(8,128)(2,1)S(1)} %fusion.6), channel_id=1, source_target_pairs={{0,8},{1,9},{2,10},{3,11},{4,12},{5,13},{6,14},{7,15},{8,0},{9,1},... | collective-permute-start | bytes 393224 | tf_op jit(solution)/shard_map/ppermute | solution.py:253
  70.3 6.4 %collective-permute-start.24 = (bf16[2,128,512]{2,1,0:T(8,128)(2,1)S(1)}, bf16[2,128,512]{2,1,0:T(8,128)(2,1)S(1)}, u32[]{:S(2)}, u32[]{:S(2)}) collective-permute-start(bf16[2,128,512]{2,1,0:T(8,128)(2,1)S(1)} %add_convert_fusion.2), channel_id=1, source_target_pairs={{0,4},{1,3},{2,6},{3,1},{4,0},{5,7},{6,2},{7,5},{8,12},{9,11},{10,... | collective-permute-start | bytes 786440 | tf_op jit(solution)/shard_map/ppermute | solution.py:256
  73.8 6.0 %collective-permute-start.29 = (bf16[128,512]{1,0:T(8,128)(2,1)S(1)}, bf16[128,512]{1,0:T(8,128)(2,1)S(1)}, u32[]{:S(2)}, u32[]{:S(2)}) collective-permute-start(bf16[128,512]{1,0:T(8,128)(2,1)S(1)} %fusion.1), channel_id=1, source_target_pairs={{0,16},{1,17},{2,18},{3,19},{4,20},{5,21},{6,22},{7,23},{8,24},{9,... | collective-permute-start | bytes 393224 | tf_op jit(solution)/shard_map/ppermute | solution.py:253
  76.9 5.5 %collective-permute-start.25 = (bf16[128,512]{1,0:T(8,128)(2,1)S(1)}, bf16[128,512]{1,0:T(8,128)(2,1)S(1)}, u32[]{:S(2)}, u32[]{:S(2)}) collective-permute-start(bf16[128,512]{1,0:T(8,128)(2,1)S(1)} %fusion.5), channel_id=1, source_target_pairs={{0,8},{1,9},{2,10},{3,11},{4,12},{5,13},{6,14},{7,15},{8,0},{9,1},... | collective-permute-start | bytes 393224 | tf_op jit(solution)/shard_map/ppermute | solution.py:253

commit v9 on v8

--- a/solution.py
+++ b/solution.py
@@ -40,6 +40,11 @@
     return pltpu.with_memory_space_constraint(x, pltpu.HBM)
 
 
+def device(where, symbol):
+    const, (i, j) = symbol
+    return where[3 * i + j] ^ const
+
+
 def dot(a, b):
     return jnp.dot(a, b, preferred_element_type=jnp.float32)
 
@@ -47,7 +52,7 @@
 def fetch_kernel(symbols, width, where, source, target, sems):
     copies = []
     for i, (const, pick) in enumerate(symbols):
-        start = pl.multiple_of((where[pick] ^ const) * width, LANE)
+        start = pl.multiple_of((device(where, (const, pick))) * width, LANE)
         copy = pltpu.make_async_copy(
             source.at[:, pl.ds(start, width)], target.at[i], sems.at[i]
         )
@@ -88,12 +93,11 @@
     core0 = (me & CORE) == 0
     for h in range(KVH):
         off = h ^ (me >> shared)
-        spot = 0
-        for b in range(KVH.bit_length() - 1):
-            spot = spot * 2 + (1 - ((off >> b) & 1))
+        low, a, b = off & 1, (off >> 1) & 1, (off >> 2) & 1
+        spot_0, spot_1 = 7 - (4 * low + 2 * b + a), 7 - (4 * low + 2 * a + b)
         kh, vh = k[:, h * HEAD : (h + 1) * HEAD], v[:, h * HEAD : (h + 1) * HEAD]
-        keep[spot] = jnp.where(core0, kh, vh)
-        send[spot] = jnp.where(core0, vh, kh)
+        keep[jnp.where(core0, spot_0, spot_1)] = jnp.where(core0, kh, vh)
+        send[jnp.where(core0, spot_1, spot_0)] = jnp.where(core0, vh, kh)
 
 
 def kv_terms(shared, where, act, gain, wk, wv):
@@ -158,7 +162,7 @@
     width = pieces[0].shape[2]
     for piece, blocks in zip(pieces, places):
         for block, (const, pick) in enumerate(blocks):
-            span = pl.ds(pl.multiple_of((where[pick] ^ const) * width, LANE), width)
+            span = pl.ds(pl.multiple_of((device(where, (const, pick))) * width, LANE), width)
             x = piece[block].astype(jnp.float32)
             for c in range(0, width, LANE):
                 square = x[:, c : c + LANE] * x[:, c : c + LANE]
@@ -212,23 +216,52 @@
             out[block] = dot(left, weight[spot]).astype(out.dtype)
 
 
-def output_call(attended, held, width, groups):
-    weight, order = held
+def output_fetch_kernel(groups, where, attended, weight, *refs):
+    outs, buf, sems = refs[: len(groups)], refs[-2], refs[-1]
+    copies = []
+    for i, (const, pick) in enumerate(sum(groups, [])):
+        width = buf.shape[2]
+        start = pl.multiple_of((device(where, (const, pick))) * width, LANE)
+        copy = pltpu.make_async_copy(weight.at[:, pl.ds(start, width)], buf.at[i], sems.at[i])
+        copy.start()
+        copies.append(copy)
+    left = attended[...]
+    i = 0
+    for symbols, out in zip(groups, outs):
+        for block in range(len(symbols)):
+            copies[i].wait()
+            out[block] = dot(left, buf[i]).astype(out.dtype)
+            i += 1
+
+
+def output_call(attended, width, groups, held=None, where=None, weight=None):
     tokens, depth = attended.shape
-    spots = [[order.index(s) for s in symbols] for symbols, _ in groups]
-    columns = width * sum(len(s) for s in spots)
+    blocks = sum(len(s) for s, _ in groups)
+    if held is not None:
+        kernel = functools.partial(
+            output_kernel, [[held[1].index(s) for s in symbols] for symbols, _ in groups]
+        )
+        operands, specs, scratch = (attended, held[0]), [vmem(), vmem()], []
+    else:
+        kernel = functools.partial(output_fetch_kernel, [symbols for symbols, _ in groups])
+        operands, specs = (where, attended, in_hbm(weight)), [smem(), vmem(), hbm()]
+        scratch = [
+            pltpu.VMEM((blocks, depth, width), weight.dtype),
+            pltpu.SemaphoreType.DMA((blocks,)),
+        ]
     return pl.pallas_call(
-        functools.partial(output_kernel, spots),
+        kernel,
         out_shape=[jax.ShapeDtypeStruct((len(s), tokens, width), t) for s, t in groups],
-        in_specs=[vmem(), vmem()],
+        in_specs=specs,
         out_specs=[vmem()] * len(groups),
-        compiler_params=pltpu.CompilerParams(vmem_limit_bytes=4 * MIB),
+        scratch_shapes=scratch,
+        compiler_params=pltpu.CompilerParams(vmem_limit_bytes=10 * MIB),
         cost_estimate=pl.CostEstimate(
-            flops=2 * tokens * depth * columns,
-            bytes_accessed=2 * depth * columns,
+            flops=2 * tokens * depth * width * blocks,
+            bytes_accessed=2 * depth * width * blocks,
             transcendentals=0,
         ),
-    )(attended, weight)
+    )(*operands)
 
 
 def rotary_tables(tokens):
@@ -245,25 +278,34 @@
     bits = [1 << i for i in range(n.bit_length() - 1)]
     ways = (bits[1], bits[2])
     diagonal = bits[1] ^ bits[2]
-    near, top = combos(bits[3:-1]), bits[-1]
-    far = [o ^ top for o in near]
+    low, z_ways = combos(bits[3:-2]), (bits[-2], bits[-1])
     f32, bf16 = jnp.float32, jnp.bfloat16
 
     def swap(x, offset):
         return lax.ppermute(x, "wide", [(i, i ^ offset) for i in range(n)])
 
+    def by_core(x, pair, step):
+        return lax.ppermute(x, "wide", [(i, i ^ pair[(step + (i & CORE)) % 2]) for i in range(n)])
+
     def turn(x, step):
-        return lax.ppermute(x, "wide", [(i, i ^ ways[(step + (i & CORE)) % 2]) for i in range(n)])
-
-    bit = jnp.where((me & CORE) == 0, ways[0], ways[1])
-    where = jnp.stack([me, me ^ bit, me ^ bit ^ diagonal]).astype(jnp.int32)
+        return by_core(x, ways, step)
+
+    def along(x, step):
+        return by_core(x, z_ways, step)
+
+    def steps(pair):
+        first = jnp.where((me & CORE) == 0, pair[0], pair[1])
+        return [jnp.zeros_like(me), first, first ^ pair[0] ^ pair[1]]
+
+    where = jnp.stack([me ^ i ^ j for i in steps(ways) for j in steps(z_ways)]).astype(jnp.int32)
     gain = norm_gain.reshape(1, -1)
 
-    def plain(offsets, pick=0):
-        return [(o, pick) for o in offsets]
-
     def across(symbols):
-        return [(const ^ CORE, (0, 2, 1)[pick]) for const, pick in symbols]
+        flip = (0, 2, 1)
+        return [(const ^ CORE, (flip[i], flip[j])) for const, (i, j) in symbols]
+
+    near = [(o, j) for j in (0, 1) for o in low]
+    far = [(o, 2) for o in low] + [(o ^ z_ways[0] ^ z_ways[1], 0) for o in low]
 
     def after(x, *others):
         return lax.optimization_barrier((x, *others))[0]
@@ -274,7 +316,7 @@
 
     def symbols_of(offsets):
         square = [(0, 0), (0, 1), (0, 2), (diagonal, 0)]
-        return [[(const ^ o, pick) for o in offsets] for const, pick in square]
+        return [[(const ^ o, (i, j)) for o, j in offsets] for const, i in square]
 
     def other(pieces):
         return [(swap(x, CORE), across(symbols)) for x, symbols in pieces]
@@ -287,40 +329,30 @@
         own = sum(order(offsets), [])
         return own + across(own)
 
-    def halved(kv, arrived=None, offset=0):
+    def halved(kv, send, way):
         half = kv.shape[0] // 2
-        if arrived is None:
-            arrived = swap(kv[:half].astype(bf16), offset)
-        return kv[half:] + arrived.astype(f32)
-
-    kv = halved(kv_keep + swap(kv_send, CORE), offset=bits[shared])
-    row = jnp.stack([act, swap(raw, top)])
+        return kv[half:] + send(kv[:half].astype(bf16), way).astype(f32)
+
+    kv = halved(kv_keep + swap(kv_send, CORE), swap, bits[shared])
     far_blocks, far_symbols = fetched(where, wo, width, columns_of(far))
+    row = jnp.stack([act] + [swap(raw, o) for o in low[1:]])
+    row = jnp.concatenate([row, along(row, 0)])
     row, kv, far_blocks = lax.optimization_barrier((row, kv, far_blocks))
     far_held = (far_blocks, far_symbols)
-    ride = bits[shared + 1]
-    side = turn(row, 0)
-    rest = []
-    for o in near[1:]:
-        if o == ride:
-            got = swap(jnp.concatenate([row, kv[: kv.shape[0] // 2].astype(bf16)], axis=2), o)
-            kv = halved(kv, got[:, :, width:])
-            got = got[:, :, :width]
+    groups = []
+    for offsets in (near, far):
+        if offsets is far:
+            half = kv[: kv.shape[0] // 2].astype(bf16)
+            k = min(row.shape[0], half.shape[0])
+            extra = jnp.zeros((row.shape[0], *half.shape[1:]), bf16).at[:k].set(half[:k])
+            got = along(jnp.concatenate([row, extra], axis=2), 1)
+            row = got[:, :, :width]
+            kv = kv[kv.shape[0] // 2 :] + got[:k, :, width:].astype(f32)
+            side = turn(row, 0)
+            kv = halved(kv, along, 0)
+            side, kv = lax.optimization_barrier((side, kv))
         else:
-            got = swap(row, o)
-        rest.append(got)
-    groups = []
-    for offsets, row, side in (
-        ([0, top], row, side),
-        ([o ^ t for o in near[1:] for t in (0, top)], jnp.concatenate(rest), None),
-    ):
-        if side is None:
             side = turn(row, 0)
-            for b in bits[shared + 2 :]:
-                kv = halved(kv, offset=b)
-            near_blocks, near_symbols = fetched(after(where, row), wo, width, columns_of(near))
-            side, kv, near_blocks = lax.optimization_barrier((side, kv, near_blocks))
-            near_held = (near_blocks, near_symbols)
         both = turn(jnp.concatenate([row, side]), 1)
         at = symbols_of(offsets)
         groups.append([(row, at[0]), (side, at[1]), (both, at[2] + at[3])])
@@ -345,17 +377,12 @@
         got = turn(first, 0)
         k = got.shape[0] // 2
         two = added_up(*two, got[:k]).astype(bf16)
-        return [*home, got[k:], turn(two, 1)], two
+        return [*home, got[k:]], two
 
     def added_up(home, *arrived):
         for x in arrived:
             home = home + x.astype(f32)
         return home
-
-    def along_z(blocks):
-        return added_up(
-            blocks[0], *[swap(blocks[i].astype(bf16), o) for i, o in enumerate(near) if o]
-        )
 
     def theirs(symbols):
         return [(across(s), bf16) for s in symbols]
@@ -371,15 +398,22 @@
     own = project(after(attended, *sent), groups=ours(order(far)))
     first = added_up(own[0], swap(sent[0], CORE)).astype(bf16)
     sent = project(after(attended, first), groups=theirs(order(far)[1:]))
-    far_sums, two = round_square(first, *paired(own[1:], sent))
-    project = functools.partial(output_call, held=near_held, width=width)
+    far_home, far_two = round_square(first, *paired(own[1:], sent))
+    far_sum = added_up(*far_home, turn(far_two, 1))
+    project = functools.partial(output_call, width=width, where=where, weight=wo)
     sent = project(after(attended, sent[-1]), groups=theirs(order(near)))
     own = project(after(attended, sent[0]), groups=ours(order(near)))
     pairs = paired(own, sent)
-    first = added_up(after(pairs[0][0], two), pairs[0][1]).astype(bf16)
-    near_sums, _ = round_square(first, *pairs[1:])
-    got = swap(along_z(added_up(*far_sums)).astype(bf16), top)
-    out = added_up(along_z(added_up(*near_sums)), got)
+    first = added_up(after(pairs[0][0], far_two), pairs[0][1]).astype(bf16)
+    near_home, near_two = round_square(first, *pairs[1:])
+    k = len(low)
+    far_sum = added_up(far_sum[:k], along(far_sum[k:].astype(bf16), 0))
+    far_got = along(far_sum.astype(bf16), 1)
+    got = [turn(near_two[k:], 1), turn(near_two[:k], 1)]
+    near_sum = added_up(*[x[k:] for x in near_home], got[0])
+    home_sum = added_up(*[x[:k] for x in near_home], got[1])
+    home_sum = added_up(home_sum, along(near_sum.astype(bf16), 0), far_got)
+    out = added_up(home_sum[0], *[swap(home_sum[i].astype(bf16), o) for i, o in enumerate(low) if o])
     return out.astype(bf16)
 
 

time: 83.2 us -> 83.5 us (level)
  waiting for transfers between devices: 34.8 us -> 30.6 us
  starting transfers between devices: 25.2 us -> 27.9 us
  Pallas kernels: 20.3 us -> 22.1 us
    ppermute x8 -> x15, starting transfers between devices: 8.94 us -> 21.9 us  [by_core(): lax.ppermute(x, 'wide', [(i, i ^ pair[(step + (i & CORE)) % 2]) for i in...]
    ppermute x22 -> x16, waiting for transfers between devices: 14.4 us -> 2.04 us  [swap(): return lax.ppermute(x, 'wide', [(i, i ^ offset) for i in range(n)])]
    ppermute x22 -> x16, starting transfers between devices: 16.3 us -> 6.01 us  [swap(): return lax.ppermute(x, 'wide', [(i, i ^ offset) for i in range(n)])]
    ppermute x8 -> x15, waiting for transfers between devices: 20.4 us -> 28.5 us  [by_core(): lax.ppermute(x, 'wide', [(i, i ^ pair[(step + (i & CORE)) % 2]) for i in...]
    pallas_call x5, Pallas kernels: 3.03 us -> 8.66 us  [output_call(): pl.pallas_call(kernel, out_shape=[jax.ShapeDtypeStruct((len(s), tokens, w...]
    pallas_call x2 -> x1, Pallas kernels: 8.7 us -> 4.89 us  [fetched(): pl.pallas_call(functools.partial(fetch_kernel, symbols, width), out_shape...]
  transfers between devices with their start and end apart: 30 -> 31, of which waited for: 13 -> 12; matrix products, arithmetic and copies ran while one was open for 2% -> 2% of each run, Pallas kernels for 19% -> 21%
where the time goes in v9:
time: 83.5 us; the launch traced here: 83.3 us
  waiting for transfers between devices  30.6 us (37%)
  starting transfers between devices  27.9 us (33%)
  Pallas kernels  22.1 us (26%)
  other arithmetic  2.21 us (3%)
    ppermute x15, waiting for transfers between devices, by_core(): lax.ppermute(x, 'wide', [(i, i ^ pair[(step + (i & CORE)) % 2]) for i in...  28.5 us
    ppermute x15, starting transfers between devices, by_core(): lax.ppermute(x, 'wide', [(i, i ^ pair[(step + (i & CORE)) % 2]) for i in...  21.9 us
    pallas_call x5, Pallas kernels, output_call(): pl.pallas_call(kernel, out_shape=[jax.ShapeDtypeStruct((len(s), tokens, w...  8.66 us
    ppermute x16, starting transfers between devices, swap(): return lax.ppermute(x, 'wide', [(i, i ^ offset) for i in range(n)])  6.01 us
    pallas_call x4, Pallas kernels, query_call(): pl.pallas_call(functools.partial(query_kernel, places, bool(carry), bool(...  5.88 us
    pallas_call x1, Pallas kernels, fetched(): pl.pallas_call(functools.partial(fetch_kernel, symbols, width), out_shape...  4.89 us
    pallas_call x1, Pallas kernels, kv_terms(): pl.pallas_call(functools.partial(kv_kernel, shared), out_shape=[jax.Shape...  2.68 us
    ppermute x16, waiting for transfers between devices, swap(): return lax.ppermute(x, 'wide', [(i, i ^ offset) for i in range(n)])  2.04 us
  transfers between devices with their start and end apart: 31, of which 12 were waited for; matrix products, arithmetic and copies ran while one was open for 2% of the time, Pallas kernels for 21%

profile of v9, /device:TPU:0, one launch (start us, length us, event | category | flops | bytes accessed | tf_op | source)
XLA Modules:
  0.0 83.3 jit_solution(13138316350364044434)
XLA Ops:
  0.1 2.7 %shard_map.69 = (f32[8,128,128]{2,1,0:T(8,128)S(1)}, f32[8,128,128]{2,1,0:T(8,128)S(1)}, bf16[128,512]{1,0:T(8,128)(2,1)S(1)}, f32[1,16384]{1,0:T(1,128)S(1)}) custom-call(s32[9]{0:T(128)S(1)} %stack.42.where.refs_0_, bf16[128,512]{1,0:T(8,128)(2,1)} %act.1, f32[1,16384]{1,0:T(1,128)} %bitcast.20, bf16[512,1024]{1,0:T(8,128)(2,1)} %wk.1, bf16[512,1024]{1,0:T(8,128)(2,1)} %wv.1), custom_call_target="tpu_custom_call" | custom-call | flops 4294967296 | bytes 33554432 | tf_op jit(solution)/shard_map/pallas_call | solution.py:105
  2.8 0.5 collective-permute-start.1
  3.3 2.7 %collective-permute-start = (bf16[1,128,512]{2,1,0:T(8,128)(2,1)S(1)}, bf16[1,128,512]{2,1,0:T(8,128)(2,1)S(1)}, u32[]{:S(2)}, u32[]{:S(2)}) collective-permute-start(bf16[1,128,512]{2,1,0:T(8,128)(2,1)S(1)} %bitcast.18), channel_id=1, source_target_pairs={{0,8},{1,17},{2,10},{3,19},{4,12},{5,21},{6,14},{7,23},{8,0},{9,25... | collective-permute-start | bytes 393224 | tf_op jit(solution)/shard_map/ppermute | solution.py:288
  6.1 1.8 %collective-permute-start.2 = (bf16[4,128,128]{2,1,0:T(8,128)(2,1)S(1)}, bf16[4,128,128]{2,1,0:T(8,128)(2,1)S(1)}, u32[]{:S(2)}, u32[]{:S(2)}) collective-permute-start(bf16[4,128,128]{2,1,0:T(8,128)(2,1)S(1)} %slice.151), channel_id=1, source_target_pairs={{0,4},{1,5},{2,6},{3,7},{4,0},{5,1},{6,2},{7,3},{8,12},{9,13},{10,... | collective-permute-start | bytes 393224 | tf_op jit(solution)/shard_map/ppermute | solution.py:285
  7.9 4.9 %shard_map.70.weight = bf16[16,512,512]{2,1,0:T(8,128)(2,1)S(1)} custom-call(s32[9]{0:T(128)S(1)} %stack.42.where.refs_0_, bf16[512,16384]{1,0:T(8,128)(2,1)} %weight.3), custom_call_target="tpu_custom_call" | custom-call | bytes 16777216 | tf_op jit(solution)/shard_map/pallas_call | solution.py:67
  12.9 1.6 %collective-permute-start.9 = (bf16[2,128,512]{2,1,0:T(8,128)(2,1)S(1)}, bf16[2,128,512]{2,1,0:T(8,128)(2,1)S(1)}, u32[]{:S(2)}, u32[]{:S(2)}) collective-permute-start(bf16[2,128,512]{2,1,0:T(8,128)(2,1)S(1)} %pad_maximum_fusion.3.refs_2_), channel_id=1, source_target_pairs={{0,2},{1,5},{2,0},{3,7},{4,6},{5,1},{6,4},{7,3},{8,10},{9,13},{10,... | collective-permute-start | bytes 786440 | tf_op jit(solution)/shard_map/ppermute | solution.py:288
  14.5 2.7 %collective-permute-start.3 = (bf16[2,128,640]{2,1,0:T(8,128)(2,1)S(1)}, bf16[2,128,640]{2,1,0:T(8,128)(2,1)S(1)}, u32[]{:S(2)}, u32[]{:S(2)}) collective-permute-start(bf16[2,128,640]{2,1,0:T(8,128)(2,1)S(1)} %pad_maximum_fusion.2), channel_id=1, source_target_pairs={{0,16},{1,9},{2,18},{3,11},{4,20},{5,13},{6,22},{7,15},{8,24},{9,1... | collective-permute-start | bytes 983048 | tf_op jit(solution)/shard_map/ppermute | solution.py:288
  17.2 2.2 %collective-permute-done.9.refs_3_ = bf16[2,128,512]{2,1,0:T(8,128)(2,1)S(1)} collective-permute-done((bf16[2,128,512]{2,1,0:T(8,128)(2,1)S(1)}, bf16[2,128,512]{2,1,0:T(8,128)(2,1)S(1)}, u32[]{:S(2)}, u32[]{:S(2)}) %collective-permute-start.9) | collective-permute-done | bytes 262176 | tf_op jit(solution)/shard_map/ppermute | solution.py:288
  19.4 1.4 %collective-permute-start.10 = (bf16[4,128,512]{2,1,0:T(8,128)(2,1)S(1)}, bf16[4,128,512]{2,1,0:T(8,128)(2,1)S(1)}, u32[]{:S(2)}, u32[]{:S(2)}) collective-permute-start(bf16[4,128,512]{2,1,0:T(8,128)(2,1)S(1)} %pad_maximum_fusion.1), channel_id=1, source_target_pairs={{0,4},{1,3},{2,6},{3,1},{4,0},{5,7},{6,2},{7,5},{8,12},{9,11},{10,... | collective-permute-start | bytes 1572872 | tf_op jit(solution)/shard_map/ppermute | solution.py:288
  20.8 5.3 %collective-permute-done.3 = bf16[2,128,640]{2,1,0:T(8,128)(2,1)S(1)} collective-permute-done((bf16[2,128,640]{2,1,0:T(8,128)(2,1)S(1)}, bf16[2,128,640]{2,1,0:T(8,128)(2,1)S(1)}, u32[]{:S(2)}, u32[]{:S(2)}) %collective-permute-start.3) | collective-permute-done | bytes 327712 | tf_op jit(solution)/shard_map/ppermute | solution.py:288
  26.1 0.6 collective-permute-start.4
  26.8 1.0 %collective-permute-start.5 = (bf16[1,128,128]{2,1,0:T(8,128)(2,1)S(1)}, bf16[1,128,128]{2,1,0:T(8,128)(2,1)S(1)}, u32[]{:S(2)}, u32[]{:S(2)}) collective-permute-start(bf16[1,128,128]{2,1,0:T(8,128)(2,1)S(1)} %slice.153), channel_id=1, source_target_pairs={{0,8},{1,17},{2,10},{3,19},{4,12},{5,21},{6,14},{7,23},{8,0},{9,25... | collective-permute-start | bytes 98312 | tf_op jit(solution)/shard_map/ppermute | solution.py:288
  27.7 3.7 %collective-permute-done.10.refs_4_ = bf16[4,128,512]{2,1,0:T(8,128)(2,1)S(1)} collective-permute-done((bf16[4,128,512]{2,1,0:T(8,128)(2,1)S(1)}, bf16[4,128,512]{2,1,0:T(8,128)(2,1)S(1)}, u32[]{:S(2)}, u32[]{:S(2)}) %collective-permute-start.10) | collective-permute-done | bytes 524320 | tf_op jit(solution)/shard_map/ppermute | solution.py:288
  31.5 1.1 %collective-permute-done.4.refs_3_ = bf16[2,128,512]{2,1,0:T(8,128)(2,1)S(1)} collective-permute-done((bf16[2,128,512]{2,1,0:T(8,128)(2,1)S(1)}, bf16[2,128,512]{2,1,0:T(8,128)(2,1)S(1)}, u32[]{:S(2)}, u32[]{:S(2)}) %collective-permute-start.4) | collective-permute-done | bytes 262176 | tf_op jit(solution)/shard_map/ppermute | solution.py:288
  32.6 1.4 %collective-permute-start.6 = (bf16[4,128,512]{2,1,0:T(8,128)(2,1)S(1)}, bf16[4,128,512]{2,1,0:T(8,128)(2,1)S(1)}, u32[]{:S(2)}, u32[]{:S(2)}) collective-permute-start(bf16[4,128,512]{2,1,0:T(8,128)(2,1)S(1)} %pad_maximum_fusion), channel_id=1, source_target_pairs={{0,4},{1,3},{2,6},{3,1},{4,0},{5,7},{6,2},{7,5},{8,12},{9,11},{10,... | collective-permute-start | bytes 1572872 | tf_op jit(solution)/shard_map/ppermute | solution.py:288
  34.1 0.5 collective-permute-start.7
  34.7 0.9 %collective-permute-done.12.refs_6_ = bf16[2,128,512]{2,1,0:T(8,128)(2,1)S(1)} collective-permute-done((bf16[2,128,512]{2,1,0:T(8,128)(2,1)S(1)}, bf16[2,128,512]{2,1,0:T(8,128)(2,1)S(1)}, u32[]{:S(2)}, u32[]{:S(2)}) %collective-permute-start.12) | collective-permute-done | bytes 262176 | tf_op jit(solution)/shard_map/ppermute | solution.py:285
  35.6 0.5 collective-permute-start.15
  36.2 2.0 %shard_map.71 = (f32[128,512]{1,0:T(8,128)S(1)}, f32[128,128]{1,0:T(8,128)S(1)}) custom-call(s32[9]{0:T(128)S(1)} %stack.42.where.refs_0_, f32[1,16384]{1,0:T(1,128)S(1)} %get-tuple-element.60.refs_1_, bf16[2,128,512]{2,1,0:T(8,128)(2,1)S(1)} %pad_maximum_fusion.3.refs_2_, bf16[2,128,512]{2,1,0:T(8,128)(2,1)S(1)} %collective-permute-done.9.refs_3_, ...), custom_call_target="tpu_custom_call" | custom-call | flops 1073741824 | bytes 8388608 | tf_op jit(solution)/shard_map/pallas_call | solution.py:198
  38.2 1.3 %shard_map.72 = (f32[128,512]{1,0:T(8,128)S(1)}, f32[128,128]{1,0:T(8,128)S(1)}) custom-call(s32[9]{0:T(128)S(1)} %stack.42.where.refs_0_, f32[1,16384]{1,0:T(1,128)S(1)} %get-tuple-element.60.refs_1_, bf16[2,128,512]{2,1,0:T(8,128)(2,1)S(1)} %slice.113.refs_2_, bf16[2,128,512]{2,1,0:T(8,128)(2,1)S(1)} %collective-permute-done.4.refs_3_, ...), custom_call_target="tpu_custom_call" | custom-call | flops 536870912 | bytes 4194304 | tf_op jit(solution)/shard_map/pallas_call | solution.py:198
  39.5 2.4 %collective-permute-done.6.refs_2_ = bf16[4,128,512]{2,1,0:T(8,128)(2,1)S(1)} collective-permute-done((bf16[4,128,512]{2,1,0:T(8,128)(2,1)S(1)}, bf16[4,128,512]{2,1,0:T(8,128)(2,1)S(1)}, u32[]{:S(2)}, u32[]{:S(2)}) %collective-permute-start.6) | collective-permute-done | bytes 524320 | tf_op jit(solution)/shard_map/ppermute | solution.py:288
  41.9 0.3 fusion.4
  42.2 0.6 collective-permute-start.16
  42.8 1.0 %shard_map.73 = (f32[128,512]{1,0:T(8,128)S(1)}, f32[128,128]{1,0:T(8,128)S(1)}) custom-call(s32[9]{0:T(128)S(1)} %stack.42.where.refs_0_, f32[1,16384]{1,0:T(1,128)S(1)} %get-tuple-element.60.refs_1_, bf16[4,128,512]{2,1,0:T(8,128)(2,1)S(1)} %collective-permute-done.6.refs_2_, bf16[16384,512]{1,0:T(8,128)(2,1)S(1)} %bitcast.17, ...), custom_call_target="tpu_custom_call" | custom-call | flops 268435456 | bytes 2097152 | tf_op jit(solution)/shard_map/pallas_call | solution.py:198
  43.9 1.6 %shard_map.74.attended = bf16[128,512]{1,0:T(8,128)(2,1)S(1)} custom-call(s32[9]{0:T(128)S(1)} %stack.42.where.refs_0_, f32[1,16384]{1,0:T(1,128)S(1)} %get-tuple-element.60.refs_1_, bf16[4,128,512]{2,1,0:T(8,128)(2,1)S(1)} %collective-permute-done.14.refs_2_, bf16[16384,512]{1,0:T(8,128)(2,1)S(1)} %bitcast.17, f32[128,512]{1,0:T(8,128)S(1)} %get-tuple-element.74.refs_4_, ...), custom_call_target="tpu_custom_call" | custom-call | flops 268435456 | bytes 2097152 | tf_op jit(solution)/shard_map/pallas_call | solution.py:198
  45.5 0.4 shard_map.75
  46.1 0.7 shard_map.76
  46.8 1.1 %collective-permute-done.17 = bf16[4,128,512]{2,1,0:T(8,128)(2,1)S(1)} collective-permute-done((bf16[4,128,512]{2,1,0:T(8,128)(2,1)S(1)}, bf16[4,128,512]{2,1,0:T(8,128)(2,1)S(1)}, u32[]{:S(2)}, u32[]{:S(2)}) %collective-permute-start.17) | collective-permute-done | bytes 524320 | tf_op jit(solution)/shard_map/ppermute | solution.py:285
  48.1 0.6 collective-permute-start.20
  48.7 0.4 shard_map.77
  49.1 3.5 %shard_map.78 = (bf16[4,128,512]{2,1,0:T(8,128)(2,1)S(1)}, bf16[2,128,512]{2,1,0:T(8,128)(2,1)S(1)}, bf16[2,128,512]{2,1,0:T(8,128)(2,1)S(1)}) custom-call(s32[9]{0:T(128)S(1)} %stack.42.where.refs_0_, bf16[128,512]{1,0:T(8,128)(2,1)S(1)} %shard_map.74.attended, bf16[512,16384]{1,0:T(8,128)(2,1)} %weight.3), custom_call_target="tpu_custom_call" | custom-call | flops 536870912 | bytes 4194304 | tf_op jit(solution)/shard_map/pallas_call | solution.py:252
  52.6 0.8 collective-permute-start.21
  53.5 0.4 collective-permute-start.27
  53.9 3.5 %shard_map.79 = (f32[4,128,512]{2,1,0:T(8,128)S(1)}, f32[2,128,512]{2,1,0:T(8,128)S(1)}, f32[2,128,512]{2,1,0:T(8,128)S(1)}) custom-call(s32[9]{0:T(128)S(1)} %stack.42.where.refs_0_, bf16[128,512]{1,0:T(8,128)(2,1)S(1)} %shard_map.74.attended, bf16[512,16384]{1,0:T(8,128)(2,1)} %weight.3), custom_call_target="tpu_custom_call" | custom-call | flops 536870912 | bytes 4194304 | tf_op jit(solution)/shard_map/pallas_call | solution.py:252
  57.6 1.2 %collective-permute-start.28 = (bf16[2,128,512]{2,1,0:T(8,128)(2,1)S(1)}, bf16[2,128,512]{2,1,0:T(8,128)(2,1)S(1)}, u32[]{:S(2)}, u32[]{:S(2)}) collective-permute-start(bf16[2,128,512]{2,1,0:T(8,128)(2,1)S(1)} %add_convert_fusion.3), channel_id=1, source_target_pairs={{0,4},{1,3},{2,6},{3,1},{4,0},{5,7},{6,2},{7,5},{8,12},{9,11},{10,... | collective-permute-start | bytes 786440 | tf_op jit(solution)/shard_map/ppermute | solution.py:288
  59.0 1.1 %collective-permute-start.22 = (bf16[4,128,512]{2,1,0:T(8,128)(2,1)S(1)}, bf16[4,128,512]{2,1,0:T(8,128)(2,1)S(1)}, u32[]{:S(2)}, u32[]{:S(2)}) collective-permute-start(bf16[4,128,512]{2,1,0:T(8,128)(2,1)S(1)} %add_convert_fusion), channel_id=1, source_target_pairs={{0,2},{1,5},{2,0},{3,7},{4,6},{5,1},{6,4},{7,3},{8,10},{9,13},{10,... | collective-permute-start | bytes 1572872 | tf_op jit(solution)/shard_map/ppermute | solution.py:288
  60.2 0.5 collective-permute-start.18
  60.7 5.9 %collective-permute-done.28 = bf16[2,128,512]{2,1,0:T(8,128)(2,1)S(1)} collective-permute-done((bf16[2,128,512]{2,1,0:T(8,128)(2,1)S(1)}, bf16[2,128,512]{2,1,0:T(8,128)(2,1)S(1)}, u32[]{:S(2)}, u32[]{:S(2)}) %collective-permute-start.28) | collective-permute-done | bytes 262176 | tf_op jit(solution)/shard_map/ppermute | solution.py:288
  66.7 1.1 %collective-permute-start.29 = (bf16[1,128,512]{2,1,0:T(8,128)(2,1)S(1)}, bf16[1,128,512]{2,1,0:T(8,128)(2,1)S(1)}, u32[]{:S(2)}, u32[]{:S(2)}) collective-permute-start(bf16[1,128,512]{2,1,0:T(8,128)(2,1)S(1)} %slice.150), channel_id=1, source_target_pairs={{0,8},{1,17},{2,10},{3,19},{4,12},{5,21},{6,14},{7,23},{8,0},{9,25... | collective-permute-start | bytes 393224 | tf_op jit(solution)/shard_map/ppermute | solution.py:288
  67.9 0.9 %collective-permute-done.22 = bf16[4,128,512]{2,1,0:T(8,128)(2,1)S(1)} collective-permute-done((bf16[4,128,512]{2,1,0:T(8,128)(2,1)S(1)}, bf16[4,128,512]{2,1,0:T(8,128)(2,1)S(1)}, u32[]{:S(2)}, u32[]{:S(2)}) %collective-permute-start.22) | collective-permute-done | bytes 524320 | tf_op jit(solution)/shard_map/ppermute | solution.py:288
  68.9 1.2 %collective-permute-start.25 = (bf16[1,128,512]{2,1,0:T(8,128)(2,1)S(1)}, bf16[1,128,512]{2,1,0:T(8,128)(2,1)S(1)}, u32[]{:S(2)}, u32[]{:S(2)}) collective-permute-start(bf16[1,128,512]{2,1,0:T(8,128)(2,1)S(1)} %get-tuple-element.96), channel_id=1, source_target_pairs={{0,4},{1,3},{2,6},{3,1},{4,0},{5,7},{6,2},{7,5},{8,12},{9,11},{10,... | collective-permute-start | bytes 393224 | tf_op jit(solution)/shard_map/ppermute | solution.py:288
  70.1 2.0 %collective-permute-done.29 = bf16[1,128,512]{2,1,0:T(8,128)(2,1)S(1)} collective-permute-done((bf16[1,128,512]{2,1,0:T(8,128)(2,1)S(1)}, bf16[1,128,512]{2,1,0:T(8,128)(2,1)S(1)}, u32[]{:S(2)}, u32[]{:S(2)}) %collective-permute-start.29) | collective-permute-done | bytes 131104 | tf_op jit(solution)/shard_map/ppermute | solution.py:288
  72.2 2.1 %collective-permute-start.30 = (bf16[1,128,512]{2,1,0:T(8,128)(2,1)S(1)}, bf16[1,128,512]{2,1,0:T(8,128)(2,1)S(1)}, u32[]{:S(2)}, u32[]{:S(2)}) collective-permute-start(bf16[1,128,512]{2,1,0:T(8,128)(2,1)S(1)} %fusion), channel_id=1, source_target_pairs={{0,16},{1,9},{2,18},{3,11},{4,20},{5,13},{6,22},{7,15},{8,24},{9,1... | collective-permute-start | bytes 393224 | tf_op jit(solution)/shard_map/ppermute | solution.py:288
  74.3 1.1 %collective-permute-start.24 = (bf16[1,128,512]{2,1,0:T(8,128)(2,1)S(1)}, bf16[1,128,512]{2,1,0:T(8,128)(2,1)S(1)}, u32[]{:S(2)}, u32[]{:S(2)}) collective-permute-start(bf16[1,128,512]{2,1,0:T(8,128)(2,1)S(1)} %get-tuple-element.95), channel_id=1, source_target_pairs={{0,4},{1,3},{2,6},{3,1},{4,0},{5,7},{6,2},{7,5},{8,12},{9,11},{10,... | collective-permute-start | bytes 393224 | tf_op jit(solution)/shard_map/ppermute | solution.py:288
  75.4 2.1 %collective-permute-start.26 = (bf16[1,128,512]{2,1,0:T(8,128)(2,1)S(1)}, bf16[1,128,512]{2,1,0:T(8,128)(2,1)S(1)}, u32[]{:S(2)}, u32[]{:S(2)}) collective-permute-start(bf16[1,128,512]{2,1,0:T(8,128)(2,1)S(1)} %add_convert_fusion.5), channel_id=1, source_target_pairs={{0,8},{1,17},{2,10},{3,19},{4,12},{5,21},{6,14},{7,23},{8,0},{9,25... | collective-permute-start | bytes 393224 | tf_op jit(solution)/shard_map/ppermute | solution.py:288
  77.5 4.2 %collective-permute-done.30 = bf16[1,128,512]{2,1,0:T(8,128)(2,1)S(1)} collective-permute-done((bf16[1,128,512]{2,1,0:T(8,128)(2,1)S(1)}, bf16[1,128,512]{2,1,0:T(8,128)(2,1)S(1)}, u32[]{:S(2)}, u32[]{:S(2)}) %collective-permute-start.30) | collective-permute-done | bytes 131104 | tf_op jit(solution)/shard_map/ppermute | solution.py:288
  81.7 0.9 %collective-permute-done.26 = bf16[1,128,512]{2,1,0:T(8,128)(2,1)S(1)} collective-permute-done((bf16[1,128,512]{2,1,0:T(8,128)(2,1)S(1)}, bf16[1,128,512]{2,1,0:T(8,128)(2,1)S(1)}, u32[]{:S(2)}, u32[]{:S(2)}) %collective-permute-start.26) | collective-permute-done | bytes 131104 | tf_op jit(solution)/shard_map/ppermute | solution.py:288
  82.6 0.8 fusion.1
  (62 shorter events, 1.8 us)
Async XLA Ops:
  2.8 33.4 %slice-start = ((s8[16777216]{0:T(1024)(128)(4,1)}), s8[4194304]{0:T(1024)(128)(4,1)S(1)}, s32[]{:S(2)}) async-start(s8[16777216]{0:T(1024)(128)(4,1)} %bitcast.16), calls=%async_computation | async-start | bytes 8388608
  2.8 3.2 %collective-permute-start.1 = (f32[8,128,128]{2,1,0:T(8,128)S(1)}, f32[8,128,128]{2,1,0:T(8,128)S(1)}, u32[]{:S(2)}, u32[]{:S(2)}) collective-permute-start(f32[8,128,128]{2,1,0:T(8,128)S(1)} %get-tuple-element.63), channel_id=1, source_target_pairs={{0,1},{1,0},{2,3},{3,2},{4,5},{5,4},{6,7},{7,6},{8,9},{9,8},{10,11... | collective-permute-start | bytes 1572872 | tf_op jit(solution)/shard_map/ppermute | solution.py:285
  3.3 9.5 %collective-permute-start = (bf16[1,128,512]{2,1,0:T(8,128)(2,1)S(1)}, bf16[1,128,512]{2,1,0:T(8,128)(2,1)S(1)}, u32[]{:S(2)}, u32[]{:S(2)}) collective-permute-start(bf16[1,128,512]{2,1,0:T(8,128)(2,1)S(1)} %bitcast.18), channel_id=1, source_target_pairs={{0,8},{1,17},{2,10},{3,19},{4,12},{5,21},{6,14},{7,23},{8,0},{9,25... | collective-permute-start | bytes 393224 | tf_op jit(solution)/shard_map/ppermute | solution.py:288
  6.1 30.1 %slice-start.1 = ((s8[16777216]{0:T(1024)(128)(4,1)}), s8[4194304]{0:T(1024)(128)(4,1)S(1)}, s32[]{:S(2)}) async-start(s8[16777216]{0:T(1024)(128)(4,1)} %bitcast.16), calls=%async_computation.1 | async-start | bytes 8388608
  6.1 30.1 %slice-start.2 = ((s8[16777216]{0:T(1024)(128)(4,1)}), s8[4194304]{0:T(1024)(128)(4,1)S(1)}, s32[]{:S(2)}) async-start(s8[16777216]{0:T(1024)(128)(4,1)} %bitcast.16), calls=%async_computation.2 | async-start | bytes 8388608
  6.1 30.1 %slice-start.3 = ((s8[16777216]{0:T(1024)(128)(4,1)}), s8[4194304]{0:T(1024)(128)(4,1)S(1)}, s32[]{:S(2)}) async-start(s8[16777216]{0:T(1024)(128)(4,1)} %bitcast.16), calls=%async_computation.3 | async-start | bytes 8388608
  6.1 6.8 %collective-permute-start.2 = (bf16[4,128,128]{2,1,0:T(8,128)(2,1)S(1)}, bf16[4,128,128]{2,1,0:T(8,128)(2,1)S(1)}, u32[]{:S(2)}, u32[]{:S(2)}) collective-permute-start(bf16[4,128,128]{2,1,0:T(8,128)(2,1)S(1)} %slice.151), channel_id=1, source_target_pairs={{0,4},{1,5},{2,6},{3,7},{4,0},{5,1},{6,2},{7,3},{8,12},{9,13},{10,... | collective-permute-start | bytes 393224 | tf_op jit(solution)/shard_map/ppermute | solution.py:285
  12.9 6.4 %collective-permute-start.9 = (bf16[2,128,512]{2,1,0:T(8,128)(2,1)S(1)}, bf16[2,128,512]{2,1,0:T(8,128)(2,1)S(1)}, u32[]{:S(2)}, u32[]{:S(2)}) collective-permute-start(bf16[2,128,512]{2,1,0:T(8,128)(2,1)S(1)} %pad_maximum_fusion.3.refs_2_), channel_id=1, source_target_pairs={{0,2},{1,5},{2,0},{3,7},{4,6},{5,1},{6,4},{7,3},{8,10},{9,13},{10,... | collective-permute-start | bytes 786440 | tf_op jit(solution)/shard_map/ppermute | solution.py:288
  14.5 11.6 %collective-permute-start.3 = (bf16[2,128,640]{2,1,0:T(8,128)(2,1)S(1)}, bf16[2,128,640]{2,1,0:T(8,128)(2,1)S(1)}, u32[]{:S(2)}, u32[]{:S(2)}) collective-permute-start(bf16[2,128,640]{2,1,0:T(8,128)(2,1)S(1)} %pad_maximum_fusion.2), channel_id=1, source_target_pairs={{0,16},{1,9},{2,18},{3,11},{4,20},{5,13},{6,22},{7,15},{8,24},{9,1... | collective-permute-start | bytes 983048 | tf_op jit(solution)/shard_map/ppermute | solution.py:288
  19.4 12.1 %collective-permute-start.10 = (bf16[4,128,512]{2,1,0:T(8,128)(2,1)S(1)}, bf16[4,128,512]{2,1,0:T(8,128)(2,1)S(1)}, u32[]{:S(2)}, u32[]{:S(2)}) collective-permute-start(bf16[4,128,512]{2,1,0:T(8,128)(2,1)S(1)} %pad_maximum_fusion.1), channel_id=1, source_target_pairs={{0,4},{1,3},{2,6},{3,1},{4,0},{5,7},{6,2},{7,5},{8,12},{9,11},{10,... | collective-permute-start | bytes 1572872 | tf_op jit(solution)/shard_map/ppermute | solution.py:288
  26.1 6.4 %collective-permute-start.4 = (bf16[2,128,512]{2,1,0:T(8,128)(2,1)S(1)}, bf16[2,128,512]{2,1,0:T(8,128)(2,1)S(1)}, u32[]{:S(2)}, u32[]{:S(2)}) collective-permute-start(bf16[2,128,512]{2,1,0:T(8,128)(2,1)S(1)} %slice.113.refs_2_), channel_id=1, source_target_pairs={{0,2},{1,5},{2,0},{3,7},{4,6},{5,1},{6,4},{7,3},{8,10},{9,13},{10,... | collective-permute-start | bytes 786440 | tf_op jit(solution)/shard_map/ppermute | solution.py:288
  26.8 4.7 %collective-permute-start.5 = (bf16[1,128,128]{2,1,0:T(8,128)(2,1)S(1)}, bf16[1,128,128]{2,1,0:T(8,128)(2,1)S(1)}, u32[]{:S(2)}, u32[]{:S(2)}) collective-permute-start(bf16[1,128,128]{2,1,0:T(8,128)(2,1)S(1)} %slice.153), channel_id=1, source_target_pairs={{0,8},{1,17},{2,10},{3,19},{4,12},{5,21},{6,14},{7,23},{8,0},{9,25... | collective-permute-start | bytes 98312 | tf_op jit(solution)/shard_map/ppermute | solution.py:288
  27.7 6.8 %collective-permute-start.11 = (bf16[2,128,512]{2,1,0:T(8,128)(2,1)S(1)}, bf16[2,128,512]{2,1,0:T(8,128)(2,1)S(1)}, u32[]{:S(2)}, u32[]{:S(2)}) collective-permute-start(bf16[2,128,512]{2,1,0:T(8,128)(2,1)S(1)} %pad_maximum_fusion.3.refs_2_), channel_id=1, source_target_pairs={{0,1},{1,0},{2,3},{3,2},{4,5},{5,4},{6,7},{7,6},{8,9},{9,8},{10,11... | collective-permute-start | bytes 786440 | tf_op jit(solution)/shard_map/ppermute | solution.py:285
  31.5 4.7 %collective-permute-start.13 = (bf16[4,128,512]{2,1,0:T(8,128)(2,1)S(1)}, bf16[4,128,512]{2,1,0:T(8,128)(2,1)S(1)}, u32[]{:S(2)}, u32[]{:S(2)}) collective-permute-start(bf16[4,128,512]{2,1,0:T(8,128)(2,1)S(1)} %collective-permute-done.10.refs_4_), channel_id=1, source_target_pairs={{0,1},{1,0},{2,3},{3,2},{4,5},{5,4},{6,7},{7,6},{8,9},{9,8},{10,11... | collective-permute-start | bytes 1572872 | tf_op jit(solution)/shard_map/ppermute | solution.py:285
  32.6 9.2 %collective-permute-start.6 = (bf16[4,128,512]{2,1,0:T(8,128)(2,1)S(1)}, bf16[4,128,512]{2,1,0:T(8,128)(2,1)S(1)}, u32[]{:S(2)}, u32[]{:S(2)}) collective-permute-start(bf16[4,128,512]{2,1,0:T(8,128)(2,1)S(1)} %pad_maximum_fusion), channel_id=1, source_target_pairs={{0,4},{1,3},{2,6},{3,1},{4,0},{5,7},{6,2},{7,5},{8,12},{9,11},{10,... | collective-permute-start | bytes 1572872 | tf_op jit(solution)/shard_map/ppermute | solution.py:288
  34.1 1.5 %collective-permute-start.12 = (bf16[2,128,512]{2,1,0:T(8,128)(2,1)S(1)}, bf16[2,128,512]{2,1,0:T(8,128)(2,1)S(1)}, u32[]{:S(2)}, u32[]{:S(2)}) collective-permute-start(bf16[2,128,512]{2,1,0:T(8,128)(2,1)S(1)} %collective-permute-done.9.refs_3_), channel_id=1, source_target_pairs={{0,1},{1,0},{2,3},{3,2},{4,5},{5,4},{6,7},{7,6},{8,9},{9,8},{10,11... | collective-permute-start | bytes 786440 | tf_op jit(solution)/shard_map/ppermute | solution.py:285
  34.1 4.1 %collective-permute-start.7 = (bf16[2,128,512]{2,1,0:T(8,128)(2,1)S(1)}, bf16[2,128,512]{2,1,0:T(8,128)(2,1)S(1)}, u32[]{:S(2)}, u32[]{:S(2)}) collective-permute-start(bf16[2,128,512]{2,1,0:T(8,128)(2,1)S(1)} %slice.113.refs_2_), channel_id=1, source_target_pairs={{0,1},{1,0},{2,3},{3,2},{4,5},{5,4},{6,7},{7,6},{8,9},{9,8},{10,11... | collective-permute-start | bytes 786440 | tf_op jit(solution)/shard_map/ppermute | solution.py:285
  34.6 3.6 %collective-permute-start.8 = (bf16[2,128,512]{2,1,0:T(8,128)(2,1)S(1)}, bf16[2,128,512]{2,1,0:T(8,128)(2,1)S(1)}, u32[]{:S(2)}, u32[]{:S(2)}) collective-permute-start(bf16[2,128,512]{2,1,0:T(8,128)(2,1)S(1)} %collective-permute-done.4.refs_3_), channel_id=1, source_target_pairs={{0,1},{1,0},{2,3},{3,2},{4,5},{5,4},{6,7},{7,6},{8,9},{9,8},{10,11... | collective-permute-start | bytes 786440 | tf_op jit(solution)/shard_map/ppermute | solution.py:285
  35.6 6.5 %collective-permute-start.15 = (bf16[128,128]{1,0:T(8,128)(2,1)S(1)}, bf16[128,128]{1,0:T(8,128)(2,1)S(1)}, u32[]{:S(2)}, u32[]{:S(2)}) collective-permute-start(bf16[128,128]{1,0:T(8,128)(2,1)S(1)} %bitcast_convert_fusion), channel_id=1, source_target_pairs={{0,2},{1,3},{2,0},{3,1},{4,6},{5,7},{6,4},{7,5},{8,10},{9,11},{10,... | collective-permute-start | bytes 98312 | tf_op jit(solution)/shard_map/ppermute | solution.py:285
  41.9 2.0 %collective-permute-start.14 = (bf16[4,128,512]{2,1,0:T(8,128)(2,1)S(1)}, bf16[4,128,512]{2,1,0:T(8,128)(2,1)S(1)}, u32[]{:S(2)}, u32[]{:S(2)}) collective-permute-start(bf16[4,128,512]{2,1,0:T(8,128)(2,1)S(1)} %collective-permute-done.6.refs_2_), channel_id=1, source_target_pairs={{0,1},{1,0},{2,3},{3,2},{4,5},{5,4},{6,7},{7,6},{8,9},{9,8},{10,11... | collective-permute-start | bytes 1572872 | tf_op jit(solution)/shard_map/ppermute | solution.py:285
  42.2 1.7 %collective-permute-start.16 = (f32[128,128]{1,0:T(8,128)S(1)}, f32[128,128]{1,0:T(8,128)S(1)}, u32[]{:S(2)}, u32[]{:S(2)}) collective-permute-start(f32[128,128]{1,0:T(8,128)S(1)} %bitcast_add_fusion.refs_6_), channel_id=1, source_target_pairs={{0,1},{1,0},{2,3},{3,2},{4,5},{5,4},{6,7},{7,6},{8,9},{9,8},{10,11... | collective-permute-start | bytes 196616 | tf_op jit(solution)/shard_map/ppermute | solution.py:285
  45.9 2.0 %collective-permute-start.17 = (bf16[4,128,512]{2,1,0:T(8,128)(2,1)S(1)}, bf16[4,128,512]{2,1,0:T(8,128)(2,1)S(1)}, u32[]{:S(2)}, u32[]{:S(2)}) collective-permute-start(bf16[4,128,512]{2,1,0:T(8,128)(2,1)S(1)} %shard_map.75), channel_id=1, source_target_pairs={{0,1},{1,0},{2,3},{3,2},{4,5},{5,4},{6,7},{7,6},{8,9},{9,8},{10,11... | collective-permute-start | bytes 1572872 | tf_op jit(solution)/shard_map/ppermute | solution.py:285
  48.1 9.4 %collective-permute-start.20 = (bf16[4,128,512]{2,1,0:T(8,128)(2,1)S(1)}, bf16[4,128,512]{2,1,0:T(8,128)(2,1)S(1)}, u32[]{:S(2)}, u32[]{:S(2)}) collective-permute-start(bf16[4,128,512]{2,1,0:T(8,128)(2,1)S(1)} %add_convert_fusion.1), channel_id=1, source_target_pairs={{0,2},{1,5},{2,0},{3,7},{4,6},{5,1},{6,4},{7,3},{8,10},{9,13},{10,... | collective-permute-start | bytes 1572872 | tf_op jit(solution)/shard_map/ppermute | solution.py:288
  52.6 6.2 %collective-permute-start.21 = (bf16[4,128,512]{2,1,0:T(8,128)(2,1)S(1)}, bf16[4,128,512]{2,1,0:T(8,128)(2,1)S(1)}, u32[]{:S(2)}, u32[]{:S(2)}) collective-permute-start(bf16[4,128,512]{2,1,0:T(8,128)(2,1)S(1)} %get-tuple-element.84), channel_id=1, source_target_pairs={{0,1},{1,0},{2,3},{3,2},{4,5},{5,4},{6,7},{7,6},{8,9},{9,8},{10,11... | collective-permute-start | bytes 1572872 | tf_op jit(solution)/shard_map/ppermute | solution.py:285
  53.4 4.1 %collective-permute-start.19 = (bf16[2,128,512]{2,1,0:T(8,128)(2,1)S(1)}, bf16[2,128,512]{2,1,0:T(8,128)(2,1)S(1)}, u32[]{:S(2)}, u32[]{:S(2)}) collective-permute-start(bf16[2,128,512]{2,1,0:T(8,128)(2,1)S(1)} %get-tuple-element.90), channel_id=1, source_target_pairs={{0,1},{1,0},{2,3},{3,2},{4,5},{5,4},{6,7},{7,6},{8,9},{9,8},{10,11... | collective-permute-start | bytes 786440 | tf_op jit(solution)/shard_map/ppermute | solution.py:285
  53.5 7.2 %collective-permute-start.27 = (bf16[2,128,512]{2,1,0:T(8,128)(2,1)S(1)}, bf16[2,128,512]{2,1,0:T(8,128)(2,1)S(1)}, u32[]{:S(2)}, u32[]{:S(2)}) collective-permute-start(bf16[2,128,512]{2,1,0:T(8,128)(2,1)S(1)} %get-tuple-element.82), channel_id=1, source_target_pairs={{0,1},{1,0},{2,3},{3,2},{4,5},{5,4},{6,7},{7,6},{8,9},{9,8},{10,11... | collective-permute-start | bytes 786440 | tf_op jit(solution)/shard_map/ppermute | solution.py:285
  57.6 9.0 %collective-permute-start.28 = (bf16[2,128,512]{2,1,0:T(8,128)(2,1)S(1)}, bf16[2,128,512]{2,1,0:T(8,128)(2,1)S(1)}, u32[]{:S(2)}, u32[]{:S(2)}) collective-permute-start(bf16[2,128,512]{2,1,0:T(8,128)(2,1)S(1)} %add_convert_fusion.3), channel_id=1, source_target_pairs={{0,4},{1,3},{2,6},{3,1},{4,0},{5,7},{6,2},{7,5},{8,12},{9,11},{10,... | collective-permute-start | bytes 786440 | tf_op jit(solution)/shard_map/ppermute | solution.py:288
  59.0 9.7 %collective-permute-start.22 = (bf16[4,128,512]{2,1,0:T(8,128)(2,1)S(1)}, bf16[4,128,512]{2,1,0:T(8,128)(2,1)S(1)}, u32[]{:S(2)}, u32[]{:S(2)}) collective-permute-start(bf16[4,128,512]{2,1,0:T(8,128)(2,1)S(1)} %add_convert_fusion), channel_id=1, source_target_pairs={{0,2},{1,5},{2,0},{3,7},{4,6},{5,1},{6,4},{7,3},{8,10},{9,13},{10,... | collective-permute-start | bytes 1572872 | tf_op jit(solution)/shard_map/ppermute | solution.py:288
  60.2 7.7 %collective-permute-start.23 = (bf16[2,128,512]{2,1,0:T(8,128)(2,1)S(1)}, bf16[2,128,512]{2,1,0:T(8,128)(2,1)S(1)}, u32[]{:S(2)}, u32[]{:S(2)}) collective-permute-start(bf16[2,128,512]{2,1,0:T(8,128)(2,1)S(1)} %get-tuple-element.93), channel_id=1, source_target_pairs={{0,1},{1,0},{2,3},{3,2},{4,5},{5,4},{6,7},{7,6},{8,9},{9,8},{10,11... | collective-permute-start | bytes 786440 | tf_op jit(solution)/shard_map/ppermute | solution.py:285
  60.2 15.2 %collective-permute-start.18 = (bf16[2,128,512]{2,1,0:T(8,128)(2,1)S(1)}, bf16[2,128,512]{2,1,0:T(8,128)(2,1)S(1)}, u32[]{:S(2)}, u32[]{:S(2)}) collective-permute-start(bf16[2,128,512]{2,1,0:T(8,128)(2,1)S(1)} %get-tuple-element.87), channel_id=1, source_target_pairs={{0,1},{1,0},{2,3},{3,2},{4,5},{5,4},{6,7},{7,6},{8,9},{9,8},{10,11... | collective-permute-start | bytes 786440 | tf_op jit(solution)/shard_map/ppermute | solution.py:285
  66.7 5.4 %collective-permute-start.29 = (bf16[1,128,512]{2,1,0:T(8,128)(2,1)S(1)}, bf16[1,128,512]{2,1,0:T(8,128)(2,1)S(1)}, u32[]{:S(2)}, u32[]{:S(2)}) collective-permute-start(bf16[1,128,512]{2,1,0:T(8,128)(2,1)S(1)} %slice.150), channel_id=1, source_target_pairs={{0,8},{1,17},{2,10},{3,19},{4,12},{5,21},{6,14},{7,23},{8,0},{9,25... | collective-permute-start | bytes 393224 | tf_op jit(solution)/shard_map/ppermute | solution.py:288
  68.9 6.5 %collective-permute-start.25 = (bf16[1,128,512]{2,1,0:T(8,128)(2,1)S(1)}, bf16[1,128,512]{2,1,0:T(8,128)(2,1)S(1)}, u32[]{:S(2)}, u32[]{:S(2)}) collective-permute-start(bf16[1,128,512]{2,1,0:T(8,128)(2,1)S(1)} %get-tuple-element.96), channel_id=1, source_target_pairs={{0,4},{1,3},{2,6},{3,1},{4,0},{5,7},{6,2},{7,5},{8,12},{9,11},{10,... | collective-permute-start | bytes 393224 | tf_op jit(solution)/shard_map/ppermute | solution.py:288
  72.2 9.5 %collective-permute-start.30 = (bf16[1,128,512]{2,1,0:T(8,128)(2,1)S(1)}, bf16[1,128,512]{2,1,0:T(8,128)(2,1)S(1)}, u32[]{:S(2)}, u32[]{:S(2)}) collective-permute-start(bf16[1,128,512]{2,1,0:T(8,128)(2,1)S(1)} %fusion), channel_id=1, source_target_pairs={{0,16},{1,9},{2,18},{3,11},{4,20},{5,13},{6,22},{7,15},{8,24},{9,1... | collective-permute-start | bytes 393224 | tf_op jit(solution)/shard_map/ppermute | solution.py:288
  74.3 7.4 %collective-permute-start.24 = (bf16[1,128,512]{2,1,0:T(8,128)(2,1)S(1)}, bf16[1,128,512]{2,1,0:T(8,128)(2,1)S(1)}, u32[]{:S(2)}, u32[]{:S(2)}) collective-permute-start(bf16[1,128,512]{2,1,0:T(8,128)(2,1)S(1)} %get-tuple-element.95), channel_id=1, source_target_pairs={{0,4},{1,3},{2,6},{3,1},{4,0},{5,7},{6,2},{7,5},{8,12},{9,11},{10,... | collective-permute-start | bytes 393224 | tf_op jit(solution)/shard_map/ppermute | solution.py:288
  75.4 7.1 %collective-permute-start.26 = (bf16[1,128,512]{2,1,0:T(8,128)(2,1)S(1)}, bf16[1,128,512]{2,1,0:T(8,128)(2,1)S(1)}, u32[]{:S(2)}, u32[]{:S(2)}) collective-permute-start(bf16[1,128,512]{2,1,0:T(8,128)(2,1)S(1)} %add_convert_fusion.5), channel_id=1, source_target_pairs={{0,8},{1,17},{2,10},{3,19},{4,12},{5,21},{6,14},{7,23},{8,0},{9,25... | collective-permute-start | bytes 393224 | tf_op jit(solution)/shard_map/ppermute | solution.py:288

commit v10 on v9

--- a/solution.py
+++ b/solution.py
@@ -334,29 +334,34 @@
         return kv[half:] + send(kv[:half].astype(bf16), way).astype(f32)
 
     kv = halved(kv_keep + swap(kv_send, CORE), swap, bits[shared])
-    far_blocks, far_symbols = fetched(where, wo, width, columns_of(far))
+    home, mid = near[: len(low)], near[len(low) :]
     row = jnp.stack([act] + [swap(raw, o) for o in low[1:]])
-    row = jnp.concatenate([row, along(row, 0)])
-    row, kv, far_blocks = lax.optimization_barrier((row, kv, far_blocks))
-    far_held = (far_blocks, far_symbols)
-    groups = []
-    for offsets in (near, far):
-        if offsets is far:
+    groups, kept = [], None
+    for offsets in (home, mid, far):
+        if offsets is mid:
+            kept, row, kv = lax.optimization_barrier((row, along(row, 0), kv))
+            row, kv = lax.optimization_barrier((row, kv, groups[0][1][0]))[:2]
+        elif offsets is far:
             half = kv[: kv.shape[0] // 2].astype(bf16)
+            row = jnp.concatenate([kept, row])
             k = min(row.shape[0], half.shape[0])
             extra = jnp.zeros((row.shape[0], *half.shape[1:]), bf16).at[:k].set(half[:k])
             got = along(jnp.concatenate([row, extra], axis=2), 1)
+            got = after(got, groups[1][2][0])
             row = got[:, :, :width]
             kv = kv[kv.shape[0] // 2 :] + got[:k, :, width:].astype(f32)
-            side = turn(row, 0)
+        side = turn(row, 0)
+        if offsets is far:
             kv = halved(kv, along, 0)
-            side, kv = lax.optimization_barrier((side, kv))
-        else:
-            side = turn(row, 0)
+            blocks, far_symbols = fetched(after(where, row), wo, width, columns_of(far))
+            side, kv, blocks = lax.optimization_barrier((side, kv, blocks))
+            far_held = (blocks, far_symbols)
+        elif offsets is mid:
+            side = after(side, groups[0][2][0])
         both = turn(jnp.concatenate([row, side]), 1)
         at = symbols_of(offsets)
         groups.append([(row, at[0]), (side, at[1]), (both, at[2] + at[3])])
-    early, last = groups
+    early, last = groups[0] + groups[1], groups[2]
     partners = [swap(kv[0].astype(bf16), o) for o in combos(bits[1:shared])[1:]]
 
     call = functools.partial(query_call, where, gain, weight=wq)
@@ -406,13 +411,12 @@
     pairs = paired(own, sent)
     first = added_up(after(pairs[0][0], far_two), pairs[0][1]).astype(bf16)
     near_home, near_two = round_square(first, *pairs[1:])
+    far_got = along(far_sum.astype(bf16), 1)
     k = len(low)
-    far_sum = added_up(far_sum[:k], along(far_sum[k:].astype(bf16), 0))
-    far_got = along(far_sum.astype(bf16), 1)
     got = [turn(near_two[k:], 1), turn(near_two[:k], 1)]
-    near_sum = added_up(*[x[k:] for x in near_home], got[0])
-    home_sum = added_up(*[x[:k] for x in near_home], got[1])
-    home_sum = added_up(home_sum, along(near_sum.astype(bf16), 0), far_got)
+    near_sum = added_up(*[x[k:] for x in near_home], got[0], far_got[k:])
+    home_sum = added_up(*[x[:k] for x in near_home], got[1], far_got[:k])
+    home_sum = added_up(home_sum, along(near_sum.astype(bf16), 0))
     out = added_up(home_sum[0], *[swap(home_sum[i].astype(bf16), o) for i, o in enumerate(low) if o])
     return out.astype(bf16)
 

time: 83.5 us -> 84.4 us (1.011)
  waiting for transfers between devices: 30.6 us -> 34.1 us
  starting transfers between devices: 27.9 us -> 25.3 us
    ppermute x15 -> x16, starting transfers between devices: 21.9 us -> 18.6 us  [by_core(): lax.ppermute(x, 'wide', [(i, i ^ pair[(step + (i & CORE)) % 2]) for i in...]
    ppermute x15 -> x16, waiting for transfers between devices: 28.5 us -> 30.8 us  [by_core(): lax.ppermute(x, 'wide', [(i, i ^ pair[(step + (i & CORE)) % 2]) for i in...]
    ppermute x16 -> x19, waiting for transfers between devices: 2.04 us -> 3.34 us  [swap(): return lax.ppermute(x, 'wide', [(i, i ^ offset) for i in range(n)])]
    ppermute x16 -> x19, starting transfers between devices: 6.01 us -> 6.77 us  [swap(): return lax.ppermute(x, 'wide', [(i, i ^ offset) for i in range(n)])]
  transfers between devices with their start and end apart: 31 -> 35, of which waited for: 12 -> 12; matrix products, arithmetic and copies ran while one was open for 2% -> 2% of each run, Pallas kernels for 21% -> 21%
where the time goes in v10:
time: 84.4 us; the launch traced here: 84.3 us
  waiting for transfers between devices  34.1 us (40%)
  starting transfers between devices  25.3 us (30%)
  Pallas kernels  22.1 us (26%)
  other arithmetic  2.18 us (3%)
    ppermute x16, waiting for transfers between devices, by_core(): lax.ppermute(x, 'wide', [(i, i ^ pair[(step + (i & CORE)) % 2]) for i in...  30.8 us
    ppermute x16, starting transfers between devices, by_core(): lax.ppermute(x, 'wide', [(i, i ^ pair[(step + (i & CORE)) % 2]) for i in...  18.6 us
    pallas_call x5, Pallas kernels, output_call(): pl.pallas_call(kernel, out_shape=[jax.ShapeDtypeStruct((len(s), tokens, w...  8.66 us
    ppermute x19, starting transfers between devices, swap(): return lax.ppermute(x, 'wide', [(i, i ^ offset) for i in range(n)])  6.77 us
    pallas_call x4, Pallas kernels, query_call(): pl.pallas_call(functools.partial(query_kernel, places, bool(carry), bool(...  5.85 us
    pallas_call x1, Pallas kernels, fetched(): pl.pallas_call(functools.partial(fetch_kernel, symbols, width), out_shape...  4.89 us
    ppermute x19, waiting for transfers between devices, swap(): return lax.ppermute(x, 'wide', [(i, i ^ offset) for i in range(n)])  3.34 us
    pallas_call x1, Pallas kernels, kv_terms(): pl.pallas_call(functools.partial(kv_kernel, shared), out_shape=[jax.Shape...  2.69 us
  transfers between devices with their start and end apart: 35, of which 12 were waited for; matrix products, arithmetic and copies ran while one was open for 2% of the time, Pallas kernels for 21%

profile of v10, /device:TPU:0, one launch (start us, length us, event | category | flops | bytes accessed | tf_op | source)
XLA Modules:
  0.0 84.3 jit_solution(10208662059687295406)
XLA Ops:
  0.1 2.7 %shard_map.69 = (f32[8,128,128]{2,1,0:T(8,128)S(1)}, f32[8,128,128]{2,1,0:T(8,128)S(1)}, bf16[128,512]{1,0:T(8,128)(2,1)S(1)}, f32[1,16384]{1,0:T(1,128)S(1)}) custom-call(s32[9]{0:T(128)S(1)} %stack.42.where.refs_0_, bf16[128,512]{1,0:T(8,128)(2,1)} %act.1, f32[1,16384]{1,0:T(1,128)} %bitcast.24, bf16[512,1024]{1,0:T(8,128)(2,1)} %wk.1, bf16[512,1024]{1,0:T(8,128)(2,1)} %wv.1), custom_call_target="tpu_custom_call" | custom-call | flops 4294967296 | bytes 33554432 | tf_op jit(solution)/shard_map/pallas_call | solution.py:105
  2.8 0.5 collective-permute-start.1
  3.3 2.6 %collective-permute-start.3 = (bf16[1,128,512]{2,1,0:T(8,128)(2,1)S(1)}, bf16[1,128,512]{2,1,0:T(8,128)(2,1)S(1)}, u32[]{:S(2)}, u32[]{:S(2)}) collective-permute-start(bf16[1,128,512]{2,1,0:T(8,128)(2,1)S(1)} %bitcast.18), channel_id=1, source_target_pairs={{0,2},{1,5},{2,0},{3,7},{4,6},{5,1},{6,4},{7,3},{8,10},{9,13},{10,... | collective-permute-start | bytes 393224 | tf_op jit(solution)/shard_map/ppermute | solution.py:288
  6.0 1.9 %collective-permute-start.2 = (bf16[4,128,128]{2,1,0:T(8,128)(2,1)S(1)}, bf16[4,128,128]{2,1,0:T(8,128)(2,1)S(1)}, u32[]{:S(2)}, u32[]{:S(2)}) collective-permute-start(bf16[4,128,128]{2,1,0:T(8,128)(2,1)S(1)} %slice.145), channel_id=1, source_target_pairs={{0,4},{1,5},{2,6},{3,7},{4,0},{5,1},{6,2},{7,3},{8,12},{9,13},{10,... | collective-permute-start | bytes 393224 | tf_op jit(solution)/shard_map/ppermute | solution.py:285
  7.9 1.6 %collective-permute-start = (bf16[1,128,512]{2,1,0:T(8,128)(2,1)S(1)}, bf16[1,128,512]{2,1,0:T(8,128)(2,1)S(1)}, u32[]{:S(2)}, u32[]{:S(2)}) collective-permute-start(bf16[1,128,512]{2,1,0:T(8,128)(2,1)S(1)} %bitcast.19), channel_id=1, source_target_pairs={{0,8},{1,17},{2,10},{3,19},{4,12},{5,21},{6,14},{7,23},{8,0},{9,25... | collective-permute-start | bytes 393224 | tf_op jit(solution)/shard_map/ppermute | solution.py:288
  9.5 1.5 %collective-permute-start.6 = (bf16[2,128,512]{2,1,0:T(8,128)(2,1)S(1)}, bf16[2,128,512]{2,1,0:T(8,128)(2,1)S(1)}, u32[]{:S(2)}, u32[]{:S(2)}) collective-permute-start(bf16[2,128,512]{2,1,0:T(8,128)(2,1)S(1)} %pad_maximum_fusion.2), channel_id=1, source_target_pairs={{0,4},{1,3},{2,6},{3,1},{4,0},{5,7},{6,2},{7,5},{8,12},{9,11},{10,... | collective-permute-start | bytes 786440 | tf_op jit(solution)/shard_map/ppermute | solution.py:288
  11.0 0.7 collective-permute-done.2
  11.7 2.2 %collective-permute-done.refs_5_ = bf16[1,128,512]{2,1,0:T(8,128)(2,1)S(1)} collective-permute-done((bf16[1,128,512]{2,1,0:T(8,128)(2,1)S(1)}, bf16[1,128,512]{2,1,0:T(8,128)(2,1)S(1)}, u32[]{:S(2)}, u32[]{:S(2)}) %collective-permute-start) | collective-permute-done | bytes 131104 | tf_op jit(solution)/shard_map/ppermute | solution.py:288
  13.9 1.5 %collective-permute-start.5 = (bf16[1,128,512]{2,1,0:T(8,128)(2,1)S(1)}, bf16[1,128,512]{2,1,0:T(8,128)(2,1)S(1)}, u32[]{:S(2)}, u32[]{:S(2)}) collective-permute-start(bf16[1,128,512]{2,1,0:T(8,128)(2,1)S(1)} %collective-permute-done.refs_5_), channel_id=1, source_target_pairs={{0,2},{1,5},{2,0},{3,7},{4,6},{5,1},{6,4},{7,3},{8,10},{9,13},{10,... | collective-permute-start | bytes 393224 | tf_op jit(solution)/shard_map/ppermute | solution.py:288
  15.4 1.9 %collective-permute-start.4 = (bf16[2,128,640]{2,1,0:T(8,128)(2,1)S(1)}, bf16[2,128,640]{2,1,0:T(8,128)(2,1)S(1)}, u32[]{:S(2)}, u32[]{:S(2)}) collective-permute-start(bf16[2,128,640]{2,1,0:T(8,128)(2,1)S(1)} %pad_maximum_fusion.1), channel_id=1, source_target_pairs={{0,16},{1,9},{2,18},{3,11},{4,20},{5,13},{6,22},{7,15},{8,24},{9,1... | collective-permute-start | bytes 983048 | tf_op jit(solution)/shard_map/ppermute | solution.py:288
  17.4 1.5 %collective-permute-done.5.refs_6_ = bf16[1,128,512]{2,1,0:T(8,128)(2,1)S(1)} collective-permute-done((bf16[1,128,512]{2,1,0:T(8,128)(2,1)S(1)}, bf16[1,128,512]{2,1,0:T(8,128)(2,1)S(1)}, u32[]{:S(2)}, u32[]{:S(2)}) %collective-permute-start.5) | collective-permute-done | bytes 131104 | tf_op jit(solution)/shard_map/ppermute | solution.py:288
  18.9 0.3 collective-permute-start.7
  19.2 7.8 %collective-permute-done.4 = bf16[2,128,640]{2,1,0:T(8,128)(2,1)S(1)} collective-permute-done((bf16[2,128,640]{2,1,0:T(8,128)(2,1)S(1)}, bf16[2,128,640]{2,1,0:T(8,128)(2,1)S(1)}, u32[]{:S(2)}, u32[]{:S(2)}) %collective-permute-start.4) | collective-permute-done | bytes 327712 | tf_op jit(solution)/shard_map/ppermute | solution.py:288
  27.1 0.6 collective-permute-start.8
  27.7 1.3 %collective-permute-start.9 = (bf16[1,128,128]{2,1,0:T(8,128)(2,1)S(1)}, bf16[1,128,128]{2,1,0:T(8,128)(2,1)S(1)}, u32[]{:S(2)}, u32[]{:S(2)}) collective-permute-start(bf16[1,128,128]{2,1,0:T(8,128)(2,1)S(1)} %slice.147), channel_id=1, source_target_pairs={{0,8},{1,17},{2,10},{3,19},{4,12},{5,21},{6,14},{7,23},{8,0},{9,25... | collective-permute-start | bytes 98312 | tf_op jit(solution)/shard_map/ppermute | solution.py:288
  29.0 0.5 collective-permute-start.15
  29.5 4.9 %shard_map.70.weight = bf16[16,512,512]{2,1,0:T(8,128)(2,1)S(1)} custom-call(s32[9]{0:T(128)S(1)} %stack.42.where.refs_0_, bf16[512,16384]{1,0:T(8,128)(2,1)} %weight.3), custom_call_target="tpu_custom_call" | custom-call | bytes 16777216 | tf_op jit(solution)/shard_map/pallas_call | solution.py:67
  34.5 0.6 collective-permute-start.10
  35.1 0.5 collective-permute-start.16
  35.6 0.8 collective-permute-done.14.refs_9_
  36.6 0.4 collective-permute-start.11
  37.1 0.7 collective-permute-done.17.refs_12_
  37.8 0.7 collective-permute-start.20
  38.5 2.0 %shard_map.71 = (f32[128,512]{1,0:T(8,128)S(1)}, f32[128,128]{1,0:T(8,128)S(1)}) custom-call(s32[9]{0:T(128)S(1)} %stack.42.where.refs_0_, f32[1,16384]{1,0:T(1,128)S(1)} %get-tuple-element.66.refs_1_, bf16[1,128,512]{2,1,0:T(8,128)(2,1)S(1)} %bitcast.23, bf16[1,128,512]{2,1,0:T(8,128)(2,1)S(1)} %collective-permute-done.3.refs_3_, ...), custom_call_target="tpu_custom_call" | custom-call | flops 1073741824 | bytes 8388608 | tf_op jit(solution)/shard_map/pallas_call | solution.py:198
  40.5 1.3 %shard_map.72 = (f32[128,512]{1,0:T(8,128)S(1)}, f32[128,128]{1,0:T(8,128)S(1)}) custom-call(s32[9]{0:T(128)S(1)} %stack.42.where.refs_0_, f32[1,16384]{1,0:T(1,128)S(1)} %get-tuple-element.66.refs_1_, bf16[2,128,512]{2,1,0:T(8,128)(2,1)S(1)} %slice.91.refs_2_, bf16[2,128,512]{2,1,0:T(8,128)(2,1)S(1)} %collective-permute-done.8.refs_3_, ...), custom_call_target="tpu_custom_call" | custom-call | flops 536870912 | bytes 4194304 | tf_op jit(solution)/shard_map/pallas_call | solution.py:198
  41.8 1.9 %collective-permute-done.10.refs_2_ = bf16[4,128,512]{2,1,0:T(8,128)(2,1)S(1)} collective-permute-done((bf16[4,128,512]{2,1,0:T(8,128)(2,1)S(1)}, bf16[4,128,512]{2,1,0:T(8,128)(2,1)S(1)}, u32[]{:S(2)}, u32[]{:S(2)}) %collective-permute-start.10) | collective-permute-done | bytes 524320 | tf_op jit(solution)/shard_map/ppermute | solution.py:288
  44.0 0.6 collective-permute-start.21
  44.7 1.0 %shard_map.73 = (f32[128,512]{1,0:T(8,128)S(1)}, f32[128,128]{1,0:T(8,128)S(1)}) custom-call(s32[9]{0:T(128)S(1)} %stack.42.where.refs_0_, f32[1,16384]{1,0:T(1,128)S(1)} %get-tuple-element.66.refs_1_, bf16[4,128,512]{2,1,0:T(8,128)(2,1)S(1)} %collective-permute-done.10.refs_2_, bf16[16384,512]{1,0:T(8,128)(2,1)S(1)} %bitcast.17, ...), custom_call_target="tpu_custom_call" | custom-call | flops 268435456 | bytes 2097152 | tf_op jit(solution)/shard_map/pallas_call | solution.py:198
  45.8 1.6 %shard_map.74.attended = bf16[128,512]{1,0:T(8,128)(2,1)S(1)} custom-call(s32[9]{0:T(128)S(1)} %stack.42.where.refs_0_, f32[1,16384]{1,0:T(1,128)S(1)} %get-tuple-element.66.refs_1_, bf16[4,128,512]{2,1,0:T(8,128)(2,1)S(1)} %collective-permute-done.19.refs_2_, bf16[16384,512]{1,0:T(8,128)(2,1)S(1)} %bitcast.17, f32[128,512]{1,0:T(8,128)S(1)} %get-tuple-element.86.refs_4_, ...), custom_call_target="tpu_custom_call" | custom-call | flops 268435456 | bytes 2097152 | tf_op jit(solution)/shard_map/pallas_call | solution.py:198
  47.3 0.4 shard_map.75
  48.0 0.7 shard_map.76
  48.7 1.1 %collective-permute-done.22 = bf16[4,128,512]{2,1,0:T(8,128)(2,1)S(1)} collective-permute-done((bf16[4,128,512]{2,1,0:T(8,128)(2,1)S(1)}, bf16[4,128,512]{2,1,0:T(8,128)(2,1)S(1)}, u32[]{:S(2)}, u32[]{:S(2)}) %collective-permute-start.22) | collective-permute-done | bytes 524320 | tf_op jit(solution)/shard_map/ppermute | solution.py:285
  49.9 0.5 collective-permute-start.25
  50.4 0.4 shard_map.77
  50.9 3.5 %shard_map.78 = (bf16[4,128,512]{2,1,0:T(8,128)(2,1)S(1)}, bf16[2,128,512]{2,1,0:T(8,128)(2,1)S(1)}, bf16[2,128,512]{2,1,0:T(8,128)(2,1)S(1)}) custom-call(s32[9]{0:T(128)S(1)} %stack.42.where.refs_0_, bf16[128,512]{1,0:T(8,128)(2,1)S(1)} %shard_map.74.attended, bf16[512,16384]{1,0:T(8,128)(2,1)} %weight.3), custom_call_target="tpu_custom_call" | custom-call | flops 536870912 | bytes 4194304 | tf_op jit(solution)/shard_map/pallas_call | solution.py:252
  54.5 0.5 collective-permute-start.24
  55.1 3.5 %shard_map.79 = (f32[4,128,512]{2,1,0:T(8,128)S(1)}, f32[2,128,512]{2,1,0:T(8,128)S(1)}, f32[2,128,512]{2,1,0:T(8,128)S(1)}) custom-call(s32[9]{0:T(128)S(1)} %stack.42.where.refs_0_, bf16[128,512]{1,0:T(8,128)(2,1)S(1)} %shard_map.74.attended, bf16[512,16384]{1,0:T(8,128)(2,1)} %weight.3), custom_call_target="tpu_custom_call" | custom-call | flops 536870912 | bytes 4194304 | tf_op jit(solution)/shard_map/pallas_call | solution.py:252
  58.6 0.6 collective-permute-done.25
  59.3 0.9 %collective-permute-start.31 = (bf16[2,128,512]{2,1,0:T(8,128)(2,1)S(1)}, bf16[2,128,512]{2,1,0:T(8,128)(2,1)S(1)}, u32[]{:S(2)}, u32[]{:S(2)}) collective-permute-start(bf16[2,128,512]{2,1,0:T(8,128)(2,1)S(1)} %add_convert_fusion.4), channel_id=1, source_target_pairs={{0,4},{1,3},{2,6},{3,1},{4,0},{5,7},{6,2},{7,5},{8,12},{9,11},{10,... | collective-permute-start | bytes 786440 | tf_op jit(solution)/shard_map/ppermute | solution.py:288
  60.4 0.8 collective-permute-start.27
  61.2 0.5 collective-permute-start.28
  61.7 6.3 %collective-permute-done.31 = bf16[2,128,512]{2,1,0:T(8,128)(2,1)S(1)} collective-permute-done((bf16[2,128,512]{2,1,0:T(8,128)(2,1)S(1)}, bf16[2,128,512]{2,1,0:T(8,128)(2,1)S(1)}, u32[]{:S(2)}, u32[]{:S(2)}) %collective-permute-start.31) | collective-permute-done | bytes 262176 | tf_op jit(solution)/shard_map/ppermute | solution.py:288
  68.2 2.4 %collective-permute-start.32 = (bf16[2,128,512]{2,1,0:T(8,128)(2,1)S(1)}, bf16[2,128,512]{2,1,0:T(8,128)(2,1)S(1)}, u32[]{:S(2)}, u32[]{:S(2)}) collective-permute-start(bf16[2,128,512]{2,1,0:T(8,128)(2,1)S(1)} %add_convert_fusion.2), channel_id=1, source_target_pairs={{0,16},{1,9},{2,18},{3,11},{4,20},{5,13},{6,22},{7,15},{8,24},{9,1... | collective-permute-start | bytes 786440 | tf_op jit(solution)/shard_map/ppermute | solution.py:288
  70.7 1.0 %collective-permute-start.33 = (bf16[1,128,512]{2,1,0:T(8,128)(2,1)S(1)}, bf16[1,128,512]{2,1,0:T(8,128)(2,1)S(1)}, u32[]{:S(2)}, u32[]{:S(2)}) collective-permute-start(bf16[1,128,512]{2,1,0:T(8,128)(2,1)S(1)} %get-tuple-element.108), channel_id=1, source_target_pairs={{0,4},{1,3},{2,6},{3,1},{4,0},{5,7},{6,2},{7,5},{8,12},{9,11},{10,... | collective-permute-start | bytes 393224 | tf_op jit(solution)/shard_map/ppermute | solution.py:288
  71.8 1.1 %collective-permute-start.29 = (bf16[1,128,512]{2,1,0:T(8,128)(2,1)S(1)}, bf16[1,128,512]{2,1,0:T(8,128)(2,1)S(1)}, u32[]{:S(2)}, u32[]{:S(2)}) collective-permute-start(bf16[1,128,512]{2,1,0:T(8,128)(2,1)S(1)} %get-tuple-element.107), channel_id=1, source_target_pairs={{0,4},{1,3},{2,6},{3,1},{4,0},{5,7},{6,2},{7,5},{8,12},{9,11},{10,... | collective-permute-start | bytes 393224 | tf_op jit(solution)/shard_map/ppermute | solution.py:288
  72.8 5.5 %collective-permute-done.32 = bf16[2,128,512]{2,1,0:T(8,128)(2,1)S(1)} collective-permute-done((bf16[2,128,512]{2,1,0:T(8,128)(2,1)S(1)}, bf16[2,128,512]{2,1,0:T(8,128)(2,1)S(1)}, u32[]{:S(2)}, u32[]{:S(2)}) %collective-permute-start.32) | collective-permute-done | bytes 262176 | tf_op jit(solution)/shard_map/ppermute | solution.py:288
  78.6 4.9 %collective-permute-done.34 = bf16[1,128,512]{2,1,0:T(8,128)(2,1)S(1)} collective-permute-done((bf16[1,128,512]{2,1,0:T(8,128)(2,1)S(1)}, bf16[1,128,512]{2,1,0:T(8,128)(2,1)S(1)}, u32[]{:S(2)}, u32[]{:S(2)}) %collective-permute-start.34) | collective-permute-done | bytes 131104 | tf_op jit(solution)/shard_map/ppermute | solution.py:288
  83.5 0.8 fusion
  (68 shorter events, 2.4 us)
Async XLA Ops:
  2.8 35.7 %slice-start = ((s8[16777216]{0:T(1024)(128)(4,1)}), s8[4194304]{0:T(1024)(128)(4,1)S(1)}, s32[]{:S(2)}) async-start(s8[16777216]{0:T(1024)(128)(4,1)} %bitcast.16), calls=%async_computation | async-start | bytes 8388608
  2.8 3.1 %collective-permute-start.1 = (f32[8,128,128]{2,1,0:T(8,128)S(1)}, f32[8,128,128]{2,1,0:T(8,128)S(1)}, u32[]{:S(2)}, u32[]{:S(2)}) collective-permute-start(f32[8,128,128]{2,1,0:T(8,128)S(1)} %get-tuple-element.69), channel_id=1, source_target_pairs={{0,1},{1,0},{2,3},{3,2},{4,5},{5,4},{6,7},{7,6},{8,9},{9,8},{10,11... | collective-permute-start | bytes 1572872 | tf_op jit(solution)/shard_map/ppermute | solution.py:285
  3.3 6.2 %collective-permute-start.3 = (bf16[1,128,512]{2,1,0:T(8,128)(2,1)S(1)}, bf16[1,128,512]{2,1,0:T(8,128)(2,1)S(1)}, u32[]{:S(2)}, u32[]{:S(2)}) collective-permute-start(bf16[1,128,512]{2,1,0:T(8,128)(2,1)S(1)} %bitcast.18), channel_id=1, source_target_pairs={{0,2},{1,5},{2,0},{3,7},{4,6},{5,1},{6,4},{7,3},{8,10},{9,13},{10,... | collective-permute-start | bytes 393224 | tf_op jit(solution)/shard_map/ppermute | solution.py:288
  6.0 5.7 %collective-permute-start.2 = (bf16[4,128,128]{2,1,0:T(8,128)(2,1)S(1)}, bf16[4,128,128]{2,1,0:T(8,128)(2,1)S(1)}, u32[]{:S(2)}, u32[]{:S(2)}) collective-permute-start(bf16[4,128,128]{2,1,0:T(8,128)(2,1)S(1)} %slice.145), channel_id=1, source_target_pairs={{0,4},{1,5},{2,6},{3,7},{4,0},{5,1},{6,2},{7,3},{8,12},{9,13},{10,... | collective-permute-start | bytes 393224 | tf_op jit(solution)/shard_map/ppermute | solution.py:285
  7.9 6.0 %collective-permute-start = (bf16[1,128,512]{2,1,0:T(8,128)(2,1)S(1)}, bf16[1,128,512]{2,1,0:T(8,128)(2,1)S(1)}, u32[]{:S(2)}, u32[]{:S(2)}) collective-permute-start(bf16[1,128,512]{2,1,0:T(8,128)(2,1)S(1)} %bitcast.19), channel_id=1, source_target_pairs={{0,8},{1,17},{2,10},{3,19},{4,12},{5,21},{6,14},{7,23},{8,0},{9,25... | collective-permute-start | bytes 393224 | tf_op jit(solution)/shard_map/ppermute | solution.py:288
  9.5 7.9 %collective-permute-start.6 = (bf16[2,128,512]{2,1,0:T(8,128)(2,1)S(1)}, bf16[2,128,512]{2,1,0:T(8,128)(2,1)S(1)}, u32[]{:S(2)}, u32[]{:S(2)}) collective-permute-start(bf16[2,128,512]{2,1,0:T(8,128)(2,1)S(1)} %pad_maximum_fusion.2), channel_id=1, source_target_pairs={{0,4},{1,3},{2,6},{3,1},{4,0},{5,7},{6,2},{7,5},{8,12},{9,11},{10,... | collective-permute-start | bytes 786440 | tf_op jit(solution)/shard_map/ppermute | solution.py:288
  13.9 5.0 %collective-permute-start.5 = (bf16[1,128,512]{2,1,0:T(8,128)(2,1)S(1)}, bf16[1,128,512]{2,1,0:T(8,128)(2,1)S(1)}, u32[]{:S(2)}, u32[]{:S(2)}) collective-permute-start(bf16[1,128,512]{2,1,0:T(8,128)(2,1)S(1)} %collective-permute-done.refs_5_), channel_id=1, source_target_pairs={{0,2},{1,5},{2,0},{3,7},{4,6},{5,1},{6,4},{7,3},{8,10},{9,13},{10,... | collective-permute-start | bytes 393224 | tf_op jit(solution)/shard_map/ppermute | solution.py:288
  15.4 11.6 %collective-permute-start.4 = (bf16[2,128,640]{2,1,0:T(8,128)(2,1)S(1)}, bf16[2,128,640]{2,1,0:T(8,128)(2,1)S(1)}, u32[]{:S(2)}, u32[]{:S(2)}) collective-permute-start(bf16[2,128,640]{2,1,0:T(8,128)(2,1)S(1)} %pad_maximum_fusion.1), channel_id=1, source_target_pairs={{0,16},{1,9},{2,18},{3,11},{4,20},{5,13},{6,22},{7,15},{8,24},{9,1... | collective-permute-start | bytes 983048 | tf_op jit(solution)/shard_map/ppermute | solution.py:288
  18.9 8.1 %collective-permute-start.7 = (bf16[2,128,512]{2,1,0:T(8,128)(2,1)S(1)}, bf16[2,128,512]{2,1,0:T(8,128)(2,1)S(1)}, u32[]{:S(2)}, u32[]{:S(2)}) collective-permute-start(bf16[2,128,512]{2,1,0:T(8,128)(2,1)S(1)} %pad_maximum_fusion.3), channel_id=1, source_target_pairs={{0,4},{1,3},{2,6},{3,1},{4,0},{5,7},{6,2},{7,5},{8,12},{9,11},{10,... | collective-permute-start | bytes 786440 | tf_op jit(solution)/shard_map/ppermute | solution.py:288
  27.1 7.4 %collective-permute-start.8 = (bf16[2,128,512]{2,1,0:T(8,128)(2,1)S(1)}, bf16[2,128,512]{2,1,0:T(8,128)(2,1)S(1)}, u32[]{:S(2)}, u32[]{:S(2)}) collective-permute-start(bf16[2,128,512]{2,1,0:T(8,128)(2,1)S(1)} %slice.91.refs_2_), channel_id=1, source_target_pairs={{0,2},{1,5},{2,0},{3,7},{4,6},{5,1},{6,4},{7,3},{8,10},{9,13},{10,... | collective-permute-start | bytes 786440 | tf_op jit(solution)/shard_map/ppermute | solution.py:288
  27.7 10.8 %slice-start.1 = ((s8[16777216]{0:T(1024)(128)(4,1)}), s8[4194304]{0:T(1024)(128)(4,1)S(1)}, s32[]{:S(2)}) async-start(s8[16777216]{0:T(1024)(128)(4,1)} %bitcast.16), calls=%async_computation.1 | async-start | bytes 8388608
  27.7 10.8 %slice-start.2 = ((s8[16777216]{0:T(1024)(128)(4,1)}), s8[4194304]{0:T(1024)(128)(4,1)S(1)}, s32[]{:S(2)}) async-start(s8[16777216]{0:T(1024)(128)(4,1)} %bitcast.16), calls=%async_computation.2 | async-start | bytes 8388608
  27.7 10.8 %slice-start.3 = ((s8[16777216]{0:T(1024)(128)(4,1)}), s8[4194304]{0:T(1024)(128)(4,1)S(1)}, s32[]{:S(2)}) async-start(s8[16777216]{0:T(1024)(128)(4,1)} %bitcast.16), calls=%async_computation.3 | async-start | bytes 8388608
  27.7 6.7 %collective-permute-start.9 = (bf16[1,128,128]{2,1,0:T(8,128)(2,1)S(1)}, bf16[1,128,128]{2,1,0:T(8,128)(2,1)S(1)}, u32[]{:S(2)}, u32[]{:S(2)}) collective-permute-start(bf16[1,128,128]{2,1,0:T(8,128)(2,1)S(1)} %slice.147), channel_id=1, source_target_pairs={{0,8},{1,17},{2,10},{3,19},{4,12},{5,21},{6,14},{7,23},{8,0},{9,25... | collective-permute-start | bytes 98312 | tf_op jit(solution)/shard_map/ppermute | solution.py:288
  29.0 6.6 %collective-permute-start.13 = (bf16[1,128,512]{2,1,0:T(8,128)(2,1)S(1)}, bf16[1,128,512]{2,1,0:T(8,128)(2,1)S(1)}, u32[]{:S(2)}, u32[]{:S(2)}) collective-permute-start(bf16[1,128,512]{2,1,0:T(8,128)(2,1)S(1)} %bitcast.22), channel_id=1, source_target_pairs={{0,1},{1,0},{2,3},{3,2},{4,5},{5,4},{6,7},{7,6},{8,9},{9,8},{10,11... | collective-permute-start | bytes 393224 | tf_op jit(solution)/shard_map/ppermute | solution.py:285
  29.0 7.6 %collective-permute-start.15 = (bf16[2,128,512]{2,1,0:T(8,128)(2,1)S(1)}, bf16[2,128,512]{2,1,0:T(8,128)(2,1)S(1)}, u32[]{:S(2)}, u32[]{:S(2)}) collective-permute-start(bf16[2,128,512]{2,1,0:T(8,128)(2,1)S(1)} %collective-permute-done.6.refs_4_), channel_id=1, source_target_pairs={{0,1},{1,0},{2,3},{3,2},{4,5},{5,4},{6,7},{7,6},{8,9},{9,8},{10,11... | collective-permute-start | bytes 786440 | tf_op jit(solution)/shard_map/ppermute | solution.py:285
  34.5 9.2 %collective-permute-start.10 = (bf16[4,128,512]{2,1,0:T(8,128)(2,1)S(1)}, bf16[4,128,512]{2,1,0:T(8,128)(2,1)S(1)}, u32[]{:S(2)}, u32[]{:S(2)}) collective-permute-start(bf16[4,128,512]{2,1,0:T(8,128)(2,1)S(1)} %pad_maximum_fusion), channel_id=1, source_target_pairs={{0,4},{1,3},{2,6},{3,1},{4,0},{5,7},{6,2},{7,5},{8,12},{9,11},{10,... | collective-permute-start | bytes 1572872 | tf_op jit(solution)/shard_map/ppermute | solution.py:288
  35.1 1.3 %collective-permute-start.14 = (bf16[1,128,512]{2,1,0:T(8,128)(2,1)S(1)}, bf16[1,128,512]{2,1,0:T(8,128)(2,1)S(1)}, u32[]{:S(2)}, u32[]{:S(2)}) collective-permute-start(bf16[1,128,512]{2,1,0:T(8,128)(2,1)S(1)} %collective-permute-done.3.refs_3_), channel_id=1, source_target_pairs={{0,1},{1,0},{2,3},{3,2},{4,5},{5,4},{6,7},{7,6},{8,9},{9,8},{10,11... | collective-permute-start | bytes 393224 | tf_op jit(solution)/shard_map/ppermute | solution.py:285
  35.1 1.9 %collective-permute-start.16 = (bf16[1,128,512]{2,1,0:T(8,128)(2,1)S(1)}, bf16[1,128,512]{2,1,0:T(8,128)(2,1)S(1)}, u32[]{:S(2)}, u32[]{:S(2)}) collective-permute-start(bf16[1,128,512]{2,1,0:T(8,128)(2,1)S(1)} %collective-permute-done.refs_5_), channel_id=1, source_target_pairs={{0,1},{1,0},{2,3},{3,2},{4,5},{5,4},{6,7},{7,6},{8,9},{9,8},{10,11... | collective-permute-start | bytes 393224 | tf_op jit(solution)/shard_map/ppermute | solution.py:285
  35.6 2.9 %collective-permute-start.18 = (bf16[2,128,512]{2,1,0:T(8,128)(2,1)S(1)}, bf16[2,128,512]{2,1,0:T(8,128)(2,1)S(1)}, u32[]{:S(2)}, u32[]{:S(2)}) collective-permute-start(bf16[2,128,512]{2,1,0:T(8,128)(2,1)S(1)} %collective-permute-done.7.refs_7_), channel_id=1, source_target_pairs={{0,1},{1,0},{2,3},{3,2},{4,5},{5,4},{6,7},{7,6},{8,9},{9,8},{10,11... | collective-permute-start | bytes 786440 | tf_op jit(solution)/shard_map/ppermute | solution.py:285
  36.4 1.3 %collective-permute-start.17 = (bf16[1,128,512]{2,1,0:T(8,128)(2,1)S(1)}, bf16[1,128,512]{2,1,0:T(8,128)(2,1)S(1)}, u32[]{:S(2)}, u32[]{:S(2)}) collective-permute-start(bf16[1,128,512]{2,1,0:T(8,128)(2,1)S(1)} %collective-permute-done.5.refs_6_), channel_id=1, source_target_pairs={{0,1},{1,0},{2,3},{3,2},{4,5},{5,4},{6,7},{7,6},{8,9},{9,8},{10,11... | collective-permute-start | bytes 393224 | tf_op jit(solution)/shard_map/ppermute | solution.py:285
  36.6 3.9 %collective-permute-start.11 = (bf16[2,128,512]{2,1,0:T(8,128)(2,1)S(1)}, bf16[2,128,512]{2,1,0:T(8,128)(2,1)S(1)}, u32[]{:S(2)}, u32[]{:S(2)}) collective-permute-start(bf16[2,128,512]{2,1,0:T(8,128)(2,1)S(1)} %slice.91.refs_2_), channel_id=1, source_target_pairs={{0,1},{1,0},{2,3},{3,2},{4,5},{5,4},{6,7},{7,6},{8,9},{9,8},{10,11... | collective-permute-start | bytes 786440 | tf_op jit(solution)/shard_map/ppermute | solution.py:285
  36.9 3.6 %collective-permute-start.12 = (bf16[2,128,512]{2,1,0:T(8,128)(2,1)S(1)}, bf16[2,128,512]{2,1,0:T(8,128)(2,1)S(1)}, u32[]{:S(2)}, u32[]{:S(2)}) collective-permute-start(bf16[2,128,512]{2,1,0:T(8,128)(2,1)S(1)} %collective-permute-done.8.refs_3_), channel_id=1, source_target_pairs={{0,1},{1,0},{2,3},{3,2},{4,5},{5,4},{6,7},{7,6},{8,9},{9,8},{10,11... | collective-permute-start | bytes 786440 | tf_op jit(solution)/shard_map/ppermute | solution.py:285
  37.8 6.2 %collective-permute-start.20 = (bf16[128,128]{1,0:T(8,128)(2,1)S(1)}, bf16[128,128]{1,0:T(8,128)(2,1)S(1)}, u32[]{:S(2)}, u32[]{:S(2)}) collective-permute-start(bf16[128,128]{1,0:T(8,128)(2,1)S(1)} %bitcast_convert_fusion), channel_id=1, source_target_pairs={{0,2},{1,3},{2,0},{3,1},{4,6},{5,7},{6,4},{7,5},{8,10},{9,11},{10,... | collective-permute-start | bytes 98312 | tf_op jit(solution)/shard_map/ppermute | solution.py:285
  43.7 2.0 %collective-permute-start.19 = (bf16[4,128,512]{2,1,0:T(8,128)(2,1)S(1)}, bf16[4,128,512]{2,1,0:T(8,128)(2,1)S(1)}, u32[]{:S(2)}, u32[]{:S(2)}) collective-permute-start(bf16[4,128,512]{2,1,0:T(8,128)(2,1)S(1)} %collective-permute-done.10.refs_2_), channel_id=1, source_target_pairs={{0,1},{1,0},{2,3},{3,2},{4,5},{5,4},{6,7},{7,6},{8,9},{9,8},{10,11... | collective-permute-start | bytes 1572872 | tf_op jit(solution)/shard_map/ppermute | solution.py:285
  44.0 1.7 %collective-permute-start.21 = (f32[128,128]{1,0:T(8,128)S(1)}, f32[128,128]{1,0:T(8,128)S(1)}, u32[]{:S(2)}, u32[]{:S(2)}) collective-permute-start(f32[128,128]{1,0:T(8,128)S(1)} %bitcast_add_fusion.refs_6_), channel_id=1, source_target_pairs={{0,1},{1,0},{2,3},{3,2},{4,5},{5,4},{6,7},{7,6},{8,9},{9,8},{10,11... | collective-permute-start | bytes 196616 | tf_op jit(solution)/shard_map/ppermute | solution.py:285
  47.8 2.0 %collective-permute-start.22 = (bf16[4,128,512]{2,1,0:T(8,128)(2,1)S(1)}, bf16[4,128,512]{2,1,0:T(8,128)(2,1)S(1)}, u32[]{:S(2)}, u32[]{:S(2)}) collective-permute-start(bf16[4,128,512]{2,1,0:T(8,128)(2,1)S(1)} %shard_map.75), channel_id=1, source_target_pairs={{0,1},{1,0},{2,3},{3,2},{4,5},{5,4},{6,7},{7,6},{8,9},{9,8},{10,11... | collective-permute-start | bytes 1572872 | tf_op jit(solution)/shard_map/ppermute | solution.py:285
  49.9 9.2 %collective-permute-start.25 = (bf16[4,128,512]{2,1,0:T(8,128)(2,1)S(1)}, bf16[4,128,512]{2,1,0:T(8,128)(2,1)S(1)}, u32[]{:S(2)}, u32[]{:S(2)}) collective-permute-start(bf16[4,128,512]{2,1,0:T(8,128)(2,1)S(1)} %add_convert_fusion.1), channel_id=1, source_target_pairs={{0,2},{1,5},{2,0},{3,7},{4,6},{5,1},{6,4},{7,3},{8,10},{9,13},{10,... | collective-permute-start | bytes 1572872 | tf_op jit(solution)/shard_map/ppermute | solution.py:288
  54.4 5.8 %collective-permute-start.26 = (bf16[4,128,512]{2,1,0:T(8,128)(2,1)S(1)}, bf16[4,128,512]{2,1,0:T(8,128)(2,1)S(1)}, u32[]{:S(2)}, u32[]{:S(2)}) collective-permute-start(bf16[4,128,512]{2,1,0:T(8,128)(2,1)S(1)} %get-tuple-element.96), channel_id=1, source_target_pairs={{0,1},{1,0},{2,3},{3,2},{4,5},{5,4},{6,7},{7,6},{8,9},{9,8},{10,11... | collective-permute-start | bytes 1572872 | tf_op jit(solution)/shard_map/ppermute | solution.py:285
  54.5 4.1 %collective-permute-start.24 = (bf16[2,128,512]{2,1,0:T(8,128)(2,1)S(1)}, bf16[2,128,512]{2,1,0:T(8,128)(2,1)S(1)}, u32[]{:S(2)}, u32[]{:S(2)}) collective-permute-start(bf16[2,128,512]{2,1,0:T(8,128)(2,1)S(1)} %get-tuple-element.102), channel_id=1, source_target_pairs={{0,1},{1,0},{2,3},{3,2},{4,5},{5,4},{6,7},{7,6},{8,9},{9,8},{10,11... | collective-permute-start | bytes 786440 | tf_op jit(solution)/shard_map/ppermute | solution.py:285
  55.0 6.7 %collective-permute-start.30 = (bf16[2,128,512]{2,1,0:T(8,128)(2,1)S(1)}, bf16[2,128,512]{2,1,0:T(8,128)(2,1)S(1)}, u32[]{:S(2)}, u32[]{:S(2)}) collective-permute-start(bf16[2,128,512]{2,1,0:T(8,128)(2,1)S(1)} %get-tuple-element.94), channel_id=1, source_target_pairs={{0,1},{1,0},{2,3},{3,2},{4,5},{5,4},{6,7},{7,6},{8,9},{9,8},{10,11... | collective-permute-start | bytes 786440 | tf_op jit(solution)/shard_map/ppermute | solution.py:285
  59.3 8.8 %collective-permute-start.31 = (bf16[2,128,512]{2,1,0:T(8,128)(2,1)S(1)}, bf16[2,128,512]{2,1,0:T(8,128)(2,1)S(1)}, u32[]{:S(2)}, u32[]{:S(2)}) collective-permute-start(bf16[2,128,512]{2,1,0:T(8,128)(2,1)S(1)} %add_convert_fusion.4), channel_id=1, source_target_pairs={{0,4},{1,3},{2,6},{3,1},{4,0},{5,7},{6,2},{7,5},{8,12},{9,11},{10,... | collective-permute-start | bytes 786440 | tf_op jit(solution)/shard_map/ppermute | solution.py:288
  60.4 10.2 %collective-permute-start.27 = (bf16[4,128,512]{2,1,0:T(8,128)(2,1)S(1)}, bf16[4,128,512]{2,1,0:T(8,128)(2,1)S(1)}, u32[]{:S(2)}, u32[]{:S(2)}) collective-permute-start(bf16[4,128,512]{2,1,0:T(8,128)(2,1)S(1)} %add_convert_fusion), channel_id=1, source_target_pairs={{0,2},{1,5},{2,0},{3,7},{4,6},{5,1},{6,4},{7,3},{8,10},{9,13},{10,... | collective-permute-start | bytes 1572872 | tf_op jit(solution)/shard_map/ppermute | solution.py:288
  61.2 11.6 %collective-permute-start.23 = (bf16[2,128,512]{2,1,0:T(8,128)(2,1)S(1)}, bf16[2,128,512]{2,1,0:T(8,128)(2,1)S(1)}, u32[]{:S(2)}, u32[]{:S(2)}) collective-permute-start(bf16[2,128,512]{2,1,0:T(8,128)(2,1)S(1)} %get-tuple-element.99), channel_id=1, source_target_pairs={{0,1},{1,0},{2,3},{3,2},{4,5},{5,4},{6,7},{7,6},{8,9},{9,8},{10,11... | collective-permute-start | bytes 786440 | tf_op jit(solution)/shard_map/ppermute | solution.py:285
  61.2 9.4 %collective-permute-start.28 = (bf16[2,128,512]{2,1,0:T(8,128)(2,1)S(1)}, bf16[2,128,512]{2,1,0:T(8,128)(2,1)S(1)}, u32[]{:S(2)}, u32[]{:S(2)}) collective-permute-start(bf16[2,128,512]{2,1,0:T(8,128)(2,1)S(1)} %get-tuple-element.105), channel_id=1, source_target_pairs={{0,1},{1,0},{2,3},{3,2},{4,5},{5,4},{6,7},{7,6},{8,9},{9,8},{10,11... | collective-permute-start | bytes 786440 | tf_op jit(solution)/shard_map/ppermute | solution.py:285
  68.2 10.1 %collective-permute-start.32 = (bf16[2,128,512]{2,1,0:T(8,128)(2,1)S(1)}, bf16[2,128,512]{2,1,0:T(8,128)(2,1)S(1)}, u32[]{:S(2)}, u32[]{:S(2)}) collective-permute-start(bf16[2,128,512]{2,1,0:T(8,128)(2,1)S(1)} %add_convert_fusion.2), channel_id=1, source_target_pairs={{0,16},{1,9},{2,18},{3,11},{4,20},{5,13},{6,22},{7,15},{8,24},{9,1... | collective-permute-start | bytes 786440 | tf_op jit(solution)/shard_map/ppermute | solution.py:288
  70.7 7.6 %collective-permute-start.33 = (bf16[1,128,512]{2,1,0:T(8,128)(2,1)S(1)}, bf16[1,128,512]{2,1,0:T(8,128)(2,1)S(1)}, u32[]{:S(2)}, u32[]{:S(2)}) collective-permute-start(bf16[1,128,512]{2,1,0:T(8,128)(2,1)S(1)} %get-tuple-element.108), channel_id=1, source_target_pairs={{0,4},{1,3},{2,6},{3,1},{4,0},{5,7},{6,2},{7,5},{8,12},{9,11},{10,... | collective-permute-start | bytes 393224 | tf_op jit(solution)/shard_map/ppermute | solution.py:288
  71.8 6.8 %collective-permute-start.29 = (bf16[1,128,512]{2,1,0:T(8,128)(2,1)S(1)}, bf16[1,128,512]{2,1,0:T(8,128)(2,1)S(1)}, u32[]{:S(2)}, u32[]{:S(2)}) collective-permute-start(bf16[1,128,512]{2,1,0:T(8,128)(2,1)S(1)} %get-tuple-element.107), channel_id=1, source_target_pairs={{0,4},{1,3},{2,6},{3,1},{4,0},{5,7},{6,2},{7,5},{8,12},{9,11},{10,... | collective-permute-start | bytes 393224 | tf_op jit(solution)/shard_map/ppermute | solution.py:288
  78.5 5.0 %collective-permute-start.34 = (bf16[1,128,512]{2,1,0:T(8,128)(2,1)S(1)}, bf16[1,128,512]{2,1,0:T(8,128)(2,1)S(1)}, u32[]{:S(2)}, u32[]{:S(2)}) collective-permute-start(bf16[1,128,512]{2,1,0:T(8,128)(2,1)S(1)} %add_convert_fusion.6), channel_id=1, source_target_pairs={{0,8},{1,17},{2,10},{3,19},{4,12},{5,21},{6,14},{7,23},{8,0},{9,25... | collective-permute-start | bytes 393224 | tf_op jit(solution)/shard_map/ppermute | solution.py:288

commit v11 on v9

--- a/solution.py
+++ b/solution.py
@@ -329,34 +329,38 @@
         own = sum(order(offsets), [])
         return own + across(own)
 
-    def halved(kv, send, way):
+    home, mid = near[: len(low)], near[len(low) :]
+    own = jnp.stack([act] + [swap(raw, o) for o in low[1:]])
+    side = turn(own, 0)
+    both = turn(jnp.concatenate([own, side]), 1)
+    middle = after(along(own, 0), side)
+    last_row = along(jnp.concatenate([own, middle]), 1)
+    middle_side = after(turn(middle, 0), both)
+    joined = jnp.concatenate([middle, middle_side])
+    middle_both = turn(joined, 1)
+    last_row = after(last_row, middle_both)
+    last_side = turn(last_row, 0)
+    blocks, far_symbols = fetched(after(where, last_row), wo, width, columns_of(far))
+    last_side, blocks = lax.optimization_barrier((last_side, blocks))
+    far_held = (blocks, far_symbols)
+    last_both = turn(jnp.concatenate([last_row, last_side]), 1)
+
+    kv = kv_keep + swap(kv_send, CORE)
+    for send, way, then in (
+        (swap, bits[shared], middle),
+        (along, 1, middle_side),
+        (along, 0, last_side),
+    ):
         half = kv.shape[0] // 2
-        return kv[half:] + send(kv[:half].astype(bf16), way).astype(f32)
-
-    kv = halved(kv_keep + swap(kv_send, CORE), swap, bits[shared])
-    far_blocks, far_symbols = fetched(where, wo, width, columns_of(far))
-    row = jnp.stack([act] + [swap(raw, o) for o in low[1:]])
-    row = jnp.concatenate([row, along(row, 0)])
-    row, kv, far_blocks = lax.optimization_barrier((row, kv, far_blocks))
-    far_held = (far_blocks, far_symbols)
-    groups = []
-    for offsets in (near, far):
-        if offsets is far:
-            half = kv[: kv.shape[0] // 2].astype(bf16)
-            k = min(row.shape[0], half.shape[0])
-            extra = jnp.zeros((row.shape[0], *half.shape[1:]), bf16).at[:k].set(half[:k])
-            got = along(jnp.concatenate([row, extra], axis=2), 1)
-            row = got[:, :, :width]
-            kv = kv[kv.shape[0] // 2 :] + got[:k, :, width:].astype(f32)
-            side = turn(row, 0)
-            kv = halved(kv, along, 0)
-            side, kv = lax.optimization_barrier((side, kv))
-        else:
-            side = turn(row, 0)
-        both = turn(jnp.concatenate([row, side]), 1)
+        got = after(send(kv[:half].astype(bf16), way), then)
+        kv = kv[half:] + got.astype(f32)
+
+    def pieces_of(row, side, both, offsets):
         at = symbols_of(offsets)
-        groups.append([(row, at[0]), (side, at[1]), (both, at[2] + at[3])])
-    early, last = groups
+        return [(row, at[0]), (side, at[1]), (both, at[2] + at[3])]
+
+    early = pieces_of(own, side, both, home) + pieces_of(middle, middle_side, middle_both, mid)
+    last = pieces_of(last_row, last_side, last_both, far)
     partners = [swap(kv[0].astype(bf16), o) for o in combos(bits[1:shared])[1:]]
 
     call = functools.partial(query_call, where, gain, weight=wq)
@@ -406,13 +410,10 @@
     pairs = paired(own, sent)
     first = added_up(after(pairs[0][0], far_two), pairs[0][1]).astype(bf16)
     near_home, near_two = round_square(first, *pairs[1:])
+    far_got = along(far_sum.astype(bf16), 1)
     k = len(low)
-    far_sum = added_up(far_sum[:k], along(far_sum[k:].astype(bf16), 0))
-    far_got = along(far_sum.astype(bf16), 1)
-    got = [turn(near_two[k:], 1), turn(near_two[:k], 1)]
-    near_sum = added_up(*[x[k:] for x in near_home], got[0])
-    home_sum = added_up(*[x[:k] for x in near_home], got[1])
-    home_sum = added_up(home_sum, along(near_sum.astype(bf16), 0), far_got)
+    near_sum = added_up(*near_home, turn(near_two, 1), far_got)
+    home_sum = added_up(near_sum[:k], along(near_sum[k:].astype(bf16), 0))
     out = added_up(home_sum[0], *[swap(home_sum[i].astype(bf16), o) for i, o in enumerate(low) if o])
     return out.astype(bf16)
 

time: 83.5 us -> 88.2 us (1.056)
  waiting for transfers between devices: 30.6 us -> 33.1 us
  starting transfers between devices: 27.9 us -> 30.2 us
    ppermute x15 -> x16, waiting for transfers between devices: 28.5 us -> 31.7 us  [by_core(): lax.ppermute(x, 'wide', [(i, i ^ pair[(step + (i & CORE)) % 2]) for i in...]
    ppermute x15 -> x16, starting transfers between devices: 21.9 us -> 24.6 us  [by_core(): lax.ppermute(x, 'wide', [(i, i ^ pair[(step + (i & CORE)) % 2]) for i in...]
    ppermute x16 -> x19, waiting for transfers between devices: 2.04 us -> 1.33 us  [swap(): return lax.ppermute(x, 'wide', [(i, i ^ offset) for i in range(n)])]
    ppermute x16 -> x19, starting transfers between devices: 6.01 us -> 5.6 us  [swap(): return lax.ppermute(x, 'wide', [(i, i ^ offset) for i in range(n)])]
  transfers between devices with their start and end apart: 31 -> 35, of which waited for: 12 -> 13; matrix products, arithmetic and copies ran while one was open for 2% -> 1% of each run, Pallas kernels for 21% -> 20%
where the time goes in v11:
time: 88.2 us; the launch traced here: 88 us
  waiting for transfers between devices  33.1 us (38%)
  starting transfers between devices  30.2 us (34%)
  Pallas kernels  22 us (25%)
  other arithmetic  2.18 us (2%)
    ppermute x16, waiting for transfers between devices, by_core(): lax.ppermute(x, 'wide', [(i, i ^ pair[(step + (i & CORE)) % 2]) for i in...  31.7 us
    ppermute x16, starting transfers between devices, by_core(): lax.ppermute(x, 'wide', [(i, i ^ pair[(step + (i & CORE)) % 2]) for i in...  24.6 us
    pallas_call x5, Pallas kernels, output_call(): pl.pallas_call(kernel, out_shape=[jax.ShapeDtypeStruct((len(s), tokens, w...  8.67 us
    pallas_call x4, Pallas kernels, query_call(): pl.pallas_call(functools.partial(query_kernel, places, bool(carry), bool(...  5.85 us
    ppermute x19, starting transfers between devices, swap(): return lax.ppermute(x, 'wide', [(i, i ^ offset) for i in range(n)])  5.6 us
    pallas_call x1, Pallas kernels, fetched(): pl.pallas_call(functools.partial(fetch_kernel, symbols, width), out_shape...  4.77 us
    pallas_call x1, Pallas kernels, kv_terms(): pl.pallas_call(functools.partial(kv_kernel, shared), out_shape=[jax.Shape...  2.69 us
  transfers between devices with their start and end apart: 35, of which 13 were waited for; matrix products, arithmetic and copies ran while one was open for 1% of the time, Pallas kernels for 20%

profile of v11, /device:TPU:0, one launch (start us, length us, event | category | flops | bytes accessed | tf_op | source)
XLA Modules:
  0.0 88.0 jit_solution(4252565381849215524)
XLA Ops:
  0.1 2.7 %shard_map.64 = (f32[8,128,128]{2,1,0:T(8,128)S(1)}, f32[8,128,128]{2,1,0:T(8,128)S(1)}, bf16[128,512]{1,0:T(8,128)(2,1)S(1)}, f32[1,16384]{1,0:T(1,128)S(1)}) custom-call(s32[9]{0:T(128)S(1)} %stack.42.where.refs_0_, bf16[128,512]{1,0:T(8,128)(2,1)} %act.1, f32[1,16384]{1,0:T(1,128)} %bitcast.27, bf16[512,1024]{1,0:T(8,128)(2,1)} %wk.1, bf16[512,1024]{1,0:T(8,128)(2,1)} %wv.1), custom_call_target="tpu_custom_call" | custom-call | flops 4294967296 | bytes 33554432 | tf_op jit(solution)/shard_map/pallas_call | solution.py:105
  2.8 3.0 %collective-permute-start.1 = (bf16[1,128,512]{2,1,0:T(8,128)(2,1)S(1)}, bf16[1,128,512]{2,1,0:T(8,128)(2,1)S(1)}, u32[]{:S(2)}, u32[]{:S(2)}) collective-permute-start(bf16[1,128,512]{2,1,0:T(8,128)(2,1)S(1)} %bitcast.21), channel_id=1, source_target_pairs={{0,2},{1,5},{2,0},{3,7},{4,6},{5,1},{6,4},{7,3},{8,10},{9,13},{10,... | collective-permute-start | bytes 393224 | tf_op jit(solution)/shard_map/ppermute | solution.py:288
  5.8 1.6 %collective-permute-start = (bf16[1,128,512]{2,1,0:T(8,128)(2,1)S(1)}, bf16[1,128,512]{2,1,0:T(8,128)(2,1)S(1)}, u32[]{:S(2)}, u32[]{:S(2)}) collective-permute-start(bf16[1,128,512]{2,1,0:T(8,128)(2,1)S(1)} %bitcast.22), channel_id=1, source_target_pairs={{0,8},{1,17},{2,10},{3,19},{4,12},{5,21},{6,14},{7,23},{8,0},{9,25... | collective-permute-start | bytes 393224 | tf_op jit(solution)/shard_map/ppermute | solution.py:288
  7.4 0.3 collective-permute-start.17
  7.7 1.1 %collective-permute-done.1.refs_3_ = bf16[1,128,512]{2,1,0:T(8,128)(2,1)S(1)} collective-permute-done((bf16[1,128,512]{2,1,0:T(8,128)(2,1)S(1)}, bf16[1,128,512]{2,1,0:T(8,128)(2,1)S(1)}, u32[]{:S(2)}, u32[]{:S(2)}) %collective-permute-start.1) | collective-permute-done | bytes 131104 | tf_op jit(solution)/shard_map/ppermute | solution.py:288
  8.8 2.1 %collective-permute-start.4 = (bf16[2,128,512]{2,1,0:T(8,128)(2,1)S(1)}, bf16[2,128,512]{2,1,0:T(8,128)(2,1)S(1)}, u32[]{:S(2)}, u32[]{:S(2)}) collective-permute-start(bf16[2,128,512]{2,1,0:T(8,128)(2,1)S(1)} %pad_maximum_fusion.1), channel_id=1, source_target_pairs={{0,4},{1,3},{2,6},{3,1},{4,0},{5,7},{6,2},{7,5},{8,12},{9,11},{10,... | collective-permute-start | bytes 786440 | tf_op jit(solution)/shard_map/ppermute | solution.py:288
  10.9 0.5 collective-permute-done.refs_5_
  11.4 1.0 %collective-permute-start.3 = (bf16[1,128,512]{2,1,0:T(8,128)(2,1)S(1)}, bf16[1,128,512]{2,1,0:T(8,128)(2,1)S(1)}, u32[]{:S(2)}, u32[]{:S(2)}) collective-permute-start(bf16[1,128,512]{2,1,0:T(8,128)(2,1)S(1)} %collective-permute-done.refs_5_), channel_id=1, source_target_pairs={{0,2},{1,5},{2,0},{3,7},{4,6},{5,1},{6,4},{7,3},{8,10},{9,13},{10,... | collective-permute-start | bytes 393224 | tf_op jit(solution)/shard_map/ppermute | solution.py:288
  12.4 4.0 %collective-permute-done.3.refs_6_ = bf16[1,128,512]{2,1,0:T(8,128)(2,1)S(1)} collective-permute-done((bf16[1,128,512]{2,1,0:T(8,128)(2,1)S(1)}, bf16[1,128,512]{2,1,0:T(8,128)(2,1)S(1)}, u32[]{:S(2)}, u32[]{:S(2)}) %collective-permute-start.3) | collective-permute-done | bytes 131104 | tf_op jit(solution)/shard_map/ppermute | solution.py:288
  16.4 2.4 %collective-permute-start.5 = (bf16[2,128,512]{2,1,0:T(8,128)(2,1)S(1)}, bf16[2,128,512]{2,1,0:T(8,128)(2,1)S(1)}, u32[]{:S(2)}, u32[]{:S(2)}) collective-permute-start(bf16[2,128,512]{2,1,0:T(8,128)(2,1)S(1)} %get-tuple-element.83), channel_id=1, source_target_pairs={{0,4},{1,3},{2,6},{3,1},{4,0},{5,7},{6,2},{7,5},{8,12},{9,11},{10,... | collective-permute-start | bytes 786440 | tf_op jit(solution)/shard_map/ppermute | solution.py:288
  18.8 2.2 %collective-permute-start.2 = (bf16[2,128,512]{2,1,0:T(8,128)(2,1)S(1)}, bf16[2,128,512]{2,1,0:T(8,128)(2,1)S(1)}, u32[]{:S(2)}, u32[]{:S(2)}) collective-permute-start(bf16[2,128,512]{2,1,0:T(8,128)(2,1)S(1)} %get-tuple-element.84), channel_id=1, source_target_pairs={{0,16},{1,9},{2,18},{3,11},{4,20},{5,13},{6,22},{7,15},{8,24},{9,1... | collective-permute-start | bytes 786440 | tf_op jit(solution)/shard_map/ppermute | solution.py:288
  21.1 0.9 %collective-permute-start.18 = (bf16[4,128,128]{2,1,0:T(8,128)(2,1)S(1)}, bf16[4,128,128]{2,1,0:T(8,128)(2,1)S(1)}, u32[]{:S(2)}, u32[]{:S(2)}) collective-permute-start(bf16[4,128,128]{2,1,0:T(8,128)(2,1)S(1)} %slice.87), channel_id=1, source_target_pairs={{0,4},{1,5},{2,6},{3,7},{4,0},{5,1},{6,2},{7,3},{8,12},{9,13},{10,... | collective-permute-start | bytes 393224 | tf_op jit(solution)/shard_map/ppermute | solution.py:285
  22.0 2.3 %collective-permute-done.5.refs_7_ = bf16[2,128,512]{2,1,0:T(8,128)(2,1)S(1)} collective-permute-done((bf16[2,128,512]{2,1,0:T(8,128)(2,1)S(1)}, bf16[2,128,512]{2,1,0:T(8,128)(2,1)S(1)}, u32[]{:S(2)}, u32[]{:S(2)}) %collective-permute-start.5) | collective-permute-done | bytes 262176 | tf_op jit(solution)/shard_map/ppermute | solution.py:288
  24.3 4.5 %collective-permute-done.2.refs_2_ = bf16[2,128,512]{2,1,0:T(8,128)(2,1)S(1)} collective-permute-done((bf16[2,128,512]{2,1,0:T(8,128)(2,1)S(1)}, bf16[2,128,512]{2,1,0:T(8,128)(2,1)S(1)}, u32[]{:S(2)}, u32[]{:S(2)}) %collective-permute-start.2) | collective-permute-done | bytes 262176 | tf_op jit(solution)/shard_map/ppermute | solution.py:288
  28.9 1.5 %collective-permute-start.6 = (bf16[2,128,512]{2,1,0:T(8,128)(2,1)S(1)}, bf16[2,128,512]{2,1,0:T(8,128)(2,1)S(1)}, u32[]{:S(2)}, u32[]{:S(2)}) collective-permute-start(bf16[2,128,512]{2,1,0:T(8,128)(2,1)S(1)} %collective-permute-done.2.refs_2_), channel_id=1, source_target_pairs={{0,2},{1,5},{2,0},{3,7},{4,6},{5,1},{6,4},{7,3},{8,10},{9,13},{10,... | collective-permute-start | bytes 786440 | tf_op jit(solution)/shard_map/ppermute | solution.py:288
  30.4 0.4 collective-permute-start.19
  30.8 0.5 collective-permute-start.11
  31.3 4.8 %shard_map.65.weight = bf16[16,512,512]{2,1,0:T(8,128)(2,1)S(1)} custom-call(s32[9]{0:T(128)S(1)} %stack.42.where.refs_0_, bf16[512,16384]{1,0:T(8,128)(2,1)} %weight.3), custom_call_target="tpu_custom_call" | custom-call | bytes 16777216 | tf_op jit(solution)/shard_map/pallas_call | solution.py:67
  36.1 0.3 collective-permute-done.19
  36.5 3.5 %collective-permute-start.20 = (bf16[1,128,128]{2,1,0:T(8,128)(2,1)S(1)}, bf16[1,128,128]{2,1,0:T(8,128)(2,1)S(1)}, u32[]{:S(2)}, u32[]{:S(2)}) collective-permute-start(bf16[1,128,128]{2,1,0:T(8,128)(2,1)S(1)} %slice.89), channel_id=1, source_target_pairs={{0,8},{1,17},{2,10},{3,19},{4,12},{5,21},{6,14},{7,23},{8,0},{9,25... | collective-permute-start | bytes 98312 | tf_op jit(solution)/shard_map/ppermute | solution.py:288
  40.0 0.5 collective-permute-start.14
  40.6 1.3 %collective-permute-done.20 = bf16[1,128,128]{2,1,0:T(8,128)(2,1)S(1)} collective-permute-done((bf16[1,128,128]{2,1,0:T(8,128)(2,1)S(1)}, bf16[1,128,128]{2,1,0:T(8,128)(2,1)S(1)}, u32[]{:S(2)}, u32[]{:S(2)}) %collective-permute-start.20) | collective-permute-done | bytes 32800 | tf_op jit(solution)/shard_map/ppermute | solution.py:288
  42.0 0.6 collective-permute-start.8
  42.6 0.6 collective-permute-start.21
  43.5 2.0 %shard_map.66 = (f32[128,512]{1,0:T(8,128)S(1)}, f32[128,128]{1,0:T(8,128)S(1)}) custom-call(s32[9]{0:T(128)S(1)} %stack.42.where.refs_0_, f32[1,16384]{1,0:T(1,128)S(1)} %get-tuple-element.44.refs_1_, bf16[1,128,512]{2,1,0:T(8,128)(2,1)S(1)} %bitcast.26, bf16[1,128,512]{2,1,0:T(8,128)(2,1)S(1)} %collective-permute-done.1.refs_3_, ...), custom_call_target="tpu_custom_call" | custom-call | flops 1073741824 | bytes 8388608 | tf_op jit(solution)/shard_map/pallas_call | solution.py:198
  45.5 1.3 %shard_map.67 = (f32[128,512]{1,0:T(8,128)S(1)}, f32[128,128]{1,0:T(8,128)S(1)}) custom-call(s32[9]{0:T(128)S(1)} %stack.42.where.refs_0_, f32[1,16384]{1,0:T(1,128)S(1)} %get-tuple-element.44.refs_1_, bf16[2,128,512]{2,1,0:T(8,128)(2,1)S(1)} %collective-permute-done.2.refs_2_, bf16[2,128,512]{2,1,0:T(8,128)(2,1)S(1)} %collective-permute-done.6.refs_3_, ...), custom_call_target="tpu_custom_call" | custom-call | flops 536870912 | bytes 4194304 | tf_op jit(solution)/shard_map/pallas_call | solution.py:198
  47.3 0.5 collective-permute-start.22
  47.9 1.0 %shard_map.68 = (f32[128,512]{1,0:T(8,128)S(1)}, f32[128,128]{1,0:T(8,128)S(1)}) custom-call(s32[9]{0:T(128)S(1)} %stack.42.where.refs_0_, f32[1,16384]{1,0:T(1,128)S(1)} %get-tuple-element.44.refs_1_, bf16[4,128,512]{2,1,0:T(8,128)(2,1)S(1)} %collective-permute-done.7.refs_2_, bf16[16384,512]{1,0:T(8,128)(2,1)S(1)} %bitcast.20, ...), custom_call_target="tpu_custom_call" | custom-call | flops 268435456 | bytes 2097152 | tf_op jit(solution)/shard_map/pallas_call | solution.py:198
  48.9 1.6 %shard_map.69.attended = bf16[128,512]{1,0:T(8,128)(2,1)S(1)} custom-call(s32[9]{0:T(128)S(1)} %stack.42.where.refs_0_, f32[1,16384]{1,0:T(1,128)S(1)} %get-tuple-element.44.refs_1_, bf16[4,128,512]{2,1,0:T(8,128)(2,1)S(1)} %collective-permute-done.16.refs_2_, bf16[16384,512]{1,0:T(8,128)(2,1)S(1)} %bitcast.20, f32[128,512]{1,0:T(8,128)S(1)} %get-tuple-element.58.refs_4_, ...), custom_call_target="tpu_custom_call" | custom-call | flops 268435456 | bytes 2097152 | tf_op jit(solution)/shard_map/pallas_call | solution.py:198
  50.5 0.4 shard_map.70
  51.1 0.7 shard_map.71
  51.8 1.1 %collective-permute-done.23 = bf16[4,128,512]{2,1,0:T(8,128)(2,1)S(1)} collective-permute-done((bf16[4,128,512]{2,1,0:T(8,128)(2,1)S(1)}, bf16[4,128,512]{2,1,0:T(8,128)(2,1)S(1)}, u32[]{:S(2)}, u32[]{:S(2)}) %collective-permute-start.23) | collective-permute-done | bytes 524320 | tf_op jit(solution)/shard_map/ppermute | solution.py:285
  53.1 1.4 %collective-permute-start.26 = (bf16[4,128,512]{2,1,0:T(8,128)(2,1)S(1)}, bf16[4,128,512]{2,1,0:T(8,128)(2,1)S(1)}, u32[]{:S(2)}, u32[]{:S(2)}) collective-permute-start(bf16[4,128,512]{2,1,0:T(8,128)(2,1)S(1)} %add_convert_fusion.1), channel_id=1, source_target_pairs={{0,2},{1,5},{2,0},{3,7},{4,6},{5,1},{6,4},{7,3},{8,10},{9,13},{10,... | collective-permute-start | bytes 1572872 | tf_op jit(solution)/shard_map/ppermute | solution.py:288
  54.4 0.4 shard_map.72
  54.9 3.5 %shard_map.73 = (bf16[4,128,512]{2,1,0:T(8,128)(2,1)S(1)}, bf16[2,128,512]{2,1,0:T(8,128)(2,1)S(1)}, bf16[2,128,512]{2,1,0:T(8,128)(2,1)S(1)}) custom-call(s32[9]{0:T(128)S(1)} %stack.42.where.refs_0_, bf16[128,512]{1,0:T(8,128)(2,1)S(1)} %shard_map.69.attended, bf16[512,16384]{1,0:T(8,128)(2,1)} %weight.3), custom_call_target="tpu_custom_call" | custom-call | flops 536870912 | bytes 4194304 | tf_op jit(solution)/shard_map/pallas_call | solution.py:252
  58.5 0.5 collective-permute-start.25
  59.1 3.5 %shard_map.74 = (f32[4,128,512]{2,1,0:T(8,128)S(1)}, f32[2,128,512]{2,1,0:T(8,128)S(1)}, f32[2,128,512]{2,1,0:T(8,128)S(1)}) custom-call(s32[9]{0:T(128)S(1)} %stack.42.where.refs_0_, bf16[128,512]{1,0:T(8,128)(2,1)S(1)} %shard_map.69.attended, bf16[512,16384]{1,0:T(8,128)(2,1)} %weight.3), custom_call_target="tpu_custom_call" | custom-call | flops 536870912 | bytes 4194304 | tf_op jit(solution)/shard_map/pallas_call | solution.py:252
  62.8 1.4 %collective-permute-start.32 = (bf16[2,128,512]{2,1,0:T(8,128)(2,1)S(1)}, bf16[2,128,512]{2,1,0:T(8,128)(2,1)S(1)}, u32[]{:S(2)}, u32[]{:S(2)}) collective-permute-start(bf16[2,128,512]{2,1,0:T(8,128)(2,1)S(1)} %add_convert_fusion.4), channel_id=1, source_target_pairs={{0,4},{1,3},{2,6},{3,1},{4,0},{5,7},{6,2},{7,5},{8,12},{9,11},{10,... | collective-permute-start | bytes 786440 | tf_op jit(solution)/shard_map/ppermute | solution.py:288
  64.3 1.0 %collective-permute-start.28 = (bf16[4,128,512]{2,1,0:T(8,128)(2,1)S(1)}, bf16[4,128,512]{2,1,0:T(8,128)(2,1)S(1)}, u32[]{:S(2)}, u32[]{:S(2)}) collective-permute-start(bf16[4,128,512]{2,1,0:T(8,128)(2,1)S(1)} %add_convert_fusion), channel_id=1, source_target_pairs={{0,2},{1,5},{2,0},{3,7},{4,6},{5,1},{6,4},{7,3},{8,10},{9,13},{10,... | collective-permute-start | bytes 1572872 | tf_op jit(solution)/shard_map/ppermute | solution.py:288
  65.4 0.5 collective-permute-start.29
  65.9 5.9 %collective-permute-done.32 = bf16[2,128,512]{2,1,0:T(8,128)(2,1)S(1)} collective-permute-done((bf16[2,128,512]{2,1,0:T(8,128)(2,1)S(1)}, bf16[2,128,512]{2,1,0:T(8,128)(2,1)S(1)}, u32[]{:S(2)}, u32[]{:S(2)}) %collective-permute-start.32) | collective-permute-done | bytes 262176 | tf_op jit(solution)/shard_map/ppermute | solution.py:288
  71.9 1.0 %collective-permute-start.33 = (bf16[2,128,512]{2,1,0:T(8,128)(2,1)S(1)}, bf16[2,128,512]{2,1,0:T(8,128)(2,1)S(1)}, u32[]{:S(2)}, u32[]{:S(2)}) collective-permute-start(bf16[2,128,512]{2,1,0:T(8,128)(2,1)S(1)} %add_convert_fusion.2), channel_id=1, source_target_pairs={{0,16},{1,9},{2,18},{3,11},{4,20},{5,13},{6,22},{7,15},{8,24},{9,1... | collective-permute-start | bytes 786440 | tf_op jit(solution)/shard_map/ppermute | solution.py:288
  72.9 1.3 %collective-permute-done.28 = bf16[4,128,512]{2,1,0:T(8,128)(2,1)S(1)} collective-permute-done((bf16[4,128,512]{2,1,0:T(8,128)(2,1)S(1)}, bf16[4,128,512]{2,1,0:T(8,128)(2,1)S(1)}, u32[]{:S(2)}, u32[]{:S(2)}) %collective-permute-start.28) | collective-permute-done | bytes 524320 | tf_op jit(solution)/shard_map/ppermute | solution.py:288
  74.4 1.4 %collective-permute-start.30 = (bf16[2,128,512]{2,1,0:T(8,128)(2,1)S(1)}, bf16[2,128,512]{2,1,0:T(8,128)(2,1)S(1)}, u32[]{:S(2)}, u32[]{:S(2)}) collective-permute-start(bf16[2,128,512]{2,1,0:T(8,128)(2,1)S(1)} %add_convert_fusion.3), channel_id=1, source_target_pairs={{0,4},{1,3},{2,6},{3,1},{4,0},{5,7},{6,2},{7,5},{8,12},{9,11},{10,... | collective-permute-start | bytes 786440 | tf_op jit(solution)/shard_map/ppermute | solution.py:288
  75.8 6.3 %collective-permute-done.33 = bf16[2,128,512]{2,1,0:T(8,128)(2,1)S(1)} collective-permute-done((bf16[2,128,512]{2,1,0:T(8,128)(2,1)S(1)}, bf16[2,128,512]{2,1,0:T(8,128)(2,1)S(1)}, u32[]{:S(2)}, u32[]{:S(2)}) %collective-permute-start.33) | collective-permute-done | bytes 262176 | tf_op jit(solution)/shard_map/ppermute | solution.py:288
  82.3 0.8 collective-permute-start.34
  83.1 4.2 %collective-permute-done.34 = bf16[1,128,512]{2,1,0:T(8,128)(2,1)S(1)} collective-permute-done((bf16[1,128,512]{2,1,0:T(8,128)(2,1)S(1)}, bf16[1,128,512]{2,1,0:T(8,128)(2,1)S(1)}, u32[]{:S(2)}, u32[]{:S(2)}) %collective-permute-start.34) | collective-permute-done | bytes 131104 | tf_op jit(solution)/shard_map/ppermute | solution.py:288
  87.3 0.7 fusion.1
  (65 shorter events, 2.7 us)
Async XLA Ops:
  2.8 40.7 %slice-start = ((s8[16777216]{0:T(1024)(128)(4,1)}), s8[4194304]{0:T(1024)(128)(4,1)S(1)}, s32[]{:S(2)}) async-start(s8[16777216]{0:T(1024)(128)(4,1)} %bitcast.19), calls=%async_computation | async-start | bytes 8388608
  2.8 5.9 %collective-permute-start.1 = (bf16[1,128,512]{2,1,0:T(8,128)(2,1)S(1)}, bf16[1,128,512]{2,1,0:T(8,128)(2,1)S(1)}, u32[]{:S(2)}, u32[]{:S(2)}) collective-permute-start(bf16[1,128,512]{2,1,0:T(8,128)(2,1)S(1)} %bitcast.21), channel_id=1, source_target_pairs={{0,2},{1,5},{2,0},{3,7},{4,6},{5,1},{6,4},{7,3},{8,10},{9,13},{10,... | collective-permute-start | bytes 393224 | tf_op jit(solution)/shard_map/ppermute | solution.py:288
  5.8 5.6 %collective-permute-start = (bf16[1,128,512]{2,1,0:T(8,128)(2,1)S(1)}, bf16[1,128,512]{2,1,0:T(8,128)(2,1)S(1)}, u32[]{:S(2)}, u32[]{:S(2)}) collective-permute-start(bf16[1,128,512]{2,1,0:T(8,128)(2,1)S(1)} %bitcast.22), channel_id=1, source_target_pairs={{0,8},{1,17},{2,10},{3,19},{4,12},{5,21},{6,14},{7,23},{8,0},{9,25... | collective-permute-start | bytes 393224 | tf_op jit(solution)/shard_map/ppermute | solution.py:288
  7.4 13.6 %collective-permute-start.17 = (f32[8,128,128]{2,1,0:T(8,128)S(1)}, f32[8,128,128]{2,1,0:T(8,128)S(1)}, u32[]{:S(2)}, u32[]{:S(2)}) collective-permute-start(f32[8,128,128]{2,1,0:T(8,128)S(1)} %get-tuple-element.61), channel_id=1, source_target_pairs={{0,1},{1,0},{2,3},{3,2},{4,5},{5,4},{6,7},{7,6},{8,9},{9,8},{10,11... | collective-permute-start | bytes 1572872 | tf_op jit(solution)/shard_map/ppermute | solution.py:285
  8.8 7.6 %collective-permute-start.4 = (bf16[2,128,512]{2,1,0:T(8,128)(2,1)S(1)}, bf16[2,128,512]{2,1,0:T(8,128)(2,1)S(1)}, u32[]{:S(2)}, u32[]{:S(2)}) collective-permute-start(bf16[2,128,512]{2,1,0:T(8,128)(2,1)S(1)} %pad_maximum_fusion.1), channel_id=1, source_target_pairs={{0,4},{1,3},{2,6},{3,1},{4,0},{5,7},{6,2},{7,5},{8,12},{9,11},{10,... | collective-permute-start | bytes 786440 | tf_op jit(solution)/shard_map/ppermute | solution.py:288
  11.4 5.0 %collective-permute-start.3 = (bf16[1,128,512]{2,1,0:T(8,128)(2,1)S(1)}, bf16[1,128,512]{2,1,0:T(8,128)(2,1)S(1)}, u32[]{:S(2)}, u32[]{:S(2)}) collective-permute-start(bf16[1,128,512]{2,1,0:T(8,128)(2,1)S(1)} %collective-permute-done.refs_5_), channel_id=1, source_target_pairs={{0,2},{1,5},{2,0},{3,7},{4,6},{5,1},{6,4},{7,3},{8,10},{9,13},{10,... | collective-permute-start | bytes 393224 | tf_op jit(solution)/shard_map/ppermute | solution.py:288
  16.4 7.9 %collective-permute-start.5 = (bf16[2,128,512]{2,1,0:T(8,128)(2,1)S(1)}, bf16[2,128,512]{2,1,0:T(8,128)(2,1)S(1)}, u32[]{:S(2)}, u32[]{:S(2)}) collective-permute-start(bf16[2,128,512]{2,1,0:T(8,128)(2,1)S(1)} %get-tuple-element.83), channel_id=1, source_target_pairs={{0,4},{1,3},{2,6},{3,1},{4,0},{5,7},{6,2},{7,5},{8,12},{9,11},{10,... | collective-permute-start | bytes 786440 | tf_op jit(solution)/shard_map/ppermute | solution.py:288
  18.8 10.1 %collective-permute-start.2 = (bf16[2,128,512]{2,1,0:T(8,128)(2,1)S(1)}, bf16[2,128,512]{2,1,0:T(8,128)(2,1)S(1)}, u32[]{:S(2)}, u32[]{:S(2)}) collective-permute-start(bf16[2,128,512]{2,1,0:T(8,128)(2,1)S(1)} %get-tuple-element.84), channel_id=1, source_target_pairs={{0,16},{1,9},{2,18},{3,11},{4,20},{5,13},{6,22},{7,15},{8,24},{9,1... | collective-permute-start | bytes 786440 | tf_op jit(solution)/shard_map/ppermute | solution.py:288
  21.1 9.3 %collective-permute-start.18 = (bf16[4,128,128]{2,1,0:T(8,128)(2,1)S(1)}, bf16[4,128,128]{2,1,0:T(8,128)(2,1)S(1)}, u32[]{:S(2)}, u32[]{:S(2)}) collective-permute-start(bf16[4,128,128]{2,1,0:T(8,128)(2,1)S(1)} %slice.87), channel_id=1, source_target_pairs={{0,4},{1,5},{2,6},{3,7},{4,0},{5,1},{6,2},{7,3},{8,12},{9,13},{10,... | collective-permute-start | bytes 393224 | tf_op jit(solution)/shard_map/ppermute | solution.py:285
  28.9 7.5 %collective-permute-start.6 = (bf16[2,128,512]{2,1,0:T(8,128)(2,1)S(1)}, bf16[2,128,512]{2,1,0:T(8,128)(2,1)S(1)}, u32[]{:S(2)}, u32[]{:S(2)}) collective-permute-start(bf16[2,128,512]{2,1,0:T(8,128)(2,1)S(1)} %collective-permute-done.2.refs_2_), channel_id=1, source_target_pairs={{0,2},{1,5},{2,0},{3,7},{4,6},{5,1},{6,4},{7,3},{8,10},{9,13},{10,... | collective-permute-start | bytes 786440 | tf_op jit(solution)/shard_map/ppermute | solution.py:288
  30.4 13.1 %slice-start.1 = ((s8[16777216]{0:T(1024)(128)(4,1)}), s8[4194304]{0:T(1024)(128)(4,1)S(1)}, s32[]{:S(2)}) async-start(s8[16777216]{0:T(1024)(128)(4,1)} %bitcast.19), calls=%async_computation.1 | async-start | bytes 8388608
  30.4 13.1 %slice-start.2 = ((s8[16777216]{0:T(1024)(128)(4,1)}), s8[4194304]{0:T(1024)(128)(4,1)S(1)}, s32[]{:S(2)}) async-start(s8[16777216]{0:T(1024)(128)(4,1)} %bitcast.19), calls=%async_computation.2 | async-start | bytes 8388608
  30.4 13.1 %slice-start.3 = ((s8[16777216]{0:T(1024)(128)(4,1)}), s8[4194304]{0:T(1024)(128)(4,1)S(1)}, s32[]{:S(2)}) async-start(s8[16777216]{0:T(1024)(128)(4,1)} %bitcast.19), calls=%async_computation.3 | async-start | bytes 8388608
  30.4 5.9 %collective-permute-start.19 = (bf16[2,128,128]{2,1,0:T(8,128)(2,1)S(1)}, bf16[2,128,128]{2,1,0:T(8,128)(2,1)S(1)}, u32[]{:S(2)}, u32[]{:S(2)}) collective-permute-start(bf16[2,128,128]{2,1,0:T(8,128)(2,1)S(1)} %slice.88), channel_id=1, source_target_pairs={{0,16},{1,9},{2,18},{3,11},{4,20},{5,13},{6,22},{7,15},{8,24},{9,1... | collective-permute-start | bytes 196616 | tf_op jit(solution)/shard_map/ppermute | solution.py:288
  30.8 9.2 %collective-permute-start.10 = (bf16[1,128,512]{2,1,0:T(8,128)(2,1)S(1)}, bf16[1,128,512]{2,1,0:T(8,128)(2,1)S(1)}, u32[]{:S(2)}, u32[]{:S(2)}) collective-permute-start(bf16[1,128,512]{2,1,0:T(8,128)(2,1)S(1)} %bitcast.25), channel_id=1, source_target_pairs={{0,1},{1,0},{2,3},{3,2},{4,5},{5,4},{6,7},{7,6},{8,9},{9,8},{10,11... | collective-permute-start | bytes 393224 | tf_op jit(solution)/shard_map/ppermute | solution.py:285
  30.8 9.8 %collective-permute-start.11 = (bf16[1,128,512]{2,1,0:T(8,128)(2,1)S(1)}, bf16[1,128,512]{2,1,0:T(8,128)(2,1)S(1)}, u32[]{:S(2)}, u32[]{:S(2)}) collective-permute-start(bf16[1,128,512]{2,1,0:T(8,128)(2,1)S(1)} %collective-permute-done.1.refs_3_), channel_id=1, source_target_pairs={{0,1},{1,0},{2,3},{3,2},{4,5},{5,4},{6,7},{7,6},{8,9},{9,8},{10,11... | collective-permute-start | bytes 393224 | tf_op jit(solution)/shard_map/ppermute | solution.py:285
  36.4 10.4 %collective-permute-start.7 = (bf16[4,128,512]{2,1,0:T(8,128)(2,1)S(1)}, bf16[4,128,512]{2,1,0:T(8,128)(2,1)S(1)}, u32[]{:S(2)}, u32[]{:S(2)}) collective-permute-start(bf16[4,128,512]{2,1,0:T(8,128)(2,1)S(1)} %pad_maximum_fusion), channel_id=1, source_target_pairs={{0,4},{1,3},{2,6},{3,1},{4,0},{5,7},{6,2},{7,5},{8,12},{9,11},{10,... | collective-permute-start | bytes 1572872 | tf_op jit(solution)/shard_map/ppermute | solution.py:288
  36.5 5.4 %collective-permute-start.20 = (bf16[1,128,128]{2,1,0:T(8,128)(2,1)S(1)}, bf16[1,128,128]{2,1,0:T(8,128)(2,1)S(1)}, u32[]{:S(2)}, u32[]{:S(2)}) collective-permute-start(bf16[1,128,128]{2,1,0:T(8,128)(2,1)S(1)} %slice.89), channel_id=1, source_target_pairs={{0,8},{1,17},{2,10},{3,19},{4,12},{5,21},{6,14},{7,23},{8,0},{9,25... | collective-permute-start | bytes 98312 | tf_op jit(solution)/shard_map/ppermute | solution.py:288
  40.0 1.9 %collective-permute-start.13 = (bf16[1,128,512]{2,1,0:T(8,128)(2,1)S(1)}, bf16[1,128,512]{2,1,0:T(8,128)(2,1)S(1)}, u32[]{:S(2)}, u32[]{:S(2)}) collective-permute-start(bf16[1,128,512]{2,1,0:T(8,128)(2,1)S(1)} %collective-permute-done.refs_5_), channel_id=1, source_target_pairs={{0,1},{1,0},{2,3},{3,2},{4,5},{5,4},{6,7},{7,6},{8,9},{9,8},{10,11... | collective-permute-start | bytes 393224 | tf_op jit(solution)/shard_map/ppermute | solution.py:285
  40.0 2.5 %collective-permute-start.14 = (bf16[1,128,512]{2,1,0:T(8,128)(2,1)S(1)}, bf16[1,128,512]{2,1,0:T(8,128)(2,1)S(1)}, u32[]{:S(2)}, u32[]{:S(2)}) collective-permute-start(bf16[1,128,512]{2,1,0:T(8,128)(2,1)S(1)} %collective-permute-done.3.refs_6_), channel_id=1, source_target_pairs={{0,1},{1,0},{2,3},{3,2},{4,5},{5,4},{6,7},{7,6},{8,9},{9,8},{10,11... | collective-permute-start | bytes 393224 | tf_op jit(solution)/shard_map/ppermute | solution.py:285
  40.6 2.1 %collective-permute-start.12 = (bf16[2,128,512]{2,1,0:T(8,128)(2,1)S(1)}, bf16[2,128,512]{2,1,0:T(8,128)(2,1)S(1)}, u32[]{:S(2)}, u32[]{:S(2)}) collective-permute-start(bf16[2,128,512]{2,1,0:T(8,128)(2,1)S(1)} %collective-permute-done.4.refs_4_), channel_id=1, source_target_pairs={{0,1},{1,0},{2,3},{3,2},{4,5},{5,4},{6,7},{7,6},{8,9},{9,8},{10,11... | collective-permute-start | bytes 786440 | tf_op jit(solution)/shard_map/ppermute | solution.py:285
  41.9 1.5 %collective-permute-start.15 = (bf16[2,128,512]{2,1,0:T(8,128)(2,1)S(1)}, bf16[2,128,512]{2,1,0:T(8,128)(2,1)S(1)}, u32[]{:S(2)}, u32[]{:S(2)}) collective-permute-start(bf16[2,128,512]{2,1,0:T(8,128)(2,1)S(1)} %collective-permute-done.5.refs_7_), channel_id=1, source_target_pairs={{0,1},{1,0},{2,3},{3,2},{4,5},{5,4},{6,7},{7,6},{8,9},{9,8},{10,11... | collective-permute-start | bytes 786440 | tf_op jit(solution)/shard_map/ppermute | solution.py:285
  42.0 3.5 %collective-permute-start.8 = (bf16[2,128,512]{2,1,0:T(8,128)(2,1)S(1)}, bf16[2,128,512]{2,1,0:T(8,128)(2,1)S(1)}, u32[]{:S(2)}, u32[]{:S(2)}) collective-permute-start(bf16[2,128,512]{2,1,0:T(8,128)(2,1)S(1)} %collective-permute-done.2.refs_2_), channel_id=1, source_target_pairs={{0,1},{1,0},{2,3},{3,2},{4,5},{5,4},{6,7},{7,6},{8,9},{9,8},{10,11... | collective-permute-start | bytes 786440 | tf_op jit(solution)/shard_map/ppermute | solution.py:285
  42.5 2.9 %collective-permute-start.9 = (bf16[2,128,512]{2,1,0:T(8,128)(2,1)S(1)}, bf16[2,128,512]{2,1,0:T(8,128)(2,1)S(1)}, u32[]{:S(2)}, u32[]{:S(2)}) collective-permute-start(bf16[2,128,512]{2,1,0:T(8,128)(2,1)S(1)} %collective-permute-done.6.refs_3_), channel_id=1, source_target_pairs={{0,1},{1,0},{2,3},{3,2},{4,5},{5,4},{6,7},{7,6},{8,9},{9,8},{10,11... | collective-permute-start | bytes 786440 | tf_op jit(solution)/shard_map/ppermute | solution.py:285
  42.6 4.6 %collective-permute-start.21 = (bf16[128,128]{1,0:T(8,128)(2,1)S(1)}, bf16[128,128]{1,0:T(8,128)(2,1)S(1)}, u32[]{:S(2)}, u32[]{:S(2)}) collective-permute-start(bf16[128,128]{1,0:T(8,128)(2,1)S(1)} %fusion.5), channel_id=1, source_target_pairs={{0,2},{1,3},{2,0},{3,1},{4,6},{5,7},{6,4},{7,5},{8,10},{9,11},{10,... | collective-permute-start | bytes 98312 | tf_op jit(solution)/shard_map/ppermute | solution.py:285
  46.8 2.1 %collective-permute-start.16 = (bf16[4,128,512]{2,1,0:T(8,128)(2,1)S(1)}, bf16[4,128,512]{2,1,0:T(8,128)(2,1)S(1)}, u32[]{:S(2)}, u32[]{:S(2)}) collective-permute-start(bf16[4,128,512]{2,1,0:T(8,128)(2,1)S(1)} %collective-permute-done.7.refs_2_), channel_id=1, source_target_pairs={{0,1},{1,0},{2,3},{3,2},{4,5},{5,4},{6,7},{7,6},{8,9},{9,8},{10,11... | collective-permute-start | bytes 1572872 | tf_op jit(solution)/shard_map/ppermute | solution.py:285
  47.3 1.6 %collective-permute-start.22 = (f32[128,128]{1,0:T(8,128)S(1)}, f32[128,128]{1,0:T(8,128)S(1)}, u32[]{:S(2)}, u32[]{:S(2)}) collective-permute-start(f32[128,128]{1,0:T(8,128)S(1)} %convert_add_fusion.1.refs_6_), channel_id=1, source_target_pairs={{0,1},{1,0},{2,3},{3,2},{4,5},{5,4},{6,7},{7,6},{8,9},{9,8},{10,11... | collective-permute-start | bytes 196616 | tf_op jit(solution)/shard_map/ppermute | solution.py:285
  50.9 2.0 %collective-permute-start.23 = (bf16[4,128,512]{2,1,0:T(8,128)(2,1)S(1)}, bf16[4,128,512]{2,1,0:T(8,128)(2,1)S(1)}, u32[]{:S(2)}, u32[]{:S(2)}) collective-permute-start(bf16[4,128,512]{2,1,0:T(8,128)(2,1)S(1)} %shard_map.70), channel_id=1, source_target_pairs={{0,1},{1,0},{2,3},{3,2},{4,5},{5,4},{6,7},{7,6},{8,9},{9,8},{10,11... | collective-permute-start | bytes 1572872 | tf_op jit(solution)/shard_map/ppermute | solution.py:285
  53.1 9.6 %collective-permute-start.26 = (bf16[4,128,512]{2,1,0:T(8,128)(2,1)S(1)}, bf16[4,128,512]{2,1,0:T(8,128)(2,1)S(1)}, u32[]{:S(2)}, u32[]{:S(2)}) collective-permute-start(bf16[4,128,512]{2,1,0:T(8,128)(2,1)S(1)} %add_convert_fusion.1), channel_id=1, source_target_pairs={{0,2},{1,5},{2,0},{3,7},{4,6},{5,1},{6,4},{7,3},{8,10},{9,13},{10,... | collective-permute-start | bytes 1572872 | tf_op jit(solution)/shard_map/ppermute | solution.py:288
  58.4 5.7 %collective-permute-start.27 = (bf16[4,128,512]{2,1,0:T(8,128)(2,1)S(1)}, bf16[4,128,512]{2,1,0:T(8,128)(2,1)S(1)}, u32[]{:S(2)}, u32[]{:S(2)}) collective-permute-start(bf16[4,128,512]{2,1,0:T(8,128)(2,1)S(1)} %get-tuple-element.72), channel_id=1, source_target_pairs={{0,1},{1,0},{2,3},{3,2},{4,5},{5,4},{6,7},{7,6},{8,9},{9,8},{10,11... | collective-permute-start | bytes 1572872 | tf_op jit(solution)/shard_map/ppermute | solution.py:285
  58.5 4.1 %collective-permute-start.25 = (bf16[2,128,512]{2,1,0:T(8,128)(2,1)S(1)}, bf16[2,128,512]{2,1,0:T(8,128)(2,1)S(1)}, u32[]{:S(2)}, u32[]{:S(2)}) collective-permute-start(bf16[2,128,512]{2,1,0:T(8,128)(2,1)S(1)} %get-tuple-element.78), channel_id=1, source_target_pairs={{0,1},{1,0},{2,3},{3,2},{4,5},{5,4},{6,7},{7,6},{8,9},{9,8},{10,11... | collective-permute-start | bytes 786440 | tf_op jit(solution)/shard_map/ppermute | solution.py:285
  59.0 6.9 %collective-permute-start.31 = (bf16[2,128,512]{2,1,0:T(8,128)(2,1)S(1)}, bf16[2,128,512]{2,1,0:T(8,128)(2,1)S(1)}, u32[]{:S(2)}, u32[]{:S(2)}) collective-permute-start(bf16[2,128,512]{2,1,0:T(8,128)(2,1)S(1)} %get-tuple-element.70), channel_id=1, source_target_pairs={{0,1},{1,0},{2,3},{3,2},{4,5},{5,4},{6,7},{7,6},{8,9},{9,8},{10,11... | collective-permute-start | bytes 786440 | tf_op jit(solution)/shard_map/ppermute | solution.py:285
  62.8 9.0 %collective-permute-start.32 = (bf16[2,128,512]{2,1,0:T(8,128)(2,1)S(1)}, bf16[2,128,512]{2,1,0:T(8,128)(2,1)S(1)}, u32[]{:S(2)}, u32[]{:S(2)}) collective-permute-start(bf16[2,128,512]{2,1,0:T(8,128)(2,1)S(1)} %add_convert_fusion.4), channel_id=1, source_target_pairs={{0,4},{1,3},{2,6},{3,1},{4,0},{5,7},{6,2},{7,5},{8,12},{9,11},{10,... | collective-permute-start | bytes 786440 | tf_op jit(solution)/shard_map/ppermute | solution.py:288
  64.3 9.9 %collective-permute-start.28 = (bf16[4,128,512]{2,1,0:T(8,128)(2,1)S(1)}, bf16[4,128,512]{2,1,0:T(8,128)(2,1)S(1)}, u32[]{:S(2)}, u32[]{:S(2)}) collective-permute-start(bf16[4,128,512]{2,1,0:T(8,128)(2,1)S(1)} %add_convert_fusion), channel_id=1, source_target_pairs={{0,2},{1,5},{2,0},{3,7},{4,6},{5,1},{6,4},{7,3},{8,10},{9,13},{10,... | collective-permute-start | bytes 1572872 | tf_op jit(solution)/shard_map/ppermute | solution.py:288
  65.4 10.4 %collective-permute-start.24 = (bf16[2,128,512]{2,1,0:T(8,128)(2,1)S(1)}, bf16[2,128,512]{2,1,0:T(8,128)(2,1)S(1)}, u32[]{:S(2)}, u32[]{:S(2)}) collective-permute-start(bf16[2,128,512]{2,1,0:T(8,128)(2,1)S(1)} %get-tuple-element.75), channel_id=1, source_target_pairs={{0,1},{1,0},{2,3},{3,2},{4,5},{5,4},{6,7},{7,6},{8,9},{9,8},{10,11... | collective-permute-start | bytes 786440 | tf_op jit(solution)/shard_map/ppermute | solution.py:285
  65.4 7.6 %collective-permute-start.29 = (bf16[2,128,512]{2,1,0:T(8,128)(2,1)S(1)}, bf16[2,128,512]{2,1,0:T(8,128)(2,1)S(1)}, u32[]{:S(2)}, u32[]{:S(2)}) collective-permute-start(bf16[2,128,512]{2,1,0:T(8,128)(2,1)S(1)} %get-tuple-element.81), channel_id=1, source_target_pairs={{0,1},{1,0},{2,3},{3,2},{4,5},{5,4},{6,7},{7,6},{8,9},{9,8},{10,11... | collective-permute-start | bytes 786440 | tf_op jit(solution)/shard_map/ppermute | solution.py:285
  71.9 10.1 %collective-permute-start.33 = (bf16[2,128,512]{2,1,0:T(8,128)(2,1)S(1)}, bf16[2,128,512]{2,1,0:T(8,128)(2,1)S(1)}, u32[]{:S(2)}, u32[]{:S(2)}) collective-permute-start(bf16[2,128,512]{2,1,0:T(8,128)(2,1)S(1)} %add_convert_fusion.2), channel_id=1, source_target_pairs={{0,16},{1,9},{2,18},{3,11},{4,20},{5,13},{6,22},{7,15},{8,24},{9,1... | collective-permute-start | bytes 786440 | tf_op jit(solution)/shard_map/ppermute | solution.py:288
  74.4 7.7 %collective-permute-start.30 = (bf16[2,128,512]{2,1,0:T(8,128)(2,1)S(1)}, bf16[2,128,512]{2,1,0:T(8,128)(2,1)S(1)}, u32[]{:S(2)}, u32[]{:S(2)}) collective-permute-start(bf16[2,128,512]{2,1,0:T(8,128)(2,1)S(1)} %add_convert_fusion.3), channel_id=1, source_target_pairs={{0,4},{1,3},{2,6},{3,1},{4,0},{5,7},{6,2},{7,5},{8,12},{9,11},{10,... | collective-permute-start | bytes 786440 | tf_op jit(solution)/shard_map/ppermute | solution.py:288
  82.3 5.0 %collective-permute-start.34 = (bf16[1,128,512]{2,1,0:T(8,128)(2,1)S(1)}, bf16[1,128,512]{2,1,0:T(8,128)(2,1)S(1)}, u32[]{:S(2)}, u32[]{:S(2)}) collective-permute-start(bf16[1,128,512]{2,1,0:T(8,128)(2,1)S(1)} %slice.86), channel_id=1, source_target_pairs={{0,8},{1,17},{2,10},{3,19},{4,12},{5,21},{6,14},{7,23},{8,0},{9,25... | collective-permute-start | bytes 393224 | tf_op jit(solution)/shard_map/ppermute | solution.py:288

commit v12 on v9

--- a/solution.py
+++ b/solution.py
@@ -334,11 +334,8 @@
         return kv[half:] + send(kv[:half].astype(bf16), way).astype(f32)
 
     kv = halved(kv_keep + swap(kv_send, CORE), swap, bits[shared])
-    far_blocks, far_symbols = fetched(where, wo, width, columns_of(far))
     row = jnp.stack([act] + [swap(raw, o) for o in low[1:]])
     row = jnp.concatenate([row, along(row, 0)])
-    row, kv, far_blocks = lax.optimization_barrier((row, kv, far_blocks))
-    far_held = (far_blocks, far_symbols)
     groups = []
     for offsets in (near, far):
         if offsets is far:
@@ -350,13 +347,16 @@
             kv = kv[kv.shape[0] // 2 :] + got[:k, :, width:].astype(f32)
             side = turn(row, 0)
             kv = halved(kv, along, 0)
-            side, kv = lax.optimization_barrier((side, kv))
+            blocks, far_symbols = fetched(after(where, row), wo, width, columns_of(far))
+            side, kv, blocks = lax.optimization_barrier((side, kv, blocks))
+            far_held = (blocks, far_symbols)
         else:
             side = turn(row, 0)
         both = turn(jnp.concatenate([row, side]), 1)
         at = symbols_of(offsets)
         groups.append([(row, at[0]), (side, at[1]), (both, at[2] + at[3])])
     early, last = groups
+    early[2] = (after(early[2][0], blocks), early[2][1])
     partners = [swap(kv[0].astype(bf16), o) for o in combos(bits[1:shared])[1:]]
 
     call = functools.partial(query_call, where, gain, weight=wq)
@@ -409,10 +409,8 @@
     k = len(low)
     far_sum = added_up(far_sum[:k], along(far_sum[k:].astype(bf16), 0))
     far_got = along(far_sum.astype(bf16), 1)
-    got = [turn(near_two[k:], 1), turn(near_two[:k], 1)]
-    near_sum = added_up(*[x[k:] for x in near_home], got[0])
-    home_sum = added_up(*[x[:k] for x in near_home], got[1])
-    home_sum = added_up(home_sum, along(near_sum.astype(bf16), 0), far_got)
+    near_sum = added_up(*near_home, turn(near_two, 1))
+    home_sum = added_up(near_sum[:k], along(near_sum[k:].astype(bf16), 0), far_got)
     out = added_up(home_sum[0], *[swap(home_sum[i].astype(bf16), o) for i, o in enumerate(low) if o])
     return out.astype(bf16)
 

time: 83.5 us -> 82.1 us (0.983)
  waiting for transfers between devices: 30.6 us -> 24.6 us
  starting transfers between devices: 27.9 us -> 32.8 us
    ppermute x15 -> x14, waiting for transfers between devices: 28.5 us -> 22.6 us  [by_core(): lax.ppermute(x, 'wide', [(i, i ^ pair[(step + (i & CORE)) % 2]) for i in...]
    ppermute x15 -> x14, starting transfers between devices: 21.9 us -> 25.9 us  [by_core(): lax.ppermute(x, 'wide', [(i, i ^ pair[(step + (i & CORE)) % 2]) for i in...]
    ppermute x16, starting transfers between devices: 6.01 us -> 6.94 us  [swap(): return lax.ppermute(x, 'wide', [(i, i ^ offset) for i in range(n)])]
  transfers between devices with their start and end apart: 31 -> 30, of which waited for: 12 -> 12; matrix products, arithmetic and copies ran while one was open for 2% -> 2% of each run, Pallas kernels for 21% -> 21%
where the time goes in v12:
time: 82.1 us; the launch traced here: 81.9 us
  starting transfers between devices  32.8 us (40%)
  waiting for transfers between devices  24.6 us (30%)
  Pallas kernels  21.7 us (26%)
  other arithmetic  2.23 us (3%)
    ppermute x14, starting transfers between devices, by_core(): lax.ppermute(x, 'wide', [(i, i ^ pair[(step + (i & CORE)) % 2]) for i in...  25.9 us
    ppermute x14, waiting for transfers between devices, by_core(): lax.ppermute(x, 'wide', [(i, i ^ pair[(step + (i & CORE)) % 2]) for i in...  22.6 us
    pallas_call x5, Pallas kernels, output_call(): pl.pallas_call(kernel, out_shape=[jax.ShapeDtypeStruct((len(s), tokens, w...  8.67 us
    ppermute x16, starting transfers between devices, swap(): return lax.ppermute(x, 'wide', [(i, i ^ offset) for i in range(n)])  6.94 us
    pallas_call x4, Pallas kernels, query_call(): pl.pallas_call(functools.partial(query_kernel, places, bool(carry), bool(...  5.86 us
    pallas_call x1, Pallas kernels, fetched(): pl.pallas_call(functools.partial(fetch_kernel, symbols, width), out_shape...  4.47 us
    pallas_call x1, Pallas kernels, kv_terms(): pl.pallas_call(functools.partial(kv_kernel, shared), out_shape=[jax.Shape...  2.69 us
    ppermute x16, waiting for transfers between devices, swap(): return lax.ppermute(x, 'wide', [(i, i ^ offset) for i in range(n)])  2.03 us
  transfers between devices with their start and end apart: 30, of which 12 were waited for; matrix products, arithmetic and copies ran while one was open for 2% of the time, Pallas kernels for 21%

profile of v12, /device:TPU:0, one launch (start us, length us, event | category | flops | bytes accessed | tf_op | source)
XLA Modules:
  0.0 81.9 jit_solution(15298883506753116375)
XLA Ops:
  0.1 2.7 %shard_map.69 = (f32[8,128,128]{2,1,0:T(8,128)S(1)}, f32[8,128,128]{2,1,0:T(8,128)S(1)}, bf16[128,512]{1,0:T(8,128)(2,1)S(1)}, f32[1,16384]{1,0:T(1,128)S(1)}) custom-call(s32[9]{0:T(128)S(1)} %stack.42.where.refs_0_, bf16[128,512]{1,0:T(8,128)(2,1)} %act.1, f32[1,16384]{1,0:T(1,128)} %bitcast.22, bf16[512,1024]{1,0:T(8,128)(2,1)} %wk.1, bf16[512,1024]{1,0:T(8,128)(2,1)} %wv.1), custom_call_target="tpu_custom_call" | custom-call | flops 4294967296 | bytes 33554432 | tf_op jit(solution)/shard_map/pallas_call | solution.py:105
  2.8 0.5 collective-permute-start.1
  3.3 2.7 %collective-permute-start = (bf16[1,128,512]{2,1,0:T(8,128)(2,1)S(1)}, bf16[1,128,512]{2,1,0:T(8,128)(2,1)S(1)}, u32[]{:S(2)}, u32[]{:S(2)}) collective-permute-start(bf16[1,128,512]{2,1,0:T(8,128)(2,1)S(1)} %bitcast.18), channel_id=1, source_target_pairs={{0,8},{1,17},{2,10},{3,19},{4,12},{5,21},{6,14},{7,23},{8,0},{9,25... | collective-permute-start | bytes 393224 | tf_op jit(solution)/shard_map/ppermute | solution.py:288
  6.1 1.8 %collective-permute-start.2 = (bf16[4,128,128]{2,1,0:T(8,128)(2,1)S(1)}, bf16[4,128,128]{2,1,0:T(8,128)(2,1)S(1)}, u32[]{:S(2)}, u32[]{:S(2)}) collective-permute-start(bf16[4,128,128]{2,1,0:T(8,128)(2,1)S(1)} %slice.129), channel_id=1, source_target_pairs={{0,4},{1,5},{2,6},{3,7},{4,0},{5,1},{6,2},{7,3},{8,12},{9,13},{10,... | collective-permute-start | bytes 393224 | tf_op jit(solution)/shard_map/ppermute | solution.py:285
  7.9 2.1 %collective-permute-done = bf16[1,128,512]{2,1,0:T(8,128)(2,1)S(1)} collective-permute-done((bf16[1,128,512]{2,1,0:T(8,128)(2,1)S(1)}, bf16[1,128,512]{2,1,0:T(8,128)(2,1)S(1)}, u32[]{:S(2)}, u32[]{:S(2)}) %collective-permute-start) | collective-permute-done | bytes 131104 | tf_op jit(solution)/shard_map/ppermute | solution.py:288
  10.1 2.2 %collective-permute-start.9 = (bf16[2,128,512]{2,1,0:T(8,128)(2,1)S(1)}, bf16[2,128,512]{2,1,0:T(8,128)(2,1)S(1)}, u32[]{:S(2)}, u32[]{:S(2)}) collective-permute-start(bf16[2,128,512]{2,1,0:T(8,128)(2,1)S(1)} %pad_maximum_fusion.3.refs_2_), channel_id=1, source_target_pairs={{0,2},{1,5},{2,0},{3,7},{4,6},{5,1},{6,4},{7,3},{8,10},{9,13},{10,... | collective-permute-start | bytes 786440 | tf_op jit(solution)/shard_map/ppermute | solution.py:288
  12.4 2.3 %collective-permute-start.3 = (bf16[2,128,640]{2,1,0:T(8,128)(2,1)S(1)}, bf16[2,128,640]{2,1,0:T(8,128)(2,1)S(1)}, u32[]{:S(2)}, u32[]{:S(2)}) collective-permute-start(bf16[2,128,640]{2,1,0:T(8,128)(2,1)S(1)} %pad_maximum_fusion.2), channel_id=1, source_target_pairs={{0,16},{1,9},{2,18},{3,11},{4,20},{5,13},{6,22},{7,15},{8,24},{9,1... | collective-permute-start | bytes 983048 | tf_op jit(solution)/shard_map/ppermute | solution.py:288
  14.7 2.0 %collective-permute-done.9.refs_3_ = bf16[2,128,512]{2,1,0:T(8,128)(2,1)S(1)} collective-permute-done((bf16[2,128,512]{2,1,0:T(8,128)(2,1)S(1)}, bf16[2,128,512]{2,1,0:T(8,128)(2,1)S(1)}, u32[]{:S(2)}, u32[]{:S(2)}) %collective-permute-start.9) | collective-permute-done | bytes 262176 | tf_op jit(solution)/shard_map/ppermute | solution.py:288
  16.7 2.1 %collective-permute-start.10 = (bf16[4,128,512]{2,1,0:T(8,128)(2,1)S(1)}, bf16[4,128,512]{2,1,0:T(8,128)(2,1)S(1)}, u32[]{:S(2)}, u32[]{:S(2)}) collective-permute-start(bf16[4,128,512]{2,1,0:T(8,128)(2,1)S(1)} %pad_maximum_fusion.1), channel_id=1, source_target_pairs={{0,4},{1,3},{2,6},{3,1},{4,0},{5,7},{6,2},{7,5},{8,12},{9,11},{10,... | collective-permute-start | bytes 1572872 | tf_op jit(solution)/shard_map/ppermute | solution.py:288
  18.8 5.2 %collective-permute-done.3 = bf16[2,128,640]{2,1,0:T(8,128)(2,1)S(1)} collective-permute-done((bf16[2,128,640]{2,1,0:T(8,128)(2,1)S(1)}, bf16[2,128,640]{2,1,0:T(8,128)(2,1)S(1)}, u32[]{:S(2)}, u32[]{:S(2)}) %collective-permute-start.3) | collective-permute-done | bytes 327712 | tf_op jit(solution)/shard_map/ppermute | solution.py:288
  24.0 1.9 %collective-permute-start.4 = (bf16[2,128,512]{2,1,0:T(8,128)(2,1)S(1)}, bf16[2,128,512]{2,1,0:T(8,128)(2,1)S(1)}, u32[]{:S(2)}, u32[]{:S(2)}) collective-permute-start(bf16[2,128,512]{2,1,0:T(8,128)(2,1)S(1)} %slice.91.refs_2_), channel_id=1, source_target_pairs={{0,2},{1,5},{2,0},{3,7},{4,6},{5,1},{6,4},{7,3},{8,10},{9,13},{10,... | collective-permute-start | bytes 786440 | tf_op jit(solution)/shard_map/ppermute | solution.py:288
  26.2 4.5 %shard_map.70.weight = bf16[16,512,512]{2,1,0:T(8,128)(2,1)S(1)} custom-call(s32[9]{0:T(128)S(1)} %stack.42.where.refs_0_, bf16[512,16384]{1,0:T(8,128)(2,1)} %weight.3), custom_call_target="tpu_custom_call" | custom-call | bytes 16777216 | tf_op jit(solution)/shard_map/pallas_call | solution.py:67
  30.8 0.5 collective-permute-start.11
  31.3 1.7 %collective-permute-start.6 = (bf16[4,128,512]{2,1,0:T(8,128)(2,1)S(1)}, bf16[4,128,512]{2,1,0:T(8,128)(2,1)S(1)}, u32[]{:S(2)}, u32[]{:S(2)}) collective-permute-start(bf16[4,128,512]{2,1,0:T(8,128)(2,1)S(1)} %pad_maximum_fusion), channel_id=1, source_target_pairs={{0,4},{1,3},{2,6},{3,1},{4,0},{5,7},{6,2},{7,5},{8,12},{9,11},{10,... | collective-permute-start | bytes 1572872 | tf_op jit(solution)/shard_map/ppermute | solution.py:288
  33.0 0.5 collective-permute-start.7
  33.6 0.9 %collective-permute-done.12.refs_6_ = bf16[2,128,512]{2,1,0:T(8,128)(2,1)S(1)} collective-permute-done((bf16[2,128,512]{2,1,0:T(8,128)(2,1)S(1)}, bf16[2,128,512]{2,1,0:T(8,128)(2,1)S(1)}, u32[]{:S(2)}, u32[]{:S(2)}) %collective-permute-start.12) | collective-permute-done | bytes 262176 | tf_op jit(solution)/shard_map/ppermute | solution.py:285
  34.5 1.5 %collective-permute-start.15 = (bf16[128,128]{1,0:T(8,128)(2,1)S(1)}, bf16[128,128]{1,0:T(8,128)(2,1)S(1)}, u32[]{:S(2)}, u32[]{:S(2)}) collective-permute-start(bf16[128,128]{1,0:T(8,128)(2,1)S(1)} %bitcast_convert_fusion), channel_id=1, source_target_pairs={{0,2},{1,3},{2,0},{3,1},{4,6},{5,7},{6,4},{7,5},{8,10},{9,11},{10,... | collective-permute-start | bytes 98312 | tf_op jit(solution)/shard_map/ppermute | solution.py:285
  36.1 2.0 %shard_map.71 = (f32[128,512]{1,0:T(8,128)S(1)}, f32[128,128]{1,0:T(8,128)S(1)}) custom-call(s32[9]{0:T(128)S(1)} %stack.42.where.refs_0_, f32[1,16384]{1,0:T(1,128)S(1)} %get-tuple-element.60.refs_1_, bf16[2,128,512]{2,1,0:T(8,128)(2,1)S(1)} %pad_maximum_fusion.3.refs_2_, bf16[2,128,512]{2,1,0:T(8,128)(2,1)S(1)} %collective-permute-done.9.refs_3_, ...), custom_call_target="tpu_custom_call" | custom-call | flops 1073741824 | bytes 8388608 | tf_op jit(solution)/shard_map/pallas_call | solution.py:198
  38.1 1.3 %shard_map.72 = (f32[128,512]{1,0:T(8,128)S(1)}, f32[128,128]{1,0:T(8,128)S(1)}) custom-call(s32[9]{0:T(128)S(1)} %stack.42.where.refs_0_, f32[1,16384]{1,0:T(1,128)S(1)} %get-tuple-element.60.refs_1_, bf16[2,128,512]{2,1,0:T(8,128)(2,1)S(1)} %slice.91.refs_2_, bf16[2,128,512]{2,1,0:T(8,128)(2,1)S(1)} %collective-permute-done.4.refs_3_, ...), custom_call_target="tpu_custom_call" | custom-call | flops 536870912 | bytes 4194304 | tf_op jit(solution)/shard_map/pallas_call | solution.py:198
  39.4 1.2 %collective-permute-done.6.refs_2_ = bf16[4,128,512]{2,1,0:T(8,128)(2,1)S(1)} collective-permute-done((bf16[4,128,512]{2,1,0:T(8,128)(2,1)S(1)}, bf16[4,128,512]{2,1,0:T(8,128)(2,1)S(1)}, u32[]{:S(2)}, u32[]{:S(2)}) %collective-permute-start.6) | collective-permute-done | bytes 524320 | tf_op jit(solution)/shard_map/ppermute | solution.py:288
  40.6 0.3 fusion.6
  40.9 0.6 collective-permute-start.16
  41.6 1.0 %shard_map.73 = (f32[128,512]{1,0:T(8,128)S(1)}, f32[128,128]{1,0:T(8,128)S(1)}) custom-call(s32[9]{0:T(128)S(1)} %stack.42.where.refs_0_, f32[1,16384]{1,0:T(1,128)S(1)} %get-tuple-element.60.refs_1_, bf16[4,128,512]{2,1,0:T(8,128)(2,1)S(1)} %collective-permute-done.6.refs_2_, bf16[16384,512]{1,0:T(8,128)(2,1)S(1)} %bitcast.17, ...), custom_call_target="tpu_custom_call" | custom-call | flops 268435456 | bytes 2097152 | tf_op jit(solution)/shard_map/pallas_call | solution.py:198
  42.6 1.6 %shard_map.74.attended = bf16[128,512]{1,0:T(8,128)(2,1)S(1)} custom-call(s32[9]{0:T(128)S(1)} %stack.42.where.refs_0_, f32[1,16384]{1,0:T(1,128)S(1)} %get-tuple-element.60.refs_1_, bf16[4,128,512]{2,1,0:T(8,128)(2,1)S(1)} %collective-permute-done.14.refs_2_, bf16[16384,512]{1,0:T(8,128)(2,1)S(1)} %bitcast.17, f32[128,512]{1,0:T(8,128)S(1)} %get-tuple-element.75.refs_4_, ...), custom_call_target="tpu_custom_call" | custom-call | flops 268435456 | bytes 2097152 | tf_op jit(solution)/shard_map/pallas_call | solution.py:198
  44.2 0.4 shard_map.75
  44.6 0.2 collective-permute-start.17
  44.8 0.7 shard_map.76
  45.5 1.1 %collective-permute-done.17 = bf16[4,128,512]{2,1,0:T(8,128)(2,1)S(1)} collective-permute-done((bf16[4,128,512]{2,1,0:T(8,128)(2,1)S(1)}, bf16[4,128,512]{2,1,0:T(8,128)(2,1)S(1)}, u32[]{:S(2)}, u32[]{:S(2)}) %collective-permute-start.17) | collective-permute-done | bytes 524320 | tf_op jit(solution)/shard_map/ppermute | solution.py:285
  46.6 0.2 add_convert_fusion.1
  46.8 1.6 %collective-permute-start.20 = (bf16[4,128,512]{2,1,0:T(8,128)(2,1)S(1)}, bf16[4,128,512]{2,1,0:T(8,128)(2,1)S(1)}, u32[]{:S(2)}, u32[]{:S(2)}) collective-permute-start(bf16[4,128,512]{2,1,0:T(8,128)(2,1)S(1)} %add_convert_fusion.1), channel_id=1, source_target_pairs={{0,2},{1,5},{2,0},{3,7},{4,6},{5,1},{6,4},{7,3},{8,10},{9,13},{10,... | collective-permute-start | bytes 1572872 | tf_op jit(solution)/shard_map/ppermute | solution.py:288
  48.4 0.4 shard_map.77
  48.8 3.5 %shard_map.78 = (bf16[4,128,512]{2,1,0:T(8,128)(2,1)S(1)}, bf16[2,128,512]{2,1,0:T(8,128)(2,1)S(1)}, bf16[2,128,512]{2,1,0:T(8,128)(2,1)S(1)}) custom-call(s32[9]{0:T(128)S(1)} %stack.42.where.refs_0_, bf16[128,512]{1,0:T(8,128)(2,1)S(1)} %shard_map.74.attended, bf16[512,16384]{1,0:T(8,128)(2,1)} %weight.3), custom_call_target="tpu_custom_call" | custom-call | flops 536870912 | bytes 4194304 | tf_op jit(solution)/shard_map/pallas_call | solution.py:252
  52.5 0.5 collective-permute-start.19
  53.1 3.5 %shard_map.79 = (f32[4,128,512]{2,1,0:T(8,128)S(1)}, f32[2,128,512]{2,1,0:T(8,128)S(1)}, f32[2,128,512]{2,1,0:T(8,128)S(1)}) custom-call(s32[9]{0:T(128)S(1)} %stack.42.where.refs_0_, bf16[128,512]{1,0:T(8,128)(2,1)S(1)} %shard_map.74.attended, bf16[512,16384]{1,0:T(8,128)(2,1)} %weight.3), custom_call_target="tpu_custom_call" | custom-call | flops 536870912 | bytes 4194304 | tf_op jit(solution)/shard_map/pallas_call | solution.py:252
  56.7 1.6 %collective-permute-start.27 = (bf16[2,128,512]{2,1,0:T(8,128)(2,1)S(1)}, bf16[2,128,512]{2,1,0:T(8,128)(2,1)S(1)}, u32[]{:S(2)}, u32[]{:S(2)}) collective-permute-start(bf16[2,128,512]{2,1,0:T(8,128)(2,1)S(1)} %add_convert_fusion.3), channel_id=1, source_target_pairs={{0,4},{1,3},{2,6},{3,1},{4,0},{5,7},{6,2},{7,5},{8,12},{9,11},{10,... | collective-permute-start | bytes 786440 | tf_op jit(solution)/shard_map/ppermute | solution.py:288
  58.3 0.2 add_convert_fusion
  58.5 1.0 %collective-permute-start.22 = (bf16[4,128,512]{2,1,0:T(8,128)(2,1)S(1)}, bf16[4,128,512]{2,1,0:T(8,128)(2,1)S(1)}, u32[]{:S(2)}, u32[]{:S(2)}) collective-permute-start(bf16[4,128,512]{2,1,0:T(8,128)(2,1)S(1)} %add_convert_fusion), channel_id=1, source_target_pairs={{0,2},{1,5},{2,0},{3,7},{4,6},{5,1},{6,4},{7,3},{8,10},{9,13},{10,... | collective-permute-start | bytes 1572872 | tf_op jit(solution)/shard_map/ppermute | solution.py:288
  59.5 0.5 collective-permute-start.18
  60.1 5.6 %collective-permute-done.27 = bf16[2,128,512]{2,1,0:T(8,128)(2,1)S(1)} collective-permute-done((bf16[2,128,512]{2,1,0:T(8,128)(2,1)S(1)}, bf16[2,128,512]{2,1,0:T(8,128)(2,1)S(1)}, u32[]{:S(2)}, u32[]{:S(2)}) %collective-permute-start.27) | collective-permute-done | bytes 262176 | tf_op jit(solution)/shard_map/ppermute | solution.py:288
  65.8 2.3 %collective-permute-start.28 = (bf16[1,128,512]{2,1,0:T(8,128)(2,1)S(1)}, bf16[1,128,512]{2,1,0:T(8,128)(2,1)S(1)}, u32[]{:S(2)}, u32[]{:S(2)}) collective-permute-start(bf16[1,128,512]{2,1,0:T(8,128)(2,1)S(1)} %slice.127), channel_id=1, source_target_pairs={{0,8},{1,17},{2,10},{3,19},{4,12},{5,21},{6,14},{7,23},{8,0},{9,25... | collective-permute-start | bytes 393224 | tf_op jit(solution)/shard_map/ppermute | solution.py:288
  68.4 1.6 %collective-permute-start.24 = (bf16[2,128,512]{2,1,0:T(8,128)(2,1)S(1)}, bf16[2,128,512]{2,1,0:T(8,128)(2,1)S(1)}, u32[]{:S(2)}, u32[]{:S(2)}) collective-permute-start(bf16[2,128,512]{2,1,0:T(8,128)(2,1)S(1)} %add_convert_fusion.2), channel_id=1, source_target_pairs={{0,4},{1,3},{2,6},{3,1},{4,0},{5,7},{6,2},{7,5},{8,12},{9,11},{10,... | collective-permute-start | bytes 786440 | tf_op jit(solution)/shard_map/ppermute | solution.py:288
  69.9 1.2 %collective-permute-done.28 = bf16[1,128,512]{2,1,0:T(8,128)(2,1)S(1)} collective-permute-done((bf16[1,128,512]{2,1,0:T(8,128)(2,1)S(1)}, bf16[1,128,512]{2,1,0:T(8,128)(2,1)S(1)}, u32[]{:S(2)}, u32[]{:S(2)}) %collective-permute-start.28) | collective-permute-done | bytes 131104 | tf_op jit(solution)/shard_map/ppermute | solution.py:288
  71.1 3.0 %collective-permute-start.29 = (bf16[1,128,512]{2,1,0:T(8,128)(2,1)S(1)}, bf16[1,128,512]{2,1,0:T(8,128)(2,1)S(1)}, u32[]{:S(2)}, u32[]{:S(2)}) collective-permute-start(bf16[1,128,512]{2,1,0:T(8,128)(2,1)S(1)} %fusion), channel_id=1, source_target_pairs={{0,16},{1,9},{2,18},{3,11},{4,20},{5,13},{6,22},{7,15},{8,24},{9,1... | collective-permute-start | bytes 393224 | tf_op jit(solution)/shard_map/ppermute | solution.py:288
  74.1 0.7 collective-permute-done.24
  75.0 1.8 %collective-permute-start.25 = (bf16[1,128,512]{2,1,0:T(8,128)(2,1)S(1)}, bf16[1,128,512]{2,1,0:T(8,128)(2,1)S(1)}, u32[]{:S(2)}, u32[]{:S(2)}) collective-permute-start(bf16[1,128,512]{2,1,0:T(8,128)(2,1)S(1)} %slice.128), channel_id=1, source_target_pairs={{0,8},{1,17},{2,10},{3,19},{4,12},{5,21},{6,14},{7,23},{8,0},{9,25... | collective-permute-start | bytes 393224 | tf_op jit(solution)/shard_map/ppermute | solution.py:288
  76.8 0.3 collective-permute-done.29
  77.1 4.2 %collective-permute-done.25 = bf16[1,128,512]{2,1,0:T(8,128)(2,1)S(1)} collective-permute-done((bf16[1,128,512]{2,1,0:T(8,128)(2,1)S(1)}, bf16[1,128,512]{2,1,0:T(8,128)(2,1)S(1)}, u32[]{:S(2)}, u32[]{:S(2)}) %collective-permute-start.25) | collective-permute-done | bytes 131104 | tf_op jit(solution)/shard_map/ppermute | solution.py:288
  81.2 0.7 fusion.3
  (60 shorter events, 1.8 us)
Async XLA Ops:
  2.8 33.2 %slice-start = ((s8[16777216]{0:T(1024)(128)(4,1)}), s8[4194304]{0:T(1024)(128)(4,1)S(1)}, s32[]{:S(2)}) async-start(s8[16777216]{0:T(1024)(128)(4,1)} %bitcast.16), calls=%async_computation | async-start | bytes 8388608
  2.8 3.2 %collective-permute-start.1 = (f32[8,128,128]{2,1,0:T(8,128)S(1)}, f32[8,128,128]{2,1,0:T(8,128)S(1)}, u32[]{:S(2)}, u32[]{:S(2)}) collective-permute-start(f32[8,128,128]{2,1,0:T(8,128)S(1)} %get-tuple-element.63), channel_id=1, source_target_pairs={{0,1},{1,0},{2,3},{3,2},{4,5},{5,4},{6,7},{7,6},{8,9},{9,8},{10,11... | collective-permute-start | bytes 1572872 | tf_op jit(solution)/shard_map/ppermute | solution.py:285
  3.3 6.7 %collective-permute-start = (bf16[1,128,512]{2,1,0:T(8,128)(2,1)S(1)}, bf16[1,128,512]{2,1,0:T(8,128)(2,1)S(1)}, u32[]{:S(2)}, u32[]{:S(2)}) collective-permute-start(bf16[1,128,512]{2,1,0:T(8,128)(2,1)S(1)} %bitcast.18), channel_id=1, source_target_pairs={{0,8},{1,17},{2,10},{3,19},{4,12},{5,21},{6,14},{7,23},{8,0},{9,25... | collective-permute-start | bytes 393224 | tf_op jit(solution)/shard_map/ppermute | solution.py:288
  6.1 6.2 %collective-permute-start.2 = (bf16[4,128,128]{2,1,0:T(8,128)(2,1)S(1)}, bf16[4,128,128]{2,1,0:T(8,128)(2,1)S(1)}, u32[]{:S(2)}, u32[]{:S(2)}) collective-permute-start(bf16[4,128,128]{2,1,0:T(8,128)(2,1)S(1)} %slice.129), channel_id=1, source_target_pairs={{0,4},{1,5},{2,6},{3,7},{4,0},{5,1},{6,2},{7,3},{8,12},{9,13},{10,... | collective-permute-start | bytes 393224 | tf_op jit(solution)/shard_map/ppermute | solution.py:285
  10.1 6.6 %collective-permute-start.9 = (bf16[2,128,512]{2,1,0:T(8,128)(2,1)S(1)}, bf16[2,128,512]{2,1,0:T(8,128)(2,1)S(1)}, u32[]{:S(2)}, u32[]{:S(2)}) collective-permute-start(bf16[2,128,512]{2,1,0:T(8,128)(2,1)S(1)} %pad_maximum_fusion.3.refs_2_), channel_id=1, source_target_pairs={{0,2},{1,5},{2,0},{3,7},{4,6},{5,1},{6,4},{7,3},{8,10},{9,13},{10,... | collective-permute-start | bytes 786440 | tf_op jit(solution)/shard_map/ppermute | solution.py:288
  12.4 11.6 %collective-permute-start.3 = (bf16[2,128,640]{2,1,0:T(8,128)(2,1)S(1)}, bf16[2,128,640]{2,1,0:T(8,128)(2,1)S(1)}, u32[]{:S(2)}, u32[]{:S(2)}) collective-permute-start(bf16[2,128,640]{2,1,0:T(8,128)(2,1)S(1)} %pad_maximum_fusion.2), channel_id=1, source_target_pairs={{0,16},{1,9},{2,18},{3,11},{4,20},{5,13},{6,22},{7,15},{8,24},{9,1... | collective-permute-start | bytes 983048 | tf_op jit(solution)/shard_map/ppermute | solution.py:288
  16.7 14.0 %collective-permute-start.10 = (bf16[4,128,512]{2,1,0:T(8,128)(2,1)S(1)}, bf16[4,128,512]{2,1,0:T(8,128)(2,1)S(1)}, u32[]{:S(2)}, u32[]{:S(2)}) collective-permute-start(bf16[4,128,512]{2,1,0:T(8,128)(2,1)S(1)} %pad_maximum_fusion.1), channel_id=1, source_target_pairs={{0,4},{1,3},{2,6},{3,1},{4,0},{5,7},{6,2},{7,5},{8,12},{9,11},{10,... | collective-permute-start | bytes 1572872 | tf_op jit(solution)/shard_map/ppermute | solution.py:288
  24.0 6.7 %collective-permute-start.4 = (bf16[2,128,512]{2,1,0:T(8,128)(2,1)S(1)}, bf16[2,128,512]{2,1,0:T(8,128)(2,1)S(1)}, u32[]{:S(2)}, u32[]{:S(2)}) collective-permute-start(bf16[2,128,512]{2,1,0:T(8,128)(2,1)S(1)} %slice.91.refs_2_), channel_id=1, source_target_pairs={{0,2},{1,5},{2,0},{3,7},{4,6},{5,1},{6,4},{7,3},{8,10},{9,13},{10,... | collective-permute-start | bytes 786440 | tf_op jit(solution)/shard_map/ppermute | solution.py:288
  26.0 10.0 %slice-start.1 = ((s8[16777216]{0:T(1024)(128)(4,1)}), s8[4194304]{0:T(1024)(128)(4,1)S(1)}, s32[]{:S(2)}) async-start(s8[16777216]{0:T(1024)(128)(4,1)} %bitcast.16), calls=%async_computation.1 | async-start | bytes 8388608
  26.0 10.0 %slice-start.2 = ((s8[16777216]{0:T(1024)(128)(4,1)}), s8[4194304]{0:T(1024)(128)(4,1)S(1)}, s32[]{:S(2)}) async-start(s8[16777216]{0:T(1024)(128)(4,1)} %bitcast.16), calls=%async_computation.2 | async-start | bytes 8388608
  26.0 10.0 %slice-start.3 = ((s8[16777216]{0:T(1024)(128)(4,1)}), s8[4194304]{0:T(1024)(128)(4,1)S(1)}, s32[]{:S(2)}) async-start(s8[16777216]{0:T(1024)(128)(4,1)} %bitcast.16), calls=%async_computation.3 | async-start | bytes 8388608
  26.0 4.6 %collective-permute-start.5 = (bf16[1,128,128]{2,1,0:T(8,128)(2,1)S(1)}, bf16[1,128,128]{2,1,0:T(8,128)(2,1)S(1)}, u32[]{:S(2)}, u32[]{:S(2)}) collective-permute-start(bf16[1,128,128]{2,1,0:T(8,128)(2,1)S(1)} %slice.131), channel_id=1, source_target_pairs={{0,8},{1,17},{2,10},{3,19},{4,12},{5,21},{6,14},{7,23},{8,0},{9,25... | collective-permute-start | bytes 98312 | tf_op jit(solution)/shard_map/ppermute | solution.py:288
  30.7 5.3 %collective-permute-start.13 = (bf16[4,128,512]{2,1,0:T(8,128)(2,1)S(1)}, bf16[4,128,512]{2,1,0:T(8,128)(2,1)S(1)}, u32[]{:S(2)}, u32[]{:S(2)}) collective-permute-start(bf16[4,128,512]{2,1,0:T(8,128)(2,1)S(1)} %collective-permute-done.10.refs_4_), channel_id=1, source_target_pairs={{0,1},{1,0},{2,3},{3,2},{4,5},{5,4},{6,7},{7,6},{8,9},{9,8},{10,11... | collective-permute-start | bytes 1572872 | tf_op jit(solution)/shard_map/ppermute | solution.py:285
  30.8 2.7 %collective-permute-start.11 = (bf16[2,128,512]{2,1,0:T(8,128)(2,1)S(1)}, bf16[2,128,512]{2,1,0:T(8,128)(2,1)S(1)}, u32[]{:S(2)}, u32[]{:S(2)}) collective-permute-start(bf16[2,128,512]{2,1,0:T(8,128)(2,1)S(1)} %pad_maximum_fusion.3.refs_2_), channel_id=1, source_target_pairs={{0,1},{1,0},{2,3},{3,2},{4,5},{5,4},{6,7},{7,6},{8,9},{9,8},{10,11... | collective-permute-start | bytes 786440 | tf_op jit(solution)/shard_map/ppermute | solution.py:285
  31.3 9.2 %collective-permute-start.6 = (bf16[4,128,512]{2,1,0:T(8,128)(2,1)S(1)}, bf16[4,128,512]{2,1,0:T(8,128)(2,1)S(1)}, u32[]{:S(2)}, u32[]{:S(2)}) collective-permute-start(bf16[4,128,512]{2,1,0:T(8,128)(2,1)S(1)} %pad_maximum_fusion), channel_id=1, source_target_pairs={{0,4},{1,3},{2,6},{3,1},{4,0},{5,7},{6,2},{7,5},{8,12},{9,11},{10,... | collective-permute-start | bytes 1572872 | tf_op jit(solution)/shard_map/ppermute | solution.py:288
  33.0 1.5 %collective-permute-start.12 = (bf16[2,128,512]{2,1,0:T(8,128)(2,1)S(1)}, bf16[2,128,512]{2,1,0:T(8,128)(2,1)S(1)}, u32[]{:S(2)}, u32[]{:S(2)}) collective-permute-start(bf16[2,128,512]{2,1,0:T(8,128)(2,1)S(1)} %collective-permute-done.9.refs_3_), channel_id=1, source_target_pairs={{0,1},{1,0},{2,3},{3,2},{4,5},{5,4},{6,7},{7,6},{8,9},{9,8},{10,11... | collective-permute-start | bytes 786440 | tf_op jit(solution)/shard_map/ppermute | solution.py:285
  33.0 5.0 %collective-permute-start.7 = (bf16[2,128,512]{2,1,0:T(8,128)(2,1)S(1)}, bf16[2,128,512]{2,1,0:T(8,128)(2,1)S(1)}, u32[]{:S(2)}, u32[]{:S(2)}) collective-permute-start(bf16[2,128,512]{2,1,0:T(8,128)(2,1)S(1)} %slice.91.refs_2_), channel_id=1, source_target_pairs={{0,1},{1,0},{2,3},{3,2},{4,5},{5,4},{6,7},{7,6},{8,9},{9,8},{10,11... | collective-permute-start | bytes 786440 | tf_op jit(solution)/shard_map/ppermute | solution.py:285
  33.5 4.5 %collective-permute-start.8 = (bf16[2,128,512]{2,1,0:T(8,128)(2,1)S(1)}, bf16[2,128,512]{2,1,0:T(8,128)(2,1)S(1)}, u32[]{:S(2)}, u32[]{:S(2)}) collective-permute-start(bf16[2,128,512]{2,1,0:T(8,128)(2,1)S(1)} %collective-permute-done.4.refs_3_), channel_id=1, source_target_pairs={{0,1},{1,0},{2,3},{3,2},{4,5},{5,4},{6,7},{7,6},{8,9},{9,8},{10,11... | collective-permute-start | bytes 786440 | tf_op jit(solution)/shard_map/ppermute | solution.py:285
  34.5 6.3 %collective-permute-start.15 = (bf16[128,128]{1,0:T(8,128)(2,1)S(1)}, bf16[128,128]{1,0:T(8,128)(2,1)S(1)}, u32[]{:S(2)}, u32[]{:S(2)}) collective-permute-start(bf16[128,128]{1,0:T(8,128)(2,1)S(1)} %bitcast_convert_fusion), channel_id=1, source_target_pairs={{0,2},{1,3},{2,0},{3,1},{4,6},{5,7},{6,4},{7,5},{8,10},{9,11},{10,... | collective-permute-start | bytes 98312 | tf_op jit(solution)/shard_map/ppermute | solution.py:285
  40.6 2.0 %collective-permute-start.14 = (bf16[4,128,512]{2,1,0:T(8,128)(2,1)S(1)}, bf16[4,128,512]{2,1,0:T(8,128)(2,1)S(1)}, u32[]{:S(2)}, u32[]{:S(2)}) collective-permute-start(bf16[4,128,512]{2,1,0:T(8,128)(2,1)S(1)} %collective-permute-done.6.refs_2_), channel_id=1, source_target_pairs={{0,1},{1,0},{2,3},{3,2},{4,5},{5,4},{6,7},{7,6},{8,9},{9,8},{10,11... | collective-permute-start | bytes 1572872 | tf_op jit(solution)/shard_map/ppermute | solution.py:285
  40.9 1.7 %collective-permute-start.16 = (f32[128,128]{1,0:T(8,128)S(1)}, f32[128,128]{1,0:T(8,128)S(1)}, u32[]{:S(2)}, u32[]{:S(2)}) collective-permute-start(f32[128,128]{1,0:T(8,128)S(1)} %bitcast_add_fusion.refs_6_), channel_id=1, source_target_pairs={{0,1},{1,0},{2,3},{3,2},{4,5},{5,4},{6,7},{7,6},{8,9},{9,8},{10,11... | collective-permute-start | bytes 196616 | tf_op jit(solution)/shard_map/ppermute | solution.py:285
  44.6 2.0 %collective-permute-start.17 = (bf16[4,128,512]{2,1,0:T(8,128)(2,1)S(1)}, bf16[4,128,512]{2,1,0:T(8,128)(2,1)S(1)}, u32[]{:S(2)}, u32[]{:S(2)}) collective-permute-start(bf16[4,128,512]{2,1,0:T(8,128)(2,1)S(1)} %shard_map.75), channel_id=1, source_target_pairs={{0,1},{1,0},{2,3},{3,2},{4,5},{5,4},{6,7},{7,6},{8,9},{9,8},{10,11... | collective-permute-start | bytes 1572872 | tf_op jit(solution)/shard_map/ppermute | solution.py:285
  46.8 9.9 %collective-permute-start.20 = (bf16[4,128,512]{2,1,0:T(8,128)(2,1)S(1)}, bf16[4,128,512]{2,1,0:T(8,128)(2,1)S(1)}, u32[]{:S(2)}, u32[]{:S(2)}) collective-permute-start(bf16[4,128,512]{2,1,0:T(8,128)(2,1)S(1)} %add_convert_fusion.1), channel_id=1, source_target_pairs={{0,2},{1,5},{2,0},{3,7},{4,6},{5,1},{6,4},{7,3},{8,10},{9,13},{10,... | collective-permute-start | bytes 1572872 | tf_op jit(solution)/shard_map/ppermute | solution.py:288
  52.4 5.9 %collective-permute-start.21 = (bf16[4,128,512]{2,1,0:T(8,128)(2,1)S(1)}, bf16[4,128,512]{2,1,0:T(8,128)(2,1)S(1)}, u32[]{:S(2)}, u32[]{:S(2)}) collective-permute-start(bf16[4,128,512]{2,1,0:T(8,128)(2,1)S(1)} %get-tuple-element.84), channel_id=1, source_target_pairs={{0,1},{1,0},{2,3},{3,2},{4,5},{5,4},{6,7},{7,6},{8,9},{9,8},{10,11... | collective-permute-start | bytes 1572872 | tf_op jit(solution)/shard_map/ppermute | solution.py:285
  52.5 4.1 %collective-permute-start.19 = (bf16[2,128,512]{2,1,0:T(8,128)(2,1)S(1)}, bf16[2,128,512]{2,1,0:T(8,128)(2,1)S(1)}, u32[]{:S(2)}, u32[]{:S(2)}) collective-permute-start(bf16[2,128,512]{2,1,0:T(8,128)(2,1)S(1)} %get-tuple-element.90), channel_id=1, source_target_pairs={{0,1},{1,0},{2,3},{3,2},{4,5},{5,4},{6,7},{7,6},{8,9},{9,8},{10,11... | collective-permute-start | bytes 786440 | tf_op jit(solution)/shard_map/ppermute | solution.py:285
  53.0 7.1 %collective-permute-start.26 = (bf16[2,128,512]{2,1,0:T(8,128)(2,1)S(1)}, bf16[2,128,512]{2,1,0:T(8,128)(2,1)S(1)}, u32[]{:S(2)}, u32[]{:S(2)}) collective-permute-start(bf16[2,128,512]{2,1,0:T(8,128)(2,1)S(1)} %get-tuple-element.82), channel_id=1, source_target_pairs={{0,1},{1,0},{2,3},{3,2},{4,5},{5,4},{6,7},{7,6},{8,9},{9,8},{10,11... | collective-permute-start | bytes 786440 | tf_op jit(solution)/shard_map/ppermute | solution.py:285
  56.7 8.9 %collective-permute-start.27 = (bf16[2,128,512]{2,1,0:T(8,128)(2,1)S(1)}, bf16[2,128,512]{2,1,0:T(8,128)(2,1)S(1)}, u32[]{:S(2)}, u32[]{:S(2)}) collective-permute-start(bf16[2,128,512]{2,1,0:T(8,128)(2,1)S(1)} %add_convert_fusion.3), channel_id=1, source_target_pairs={{0,4},{1,3},{2,6},{3,1},{4,0},{5,7},{6,2},{7,5},{8,12},{9,11},{10,... | collective-permute-start | bytes 786440 | tf_op jit(solution)/shard_map/ppermute | solution.py:288
  58.5 9.7 %collective-permute-start.22 = (bf16[4,128,512]{2,1,0:T(8,128)(2,1)S(1)}, bf16[4,128,512]{2,1,0:T(8,128)(2,1)S(1)}, u32[]{:S(2)}, u32[]{:S(2)}) collective-permute-start(bf16[4,128,512]{2,1,0:T(8,128)(2,1)S(1)} %add_convert_fusion), channel_id=1, source_target_pairs={{0,2},{1,5},{2,0},{3,7},{4,6},{5,1},{6,4},{7,3},{8,10},{9,13},{10,... | collective-permute-start | bytes 1572872 | tf_op jit(solution)/shard_map/ppermute | solution.py:288
  59.5 8.6 %collective-permute-start.23 = (bf16[2,128,512]{2,1,0:T(8,128)(2,1)S(1)}, bf16[2,128,512]{2,1,0:T(8,128)(2,1)S(1)}, u32[]{:S(2)}, u32[]{:S(2)}) collective-permute-start(bf16[2,128,512]{2,1,0:T(8,128)(2,1)S(1)} %get-tuple-element.93), channel_id=1, source_target_pairs={{0,1},{1,0},{2,3},{3,2},{4,5},{5,4},{6,7},{7,6},{8,9},{9,8},{10,11... | collective-permute-start | bytes 786440 | tf_op jit(solution)/shard_map/ppermute | solution.py:285
  59.5 14.6 %collective-permute-start.18 = (bf16[2,128,512]{2,1,0:T(8,128)(2,1)S(1)}, bf16[2,128,512]{2,1,0:T(8,128)(2,1)S(1)}, u32[]{:S(2)}, u32[]{:S(2)}) collective-permute-start(bf16[2,128,512]{2,1,0:T(8,128)(2,1)S(1)} %get-tuple-element.87), channel_id=1, source_target_pairs={{0,1},{1,0},{2,3},{3,2},{4,5},{5,4},{6,7},{7,6},{8,9},{9,8},{10,11... | collective-permute-start | bytes 786440 | tf_op jit(solution)/shard_map/ppermute | solution.py:285
  65.8 5.3 %collective-permute-start.28 = (bf16[1,128,512]{2,1,0:T(8,128)(2,1)S(1)}, bf16[1,128,512]{2,1,0:T(8,128)(2,1)S(1)}, u32[]{:S(2)}, u32[]{:S(2)}) collective-permute-start(bf16[1,128,512]{2,1,0:T(8,128)(2,1)S(1)} %slice.127), channel_id=1, source_target_pairs={{0,8},{1,17},{2,10},{3,19},{4,12},{5,21},{6,14},{7,23},{8,0},{9,25... | collective-permute-start | bytes 393224 | tf_op jit(solution)/shard_map/ppermute | solution.py:288
  68.4 6.4 %collective-permute-start.24 = (bf16[2,128,512]{2,1,0:T(8,128)(2,1)S(1)}, bf16[2,128,512]{2,1,0:T(8,128)(2,1)S(1)}, u32[]{:S(2)}, u32[]{:S(2)}) collective-permute-start(bf16[2,128,512]{2,1,0:T(8,128)(2,1)S(1)} %add_convert_fusion.2), channel_id=1, source_target_pairs={{0,4},{1,3},{2,6},{3,1},{4,0},{5,7},{6,2},{7,5},{8,12},{9,11},{10,... | collective-permute-start | bytes 786440 | tf_op jit(solution)/shard_map/ppermute | solution.py:288
  71.1 5.9 %collective-permute-start.29 = (bf16[1,128,512]{2,1,0:T(8,128)(2,1)S(1)}, bf16[1,128,512]{2,1,0:T(8,128)(2,1)S(1)}, u32[]{:S(2)}, u32[]{:S(2)}) collective-permute-start(bf16[1,128,512]{2,1,0:T(8,128)(2,1)S(1)} %fusion), channel_id=1, source_target_pairs={{0,16},{1,9},{2,18},{3,11},{4,20},{5,13},{6,22},{7,15},{8,24},{9,1... | collective-permute-start | bytes 393224 | tf_op jit(solution)/shard_map/ppermute | solution.py:288
  75.0 6.3 %collective-permute-start.25 = (bf16[1,128,512]{2,1,0:T(8,128)(2,1)S(1)}, bf16[1,128,512]{2,1,0:T(8,128)(2,1)S(1)}, u32[]{:S(2)}, u32[]{:S(2)}) collective-permute-start(bf16[1,128,512]{2,1,0:T(8,128)(2,1)S(1)} %slice.128), channel_id=1, source_target_pairs={{0,8},{1,17},{2,10},{3,19},{4,12},{5,21},{6,14},{7,23},{8,0},{9,25... | collective-permute-start | bytes 393224 | tf_op jit(solution)/shard_map/ppermute | solution.py:288

commit v13 on v12

--- a/solution.py
+++ b/solution.py
@@ -86,10 +86,13 @@
     copies = [pltpu.make_async_copy(x, y, sems.at[i]) for i, (x, y) in enumerate(pairs)]
     for c in copies:
         c.start()
-    for c in copies:
-        c.wait()
+    copies[0].wait()
+    copies[1].wait()
     scaled = (abuf[...].astype(jnp.float32) * gbuf[:, own]).astype(jnp.bfloat16)
-    k, v = dot(scaled, kbuf[...]), dot(scaled, vbuf[...])
+    copies[2].wait()
+    k = dot(scaled, kbuf[...])
+    copies[3].wait()
+    v = dot(scaled, vbuf[...])
     core0 = (me & CORE) == 0
     for h in range(KVH):
         off = h ^ (me >> shared)
@@ -216,52 +219,23 @@
             out[block] = dot(left, weight[spot]).astype(out.dtype)
 
 
-def output_fetch_kernel(groups, where, attended, weight, *refs):
-    outs, buf, sems = refs[: len(groups)], refs[-2], refs[-1]
-    copies = []
-    for i, (const, pick) in enumerate(sum(groups, [])):
-        width = buf.shape[2]
-        start = pl.multiple_of((device(where, (const, pick))) * width, LANE)
-        copy = pltpu.make_async_copy(weight.at[:, pl.ds(start, width)], buf.at[i], sems.at[i])
-        copy.start()
-        copies.append(copy)
-    left = attended[...]
-    i = 0
-    for symbols, out in zip(groups, outs):
-        for block in range(len(symbols)):
-            copies[i].wait()
-            out[block] = dot(left, buf[i]).astype(out.dtype)
-            i += 1
-
-
-def output_call(attended, width, groups, held=None, where=None, weight=None):
+def output_call(attended, width, groups, held):
+    weight, order = held
     tokens, depth = attended.shape
-    blocks = sum(len(s) for s, _ in groups)
-    if held is not None:
-        kernel = functools.partial(
-            output_kernel, [[held[1].index(s) for s in symbols] for symbols, _ in groups]
-        )
-        operands, specs, scratch = (attended, held[0]), [vmem(), vmem()], []
-    else:
-        kernel = functools.partial(output_fetch_kernel, [symbols for symbols, _ in groups])
-        operands, specs = (where, attended, in_hbm(weight)), [smem(), vmem(), hbm()]
-        scratch = [
-            pltpu.VMEM((blocks, depth, width), weight.dtype),
-            pltpu.SemaphoreType.DMA((blocks,)),
-        ]
+    spots = [[order.index(s) for s in symbols] for symbols, _ in groups]
+    columns = width * sum(len(s) for s in spots)
     return pl.pallas_call(
-        kernel,
+        functools.partial(output_kernel, spots),
         out_shape=[jax.ShapeDtypeStruct((len(s), tokens, width), t) for s, t in groups],
-        in_specs=specs,
+        in_specs=[vmem(), vmem()],
         out_specs=[vmem()] * len(groups),
-        scratch_shapes=scratch,
-        compiler_params=pltpu.CompilerParams(vmem_limit_bytes=10 * MIB),
+        compiler_params=pltpu.CompilerParams(vmem_limit_bytes=4 * MIB),
         cost_estimate=pl.CostEstimate(
-            flops=2 * tokens * depth * width * blocks,
-            bytes_accessed=2 * depth * width * blocks,
+            flops=2 * tokens * depth * columns,
+            bytes_accessed=2 * depth * columns,
             transcendentals=0,
         ),
-    )(*operands)
+    )(attended, weight)
 
 
 def rotary_tables(tokens):
@@ -343,6 +317,9 @@
             k = min(row.shape[0], half.shape[0])
             extra = jnp.zeros((row.shape[0], *half.shape[1:]), bf16).at[:k].set(half[:k])
             got = along(jnp.concatenate([row, extra], axis=2), 1)
+            near_blocks, near_symbols = fetched(after(where, joined), wo, width, columns_of(near))
+            got, near_blocks = lax.optimization_barrier((got, near_blocks))
+            near_held = (near_blocks, near_symbols)
             row = got[:, :, :width]
             kv = kv[kv.shape[0] // 2 :] + got[:k, :, width:].astype(f32)
             side = turn(row, 0)
@@ -352,7 +329,8 @@
             far_held = (blocks, far_symbols)
         else:
             side = turn(row, 0)
-        both = turn(jnp.concatenate([row, side]), 1)
+        joined = jnp.concatenate([row, side])
+        both = turn(joined, 1)
         at = symbols_of(offsets)
         groups.append([(row, at[0]), (side, at[1]), (both, at[2] + at[3])])
     early, last = groups
@@ -394,15 +372,19 @@
         return [(x, swap(y, CORE)) for x, y in zip(own, sent)]
 
     project = functools.partial(output_call, held=far_held, width=width)
-    sent = project(attended, groups=theirs(order(far)[:1]))
-    own = project(after(attended, *sent), groups=ours(order(far)))
+    home, one, two, corner = symbols_of(far)
+    sent = project(attended, groups=theirs([corner]))
+    own = project(after(attended, *sent), groups=ours([corner, one, two, home]))
     first = added_up(own[0], swap(sent[0], CORE)).astype(bf16)
-    sent = project(after(attended, first), groups=theirs(order(far)[1:]))
-    far_home, far_two = round_square(first, *paired(own[1:], sent))
-    far_sum = added_up(*far_home, turn(far_two, 1))
-    project = functools.partial(output_call, width=width, where=where, weight=wo)
+    from_corner = turn(first, 0)
+    sent = project(after(attended, first), groups=theirs([one, two, home]))
+    one, two, home = paired(own[1:], sent)
+    got_one = turn(added_up(*one).astype(bf16), 0)
+    far_two = added_up(*two, from_corner).astype(bf16)
+    far_sum = added_up(*home, got_one, turn(far_two, 1))
+    project = functools.partial(output_call, held=near_held, width=width)
     sent = project(after(attended, sent[-1]), groups=theirs(order(near)))
-    own = project(after(attended, sent[0]), groups=ours(order(near)))
+    own = project(after(attended, sent[0], got_one), groups=ours(order(near)))
     pairs = paired(own, sent)
     first = added_up(after(pairs[0][0], far_two), pairs[0][1]).astype(bf16)
     near_home, near_two = round_square(first, *pairs[1:])

time: 82.1 us -> 81 us (0.987)
  Pallas kernels: 21.7 us -> 20.3 us
    pallas_call x5, Pallas kernels: 8.67 us -> 3.01 us  [output_call(): pl.pallas_call(functools.partial(output_kernel, spots), out_shape=[jax.Sh...]
    pallas_call x1 -> x2, Pallas kernels: 4.47 us -> 8.85 us  [fetched(): pl.pallas_call(functools.partial(fetch_kernel, symbols, width), out_shape...]
    ppermute x14 -> x15, waiting for transfers between devices: 22.6 us -> 23.2 us  [by_core(): lax.ppermute(x, 'wide', [(i, i ^ pair[(step + (i & CORE)) % 2]) for i in...]
    ppermute x16 -> x17, waiting for transfers between devices: 2.03 us -> 1.67 us  [swap(): return lax.ppermute(x, 'wide', [(i, i ^ offset) for i in range(n)])]
    ppermute x16 -> x17, starting transfers between devices: 6.94 us -> 7.21 us  [swap(): return lax.ppermute(x, 'wide', [(i, i ^ offset) for i in range(n)])]
    ppermute x14 -> x15, starting transfers between devices: 25.9 us -> 25.8 us  [by_core(): lax.ppermute(x, 'wide', [(i, i ^ pair[(step + (i & CORE)) % 2]) for i in...]
  transfers between devices with their start and end apart: 30 -> 32, of which waited for: 12 -> 13; matrix products, arithmetic and copies ran while one was open for 2% -> 2% of each run, Pallas kernels for 21% -> 19%
where the time goes in v13:
time: 81 us; the launch traced here: 80.8 us
  starting transfers between devices  33 us (41%)
  waiting for transfers between devices  24.8 us (31%)
  Pallas kernels  20.3 us (25%)
  other arithmetic  2.17 us (3%)
    ppermute x15, starting transfers between devices, by_core(): lax.ppermute(x, 'wide', [(i, i ^ pair[(step + (i & CORE)) % 2]) for i in...  25.8 us
    ppermute x15, waiting for transfers between devices, by_core(): lax.ppermute(x, 'wide', [(i, i ^ pair[(step + (i & CORE)) % 2]) for i in...  23.2 us
    pallas_call x2, Pallas kernels, fetched(): pl.pallas_call(functools.partial(fetch_kernel, symbols, width), out_shape...  8.85 us
    ppermute x17, starting transfers between devices, swap(): return lax.ppermute(x, 'wide', [(i, i ^ offset) for i in range(n)])  7.21 us
    pallas_call x4, Pallas kernels, query_call(): pl.pallas_call(functools.partial(query_kernel, places, bool(carry), bool(...  5.87 us
    pallas_call x5, Pallas kernels, output_call(): pl.pallas_call(functools.partial(output_kernel, spots), out_shape=[jax.Sh...  3.01 us
    pallas_call x1, Pallas kernels, kv_terms(): pl.pallas_call(functools.partial(kv_kernel, shared), out_shape=[jax.Shape...  2.55 us
    ppermute x17, waiting for transfers between devices, swap(): return lax.ppermute(x, 'wide', [(i, i ^ offset) for i in range(n)])  1.67 us
  transfers between devices with their start and end apart: 32, of which 13 were waited for; matrix products, arithmetic and copies ran while one was open for 2% of the time, Pallas kernels for 19%

profile of v13, /device:TPU:0, one launch (start us, length us, event | category | flops | bytes accessed | tf_op | source)
XLA Modules:
  0.0 80.8 jit_solution(13200719915183548269)
XLA Ops:
  0.1 2.6 %shard_map.69 = (f32[8,128,128]{2,1,0:T(8,128)S(1)}, f32[8,128,128]{2,1,0:T(8,128)S(1)}, bf16[128,512]{1,0:T(8,128)(2,1)S(1)}, f32[1,16384]{1,0:T(1,128)S(1)}) custom-call(s32[9]{0:T(128)S(1)} %stack.42.where.refs_0_, bf16[128,512]{1,0:T(8,128)(2,1)} %act.1, f32[1,16384]{1,0:T(1,128)} %bitcast.22, bf16[512,1024]{1,0:T(8,128)(2,1)} %wk.1, bf16[512,1024]{1,0:T(8,128)(2,1)} %wv.1), custom_call_target="tpu_custom_call" | custom-call | flops 4294967296 | bytes 33554432 | tf_op jit(solution)/shard_map/pallas_call | solution.py:108
  2.6 0.5 collective-permute-start.1
  3.2 2.6 %collective-permute-start = (bf16[1,128,512]{2,1,0:T(8,128)(2,1)S(1)}, bf16[1,128,512]{2,1,0:T(8,128)(2,1)S(1)}, u32[]{:S(2)}, u32[]{:S(2)}) collective-permute-start(bf16[1,128,512]{2,1,0:T(8,128)(2,1)S(1)} %bitcast.18), channel_id=1, source_target_pairs={{0,8},{1,17},{2,10},{3,19},{4,12},{5,21},{6,14},{7,23},{8,0},{9,25... | collective-permute-start | bytes 393224 | tf_op jit(solution)/shard_map/ppermute | solution.py:262
  5.9 1.8 %collective-permute-start.2 = (bf16[4,128,128]{2,1,0:T(8,128)(2,1)S(1)}, bf16[4,128,128]{2,1,0:T(8,128)(2,1)S(1)}, u32[]{:S(2)}, u32[]{:S(2)}) collective-permute-start(bf16[4,128,128]{2,1,0:T(8,128)(2,1)S(1)} %slice.115), channel_id=1, source_target_pairs={{0,4},{1,5},{2,6},{3,7},{4,0},{5,1},{6,2},{7,3},{8,12},{9,13},{10,... | collective-permute-start | bytes 393224 | tf_op jit(solution)/shard_map/ppermute | solution.py:259
  7.8 2.1 %collective-permute-done = bf16[1,128,512]{2,1,0:T(8,128)(2,1)S(1)} collective-permute-done((bf16[1,128,512]{2,1,0:T(8,128)(2,1)S(1)}, bf16[1,128,512]{2,1,0:T(8,128)(2,1)S(1)}, u32[]{:S(2)}, u32[]{:S(2)}) %collective-permute-start) | collective-permute-done | bytes 131104 | tf_op jit(solution)/shard_map/ppermute | solution.py:262
  9.9 2.2 %collective-permute-start.4 = (bf16[2,128,512]{2,1,0:T(8,128)(2,1)S(1)}, bf16[2,128,512]{2,1,0:T(8,128)(2,1)S(1)}, u32[]{:S(2)}, u32[]{:S(2)}) collective-permute-start(bf16[2,128,512]{2,1,0:T(8,128)(2,1)S(1)} %pad_maximum_fusion.3.refs_2_), channel_id=1, source_target_pairs={{0,2},{1,5},{2,0},{3,7},{4,6},{5,1},{6,4},{7,3},{8,10},{9,13},{10,... | collective-permute-start | bytes 786440 | tf_op jit(solution)/shard_map/ppermute | solution.py:262
  12.2 2.3 %collective-permute-start.3 = (bf16[2,128,640]{2,1,0:T(8,128)(2,1)S(1)}, bf16[2,128,640]{2,1,0:T(8,128)(2,1)S(1)}, u32[]{:S(2)}, u32[]{:S(2)}) collective-permute-start(bf16[2,128,640]{2,1,0:T(8,128)(2,1)S(1)} %pad_maximum_fusion.2), channel_id=1, source_target_pairs={{0,16},{1,9},{2,18},{3,11},{4,20},{5,13},{6,22},{7,15},{8,24},{9,1... | collective-permute-start | bytes 983048 | tf_op jit(solution)/shard_map/ppermute | solution.py:262
  14.5 2.0 %collective-permute-done.4.refs_3_ = bf16[2,128,512]{2,1,0:T(8,128)(2,1)S(1)} collective-permute-done((bf16[2,128,512]{2,1,0:T(8,128)(2,1)S(1)}, bf16[2,128,512]{2,1,0:T(8,128)(2,1)S(1)}, u32[]{:S(2)}, u32[]{:S(2)}) %collective-permute-start.4) | collective-permute-done | bytes 262176 | tf_op jit(solution)/shard_map/ppermute | solution.py:262
  16.6 2.1 %collective-permute-start.10 = (bf16[4,128,512]{2,1,0:T(8,128)(2,1)S(1)}, bf16[4,128,512]{2,1,0:T(8,128)(2,1)S(1)}, u32[]{:S(2)}, u32[]{:S(2)}) collective-permute-start(bf16[4,128,512]{2,1,0:T(8,128)(2,1)S(1)} %pad_maximum_fusion), channel_id=1, source_target_pairs={{0,4},{1,3},{2,6},{3,1},{4,0},{5,7},{6,2},{7,5},{8,12},{9,11},{10,... | collective-permute-start | bytes 1572872 | tf_op jit(solution)/shard_map/ppermute | solution.py:262
  18.7 4.4 %shard_map.70.weight = bf16[16,512,512]{2,1,0:T(8,128)(2,1)S(1)} custom-call(s32[9]{0:T(128)S(1)} %stack.42.where.refs_0_, bf16[512,16384]{1,0:T(8,128)(2,1)} %source.3), custom_call_target="tpu_custom_call" | custom-call | bytes 16777216 | tf_op jit(solution)/shard_map/pallas_call | solution.py:67
  23.1 0.8 collective-permute-done.3
  23.9 1.9 %collective-permute-start.5 = (bf16[2,128,512]{2,1,0:T(8,128)(2,1)S(1)}, bf16[2,128,512]{2,1,0:T(8,128)(2,1)S(1)}, u32[]{:S(2)}, u32[]{:S(2)}) collective-permute-start(bf16[2,128,512]{2,1,0:T(8,128)(2,1)S(1)} %slice.69.refs_2_), channel_id=1, source_target_pairs={{0,2},{1,5},{2,0},{3,7},{4,6},{5,1},{6,4},{7,3},{8,10},{9,13},{10,... | collective-permute-start | bytes 786440 | tf_op jit(solution)/shard_map/ppermute | solution.py:262
  26.0 4.5 %shard_map.71.weight = bf16[16,512,512]{2,1,0:T(8,128)(2,1)S(1)} custom-call(s32[9]{0:T(128)S(1)} %stack.42.where.refs_0_, bf16[512,16384]{1,0:T(8,128)(2,1)} %source.3), custom_call_target="tpu_custom_call" | custom-call | bytes 16777216 | tf_op jit(solution)/shard_map/pallas_call | solution.py:67
  30.6 0.5 collective-permute-start.11
  31.2 1.7 %collective-permute-start.7 = (bf16[4,128,512]{2,1,0:T(8,128)(2,1)S(1)}, bf16[4,128,512]{2,1,0:T(8,128)(2,1)S(1)}, u32[]{:S(2)}, u32[]{:S(2)}) collective-permute-start(bf16[4,128,512]{2,1,0:T(8,128)(2,1)S(1)} %pad_maximum_fusion.1), channel_id=1, source_target_pairs={{0,4},{1,3},{2,6},{3,1},{4,0},{5,7},{6,2},{7,5},{8,12},{9,11},{10,... | collective-permute-start | bytes 1572872 | tf_op jit(solution)/shard_map/ppermute | solution.py:262
  32.9 0.5 collective-permute-start.8
  33.5 0.9 %collective-permute-done.12.refs_6_ = bf16[2,128,512]{2,1,0:T(8,128)(2,1)S(1)} collective-permute-done((bf16[2,128,512]{2,1,0:T(8,128)(2,1)S(1)}, bf16[2,128,512]{2,1,0:T(8,128)(2,1)S(1)}, u32[]{:S(2)}, u32[]{:S(2)}) %collective-permute-start.12) | collective-permute-done | bytes 262176 | tf_op jit(solution)/shard_map/ppermute | solution.py:259
  34.4 1.5 %collective-permute-start.15 = (bf16[128,128]{1,0:T(8,128)(2,1)S(1)}, bf16[128,128]{1,0:T(8,128)(2,1)S(1)}, u32[]{:S(2)}, u32[]{:S(2)}) collective-permute-start(bf16[128,128]{1,0:T(8,128)(2,1)S(1)} %bitcast_convert_fusion), channel_id=1, source_target_pairs={{0,2},{1,3},{2,0},{3,1},{4,6},{5,7},{6,4},{7,5},{8,10},{9,11},{10,... | collective-permute-start | bytes 98312 | tf_op jit(solution)/shard_map/ppermute | solution.py:259
  35.9 2.0 %shard_map.72 = (f32[128,512]{1,0:T(8,128)S(1)}, f32[128,128]{1,0:T(8,128)S(1)}) custom-call(s32[9]{0:T(128)S(1)} %stack.42.where.refs_0_, f32[1,16384]{1,0:T(1,128)S(1)} %get-tuple-element.65.refs_1_, bf16[2,128,512]{2,1,0:T(8,128)(2,1)S(1)} %pad_maximum_fusion.3.refs_2_, bf16[2,128,512]{2,1,0:T(8,128)(2,1)S(1)} %collective-permute-done.4.refs_3_, ...), custom_call_target="tpu_custom_call" | custom-call | flops 1073741824 | bytes 8388608 | tf_op jit(solution)/shard_map/pallas_call | solution.py:201
  37.9 1.3 %shard_map.73 = (f32[128,512]{1,0:T(8,128)S(1)}, f32[128,128]{1,0:T(8,128)S(1)}) custom-call(s32[9]{0:T(128)S(1)} %stack.42.where.refs_0_, f32[1,16384]{1,0:T(1,128)S(1)} %get-tuple-element.65.refs_1_, bf16[2,128,512]{2,1,0:T(8,128)(2,1)S(1)} %slice.69.refs_2_, bf16[2,128,512]{2,1,0:T(8,128)(2,1)S(1)} %collective-permute-done.5.refs_3_, ...), custom_call_target="tpu_custom_call" | custom-call | flops 536870912 | bytes 4194304 | tf_op jit(solution)/shard_map/pallas_call | solution.py:201
  39.2 1.2 %collective-permute-done.7.refs_2_ = bf16[4,128,512]{2,1,0:T(8,128)(2,1)S(1)} collective-permute-done((bf16[4,128,512]{2,1,0:T(8,128)(2,1)S(1)}, bf16[4,128,512]{2,1,0:T(8,128)(2,1)S(1)}, u32[]{:S(2)}, u32[]{:S(2)}) %collective-permute-start.7) | collective-permute-done | bytes 524320 | tf_op jit(solution)/shard_map/ppermute | solution.py:262
  40.7 0.6 collective-permute-start.16
  41.4 1.0 %shard_map.74 = (f32[128,512]{1,0:T(8,128)S(1)}, f32[128,128]{1,0:T(8,128)S(1)}) custom-call(s32[9]{0:T(128)S(1)} %stack.42.where.refs_0_, f32[1,16384]{1,0:T(1,128)S(1)} %get-tuple-element.65.refs_1_, bf16[4,128,512]{2,1,0:T(8,128)(2,1)S(1)} %collective-permute-done.7.refs_2_, bf16[16384,512]{1,0:T(8,128)(2,1)S(1)} %bitcast.17, ...), custom_call_target="tpu_custom_call" | custom-call | flops 268435456 | bytes 2097152 | tf_op jit(solution)/shard_map/pallas_call | solution.py:201
  42.4 1.6 %shard_map.75.attended = bf16[128,512]{1,0:T(8,128)(2,1)S(1)} custom-call(s32[9]{0:T(128)S(1)} %stack.42.where.refs_0_, f32[1,16384]{1,0:T(1,128)S(1)} %get-tuple-element.65.refs_1_, bf16[4,128,512]{2,1,0:T(8,128)(2,1)S(1)} %collective-permute-done.14.refs_2_, bf16[16384,512]{1,0:T(8,128)(2,1)S(1)} %bitcast.17, f32[128,512]{1,0:T(8,128)S(1)} %get-tuple-element.82.refs_4_, ...), custom_call_target="tpu_custom_call" | custom-call | flops 268435456 | bytes 2097152 | tf_op jit(solution)/shard_map/pallas_call | solution.py:201
  44.0 0.3 shard_map.76
  44.5 0.7 shard_map.77
  45.2 0.7 collective-permute-done.17
  46.0 0.6 shard_map.78
  46.8 1.6 %collective-permute-start.22 = (bf16[2,128,512]{2,1,0:T(8,128)(2,1)S(1)}, bf16[2,128,512]{2,1,0:T(8,128)(2,1)S(1)}, u32[]{:S(2)}, u32[]{:S(2)}) collective-permute-start(bf16[2,128,512]{2,1,0:T(8,128)(2,1)S(1)} %add_convert_fusion.4), channel_id=1, source_target_pairs={{0,2},{1,5},{2,0},{3,7},{4,6},{5,1},{6,4},{7,3},{8,10},{9,13},{10,... | collective-permute-start | bytes 786440 | tf_op jit(solution)/shard_map/ppermute | solution.py:262
  48.5 0.7 shard_map.79
  49.2 0.5 collective-permute-start.23
  49.7 1.2 %collective-permute-start.19 = (bf16[2,128,512]{2,1,0:T(8,128)(2,1)S(1)}, bf16[2,128,512]{2,1,0:T(8,128)(2,1)S(1)}, u32[]{:S(2)}, u32[]{:S(2)}) collective-permute-start(bf16[2,128,512]{2,1,0:T(8,128)(2,1)S(1)} %add_convert_fusion.3), channel_id=1, source_target_pairs={{0,2},{1,5},{2,0},{3,7},{4,6},{5,1},{6,4},{7,3},{8,10},{9,13},{10,... | collective-permute-start | bytes 786440 | tf_op jit(solution)/shard_map/ppermute | solution.py:262
  51.1 2.1 %collective-permute-done.22 = bf16[2,128,512]{2,1,0:T(8,128)(2,1)S(1)} collective-permute-done((bf16[2,128,512]{2,1,0:T(8,128)(2,1)S(1)}, bf16[2,128,512]{2,1,0:T(8,128)(2,1)S(1)}, u32[]{:S(2)}, u32[]{:S(2)}) %collective-permute-start.22) | collective-permute-done | bytes 262176 | tf_op jit(solution)/shard_map/ppermute | solution.py:262
  53.3 1.6 %collective-permute-start.29 = (bf16[2,128,512]{2,1,0:T(8,128)(2,1)S(1)}, bf16[2,128,512]{2,1,0:T(8,128)(2,1)S(1)}, u32[]{:S(2)}, u32[]{:S(2)}) collective-permute-start(bf16[2,128,512]{2,1,0:T(8,128)(2,1)S(1)} %add_convert_fusion.2), channel_id=1, source_target_pairs={{0,4},{1,3},{2,6},{3,1},{4,0},{5,7},{6,2},{7,5},{8,12},{9,11},{10,... | collective-permute-start | bytes 786440 | tf_op jit(solution)/shard_map/ppermute | solution.py:262
  54.9 1.9 %collective-permute-done.19 = bf16[2,128,512]{2,1,0:T(8,128)(2,1)S(1)} collective-permute-done((bf16[2,128,512]{2,1,0:T(8,128)(2,1)S(1)}, bf16[2,128,512]{2,1,0:T(8,128)(2,1)S(1)}, u32[]{:S(2)}, u32[]{:S(2)}) %collective-permute-start.19) | collective-permute-done | bytes 262176 | tf_op jit(solution)/shard_map/ppermute | solution.py:262
  56.8 0.7 shard_map.80
  57.7 1.2 %collective-permute-start.24 = (bf16[4,128,512]{2,1,0:T(8,128)(2,1)S(1)}, bf16[4,128,512]{2,1,0:T(8,128)(2,1)S(1)}, u32[]{:S(2)}, u32[]{:S(2)}) collective-permute-start(bf16[4,128,512]{2,1,0:T(8,128)(2,1)S(1)} %add_convert_fusion), channel_id=1, source_target_pairs={{0,2},{1,5},{2,0},{3,7},{4,6},{5,1},{6,4},{7,3},{8,10},{9,13},{10,... | collective-permute-start | bytes 1572872 | tf_op jit(solution)/shard_map/ppermute | solution.py:262
  59.0 0.5 collective-permute-start.20
  59.5 0.8 %collective-permute-done.29 = bf16[2,128,512]{2,1,0:T(8,128)(2,1)S(1)} collective-permute-done((bf16[2,128,512]{2,1,0:T(8,128)(2,1)S(1)}, bf16[2,128,512]{2,1,0:T(8,128)(2,1)S(1)}, u32[]{:S(2)}, u32[]{:S(2)}) %collective-permute-start.29) | collective-permute-done | bytes 262176 | tf_op jit(solution)/shard_map/ppermute | solution.py:262
  60.5 1.7 %collective-permute-start.30 = (bf16[1,128,512]{2,1,0:T(8,128)(2,1)S(1)}, bf16[1,128,512]{2,1,0:T(8,128)(2,1)S(1)}, u32[]{:S(2)}, u32[]{:S(2)}) collective-permute-start(bf16[1,128,512]{2,1,0:T(8,128)(2,1)S(1)} %slice.113), channel_id=1, source_target_pairs={{0,8},{1,17},{2,10},{3,19},{4,12},{5,21},{6,14},{7,23},{8,0},{9,25... | collective-permute-start | bytes 393224 | tf_op jit(solution)/shard_map/ppermute | solution.py:262
  62.1 4.8 %collective-permute-done.24 = bf16[4,128,512]{2,1,0:T(8,128)(2,1)S(1)} collective-permute-done((bf16[4,128,512]{2,1,0:T(8,128)(2,1)S(1)}, bf16[4,128,512]{2,1,0:T(8,128)(2,1)S(1)}, u32[]{:S(2)}, u32[]{:S(2)}) %collective-permute-start.24) | collective-permute-done | bytes 524320 | tf_op jit(solution)/shard_map/ppermute | solution.py:262
  67.1 1.5 %collective-permute-start.26 = (bf16[2,128,512]{2,1,0:T(8,128)(2,1)S(1)}, bf16[2,128,512]{2,1,0:T(8,128)(2,1)S(1)}, u32[]{:S(2)}, u32[]{:S(2)}) collective-permute-start(bf16[2,128,512]{2,1,0:T(8,128)(2,1)S(1)} %add_convert_fusion.1), channel_id=1, source_target_pairs={{0,4},{1,3},{2,6},{3,1},{4,0},{5,7},{6,2},{7,5},{8,12},{9,11},{10,... | collective-permute-start | bytes 786440 | tf_op jit(solution)/shard_map/ppermute | solution.py:262
  68.7 2.6 %collective-permute-start.31 = (bf16[1,128,512]{2,1,0:T(8,128)(2,1)S(1)}, bf16[1,128,512]{2,1,0:T(8,128)(2,1)S(1)}, u32[]{:S(2)}, u32[]{:S(2)}) collective-permute-start(bf16[1,128,512]{2,1,0:T(8,128)(2,1)S(1)} %fusion), channel_id=1, source_target_pairs={{0,16},{1,9},{2,18},{3,11},{4,20},{5,13},{6,22},{7,15},{8,24},{9,1... | collective-permute-start | bytes 393224 | tf_op jit(solution)/shard_map/ppermute | solution.py:262
  71.2 2.3 %collective-permute-done.26 = bf16[2,128,512]{2,1,0:T(8,128)(2,1)S(1)} collective-permute-done((bf16[2,128,512]{2,1,0:T(8,128)(2,1)S(1)}, bf16[2,128,512]{2,1,0:T(8,128)(2,1)S(1)}, u32[]{:S(2)}, u32[]{:S(2)}) %collective-permute-start.26) | collective-permute-done | bytes 262176 | tf_op jit(solution)/shard_map/ppermute | solution.py:262
  73.7 1.3 %collective-permute-start.27 = (bf16[1,128,512]{2,1,0:T(8,128)(2,1)S(1)}, bf16[1,128,512]{2,1,0:T(8,128)(2,1)S(1)}, u32[]{:S(2)}, u32[]{:S(2)}) collective-permute-start(bf16[1,128,512]{2,1,0:T(8,128)(2,1)S(1)} %slice.114), channel_id=1, source_target_pairs={{0,8},{1,17},{2,10},{3,19},{4,12},{5,21},{6,14},{7,23},{8,0},{9,25... | collective-permute-start | bytes 393224 | tf_op jit(solution)/shard_map/ppermute | solution.py:262
  75.0 3.1 %collective-permute-done.31 = bf16[1,128,512]{2,1,0:T(8,128)(2,1)S(1)} collective-permute-done((bf16[1,128,512]{2,1,0:T(8,128)(2,1)S(1)}, bf16[1,128,512]{2,1,0:T(8,128)(2,1)S(1)}, u32[]{:S(2)}, u32[]{:S(2)}) %collective-permute-start.31) | collective-permute-done | bytes 131104 | tf_op jit(solution)/shard_map/ppermute | solution.py:262
  78.0 2.1 %collective-permute-done.27 = bf16[1,128,512]{2,1,0:T(8,128)(2,1)S(1)} collective-permute-done((bf16[1,128,512]{2,1,0:T(8,128)(2,1)S(1)}, bf16[1,128,512]{2,1,0:T(8,128)(2,1)S(1)}, u32[]{:S(2)}, u32[]{:S(2)}) %collective-permute-start.27) | collective-permute-done | bytes 131104 | tf_op jit(solution)/shard_map/ppermute | solution.py:262
  80.1 0.7 fusion.3
  (66 shorter events, 2.7 us)
Async XLA Ops:
  2.6 3.2 %collective-permute-start.1 = (f32[8,128,128]{2,1,0:T(8,128)S(1)}, f32[8,128,128]{2,1,0:T(8,128)S(1)}, u32[]{:S(2)}, u32[]{:S(2)}) collective-permute-start(f32[8,128,128]{2,1,0:T(8,128)S(1)} %get-tuple-element.68), channel_id=1, source_target_pairs={{0,1},{1,0},{2,3},{3,2},{4,5},{5,4},{6,7},{7,6},{8,9},{9,8},{10,11... | collective-permute-start | bytes 1572872 | tf_op jit(solution)/shard_map/ppermute | solution.py:259
  3.2 6.7 %collective-permute-start = (bf16[1,128,512]{2,1,0:T(8,128)(2,1)S(1)}, bf16[1,128,512]{2,1,0:T(8,128)(2,1)S(1)}, u32[]{:S(2)}, u32[]{:S(2)}) collective-permute-start(bf16[1,128,512]{2,1,0:T(8,128)(2,1)S(1)} %bitcast.18), channel_id=1, source_target_pairs={{0,8},{1,17},{2,10},{3,19},{4,12},{5,21},{6,14},{7,23},{8,0},{9,25... | collective-permute-start | bytes 393224 | tf_op jit(solution)/shard_map/ppermute | solution.py:262
  5.9 6.2 %collective-permute-start.2 = (bf16[4,128,128]{2,1,0:T(8,128)(2,1)S(1)}, bf16[4,128,128]{2,1,0:T(8,128)(2,1)S(1)}, u32[]{:S(2)}, u32[]{:S(2)}) collective-permute-start(bf16[4,128,128]{2,1,0:T(8,128)(2,1)S(1)} %slice.115), channel_id=1, source_target_pairs={{0,4},{1,5},{2,6},{3,7},{4,0},{5,1},{6,2},{7,3},{8,12},{9,13},{10,... | collective-permute-start | bytes 393224 | tf_op jit(solution)/shard_map/ppermute | solution.py:259
  9.9 6.6 %collective-permute-start.4 = (bf16[2,128,512]{2,1,0:T(8,128)(2,1)S(1)}, bf16[2,128,512]{2,1,0:T(8,128)(2,1)S(1)}, u32[]{:S(2)}, u32[]{:S(2)}) collective-permute-start(bf16[2,128,512]{2,1,0:T(8,128)(2,1)S(1)} %pad_maximum_fusion.3.refs_2_), channel_id=1, source_target_pairs={{0,2},{1,5},{2,0},{3,7},{4,6},{5,1},{6,4},{7,3},{8,10},{9,13},{10,... | collective-permute-start | bytes 786440 | tf_op jit(solution)/shard_map/ppermute | solution.py:262
  12.2 11.6 %collective-permute-start.3 = (bf16[2,128,640]{2,1,0:T(8,128)(2,1)S(1)}, bf16[2,128,640]{2,1,0:T(8,128)(2,1)S(1)}, u32[]{:S(2)}, u32[]{:S(2)}) collective-permute-start(bf16[2,128,640]{2,1,0:T(8,128)(2,1)S(1)} %pad_maximum_fusion.2), channel_id=1, source_target_pairs={{0,16},{1,9},{2,18},{3,11},{4,20},{5,13},{6,22},{7,15},{8,24},{9,1... | collective-permute-start | bytes 983048 | tf_op jit(solution)/shard_map/ppermute | solution.py:262
  16.6 14.0 %collective-permute-start.10 = (bf16[4,128,512]{2,1,0:T(8,128)(2,1)S(1)}, bf16[4,128,512]{2,1,0:T(8,128)(2,1)S(1)}, u32[]{:S(2)}, u32[]{:S(2)}) collective-permute-start(bf16[4,128,512]{2,1,0:T(8,128)(2,1)S(1)} %pad_maximum_fusion), channel_id=1, source_target_pairs={{0,4},{1,3},{2,6},{3,1},{4,0},{5,7},{6,2},{7,5},{8,12},{9,11},{10,... | collective-permute-start | bytes 1572872 | tf_op jit(solution)/shard_map/ppermute | solution.py:262
  18.7 17.2 %slice-start = ((s8[16777216]{0:T(1024)(128)(4,1)}), s8[4194304]{0:T(1024)(128)(4,1)S(1)}, s32[]{:S(2)}) async-start(s8[16777216]{0:T(1024)(128)(4,1)} %bitcast.16), calls=%async_computation | async-start | bytes 8388608
  18.7 17.2 %slice-start.1 = ((s8[16777216]{0:T(1024)(128)(4,1)}), s8[4194304]{0:T(1024)(128)(4,1)S(1)}, s32[]{:S(2)}) async-start(s8[16777216]{0:T(1024)(128)(4,1)} %bitcast.16), calls=%async_computation.1 | async-start | bytes 8388608
  23.9 6.7 %collective-permute-start.5 = (bf16[2,128,512]{2,1,0:T(8,128)(2,1)S(1)}, bf16[2,128,512]{2,1,0:T(8,128)(2,1)S(1)}, u32[]{:S(2)}, u32[]{:S(2)}) collective-permute-start(bf16[2,128,512]{2,1,0:T(8,128)(2,1)S(1)} %slice.69.refs_2_), channel_id=1, source_target_pairs={{0,2},{1,5},{2,0},{3,7},{4,6},{5,1},{6,4},{7,3},{8,10},{9,13},{10,... | collective-permute-start | bytes 786440 | tf_op jit(solution)/shard_map/ppermute | solution.py:262
  25.8 10.0 %slice-start.2 = ((s8[16777216]{0:T(1024)(128)(4,1)}), s8[4194304]{0:T(1024)(128)(4,1)S(1)}, s32[]{:S(2)}) async-start(s8[16777216]{0:T(1024)(128)(4,1)} %bitcast.16), calls=%async_computation.2 | async-start | bytes 8388608
  25.9 10.0 %slice-start.3 = ((s8[16777216]{0:T(1024)(128)(4,1)}), s8[4194304]{0:T(1024)(128)(4,1)S(1)}, s32[]{:S(2)}) async-start(s8[16777216]{0:T(1024)(128)(4,1)} %bitcast.16), calls=%async_computation.3 | async-start | bytes 8388608
  25.9 4.6 %collective-permute-start.6 = (bf16[1,128,128]{2,1,0:T(8,128)(2,1)S(1)}, bf16[1,128,128]{2,1,0:T(8,128)(2,1)S(1)}, u32[]{:S(2)}, u32[]{:S(2)}) collective-permute-start(bf16[1,128,128]{2,1,0:T(8,128)(2,1)S(1)} %slice.117), channel_id=1, source_target_pairs={{0,8},{1,17},{2,10},{3,19},{4,12},{5,21},{6,14},{7,23},{8,0},{9,25... | collective-permute-start | bytes 98312 | tf_op jit(solution)/shard_map/ppermute | solution.py:262
  30.5 5.3 %collective-permute-start.13 = (bf16[4,128,512]{2,1,0:T(8,128)(2,1)S(1)}, bf16[4,128,512]{2,1,0:T(8,128)(2,1)S(1)}, u32[]{:S(2)}, u32[]{:S(2)}) collective-permute-start(bf16[4,128,512]{2,1,0:T(8,128)(2,1)S(1)} %collective-permute-done.10.refs_4_), channel_id=1, source_target_pairs={{0,1},{1,0},{2,3},{3,2},{4,5},{5,4},{6,7},{7,6},{8,9},{9,8},{10,11... | collective-permute-start | bytes 1572872 | tf_op jit(solution)/shard_map/ppermute | solution.py:259
  30.6 2.7 %collective-permute-start.11 = (bf16[2,128,512]{2,1,0:T(8,128)(2,1)S(1)}, bf16[2,128,512]{2,1,0:T(8,128)(2,1)S(1)}, u32[]{:S(2)}, u32[]{:S(2)}) collective-permute-start(bf16[2,128,512]{2,1,0:T(8,128)(2,1)S(1)} %pad_maximum_fusion.3.refs_2_), channel_id=1, source_target_pairs={{0,1},{1,0},{2,3},{3,2},{4,5},{5,4},{6,7},{7,6},{8,9},{9,8},{10,11... | collective-permute-start | bytes 786440 | tf_op jit(solution)/shard_map/ppermute | solution.py:259
  31.2 9.2 %collective-permute-start.7 = (bf16[4,128,512]{2,1,0:T(8,128)(2,1)S(1)}, bf16[4,128,512]{2,1,0:T(8,128)(2,1)S(1)}, u32[]{:S(2)}, u32[]{:S(2)}) collective-permute-start(bf16[4,128,512]{2,1,0:T(8,128)(2,1)S(1)} %pad_maximum_fusion.1), channel_id=1, source_target_pairs={{0,4},{1,3},{2,6},{3,1},{4,0},{5,7},{6,2},{7,5},{8,12},{9,11},{10,... | collective-permute-start | bytes 1572872 | tf_op jit(solution)/shard_map/ppermute | solution.py:262
  32.8 1.5 %collective-permute-start.12 = (bf16[2,128,512]{2,1,0:T(8,128)(2,1)S(1)}, bf16[2,128,512]{2,1,0:T(8,128)(2,1)S(1)}, u32[]{:S(2)}, u32[]{:S(2)}) collective-permute-start(bf16[2,128,512]{2,1,0:T(8,128)(2,1)S(1)} %collective-permute-done.4.refs_3_), channel_id=1, source_target_pairs={{0,1},{1,0},{2,3},{3,2},{4,5},{5,4},{6,7},{7,6},{8,9},{9,8},{10,11... | collective-permute-start | bytes 786440 | tf_op jit(solution)/shard_map/ppermute | solution.py:259
  32.9 5.0 %collective-permute-start.8 = (bf16[2,128,512]{2,1,0:T(8,128)(2,1)S(1)}, bf16[2,128,512]{2,1,0:T(8,128)(2,1)S(1)}, u32[]{:S(2)}, u32[]{:S(2)}) collective-permute-start(bf16[2,128,512]{2,1,0:T(8,128)(2,1)S(1)} %slice.69.refs_2_), channel_id=1, source_target_pairs={{0,1},{1,0},{2,3},{3,2},{4,5},{5,4},{6,7},{7,6},{8,9},{9,8},{10,11... | collective-permute-start | bytes 786440 | tf_op jit(solution)/shard_map/ppermute | solution.py:259
  33.4 4.5 %collective-permute-start.9 = (bf16[2,128,512]{2,1,0:T(8,128)(2,1)S(1)}, bf16[2,128,512]{2,1,0:T(8,128)(2,1)S(1)}, u32[]{:S(2)}, u32[]{:S(2)}) collective-permute-start(bf16[2,128,512]{2,1,0:T(8,128)(2,1)S(1)} %collective-permute-done.5.refs_3_), channel_id=1, source_target_pairs={{0,1},{1,0},{2,3},{3,2},{4,5},{5,4},{6,7},{7,6},{8,9},{9,8},{10,11... | collective-permute-start | bytes 786440 | tf_op jit(solution)/shard_map/ppermute | solution.py:259
  34.4 6.3 %collective-permute-start.15 = (bf16[128,128]{1,0:T(8,128)(2,1)S(1)}, bf16[128,128]{1,0:T(8,128)(2,1)S(1)}, u32[]{:S(2)}, u32[]{:S(2)}) collective-permute-start(bf16[128,128]{1,0:T(8,128)(2,1)S(1)} %bitcast_convert_fusion), channel_id=1, source_target_pairs={{0,2},{1,3},{2,0},{3,1},{4,6},{5,7},{6,4},{7,5},{8,10},{9,11},{10,... | collective-permute-start | bytes 98312 | tf_op jit(solution)/shard_map/ppermute | solution.py:259
  40.4 2.0 %collective-permute-start.14 = (bf16[4,128,512]{2,1,0:T(8,128)(2,1)S(1)}, bf16[4,128,512]{2,1,0:T(8,128)(2,1)S(1)}, u32[]{:S(2)}, u32[]{:S(2)}) collective-permute-start(bf16[4,128,512]{2,1,0:T(8,128)(2,1)S(1)} %collective-permute-done.7.refs_2_), channel_id=1, source_target_pairs={{0,1},{1,0},{2,3},{3,2},{4,5},{5,4},{6,7},{7,6},{8,9},{9,8},{10,11... | collective-permute-start | bytes 1572872 | tf_op jit(solution)/shard_map/ppermute | solution.py:259
  40.7 1.7 %collective-permute-start.16 = (f32[128,128]{1,0:T(8,128)S(1)}, f32[128,128]{1,0:T(8,128)S(1)}, u32[]{:S(2)}, u32[]{:S(2)}) collective-permute-start(f32[128,128]{1,0:T(8,128)S(1)} %bitcast_add_fusion.refs_6_), channel_id=1, source_target_pairs={{0,1},{1,0},{2,3},{3,2},{4,5},{5,4},{6,7},{7,6},{8,9},{9,8},{10,11... | collective-permute-start | bytes 196616 | tf_op jit(solution)/shard_map/ppermute | solution.py:259
  44.3 1.6 %collective-permute-start.17 = (bf16[2,128,512]{2,1,0:T(8,128)(2,1)S(1)}, bf16[2,128,512]{2,1,0:T(8,128)(2,1)S(1)}, u32[]{:S(2)}, u32[]{:S(2)}) collective-permute-start(bf16[2,128,512]{2,1,0:T(8,128)(2,1)S(1)} %shard_map.76), channel_id=1, source_target_pairs={{0,1},{1,0},{2,3},{3,2},{4,5},{5,4},{6,7},{7,6},{8,9},{9,8},{10,11... | collective-permute-start | bytes 786440 | tf_op jit(solution)/shard_map/ppermute | solution.py:259
  46.6 3.1 %collective-permute-start.18 = (bf16[2,128,512]{2,1,0:T(8,128)(2,1)S(1)}, bf16[2,128,512]{2,1,0:T(8,128)(2,1)S(1)}, u32[]{:S(2)}, u32[]{:S(2)}) collective-permute-start(bf16[2,128,512]{2,1,0:T(8,128)(2,1)S(1)} %get-tuple-element.94), channel_id=1, source_target_pairs={{0,1},{1,0},{2,3},{3,2},{4,5},{5,4},{6,7},{7,6},{8,9},{9,8},{10,11... | collective-permute-start | bytes 786440 | tf_op jit(solution)/shard_map/ppermute | solution.py:259
  46.8 6.4 %collective-permute-start.22 = (bf16[2,128,512]{2,1,0:T(8,128)(2,1)S(1)}, bf16[2,128,512]{2,1,0:T(8,128)(2,1)S(1)}, u32[]{:S(2)}, u32[]{:S(2)}) collective-permute-start(bf16[2,128,512]{2,1,0:T(8,128)(2,1)S(1)} %add_convert_fusion.4), channel_id=1, source_target_pairs={{0,2},{1,5},{2,0},{3,7},{4,6},{5,1},{6,4},{7,3},{8,10},{9,13},{10,... | collective-permute-start | bytes 786440 | tf_op jit(solution)/shard_map/ppermute | solution.py:262
  48.4 2.7 %collective-permute-start.21 = (bf16[2,128,512]{2,1,0:T(8,128)(2,1)S(1)}, bf16[2,128,512]{2,1,0:T(8,128)(2,1)S(1)}, u32[]{:S(2)}, u32[]{:S(2)}) collective-permute-start(bf16[2,128,512]{2,1,0:T(8,128)(2,1)S(1)} %get-tuple-element.100), channel_id=1, source_target_pairs={{0,1},{1,0},{2,3},{3,2},{4,5},{5,4},{6,7},{7,6},{8,9},{9,8},{10,11... | collective-permute-start | bytes 786440 | tf_op jit(solution)/shard_map/ppermute | solution.py:259
  49.2 8.4 %collective-permute-start.23 = (bf16[4,128,512]{2,1,0:T(8,128)(2,1)S(1)}, bf16[4,128,512]{2,1,0:T(8,128)(2,1)S(1)}, u32[]{:S(2)}, u32[]{:S(2)}) collective-permute-start(bf16[4,128,512]{2,1,0:T(8,128)(2,1)S(1)} %get-tuple-element.92), channel_id=1, source_target_pairs={{0,1},{1,0},{2,3},{3,2},{4,5},{5,4},{6,7},{7,6},{8,9},{9,8},{10,11... | collective-permute-start | bytes 1572872 | tf_op jit(solution)/shard_map/ppermute | solution.py:259
  49.7 7.1 %collective-permute-start.19 = (bf16[2,128,512]{2,1,0:T(8,128)(2,1)S(1)}, bf16[2,128,512]{2,1,0:T(8,128)(2,1)S(1)}, u32[]{:S(2)}, u32[]{:S(2)}) collective-permute-start(bf16[2,128,512]{2,1,0:T(8,128)(2,1)S(1)} %add_convert_fusion.3), channel_id=1, source_target_pairs={{0,2},{1,5},{2,0},{3,7},{4,6},{5,1},{6,4},{7,3},{8,10},{9,13},{10,... | collective-permute-start | bytes 786440 | tf_op jit(solution)/shard_map/ppermute | solution.py:262
  50.9 8.6 %collective-permute-start.28 = (bf16[2,128,512]{2,1,0:T(8,128)(2,1)S(1)}, bf16[2,128,512]{2,1,0:T(8,128)(2,1)S(1)}, u32[]{:S(2)}, u32[]{:S(2)}) collective-permute-start(bf16[2,128,512]{2,1,0:T(8,128)(2,1)S(1)} %get-tuple-element.89), channel_id=1, source_target_pairs={{0,1},{1,0},{2,3},{3,2},{4,5},{5,4},{6,7},{7,6},{8,9},{9,8},{10,11... | collective-permute-start | bytes 786440 | tf_op jit(solution)/shard_map/ppermute | solution.py:259
  53.3 7.0 %collective-permute-start.29 = (bf16[2,128,512]{2,1,0:T(8,128)(2,1)S(1)}, bf16[2,128,512]{2,1,0:T(8,128)(2,1)S(1)}, u32[]{:S(2)}, u32[]{:S(2)}) collective-permute-start(bf16[2,128,512]{2,1,0:T(8,128)(2,1)S(1)} %add_convert_fusion.2), channel_id=1, source_target_pairs={{0,4},{1,3},{2,6},{3,1},{4,0},{5,7},{6,2},{7,5},{8,12},{9,11},{10,... | collective-permute-start | bytes 786440 | tf_op jit(solution)/shard_map/ppermute | solution.py:262
  57.7 9.2 %collective-permute-start.24 = (bf16[4,128,512]{2,1,0:T(8,128)(2,1)S(1)}, bf16[4,128,512]{2,1,0:T(8,128)(2,1)S(1)}, u32[]{:S(2)}, u32[]{:S(2)}) collective-permute-start(bf16[4,128,512]{2,1,0:T(8,128)(2,1)S(1)} %add_convert_fusion), channel_id=1, source_target_pairs={{0,2},{1,5},{2,0},{3,7},{4,6},{5,1},{6,4},{7,3},{8,10},{9,13},{10,... | collective-permute-start | bytes 1572872 | tf_op jit(solution)/shard_map/ppermute | solution.py:262
  59.0 3.2 %collective-permute-start.25 = (bf16[2,128,512]{2,1,0:T(8,128)(2,1)S(1)}, bf16[2,128,512]{2,1,0:T(8,128)(2,1)S(1)}, u32[]{:S(2)}, u32[]{:S(2)}) collective-permute-start(bf16[2,128,512]{2,1,0:T(8,128)(2,1)S(1)} %get-tuple-element.103), channel_id=1, source_target_pairs={{0,1},{1,0},{2,3},{3,2},{4,5},{5,4},{6,7},{7,6},{8,9},{9,8},{10,11... | collective-permute-start | bytes 786440 | tf_op jit(solution)/shard_map/ppermute | solution.py:259
  59.0 12.3 %collective-permute-start.20 = (bf16[2,128,512]{2,1,0:T(8,128)(2,1)S(1)}, bf16[2,128,512]{2,1,0:T(8,128)(2,1)S(1)}, u32[]{:S(2)}, u32[]{:S(2)}) collective-permute-start(bf16[2,128,512]{2,1,0:T(8,128)(2,1)S(1)} %get-tuple-element.97), channel_id=1, source_target_pairs={{0,1},{1,0},{2,3},{3,2},{4,5},{5,4},{6,7},{7,6},{8,9},{9,8},{10,11... | collective-permute-start | bytes 786440 | tf_op jit(solution)/shard_map/ppermute | solution.py:259
  60.5 8.2 %collective-permute-start.30 = (bf16[1,128,512]{2,1,0:T(8,128)(2,1)S(1)}, bf16[1,128,512]{2,1,0:T(8,128)(2,1)S(1)}, u32[]{:S(2)}, u32[]{:S(2)}) collective-permute-start(bf16[1,128,512]{2,1,0:T(8,128)(2,1)S(1)} %slice.113), channel_id=1, source_target_pairs={{0,8},{1,17},{2,10},{3,19},{4,12},{5,21},{6,14},{7,23},{8,0},{9,25... | collective-permute-start | bytes 393224 | tf_op jit(solution)/shard_map/ppermute | solution.py:262
  67.1 6.4 %collective-permute-start.26 = (bf16[2,128,512]{2,1,0:T(8,128)(2,1)S(1)}, bf16[2,128,512]{2,1,0:T(8,128)(2,1)S(1)}, u32[]{:S(2)}, u32[]{:S(2)}) collective-permute-start(bf16[2,128,512]{2,1,0:T(8,128)(2,1)S(1)} %add_convert_fusion.1), channel_id=1, source_target_pairs={{0,4},{1,3},{2,6},{3,1},{4,0},{5,7},{6,2},{7,5},{8,12},{9,11},{10,... | collective-permute-start | bytes 786440 | tf_op jit(solution)/shard_map/ppermute | solution.py:262
  68.7 9.4 %collective-permute-start.31 = (bf16[1,128,512]{2,1,0:T(8,128)(2,1)S(1)}, bf16[1,128,512]{2,1,0:T(8,128)(2,1)S(1)}, u32[]{:S(2)}, u32[]{:S(2)}) collective-permute-start(bf16[1,128,512]{2,1,0:T(8,128)(2,1)S(1)} %fusion), channel_id=1, source_target_pairs={{0,16},{1,9},{2,18},{3,11},{4,20},{5,13},{6,22},{7,15},{8,24},{9,1... | collective-permute-start | bytes 393224 | tf_op jit(solution)/shard_map/ppermute | solution.py:262
  73.7 6.4 %collective-permute-start.27 = (bf16[1,128,512]{2,1,0:T(8,128)(2,1)S(1)}, bf16[1,128,512]{2,1,0:T(8,128)(2,1)S(1)}, u32[]{:S(2)}, u32[]{:S(2)}) collective-permute-start(bf16[1,128,512]{2,1,0:T(8,128)(2,1)S(1)} %slice.114), channel_id=1, source_target_pairs={{0,8},{1,17},{2,10},{3,19},{4,12},{5,21},{6,14},{7,23},{8,0},{9,25... | collective-permute-start | bytes 393224 | tf_op jit(solution)/shard_map/ppermute | solution.py:262

commit v14 on v13

--- a/solution.py
+++ b/solution.py
@@ -374,11 +374,10 @@
     project = functools.partial(output_call, held=far_held, width=width)
     home, one, two, corner = symbols_of(far)
     sent = project(attended, groups=theirs([corner]))
-    own = project(after(attended, *sent), groups=ours([corner, one, two, home]))
-    first = added_up(own[0], swap(sent[0], CORE)).astype(bf16)
-    from_corner = turn(first, 0)
-    sent = project(after(attended, first), groups=theirs([one, two, home]))
-    one, two, home = paired(own[1:], sent)
+    sent += project(after(attended, *sent), groups=theirs([one, two, home]))
+    own = project(after(attended, sent[-1]), groups=ours([corner, one, two, home]))
+    corner, one, two, home = paired(own, sent)
+    from_corner = turn(added_up(*corner).astype(bf16), 0)
     got_one = turn(added_up(*one).astype(bf16), 0)
     far_two = added_up(*two, from_corner).astype(bf16)
     far_sum = added_up(*home, got_one, turn(far_two, 1))
@@ -388,11 +387,10 @@
     pairs = paired(own, sent)
     first = added_up(after(pairs[0][0], far_two), pairs[0][1]).astype(bf16)
     near_home, near_two = round_square(first, *pairs[1:])
+    far_got = along(far_sum.astype(bf16), 1)
+    near_sum = added_up(*near_home, turn(near_two, 1), far_got)
     k = len(low)
-    far_sum = added_up(far_sum[:k], along(far_sum[k:].astype(bf16), 0))
-    far_got = along(far_sum.astype(bf16), 1)
-    near_sum = added_up(*near_home, turn(near_two, 1))
-    home_sum = added_up(near_sum[:k], along(near_sum[k:].astype(bf16), 0), far_got)
+    home_sum = added_up(near_sum[:k], along(near_sum[k:].astype(bf16), 0))
     out = added_up(home_sum[0], *[swap(home_sum[i].astype(bf16), o) for i, o in enumerate(low) if o])
     return out.astype(bf16)
 

time: 81 us -> 79.4 us (0.980)
  waiting for transfers between devices: 24.8 us -> 23.3 us
    ppermute x15 -> x14, waiting for transfers between devices: 23.2 us -> 22.3 us  [by_core(): lax.ppermute(x, 'wide', [(i, i ^ pair[(step + (i & CORE)) % 2]) for i in...]
    ppermute x15 -> x14, starting transfers between devices: 25.8 us -> 25.8 us  [by_core(): lax.ppermute(x, 'wide', [(i, i ^ pair[(step + (i & CORE)) % 2]) for i in...]
  transfers between devices with their start and end apart: 32 -> 31, of which waited for: 13 -> 12; matrix products, arithmetic and copies ran while one was open for 2% -> 2% of each run, Pallas kernels for 19% -> 20%
where the time goes in v14:
time: 79.4 us; the launch traced here: 79.3 us
  starting transfers between devices  33 us (42%)
  waiting for transfers between devices  23.3 us (29%)
  Pallas kernels  20.3 us (26%)
  other arithmetic  2.19 us (3%)
    ppermute x14, starting transfers between devices, by_core(): lax.ppermute(x, 'wide', [(i, i ^ pair[(step + (i & CORE)) % 2]) for i in...  25.8 us
    ppermute x14, waiting for transfers between devices, by_core(): lax.ppermute(x, 'wide', [(i, i ^ pair[(step + (i & CORE)) % 2]) for i in...  22.3 us
    pallas_call x2, Pallas kernels, fetched(): pl.pallas_call(functools.partial(fetch_kernel, symbols, width), out_shape...  8.85 us
    ppermute x17, starting transfers between devices, swap(): return lax.ppermute(x, 'wide', [(i, i ^ offset) for i in range(n)])  7.14 us
    pallas_call x4, Pallas kernels, query_call(): pl.pallas_call(functools.partial(query_kernel, places, bool(carry), bool(...  5.87 us
    pallas_call x5, Pallas kernels, output_call(): pl.pallas_call(functools.partial(output_kernel, spots), out_shape=[jax.Sh...  3.02 us
    pallas_call x1, Pallas kernels, kv_terms(): pl.pallas_call(functools.partial(kv_kernel, shared), out_shape=[jax.Shape...  2.55 us
  transfers between devices with their start and end apart: 31, of which 12 were waited for; matrix products, arithmetic and copies ran while one was open for 2% of the time, Pallas kernels for 20%

profile of v14, /device:TPU:0, one launch (start us, length us, event | category | flops | bytes accessed | tf_op | source)
XLA Modules:
  0.0 79.3 jit_solution(11683495395475807845)
XLA Ops:
  0.1 2.6 %shard_map.69 = (f32[8,128,128]{2,1,0:T(8,128)S(1)}, f32[8,128,128]{2,1,0:T(8,128)S(1)}, bf16[128,512]{1,0:T(8,128)(2,1)S(1)}, f32[1,16384]{1,0:T(1,128)S(1)}) custom-call(s32[9]{0:T(128)S(1)} %stack.42.where.refs_0_, bf16[128,512]{1,0:T(8,128)(2,1)} %act.1, f32[1,16384]{1,0:T(1,128)} %bitcast.22, bf16[512,1024]{1,0:T(8,128)(2,1)} %wk.1, bf16[512,1024]{1,0:T(8,128)(2,1)} %wv.1), custom_call_target="tpu_custom_call" | custom-call | flops 4294967296 | bytes 33554432 | tf_op jit(solution)/shard_map/pallas_call | solution.py:108
  2.6 0.5 collective-permute-start.1
  3.2 2.6 %collective-permute-start = (bf16[1,128,512]{2,1,0:T(8,128)(2,1)S(1)}, bf16[1,128,512]{2,1,0:T(8,128)(2,1)S(1)}, u32[]{:S(2)}, u32[]{:S(2)}) collective-permute-start(bf16[1,128,512]{2,1,0:T(8,128)(2,1)S(1)} %bitcast.18), channel_id=1, source_target_pairs={{0,8},{1,17},{2,10},{3,19},{4,12},{5,21},{6,14},{7,23},{8,0},{9,25... | collective-permute-start | bytes 393224 | tf_op jit(solution)/shard_map/ppermute | solution.py:262
  5.9 1.8 %collective-permute-start.2 = (bf16[4,128,128]{2,1,0:T(8,128)(2,1)S(1)}, bf16[4,128,128]{2,1,0:T(8,128)(2,1)S(1)}, u32[]{:S(2)}, u32[]{:S(2)}) collective-permute-start(bf16[4,128,128]{2,1,0:T(8,128)(2,1)S(1)} %slice.97), channel_id=1, source_target_pairs={{0,4},{1,5},{2,6},{3,7},{4,0},{5,1},{6,2},{7,3},{8,12},{9,13},{10,... | collective-permute-start | bytes 393224 | tf_op jit(solution)/shard_map/ppermute | solution.py:259
  7.8 2.1 %collective-permute-done = bf16[1,128,512]{2,1,0:T(8,128)(2,1)S(1)} collective-permute-done((bf16[1,128,512]{2,1,0:T(8,128)(2,1)S(1)}, bf16[1,128,512]{2,1,0:T(8,128)(2,1)S(1)}, u32[]{:S(2)}, u32[]{:S(2)}) %collective-permute-start) | collective-permute-done | bytes 131104 | tf_op jit(solution)/shard_map/ppermute | solution.py:262
  9.9 2.2 %collective-permute-start.4 = (bf16[2,128,512]{2,1,0:T(8,128)(2,1)S(1)}, bf16[2,128,512]{2,1,0:T(8,128)(2,1)S(1)}, u32[]{:S(2)}, u32[]{:S(2)}) collective-permute-start(bf16[2,128,512]{2,1,0:T(8,128)(2,1)S(1)} %pad_maximum_fusion.3.refs_2_), channel_id=1, source_target_pairs={{0,2},{1,5},{2,0},{3,7},{4,6},{5,1},{6,4},{7,3},{8,10},{9,13},{10,... | collective-permute-start | bytes 786440 | tf_op jit(solution)/shard_map/ppermute | solution.py:262
  12.2 2.3 %collective-permute-start.3 = (bf16[2,128,640]{2,1,0:T(8,128)(2,1)S(1)}, bf16[2,128,640]{2,1,0:T(8,128)(2,1)S(1)}, u32[]{:S(2)}, u32[]{:S(2)}) collective-permute-start(bf16[2,128,640]{2,1,0:T(8,128)(2,1)S(1)} %pad_maximum_fusion.2), channel_id=1, source_target_pairs={{0,16},{1,9},{2,18},{3,11},{4,20},{5,13},{6,22},{7,15},{8,24},{9,1... | collective-permute-start | bytes 983048 | tf_op jit(solution)/shard_map/ppermute | solution.py:262
  14.5 2.0 %collective-permute-done.4.refs_3_ = bf16[2,128,512]{2,1,0:T(8,128)(2,1)S(1)} collective-permute-done((bf16[2,128,512]{2,1,0:T(8,128)(2,1)S(1)}, bf16[2,128,512]{2,1,0:T(8,128)(2,1)S(1)}, u32[]{:S(2)}, u32[]{:S(2)}) %collective-permute-start.4) | collective-permute-done | bytes 262176 | tf_op jit(solution)/shard_map/ppermute | solution.py:262
  16.6 2.1 %collective-permute-start.10 = (bf16[4,128,512]{2,1,0:T(8,128)(2,1)S(1)}, bf16[4,128,512]{2,1,0:T(8,128)(2,1)S(1)}, u32[]{:S(2)}, u32[]{:S(2)}) collective-permute-start(bf16[4,128,512]{2,1,0:T(8,128)(2,1)S(1)} %pad_maximum_fusion), channel_id=1, source_target_pairs={{0,4},{1,3},{2,6},{3,1},{4,0},{5,7},{6,2},{7,5},{8,12},{9,11},{10,... | collective-permute-start | bytes 1572872 | tf_op jit(solution)/shard_map/ppermute | solution.py:262
  18.7 4.4 %shard_map.70.weight = bf16[16,512,512]{2,1,0:T(8,128)(2,1)S(1)} custom-call(s32[9]{0:T(128)S(1)} %stack.42.where.refs_0_, bf16[512,16384]{1,0:T(8,128)(2,1)} %source.3), custom_call_target="tpu_custom_call" | custom-call | bytes 16777216 | tf_op jit(solution)/shard_map/pallas_call | solution.py:67
  23.1 0.8 collective-permute-done.3
  23.9 1.9 %collective-permute-start.5 = (bf16[2,128,512]{2,1,0:T(8,128)(2,1)S(1)}, bf16[2,128,512]{2,1,0:T(8,128)(2,1)S(1)}, u32[]{:S(2)}, u32[]{:S(2)}) collective-permute-start(bf16[2,128,512]{2,1,0:T(8,128)(2,1)S(1)} %slice.62.refs_2_), channel_id=1, source_target_pairs={{0,2},{1,5},{2,0},{3,7},{4,6},{5,1},{6,4},{7,3},{8,10},{9,13},{10,... | collective-permute-start | bytes 786440 | tf_op jit(solution)/shard_map/ppermute | solution.py:262
  26.0 4.5 %shard_map.71.weight = bf16[16,512,512]{2,1,0:T(8,128)(2,1)S(1)} custom-call(s32[9]{0:T(128)S(1)} %stack.42.where.refs_0_, bf16[512,16384]{1,0:T(8,128)(2,1)} %source.3), custom_call_target="tpu_custom_call" | custom-call | bytes 16777216 | tf_op jit(solution)/shard_map/pallas_call | solution.py:67
  30.6 0.5 collective-permute-start.11
  31.2 1.7 %collective-permute-start.7 = (bf16[4,128,512]{2,1,0:T(8,128)(2,1)S(1)}, bf16[4,128,512]{2,1,0:T(8,128)(2,1)S(1)}, u32[]{:S(2)}, u32[]{:S(2)}) collective-permute-start(bf16[4,128,512]{2,1,0:T(8,128)(2,1)S(1)} %pad_maximum_fusion.1), channel_id=1, source_target_pairs={{0,4},{1,3},{2,6},{3,1},{4,0},{5,7},{6,2},{7,5},{8,12},{9,11},{10,... | collective-permute-start | bytes 1572872 | tf_op jit(solution)/shard_map/ppermute | solution.py:262
  32.9 0.5 collective-permute-start.8
  33.5 0.9 %collective-permute-done.12.refs_6_ = bf16[2,128,512]{2,1,0:T(8,128)(2,1)S(1)} collective-permute-done((bf16[2,128,512]{2,1,0:T(8,128)(2,1)S(1)}, bf16[2,128,512]{2,1,0:T(8,128)(2,1)S(1)}, u32[]{:S(2)}, u32[]{:S(2)}) %collective-permute-start.12) | collective-permute-done | bytes 262176 | tf_op jit(solution)/shard_map/ppermute | solution.py:259
  34.4 1.5 %collective-permute-start.15 = (bf16[128,128]{1,0:T(8,128)(2,1)S(1)}, bf16[128,128]{1,0:T(8,128)(2,1)S(1)}, u32[]{:S(2)}, u32[]{:S(2)}) collective-permute-start(bf16[128,128]{1,0:T(8,128)(2,1)S(1)} %bitcast_convert_fusion), channel_id=1, source_target_pairs={{0,2},{1,3},{2,0},{3,1},{4,6},{5,7},{6,4},{7,5},{8,10},{9,11},{10,... | collective-permute-start | bytes 98312 | tf_op jit(solution)/shard_map/ppermute | solution.py:259
  35.9 2.0 %shard_map.72 = (f32[128,512]{1,0:T(8,128)S(1)}, f32[128,128]{1,0:T(8,128)S(1)}) custom-call(s32[9]{0:T(128)S(1)} %stack.42.where.refs_0_, f32[1,16384]{1,0:T(1,128)S(1)} %get-tuple-element.64.refs_1_, bf16[2,128,512]{2,1,0:T(8,128)(2,1)S(1)} %pad_maximum_fusion.3.refs_2_, bf16[2,128,512]{2,1,0:T(8,128)(2,1)S(1)} %collective-permute-done.4.refs_3_, ...), custom_call_target="tpu_custom_call" | custom-call | flops 1073741824 | bytes 8388608 | tf_op jit(solution)/shard_map/pallas_call | solution.py:201
  37.9 1.3 %shard_map.73 = (f32[128,512]{1,0:T(8,128)S(1)}, f32[128,128]{1,0:T(8,128)S(1)}) custom-call(s32[9]{0:T(128)S(1)} %stack.42.where.refs_0_, f32[1,16384]{1,0:T(1,128)S(1)} %get-tuple-element.64.refs_1_, bf16[2,128,512]{2,1,0:T(8,128)(2,1)S(1)} %slice.62.refs_2_, bf16[2,128,512]{2,1,0:T(8,128)(2,1)S(1)} %collective-permute-done.5.refs_3_, ...), custom_call_target="tpu_custom_call" | custom-call | flops 536870912 | bytes 4194304 | tf_op jit(solution)/shard_map/pallas_call | solution.py:201
  39.2 1.2 %collective-permute-done.7.refs_2_ = bf16[4,128,512]{2,1,0:T(8,128)(2,1)S(1)} collective-permute-done((bf16[4,128,512]{2,1,0:T(8,128)(2,1)S(1)}, bf16[4,128,512]{2,1,0:T(8,128)(2,1)S(1)}, u32[]{:S(2)}, u32[]{:S(2)}) %collective-permute-start.7) | collective-permute-done | bytes 524320 | tf_op jit(solution)/shard_map/ppermute | solution.py:262
  40.4 0.3 fusion.4
  40.7 0.6 collective-permute-start.16
  41.4 1.0 %shard_map.74 = (f32[128,512]{1,0:T(8,128)S(1)}, f32[128,128]{1,0:T(8,128)S(1)}) custom-call(s32[9]{0:T(128)S(1)} %stack.42.where.refs_0_, f32[1,16384]{1,0:T(1,128)S(1)} %get-tuple-element.64.refs_1_, bf16[4,128,512]{2,1,0:T(8,128)(2,1)S(1)} %collective-permute-done.7.refs_2_, bf16[16384,512]{1,0:T(8,128)(2,1)S(1)} %bitcast.17, ...), custom_call_target="tpu_custom_call" | custom-call | flops 268435456 | bytes 2097152 | tf_op jit(solution)/shard_map/pallas_call | solution.py:201
  42.4 1.6 %shard_map.75.attended = bf16[128,512]{1,0:T(8,128)(2,1)S(1)} custom-call(s32[9]{0:T(128)S(1)} %stack.42.where.refs_0_, f32[1,16384]{1,0:T(1,128)S(1)} %get-tuple-element.64.refs_1_, bf16[4,128,512]{2,1,0:T(8,128)(2,1)S(1)} %collective-permute-done.14.refs_2_, bf16[16384,512]{1,0:T(8,128)(2,1)S(1)} %bitcast.17, f32[128,512]{1,0:T(8,128)S(1)} %get-tuple-element.81.refs_4_, ...), custom_call_target="tpu_custom_call" | custom-call | flops 268435456 | bytes 2097152 | tf_op jit(solution)/shard_map/pallas_call | solution.py:201
  44.0 0.3 shard_map.76
  44.3 0.2 collective-permute-start.21
  44.5 0.6 shard_map.77
  45.1 0.4 collective-permute-start.20
  45.7 0.7 shard_map.79
  46.5 1.6 %collective-permute-start.22 = (bf16[2,128,512]{2,1,0:T(8,128)(2,1)S(1)}, bf16[2,128,512]{2,1,0:T(8,128)(2,1)S(1)}, u32[]{:S(2)}, u32[]{:S(2)}) collective-permute-start(bf16[2,128,512]{2,1,0:T(8,128)(2,1)S(1)} %add_convert_fusion.4), channel_id=1, source_target_pairs={{0,2},{1,5},{2,0},{3,7},{4,6},{5,1},{6,4},{7,3},{8,10},{9,13},{10,... | collective-permute-start | bytes 786440 | tf_op jit(solution)/shard_map/ppermute | solution.py:262
  48.1 0.7 shard_map.78
  49.1 1.6 %collective-permute-start.18 = (bf16[2,128,512]{2,1,0:T(8,128)(2,1)S(1)}, bf16[2,128,512]{2,1,0:T(8,128)(2,1)S(1)}, u32[]{:S(2)}, u32[]{:S(2)}) collective-permute-start(bf16[2,128,512]{2,1,0:T(8,128)(2,1)S(1)} %add_convert_fusion.5), channel_id=1, source_target_pairs={{0,2},{1,5},{2,0},{3,7},{4,6},{5,1},{6,4},{7,3},{8,10},{9,13},{10,... | collective-permute-start | bytes 786440 | tf_op jit(solution)/shard_map/ppermute | solution.py:262
  50.8 2.1 %collective-permute-done.22 = bf16[2,128,512]{2,1,0:T(8,128)(2,1)S(1)} collective-permute-done((bf16[2,128,512]{2,1,0:T(8,128)(2,1)S(1)}, bf16[2,128,512]{2,1,0:T(8,128)(2,1)S(1)}, u32[]{:S(2)}, u32[]{:S(2)}) %collective-permute-start.22) | collective-permute-done | bytes 262176 | tf_op jit(solution)/shard_map/ppermute | solution.py:262
  53.1 1.7 %collective-permute-start.28 = (bf16[2,128,512]{2,1,0:T(8,128)(2,1)S(1)}, bf16[2,128,512]{2,1,0:T(8,128)(2,1)S(1)}, u32[]{:S(2)}, u32[]{:S(2)}) collective-permute-start(bf16[2,128,512]{2,1,0:T(8,128)(2,1)S(1)} %add_convert_fusion.3), channel_id=1, source_target_pairs={{0,4},{1,3},{2,6},{3,1},{4,0},{5,7},{6,2},{7,5},{8,12},{9,11},{10,... | collective-permute-start | bytes 786440 | tf_op jit(solution)/shard_map/ppermute | solution.py:262
  54.7 1.5 %collective-permute-done.18 = bf16[2,128,512]{2,1,0:T(8,128)(2,1)S(1)} collective-permute-done((bf16[2,128,512]{2,1,0:T(8,128)(2,1)S(1)}, bf16[2,128,512]{2,1,0:T(8,128)(2,1)S(1)}, u32[]{:S(2)}, u32[]{:S(2)}) %collective-permute-start.18) | collective-permute-done | bytes 262176 | tf_op jit(solution)/shard_map/ppermute | solution.py:262
  56.2 0.7 shard_map.80
  57.1 1.6 %collective-permute-start.24 = (bf16[4,128,512]{2,1,0:T(8,128)(2,1)S(1)}, bf16[4,128,512]{2,1,0:T(8,128)(2,1)S(1)}, u32[]{:S(2)}, u32[]{:S(2)}) collective-permute-start(bf16[4,128,512]{2,1,0:T(8,128)(2,1)S(1)} %add_convert_fusion), channel_id=1, source_target_pairs={{0,2},{1,5},{2,0},{3,7},{4,6},{5,1},{6,4},{7,3},{8,10},{9,13},{10,... | collective-permute-start | bytes 1572872 | tf_op jit(solution)/shard_map/ppermute | solution.py:262
  58.7 0.5 collective-permute-start.19
  59.2 0.8 %collective-permute-done.28 = bf16[2,128,512]{2,1,0:T(8,128)(2,1)S(1)} collective-permute-done((bf16[2,128,512]{2,1,0:T(8,128)(2,1)S(1)}, bf16[2,128,512]{2,1,0:T(8,128)(2,1)S(1)}, u32[]{:S(2)}, u32[]{:S(2)}) %collective-permute-start.28) | collective-permute-done | bytes 262176 | tf_op jit(solution)/shard_map/ppermute | solution.py:262
  60.2 2.9 %collective-permute-start.29 = (bf16[2,128,512]{2,1,0:T(8,128)(2,1)S(1)}, bf16[2,128,512]{2,1,0:T(8,128)(2,1)S(1)}, u32[]{:S(2)}, u32[]{:S(2)}) collective-permute-start(bf16[2,128,512]{2,1,0:T(8,128)(2,1)S(1)} %add_convert_fusion.1), channel_id=1, source_target_pairs={{0,16},{1,9},{2,18},{3,11},{4,20},{5,13},{6,22},{7,15},{8,24},{9,1... | collective-permute-start | bytes 786440 | tf_op jit(solution)/shard_map/ppermute | solution.py:262
  63.1 3.2 %collective-permute-done.24 = bf16[4,128,512]{2,1,0:T(8,128)(2,1)S(1)} collective-permute-done((bf16[4,128,512]{2,1,0:T(8,128)(2,1)S(1)}, bf16[4,128,512]{2,1,0:T(8,128)(2,1)S(1)}, u32[]{:S(2)}, u32[]{:S(2)}) %collective-permute-start.24) | collective-permute-done | bytes 524320 | tf_op jit(solution)/shard_map/ppermute | solution.py:262
  66.4 1.7 %collective-permute-start.26 = (bf16[2,128,512]{2,1,0:T(8,128)(2,1)S(1)}, bf16[2,128,512]{2,1,0:T(8,128)(2,1)S(1)}, u32[]{:S(2)}, u32[]{:S(2)}) collective-permute-start(bf16[2,128,512]{2,1,0:T(8,128)(2,1)S(1)} %add_convert_fusion.2), channel_id=1, source_target_pairs={{0,4},{1,3},{2,6},{3,1},{4,0},{5,7},{6,2},{7,5},{8,12},{9,11},{10,... | collective-permute-start | bytes 786440 | tf_op jit(solution)/shard_map/ppermute | solution.py:262
  68.1 2.3 %collective-permute-done.29 = bf16[2,128,512]{2,1,0:T(8,128)(2,1)S(1)} collective-permute-done((bf16[2,128,512]{2,1,0:T(8,128)(2,1)S(1)}, bf16[2,128,512]{2,1,0:T(8,128)(2,1)S(1)}, u32[]{:S(2)}, u32[]{:S(2)}) %collective-permute-start.29) | collective-permute-done | bytes 262176 | tf_op jit(solution)/shard_map/ppermute | solution.py:262
  70.4 2.5 %collective-permute-done.26 = bf16[2,128,512]{2,1,0:T(8,128)(2,1)S(1)} collective-permute-done((bf16[2,128,512]{2,1,0:T(8,128)(2,1)S(1)}, bf16[2,128,512]{2,1,0:T(8,128)(2,1)S(1)}, u32[]{:S(2)}, u32[]{:S(2)}) %collective-permute-start.26) | collective-permute-done | bytes 262176 | tf_op jit(solution)/shard_map/ppermute | solution.py:262
  73.1 1.6 %collective-permute-start.30 = (bf16[1,128,512]{2,1,0:T(8,128)(2,1)S(1)}, bf16[1,128,512]{2,1,0:T(8,128)(2,1)S(1)}, u32[]{:S(2)}, u32[]{:S(2)}) collective-permute-start(bf16[1,128,512]{2,1,0:T(8,128)(2,1)S(1)} %slice.96), channel_id=1, source_target_pairs={{0,8},{1,17},{2,10},{3,19},{4,12},{5,21},{6,14},{7,23},{8,0},{9,25... | collective-permute-start | bytes 393224 | tf_op jit(solution)/shard_map/ppermute | solution.py:262
  74.7 3.9 %collective-permute-done.30 = bf16[1,128,512]{2,1,0:T(8,128)(2,1)S(1)} collective-permute-done((bf16[1,128,512]{2,1,0:T(8,128)(2,1)S(1)}, bf16[1,128,512]{2,1,0:T(8,128)(2,1)S(1)}, u32[]{:S(2)}, u32[]{:S(2)}) %collective-permute-start.30) | collective-permute-done | bytes 131104 | tf_op jit(solution)/shard_map/ppermute | solution.py:262
  78.6 0.7 fusion.1
  (62 shorter events, 2.2 us)
Async XLA Ops:
  2.6 3.2 %collective-permute-start.1 = (f32[8,128,128]{2,1,0:T(8,128)S(1)}, f32[8,128,128]{2,1,0:T(8,128)S(1)}, u32[]{:S(2)}, u32[]{:S(2)}) collective-permute-start(f32[8,128,128]{2,1,0:T(8,128)S(1)} %get-tuple-element.67), channel_id=1, source_target_pairs={{0,1},{1,0},{2,3},{3,2},{4,5},{5,4},{6,7},{7,6},{8,9},{9,8},{10,11... | collective-permute-start | bytes 1572872 | tf_op jit(solution)/shard_map/ppermute | solution.py:259
  3.2 6.7 %collective-permute-start = (bf16[1,128,512]{2,1,0:T(8,128)(2,1)S(1)}, bf16[1,128,512]{2,1,0:T(8,128)(2,1)S(1)}, u32[]{:S(2)}, u32[]{:S(2)}) collective-permute-start(bf16[1,128,512]{2,1,0:T(8,128)(2,1)S(1)} %bitcast.18), channel_id=1, source_target_pairs={{0,8},{1,17},{2,10},{3,19},{4,12},{5,21},{6,14},{7,23},{8,0},{9,25... | collective-permute-start | bytes 393224 | tf_op jit(solution)/shard_map/ppermute | solution.py:262
  5.9 6.2 %collective-permute-start.2 = (bf16[4,128,128]{2,1,0:T(8,128)(2,1)S(1)}, bf16[4,128,128]{2,1,0:T(8,128)(2,1)S(1)}, u32[]{:S(2)}, u32[]{:S(2)}) collective-permute-start(bf16[4,128,128]{2,1,0:T(8,128)(2,1)S(1)} %slice.97), channel_id=1, source_target_pairs={{0,4},{1,5},{2,6},{3,7},{4,0},{5,1},{6,2},{7,3},{8,12},{9,13},{10,... | collective-permute-start | bytes 393224 | tf_op jit(solution)/shard_map/ppermute | solution.py:259
  9.9 6.6 %collective-permute-start.4 = (bf16[2,128,512]{2,1,0:T(8,128)(2,1)S(1)}, bf16[2,128,512]{2,1,0:T(8,128)(2,1)S(1)}, u32[]{:S(2)}, u32[]{:S(2)}) collective-permute-start(bf16[2,128,512]{2,1,0:T(8,128)(2,1)S(1)} %pad_maximum_fusion.3.refs_2_), channel_id=1, source_target_pairs={{0,2},{1,5},{2,0},{3,7},{4,6},{5,1},{6,4},{7,3},{8,10},{9,13},{10,... | collective-permute-start | bytes 786440 | tf_op jit(solution)/shard_map/ppermute | solution.py:262
  12.2 11.6 %collective-permute-start.3 = (bf16[2,128,640]{2,1,0:T(8,128)(2,1)S(1)}, bf16[2,128,640]{2,1,0:T(8,128)(2,1)S(1)}, u32[]{:S(2)}, u32[]{:S(2)}) collective-permute-start(bf16[2,128,640]{2,1,0:T(8,128)(2,1)S(1)} %pad_maximum_fusion.2), channel_id=1, source_target_pairs={{0,16},{1,9},{2,18},{3,11},{4,20},{5,13},{6,22},{7,15},{8,24},{9,1... | collective-permute-start | bytes 983048 | tf_op jit(solution)/shard_map/ppermute | solution.py:262
  16.6 14.0 %collective-permute-start.10 = (bf16[4,128,512]{2,1,0:T(8,128)(2,1)S(1)}, bf16[4,128,512]{2,1,0:T(8,128)(2,1)S(1)}, u32[]{:S(2)}, u32[]{:S(2)}) collective-permute-start(bf16[4,128,512]{2,1,0:T(8,128)(2,1)S(1)} %pad_maximum_fusion), channel_id=1, source_target_pairs={{0,4},{1,3},{2,6},{3,1},{4,0},{5,7},{6,2},{7,5},{8,12},{9,11},{10,... | collective-permute-start | bytes 1572872 | tf_op jit(solution)/shard_map/ppermute | solution.py:262
  18.7 17.2 %slice-start = ((s8[16777216]{0:T(1024)(128)(4,1)}), s8[4194304]{0:T(1024)(128)(4,1)S(1)}, s32[]{:S(2)}) async-start(s8[16777216]{0:T(1024)(128)(4,1)} %bitcast.16), calls=%async_computation | async-start | bytes 8388608
  18.7 17.2 %slice-start.1 = ((s8[16777216]{0:T(1024)(128)(4,1)}), s8[4194304]{0:T(1024)(128)(4,1)S(1)}, s32[]{:S(2)}) async-start(s8[16777216]{0:T(1024)(128)(4,1)} %bitcast.16), calls=%async_computation.1 | async-start | bytes 8388608
  23.9 6.7 %collective-permute-start.5 = (bf16[2,128,512]{2,1,0:T(8,128)(2,1)S(1)}, bf16[2,128,512]{2,1,0:T(8,128)(2,1)S(1)}, u32[]{:S(2)}, u32[]{:S(2)}) collective-permute-start(bf16[2,128,512]{2,1,0:T(8,128)(2,1)S(1)} %slice.62.refs_2_), channel_id=1, source_target_pairs={{0,2},{1,5},{2,0},{3,7},{4,6},{5,1},{6,4},{7,3},{8,10},{9,13},{10,... | collective-permute-start | bytes 786440 | tf_op jit(solution)/shard_map/ppermute | solution.py:262
  25.8 10.0 %slice-start.2 = ((s8[16777216]{0:T(1024)(128)(4,1)}), s8[4194304]{0:T(1024)(128)(4,1)S(1)}, s32[]{:S(2)}) async-start(s8[16777216]{0:T(1024)(128)(4,1)} %bitcast.16), calls=%async_computation.2 | async-start | bytes 8388608
  25.9 10.0 %slice-start.3 = ((s8[16777216]{0:T(1024)(128)(4,1)}), s8[4194304]{0:T(1024)(128)(4,1)S(1)}, s32[]{:S(2)}) async-start(s8[16777216]{0:T(1024)(128)(4,1)} %bitcast.16), calls=%async_computation.3 | async-start | bytes 8388608
  25.9 4.6 %collective-permute-start.6 = (bf16[1,128,128]{2,1,0:T(8,128)(2,1)S(1)}, bf16[1,128,128]{2,1,0:T(8,128)(2,1)S(1)}, u32[]{:S(2)}, u32[]{:S(2)}) collective-permute-start(bf16[1,128,128]{2,1,0:T(8,128)(2,1)S(1)} %slice.99), channel_id=1, source_target_pairs={{0,8},{1,17},{2,10},{3,19},{4,12},{5,21},{6,14},{7,23},{8,0},{9,25... | collective-permute-start | bytes 98312 | tf_op jit(solution)/shard_map/ppermute | solution.py:262
  30.5 5.3 %collective-permute-start.13 = (bf16[4,128,512]{2,1,0:T(8,128)(2,1)S(1)}, bf16[4,128,512]{2,1,0:T(8,128)(2,1)S(1)}, u32[]{:S(2)}, u32[]{:S(2)}) collective-permute-start(bf16[4,128,512]{2,1,0:T(8,128)(2,1)S(1)} %collective-permute-done.10.refs_4_), channel_id=1, source_target_pairs={{0,1},{1,0},{2,3},{3,2},{4,5},{5,4},{6,7},{7,6},{8,9},{9,8},{10,11... | collective-permute-start | bytes 1572872 | tf_op jit(solution)/shard_map/ppermute | solution.py:259
  30.6 2.7 %collective-permute-start.11 = (bf16[2,128,512]{2,1,0:T(8,128)(2,1)S(1)}, bf16[2,128,512]{2,1,0:T(8,128)(2,1)S(1)}, u32[]{:S(2)}, u32[]{:S(2)}) collective-permute-start(bf16[2,128,512]{2,1,0:T(8,128)(2,1)S(1)} %pad_maximum_fusion.3.refs_2_), channel_id=1, source_target_pairs={{0,1},{1,0},{2,3},{3,2},{4,5},{5,4},{6,7},{7,6},{8,9},{9,8},{10,11... | collective-permute-start | bytes 786440 | tf_op jit(solution)/shard_map/ppermute | solution.py:259
  31.2 9.2 %collective-permute-start.7 = (bf16[4,128,512]{2,1,0:T(8,128)(2,1)S(1)}, bf16[4,128,512]{2,1,0:T(8,128)(2,1)S(1)}, u32[]{:S(2)}, u32[]{:S(2)}) collective-permute-start(bf16[4,128,512]{2,1,0:T(8,128)(2,1)S(1)} %pad_maximum_fusion.1), channel_id=1, source_target_pairs={{0,4},{1,3},{2,6},{3,1},{4,0},{5,7},{6,2},{7,5},{8,12},{9,11},{10,... | collective-permute-start | bytes 1572872 | tf_op jit(solution)/shard_map/ppermute | solution.py:262
  32.8 1.5 %collective-permute-start.12 = (bf16[2,128,512]{2,1,0:T(8,128)(2,1)S(1)}, bf16[2,128,512]{2,1,0:T(8,128)(2,1)S(1)}, u32[]{:S(2)}, u32[]{:S(2)}) collective-permute-start(bf16[2,128,512]{2,1,0:T(8,128)(2,1)S(1)} %collective-permute-done.4.refs_3_), channel_id=1, source_target_pairs={{0,1},{1,0},{2,3},{3,2},{4,5},{5,4},{6,7},{7,6},{8,9},{9,8},{10,11... | collective-permute-start | bytes 786440 | tf_op jit(solution)/shard_map/ppermute | solution.py:259
  32.9 5.0 %collective-permute-start.8 = (bf16[2,128,512]{2,1,0:T(8,128)(2,1)S(1)}, bf16[2,128,512]{2,1,0:T(8,128)(2,1)S(1)}, u32[]{:S(2)}, u32[]{:S(2)}) collective-permute-start(bf16[2,128,512]{2,1,0:T(8,128)(2,1)S(1)} %slice.62.refs_2_), channel_id=1, source_target_pairs={{0,1},{1,0},{2,3},{3,2},{4,5},{5,4},{6,7},{7,6},{8,9},{9,8},{10,11... | collective-permute-start | bytes 786440 | tf_op jit(solution)/shard_map/ppermute | solution.py:259
  33.4 4.5 %collective-permute-start.9 = (bf16[2,128,512]{2,1,0:T(8,128)(2,1)S(1)}, bf16[2,128,512]{2,1,0:T(8,128)(2,1)S(1)}, u32[]{:S(2)}, u32[]{:S(2)}) collective-permute-start(bf16[2,128,512]{2,1,0:T(8,128)(2,1)S(1)} %collective-permute-done.5.refs_3_), channel_id=1, source_target_pairs={{0,1},{1,0},{2,3},{3,2},{4,5},{5,4},{6,7},{7,6},{8,9},{9,8},{10,11... | collective-permute-start | bytes 786440 | tf_op jit(solution)/shard_map/ppermute | solution.py:259
  34.4 6.3 %collective-permute-start.15 = (bf16[128,128]{1,0:T(8,128)(2,1)S(1)}, bf16[128,128]{1,0:T(8,128)(2,1)S(1)}, u32[]{:S(2)}, u32[]{:S(2)}) collective-permute-start(bf16[128,128]{1,0:T(8,128)(2,1)S(1)} %bitcast_convert_fusion), channel_id=1, source_target_pairs={{0,2},{1,3},{2,0},{3,1},{4,6},{5,7},{6,4},{7,5},{8,10},{9,11},{10,... | collective-permute-start | bytes 98312 | tf_op jit(solution)/shard_map/ppermute | solution.py:259
  40.4 2.0 %collective-permute-start.14 = (bf16[4,128,512]{2,1,0:T(8,128)(2,1)S(1)}, bf16[4,128,512]{2,1,0:T(8,128)(2,1)S(1)}, u32[]{:S(2)}, u32[]{:S(2)}) collective-permute-start(bf16[4,128,512]{2,1,0:T(8,128)(2,1)S(1)} %collective-permute-done.7.refs_2_), channel_id=1, source_target_pairs={{0,1},{1,0},{2,3},{3,2},{4,5},{5,4},{6,7},{7,6},{8,9},{9,8},{10,11... | collective-permute-start | bytes 1572872 | tf_op jit(solution)/shard_map/ppermute | solution.py:259
  40.7 1.7 %collective-permute-start.16 = (f32[128,128]{1,0:T(8,128)S(1)}, f32[128,128]{1,0:T(8,128)S(1)}, u32[]{:S(2)}, u32[]{:S(2)}) collective-permute-start(f32[128,128]{1,0:T(8,128)S(1)} %bitcast_add_fusion.refs_6_), channel_id=1, source_target_pairs={{0,1},{1,0},{2,3},{3,2},{4,5},{5,4},{6,7},{7,6},{8,9},{9,8},{10,11... | collective-permute-start | bytes 196616 | tf_op jit(solution)/shard_map/ppermute | solution.py:259
  44.3 2.1 %collective-permute-start.21 = (bf16[2,128,512]{2,1,0:T(8,128)(2,1)S(1)}, bf16[2,128,512]{2,1,0:T(8,128)(2,1)S(1)}, u32[]{:S(2)}, u32[]{:S(2)}) collective-permute-start(bf16[2,128,512]{2,1,0:T(8,128)(2,1)S(1)} %shard_map.76), channel_id=1, source_target_pairs={{0,1},{1,0},{2,3},{3,2},{4,5},{5,4},{6,7},{7,6},{8,9},{9,8},{10,11... | collective-permute-start | bytes 786440 | tf_op jit(solution)/shard_map/ppermute | solution.py:259
  45.1 5.7 %collective-permute-start.20 = (bf16[2,128,512]{2,1,0:T(8,128)(2,1)S(1)}, bf16[2,128,512]{2,1,0:T(8,128)(2,1)S(1)}, u32[]{:S(2)}, u32[]{:S(2)}) collective-permute-start(bf16[2,128,512]{2,1,0:T(8,128)(2,1)S(1)} %get-tuple-element.97), channel_id=1, source_target_pairs={{0,1},{1,0},{2,3},{3,2},{4,5},{5,4},{6,7},{7,6},{8,9},{9,8},{10,11... | collective-permute-start | bytes 786440 | tf_op jit(solution)/shard_map/ppermute | solution.py:259
  45.6 3.5 %collective-permute-start.17 = (bf16[2,128,512]{2,1,0:T(8,128)(2,1)S(1)}, bf16[2,128,512]{2,1,0:T(8,128)(2,1)S(1)}, u32[]{:S(2)}, u32[]{:S(2)}) collective-permute-start(bf16[2,128,512]{2,1,0:T(8,128)(2,1)S(1)} %get-tuple-element.91), channel_id=1, source_target_pairs={{0,1},{1,0},{2,3},{3,2},{4,5},{5,4},{6,7},{7,6},{8,9},{9,8},{10,11... | collective-permute-start | bytes 786440 | tf_op jit(solution)/shard_map/ppermute | solution.py:259
  46.5 6.4 %collective-permute-start.22 = (bf16[2,128,512]{2,1,0:T(8,128)(2,1)S(1)}, bf16[2,128,512]{2,1,0:T(8,128)(2,1)S(1)}, u32[]{:S(2)}, u32[]{:S(2)}) collective-permute-start(bf16[2,128,512]{2,1,0:T(8,128)(2,1)S(1)} %add_convert_fusion.4), channel_id=1, source_target_pairs={{0,2},{1,5},{2,0},{3,7},{4,6},{5,1},{6,4},{7,3},{8,10},{9,13},{10,... | collective-permute-start | bytes 786440 | tf_op jit(solution)/shard_map/ppermute | solution.py:262
  48.9 8.1 %collective-permute-start.23 = (bf16[4,128,512]{2,1,0:T(8,128)(2,1)S(1)}, bf16[4,128,512]{2,1,0:T(8,128)(2,1)S(1)}, u32[]{:S(2)}, u32[]{:S(2)}) collective-permute-start(bf16[4,128,512]{2,1,0:T(8,128)(2,1)S(1)} %get-tuple-element.89), channel_id=1, source_target_pairs={{0,1},{1,0},{2,3},{3,2},{4,5},{5,4},{6,7},{7,6},{8,9},{9,8},{10,11... | collective-permute-start | bytes 1572872 | tf_op jit(solution)/shard_map/ppermute | solution.py:259
  49.1 7.1 %collective-permute-start.18 = (bf16[2,128,512]{2,1,0:T(8,128)(2,1)S(1)}, bf16[2,128,512]{2,1,0:T(8,128)(2,1)S(1)}, u32[]{:S(2)}, u32[]{:S(2)}) collective-permute-start(bf16[2,128,512]{2,1,0:T(8,128)(2,1)S(1)} %add_convert_fusion.5), channel_id=1, source_target_pairs={{0,2},{1,5},{2,0},{3,7},{4,6},{5,1},{6,4},{7,3},{8,10},{9,13},{10,... | collective-permute-start | bytes 786440 | tf_op jit(solution)/shard_map/ppermute | solution.py:262
  50.7 8.5 %collective-permute-start.27 = (bf16[2,128,512]{2,1,0:T(8,128)(2,1)S(1)}, bf16[2,128,512]{2,1,0:T(8,128)(2,1)S(1)}, u32[]{:S(2)}, u32[]{:S(2)}) collective-permute-start(bf16[2,128,512]{2,1,0:T(8,128)(2,1)S(1)} %get-tuple-element.86), channel_id=1, source_target_pairs={{0,1},{1,0},{2,3},{3,2},{4,5},{5,4},{6,7},{7,6},{8,9},{9,8},{10,11... | collective-permute-start | bytes 786440 | tf_op jit(solution)/shard_map/ppermute | solution.py:259
  53.1 7.0 %collective-permute-start.28 = (bf16[2,128,512]{2,1,0:T(8,128)(2,1)S(1)}, bf16[2,128,512]{2,1,0:T(8,128)(2,1)S(1)}, u32[]{:S(2)}, u32[]{:S(2)}) collective-permute-start(bf16[2,128,512]{2,1,0:T(8,128)(2,1)S(1)} %add_convert_fusion.3), channel_id=1, source_target_pairs={{0,4},{1,3},{2,6},{3,1},{4,0},{5,7},{6,2},{7,5},{8,12},{9,11},{10,... | collective-permute-start | bytes 786440 | tf_op jit(solution)/shard_map/ppermute | solution.py:262
  57.1 9.2 %collective-permute-start.24 = (bf16[4,128,512]{2,1,0:T(8,128)(2,1)S(1)}, bf16[4,128,512]{2,1,0:T(8,128)(2,1)S(1)}, u32[]{:S(2)}, u32[]{:S(2)}) collective-permute-start(bf16[4,128,512]{2,1,0:T(8,128)(2,1)S(1)} %add_convert_fusion), channel_id=1, source_target_pairs={{0,2},{1,5},{2,0},{3,7},{4,6},{5,1},{6,4},{7,3},{8,10},{9,13},{10,... | collective-permute-start | bytes 1572872 | tf_op jit(solution)/shard_map/ppermute | solution.py:262
  58.7 4.4 %collective-permute-start.25 = (bf16[2,128,512]{2,1,0:T(8,128)(2,1)S(1)}, bf16[2,128,512]{2,1,0:T(8,128)(2,1)S(1)}, u32[]{:S(2)}, u32[]{:S(2)}) collective-permute-start(bf16[2,128,512]{2,1,0:T(8,128)(2,1)S(1)} %get-tuple-element.101), channel_id=1, source_target_pairs={{0,1},{1,0},{2,3},{3,2},{4,5},{5,4},{6,7},{7,6},{8,9},{9,8},{10,11... | collective-permute-start | bytes 786440 | tf_op jit(solution)/shard_map/ppermute | solution.py:259
  58.7 9.4 %collective-permute-start.19 = (bf16[2,128,512]{2,1,0:T(8,128)(2,1)S(1)}, bf16[2,128,512]{2,1,0:T(8,128)(2,1)S(1)}, u32[]{:S(2)}, u32[]{:S(2)}) collective-permute-start(bf16[2,128,512]{2,1,0:T(8,128)(2,1)S(1)} %get-tuple-element.94), channel_id=1, source_target_pairs={{0,1},{1,0},{2,3},{3,2},{4,5},{5,4},{6,7},{7,6},{8,9},{9,8},{10,11... | collective-permute-start | bytes 786440 | tf_op jit(solution)/shard_map/ppermute | solution.py:259
  60.2 10.2 %collective-permute-start.29 = (bf16[2,128,512]{2,1,0:T(8,128)(2,1)S(1)}, bf16[2,128,512]{2,1,0:T(8,128)(2,1)S(1)}, u32[]{:S(2)}, u32[]{:S(2)}) collective-permute-start(bf16[2,128,512]{2,1,0:T(8,128)(2,1)S(1)} %add_convert_fusion.1), channel_id=1, source_target_pairs={{0,16},{1,9},{2,18},{3,11},{4,20},{5,13},{6,22},{7,15},{8,24},{9,1... | collective-permute-start | bytes 786440 | tf_op jit(solution)/shard_map/ppermute | solution.py:262
  66.4 6.4 %collective-permute-start.26 = (bf16[2,128,512]{2,1,0:T(8,128)(2,1)S(1)}, bf16[2,128,512]{2,1,0:T(8,128)(2,1)S(1)}, u32[]{:S(2)}, u32[]{:S(2)}) collective-permute-start(bf16[2,128,512]{2,1,0:T(8,128)(2,1)S(1)} %add_convert_fusion.2), channel_id=1, source_target_pairs={{0,4},{1,3},{2,6},{3,1},{4,0},{5,7},{6,2},{7,5},{8,12},{9,11},{10,... | collective-permute-start | bytes 786440 | tf_op jit(solution)/shard_map/ppermute | solution.py:262
  73.1 5.5 %collective-permute-start.30 = (bf16[1,128,512]{2,1,0:T(8,128)(2,1)S(1)}, bf16[1,128,512]{2,1,0:T(8,128)(2,1)S(1)}, u32[]{:S(2)}, u32[]{:S(2)}) collective-permute-start(bf16[1,128,512]{2,1,0:T(8,128)(2,1)S(1)} %slice.96), channel_id=1, source_target_pairs={{0,8},{1,17},{2,10},{3,19},{4,12},{5,21},{6,14},{7,23},{8,0},{9,25... | collective-permute-start | bytes 393224 | tf_op jit(solution)/shard_map/ppermute | solution.py:262

commit v15 on v14

--- a/solution.py
+++ b/solution.py
@@ -340,15 +340,18 @@
     call = functools.partial(query_call, where, gain, weight=wq)
     carry = call(early + other(early))
     carry = call(last[:2] + other(last[:2]), carry=carry)
-    both, *carry = lax.optimization_barrier((last[2][0], *carry))
+    tables = rotary_tables(tokens)
+    both, tables, partners, *carry = lax.optimization_barrier(
+        (last[2][0], tables, partners, *carry)
+    )
     both = [(both, last[2][1])]
     total = kv[0]
     for x in partners:
-        total = total + after(x, carry[0]).astype(f32)
+        total = total + x.astype(f32)
     final = other(both)
     carry = call(both, carry=carry)
     (attended,) = call(
-        final, carry=carry, extra=(total, swap(total, CORE), *rotary_tables(tokens))
+        final, carry=carry, extra=(total, swap(total, CORE), *tables)
     )
 
     def round_square(first, two, home):
@@ -388,9 +391,11 @@
     first = added_up(after(pairs[0][0], far_two), pairs[0][1]).astype(bf16)
     near_home, near_two = round_square(first, *pairs[1:])
     far_got = along(far_sum.astype(bf16), 1)
-    near_sum = added_up(*near_home, turn(near_two, 1), far_got)
     k = len(low)
-    home_sum = added_up(near_sum[:k], along(near_sum[k:].astype(bf16), 0))
+    got = [turn(near_two[k:], 1), turn(near_two[:k], 1)]
+    near_sum = added_up(*[x[k:] for x in near_home], got[0], far_got[k:])
+    home_sum = added_up(*[x[:k] for x in near_home], got[1], far_got[:k])
+    home_sum = added_up(home_sum, along(near_sum.astype(bf16), 0))
     out = added_up(home_sum[0], *[swap(home_sum[i].astype(bf16), o) for i, o in enumerate(low) if o])
     return out.astype(bf16)
 

time: 79.4 us -> 78.1 us (0.984)
  starting transfers between devices: 33 us -> 30.7 us
  waiting for transfers between devices: 23.3 us -> 24.4 us
    ppermute x14 -> x15, starting transfers between devices: 25.8 us -> 23.1 us  [by_core(): lax.ppermute(x, 'wide', [(i, i ^ pair[(step + (i & CORE)) % 2]) for i in...]
    ppermute x14 -> x15, waiting for transfers between devices: 22.3 us -> 23.3 us  [by_core(): lax.ppermute(x, 'wide', [(i, i ^ pair[(step + (i & CORE)) % 2]) for i in...]
  transfers between devices with their start and end apart: 31 -> 32, of which waited for: 12 -> 14; matrix products, arithmetic and copies ran while one was open for 2% -> 2% of each run, Pallas kernels for 20% -> 20%
where the time goes in v15:
time: 78.1 us; the launch traced here: 78 us
  starting transfers between devices  30.7 us (39%)
  waiting for transfers between devices  24.4 us (31%)
  Pallas kernels  20.2 us (26%)
  other arithmetic  2.17 us (3%)
    ppermute x15, waiting for transfers between devices, by_core(): lax.ppermute(x, 'wide', [(i, i ^ pair[(step + (i & CORE)) % 2]) for i in...  23.3 us
    ppermute x15, starting transfers between devices, by_core(): lax.ppermute(x, 'wide', [(i, i ^ pair[(step + (i & CORE)) % 2]) for i in...  23.1 us
    pallas_call x2, Pallas kernels, fetched(): pl.pallas_call(functools.partial(fetch_kernel, symbols, width), out_shape...  8.81 us
    ppermute x17, starting transfers between devices, swap(): return lax.ppermute(x, 'wide', [(i, i ^ offset) for i in range(n)])  7.63 us
    pallas_call x4, Pallas kernels, query_call(): pl.pallas_call(functools.partial(query_kernel, places, bool(carry), bool(...  5.84 us
    pallas_call x5, Pallas kernels, output_call(): pl.pallas_call(functools.partial(output_kernel, spots), out_shape=[jax.Sh...  3.03 us
    pallas_call x1, Pallas kernels, kv_terms(): pl.pallas_call(functools.partial(kv_kernel, shared), out_shape=[jax.Shape...  2.55 us
  transfers between devices with their start and end apart: 32, of which 14 were waited for; matrix products, arithmetic and copies ran while one was open for 2% of the time, Pallas kernels for 20%

profile of v15, /device:TPU:0, one launch (start us, length us, event | category | flops | bytes accessed | tf_op | source)
XLA Modules:
  0.0 78.0 jit_solution(8578946929044336305)
XLA Ops:
  0.1 2.6 %shard_map.69 = (f32[8,128,128]{2,1,0:T(8,128)S(1)}, f32[8,128,128]{2,1,0:T(8,128)S(1)}, bf16[128,512]{1,0:T(8,128)(2,1)S(1)}, f32[1,16384]{1,0:T(1,128)S(1)}) custom-call(s32[9]{0:T(128)S(1)} %stack.42.where.refs_0_, bf16[128,512]{1,0:T(8,128)(2,1)} %act.1, f32[1,16384]{1,0:T(1,128)} %bitcast.22, bf16[512,1024]{1,0:T(8,128)(2,1)} %wk.1, bf16[512,1024]{1,0:T(8,128)(2,1)} %wv.1), custom_call_target="tpu_custom_call" | custom-call | flops 4294967296 | bytes 33554432 | tf_op jit(solution)/shard_map/pallas_call | solution.py:108
  2.6 0.5 collective-permute-start.1
  3.2 2.6 %collective-permute-start = (bf16[1,128,512]{2,1,0:T(8,128)(2,1)S(1)}, bf16[1,128,512]{2,1,0:T(8,128)(2,1)S(1)}, u32[]{:S(2)}, u32[]{:S(2)}) collective-permute-start(bf16[1,128,512]{2,1,0:T(8,128)(2,1)S(1)} %bitcast.18), channel_id=1, source_target_pairs={{0,8},{1,17},{2,10},{3,19},{4,12},{5,21},{6,14},{7,23},{8,0},{9,25... | collective-permute-start | bytes 393224 | tf_op jit(solution)/shard_map/ppermute | solution.py:262
  5.9 1.8 %collective-permute-start.2 = (bf16[4,128,128]{2,1,0:T(8,128)(2,1)S(1)}, bf16[4,128,128]{2,1,0:T(8,128)(2,1)S(1)}, u32[]{:S(2)}, u32[]{:S(2)}) collective-permute-start(bf16[4,128,128]{2,1,0:T(8,128)(2,1)S(1)} %slice.134), channel_id=1, source_target_pairs={{0,4},{1,5},{2,6},{3,7},{4,0},{5,1},{6,2},{7,3},{8,12},{9,13},{10,... | collective-permute-start | bytes 393224 | tf_op jit(solution)/shard_map/ppermute | solution.py:259
  7.8 2.1 %collective-permute-done = bf16[1,128,512]{2,1,0:T(8,128)(2,1)S(1)} collective-permute-done((bf16[1,128,512]{2,1,0:T(8,128)(2,1)S(1)}, bf16[1,128,512]{2,1,0:T(8,128)(2,1)S(1)}, u32[]{:S(2)}, u32[]{:S(2)}) %collective-permute-start) | collective-permute-done | bytes 131104 | tf_op jit(solution)/shard_map/ppermute | solution.py:262
  9.9 2.2 %collective-permute-start.4 = (bf16[2,128,512]{2,1,0:T(8,128)(2,1)S(1)}, bf16[2,128,512]{2,1,0:T(8,128)(2,1)S(1)}, u32[]{:S(2)}, u32[]{:S(2)}) collective-permute-start(bf16[2,128,512]{2,1,0:T(8,128)(2,1)S(1)} %pad_maximum_fusion.3.refs_2_), channel_id=1, source_target_pairs={{0,2},{1,5},{2,0},{3,7},{4,6},{5,1},{6,4},{7,3},{8,10},{9,13},{10,... | collective-permute-start | bytes 786440 | tf_op jit(solution)/shard_map/ppermute | solution.py:262
  12.2 2.3 %collective-permute-start.3 = (bf16[2,128,640]{2,1,0:T(8,128)(2,1)S(1)}, bf16[2,128,640]{2,1,0:T(8,128)(2,1)S(1)}, u32[]{:S(2)}, u32[]{:S(2)}) collective-permute-start(bf16[2,128,640]{2,1,0:T(8,128)(2,1)S(1)} %pad_maximum_fusion.2), channel_id=1, source_target_pairs={{0,16},{1,9},{2,18},{3,11},{4,20},{5,13},{6,22},{7,15},{8,24},{9,1... | collective-permute-start | bytes 983048 | tf_op jit(solution)/shard_map/ppermute | solution.py:262
  14.5 2.0 %collective-permute-done.4.refs_3_ = bf16[2,128,512]{2,1,0:T(8,128)(2,1)S(1)} collective-permute-done((bf16[2,128,512]{2,1,0:T(8,128)(2,1)S(1)}, bf16[2,128,512]{2,1,0:T(8,128)(2,1)S(1)}, u32[]{:S(2)}, u32[]{:S(2)}) %collective-permute-start.4) | collective-permute-done | bytes 262176 | tf_op jit(solution)/shard_map/ppermute | solution.py:262
  16.6 2.1 %collective-permute-start.11 = (bf16[4,128,512]{2,1,0:T(8,128)(2,1)S(1)}, bf16[4,128,512]{2,1,0:T(8,128)(2,1)S(1)}, u32[]{:S(2)}, u32[]{:S(2)}) collective-permute-start(bf16[4,128,512]{2,1,0:T(8,128)(2,1)S(1)} %pad_maximum_fusion), channel_id=1, source_target_pairs={{0,4},{1,3},{2,6},{3,1},{4,0},{5,7},{6,2},{7,5},{8,12},{9,11},{10,... | collective-permute-start | bytes 1572872 | tf_op jit(solution)/shard_map/ppermute | solution.py:262
  18.7 4.4 %shard_map.70.weight = bf16[16,512,512]{2,1,0:T(8,128)(2,1)S(1)} custom-call(s32[9]{0:T(128)S(1)} %stack.42.where.refs_0_, bf16[512,16384]{1,0:T(8,128)(2,1)} %source.3), custom_call_target="tpu_custom_call" | custom-call | bytes 16777216 | tf_op jit(solution)/shard_map/pallas_call | solution.py:67
  23.1 0.8 collective-permute-done.3
  23.9 0.5 collective-permute-start.6
  24.4 1.5 %collective-permute-start.5 = (bf16[2,128,512]{2,1,0:T(8,128)(2,1)S(1)}, bf16[2,128,512]{2,1,0:T(8,128)(2,1)S(1)}, u32[]{:S(2)}, u32[]{:S(2)}) collective-permute-start(bf16[2,128,512]{2,1,0:T(8,128)(2,1)S(1)} %slice.85.refs_2_), channel_id=1, source_target_pairs={{0,2},{1,5},{2,0},{3,7},{4,6},{5,1},{6,4},{7,3},{8,10},{9,13},{10,... | collective-permute-start | bytes 786440 | tf_op jit(solution)/shard_map/ppermute | solution.py:262
  26.0 4.4 %shard_map.71.weight = bf16[16,512,512]{2,1,0:T(8,128)(2,1)S(1)} custom-call(s32[9]{0:T(128)S(1)} %stack.42.where.refs_0_, bf16[512,16384]{1,0:T(8,128)(2,1)} %source.3), custom_call_target="tpu_custom_call" | custom-call | bytes 16777216 | tf_op jit(solution)/shard_map/pallas_call | solution.py:67
  30.8 0.7 collective-permute-start.14
  31.6 0.9 %collective-permute-start.7 = (bf16[4,128,512]{2,1,0:T(8,128)(2,1)S(1)}, bf16[4,128,512]{2,1,0:T(8,128)(2,1)S(1)}, u32[]{:S(2)}, u32[]{:S(2)}) collective-permute-start(bf16[4,128,512]{2,1,0:T(8,128)(2,1)S(1)} %pad_maximum_fusion.1), channel_id=1, source_target_pairs={{0,4},{1,3},{2,6},{3,1},{4,0},{5,7},{6,2},{7,5},{8,12},{9,11},{10,... | collective-permute-start | bytes 1572872 | tf_op jit(solution)/shard_map/ppermute | solution.py:262
  33.1 0.4 collective-permute-start.9
  33.7 0.6 collective-permute-done.13.refs_6_
  34.3 1.5 %collective-permute-start.8 = (bf16[128,128]{1,0:T(8,128)(2,1)S(1)}, bf16[128,128]{1,0:T(8,128)(2,1)S(1)}, u32[]{:S(2)}, u32[]{:S(2)}) collective-permute-start(bf16[128,128]{1,0:T(8,128)(2,1)S(1)} %bitcast_convert_fusion), channel_id=1, source_target_pairs={{0,2},{1,3},{2,0},{3,1},{4,6},{5,7},{6,4},{7,5},{8,10},{9,11},{10,... | collective-permute-start | bytes 98312 | tf_op jit(solution)/shard_map/ppermute | solution.py:259
  35.9 2.0 %shard_map.72 = (f32[128,512]{1,0:T(8,128)S(1)}, f32[128,128]{1,0:T(8,128)S(1)}) custom-call(s32[9]{0:T(128)S(1)} %stack.42.where.refs_0_, f32[1,16384]{1,0:T(1,128)S(1)} %get-tuple-element.66.refs_1_, bf16[2,128,512]{2,1,0:T(8,128)(2,1)S(1)} %pad_maximum_fusion.3.refs_2_, bf16[2,128,512]{2,1,0:T(8,128)(2,1)S(1)} %collective-permute-done.4.refs_3_, ...), custom_call_target="tpu_custom_call" | custom-call | flops 1073741824 | bytes 8388608 | tf_op jit(solution)/shard_map/pallas_call | solution.py:201
  37.8 1.3 %shard_map.73 = (f32[128,512]{1,0:T(8,128)S(1)}, f32[128,128]{1,0:T(8,128)S(1)}) custom-call(s32[9]{0:T(128)S(1)} %stack.42.where.refs_0_, f32[1,16384]{1,0:T(1,128)S(1)} %get-tuple-element.66.refs_1_, bf16[2,128,512]{2,1,0:T(8,128)(2,1)S(1)} %slice.85.refs_2_, bf16[2,128,512]{2,1,0:T(8,128)(2,1)S(1)} %collective-permute-done.5.refs_3_, ...), custom_call_target="tpu_custom_call" | custom-call | flops 536870912 | bytes 4194304 | tf_op jit(solution)/shard_map/pallas_call | solution.py:201
  39.2 1.6 %collective-permute-done.7.refs_2_ = bf16[4,128,512]{2,1,0:T(8,128)(2,1)S(1)} collective-permute-done((bf16[4,128,512]{2,1,0:T(8,128)(2,1)S(1)}, bf16[4,128,512]{2,1,0:T(8,128)(2,1)S(1)}, u32[]{:S(2)}, u32[]{:S(2)}) %collective-permute-start.7) | collective-permute-done | bytes 524320 | tf_op jit(solution)/shard_map/ppermute | solution.py:262
  40.8 0.6 collective-permute-start.16
  41.4 1.0 %shard_map.74 = (f32[128,512]{1,0:T(8,128)S(1)}, f32[128,128]{1,0:T(8,128)S(1)}) custom-call(s32[9]{0:T(128)S(1)} %stack.42.where.refs_0_, f32[1,16384]{1,0:T(1,128)S(1)} %get-tuple-element.66.refs_1_, bf16[4,128,512]{2,1,0:T(8,128)(2,1)S(1)} %collective-permute-done.7.refs_2_, bf16[16384,512]{1,0:T(8,128)(2,1)S(1)} %bitcast.17, ...), custom_call_target="tpu_custom_call" | custom-call | flops 268435456 | bytes 2097152 | tf_op jit(solution)/shard_map/pallas_call | solution.py:201
  42.4 0.4 collective-permute-done.16.refs_7_
  42.8 1.6 %shard_map.75.attended = bf16[128,512]{1,0:T(8,128)(2,1)S(1)} custom-call(s32[9]{0:T(128)S(1)} %stack.42.where.refs_0_, f32[1,16384]{1,0:T(1,128)S(1)} %get-tuple-element.66.refs_1_, bf16[4,128,512]{2,1,0:T(8,128)(2,1)S(1)} %collective-permute-done.15.refs_2_, bf16[16384,512]{1,0:T(8,128)(2,1)S(1)} %bitcast.17, f32[128,512]{1,0:T(8,128)S(1)} %get-tuple-element.84.refs_4_, ...), custom_call_target="tpu_custom_call" | custom-call | flops 268435456 | bytes 2097152 | tf_op jit(solution)/shard_map/pallas_call | solution.py:201
  44.9 0.6 shard_map.77
  45.5 0.4 collective-permute-start.20
  46.1 0.7 shard_map.79
  46.9 0.9 %collective-permute-start.22 = (bf16[2,128,512]{2,1,0:T(8,128)(2,1)S(1)}, bf16[2,128,512]{2,1,0:T(8,128)(2,1)S(1)}, u32[]{:S(2)}, u32[]{:S(2)}) collective-permute-start(bf16[2,128,512]{2,1,0:T(8,128)(2,1)S(1)} %add_convert_fusion.4), channel_id=1, source_target_pairs={{0,2},{1,5},{2,0},{3,7},{4,6},{5,1},{6,4},{7,3},{8,10},{9,13},{10,... | collective-permute-start | bytes 786440 | tf_op jit(solution)/shard_map/ppermute | solution.py:262
  47.7 0.7 shard_map.78
  48.7 1.6 %collective-permute-start.18 = (bf16[2,128,512]{2,1,0:T(8,128)(2,1)S(1)}, bf16[2,128,512]{2,1,0:T(8,128)(2,1)S(1)}, u32[]{:S(2)}, u32[]{:S(2)}) collective-permute-start(bf16[2,128,512]{2,1,0:T(8,128)(2,1)S(1)} %add_convert_fusion.5), channel_id=1, source_target_pairs={{0,2},{1,5},{2,0},{3,7},{4,6},{5,1},{6,4},{7,3},{8,10},{9,13},{10,... | collective-permute-start | bytes 786440 | tf_op jit(solution)/shard_map/ppermute | solution.py:262
  50.4 2.9 %collective-permute-done.22 = bf16[2,128,512]{2,1,0:T(8,128)(2,1)S(1)} collective-permute-done((bf16[2,128,512]{2,1,0:T(8,128)(2,1)S(1)}, bf16[2,128,512]{2,1,0:T(8,128)(2,1)S(1)}, u32[]{:S(2)}, u32[]{:S(2)}) %collective-permute-start.22) | collective-permute-done | bytes 262176 | tf_op jit(solution)/shard_map/ppermute | solution.py:262
  53.4 0.9 %collective-permute-start.28 = (bf16[2,128,512]{2,1,0:T(8,128)(2,1)S(1)}, bf16[2,128,512]{2,1,0:T(8,128)(2,1)S(1)}, u32[]{:S(2)}, u32[]{:S(2)}) collective-permute-start(bf16[2,128,512]{2,1,0:T(8,128)(2,1)S(1)} %add_convert_fusion.3), channel_id=1, source_target_pairs={{0,4},{1,3},{2,6},{3,1},{4,0},{5,7},{6,2},{7,5},{8,12},{9,11},{10,... | collective-permute-start | bytes 786440 | tf_op jit(solution)/shard_map/ppermute | solution.py:262
  54.3 2.3 %collective-permute-done.18 = bf16[2,128,512]{2,1,0:T(8,128)(2,1)S(1)} collective-permute-done((bf16[2,128,512]{2,1,0:T(8,128)(2,1)S(1)}, bf16[2,128,512]{2,1,0:T(8,128)(2,1)S(1)}, u32[]{:S(2)}, u32[]{:S(2)}) %collective-permute-start.18) | collective-permute-done | bytes 262176 | tf_op jit(solution)/shard_map/ppermute | solution.py:262
  56.6 0.7 shard_map.80
  57.5 0.8 %collective-permute-start.24 = (bf16[4,128,512]{2,1,0:T(8,128)(2,1)S(1)}, bf16[4,128,512]{2,1,0:T(8,128)(2,1)S(1)}, u32[]{:S(2)}, u32[]{:S(2)}) collective-permute-start(bf16[4,128,512]{2,1,0:T(8,128)(2,1)S(1)} %add_convert_fusion), channel_id=1, source_target_pairs={{0,2},{1,5},{2,0},{3,7},{4,6},{5,1},{6,4},{7,3},{8,10},{9,13},{10,... | collective-permute-start | bytes 1572872 | tf_op jit(solution)/shard_map/ppermute | solution.py:262
  58.3 0.5 collective-permute-start.19
  58.8 1.6 %collective-permute-done.28 = bf16[2,128,512]{2,1,0:T(8,128)(2,1)S(1)} collective-permute-done((bf16[2,128,512]{2,1,0:T(8,128)(2,1)S(1)}, bf16[2,128,512]{2,1,0:T(8,128)(2,1)S(1)}, u32[]{:S(2)}, u32[]{:S(2)}) %collective-permute-start.28) | collective-permute-done | bytes 262176 | tf_op jit(solution)/shard_map/ppermute | solution.py:262
  60.6 2.6 %collective-permute-start.29 = (bf16[2,128,512]{2,1,0:T(8,128)(2,1)S(1)}, bf16[2,128,512]{2,1,0:T(8,128)(2,1)S(1)}, u32[]{:S(2)}, u32[]{:S(2)}) collective-permute-start(bf16[2,128,512]{2,1,0:T(8,128)(2,1)S(1)} %add_convert_fusion.1), channel_id=1, source_target_pairs={{0,16},{1,9},{2,18},{3,11},{4,20},{5,13},{6,22},{7,15},{8,24},{9,1... | collective-permute-start | bytes 786440 | tf_op jit(solution)/shard_map/ppermute | solution.py:262
  63.2 3.5 %collective-permute-done.24 = bf16[4,128,512]{2,1,0:T(8,128)(2,1)S(1)} collective-permute-done((bf16[4,128,512]{2,1,0:T(8,128)(2,1)S(1)}, bf16[4,128,512]{2,1,0:T(8,128)(2,1)S(1)}, u32[]{:S(2)}, u32[]{:S(2)}) %collective-permute-start.24) | collective-permute-done | bytes 524320 | tf_op jit(solution)/shard_map/ppermute | solution.py:262
  66.9 0.9 %collective-permute-start.30 = (bf16[1,128,512]{2,1,0:T(8,128)(2,1)S(1)}, bf16[1,128,512]{2,1,0:T(8,128)(2,1)S(1)}, u32[]{:S(2)}, u32[]{:S(2)}) collective-permute-start(bf16[1,128,512]{2,1,0:T(8,128)(2,1)S(1)} %get-tuple-element.108), channel_id=1, source_target_pairs={{0,4},{1,3},{2,6},{3,1},{4,0},{5,7},{6,2},{7,5},{8,12},{9,11},{10,... | collective-permute-start | bytes 393224 | tf_op jit(solution)/shard_map/ppermute | solution.py:262
  67.8 1.2 %collective-permute-start.26 = (bf16[1,128,512]{2,1,0:T(8,128)(2,1)S(1)}, bf16[1,128,512]{2,1,0:T(8,128)(2,1)S(1)}, u32[]{:S(2)}, u32[]{:S(2)}) collective-permute-start(bf16[1,128,512]{2,1,0:T(8,128)(2,1)S(1)} %get-tuple-element.107), channel_id=1, source_target_pairs={{0,4},{1,3},{2,6},{3,1},{4,0},{5,7},{6,2},{7,5},{8,12},{9,11},{10,... | collective-permute-start | bytes 393224 | tf_op jit(solution)/shard_map/ppermute | solution.py:262
  69.0 1.8 %collective-permute-done.29 = bf16[2,128,512]{2,1,0:T(8,128)(2,1)S(1)} collective-permute-done((bf16[2,128,512]{2,1,0:T(8,128)(2,1)S(1)}, bf16[2,128,512]{2,1,0:T(8,128)(2,1)S(1)}, u32[]{:S(2)}, u32[]{:S(2)}) %collective-permute-start.29) | collective-permute-done | bytes 262176 | tf_op jit(solution)/shard_map/ppermute | solution.py:262
  70.8 1.1 %collective-permute-done.30 = bf16[1,128,512]{2,1,0:T(8,128)(2,1)S(1)} collective-permute-done((bf16[1,128,512]{2,1,0:T(8,128)(2,1)S(1)}, bf16[1,128,512]{2,1,0:T(8,128)(2,1)S(1)}, u32[]{:S(2)}, u32[]{:S(2)}) %collective-permute-start.30) | collective-permute-done | bytes 131104 | tf_op jit(solution)/shard_map/ppermute | solution.py:262
  72.0 2.0 %collective-permute-start.31 = (bf16[1,128,512]{2,1,0:T(8,128)(2,1)S(1)}, bf16[1,128,512]{2,1,0:T(8,128)(2,1)S(1)}, u32[]{:S(2)}, u32[]{:S(2)}) collective-permute-start(bf16[1,128,512]{2,1,0:T(8,128)(2,1)S(1)} %add_convert_fusion.7), channel_id=1, source_target_pairs={{0,8},{1,17},{2,10},{3,19},{4,12},{5,21},{6,14},{7,23},{8,0},{9,25... | collective-permute-start | bytes 393224 | tf_op jit(solution)/shard_map/ppermute | solution.py:262
  74.0 3.2 %collective-permute-done.31 = bf16[1,128,512]{2,1,0:T(8,128)(2,1)S(1)} collective-permute-done((bf16[1,128,512]{2,1,0:T(8,128)(2,1)S(1)}, bf16[1,128,512]{2,1,0:T(8,128)(2,1)S(1)}, u32[]{:S(2)}, u32[]{:S(2)}) %collective-permute-start.31) | collective-permute-done | bytes 131104 | tf_op jit(solution)/shard_map/ppermute | solution.py:262
  77.2 0.8 fusion
  (64 shorter events, 3.5 us)
Async XLA Ops:
  2.6 3.2 %collective-permute-start.1 = (f32[8,128,128]{2,1,0:T(8,128)S(1)}, f32[8,128,128]{2,1,0:T(8,128)S(1)}, u32[]{:S(2)}, u32[]{:S(2)}) collective-permute-start(f32[8,128,128]{2,1,0:T(8,128)S(1)} %get-tuple-element.69), channel_id=1, source_target_pairs={{0,1},{1,0},{2,3},{3,2},{4,5},{5,4},{6,7},{7,6},{8,9},{9,8},{10,11... | collective-permute-start | bytes 1572872 | tf_op jit(solution)/shard_map/ppermute | solution.py:259
  3.2 6.7 %collective-permute-start = (bf16[1,128,512]{2,1,0:T(8,128)(2,1)S(1)}, bf16[1,128,512]{2,1,0:T(8,128)(2,1)S(1)}, u32[]{:S(2)}, u32[]{:S(2)}) collective-permute-start(bf16[1,128,512]{2,1,0:T(8,128)(2,1)S(1)} %bitcast.18), channel_id=1, source_target_pairs={{0,8},{1,17},{2,10},{3,19},{4,12},{5,21},{6,14},{7,23},{8,0},{9,25... | collective-permute-start | bytes 393224 | tf_op jit(solution)/shard_map/ppermute | solution.py:262
  5.9 6.2 %collective-permute-start.2 = (bf16[4,128,128]{2,1,0:T(8,128)(2,1)S(1)}, bf16[4,128,128]{2,1,0:T(8,128)(2,1)S(1)}, u32[]{:S(2)}, u32[]{:S(2)}) collective-permute-start(bf16[4,128,128]{2,1,0:T(8,128)(2,1)S(1)} %slice.134), channel_id=1, source_target_pairs={{0,4},{1,5},{2,6},{3,7},{4,0},{5,1},{6,2},{7,3},{8,12},{9,13},{10,... | collective-permute-start | bytes 393224 | tf_op jit(solution)/shard_map/ppermute | solution.py:259
  9.9 6.6 %collective-permute-start.4 = (bf16[2,128,512]{2,1,0:T(8,128)(2,1)S(1)}, bf16[2,128,512]{2,1,0:T(8,128)(2,1)S(1)}, u32[]{:S(2)}, u32[]{:S(2)}) collective-permute-start(bf16[2,128,512]{2,1,0:T(8,128)(2,1)S(1)} %pad_maximum_fusion.3.refs_2_), channel_id=1, source_target_pairs={{0,2},{1,5},{2,0},{3,7},{4,6},{5,1},{6,4},{7,3},{8,10},{9,13},{10,... | collective-permute-start | bytes 786440 | tf_op jit(solution)/shard_map/ppermute | solution.py:262
  12.2 11.6 %collective-permute-start.3 = (bf16[2,128,640]{2,1,0:T(8,128)(2,1)S(1)}, bf16[2,128,640]{2,1,0:T(8,128)(2,1)S(1)}, u32[]{:S(2)}, u32[]{:S(2)}) collective-permute-start(bf16[2,128,640]{2,1,0:T(8,128)(2,1)S(1)} %pad_maximum_fusion.2), channel_id=1, source_target_pairs={{0,16},{1,9},{2,18},{3,11},{4,20},{5,13},{6,22},{7,15},{8,24},{9,1... | collective-permute-start | bytes 983048 | tf_op jit(solution)/shard_map/ppermute | solution.py:262
  16.6 14.3 %collective-permute-start.11 = (bf16[4,128,512]{2,1,0:T(8,128)(2,1)S(1)}, bf16[4,128,512]{2,1,0:T(8,128)(2,1)S(1)}, u32[]{:S(2)}, u32[]{:S(2)}) collective-permute-start(bf16[4,128,512]{2,1,0:T(8,128)(2,1)S(1)} %pad_maximum_fusion), channel_id=1, source_target_pairs={{0,4},{1,3},{2,6},{3,1},{4,0},{5,7},{6,2},{7,5},{8,12},{9,11},{10,... | collective-permute-start | bytes 1572872 | tf_op jit(solution)/shard_map/ppermute | solution.py:262
  18.7 17.1 %slice-start = ((s8[16777216]{0:T(1024)(128)(4,1)}), s8[4194304]{0:T(1024)(128)(4,1)S(1)}, s32[]{:S(2)}) async-start(s8[16777216]{0:T(1024)(128)(4,1)} %bitcast.16), calls=%async_computation | async-start | bytes 8388608
  18.7 17.1 %slice-start.1 = ((s8[16777216]{0:T(1024)(128)(4,1)}), s8[4194304]{0:T(1024)(128)(4,1)S(1)}, s32[]{:S(2)}) async-start(s8[16777216]{0:T(1024)(128)(4,1)} %bitcast.16), calls=%async_computation.1 | async-start | bytes 8388608
  23.9 6.6 %collective-permute-start.6 = (bf16[1,128,128]{2,1,0:T(8,128)(2,1)S(1)}, bf16[1,128,128]{2,1,0:T(8,128)(2,1)S(1)}, u32[]{:S(2)}, u32[]{:S(2)}) collective-permute-start(bf16[1,128,128]{2,1,0:T(8,128)(2,1)S(1)} %slice.136), channel_id=1, source_target_pairs={{0,8},{1,17},{2,10},{3,19},{4,12},{5,21},{6,14},{7,23},{8,0},{9,25... | collective-permute-start | bytes 98312 | tf_op jit(solution)/shard_map/ppermute | solution.py:262
  24.4 6.4 %collective-permute-start.5 = (bf16[2,128,512]{2,1,0:T(8,128)(2,1)S(1)}, bf16[2,128,512]{2,1,0:T(8,128)(2,1)S(1)}, u32[]{:S(2)}, u32[]{:S(2)}) collective-permute-start(bf16[2,128,512]{2,1,0:T(8,128)(2,1)S(1)} %slice.85.refs_2_), channel_id=1, source_target_pairs={{0,2},{1,5},{2,0},{3,7},{4,6},{5,1},{6,4},{7,3},{8,10},{9,13},{10,... | collective-permute-start | bytes 786440 | tf_op jit(solution)/shard_map/ppermute | solution.py:262
  26.0 9.9 %slice-start.2 = ((s8[16777216]{0:T(1024)(128)(4,1)}), s8[4194304]{0:T(1024)(128)(4,1)S(1)}, s32[]{:S(2)}) async-start(s8[16777216]{0:T(1024)(128)(4,1)} %bitcast.16), calls=%async_computation.2 | async-start | bytes 8388608
  26.0 9.9 %slice-start.3 = ((s8[16777216]{0:T(1024)(128)(4,1)}), s8[4194304]{0:T(1024)(128)(4,1)S(1)}, s32[]{:S(2)}) async-start(s8[16777216]{0:T(1024)(128)(4,1)} %bitcast.16), calls=%async_computation.3 | async-start | bytes 8388608
  26.0 7.5 %collective-permute-start.12 = (bf16[2,128,512]{2,1,0:T(8,128)(2,1)S(1)}, bf16[2,128,512]{2,1,0:T(8,128)(2,1)S(1)}, u32[]{:S(2)}, u32[]{:S(2)}) collective-permute-start(bf16[2,128,512]{2,1,0:T(8,128)(2,1)S(1)} %pad_maximum_fusion.3.refs_2_), channel_id=1, source_target_pairs={{0,1},{1,0},{2,3},{3,2},{4,5},{5,4},{6,7},{7,6},{8,9},{9,8},{10,11... | collective-permute-start | bytes 786440 | tf_op jit(solution)/shard_map/ppermute | solution.py:259
  30.8 5.0 %collective-permute-start.14 = (bf16[4,128,512]{2,1,0:T(8,128)(2,1)S(1)}, bf16[4,128,512]{2,1,0:T(8,128)(2,1)S(1)}, u32[]{:S(2)}, u32[]{:S(2)}) collective-permute-start(bf16[4,128,512]{2,1,0:T(8,128)(2,1)S(1)} %collective-permute-done.11.refs_4_), channel_id=1, source_target_pairs={{0,1},{1,0},{2,3},{3,2},{4,5},{5,4},{6,7},{7,6},{8,9},{9,8},{10,11... | collective-permute-start | bytes 1572872 | tf_op jit(solution)/shard_map/ppermute | solution.py:259
  31.6 9.2 %collective-permute-start.7 = (bf16[4,128,512]{2,1,0:T(8,128)(2,1)S(1)}, bf16[4,128,512]{2,1,0:T(8,128)(2,1)S(1)}, u32[]{:S(2)}, u32[]{:S(2)}) collective-permute-start(bf16[4,128,512]{2,1,0:T(8,128)(2,1)S(1)} %pad_maximum_fusion.1), channel_id=1, source_target_pairs={{0,4},{1,3},{2,6},{3,1},{4,0},{5,7},{6,2},{7,5},{8,12},{9,11},{10,... | collective-permute-start | bytes 1572872 | tf_op jit(solution)/shard_map/ppermute | solution.py:262
  32.7 1.6 %collective-permute-start.13 = (bf16[2,128,512]{2,1,0:T(8,128)(2,1)S(1)}, bf16[2,128,512]{2,1,0:T(8,128)(2,1)S(1)}, u32[]{:S(2)}, u32[]{:S(2)}) collective-permute-start(bf16[2,128,512]{2,1,0:T(8,128)(2,1)S(1)} %collective-permute-done.4.refs_3_), channel_id=1, source_target_pairs={{0,1},{1,0},{2,3},{3,2},{4,5},{5,4},{6,7},{7,6},{8,9},{9,8},{10,11... | collective-permute-start | bytes 786440 | tf_op jit(solution)/shard_map/ppermute | solution.py:259
  33.1 4.7 %collective-permute-start.9 = (bf16[2,128,512]{2,1,0:T(8,128)(2,1)S(1)}, bf16[2,128,512]{2,1,0:T(8,128)(2,1)S(1)}, u32[]{:S(2)}, u32[]{:S(2)}) collective-permute-start(bf16[2,128,512]{2,1,0:T(8,128)(2,1)S(1)} %slice.85.refs_2_), channel_id=1, source_target_pairs={{0,1},{1,0},{2,3},{3,2},{4,5},{5,4},{6,7},{7,6},{8,9},{9,8},{10,11... | collective-permute-start | bytes 786440 | tf_op jit(solution)/shard_map/ppermute | solution.py:259
  33.5 4.4 %collective-permute-start.10 = (bf16[2,128,512]{2,1,0:T(8,128)(2,1)S(1)}, bf16[2,128,512]{2,1,0:T(8,128)(2,1)S(1)}, u32[]{:S(2)}, u32[]{:S(2)}) collective-permute-start(bf16[2,128,512]{2,1,0:T(8,128)(2,1)S(1)} %collective-permute-done.5.refs_3_), channel_id=1, source_target_pairs={{0,1},{1,0},{2,3},{3,2},{4,5},{5,4},{6,7},{7,6},{8,9},{9,8},{10,11... | collective-permute-start | bytes 786440 | tf_op jit(solution)/shard_map/ppermute | solution.py:259
  34.3 4.8 %collective-permute-start.8 = (bf16[128,128]{1,0:T(8,128)(2,1)S(1)}, bf16[128,128]{1,0:T(8,128)(2,1)S(1)}, u32[]{:S(2)}, u32[]{:S(2)}) collective-permute-start(bf16[128,128]{1,0:T(8,128)(2,1)S(1)} %bitcast_convert_fusion), channel_id=1, source_target_pairs={{0,2},{1,3},{2,0},{3,1},{4,6},{5,7},{6,4},{7,5},{8,10},{9,11},{10,... | collective-permute-start | bytes 98312 | tf_op jit(solution)/shard_map/ppermute | solution.py:259
  40.8 2.0 %collective-permute-start.15 = (bf16[4,128,512]{2,1,0:T(8,128)(2,1)S(1)}, bf16[4,128,512]{2,1,0:T(8,128)(2,1)S(1)}, u32[]{:S(2)}, u32[]{:S(2)}) collective-permute-start(bf16[4,128,512]{2,1,0:T(8,128)(2,1)S(1)} %collective-permute-done.7.refs_2_), channel_id=1, source_target_pairs={{0,1},{1,0},{2,3},{3,2},{4,5},{5,4},{6,7},{7,6},{8,9},{9,8},{10,11... | collective-permute-start | bytes 1572872 | tf_op jit(solution)/shard_map/ppermute | solution.py:259
  40.8 2.0 %collective-permute-start.16 = (f32[128,128]{1,0:T(8,128)S(1)}, f32[128,128]{1,0:T(8,128)S(1)}, u32[]{:S(2)}, u32[]{:S(2)}) collective-permute-start(f32[128,128]{1,0:T(8,128)S(1)} %bitcast_add_fusion.refs_6_), channel_id=1, source_target_pairs={{0,1},{1,0},{2,3},{3,2},{4,5},{5,4},{6,7},{7,6},{8,9},{9,8},{10,11... | collective-permute-start | bytes 196616 | tf_op jit(solution)/shard_map/ppermute | solution.py:259
  44.7 2.1 %collective-permute-start.21 = (bf16[2,128,512]{2,1,0:T(8,128)(2,1)S(1)}, bf16[2,128,512]{2,1,0:T(8,128)(2,1)S(1)}, u32[]{:S(2)}, u32[]{:S(2)}) collective-permute-start(bf16[2,128,512]{2,1,0:T(8,128)(2,1)S(1)} %shard_map.76), channel_id=1, source_target_pairs={{0,1},{1,0},{2,3},{3,2},{4,5},{5,4},{6,7},{7,6},{8,9},{9,8},{10,11... | collective-permute-start | bytes 786440 | tf_op jit(solution)/shard_map/ppermute | solution.py:259
  45.5 4.9 %collective-permute-start.20 = (bf16[2,128,512]{2,1,0:T(8,128)(2,1)S(1)}, bf16[2,128,512]{2,1,0:T(8,128)(2,1)S(1)}, u32[]{:S(2)}, u32[]{:S(2)}) collective-permute-start(bf16[2,128,512]{2,1,0:T(8,128)(2,1)S(1)} %get-tuple-element.101), channel_id=1, source_target_pairs={{0,1},{1,0},{2,3},{3,2},{4,5},{5,4},{6,7},{7,6},{8,9},{9,8},{10,11... | collective-permute-start | bytes 786440 | tf_op jit(solution)/shard_map/ppermute | solution.py:259
  45.9 2.7 %collective-permute-start.17 = (bf16[2,128,512]{2,1,0:T(8,128)(2,1)S(1)}, bf16[2,128,512]{2,1,0:T(8,128)(2,1)S(1)}, u32[]{:S(2)}, u32[]{:S(2)}) collective-permute-start(bf16[2,128,512]{2,1,0:T(8,128)(2,1)S(1)} %get-tuple-element.95), channel_id=1, source_target_pairs={{0,1},{1,0},{2,3},{3,2},{4,5},{5,4},{6,7},{7,6},{8,9},{9,8},{10,11... | collective-permute-start | bytes 786440 | tf_op jit(solution)/shard_map/ppermute | solution.py:259
  46.9 6.4 %collective-permute-start.22 = (bf16[2,128,512]{2,1,0:T(8,128)(2,1)S(1)}, bf16[2,128,512]{2,1,0:T(8,128)(2,1)S(1)}, u32[]{:S(2)}, u32[]{:S(2)}) collective-permute-start(bf16[2,128,512]{2,1,0:T(8,128)(2,1)S(1)} %add_convert_fusion.4), channel_id=1, source_target_pairs={{0,2},{1,5},{2,0},{3,7},{4,6},{5,1},{6,4},{7,3},{8,10},{9,13},{10,... | collective-permute-start | bytes 786440 | tf_op jit(solution)/shard_map/ppermute | solution.py:262
  48.5 8.8 %collective-permute-start.23 = (bf16[4,128,512]{2,1,0:T(8,128)(2,1)S(1)}, bf16[4,128,512]{2,1,0:T(8,128)(2,1)S(1)}, u32[]{:S(2)}, u32[]{:S(2)}) collective-permute-start(bf16[4,128,512]{2,1,0:T(8,128)(2,1)S(1)} %get-tuple-element.93), channel_id=1, source_target_pairs={{0,1},{1,0},{2,3},{3,2},{4,5},{5,4},{6,7},{7,6},{8,9},{9,8},{10,11... | collective-permute-start | bytes 1572872 | tf_op jit(solution)/shard_map/ppermute | solution.py:259
  48.7 7.9 %collective-permute-start.18 = (bf16[2,128,512]{2,1,0:T(8,128)(2,1)S(1)}, bf16[2,128,512]{2,1,0:T(8,128)(2,1)S(1)}, u32[]{:S(2)}, u32[]{:S(2)}) collective-permute-start(bf16[2,128,512]{2,1,0:T(8,128)(2,1)S(1)} %add_convert_fusion.5), channel_id=1, source_target_pairs={{0,2},{1,5},{2,0},{3,7},{4,6},{5,1},{6,4},{7,3},{8,10},{9,13},{10,... | collective-permute-start | bytes 786440 | tf_op jit(solution)/shard_map/ppermute | solution.py:262
  50.3 8.6 %collective-permute-start.27 = (bf16[2,128,512]{2,1,0:T(8,128)(2,1)S(1)}, bf16[2,128,512]{2,1,0:T(8,128)(2,1)S(1)}, u32[]{:S(2)}, u32[]{:S(2)}) collective-permute-start(bf16[2,128,512]{2,1,0:T(8,128)(2,1)S(1)} %get-tuple-element.90), channel_id=1, source_target_pairs={{0,1},{1,0},{2,3},{3,2},{4,5},{5,4},{6,7},{7,6},{8,9},{9,8},{10,11... | collective-permute-start | bytes 786440 | tf_op jit(solution)/shard_map/ppermute | solution.py:259
  53.4 7.0 %collective-permute-start.28 = (bf16[2,128,512]{2,1,0:T(8,128)(2,1)S(1)}, bf16[2,128,512]{2,1,0:T(8,128)(2,1)S(1)}, u32[]{:S(2)}, u32[]{:S(2)}) collective-permute-start(bf16[2,128,512]{2,1,0:T(8,128)(2,1)S(1)} %add_convert_fusion.3), channel_id=1, source_target_pairs={{0,4},{1,3},{2,6},{3,1},{4,0},{5,7},{6,2},{7,5},{8,12},{9,11},{10,... | collective-permute-start | bytes 786440 | tf_op jit(solution)/shard_map/ppermute | solution.py:262
  57.5 9.2 %collective-permute-start.24 = (bf16[4,128,512]{2,1,0:T(8,128)(2,1)S(1)}, bf16[4,128,512]{2,1,0:T(8,128)(2,1)S(1)}, u32[]{:S(2)}, u32[]{:S(2)}) collective-permute-start(bf16[4,128,512]{2,1,0:T(8,128)(2,1)S(1)} %add_convert_fusion), channel_id=1, source_target_pairs={{0,2},{1,5},{2,0},{3,7},{4,6},{5,1},{6,4},{7,3},{8,10},{9,13},{10,... | collective-permute-start | bytes 1572872 | tf_op jit(solution)/shard_map/ppermute | solution.py:262
  58.3 4.9 %collective-permute-start.25 = (bf16[2,128,512]{2,1,0:T(8,128)(2,1)S(1)}, bf16[2,128,512]{2,1,0:T(8,128)(2,1)S(1)}, u32[]{:S(2)}, u32[]{:S(2)}) collective-permute-start(bf16[2,128,512]{2,1,0:T(8,128)(2,1)S(1)} %get-tuple-element.105), channel_id=1, source_target_pairs={{0,1},{1,0},{2,3},{3,2},{4,5},{5,4},{6,7},{7,6},{8,9},{9,8},{10,11... | collective-permute-start | bytes 786440 | tf_op jit(solution)/shard_map/ppermute | solution.py:259
  58.3 10.6 %collective-permute-start.19 = (bf16[2,128,512]{2,1,0:T(8,128)(2,1)S(1)}, bf16[2,128,512]{2,1,0:T(8,128)(2,1)S(1)}, u32[]{:S(2)}, u32[]{:S(2)}) collective-permute-start(bf16[2,128,512]{2,1,0:T(8,128)(2,1)S(1)} %get-tuple-element.98), channel_id=1, source_target_pairs={{0,1},{1,0},{2,3},{3,2},{4,5},{5,4},{6,7},{7,6},{8,9},{9,8},{10,11... | collective-permute-start | bytes 786440 | tf_op jit(solution)/shard_map/ppermute | solution.py:259
  60.6 10.1 %collective-permute-start.29 = (bf16[2,128,512]{2,1,0:T(8,128)(2,1)S(1)}, bf16[2,128,512]{2,1,0:T(8,128)(2,1)S(1)}, u32[]{:S(2)}, u32[]{:S(2)}) collective-permute-start(bf16[2,128,512]{2,1,0:T(8,128)(2,1)S(1)} %add_convert_fusion.1), channel_id=1, source_target_pairs={{0,16},{1,9},{2,18},{3,11},{4,20},{5,13},{6,22},{7,15},{8,24},{9,1... | collective-permute-start | bytes 786440 | tf_op jit(solution)/shard_map/ppermute | solution.py:262
  66.9 5.0 %collective-permute-start.30 = (bf16[1,128,512]{2,1,0:T(8,128)(2,1)S(1)}, bf16[1,128,512]{2,1,0:T(8,128)(2,1)S(1)}, u32[]{:S(2)}, u32[]{:S(2)}) collective-permute-start(bf16[1,128,512]{2,1,0:T(8,128)(2,1)S(1)} %get-tuple-element.108), channel_id=1, source_target_pairs={{0,4},{1,3},{2,6},{3,1},{4,0},{5,7},{6,2},{7,5},{8,12},{9,11},{10,... | collective-permute-start | bytes 393224 | tf_op jit(solution)/shard_map/ppermute | solution.py:262
  67.8 6.2 %collective-permute-start.26 = (bf16[1,128,512]{2,1,0:T(8,128)(2,1)S(1)}, bf16[1,128,512]{2,1,0:T(8,128)(2,1)S(1)}, u32[]{:S(2)}, u32[]{:S(2)}) collective-permute-start(bf16[1,128,512]{2,1,0:T(8,128)(2,1)S(1)} %get-tuple-element.107), channel_id=1, source_target_pairs={{0,4},{1,3},{2,6},{3,1},{4,0},{5,7},{6,2},{7,5},{8,12},{9,11},{10,... | collective-permute-start | bytes 393224 | tf_op jit(solution)/shard_map/ppermute | solution.py:262
  72.0 5.2 %collective-permute-start.31 = (bf16[1,128,512]{2,1,0:T(8,128)(2,1)S(1)}, bf16[1,128,512]{2,1,0:T(8,128)(2,1)S(1)}, u32[]{:S(2)}, u32[]{:S(2)}) collective-permute-start(bf16[1,128,512]{2,1,0:T(8,128)(2,1)S(1)} %add_convert_fusion.7), channel_id=1, source_target_pairs={{0,8},{1,17},{2,10},{3,19},{4,12},{5,21},{6,14},{7,23},{8,0},{9,25... | collective-permute-start | bytes 393224 | tf_op jit(solution)/shard_map/ppermute | solution.py:262

commit v16 on v15

--- a/solution.py
+++ b/solution.py
@@ -334,25 +334,21 @@
         at = symbols_of(offsets)
         groups.append([(row, at[0]), (side, at[1]), (both, at[2] + at[3])])
     early, last = groups
-    early[2] = (after(early[2][0], blocks), early[2][1])
-    partners = [swap(kv[0].astype(bf16), o) for o in combos(bits[1:shared])[1:]]
+    early[2] = (after(early[2][0], blocks, joined), early[2][1])
+    total = kv[0]
+    for b in bits[1:shared]:
+        total = total + swap(total.astype(bf16), b).astype(f32)
+    sums = (total, swap(total, CORE))
 
     call = functools.partial(query_call, where, gain, weight=wq)
     carry = call(early + other(early))
     carry = call(last[:2] + other(last[:2]), carry=carry)
     tables = rotary_tables(tokens)
-    both, tables, partners, *carry = lax.optimization_barrier(
-        (last[2][0], tables, partners, *carry)
-    )
+    both, tables, sums, *carry = lax.optimization_barrier((last[2][0], tables, sums, *carry))
     both = [(both, last[2][1])]
-    total = kv[0]
-    for x in partners:
-        total = total + x.astype(f32)
     final = other(both)
     carry = call(both, carry=carry)
-    (attended,) = call(
-        final, carry=carry, extra=(total, swap(total, CORE), *tables)
-    )
+    (attended,) = call(final, carry=carry, extra=(*sums, *tables))
 
     def round_square(first, two, home):
         got = turn(first, 0)

time: 78.1 us -> 82.3 us (1.054)
  starting transfers between devices: 30.7 us -> 32.8 us
  waiting for transfers between devices: 24.4 us -> 26.2 us
    ppermute x17, waiting for transfers between devices: 1.06 us -> 3.73 us  [swap(): return lax.ppermute(x, 'wide', [(i, i ^ offset) for i in range(n)])]
    ppermute x17, starting transfers between devices: 7.63 us -> 9.67 us  [swap(): return lax.ppermute(x, 'wide', [(i, i ^ offset) for i in range(n)])]
    ppermute x15, waiting for transfers between devices: 23.3 us -> 22.5 us  [by_core(): lax.ppermute(x, 'wide', [(i, i ^ pair[(step + (i & CORE)) % 2]) for i in...]
  transfers between devices with their start and end apart: 32 -> 32, of which waited for: 14 -> 12; matrix products, arithmetic and copies ran while one was open for 2% -> 2% of each run, Pallas kernels for 20% -> 20%
where the time goes in v16:
time: 82.3 us; the launch traced here: 82.2 us
  starting transfers between devices  32.8 us (40%)
  waiting for transfers between devices  26.2 us (32%)
  Pallas kernels  20.5 us (25%)
  other arithmetic  2.17 us (3%)
    ppermute x15, starting transfers between devices, by_core(): lax.ppermute(x, 'wide', [(i, i ^ pair[(step + (i & CORE)) % 2]) for i in...  23.1 us
    ppermute x15, waiting for transfers between devices, by_core(): lax.ppermute(x, 'wide', [(i, i ^ pair[(step + (i & CORE)) % 2]) for i in...  22.5 us
    ppermute x17, starting transfers between devices, swap(): return lax.ppermute(x, 'wide', [(i, i ^ offset) for i in range(n)])  9.67 us
    pallas_call x2, Pallas kernels, fetched(): pl.pallas_call(functools.partial(fetch_kernel, symbols, width), out_shape...  9.02 us
    pallas_call x4, Pallas kernels, query_call(): pl.pallas_call(functools.partial(query_kernel, places, bool(carry), bool(...  5.9 us
    ppermute x17, waiting for transfers between devices, swap(): return lax.ppermute(x, 'wide', [(i, i ^ offset) for i in range(n)])  3.73 us
    pallas_call x5, Pallas kernels, output_call(): pl.pallas_call(functools.partial(output_kernel, spots), out_shape=[jax.Sh...  3.02 us
    pallas_call x1, Pallas kernels, kv_terms(): pl.pallas_call(functools.partial(kv_kernel, shared), out_shape=[jax.Shape...  2.55 us
  transfers between devices with their start and end apart: 32, of which 12 were waited for; matrix products, arithmetic and copies ran while one was open for 2% of the time, Pallas kernels for 20%

profile of v16, /device:TPU:0, one launch (start us, length us, event | category | flops | bytes accessed | tf_op | source)
XLA Modules:
  0.0 82.2 jit_solution(8838469748371720806)
XLA Ops:
  0.1 2.6 %shard_map.69 = (f32[8,128,128]{2,1,0:T(8,128)S(1)}, f32[8,128,128]{2,1,0:T(8,128)S(1)}, bf16[128,512]{1,0:T(8,128)(2,1)S(1)}, f32[1,16384]{1,0:T(1,128)S(1)}) custom-call(s32[9]{0:T(128)S(1)} %stack.42.where.refs_0_, bf16[128,512]{1,0:T(8,128)(2,1)} %act.1, f32[1,16384]{1,0:T(1,128)} %bitcast.22, bf16[512,1024]{1,0:T(8,128)(2,1)} %wk.1, bf16[512,1024]{1,0:T(8,128)(2,1)} %wv.1), custom_call_target="tpu_custom_call" | custom-call | flops 4294967296 | bytes 33554432 | tf_op jit(solution)/shard_map/pallas_call | solution.py:108
  2.6 0.5 collective-permute-start.1
  3.2 2.6 %collective-permute-start = (bf16[1,128,512]{2,1,0:T(8,128)(2,1)S(1)}, bf16[1,128,512]{2,1,0:T(8,128)(2,1)S(1)}, u32[]{:S(2)}, u32[]{:S(2)}) collective-permute-start(bf16[1,128,512]{2,1,0:T(8,128)(2,1)S(1)} %bitcast.18), channel_id=1, source_target_pairs={{0,8},{1,17},{2,10},{3,19},{4,12},{5,21},{6,14},{7,23},{8,0},{9,25... | collective-permute-start | bytes 393224 | tf_op jit(solution)/shard_map/ppermute | solution.py:262
  5.9 1.8 %collective-permute-start.2 = (bf16[4,128,128]{2,1,0:T(8,128)(2,1)S(1)}, bf16[4,128,128]{2,1,0:T(8,128)(2,1)S(1)}, u32[]{:S(2)}, u32[]{:S(2)}) collective-permute-start(bf16[4,128,128]{2,1,0:T(8,128)(2,1)S(1)} %slice.134), channel_id=1, source_target_pairs={{0,4},{1,5},{2,6},{3,7},{4,0},{5,1},{6,2},{7,3},{8,12},{9,13},{10,... | collective-permute-start | bytes 393224 | tf_op jit(solution)/shard_map/ppermute | solution.py:259
  7.8 2.1 %collective-permute-done = bf16[1,128,512]{2,1,0:T(8,128)(2,1)S(1)} collective-permute-done((bf16[1,128,512]{2,1,0:T(8,128)(2,1)S(1)}, bf16[1,128,512]{2,1,0:T(8,128)(2,1)S(1)}, u32[]{:S(2)}, u32[]{:S(2)}) %collective-permute-start) | collective-permute-done | bytes 131104 | tf_op jit(solution)/shard_map/ppermute | solution.py:262
  9.9 2.2 %collective-permute-start.4 = (bf16[2,128,512]{2,1,0:T(8,128)(2,1)S(1)}, bf16[2,128,512]{2,1,0:T(8,128)(2,1)S(1)}, u32[]{:S(2)}, u32[]{:S(2)}) collective-permute-start(bf16[2,128,512]{2,1,0:T(8,128)(2,1)S(1)} %pad_maximum_fusion.3.refs_2_), channel_id=1, source_target_pairs={{0,2},{1,5},{2,0},{3,7},{4,6},{5,1},{6,4},{7,3},{8,10},{9,13},{10,... | collective-permute-start | bytes 786440 | tf_op jit(solution)/shard_map/ppermute | solution.py:262
  12.2 2.3 %collective-permute-start.3 = (bf16[2,128,640]{2,1,0:T(8,128)(2,1)S(1)}, bf16[2,128,640]{2,1,0:T(8,128)(2,1)S(1)}, u32[]{:S(2)}, u32[]{:S(2)}) collective-permute-start(bf16[2,128,640]{2,1,0:T(8,128)(2,1)S(1)} %pad_maximum_fusion.2), channel_id=1, source_target_pairs={{0,16},{1,9},{2,18},{3,11},{4,20},{5,13},{6,22},{7,15},{8,24},{9,1... | collective-permute-start | bytes 983048 | tf_op jit(solution)/shard_map/ppermute | solution.py:262
  14.5 2.0 %collective-permute-done.4.refs_3_ = bf16[2,128,512]{2,1,0:T(8,128)(2,1)S(1)} collective-permute-done((bf16[2,128,512]{2,1,0:T(8,128)(2,1)S(1)}, bf16[2,128,512]{2,1,0:T(8,128)(2,1)S(1)}, u32[]{:S(2)}, u32[]{:S(2)}) %collective-permute-start.4) | collective-permute-done | bytes 262176 | tf_op jit(solution)/shard_map/ppermute | solution.py:262
  16.6 2.1 %collective-permute-start.12 = (bf16[4,128,512]{2,1,0:T(8,128)(2,1)S(1)}, bf16[4,128,512]{2,1,0:T(8,128)(2,1)S(1)}, u32[]{:S(2)}, u32[]{:S(2)}) collective-permute-start(bf16[4,128,512]{2,1,0:T(8,128)(2,1)S(1)} %pad_maximum_fusion), channel_id=1, source_target_pairs={{0,4},{1,3},{2,6},{3,1},{4,0},{5,7},{6,2},{7,5},{8,12},{9,11},{10,... | collective-permute-start | bytes 1572872 | tf_op jit(solution)/shard_map/ppermute | solution.py:262
  18.7 4.4 %shard_map.70.weight = bf16[16,512,512]{2,1,0:T(8,128)(2,1)S(1)} custom-call(s32[9]{0:T(128)S(1)} %stack.42.where.refs_0_, bf16[512,16384]{1,0:T(8,128)(2,1)} %source.3), custom_call_target="tpu_custom_call" | custom-call | bytes 16777216 | tf_op jit(solution)/shard_map/pallas_call | solution.py:67
  23.1 0.8 collective-permute-done.3
  23.9 0.5 collective-permute-start.6
  24.4 1.5 %collective-permute-start.5 = (bf16[2,128,512]{2,1,0:T(8,128)(2,1)S(1)}, bf16[2,128,512]{2,1,0:T(8,128)(2,1)S(1)}, u32[]{:S(2)}, u32[]{:S(2)}) collective-permute-start(bf16[2,128,512]{2,1,0:T(8,128)(2,1)S(1)} %slice.85.refs_2_), channel_id=1, source_target_pairs={{0,2},{1,5},{2,0},{3,7},{4,6},{5,1},{6,4},{7,3},{8,10},{9,13},{10,... | collective-permute-start | bytes 786440 | tf_op jit(solution)/shard_map/ppermute | solution.py:262
  26.3 0.5 collective-permute-start.14
  26.8 4.6 %shard_map.71.weight = bf16[16,512,512]{2,1,0:T(8,128)(2,1)S(1)} custom-call(s32[9]{0:T(128)S(1)} %stack.42.where.refs_0_, bf16[512,16384]{1,0:T(8,128)(2,1)} %source.3), custom_call_target="tpu_custom_call" | custom-call | bytes 16777216 | tf_op jit(solution)/shard_map/pallas_call | solution.py:67
  31.6 1.6 %collective-permute-start.7 = (bf16[4,128,512]{2,1,0:T(8,128)(2,1)S(1)}, bf16[4,128,512]{2,1,0:T(8,128)(2,1)S(1)}, u32[]{:S(2)}, u32[]{:S(2)}) collective-permute-start(bf16[4,128,512]{2,1,0:T(8,128)(2,1)S(1)} %pad_maximum_fusion.1), channel_id=1, source_target_pairs={{0,4},{1,3},{2,6},{3,1},{4,0},{5,7},{6,2},{7,5},{8,12},{9,11},{10,... | collective-permute-start | bytes 1572872 | tf_op jit(solution)/shard_map/ppermute | solution.py:262
  33.1 0.9 %collective-permute-start.8 = (bf16[128,128]{1,0:T(8,128)(2,1)S(1)}, bf16[128,128]{1,0:T(8,128)(2,1)S(1)}, u32[]{:S(2)}, u32[]{:S(2)}) collective-permute-start(bf16[128,128]{1,0:T(8,128)(2,1)S(1)} %bitcast_convert_fusion), channel_id=1, source_target_pairs={{0,2},{1,3},{2,0},{3,1},{4,6},{5,7},{6,4},{7,5},{8,10},{9,11},{10,... | collective-permute-start | bytes 98312 | tf_op jit(solution)/shard_map/ppermute | solution.py:259
  34.4 3.2 %collective-permute-done.8 = bf16[128,128]{1,0:T(8,128)(2,1)S(1)} collective-permute-done((bf16[128,128]{1,0:T(8,128)(2,1)S(1)}, bf16[128,128]{1,0:T(8,128)(2,1)S(1)}, u32[]{:S(2)}, u32[]{:S(2)}) %collective-permute-start.8) | collective-permute-done | bytes 32800 | tf_op jit(solution)/shard_map/ppermute | solution.py:259
  37.5 3.4 %collective-permute-start.11 = (bf16[2,128,512]{2,1,0:T(8,128)(2,1)S(1)}, bf16[2,128,512]{2,1,0:T(8,128)(2,1)S(1)}, u32[]{:S(2)}, u32[]{:S(2)}) collective-permute-start(bf16[2,128,512]{2,1,0:T(8,128)(2,1)S(1)} %collective-permute-done.5.refs_3_), channel_id=1, source_target_pairs={{0,1},{1,0},{2,3},{3,2},{4,5},{5,4},{6,7},{7,6},{8,9},{9,8},{10,11... | collective-permute-start | bytes 786440 | tf_op jit(solution)/shard_map/ppermute | solution.py:259
  41.1 2.0 %shard_map.72 = (f32[128,512]{1,0:T(8,128)S(1)}, f32[128,128]{1,0:T(8,128)S(1)}) custom-call(s32[9]{0:T(128)S(1)} %stack.42.where.refs_0_, f32[1,16384]{1,0:T(1,128)S(1)} %get-tuple-element.67.refs_1_, bf16[2,128,512]{2,1,0:T(8,128)(2,1)S(1)} %pad_maximum_fusion.3.refs_2_, bf16[2,128,512]{2,1,0:T(8,128)(2,1)S(1)} %collective-permute-done.4.refs_3_, ...), custom_call_target="tpu_custom_call" | custom-call | flops 1073741824 | bytes 8388608 | tf_op jit(solution)/shard_map/pallas_call | solution.py:201
  43.1 1.3 %shard_map.73 = (f32[128,512]{1,0:T(8,128)S(1)}, f32[128,128]{1,0:T(8,128)S(1)}) custom-call(s32[9]{0:T(128)S(1)} %stack.42.where.refs_0_, f32[1,16384]{1,0:T(1,128)S(1)} %get-tuple-element.67.refs_1_, bf16[2,128,512]{2,1,0:T(8,128)(2,1)S(1)} %slice.85.refs_2_, bf16[2,128,512]{2,1,0:T(8,128)(2,1)S(1)} %collective-permute-done.5.refs_3_, ...), custom_call_target="tpu_custom_call" | custom-call | flops 536870912 | bytes 4194304 | tf_op jit(solution)/shard_map/pallas_call | solution.py:201
  44.4 0.5 collective-permute-start.16
  45.0 1.0 %shard_map.74 = (f32[128,512]{1,0:T(8,128)S(1)}, f32[128,128]{1,0:T(8,128)S(1)}) custom-call(s32[9]{0:T(128)S(1)} %stack.42.where.refs_0_, f32[1,16384]{1,0:T(1,128)S(1)} %get-tuple-element.67.refs_1_, bf16[4,128,512]{2,1,0:T(8,128)(2,1)S(1)} %collective-permute-done.7.refs_2_, bf16[16384,512]{1,0:T(8,128)(2,1)S(1)} %bitcast.17, ...), custom_call_target="tpu_custom_call" | custom-call | flops 268435456 | bytes 2097152 | tf_op jit(solution)/shard_map/pallas_call | solution.py:201
  46.0 0.5 collective-permute-done.16.refs_2_
  46.5 1.6 %shard_map.75.attended = bf16[128,512]{1,0:T(8,128)(2,1)S(1)} custom-call(s32[9]{0:T(128)S(1)} %stack.42.where.refs_0_, f32[1,16384]{1,0:T(1,128)S(1)} %get-tuple-element.67.refs_1_, bf16[4,128,512]{2,1,0:T(8,128)(2,1)S(1)} %collective-permute-done.16.refs_2_, bf16[16384,512]{1,0:T(8,128)(2,1)S(1)} %bitcast.17, f32[128,512]{1,0:T(8,128)S(1)} %get-tuple-element.85.refs_4_, ...), custom_call_target="tpu_custom_call" | custom-call | flops 268435456 | bytes 2097152 | tf_op jit(solution)/shard_map/pallas_call | solution.py:201
  48.4 0.4 collective-permute-start.21
  48.8 0.6 shard_map.77
  49.6 0.4 collective-permute-start.17
  50.0 0.7 shard_map.79
  50.8 0.6 collective-permute-start.22
  51.4 0.7 shard_map.78
  52.4 1.5 %collective-permute-start.18 = (bf16[2,128,512]{2,1,0:T(8,128)(2,1)S(1)}, bf16[2,128,512]{2,1,0:T(8,128)(2,1)S(1)}, u32[]{:S(2)}, u32[]{:S(2)}) collective-permute-start(bf16[2,128,512]{2,1,0:T(8,128)(2,1)S(1)} %add_convert_fusion.5), channel_id=1, source_target_pairs={{0,2},{1,5},{2,0},{3,7},{4,6},{5,1},{6,4},{7,3},{8,10},{9,13},{10,... | collective-permute-start | bytes 786440 | tf_op jit(solution)/shard_map/ppermute | solution.py:262
  53.8 3.4 %collective-permute-done.22 = bf16[2,128,512]{2,1,0:T(8,128)(2,1)S(1)} collective-permute-done((bf16[2,128,512]{2,1,0:T(8,128)(2,1)S(1)}, bf16[2,128,512]{2,1,0:T(8,128)(2,1)S(1)}, u32[]{:S(2)}, u32[]{:S(2)}) %collective-permute-start.22) | collective-permute-done | bytes 262176 | tf_op jit(solution)/shard_map/ppermute | solution.py:262
  57.3 0.9 %collective-permute-start.28 = (bf16[2,128,512]{2,1,0:T(8,128)(2,1)S(1)}, bf16[2,128,512]{2,1,0:T(8,128)(2,1)S(1)}, u32[]{:S(2)}, u32[]{:S(2)}) collective-permute-start(bf16[2,128,512]{2,1,0:T(8,128)(2,1)S(1)} %add_convert_fusion.3), channel_id=1, source_target_pairs={{0,4},{1,3},{2,6},{3,1},{4,0},{5,7},{6,2},{7,5},{8,12},{9,11},{10,... | collective-permute-start | bytes 786440 | tf_op jit(solution)/shard_map/ppermute | solution.py:262
  58.2 2.5 %collective-permute-done.18 = bf16[2,128,512]{2,1,0:T(8,128)(2,1)S(1)} collective-permute-done((bf16[2,128,512]{2,1,0:T(8,128)(2,1)S(1)}, bf16[2,128,512]{2,1,0:T(8,128)(2,1)S(1)}, u32[]{:S(2)}, u32[]{:S(2)}) %collective-permute-start.18) | collective-permute-done | bytes 262176 | tf_op jit(solution)/shard_map/ppermute | solution.py:262
  60.7 0.7 shard_map.80
  61.6 0.6 collective-permute-start.24
  62.2 0.5 collective-permute-start.19
  62.7 1.8 %collective-permute-done.28 = bf16[2,128,512]{2,1,0:T(8,128)(2,1)S(1)} collective-permute-done((bf16[2,128,512]{2,1,0:T(8,128)(2,1)S(1)}, bf16[2,128,512]{2,1,0:T(8,128)(2,1)S(1)}, u32[]{:S(2)}, u32[]{:S(2)}) %collective-permute-start.28) | collective-permute-done | bytes 262176 | tf_op jit(solution)/shard_map/ppermute | solution.py:262
  64.7 2.6 %collective-permute-start.29 = (bf16[2,128,512]{2,1,0:T(8,128)(2,1)S(1)}, bf16[2,128,512]{2,1,0:T(8,128)(2,1)S(1)}, u32[]{:S(2)}, u32[]{:S(2)}) collective-permute-start(bf16[2,128,512]{2,1,0:T(8,128)(2,1)S(1)} %add_convert_fusion.1), channel_id=1, source_target_pairs={{0,16},{1,9},{2,18},{3,11},{4,20},{5,13},{6,22},{7,15},{8,24},{9,1... | collective-permute-start | bytes 786440 | tf_op jit(solution)/shard_map/ppermute | solution.py:262
  67.3 3.5 %collective-permute-done.24 = bf16[4,128,512]{2,1,0:T(8,128)(2,1)S(1)} collective-permute-done((bf16[4,128,512]{2,1,0:T(8,128)(2,1)S(1)}, bf16[4,128,512]{2,1,0:T(8,128)(2,1)S(1)}, u32[]{:S(2)}, u32[]{:S(2)}) %collective-permute-start.24) | collective-permute-done | bytes 524320 | tf_op jit(solution)/shard_map/ppermute | solution.py:262
  71.0 0.9 %collective-permute-start.30 = (bf16[1,128,512]{2,1,0:T(8,128)(2,1)S(1)}, bf16[1,128,512]{2,1,0:T(8,128)(2,1)S(1)}, u32[]{:S(2)}, u32[]{:S(2)}) collective-permute-start(bf16[1,128,512]{2,1,0:T(8,128)(2,1)S(1)} %get-tuple-element.110), channel_id=1, source_target_pairs={{0,4},{1,3},{2,6},{3,1},{4,0},{5,7},{6,2},{7,5},{8,12},{9,11},{10,... | collective-permute-start | bytes 393224 | tf_op jit(solution)/shard_map/ppermute | solution.py:262
  71.9 1.2 %collective-permute-start.26 = (bf16[1,128,512]{2,1,0:T(8,128)(2,1)S(1)}, bf16[1,128,512]{2,1,0:T(8,128)(2,1)S(1)}, u32[]{:S(2)}, u32[]{:S(2)}) collective-permute-start(bf16[1,128,512]{2,1,0:T(8,128)(2,1)S(1)} %get-tuple-element.109), channel_id=1, source_target_pairs={{0,4},{1,3},{2,6},{3,1},{4,0},{5,7},{6,2},{7,5},{8,12},{9,11},{10,... | collective-permute-start | bytes 393224 | tf_op jit(solution)/shard_map/ppermute | solution.py:262
  73.1 1.8 %collective-permute-done.29 = bf16[2,128,512]{2,1,0:T(8,128)(2,1)S(1)} collective-permute-done((bf16[2,128,512]{2,1,0:T(8,128)(2,1)S(1)}, bf16[2,128,512]{2,1,0:T(8,128)(2,1)S(1)}, u32[]{:S(2)}, u32[]{:S(2)}) %collective-permute-start.29) | collective-permute-done | bytes 262176 | tf_op jit(solution)/shard_map/ppermute | solution.py:262
  74.9 1.1 %collective-permute-done.30 = bf16[1,128,512]{2,1,0:T(8,128)(2,1)S(1)} collective-permute-done((bf16[1,128,512]{2,1,0:T(8,128)(2,1)S(1)}, bf16[1,128,512]{2,1,0:T(8,128)(2,1)S(1)}, u32[]{:S(2)}, u32[]{:S(2)}) %collective-permute-start.30) | collective-permute-done | bytes 131104 | tf_op jit(solution)/shard_map/ppermute | solution.py:262
  76.1 1.9 %collective-permute-start.31 = (bf16[1,128,512]{2,1,0:T(8,128)(2,1)S(1)}, bf16[1,128,512]{2,1,0:T(8,128)(2,1)S(1)}, u32[]{:S(2)}, u32[]{:S(2)}) collective-permute-start(bf16[1,128,512]{2,1,0:T(8,128)(2,1)S(1)} %add_convert_fusion.7), channel_id=1, source_target_pairs={{0,8},{1,17},{2,10},{3,19},{4,12},{5,21},{6,14},{7,23},{8,0},{9,25... | collective-permute-start | bytes 393224 | tf_op jit(solution)/shard_map/ppermute | solution.py:262
  78.1 3.4 %collective-permute-done.31 = bf16[1,128,512]{2,1,0:T(8,128)(2,1)S(1)} collective-permute-done((bf16[1,128,512]{2,1,0:T(8,128)(2,1)S(1)}, bf16[1,128,512]{2,1,0:T(8,128)(2,1)S(1)}, u32[]{:S(2)}, u32[]{:S(2)}) %collective-permute-start.31) | collective-permute-done | bytes 131104 | tf_op jit(solution)/shard_map/ppermute | solution.py:262
  81.4 0.8 fusion
  (64 shorter events, 2.7 us)
Async XLA Ops:
  2.6 3.2 %collective-permute-start.1 = (f32[8,128,128]{2,1,0:T(8,128)S(1)}, f32[8,128,128]{2,1,0:T(8,128)S(1)}, u32[]{:S(2)}, u32[]{:S(2)}) collective-permute-start(f32[8,128,128]{2,1,0:T(8,128)S(1)} %get-tuple-element.70), channel_id=1, source_target_pairs={{0,1},{1,0},{2,3},{3,2},{4,5},{5,4},{6,7},{7,6},{8,9},{9,8},{10,11... | collective-permute-start | bytes 1572872 | tf_op jit(solution)/shard_map/ppermute | solution.py:259
  3.2 6.7 %collective-permute-start = (bf16[1,128,512]{2,1,0:T(8,128)(2,1)S(1)}, bf16[1,128,512]{2,1,0:T(8,128)(2,1)S(1)}, u32[]{:S(2)}, u32[]{:S(2)}) collective-permute-start(bf16[1,128,512]{2,1,0:T(8,128)(2,1)S(1)} %bitcast.18), channel_id=1, source_target_pairs={{0,8},{1,17},{2,10},{3,19},{4,12},{5,21},{6,14},{7,23},{8,0},{9,25... | collective-permute-start | bytes 393224 | tf_op jit(solution)/shard_map/ppermute | solution.py:262
  5.9 6.2 %collective-permute-start.2 = (bf16[4,128,128]{2,1,0:T(8,128)(2,1)S(1)}, bf16[4,128,128]{2,1,0:T(8,128)(2,1)S(1)}, u32[]{:S(2)}, u32[]{:S(2)}) collective-permute-start(bf16[4,128,128]{2,1,0:T(8,128)(2,1)S(1)} %slice.134), channel_id=1, source_target_pairs={{0,4},{1,5},{2,6},{3,7},{4,0},{5,1},{6,2},{7,3},{8,12},{9,13},{10,... | collective-permute-start | bytes 393224 | tf_op jit(solution)/shard_map/ppermute | solution.py:259
  9.9 6.6 %collective-permute-start.4 = (bf16[2,128,512]{2,1,0:T(8,128)(2,1)S(1)}, bf16[2,128,512]{2,1,0:T(8,128)(2,1)S(1)}, u32[]{:S(2)}, u32[]{:S(2)}) collective-permute-start(bf16[2,128,512]{2,1,0:T(8,128)(2,1)S(1)} %pad_maximum_fusion.3.refs_2_), channel_id=1, source_target_pairs={{0,2},{1,5},{2,0},{3,7},{4,6},{5,1},{6,4},{7,3},{8,10},{9,13},{10,... | collective-permute-start | bytes 786440 | tf_op jit(solution)/shard_map/ppermute | solution.py:262
  12.2 11.6 %collective-permute-start.3 = (bf16[2,128,640]{2,1,0:T(8,128)(2,1)S(1)}, bf16[2,128,640]{2,1,0:T(8,128)(2,1)S(1)}, u32[]{:S(2)}, u32[]{:S(2)}) collective-permute-start(bf16[2,128,640]{2,1,0:T(8,128)(2,1)S(1)} %pad_maximum_fusion.2), channel_id=1, source_target_pairs={{0,16},{1,9},{2,18},{3,11},{4,20},{5,13},{6,22},{7,15},{8,24},{9,1... | collective-permute-start | bytes 983048 | tf_op jit(solution)/shard_map/ppermute | solution.py:262
  16.6 16.6 %collective-permute-start.12 = (bf16[4,128,512]{2,1,0:T(8,128)(2,1)S(1)}, bf16[4,128,512]{2,1,0:T(8,128)(2,1)S(1)}, u32[]{:S(2)}, u32[]{:S(2)}) collective-permute-start(bf16[4,128,512]{2,1,0:T(8,128)(2,1)S(1)} %pad_maximum_fusion), channel_id=1, source_target_pairs={{0,4},{1,3},{2,6},{3,1},{4,0},{5,7},{6,2},{7,5},{8,12},{9,11},{10,... | collective-permute-start | bytes 1572872 | tf_op jit(solution)/shard_map/ppermute | solution.py:262
  18.7 22.4 %slice-start = ((s8[16777216]{0:T(1024)(128)(4,1)}), s8[4194304]{0:T(1024)(128)(4,1)S(1)}, s32[]{:S(2)}) async-start(s8[16777216]{0:T(1024)(128)(4,1)} %bitcast.16), calls=%async_computation | async-start | bytes 8388608
  18.7 22.4 %slice-start.1 = ((s8[16777216]{0:T(1024)(128)(4,1)}), s8[4194304]{0:T(1024)(128)(4,1)S(1)}, s32[]{:S(2)}) async-start(s8[16777216]{0:T(1024)(128)(4,1)} %bitcast.16), calls=%async_computation.1 | async-start | bytes 8388608
  23.9 7.6 %collective-permute-start.6 = (bf16[1,128,128]{2,1,0:T(8,128)(2,1)S(1)}, bf16[1,128,128]{2,1,0:T(8,128)(2,1)S(1)}, u32[]{:S(2)}, u32[]{:S(2)}) collective-permute-start(bf16[1,128,128]{2,1,0:T(8,128)(2,1)S(1)} %slice.136), channel_id=1, source_target_pairs={{0,8},{1,17},{2,10},{3,19},{4,12},{5,21},{6,14},{7,23},{8,0},{9,25... | collective-permute-start | bytes 98312 | tf_op jit(solution)/shard_map/ppermute | solution.py:262
  24.4 7.0 %collective-permute-start.5 = (bf16[2,128,512]{2,1,0:T(8,128)(2,1)S(1)}, bf16[2,128,512]{2,1,0:T(8,128)(2,1)S(1)}, u32[]{:S(2)}, u32[]{:S(2)}) collective-permute-start(bf16[2,128,512]{2,1,0:T(8,128)(2,1)S(1)} %slice.85.refs_2_), channel_id=1, source_target_pairs={{0,2},{1,5},{2,0},{3,7},{4,6},{5,1},{6,4},{7,3},{8,10},{9,13},{10,... | collective-permute-start | bytes 786440 | tf_op jit(solution)/shard_map/ppermute | solution.py:262
  26.2 14.8 %slice-start.2 = ((s8[16777216]{0:T(1024)(128)(4,1)}), s8[4194304]{0:T(1024)(128)(4,1)S(1)}, s32[]{:S(2)}) async-start(s8[16777216]{0:T(1024)(128)(4,1)} %bitcast.16), calls=%async_computation.2 | async-start | bytes 8388608
  26.2 14.8 %slice-start.3 = ((s8[16777216]{0:T(1024)(128)(4,1)}), s8[4194304]{0:T(1024)(128)(4,1)S(1)}, s32[]{:S(2)}) async-start(s8[16777216]{0:T(1024)(128)(4,1)} %bitcast.16), calls=%async_computation.3 | async-start | bytes 8388608
  26.2 7.9 %collective-permute-start.13 = (bf16[2,128,512]{2,1,0:T(8,128)(2,1)S(1)}, bf16[2,128,512]{2,1,0:T(8,128)(2,1)S(1)}, u32[]{:S(2)}, u32[]{:S(2)}) collective-permute-start(bf16[2,128,512]{2,1,0:T(8,128)(2,1)S(1)} %pad_maximum_fusion.3.refs_2_), channel_id=1, source_target_pairs={{0,1},{1,0},{2,3},{3,2},{4,5},{5,4},{6,7},{7,6},{8,9},{9,8},{10,11... | collective-permute-start | bytes 786440 | tf_op jit(solution)/shard_map/ppermute | solution.py:259
  26.3 14.6 %collective-permute-start.14 = (bf16[2,128,512]{2,1,0:T(8,128)(2,1)S(1)}, bf16[2,128,512]{2,1,0:T(8,128)(2,1)S(1)}, u32[]{:S(2)}, u32[]{:S(2)}) collective-permute-start(bf16[2,128,512]{2,1,0:T(8,128)(2,1)S(1)} %collective-permute-done.4.refs_3_), channel_id=1, source_target_pairs={{0,1},{1,0},{2,3},{3,2},{4,5},{5,4},{6,7},{7,6},{8,9},{9,8},{10,11... | collective-permute-start | bytes 786440 | tf_op jit(solution)/shard_map/ppermute | solution.py:259
  31.6 12.9 %collective-permute-start.7 = (bf16[4,128,512]{2,1,0:T(8,128)(2,1)S(1)}, bf16[4,128,512]{2,1,0:T(8,128)(2,1)S(1)}, u32[]{:S(2)}, u32[]{:S(2)}) collective-permute-start(bf16[4,128,512]{2,1,0:T(8,128)(2,1)S(1)} %pad_maximum_fusion.1), channel_id=1, source_target_pairs={{0,4},{1,3},{2,6},{3,1},{4,0},{5,7},{6,2},{7,5},{8,12},{9,11},{10,... | collective-permute-start | bytes 1572872 | tf_op jit(solution)/shard_map/ppermute | solution.py:262
  33.1 7.9 %collective-permute-start.15 = (bf16[4,128,512]{2,1,0:T(8,128)(2,1)S(1)}, bf16[4,128,512]{2,1,0:T(8,128)(2,1)S(1)}, u32[]{:S(2)}, u32[]{:S(2)}) collective-permute-start(bf16[4,128,512]{2,1,0:T(8,128)(2,1)S(1)} %collective-permute-done.12.refs_4_), channel_id=1, source_target_pairs={{0,1},{1,0},{2,3},{3,2},{4,5},{5,4},{6,7},{7,6},{8,9},{9,8},{10,11... | collective-permute-start | bytes 1572872 | tf_op jit(solution)/shard_map/ppermute | solution.py:259
  33.1 4.4 %collective-permute-start.8 = (bf16[128,128]{1,0:T(8,128)(2,1)S(1)}, bf16[128,128]{1,0:T(8,128)(2,1)S(1)}, u32[]{:S(2)}, u32[]{:S(2)}) collective-permute-start(bf16[128,128]{1,0:T(8,128)(2,1)S(1)} %bitcast_convert_fusion), channel_id=1, source_target_pairs={{0,2},{1,3},{2,0},{3,1},{4,6},{5,7},{6,4},{7,5},{8,10},{9,11},{10,... | collective-permute-start | bytes 98312 | tf_op jit(solution)/shard_map/ppermute | solution.py:259
  34.1 8.9 %collective-permute-start.10 = (bf16[2,128,512]{2,1,0:T(8,128)(2,1)S(1)}, bf16[2,128,512]{2,1,0:T(8,128)(2,1)S(1)}, u32[]{:S(2)}, u32[]{:S(2)}) collective-permute-start(bf16[2,128,512]{2,1,0:T(8,128)(2,1)S(1)} %slice.85.refs_2_), channel_id=1, source_target_pairs={{0,1},{1,0},{2,3},{3,2},{4,5},{5,4},{6,7},{7,6},{8,9},{9,8},{10,11... | collective-permute-start | bytes 786440 | tf_op jit(solution)/shard_map/ppermute | solution.py:259
  37.5 5.5 %collective-permute-start.11 = (bf16[2,128,512]{2,1,0:T(8,128)(2,1)S(1)}, bf16[2,128,512]{2,1,0:T(8,128)(2,1)S(1)}, u32[]{:S(2)}, u32[]{:S(2)}) collective-permute-start(bf16[2,128,512]{2,1,0:T(8,128)(2,1)S(1)} %collective-permute-done.5.refs_3_), channel_id=1, source_target_pairs={{0,1},{1,0},{2,3},{3,2},{4,5},{5,4},{6,7},{7,6},{8,9},{9,8},{10,11... | collective-permute-start | bytes 786440 | tf_op jit(solution)/shard_map/ppermute | solution.py:259
  40.9 3.5 %collective-permute-start.9 = (f32[128,128]{1,0:T(8,128)S(1)}, f32[128,128]{1,0:T(8,128)S(1)}, u32[]{:S(2)}, u32[]{:S(2)}) collective-permute-start(f32[128,128]{1,0:T(8,128)S(1)} %bitcast_add_fusion.refs_6_), channel_id=1, source_target_pairs={{0,1},{1,0},{2,3},{3,2},{4,5},{5,4},{6,7},{7,6},{8,9},{9,8},{10,11... | collective-permute-start | bytes 196616 | tf_op jit(solution)/shard_map/ppermute | solution.py:259
  44.4 2.1 %collective-permute-start.16 = (bf16[4,128,512]{2,1,0:T(8,128)(2,1)S(1)}, bf16[4,128,512]{2,1,0:T(8,128)(2,1)S(1)}, u32[]{:S(2)}, u32[]{:S(2)}) collective-permute-start(bf16[4,128,512]{2,1,0:T(8,128)(2,1)S(1)} %collective-permute-done.7.refs_2_), channel_id=1, source_target_pairs={{0,1},{1,0},{2,3},{3,2},{4,5},{5,4},{6,7},{7,6},{8,9},{9,8},{10,11... | collective-permute-start | bytes 1572872 | tf_op jit(solution)/shard_map/ppermute | solution.py:259
  48.4 2.3 %collective-permute-start.21 = (bf16[2,128,512]{2,1,0:T(8,128)(2,1)S(1)}, bf16[2,128,512]{2,1,0:T(8,128)(2,1)S(1)}, u32[]{:S(2)}, u32[]{:S(2)}) collective-permute-start(bf16[2,128,512]{2,1,0:T(8,128)(2,1)S(1)} %shard_map.76), channel_id=1, source_target_pairs={{0,1},{1,0},{2,3},{3,2},{4,5},{5,4},{6,7},{7,6},{8,9},{9,8},{10,11... | collective-permute-start | bytes 786440 | tf_op jit(solution)/shard_map/ppermute | solution.py:259
  49.4 4.4 %collective-permute-start.20 = (bf16[2,128,512]{2,1,0:T(8,128)(2,1)S(1)}, bf16[2,128,512]{2,1,0:T(8,128)(2,1)S(1)}, u32[]{:S(2)}, u32[]{:S(2)}) collective-permute-start(bf16[2,128,512]{2,1,0:T(8,128)(2,1)S(1)} %get-tuple-element.103), channel_id=1, source_target_pairs={{0,1},{1,0},{2,3},{3,2},{4,5},{5,4},{6,7},{7,6},{8,9},{9,8},{10,11... | collective-permute-start | bytes 786440 | tf_op jit(solution)/shard_map/ppermute | solution.py:259
  49.6 2.7 %collective-permute-start.17 = (bf16[2,128,512]{2,1,0:T(8,128)(2,1)S(1)}, bf16[2,128,512]{2,1,0:T(8,128)(2,1)S(1)}, u32[]{:S(2)}, u32[]{:S(2)}) collective-permute-start(bf16[2,128,512]{2,1,0:T(8,128)(2,1)S(1)} %get-tuple-element.97), channel_id=1, source_target_pairs={{0,1},{1,0},{2,3},{3,2},{4,5},{5,4},{6,7},{7,6},{8,9},{9,8},{10,11... | collective-permute-start | bytes 786440 | tf_op jit(solution)/shard_map/ppermute | solution.py:259
  50.8 6.4 %collective-permute-start.22 = (bf16[2,128,512]{2,1,0:T(8,128)(2,1)S(1)}, bf16[2,128,512]{2,1,0:T(8,128)(2,1)S(1)}, u32[]{:S(2)}, u32[]{:S(2)}) collective-permute-start(bf16[2,128,512]{2,1,0:T(8,128)(2,1)S(1)} %add_convert_fusion.4), channel_id=1, source_target_pairs={{0,2},{1,5},{2,0},{3,7},{4,6},{5,1},{6,4},{7,3},{8,10},{9,13},{10,... | collective-permute-start | bytes 786440 | tf_op jit(solution)/shard_map/ppermute | solution.py:262
  52.1 9.3 %collective-permute-start.23 = (bf16[4,128,512]{2,1,0:T(8,128)(2,1)S(1)}, bf16[4,128,512]{2,1,0:T(8,128)(2,1)S(1)}, u32[]{:S(2)}, u32[]{:S(2)}) collective-permute-start(bf16[4,128,512]{2,1,0:T(8,128)(2,1)S(1)} %get-tuple-element.95), channel_id=1, source_target_pairs={{0,1},{1,0},{2,3},{3,2},{4,5},{5,4},{6,7},{7,6},{8,9},{9,8},{10,11... | collective-permute-start | bytes 1572872 | tf_op jit(solution)/shard_map/ppermute | solution.py:259
  52.4 8.3 %collective-permute-start.18 = (bf16[2,128,512]{2,1,0:T(8,128)(2,1)S(1)}, bf16[2,128,512]{2,1,0:T(8,128)(2,1)S(1)}, u32[]{:S(2)}, u32[]{:S(2)}) collective-permute-start(bf16[2,128,512]{2,1,0:T(8,128)(2,1)S(1)} %add_convert_fusion.5), channel_id=1, source_target_pairs={{0,2},{1,5},{2,0},{3,7},{4,6},{5,1},{6,4},{7,3},{8,10},{9,13},{10,... | collective-permute-start | bytes 786440 | tf_op jit(solution)/shard_map/ppermute | solution.py:262
  53.8 8.9 %collective-permute-start.27 = (bf16[2,128,512]{2,1,0:T(8,128)(2,1)S(1)}, bf16[2,128,512]{2,1,0:T(8,128)(2,1)S(1)}, u32[]{:S(2)}, u32[]{:S(2)}) collective-permute-start(bf16[2,128,512]{2,1,0:T(8,128)(2,1)S(1)} %get-tuple-element.92), channel_id=1, source_target_pairs={{0,1},{1,0},{2,3},{3,2},{4,5},{5,4},{6,7},{7,6},{8,9},{9,8},{10,11... | collective-permute-start | bytes 786440 | tf_op jit(solution)/shard_map/ppermute | solution.py:259
  57.3 7.2 %collective-permute-start.28 = (bf16[2,128,512]{2,1,0:T(8,128)(2,1)S(1)}, bf16[2,128,512]{2,1,0:T(8,128)(2,1)S(1)}, u32[]{:S(2)}, u32[]{:S(2)}) collective-permute-start(bf16[2,128,512]{2,1,0:T(8,128)(2,1)S(1)} %add_convert_fusion.3), channel_id=1, source_target_pairs={{0,4},{1,3},{2,6},{3,1},{4,0},{5,7},{6,2},{7,5},{8,12},{9,11},{10,... | collective-permute-start | bytes 786440 | tf_op jit(solution)/shard_map/ppermute | solution.py:262
  61.6 9.2 %collective-permute-start.24 = (bf16[4,128,512]{2,1,0:T(8,128)(2,1)S(1)}, bf16[4,128,512]{2,1,0:T(8,128)(2,1)S(1)}, u32[]{:S(2)}, u32[]{:S(2)}) collective-permute-start(bf16[4,128,512]{2,1,0:T(8,128)(2,1)S(1)} %add_convert_fusion), channel_id=1, source_target_pairs={{0,2},{1,5},{2,0},{3,7},{4,6},{5,1},{6,4},{7,3},{8,10},{9,13},{10,... | collective-permute-start | bytes 1572872 | tf_op jit(solution)/shard_map/ppermute | solution.py:262
  62.2 5.1 %collective-permute-start.25 = (bf16[2,128,512]{2,1,0:T(8,128)(2,1)S(1)}, bf16[2,128,512]{2,1,0:T(8,128)(2,1)S(1)}, u32[]{:S(2)}, u32[]{:S(2)}) collective-permute-start(bf16[2,128,512]{2,1,0:T(8,128)(2,1)S(1)} %get-tuple-element.107), channel_id=1, source_target_pairs={{0,1},{1,0},{2,3},{3,2},{4,5},{5,4},{6,7},{7,6},{8,9},{9,8},{10,11... | collective-permute-start | bytes 786440 | tf_op jit(solution)/shard_map/ppermute | solution.py:259
  62.2 10.9 %collective-permute-start.19 = (bf16[2,128,512]{2,1,0:T(8,128)(2,1)S(1)}, bf16[2,128,512]{2,1,0:T(8,128)(2,1)S(1)}, u32[]{:S(2)}, u32[]{:S(2)}) collective-permute-start(bf16[2,128,512]{2,1,0:T(8,128)(2,1)S(1)} %get-tuple-element.100), channel_id=1, source_target_pairs={{0,1},{1,0},{2,3},{3,2},{4,5},{5,4},{6,7},{7,6},{8,9},{9,8},{10,11... | collective-permute-start | bytes 786440 | tf_op jit(solution)/shard_map/ppermute | solution.py:259
  64.7 10.1 %collective-permute-start.29 = (bf16[2,128,512]{2,1,0:T(8,128)(2,1)S(1)}, bf16[2,128,512]{2,1,0:T(8,128)(2,1)S(1)}, u32[]{:S(2)}, u32[]{:S(2)}) collective-permute-start(bf16[2,128,512]{2,1,0:T(8,128)(2,1)S(1)} %add_convert_fusion.1), channel_id=1, source_target_pairs={{0,16},{1,9},{2,18},{3,11},{4,20},{5,13},{6,22},{7,15},{8,24},{9,1... | collective-permute-start | bytes 786440 | tf_op jit(solution)/shard_map/ppermute | solution.py:262
  71.0 5.0 %collective-permute-start.30 = (bf16[1,128,512]{2,1,0:T(8,128)(2,1)S(1)}, bf16[1,128,512]{2,1,0:T(8,128)(2,1)S(1)}, u32[]{:S(2)}, u32[]{:S(2)}) collective-permute-start(bf16[1,128,512]{2,1,0:T(8,128)(2,1)S(1)} %get-tuple-element.110), channel_id=1, source_target_pairs={{0,4},{1,3},{2,6},{3,1},{4,0},{5,7},{6,2},{7,5},{8,12},{9,11},{10,... | collective-permute-start | bytes 393224 | tf_op jit(solution)/shard_map/ppermute | solution.py:262
  71.9 6.1 %collective-permute-start.26 = (bf16[1,128,512]{2,1,0:T(8,128)(2,1)S(1)}, bf16[1,128,512]{2,1,0:T(8,128)(2,1)S(1)}, u32[]{:S(2)}, u32[]{:S(2)}) collective-permute-start(bf16[1,128,512]{2,1,0:T(8,128)(2,1)S(1)} %get-tuple-element.109), channel_id=1, source_target_pairs={{0,4},{1,3},{2,6},{3,1},{4,0},{5,7},{6,2},{7,5},{8,12},{9,11},{10,... | collective-permute-start | bytes 393224 | tf_op jit(solution)/shard_map/ppermute | solution.py:262
  76.1 5.3 %collective-permute-start.31 = (bf16[1,128,512]{2,1,0:T(8,128)(2,1)S(1)}, bf16[1,128,512]{2,1,0:T(8,128)(2,1)S(1)}, u32[]{:S(2)}, u32[]{:S(2)}) collective-permute-start(bf16[1,128,512]{2,1,0:T(8,128)(2,1)S(1)} %add_convert_fusion.7), channel_id=1, source_target_pairs={{0,8},{1,17},{2,10},{3,19},{4,12},{5,21},{6,14},{7,23},{8,0},{9,25... | collective-permute-start | bytes 393224 | tf_op jit(solution)/shard_map/ppermute | solution.py:262

commit v17 on v15

--- a/solution.py
+++ b/solution.py
@@ -334,7 +334,7 @@
         at = symbols_of(offsets)
         groups.append([(row, at[0]), (side, at[1]), (both, at[2] + at[3])])
     early, last = groups
-    early[2] = (after(early[2][0], blocks), early[2][1])
+    early[2] = (after(early[2][0], blocks, joined), early[2][1])
     partners = [swap(kv[0].astype(bf16), o) for o in combos(bits[1:shared])[1:]]
 
     call = functools.partial(query_call, where, gain, weight=wq)

time: 78.1 us -> 77.9 us (level)
  waiting for transfers between devices: 24.4 us -> 21 us
  starting transfers between devices: 30.7 us -> 33.8 us
    ppermute x15, waiting for transfers between devices: 23.3 us -> 19.8 us  [by_core(): lax.ppermute(x, 'wide', [(i, i ^ pair[(step + (i & CORE)) % 2]) for i in...]
    ppermute x15, starting transfers between devices: 23.1 us -> 26.6 us  [by_core(): lax.ppermute(x, 'wide', [(i, i ^ pair[(step + (i & CORE)) % 2]) for i in...]
where the time goes in v17:
time: 77.9 us; the launch traced here: 77.7 us
  starting transfers between devices  33.8 us (43%)
  waiting for transfers between devices  21 us (27%)
  Pallas kernels  20.2 us (26%)
  other arithmetic  2.17 us (3%)
    ppermute x15, starting transfers between devices, by_core(): lax.ppermute(x, 'wide', [(i, i ^ pair[(step + (i & CORE)) % 2]) for i in...  26.6 us
    ppermute x15, waiting for transfers between devices, by_core(): lax.ppermute(x, 'wide', [(i, i ^ pair[(step + (i & CORE)) % 2]) for i in...  19.8 us
    pallas_call x2, Pallas kernels, fetched(): pl.pallas_call(functools.partial(fetch_kernel, symbols, width), out_shape...  8.81 us
    ppermute x17, starting transfers between devices, swap(): return lax.ppermute(x, 'wide', [(i, i ^ offset) for i in range(n)])  7.25 us
    pallas_call x4, Pallas kernels, query_call(): pl.pallas_call(functools.partial(query_kernel, places, bool(carry), bool(...  5.87 us
    pallas_call x5, Pallas kernels, output_call(): pl.pallas_call(functools.partial(output_kernel, spots), out_shape=[jax.Sh...  3.01 us
    pallas_call x1, Pallas kernels, kv_terms(): pl.pallas_call(functools.partial(kv_kernel, shared), out_shape=[jax.Shape...  2.55 us
  transfers between devices with their start and end apart: 32, of which 14 were waited for; matrix products, arithmetic and copies ran while one was open for 2% of the time, Pallas kernels for 20%

profile of v17, /device:TPU:0, one launch (start us, length us, event | category | flops | bytes accessed | tf_op | source)
XLA Modules:
  0.0 77.7 jit_solution(5982078752134325507)
XLA Ops:
  0.1 2.6 %shard_map.69 = (f32[8,128,128]{2,1,0:T(8,128)S(1)}, f32[8,128,128]{2,1,0:T(8,128)S(1)}, bf16[128,512]{1,0:T(8,128)(2,1)S(1)}, f32[1,16384]{1,0:T(1,128)S(1)}) custom-call(s32[9]{0:T(128)S(1)} %stack.42.where.refs_0_, bf16[128,512]{1,0:T(8,128)(2,1)} %act.1, f32[1,16384]{1,0:T(1,128)} %bitcast.22, bf16[512,1024]{1,0:T(8,128)(2,1)} %wk.1, bf16[512,1024]{1,0:T(8,128)(2,1)} %wv.1), custom_call_target="tpu_custom_call" | custom-call | flops 4294967296 | bytes 33554432 | tf_op jit(solution)/shard_map/pallas_call | solution.py:108
  2.6 0.5 collective-permute-start.1
  3.2 2.6 %collective-permute-start = (bf16[1,128,512]{2,1,0:T(8,128)(2,1)S(1)}, bf16[1,128,512]{2,1,0:T(8,128)(2,1)S(1)}, u32[]{:S(2)}, u32[]{:S(2)}) collective-permute-start(bf16[1,128,512]{2,1,0:T(8,128)(2,1)S(1)} %bitcast.18), channel_id=1, source_target_pairs={{0,8},{1,17},{2,10},{3,19},{4,12},{5,21},{6,14},{7,23},{8,0},{9,25... | collective-permute-start | bytes 393224 | tf_op jit(solution)/shard_map/ppermute | solution.py:262
  5.9 1.8 %collective-permute-start.2 = (bf16[4,128,128]{2,1,0:T(8,128)(2,1)S(1)}, bf16[4,128,128]{2,1,0:T(8,128)(2,1)S(1)}, u32[]{:S(2)}, u32[]{:S(2)}) collective-permute-start(bf16[4,128,128]{2,1,0:T(8,128)(2,1)S(1)} %slice.134), channel_id=1, source_target_pairs={{0,4},{1,5},{2,6},{3,7},{4,0},{5,1},{6,2},{7,3},{8,12},{9,13},{10,... | collective-permute-start | bytes 393224 | tf_op jit(solution)/shard_map/ppermute | solution.py:259
  7.8 2.1 %collective-permute-done = bf16[1,128,512]{2,1,0:T(8,128)(2,1)S(1)} collective-permute-done((bf16[1,128,512]{2,1,0:T(8,128)(2,1)S(1)}, bf16[1,128,512]{2,1,0:T(8,128)(2,1)S(1)}, u32[]{:S(2)}, u32[]{:S(2)}) %collective-permute-start) | collective-permute-done | bytes 131104 | tf_op jit(solution)/shard_map/ppermute | solution.py:262
  9.9 2.2 %collective-permute-start.4 = (bf16[2,128,512]{2,1,0:T(8,128)(2,1)S(1)}, bf16[2,128,512]{2,1,0:T(8,128)(2,1)S(1)}, u32[]{:S(2)}, u32[]{:S(2)}) collective-permute-start(bf16[2,128,512]{2,1,0:T(8,128)(2,1)S(1)} %pad_maximum_fusion.3.refs_2_), channel_id=1, source_target_pairs={{0,2},{1,5},{2,0},{3,7},{4,6},{5,1},{6,4},{7,3},{8,10},{9,13},{10,... | collective-permute-start | bytes 786440 | tf_op jit(solution)/shard_map/ppermute | solution.py:262
  12.2 2.3 %collective-permute-start.3 = (bf16[2,128,640]{2,1,0:T(8,128)(2,1)S(1)}, bf16[2,128,640]{2,1,0:T(8,128)(2,1)S(1)}, u32[]{:S(2)}, u32[]{:S(2)}) collective-permute-start(bf16[2,128,640]{2,1,0:T(8,128)(2,1)S(1)} %pad_maximum_fusion.2), channel_id=1, source_target_pairs={{0,16},{1,9},{2,18},{3,11},{4,20},{5,13},{6,22},{7,15},{8,24},{9,1... | collective-permute-start | bytes 983048 | tf_op jit(solution)/shard_map/ppermute | solution.py:262
  14.5 2.0 %collective-permute-done.4.refs_3_ = bf16[2,128,512]{2,1,0:T(8,128)(2,1)S(1)} collective-permute-done((bf16[2,128,512]{2,1,0:T(8,128)(2,1)S(1)}, bf16[2,128,512]{2,1,0:T(8,128)(2,1)S(1)}, u32[]{:S(2)}, u32[]{:S(2)}) %collective-permute-start.4) | collective-permute-done | bytes 262176 | tf_op jit(solution)/shard_map/ppermute | solution.py:262
  16.6 2.1 %collective-permute-start.11 = (bf16[4,128,512]{2,1,0:T(8,128)(2,1)S(1)}, bf16[4,128,512]{2,1,0:T(8,128)(2,1)S(1)}, u32[]{:S(2)}, u32[]{:S(2)}) collective-permute-start(bf16[4,128,512]{2,1,0:T(8,128)(2,1)S(1)} %pad_maximum_fusion), channel_id=1, source_target_pairs={{0,4},{1,3},{2,6},{3,1},{4,0},{5,7},{6,2},{7,5},{8,12},{9,11},{10,... | collective-permute-start | bytes 1572872 | tf_op jit(solution)/shard_map/ppermute | solution.py:262
  18.7 4.4 %shard_map.70.weight = bf16[16,512,512]{2,1,0:T(8,128)(2,1)S(1)} custom-call(s32[9]{0:T(128)S(1)} %stack.42.where.refs_0_, bf16[512,16384]{1,0:T(8,128)(2,1)} %source.3), custom_call_target="tpu_custom_call" | custom-call | bytes 16777216 | tf_op jit(solution)/shard_map/pallas_call | solution.py:67
  23.1 0.8 collective-permute-done.3
  23.9 0.5 collective-permute-start.6
  24.4 1.5 %collective-permute-start.5 = (bf16[2,128,512]{2,1,0:T(8,128)(2,1)S(1)}, bf16[2,128,512]{2,1,0:T(8,128)(2,1)S(1)}, u32[]{:S(2)}, u32[]{:S(2)}) collective-permute-start(bf16[2,128,512]{2,1,0:T(8,128)(2,1)S(1)} %slice.85.refs_2_), channel_id=1, source_target_pairs={{0,2},{1,5},{2,0},{3,7},{4,6},{5,1},{6,4},{7,3},{8,10},{9,13},{10,... | collective-permute-start | bytes 786440 | tf_op jit(solution)/shard_map/ppermute | solution.py:262
  26.0 4.4 %shard_map.71.weight = bf16[16,512,512]{2,1,0:T(8,128)(2,1)S(1)} custom-call(s32[9]{0:T(128)S(1)} %stack.42.where.refs_0_, bf16[512,16384]{1,0:T(8,128)(2,1)} %source.3), custom_call_target="tpu_custom_call" | custom-call | bytes 16777216 | tf_op jit(solution)/shard_map/pallas_call | solution.py:67
  30.9 1.6 %collective-permute-start.7 = (bf16[4,128,512]{2,1,0:T(8,128)(2,1)S(1)}, bf16[4,128,512]{2,1,0:T(8,128)(2,1)S(1)}, u32[]{:S(2)}, u32[]{:S(2)}) collective-permute-start(bf16[4,128,512]{2,1,0:T(8,128)(2,1)S(1)} %pad_maximum_fusion.1), channel_id=1, source_target_pairs={{0,4},{1,3},{2,6},{3,1},{4,0},{5,7},{6,2},{7,5},{8,12},{9,11},{10,... | collective-permute-start | bytes 1572872 | tf_op jit(solution)/shard_map/ppermute | solution.py:262
  32.7 0.6 collective-permute-start.13
  33.5 0.5 collective-permute-start.10
  34.0 0.8 collective-permute-done.13.refs_6_
  34.7 1.5 %collective-permute-start.8 = (bf16[128,128]{1,0:T(8,128)(2,1)S(1)}, bf16[128,128]{1,0:T(8,128)(2,1)S(1)}, u32[]{:S(2)}, u32[]{:S(2)}) collective-permute-start(bf16[128,128]{1,0:T(8,128)(2,1)S(1)} %bitcast_convert_fusion), channel_id=1, source_target_pairs={{0,2},{1,3},{2,0},{3,1},{4,6},{5,7},{6,4},{7,5},{8,10},{9,11},{10,... | collective-permute-start | bytes 98312 | tf_op jit(solution)/shard_map/ppermute | solution.py:259
  36.3 2.0 %shard_map.72 = (f32[128,512]{1,0:T(8,128)S(1)}, f32[128,128]{1,0:T(8,128)S(1)}) custom-call(s32[9]{0:T(128)S(1)} %stack.42.where.refs_0_, f32[1,16384]{1,0:T(1,128)S(1)} %get-tuple-element.66.refs_1_, bf16[2,128,512]{2,1,0:T(8,128)(2,1)S(1)} %pad_maximum_fusion.3.refs_2_, bf16[2,128,512]{2,1,0:T(8,128)(2,1)S(1)} %collective-permute-done.4.refs_3_, ...), custom_call_target="tpu_custom_call" | custom-call | flops 1073741824 | bytes 8388608 | tf_op jit(solution)/shard_map/pallas_call | solution.py:201
  38.3 1.3 %shard_map.73 = (f32[128,512]{1,0:T(8,128)S(1)}, f32[128,128]{1,0:T(8,128)S(1)}) custom-call(s32[9]{0:T(128)S(1)} %stack.42.where.refs_0_, f32[1,16384]{1,0:T(1,128)S(1)} %get-tuple-element.66.refs_1_, bf16[2,128,512]{2,1,0:T(8,128)(2,1)S(1)} %slice.85.refs_2_, bf16[2,128,512]{2,1,0:T(8,128)(2,1)S(1)} %collective-permute-done.5.refs_3_, ...), custom_call_target="tpu_custom_call" | custom-call | flops 536870912 | bytes 4194304 | tf_op jit(solution)/shard_map/pallas_call | solution.py:201
  39.6 0.5 collective-permute-done.7.refs_2_
  40.3 0.4 collective-permute-start.16
  40.7 1.0 %shard_map.74 = (f32[128,512]{1,0:T(8,128)S(1)}, f32[128,128]{1,0:T(8,128)S(1)}) custom-call(s32[9]{0:T(128)S(1)} %stack.42.where.refs_0_, f32[1,16384]{1,0:T(1,128)S(1)} %get-tuple-element.66.refs_1_, bf16[4,128,512]{2,1,0:T(8,128)(2,1)S(1)} %collective-permute-done.7.refs_2_, bf16[16384,512]{1,0:T(8,128)(2,1)S(1)} %bitcast.17, ...), custom_call_target="tpu_custom_call" | custom-call | flops 268435456 | bytes 2097152 | tf_op jit(solution)/shard_map/pallas_call | solution.py:201
  41.7 0.4 collective-permute-done.16.refs_7_
  42.1 1.6 %shard_map.75.attended = bf16[128,512]{1,0:T(8,128)(2,1)S(1)} custom-call(s32[9]{0:T(128)S(1)} %stack.42.where.refs_0_, f32[1,16384]{1,0:T(1,128)S(1)} %get-tuple-element.66.refs_1_, bf16[4,128,512]{2,1,0:T(8,128)(2,1)S(1)} %collective-permute-done.15.refs_2_, bf16[16384,512]{1,0:T(8,128)(2,1)S(1)} %bitcast.17, f32[128,512]{1,0:T(8,128)S(1)} %get-tuple-element.84.refs_4_, ...), custom_call_target="tpu_custom_call" | custom-call | flops 268435456 | bytes 2097152 | tf_op jit(solution)/shard_map/pallas_call | solution.py:201
  44.3 0.6 shard_map.77
  44.8 0.4 collective-permute-start.20
  45.4 0.7 shard_map.79
  46.2 1.5 %collective-permute-start.22 = (bf16[2,128,512]{2,1,0:T(8,128)(2,1)S(1)}, bf16[2,128,512]{2,1,0:T(8,128)(2,1)S(1)}, u32[]{:S(2)}, u32[]{:S(2)}) collective-permute-start(bf16[2,128,512]{2,1,0:T(8,128)(2,1)S(1)} %add_convert_fusion.4), channel_id=1, source_target_pairs={{0,2},{1,5},{2,0},{3,7},{4,6},{5,1},{6,4},{7,3},{8,10},{9,13},{10,... | collective-permute-start | bytes 786440 | tf_op jit(solution)/shard_map/ppermute | solution.py:262
  47.7 0.7 shard_map.78
  48.7 1.6 %collective-permute-start.18 = (bf16[2,128,512]{2,1,0:T(8,128)(2,1)S(1)}, bf16[2,128,512]{2,1,0:T(8,128)(2,1)S(1)}, u32[]{:S(2)}, u32[]{:S(2)}) collective-permute-start(bf16[2,128,512]{2,1,0:T(8,128)(2,1)S(1)} %add_convert_fusion.5), channel_id=1, source_target_pairs={{0,2},{1,5},{2,0},{3,7},{4,6},{5,1},{6,4},{7,3},{8,10},{9,13},{10,... | collective-permute-start | bytes 786440 | tf_op jit(solution)/shard_map/ppermute | solution.py:262
  50.4 2.2 %collective-permute-done.22 = bf16[2,128,512]{2,1,0:T(8,128)(2,1)S(1)} collective-permute-done((bf16[2,128,512]{2,1,0:T(8,128)(2,1)S(1)}, bf16[2,128,512]{2,1,0:T(8,128)(2,1)S(1)}, u32[]{:S(2)}, u32[]{:S(2)}) %collective-permute-start.22) | collective-permute-done | bytes 262176 | tf_op jit(solution)/shard_map/ppermute | solution.py:262
  52.8 1.5 %collective-permute-start.28 = (bf16[2,128,512]{2,1,0:T(8,128)(2,1)S(1)}, bf16[2,128,512]{2,1,0:T(8,128)(2,1)S(1)}, u32[]{:S(2)}, u32[]{:S(2)}) collective-permute-start(bf16[2,128,512]{2,1,0:T(8,128)(2,1)S(1)} %add_convert_fusion.3), channel_id=1, source_target_pairs={{0,4},{1,3},{2,6},{3,1},{4,0},{5,7},{6,2},{7,5},{8,12},{9,11},{10,... | collective-permute-start | bytes 786440 | tf_op jit(solution)/shard_map/ppermute | solution.py:262
  54.3 1.6 %collective-permute-done.18 = bf16[2,128,512]{2,1,0:T(8,128)(2,1)S(1)} collective-permute-done((bf16[2,128,512]{2,1,0:T(8,128)(2,1)S(1)}, bf16[2,128,512]{2,1,0:T(8,128)(2,1)S(1)}, u32[]{:S(2)}, u32[]{:S(2)}) %collective-permute-start.18) | collective-permute-done | bytes 262176 | tf_op jit(solution)/shard_map/ppermute | solution.py:262
  55.9 0.7 shard_map.80
  56.8 1.5 %collective-permute-start.24 = (bf16[4,128,512]{2,1,0:T(8,128)(2,1)S(1)}, bf16[4,128,512]{2,1,0:T(8,128)(2,1)S(1)}, u32[]{:S(2)}, u32[]{:S(2)}) collective-permute-start(bf16[4,128,512]{2,1,0:T(8,128)(2,1)S(1)} %add_convert_fusion), channel_id=1, source_target_pairs={{0,2},{1,5},{2,0},{3,7},{4,6},{5,1},{6,4},{7,3},{8,10},{9,13},{10,... | collective-permute-start | bytes 1572872 | tf_op jit(solution)/shard_map/ppermute | solution.py:262
  58.3 0.5 collective-permute-start.19
  58.8 1.0 %collective-permute-done.28 = bf16[2,128,512]{2,1,0:T(8,128)(2,1)S(1)} collective-permute-done((bf16[2,128,512]{2,1,0:T(8,128)(2,1)S(1)}, bf16[2,128,512]{2,1,0:T(8,128)(2,1)S(1)}, u32[]{:S(2)}, u32[]{:S(2)}) %collective-permute-start.28) | collective-permute-done | bytes 262176 | tf_op jit(solution)/shard_map/ppermute | solution.py:262
  60.0 3.2 %collective-permute-start.29 = (bf16[2,128,512]{2,1,0:T(8,128)(2,1)S(1)}, bf16[2,128,512]{2,1,0:T(8,128)(2,1)S(1)}, u32[]{:S(2)}, u32[]{:S(2)}) collective-permute-start(bf16[2,128,512]{2,1,0:T(8,128)(2,1)S(1)} %add_convert_fusion.1), channel_id=1, source_target_pairs={{0,16},{1,9},{2,18},{3,11},{4,20},{5,13},{6,22},{7,15},{8,24},{9,1... | collective-permute-start | bytes 786440 | tf_op jit(solution)/shard_map/ppermute | solution.py:262
  63.2 2.9 %collective-permute-done.24 = bf16[4,128,512]{2,1,0:T(8,128)(2,1)S(1)} collective-permute-done((bf16[4,128,512]{2,1,0:T(8,128)(2,1)S(1)}, bf16[4,128,512]{2,1,0:T(8,128)(2,1)S(1)}, u32[]{:S(2)}, u32[]{:S(2)}) %collective-permute-start.24) | collective-permute-done | bytes 524320 | tf_op jit(solution)/shard_map/ppermute | solution.py:262
  66.2 1.5 %collective-permute-start.30 = (bf16[1,128,512]{2,1,0:T(8,128)(2,1)S(1)}, bf16[1,128,512]{2,1,0:T(8,128)(2,1)S(1)}, u32[]{:S(2)}, u32[]{:S(2)}) collective-permute-start(bf16[1,128,512]{2,1,0:T(8,128)(2,1)S(1)} %get-tuple-element.108), channel_id=1, source_target_pairs={{0,4},{1,3},{2,6},{3,1},{4,0},{5,7},{6,2},{7,5},{8,12},{9,11},{10,... | collective-permute-start | bytes 393224 | tf_op jit(solution)/shard_map/ppermute | solution.py:262
  67.7 0.6 collective-permute-start.26
  68.3 2.0 %collective-permute-done.29 = bf16[2,128,512]{2,1,0:T(8,128)(2,1)S(1)} collective-permute-done((bf16[2,128,512]{2,1,0:T(8,128)(2,1)S(1)}, bf16[2,128,512]{2,1,0:T(8,128)(2,1)S(1)}, u32[]{:S(2)}, u32[]{:S(2)}) %collective-permute-start.29) | collective-permute-done | bytes 262176 | tf_op jit(solution)/shard_map/ppermute | solution.py:262
  70.3 0.9 %collective-permute-done.30 = bf16[1,128,512]{2,1,0:T(8,128)(2,1)S(1)} collective-permute-done((bf16[1,128,512]{2,1,0:T(8,128)(2,1)S(1)}, bf16[1,128,512]{2,1,0:T(8,128)(2,1)S(1)}, u32[]{:S(2)}, u32[]{:S(2)}) %collective-permute-start.30) | collective-permute-done | bytes 131104 | tf_op jit(solution)/shard_map/ppermute | solution.py:262
  71.3 2.3 %collective-permute-start.31 = (bf16[1,128,512]{2,1,0:T(8,128)(2,1)S(1)}, bf16[1,128,512]{2,1,0:T(8,128)(2,1)S(1)}, u32[]{:S(2)}, u32[]{:S(2)}) collective-permute-start(bf16[1,128,512]{2,1,0:T(8,128)(2,1)S(1)} %add_convert_fusion.7), channel_id=1, source_target_pairs={{0,8},{1,17},{2,10},{3,19},{4,12},{5,21},{6,14},{7,23},{8,0},{9,25... | collective-permute-start | bytes 393224 | tf_op jit(solution)/shard_map/ppermute | solution.py:262
  73.6 3.4 %collective-permute-done.31 = bf16[1,128,512]{2,1,0:T(8,128)(2,1)S(1)} collective-permute-done((bf16[1,128,512]{2,1,0:T(8,128)(2,1)S(1)}, bf16[1,128,512]{2,1,0:T(8,128)(2,1)S(1)}, u32[]{:S(2)}, u32[]{:S(2)}) %collective-permute-start.31) | collective-permute-done | bytes 131104 | tf_op jit(solution)/shard_map/ppermute | solution.py:262
  77.0 0.8 fusion
  (64 shorter events, 3.3 us)
Async XLA Ops:
  2.6 3.2 %collective-permute-start.1 = (f32[8,128,128]{2,1,0:T(8,128)S(1)}, f32[8,128,128]{2,1,0:T(8,128)S(1)}, u32[]{:S(2)}, u32[]{:S(2)}) collective-permute-start(f32[8,128,128]{2,1,0:T(8,128)S(1)} %get-tuple-element.69), channel_id=1, source_target_pairs={{0,1},{1,0},{2,3},{3,2},{4,5},{5,4},{6,7},{7,6},{8,9},{9,8},{10,11... | collective-permute-start | bytes 1572872 | tf_op jit(solution)/shard_map/ppermute | solution.py:259
  3.2 6.7 %collective-permute-start = (bf16[1,128,512]{2,1,0:T(8,128)(2,1)S(1)}, bf16[1,128,512]{2,1,0:T(8,128)(2,1)S(1)}, u32[]{:S(2)}, u32[]{:S(2)}) collective-permute-start(bf16[1,128,512]{2,1,0:T(8,128)(2,1)S(1)} %bitcast.18), channel_id=1, source_target_pairs={{0,8},{1,17},{2,10},{3,19},{4,12},{5,21},{6,14},{7,23},{8,0},{9,25... | collective-permute-start | bytes 393224 | tf_op jit(solution)/shard_map/ppermute | solution.py:262
  5.9 6.2 %collective-permute-start.2 = (bf16[4,128,128]{2,1,0:T(8,128)(2,1)S(1)}, bf16[4,128,128]{2,1,0:T(8,128)(2,1)S(1)}, u32[]{:S(2)}, u32[]{:S(2)}) collective-permute-start(bf16[4,128,128]{2,1,0:T(8,128)(2,1)S(1)} %slice.134), channel_id=1, source_target_pairs={{0,4},{1,5},{2,6},{3,7},{4,0},{5,1},{6,2},{7,3},{8,12},{9,13},{10,... | collective-permute-start | bytes 393224 | tf_op jit(solution)/shard_map/ppermute | solution.py:259
  9.9 6.6 %collective-permute-start.4 = (bf16[2,128,512]{2,1,0:T(8,128)(2,1)S(1)}, bf16[2,128,512]{2,1,0:T(8,128)(2,1)S(1)}, u32[]{:S(2)}, u32[]{:S(2)}) collective-permute-start(bf16[2,128,512]{2,1,0:T(8,128)(2,1)S(1)} %pad_maximum_fusion.3.refs_2_), channel_id=1, source_target_pairs={{0,2},{1,5},{2,0},{3,7},{4,6},{5,1},{6,4},{7,3},{8,10},{9,13},{10,... | collective-permute-start | bytes 786440 | tf_op jit(solution)/shard_map/ppermute | solution.py:262
  12.2 11.6 %collective-permute-start.3 = (bf16[2,128,640]{2,1,0:T(8,128)(2,1)S(1)}, bf16[2,128,640]{2,1,0:T(8,128)(2,1)S(1)}, u32[]{:S(2)}, u32[]{:S(2)}) collective-permute-start(bf16[2,128,640]{2,1,0:T(8,128)(2,1)S(1)} %pad_maximum_fusion.2), channel_id=1, source_target_pairs={{0,16},{1,9},{2,18},{3,11},{4,20},{5,13},{6,22},{7,15},{8,24},{9,1... | collective-permute-start | bytes 983048 | tf_op jit(solution)/shard_map/ppermute | solution.py:262
  16.6 15.9 %collective-permute-start.11 = (bf16[4,128,512]{2,1,0:T(8,128)(2,1)S(1)}, bf16[4,128,512]{2,1,0:T(8,128)(2,1)S(1)}, u32[]{:S(2)}, u32[]{:S(2)}) collective-permute-start(bf16[4,128,512]{2,1,0:T(8,128)(2,1)S(1)} %pad_maximum_fusion), channel_id=1, source_target_pairs={{0,4},{1,3},{2,6},{3,1},{4,0},{5,7},{6,2},{7,5},{8,12},{9,11},{10,... | collective-permute-start | bytes 1572872 | tf_op jit(solution)/shard_map/ppermute | solution.py:262
  18.7 17.6 %slice-start = ((s8[16777216]{0:T(1024)(128)(4,1)}), s8[4194304]{0:T(1024)(128)(4,1)S(1)}, s32[]{:S(2)}) async-start(s8[16777216]{0:T(1024)(128)(4,1)} %bitcast.16), calls=%async_computation | async-start | bytes 8388608
  18.7 17.6 %slice-start.1 = ((s8[16777216]{0:T(1024)(128)(4,1)}), s8[4194304]{0:T(1024)(128)(4,1)S(1)}, s32[]{:S(2)}) async-start(s8[16777216]{0:T(1024)(128)(4,1)} %bitcast.16), calls=%async_computation.1 | async-start | bytes 8388608
  23.9 6.6 %collective-permute-start.6 = (bf16[1,128,128]{2,1,0:T(8,128)(2,1)S(1)}, bf16[1,128,128]{2,1,0:T(8,128)(2,1)S(1)}, u32[]{:S(2)}, u32[]{:S(2)}) collective-permute-start(bf16[1,128,128]{2,1,0:T(8,128)(2,1)S(1)} %slice.136), channel_id=1, source_target_pairs={{0,8},{1,17},{2,10},{3,19},{4,12},{5,21},{6,14},{7,23},{8,0},{9,25... | collective-permute-start | bytes 98312 | tf_op jit(solution)/shard_map/ppermute | solution.py:262
  24.4 6.4 %collective-permute-start.5 = (bf16[2,128,512]{2,1,0:T(8,128)(2,1)S(1)}, bf16[2,128,512]{2,1,0:T(8,128)(2,1)S(1)}, u32[]{:S(2)}, u32[]{:S(2)}) collective-permute-start(bf16[2,128,512]{2,1,0:T(8,128)(2,1)S(1)} %slice.85.refs_2_), channel_id=1, source_target_pairs={{0,2},{1,5},{2,0},{3,7},{4,6},{5,1},{6,4},{7,3},{8,10},{9,13},{10,... | collective-permute-start | bytes 786440 | tf_op jit(solution)/shard_map/ppermute | solution.py:262
  26.0 10.3 %slice-start.2 = ((s8[16777216]{0:T(1024)(128)(4,1)}), s8[4194304]{0:T(1024)(128)(4,1)S(1)}, s32[]{:S(2)}) async-start(s8[16777216]{0:T(1024)(128)(4,1)} %bitcast.16), calls=%async_computation.2 | async-start | bytes 8388608
  26.0 10.3 %slice-start.3 = ((s8[16777216]{0:T(1024)(128)(4,1)}), s8[4194304]{0:T(1024)(128)(4,1)S(1)}, s32[]{:S(2)}) async-start(s8[16777216]{0:T(1024)(128)(4,1)} %bitcast.16), calls=%async_computation.3 | async-start | bytes 8388608
  26.0 7.5 %collective-permute-start.12 = (bf16[2,128,512]{2,1,0:T(8,128)(2,1)S(1)}, bf16[2,128,512]{2,1,0:T(8,128)(2,1)S(1)}, u32[]{:S(2)}, u32[]{:S(2)}) collective-permute-start(bf16[2,128,512]{2,1,0:T(8,128)(2,1)S(1)} %pad_maximum_fusion.3.refs_2_), channel_id=1, source_target_pairs={{0,1},{1,0},{2,3},{3,2},{4,5},{5,4},{6,7},{7,6},{8,9},{9,8},{10,11... | collective-permute-start | bytes 786440 | tf_op jit(solution)/shard_map/ppermute | solution.py:259
  30.9 9.2 %collective-permute-start.7 = (bf16[4,128,512]{2,1,0:T(8,128)(2,1)S(1)}, bf16[4,128,512]{2,1,0:T(8,128)(2,1)S(1)}, u32[]{:S(2)}, u32[]{:S(2)}) collective-permute-start(bf16[4,128,512]{2,1,0:T(8,128)(2,1)S(1)} %pad_maximum_fusion.1), channel_id=1, source_target_pairs={{0,4},{1,3},{2,6},{3,1},{4,0},{5,7},{6,2},{7,5},{8,12},{9,11},{10,... | collective-permute-start | bytes 1572872 | tf_op jit(solution)/shard_map/ppermute | solution.py:262
  32.4 3.8 %collective-permute-start.14 = (bf16[4,128,512]{2,1,0:T(8,128)(2,1)S(1)}, bf16[4,128,512]{2,1,0:T(8,128)(2,1)S(1)}, u32[]{:S(2)}, u32[]{:S(2)}) collective-permute-start(bf16[4,128,512]{2,1,0:T(8,128)(2,1)S(1)} %collective-permute-done.11.refs_4_), channel_id=1, source_target_pairs={{0,1},{1,0},{2,3},{3,2},{4,5},{5,4},{6,7},{7,6},{8,9},{9,8},{10,11... | collective-permute-start | bytes 1572872 | tf_op jit(solution)/shard_map/ppermute | solution.py:259
  32.7 2.0 %collective-permute-start.13 = (bf16[2,128,512]{2,1,0:T(8,128)(2,1)S(1)}, bf16[2,128,512]{2,1,0:T(8,128)(2,1)S(1)}, u32[]{:S(2)}, u32[]{:S(2)}) collective-permute-start(bf16[2,128,512]{2,1,0:T(8,128)(2,1)S(1)} %collective-permute-done.4.refs_3_), channel_id=1, source_target_pairs={{0,1},{1,0},{2,3},{3,2},{4,5},{5,4},{6,7},{7,6},{8,9},{9,8},{10,11... | collective-permute-start | bytes 786440 | tf_op jit(solution)/shard_map/ppermute | solution.py:259
  33.4 4.9 %collective-permute-start.9 = (bf16[2,128,512]{2,1,0:T(8,128)(2,1)S(1)}, bf16[2,128,512]{2,1,0:T(8,128)(2,1)S(1)}, u32[]{:S(2)}, u32[]{:S(2)}) collective-permute-start(bf16[2,128,512]{2,1,0:T(8,128)(2,1)S(1)} %slice.85.refs_2_), channel_id=1, source_target_pairs={{0,1},{1,0},{2,3},{3,2},{4,5},{5,4},{6,7},{7,6},{8,9},{9,8},{10,11... | collective-permute-start | bytes 786440 | tf_op jit(solution)/shard_map/ppermute | solution.py:259
  33.5 4.8 %collective-permute-start.10 = (bf16[2,128,512]{2,1,0:T(8,128)(2,1)S(1)}, bf16[2,128,512]{2,1,0:T(8,128)(2,1)S(1)}, u32[]{:S(2)}, u32[]{:S(2)}) collective-permute-start(bf16[2,128,512]{2,1,0:T(8,128)(2,1)S(1)} %collective-permute-done.5.refs_3_), channel_id=1, source_target_pairs={{0,1},{1,0},{2,3},{3,2},{4,5},{5,4},{6,7},{7,6},{8,9},{9,8},{10,11... | collective-permute-start | bytes 786440 | tf_op jit(solution)/shard_map/ppermute | solution.py:259
  34.7 4.9 %collective-permute-start.8 = (bf16[128,128]{1,0:T(8,128)(2,1)S(1)}, bf16[128,128]{1,0:T(8,128)(2,1)S(1)}, u32[]{:S(2)}, u32[]{:S(2)}) collective-permute-start(bf16[128,128]{1,0:T(8,128)(2,1)S(1)} %bitcast_convert_fusion), channel_id=1, source_target_pairs={{0,2},{1,3},{2,0},{3,1},{4,6},{5,7},{6,4},{7,5},{8,10},{9,11},{10,... | collective-permute-start | bytes 98312 | tf_op jit(solution)/shard_map/ppermute | solution.py:259
  40.1 2.0 %collective-permute-start.15 = (bf16[4,128,512]{2,1,0:T(8,128)(2,1)S(1)}, bf16[4,128,512]{2,1,0:T(8,128)(2,1)S(1)}, u32[]{:S(2)}, u32[]{:S(2)}) collective-permute-start(bf16[4,128,512]{2,1,0:T(8,128)(2,1)S(1)} %collective-permute-done.7.refs_2_), channel_id=1, source_target_pairs={{0,1},{1,0},{2,3},{3,2},{4,5},{5,4},{6,7},{7,6},{8,9},{9,8},{10,11... | collective-permute-start | bytes 1572872 | tf_op jit(solution)/shard_map/ppermute | solution.py:259
  40.3 1.8 %collective-permute-start.16 = (f32[128,128]{1,0:T(8,128)S(1)}, f32[128,128]{1,0:T(8,128)S(1)}, u32[]{:S(2)}, u32[]{:S(2)}) collective-permute-start(f32[128,128]{1,0:T(8,128)S(1)} %bitcast_add_fusion.refs_6_), channel_id=1, source_target_pairs={{0,1},{1,0},{2,3},{3,2},{4,5},{5,4},{6,7},{7,6},{8,9},{9,8},{10,11... | collective-permute-start | bytes 196616 | tf_op jit(solution)/shard_map/ppermute | solution.py:259
  44.0 2.1 %collective-permute-start.21 = (bf16[2,128,512]{2,1,0:T(8,128)(2,1)S(1)}, bf16[2,128,512]{2,1,0:T(8,128)(2,1)S(1)}, u32[]{:S(2)}, u32[]{:S(2)}) collective-permute-start(bf16[2,128,512]{2,1,0:T(8,128)(2,1)S(1)} %shard_map.76), channel_id=1, source_target_pairs={{0,1},{1,0},{2,3},{3,2},{4,5},{5,4},{6,7},{7,6},{8,9},{9,8},{10,11... | collective-permute-start | bytes 786440 | tf_op jit(solution)/shard_map/ppermute | solution.py:259
  44.8 5.6 %collective-permute-start.20 = (bf16[2,128,512]{2,1,0:T(8,128)(2,1)S(1)}, bf16[2,128,512]{2,1,0:T(8,128)(2,1)S(1)}, u32[]{:S(2)}, u32[]{:S(2)}) collective-permute-start(bf16[2,128,512]{2,1,0:T(8,128)(2,1)S(1)} %get-tuple-element.101), channel_id=1, source_target_pairs={{0,1},{1,0},{2,3},{3,2},{4,5},{5,4},{6,7},{7,6},{8,9},{9,8},{10,11... | collective-permute-start | bytes 786440 | tf_op jit(solution)/shard_map/ppermute | solution.py:259
  45.2 3.4 %collective-permute-start.17 = (bf16[2,128,512]{2,1,0:T(8,128)(2,1)S(1)}, bf16[2,128,512]{2,1,0:T(8,128)(2,1)S(1)}, u32[]{:S(2)}, u32[]{:S(2)}) collective-permute-start(bf16[2,128,512]{2,1,0:T(8,128)(2,1)S(1)} %get-tuple-element.95), channel_id=1, source_target_pairs={{0,1},{1,0},{2,3},{3,2},{4,5},{5,4},{6,7},{7,6},{8,9},{9,8},{10,11... | collective-permute-start | bytes 786440 | tf_op jit(solution)/shard_map/ppermute | solution.py:259
  46.2 6.4 %collective-permute-start.22 = (bf16[2,128,512]{2,1,0:T(8,128)(2,1)S(1)}, bf16[2,128,512]{2,1,0:T(8,128)(2,1)S(1)}, u32[]{:S(2)}, u32[]{:S(2)}) collective-permute-start(bf16[2,128,512]{2,1,0:T(8,128)(2,1)S(1)} %add_convert_fusion.4), channel_id=1, source_target_pairs={{0,2},{1,5},{2,0},{3,7},{4,6},{5,1},{6,4},{7,3},{8,10},{9,13},{10,... | collective-permute-start | bytes 786440 | tf_op jit(solution)/shard_map/ppermute | solution.py:262
  48.5 8.2 %collective-permute-start.23 = (bf16[4,128,512]{2,1,0:T(8,128)(2,1)S(1)}, bf16[4,128,512]{2,1,0:T(8,128)(2,1)S(1)}, u32[]{:S(2)}, u32[]{:S(2)}) collective-permute-start(bf16[4,128,512]{2,1,0:T(8,128)(2,1)S(1)} %get-tuple-element.93), channel_id=1, source_target_pairs={{0,1},{1,0},{2,3},{3,2},{4,5},{5,4},{6,7},{7,6},{8,9},{9,8},{10,11... | collective-permute-start | bytes 1572872 | tf_op jit(solution)/shard_map/ppermute | solution.py:259
  48.7 7.2 %collective-permute-start.18 = (bf16[2,128,512]{2,1,0:T(8,128)(2,1)S(1)}, bf16[2,128,512]{2,1,0:T(8,128)(2,1)S(1)}, u32[]{:S(2)}, u32[]{:S(2)}) collective-permute-start(bf16[2,128,512]{2,1,0:T(8,128)(2,1)S(1)} %add_convert_fusion.5), channel_id=1, source_target_pairs={{0,2},{1,5},{2,0},{3,7},{4,6},{5,1},{6,4},{7,3},{8,10},{9,13},{10,... | collective-permute-start | bytes 786440 | tf_op jit(solution)/shard_map/ppermute | solution.py:262
  50.3 8.6 %collective-permute-start.27 = (bf16[2,128,512]{2,1,0:T(8,128)(2,1)S(1)}, bf16[2,128,512]{2,1,0:T(8,128)(2,1)S(1)}, u32[]{:S(2)}, u32[]{:S(2)}) collective-permute-start(bf16[2,128,512]{2,1,0:T(8,128)(2,1)S(1)} %get-tuple-element.90), channel_id=1, source_target_pairs={{0,1},{1,0},{2,3},{3,2},{4,5},{5,4},{6,7},{7,6},{8,9},{9,8},{10,11... | collective-permute-start | bytes 786440 | tf_op jit(solution)/shard_map/ppermute | solution.py:259
  52.8 7.1 %collective-permute-start.28 = (bf16[2,128,512]{2,1,0:T(8,128)(2,1)S(1)}, bf16[2,128,512]{2,1,0:T(8,128)(2,1)S(1)}, u32[]{:S(2)}, u32[]{:S(2)}) collective-permute-start(bf16[2,128,512]{2,1,0:T(8,128)(2,1)S(1)} %add_convert_fusion.3), channel_id=1, source_target_pairs={{0,4},{1,3},{2,6},{3,1},{4,0},{5,7},{6,2},{7,5},{8,12},{9,11},{10,... | collective-permute-start | bytes 786440 | tf_op jit(solution)/shard_map/ppermute | solution.py:262
  56.8 9.2 %collective-permute-start.24 = (bf16[4,128,512]{2,1,0:T(8,128)(2,1)S(1)}, bf16[4,128,512]{2,1,0:T(8,128)(2,1)S(1)}, u32[]{:S(2)}, u32[]{:S(2)}) collective-permute-start(bf16[4,128,512]{2,1,0:T(8,128)(2,1)S(1)} %add_convert_fusion), channel_id=1, source_target_pairs={{0,2},{1,5},{2,0},{3,7},{4,6},{5,1},{6,4},{7,3},{8,10},{9,13},{10,... | collective-permute-start | bytes 1572872 | tf_op jit(solution)/shard_map/ppermute | solution.py:262
  58.3 4.9 %collective-permute-start.25 = (bf16[2,128,512]{2,1,0:T(8,128)(2,1)S(1)}, bf16[2,128,512]{2,1,0:T(8,128)(2,1)S(1)}, u32[]{:S(2)}, u32[]{:S(2)}) collective-permute-start(bf16[2,128,512]{2,1,0:T(8,128)(2,1)S(1)} %get-tuple-element.105), channel_id=1, source_target_pairs={{0,1},{1,0},{2,3},{3,2},{4,5},{5,4},{6,7},{7,6},{8,9},{9,8},{10,11... | collective-permute-start | bytes 786440 | tf_op jit(solution)/shard_map/ppermute | solution.py:259
  58.3 10.0 %collective-permute-start.19 = (bf16[2,128,512]{2,1,0:T(8,128)(2,1)S(1)}, bf16[2,128,512]{2,1,0:T(8,128)(2,1)S(1)}, u32[]{:S(2)}, u32[]{:S(2)}) collective-permute-start(bf16[2,128,512]{2,1,0:T(8,128)(2,1)S(1)} %get-tuple-element.98), channel_id=1, source_target_pairs={{0,1},{1,0},{2,3},{3,2},{4,5},{5,4},{6,7},{7,6},{8,9},{9,8},{10,11... | collective-permute-start | bytes 786440 | tf_op jit(solution)/shard_map/ppermute | solution.py:259
  60.0 10.4 %collective-permute-start.29 = (bf16[2,128,512]{2,1,0:T(8,128)(2,1)S(1)}, bf16[2,128,512]{2,1,0:T(8,128)(2,1)S(1)}, u32[]{:S(2)}, u32[]{:S(2)}) collective-permute-start(bf16[2,128,512]{2,1,0:T(8,128)(2,1)S(1)} %add_convert_fusion.1), channel_id=1, source_target_pairs={{0,16},{1,9},{2,18},{3,11},{4,20},{5,13},{6,22},{7,15},{8,24},{9,1... | collective-permute-start | bytes 786440 | tf_op jit(solution)/shard_map/ppermute | solution.py:262
  66.2 5.0 %collective-permute-start.30 = (bf16[1,128,512]{2,1,0:T(8,128)(2,1)S(1)}, bf16[1,128,512]{2,1,0:T(8,128)(2,1)S(1)}, u32[]{:S(2)}, u32[]{:S(2)}) collective-permute-start(bf16[1,128,512]{2,1,0:T(8,128)(2,1)S(1)} %get-tuple-element.108), channel_id=1, source_target_pairs={{0,4},{1,3},{2,6},{3,1},{4,0},{5,7},{6,2},{7,5},{8,12},{9,11},{10,... | collective-permute-start | bytes 393224 | tf_op jit(solution)/shard_map/ppermute | solution.py:262
  67.7 5.9 %collective-permute-start.26 = (bf16[1,128,512]{2,1,0:T(8,128)(2,1)S(1)}, bf16[1,128,512]{2,1,0:T(8,128)(2,1)S(1)}, u32[]{:S(2)}, u32[]{:S(2)}) collective-permute-start(bf16[1,128,512]{2,1,0:T(8,128)(2,1)S(1)} %get-tuple-element.107), channel_id=1, source_target_pairs={{0,4},{1,3},{2,6},{3,1},{4,0},{5,7},{6,2},{7,5},{8,12},{9,11},{10,... | collective-permute-start | bytes 393224 | tf_op jit(solution)/shard_map/ppermute | solution.py:262
  71.3 5.6 %collective-permute-start.31 = (bf16[1,128,512]{2,1,0:T(8,128)(2,1)S(1)}, bf16[1,128,512]{2,1,0:T(8,128)(2,1)S(1)}, u32[]{:S(2)}, u32[]{:S(2)}) collective-permute-start(bf16[1,128,512]{2,1,0:T(8,128)(2,1)S(1)} %add_convert_fusion.7), channel_id=1, source_target_pairs={{0,8},{1,17},{2,10},{3,19},{4,12},{5,21},{6,14},{7,23},{8,0},{9,25... | collective-permute-start | bytes 393224 | tf_op jit(solution)/shard_map/ppermute | solution.py:262
